TPU v7x, 32 devices: a whole 2x2x4 slice. The times are simulated.
32 devices in a mesh: groups: 2 (over y), dp: 4 (over z), tensor: 4 (over x, core).
Axes of the slice: x: 2, y: 2, z: 4, core: 2. Of those that a mesh axis runs over, the one named last changes fastest.
Arguments:
- tokens: bfloat16 [3072, 8192], P(('groups', 'dp'), 'tensor'), parts along dimension 0, may hold values from -6 to 6
- cotangent: bfloat16 [1024, 16384], P(('groups', 'tensor'), 'dp'), parts along dimension 0, may hold values from -6 to 6
- frozen_up_weight: bfloat16 [8192, 16384], P('tensor', 'dp'), may hold values from -0.0625 to 0.0625
- adapter_down_factor: bfloat16 [8, 8192, 64], P(('groups', 'dp'), 'tensor'), parts along dimension 0, may hold values from -0.0625 to 0.0625
- adapter_up_factor: bfloat16 [8, 64, 16384], P('groups', None, 'dp'), parts along dimension 0, may hold values from -0.75 to 0.75
- tokens_per_adapter: int32 [8], P('groups'), parts along dimension 0, may hold values from 0 to 384, as said below
- adapter_of_block: int32 [8], P('groups'), parts along dimension 0, may hold values from 0 to 3, as said below
- slot_of_block: int32 [8], P('groups'), parts along dimension 0, may hold values from 0 to 2, as said below
Outputs:
- projected: bfloat16 [1024, 16384], P(('groups', 'tensor'), 'dp'), parts along dimension 0
- adapter_down_gradient: float32 [8, 8192, 64], P(('groups', 'dp'), 'tensor'), parts along dimension 0
- adapter_up_gradient: float32 [8, 64, 16384], P('groups', None, 'dp'), parts along dimension 0
There are 2 independent parts, one for each index of `groups`. A program takes and returns all parts, laid end to end along the dimension named above; an argument that names none is the same for every part. Nothing has to cross between parts.
Inputs may be any that keep to these rules, and one draw needn't show every extreme that they name: Adapter a uses ceil(tokens_per_adapter[a] / 128) blocks, at most 3; these numbers sum to 4. One adapter holds exactly 384 tokens. `adapter_of_block`: Non-decreasing; adapter a holds ceil(tokens_per_adapter[a] / 128) consecutive entries; the last entry is 3. `slot_of_block`: blocks of one adapter sit in distinct slots of that adapter's owner.
All inputs are finite; a program needn't handle non-finite values.
Results may differ from a plain program's by a relative error of at most 0.0031.
Values may be sent and summed in bfloat16 or wider, within the bound.
No kernel may reach another device: no remote copies, remote signals or barrier semaphores. Data moves between devices by JAX's collectives and lax.ppermute only.
A program may use at most 128 MiB of HBM per device.

v0:
```python
import jax
import jax.numpy as jnp
from jax import lax
from jax.sharding import PartitionSpec as P

BLK = 128
CAP = 3


adapter_scale = 0.5


def block_live(tokens_per_adapter, adapter_of_block, block_rows):
    adapter_count = tokens_per_adapter.shape[0]
    nblocks = (tokens_per_adapter + block_rows - 1) // block_rows
    first_block = jnp.cumsum(nblocks) - nblocks
    membership_mask = (
        adapter_of_block[:, None] == jnp.arange(adapter_count, dtype=jnp.int32)[None, :]
    ).astype(jnp.int32)
    begin_block = jnp.sum(membership_mask * first_block[None, :], axis=1)
    total_rows = jnp.sum(membership_mask * tokens_per_adapter[None, :], axis=1)
    block_place = jnp.arange(adapter_of_block.shape[0], dtype=jnp.int32) - begin_block
    offset = block_place[:, None] * block_rows + jnp.arange(block_rows, dtype=jnp.int32)[None, :]
    return (offset < total_rows[:, None]).astype(jnp.float32)


def per_device(
    tokens,
    cotangent,
    frozen_up_weight,
    adapter_down_factor,
    adapter_up_factor,
    tokens_per_adapter,
    adapter_of_block,
    slot_of_block,
):
    owner_index = lax.axis_index("dp")
    block_count = adapter_of_block.shape[0]
    width_dev = tokens.shape[1]
    live_rows = block_live(tokens_per_adapter, adapter_of_block, BLK)
    keep_rows = live_rows.astype(jnp.bfloat16)[:, :, None]
    rows_per_slot = tokens.reshape(CAP, BLK, width_dev)
    partial_low = jnp.einsum(
        "mgh,hx->mgx", rows_per_slot, adapter_down_factor[0], preferred_element_type=jnp.float32
    )
    lowered = lax.psum(partial_low, "tensor").astype(jnp.bfloat16)
    every_rows, every_low = (
        lax.all_gather(rows_per_slot, "dp", axis=0, tiled=True),
        lax.all_gather(lowered, "dp", axis=0, tiled=True),
    )
    where_slot = adapter_of_block * CAP + slot_of_block
    selected_factor = every_rows[where_slot] * keep_rows
    low_rows = every_low[where_slot] * keep_rows
    flat_rows = selected_factor.reshape(block_count * BLK, width_dev)
    shared_rows = flat_rows.shape[0] // lax.axis_size("tensor")
    frozen_contribution = lax.psum_scatter(
        jnp.dot(flat_rows, frozen_up_weight, preferred_element_type=jnp.float32),
        "tensor",
        scatter_dimension=0,
        tiled=True,
    )
    part_index = lax.axis_index("tensor")
    per_part = block_count // lax.axis_size("tensor")
    rank_projected_rows = lax.dynamic_slice_in_dim(low_rows, part_index * per_part, per_part, 0)
    adapter_contribution = lax.dynamic_slice_in_dim(
        adapter_of_block, part_index * per_part, per_part, 0
    )
    adapter_side_term = jnp.einsum(
        "azs,asg->azg",
        rank_projected_rows,
        adapter_up_factor[adapter_contribution],
        preferred_element_type=jnp.float32,
    )
    projected = (
        frozen_contribution + adapter_scale * adapter_side_term.reshape(shared_rows, -1)
    ).astype(jnp.bfloat16)
    gathered = lax.all_gather(cotangent, "tensor", axis=0, tiled=True)
    masked = gathered.reshape(block_count, BLK, -1) * keep_rows
    selected_rows = adapter_up_factor[adapter_of_block]
    partial_back = jnp.einsum(
        "bkf,brf->bkr", masked, selected_rows, preferred_element_type=jnp.float32
    )
    returned_rows = lax.psum(partial_back, "dp").astype(jnp.bfloat16)
    membership_mask = (
        adapter_of_block[:, None]
        == jnp.arange(adapter_up_factor.shape[0], dtype=jnp.int32)[None, :]
    ).astype(jnp.float32)
    pieces = jnp.einsum("bkr,bkf->brf", low_rows, masked, preferred_element_type=jnp.float32)
    adapter_up_gradient = adapter_scale * jnp.einsum(
        "dg,dwq->gwq", membership_mask, pieces, precision=lax.Precision.HIGHEST
    )
    slot_match = slot_of_block[None, :] == jnp.arange(CAP, dtype=jnp.int32)[:, None]
    slot_pick = (slot_match & (adapter_of_block[None, :] == owner_index)).astype(jnp.bfloat16)
    back_slots = jnp.einsum(
        "sb,bkr->skr", slot_pick, returned_rows, preferred_element_type=jnp.float32
    ).astype(jnp.bfloat16)
    down_factor_gradient = adapter_scale * jnp.einsum(
        "skd,skr->dr", rows_per_slot, back_slots, preferred_element_type=jnp.float32
    )
    return (projected, down_factor_gradient[None], adapter_up_gradient)


def solution(mesh):
    return jax.shard_map(
        per_device,
        mesh=mesh,
        in_specs=(
            P(("groups", "dp"), "tensor"),
            P(("groups", "tensor"), "dp"),
            P("tensor", "dp"),
            P(("groups", "dp"), "tensor", None),
            P("groups", None, "dp"),
            P("groups"),
            P("groups"),
            P("groups"),
        ),
        out_specs=(
            P(("groups", "tensor"), "dp"),
            P(("groups", "dp"), "tensor", None),
            P("groups", None, "dp"),
        ),
        check_vma=False,
    )
```

profile of v0, /device:TPU:0, one launch (start us, length us, event | category | flops | bytes accessed | tf_op | source)
XLA Modules:
  0.0 247.2 jit_solution(3549088257048056065)
XLA Ops:
  7.3 0.7 all-gather.3.cloned.1.call-update
  8.0 0.7 all-gather.5.cloned.1.call-update
  8.8 0.2 reduce-window.9
  9.0 0.1 select_reduce_fusion.1
  9.2 118.6 %all-gather.3.cloned.1.call-done = bf16[12,128,2048]{2,1,0:T(8,128)(2,1)} async-done(((bf16[3,128,2048]{2,1,0:T(8,128)(2,1)}), bf16[12,128,2048]{2,1,0:T(8,128)(2,1)}) %all-gather.3.cloned.1.call-update) | async-done | bytes 6291472 | tf_op jit(solution)/shard_map/all_gather | solution.py:48
  127.7 4.8 %gather_fusion = bf16[4,128,2048]{2,1,0:T(8,128)(2,1)} fusion(bf16[12,128,2048]{2,1,0:T(8,128)(2,1)} %all-gather.3.cloned.1.call-done, s32[1024]{0:T(1024)S(1)} %pad_clamp_fusion.1), kind=kCustom, calls=%fused_computation | custom fusion | bytes 4194320 | tf_op jit(solution)/shard_map/gather | solution.py:52
  132.5 2.0 bitcast_multiply_fusion
  134.5 15.2 %fusion.28 = f32[512,4096]{1,0:T(8,128)} fusion(bf16[512,2048]{1,0:T(8,128)(2,1)S(1)} %bitcast_multiply_fusion, bf16[2048,4096]{1,0:T(8,128)(2,1)} %param.10), kind=kOutput, calls=%fused_computation.52 | convolution fusion | flops 8589934592 | bytes 27262976 | tf_op jit(solution)/shard_map/dot_general | solution.py:57
  149.8 0.6 dynamic_slice.7
  151.6 2.0 fusion.13
  153.7 13.2 %psum.14 = bf16[3,128,64]{1,2,0:T(8,128)(2,1)S(1)} all-reduce(f32[3,128,64]{1,2,0:T(8,128)S(1)} %fusion.13), channel_id=1, replica_groups=mesh['groups'=2,'dp'=4,'tensor'=4] {'tensor'}, use_global_device_ids=true, to_apply=%region_4.5 | all-reduce | flops 24576 | bytes 147456 | tf_op jit(solution)/shard_map/psum | solution.py:46
  166.9 13.6 %all_gather.10 = bf16[12,128,64]{1,2,0:T(8,128)(2,1)S(1)} all-gather(bf16[3,128,64]{1,2,0:T(8,128)(2,1)S(1)} %psum.14), channel_id=1, replica_groups=mesh['groups'=2,'dp'=4,'tensor'=4] {'dp'}, dimensions={0}, use_global_device_ids=true | all-gather | bytes 245760 | tf_op jit(solution)/shard_map/all_gather | solution.py:49
  180.5 0.6 gather_fusion.1
  181.8 2.0 gather_fusion.2
  183.8 4.1 %fusion.5 = f32[4,128,64]{2,1,0:T(8,128)S(1)} fusion(bf16[4,64,4096]{2,1,0:T(8,128)(2,1)} %gather_fusion.2, bf16[4,128,4096]{2,1,0:T(8,128)(2,1)} %bitcast.45, bf16[4,128]{1,0:T(4,128)(2,1)S(1)} %get-tuple-element.22), kind=kOutput, calls=%fused_computation.10 | convolution fusion | flops 270532608 | bytes 6423552 | tf_op jit(solution)/shard_map/bkf,brf->bkr/dot_general | solution.py:80
  188.0 21.2 %all-reduce.1 = bf16[4,128,64]{2,1,0:T(8,128)(2,1)S(1)} all-reduce(f32[4,128,64]{2,1,0:T(8,128)S(1)} %fusion.5), channel_id=1, replica_groups=mesh['groups'=2,'dp'=4,'tensor'=4] {'dp'}, use_global_device_ids=true, to_apply=%region_5.6 | all-reduce | flops 32768 | bytes 196608 | tf_op jit(solution)/shard_map/psum | solution.py:83
  209.2 0.1 copy.13
  209.3 3.1 %fusion.3 = f32[4,64,4096]{2,1,0:T(8,128)S(1)} fusion(bf16[4,128,4096]{2,1,0:T(8,128)(2,1)} %bitcast.46, bf16[4,128]{1,0:T(4,128)(2,1)S(1)} %get-tuple-element.22, bf16[4,128,64]{1,2,0:T(8,128)(2,1)S(1)} %gather_fusion.1), kind=kOutput, calls=%fused_computation.8 | convolution fusion | flops 270565376 | bytes 8455168 | tf_op jit(solution)/shard_map/bkr,bkf->brf/dot_general | solution.py:88
  212.4 6.2 %convolution_multiply_fusion = f32[4,64,4096]{2,0,1:T(4,128)S(1)} fusion(f32[4,64,4096]{2,1,0:T(8,128)S(1)} %fusion.3, s32[4]{0:T(128)S(1)} %copy-done.3), kind=kOutput, calls=%fused_computation.3 | convolution fusion | flops 51380240 | bytes 8388624 | tf_op jit(solution)/shard_map/dg,dwq->gwq/dot_general | solution.py:89
  218.6 4.4 %copy.12 = f32[4,64,4096]{2,1,0:T(8,128)} copy(f32[4,64,4096]{2,0,1:T(4,128)S(1)} %convolution_multiply_fusion) | data formatting | bytes 8388608
  223.1 0.2 fusion.21
  223.3 1.2 fusion.8
  224.5 13.2 %reduce-scatter.2.cloned.1.call-done = f32[128,4096]{1,0:T(8,128)} async-done(((f32[512,4096]{1,0:T(8,128)}), f32[128,4096]{1,0:T(8,128)}) %reduce-scatter.2.cloned.1.call-update) | async-done | bytes 2097168 | tf_op jit(solution)/shard_map/reduce_scatter | solution.py:56
  237.6 3.0 %fusion.1 = bf16[128,4096]{1,0:T(8,128)(2,1)} fusion(f32[128,4096]{1,0:T(8,128)} %reduce-scatter.2.cloned.1.call-done, bf16[4,64,4096]{2,1,0:T(8,128)(2,1)S(1)} %copy-done, s32[]{:T(128)} %bitcast.8, bf16[4,128,64]{1,2,0:T(8,128)(2,1)S(1)} %broadcast_multiply_fusion, s32[]{:T(128)S(6)} %select_n.21), kind=kOutput, calls=%fused_computation.6 | convolution fusion | flops 68681728 | bytes 3686408 | tf_op jit(solution)/shard_map/azs,asg->azg/dot_general | solution.py:68
  (25 shorter events, 0.3 us)
Async XLA Ops:
  7.2 174.6 %copy-start = (bf16[4,64,4096]{2,1,0:T(8,128)(2,1)S(1)}, bf16[4,64,4096]{2,1,0:T(8,128)(2,1)}, u32[]{:S(2)}) copy-start(bf16[4,64,4096]{2,1,0:T(8,128)(2,1)} %param.12) | copy-start | bytes 6291460
  7.2 1.6 copy-start.3
  7.2 1.6 copy-start.4
  7.2 1.6 copy-start.5
  7.2 120.5 %all-gather.3.cloned.1.call-start = ((), (), s32[]{:S(2)}) async-start(), calls=%async_computation.1 | async-start | bytes 7864320 | tf_op jit(solution)/shard_map/all_gather | solution.py:48
  7.9 175.9 %all-gather.5.cloned.1.call-start = ((), (), s32[]{:S(2)}) async-start(), calls=%async_computation.3 | async-start | bytes 5242880 | tf_op jit(solution)/shard_map/all_gather | solution.py:77
  8.7 228.9 %reduce-scatter.2.cloned.1.call-start = ((), (), s32[]{:S(2)}) async-start(), calls=%async_computation.2 | async-start | bytes 10485760 | tf_op jit(solution)/shard_map/reduce_scatter | solution.py:56
  149.7 1.9 copy-start.2
  218.6 4.6 %copy-start.1 = (bf16[384,2048]{1,0:T(8,128)(2,1)S(1)}, bf16[384,2048]{1,0:T(8,128)(2,1)}, u32[]{:S(2)}) copy-start(bf16[384,2048]{1,0:T(8,128)(2,1)} %param.8) | copy-start | bytes 4718596
Sparse Core Ops, SparseCore 0:
  9.6 118.0 all-gather.2
  129.3 33.2 all-gather.4
  165.1 72.4 reduce-scatter.1
where the time goes:
time: 248 us; the launch traced here: 247 us
  waiting for transfers between devices  133 us (54%)
  blocking collectives  48 us (19%)
  matrix products  35.1 us (14%)
  between operations  15.9 us (6%)
  local copies, waits for them, and re-layouts  12.5 us (5%)
    all_gather x1, waiting for transfers between devices, per_device(): lax.all_gather(rows_per_slot, 'dp', axis=0, tiled=True)  119 us
    psum x1, blocking collectives, per_device(): returned_rows = lax.psum(partial_back, 'dp').astype(jnp.bfloat16)  21.2 us
    dot_general x1, matrix products, per_device(): jnp.dot(flat_rows, frozen_up_weight, preferred_element_type=jnp.float32)  15.2 us
    all_gather x1, blocking collectives, per_device(): lax.all_gather(lowered, 'dp', axis=0, tiled=True)  13.6 us
    psum x1, blocking collectives, per_device(): lowered = lax.psum(partial_low, 'tensor').astype(jnp.bfloat16)  13.2 us
    reduce_scatter x1, waiting for transfers between devices, per_device(): lax.psum_scatter(jnp.dot(flat_rows, frozen_up_weight, preferred_element_t...  13.2 us
    dot_general x1, matrix products, per_device(): jnp.einsum('dg,dwq->gwq', membership_mask, pieces, precision=lax.Precisio...  6.21 us
  transfers between devices with their start and end apart: 3, of which 2 were waited for; matrix products, arithmetic and copies ran while one was open for 19% of the time, Pallas kernels for 0%

commit v1 on v0

v1 whole, which is shorter than its diff:
```python
import functools

import jax
import jax.numpy as jnp
from jax import lax
from jax.experimental import pallas as pl
from jax.experimental.pallas import tpu as pltpu
from jax.sharding import PartitionSpec as P

BLK = 128
CAP = 3
CORES = 2
UNIT_ROWS = 64
SKEW = 1

adapter_scale = 0.5


def block_live(tokens_per_adapter, adapter_of_block, block_rows):
    adapter_count = tokens_per_adapter.shape[0]
    nblocks = (tokens_per_adapter + block_rows - 1) // block_rows
    first_block = jnp.cumsum(nblocks) - nblocks
    membership_mask = (
        adapter_of_block[:, None] == jnp.arange(adapter_count, dtype=jnp.int32)[None, :]
    ).astype(jnp.int32)
    begin_block = jnp.sum(membership_mask * first_block[None, :], axis=1)
    total_rows = jnp.sum(membership_mask * tokens_per_adapter[None, :], axis=1)
    block_place = jnp.arange(adapter_of_block.shape[0], dtype=jnp.int32) - begin_block
    offset = block_place[:, None] * block_rows + jnp.arange(block_rows, dtype=jnp.int32)[None, :]
    return offset < total_rows[:, None]


def split_product_kernel(x_ref, w_ref, send_ref, keep_ref):
    half = x_ref.shape[0] // 2
    total = jnp.dot(x_ref[...], w_ref[...], preferred_element_type=jnp.float32)
    send_ref[...] = total[:half].astype(send_ref.dtype)
    keep_ref[...] = total[half:]


def split_product(rows, weight):
    count, depth = rows.shape
    width = weight.shape[1]
    tile = 512
    return pl.pallas_call(
        split_product_kernel,
        grid=(width // tile,),
        in_specs=[
            pl.BlockSpec((count, depth), lambda n: (0, 0)),
            pl.BlockSpec((depth, tile), lambda n: (0, n)),
        ],
        out_specs=[
            pl.BlockSpec((count // 2, tile), lambda n: (0, n)),
            pl.BlockSpec((count // 2, tile), lambda n: (0, n)),
        ],
        out_shape=[
            jax.ShapeDtypeStruct((count // 2, width), jnp.bfloat16),
            jax.ShapeDtypeStruct((count // 2, width), jnp.float32),
        ],
        compiler_params=pltpu.CompilerParams(vmem_limit_bytes=24 * 2**20),
        cost_estimate=pl.CostEstimate(
            flops=2 * count * depth * width,
            bytes_accessed=2 * (count * depth + depth * width) + 3 * count * width,
            transcendentals=0,
        ),
        name="split_product",
    )(rows, weight)


def per_device(
    tokens,
    cotangent,
    frozen_up_weight,
    adapter_down_factor,
    adapter_up_factor,
    tokens_per_adapter,
    adapter_of_block,
    slot_of_block,
):
    owners = lax.axis_size("dp")
    parts = lax.axis_size("tensor")
    chips = parts // CORES
    place = lax.axis_index("dp")
    part = lax.axis_index("tensor")
    chip, core = part // CORES, part % CORES
    block_count = adapter_of_block.shape[0]
    per_part = block_count // parts
    width_dev = tokens.shape[1]
    hidden_dev = cotangent.shape[1]
    rank = adapter_up_factor.shape[1]
    adapter_count = adapter_up_factor.shape[0]

    def to_other_core(value):
        return lax.ppermute(value, "tensor", [(i, i ^ 1) for i in range(parts)])

    def to_chip(value, k):
        return lax.ppermute(value, "tensor", [(i, i ^ (k * CORES)) for i in range(parts)])

    def across_dp(value, k):
        return lax.ppermute(value, "dp", [(i, i ^ k) for i in range(owners)])

    rel_core = jnp.arange(CORES, dtype=jnp.int32)[:, None, None]
    rel_chip = jnp.arange(chips, dtype=jnp.int32)[None, :, None]
    rel_block = jnp.arange(per_part, dtype=jnp.int32)[None, None, :]
    block_rel = ((chip ^ rel_chip) * CORES + (core ^ rel_core)) * per_part + rel_block
    owner_rel = adapter_of_block[block_rel]
    slot_rel = slot_of_block[block_rel]
    mine_rel = owner_rel == place
    live = block_live(tokens_per_adapter, adapter_of_block, BLK)
    keep_here = lax.dynamic_slice_in_dim(live, part * per_part, per_part, 0)[:, :, None]
    adapter_here = lax.dynamic_slice_in_dim(adapter_of_block, part * per_part, per_part, 0)

    units_per_chunk = parts * per_part
    chunks = BLK // UNIT_ROWS
    units = chunks * units_per_chunk
    order = jnp.flip(owner_rel, 0).reshape(-1), jnp.flip(slot_rel, 0).reshape(-1)
    unit_owner = jnp.tile(order[0], chunks)
    unit_start = jnp.tile(order[1], chunks) * BLK + jnp.repeat(
        jnp.arange(chunks, dtype=jnp.int32) * UNIT_ROWS, units_per_chunk
    )

    def own_rows(unit):
        return lax.dynamic_slice(tokens, (unit_start[unit], 0), (UNIT_ROWS, width_dev))

    def relay(step_in_line, perm):
        arrived = []
        for step in range(units + SKEW * (owners - 2)):
            unit = jnp.clip(step - SKEW * step_in_line, 0, units - 1)
            value = own_rows(unit)
            if step >= SKEW:
                value = jnp.where(unit_owner[unit] == place, value, arrived[step - SKEW])
            arrived.append(lax.ppermute(value, "dp", perm))
        return arrived

    down_line = relay(owners - 1 - place, [(i, i - 1) for i in range(1, owners)])
    up_line = relay(place, [(i, i + 1) for i in range(owners - 1)])

    def unit_rows(unit):
        value = own_rows(unit)
        above = down_line[unit]
        below = up_line[unit]
        for hop in range(1, owners - 1):
            above = jnp.where(place == owners - 2 - hop, down_line[unit + SKEW * hop], above)
            below = jnp.where(place == 1 + hop, up_line[unit + SKEW * hop], below)
        owner = unit_owner[unit]
        return jnp.where(owner == place, value, jnp.where(owner > place, above, below))

    rows_per_slot = tokens.reshape(CAP, BLK, width_dev)
    partial_low = jnp.einsum(
        "mgh,hx->mgx", rows_per_slot, adapter_down_factor[0], preferred_element_type=jnp.float32
    )
    in_slot = (
        slot_rel[..., None] == jnp.arange(CAP, dtype=jnp.int32)
    ) & mine_rel[..., None]
    low_rel = jnp.sum(
        jnp.where(in_slot[..., None, None], partial_low, 0.0), axis=3
    )
    low_chip = low_rel[0] + to_other_core(low_rel[1])
    low_part = low_chip[0]
    for k in range(1, chips):
        low_part = low_part + to_chip(low_chip[k], k)
    blocks_here = cotangent.reshape(per_part, BLK, hidden_dev)
    up_here = adapter_up_factor[adapter_here]
    partial_back = jnp.einsum(
        "bkf,brf->bkr", blocks_here, up_here, preferred_element_type=jnp.float32
    )
    both = jnp.concatenate([low_part, partial_back], axis=-1)
    k = 1
    while k < owners:
        both = both + across_dp(both, k)
        k *= 2
    both = jnp.where(keep_here, both, 0.0).astype(jnp.bfloat16)
    lowered, back_rows = both[..., :rank], both[..., rank:]

    def every_part(value):
        same_core = jnp.stack([value] + [to_chip(value, k) for k in range(1, chips)])
        return same_core, to_other_core(same_core)

    back_rel = jnp.stack(every_part(back_rows))
    back_slots = jnp.sum(
        jnp.where(in_slot[..., None, None], back_rel[:, :, :, None], 0), axis=(0, 1, 2)
    ).astype(jnp.bfloat16)
    down_gradient = adapter_scale * jnp.einsum(
        "skd,skr->dr", rows_per_slot, back_slots, preferred_element_type=jnp.float32
    )

    pieces = jnp.einsum(
        "bkr,bkf->brf", lowered, blocks_here, preferred_element_type=jnp.float32
    ).astype(jnp.bfloat16)
    pieces_rel = every_part(pieces)
    adapters = jnp.arange(adapter_count, dtype=jnp.int32)[:, None, None]

    def of_adapter(core_index, chip_index):
        total = None
        for i in range(per_part):
            piece = pieces_rel[core_index][chip_index, i].astype(jnp.float32)
            term = jnp.where(owner_rel[core_index, chip_index, i] == adapters, piece[None], 0.0)
            total = term if total is None else total + term
        return total

    level = [of_adapter(0, j) + of_adapter(1, j) for j in range(chips)]
    while len(level) > 1:
        level = [level[j] + level[j + 1] for j in range(0, len(level), 2)]
    up_gradient = adapter_scale * level[0]

    projected = []
    for chunk in range(chunks):
        first = chunk * units_per_chunk
        rows = jnp.concatenate([unit_rows(first + u) for u in range(units_per_chunk)], axis=0)
        send, keep = split_product(rows, frozen_up_weight)
        chip_sum = (keep + to_other_core(send).astype(jnp.float32)).reshape(
            chips, per_part, UNIT_ROWS, hidden_dev
        )
        low_chunk = lowered[:, chunk * UNIT_ROWS : (chunk + 1) * UNIT_ROWS]
        keep_chunk = keep_here[:, chunk * UNIT_ROWS : (chunk + 1) * UNIT_ROWS]
        total = chip_sum[0] + adapter_scale * jnp.einsum(
            "azs,asg->azg", low_chunk, up_here, preferred_element_type=jnp.float32
        )
        for k in range(1, chips):
            total = total + to_chip(chip_sum[k].astype(jnp.bfloat16), k).astype(jnp.float32)
        projected.append(jnp.where(keep_chunk, total, 0.0).astype(jnp.bfloat16))
    projected = jnp.concatenate(projected, axis=1).reshape(per_part * BLK, hidden_dev)
    return (projected, down_gradient[None], up_gradient)


def solution(mesh):
    return jax.shard_map(
        per_device,
        mesh=mesh,
        in_specs=(
            P(("groups", "dp"), "tensor"),
            P(("groups", "tensor"), "dp"),
            P("tensor", "dp"),
            P(("groups", "dp"), "tensor", None),
            P("groups", None, "dp"),
            P("groups"),
            P("groups"),
            P("groups"),
        ),
        out_specs=(
            P(("groups", "tensor"), "dp"),
            P(("groups", "dp"), "tensor", None),
            P("groups", None, "dp"),
        ),
        check_vma=False,
    )
```

time: 248 us -> 269 us (1.085)
  waiting for transfers between devices: 133 us -> 53.4 us
  starting transfers between devices: 0.11 us -> 73.9 us
  between operations: 15.9 us -> 77.4 us
  blocking collectives: 48 us -> 0 us
  matrix products: 35.1 us -> 5.45 us
  other arithmetic: 2.37 us -> 27 us
  Pallas kernels: 0 us -> 14.6 us
    all_gather x2 -> x0, waiting for transfers between devices: 119 us -> none  [the longest x1 119 us: per_device(): lax.all_gather(rows_per_slot, 'dp', axis=0, tiled=True)]
    ppermute x0 -> x32, starting transfers between devices: none -> 73.9 us  [the longest x20 59.1 us: relay(): arrived.append(lax.ppermute(value, 'dp', perm))]
    ppermute x0 -> x32, waiting for transfers between devices: none -> 53.4 us  [the longest x20 35 us: relay(): arrived.append(lax.ppermute(value, 'dp', perm))]
    psum x2 -> x0, blocking collectives: 34.4 us -> none  [the longest x1 21.2 us: per_device(): returned_rows = lax.psum(partial_back, 'dp').astype(jnp.bfloat16)]
    dot_general x6 -> x4, matrix products: 31.9 us -> 2.23 us  [the longest x1 1.09 us: per_device(): jnp.einsum('bkf,brf->bkr', blocks_here, up_here, preferred_element_type=j...]
    pallas_call x0 -> x2, Pallas kernels: none -> 14.6 us  [split_product(): pl.pallas_call(split_product_kernel, grid=(width // tile,), in_specs=[pl....]
    all_gather x1 -> x0, blocking collectives: 13.6 us -> none  [per_device(): lax.all_gather(lowered, 'dp', axis=0, tiled=True)]
    reduce_scatter x1 -> x0, waiting for transfers between devices: 13.2 us -> none  [per_device(): lax.psum_scatter(jnp.dot(flat_rows, frozen_up_weight, preferred_element_t...]
  transfers between devices with their start and end apart: 3 -> 32, of which waited for: 2 -> 20; matrix products, arithmetic and copies ran while one was open for 19% -> 14% of each run, Pallas kernels for 0% -> 5%
where the time goes in v1:
time: 269 us; the launch traced here: 266 us
  between operations  77.4 us (29%)
  starting transfers between devices  73.9 us (27%)
  waiting for transfers between devices  53.4 us (20%)
  other arithmetic  27 us (10%)
  local copies, waits for them, and re-layouts  14.6 us (5%)
  Pallas kernels  14.6 us (5%)
  matrix products  5.45 us (2%)
    ppermute x20, starting transfers between devices, relay(): arrived.append(lax.ppermute(value, 'dp', perm))  59.1 us
    ppermute x20, waiting for transfers between devices, relay(): arrived.append(lax.ppermute(value, 'dp', perm))  35 us
    ppermute x5, waiting for transfers between devices, to_chip(): lax.ppermute(value, 'tensor', [(i, i ^ k * CORES) for i in range(parts)])  17.7 us
    pallas_call x2, Pallas kernels, split_product(): pl.pallas_call(split_product_kernel, grid=(width // tile,), in_specs=[pl....  14.6 us
    select_n x12, other arithmetic, relay(): value = jnp.where(unit_owner[unit] == place, value, arrived[step - SKEW])  8.38 us
    ppermute x5, starting transfers between devices, to_chip(): lax.ppermute(value, 'tensor', [(i, i ^ k * CORES) for i in range(parts)])  8.09 us
    ppermute x2, starting transfers between devices, across_dp(): return lax.ppermute(value, 'dp', [(i, i ^ k) for i in range(owners)])  5.93 us
  transfers between devices with their start and end apart: 32, of which 20 were waited for; matrix products, arithmetic and copies ran while one was open for 14% of the time, Pallas kernels for 5%

profile of v1, /device:TPU:0, one launch (start us, length us, event | category | flops | bytes accessed | tf_op | source)
XLA Modules:
  0.0 266.3 jit_solution(2177463912182908434)
XLA Ops:
  28.5 2.5 collective-permute-start.14
  35.7 2.6 collective-permute-start.15
  45.4 3.3 %collective-permute-start.16 = (f32[1,128,128]{1,2,0:T(8,128)S(1)}, f32[1,128,128]{1,2,0:T(8,128)}, u32[]{:S(2)}, u32[]{:S(2)}) collective-permute-start(f32[1,128,128]{1,2,0:T(8,128)S(1)} %fusion.34), channel_id=1, source_target_pairs={{0,8},{4,12},{8,0},{12,4},{1,9},{5,13},{9,1},{13,5},{2,10},{6,14},... | collective-permute-start | bytes 196616 | tf_op jit(solution)/shard_map/ppermute | solution.py:99
  59.5 2.3 collective-permute-done.2
  63.8 4.4 %collective-permute-start.3 = (bf16[64,2048]{1,0:T(8,128)(2,1)}, bf16[64,2048]{1,0:T(8,128)(2,1)}, u32[]{:S(2)}, u32[]{:S(2)}) collective-permute-start(bf16[64,2048]{1,0:T(8,128)(2,1)} %get-tuple-element.45), channel_id=1, source_target_pairs={{0,4},{4,8},{8,12},{1,5},{5,9},{9,13},{2,6},{6,10},{10,14},{3,7},{... | collective-permute-start | bytes 786440 | tf_op jit(solution)/shard_map/ppermute | solution.py:131
  133.5 2.6 collective-permute-start.4
  139.4 2.7 %collective-permute-done.4 = bf16[64,2048]{1,0:T(8,128)(2,1)S(1)} collective-permute-done((bf16[64,2048]{1,0:T(8,128)(2,1)S(1)}, bf16[64,2048]{1,0:T(8,128)(2,1)S(1)}, u32[]{:S(2)}, u32[]{:S(2)}) %collective-permute-start.4) | collective-permute-done | bytes 262176 | tf_op jit(solution)/shard_map/ppermute | solution.py:131
  142.3 4.4 %collective-permute-start.5 = (bf16[64,2048]{1,0:T(8,128)(2,1)S(1)}, bf16[64,2048]{1,0:T(8,128)(2,1)S(1)}, u32[]{:S(2)}, u32[]{:S(2)}) collective-permute-start(bf16[64,2048]{1,0:T(8,128)(2,1)S(1)} %dynamic-slice_select_fusion.15), channel_id=1, source_target_pairs={{0,4},{4,8},{8,12},{1,5},{5,9},{9,13},{2,6},{6,10},{10,14},{3,7},{... | collective-permute-start | bytes 786440 | tf_op jit(solution)/shard_map/ppermute | solution.py:131
  148.1 3.9 %collective-permute-done.5 = bf16[64,2048]{1,0:T(8,128)(2,1)S(1)} collective-permute-done((bf16[64,2048]{1,0:T(8,128)(2,1)S(1)}, bf16[64,2048]{1,0:T(8,128)(2,1)S(1)}, u32[]{:S(2)}, u32[]{:S(2)}) %collective-permute-start.5) | collective-permute-done | bytes 262176 | tf_op jit(solution)/shard_map/ppermute | solution.py:131
  153.4 5.0 %collective-permute-start.7 = (bf16[64,2048]{1,0:T(8,128)(2,1)S(1)}, bf16[64,2048]{1,0:T(8,128)(2,1)S(1)}, u32[]{:S(2)}, u32[]{:S(2)}) collective-permute-start(bf16[64,2048]{1,0:T(8,128)(2,1)S(1)} %get-tuple-element.43), channel_id=1, source_target_pairs={{0,4},{4,8},{8,12},{1,5},{5,9},{9,13},{2,6},{6,10},{10,14},{3,7},{... | collective-permute-start | bytes 786440 | tf_op jit(solution)/shard_map/ppermute | solution.py:131
  158.7 3.0 %collective-permute-done.8 = bf16[64,2048]{1,0:T(8,128)(2,1)S(1)} collective-permute-done((bf16[64,2048]{1,0:T(8,128)(2,1)S(1)}, bf16[64,2048]{1,0:T(8,128)(2,1)S(1)}, u32[]{:S(2)}, u32[]{:S(2)}) %collective-permute-start.8) | collective-permute-done | bytes 262176 | tf_op jit(solution)/shard_map/ppermute | solution.py:131
  164.3 5.0 %collective-permute-start.9 = (bf16[64,2048]{1,0:T(8,128)(2,1)S(1)}, bf16[64,2048]{1,0:T(8,128)(2,1)S(1)}, u32[]{:S(2)}, u32[]{:S(2)}) collective-permute-start(bf16[64,2048]{1,0:T(8,128)(2,1)S(1)} %get-tuple-element.41), channel_id=1, source_target_pairs={{0,4},{4,8},{8,12},{1,5},{5,9},{9,13},{2,6},{6,10},{10,14},{3,7},{... | collective-permute-start | bytes 786440 | tf_op jit(solution)/shard_map/ppermute | solution.py:131
  174.7 5.3 %collective-permute-start.11 = (bf16[64,2048]{1,0:T(8,128)(2,1)S(1)}, bf16[64,2048]{1,0:T(8,128)(2,1)S(1)}, u32[]{:S(2)}, u32[]{:S(2)}) collective-permute-start(bf16[64,2048]{1,0:T(8,128)(2,1)S(1)} %get-tuple-element.39), channel_id=1, source_target_pairs={{0,4},{4,8},{8,12},{1,5},{5,9},{9,13},{2,6},{6,10},{10,14},{3,7},{... | collective-permute-start | bytes 786440 | tf_op jit(solution)/shard_map/ppermute | solution.py:131
  185.4 5.0 %collective-permute-start.19 = (bf16[64,2048]{1,0:T(8,128)(2,1)S(1)}, bf16[64,2048]{1,0:T(8,128)(2,1)S(1)}, u32[]{:S(2)}, u32[]{:S(2)}) collective-permute-start(bf16[64,2048]{1,0:T(8,128)(2,1)S(1)} %get-tuple-element.37), channel_id=1, source_target_pairs={{0,4},{4,8},{8,12},{1,5},{5,9},{9,13},{2,6},{6,10},{10,14},{3,7},{... | collective-permute-start | bytes 786440 | tf_op jit(solution)/shard_map/ppermute | solution.py:131
  195.8 5.0 %collective-permute-start.21 = (bf16[64,2048]{1,0:T(8,128)(2,1)S(1)}, bf16[64,2048]{1,0:T(8,128)(2,1)S(1)}, u32[]{:S(2)}, u32[]{:S(2)}) collective-permute-start(bf16[64,2048]{1,0:T(8,128)(2,1)S(1)} %get-tuple-element.35), channel_id=1, source_target_pairs={{0,4},{4,8},{8,12},{1,5},{5,9},{9,13},{2,6},{6,10},{10,14},{3,7},{... | collective-permute-start | bytes 786440 | tf_op jit(solution)/shard_map/ppermute | solution.py:131
  203.2 3.0 %collective-permute-done.21 = bf16[64,2048]{1,0:T(8,128)(2,1)S(1)} collective-permute-done((bf16[64,2048]{1,0:T(8,128)(2,1)S(1)}, bf16[64,2048]{1,0:T(8,128)(2,1)S(1)}, u32[]{:S(2)}, u32[]{:S(2)}) %collective-permute-start.21) | collective-permute-done | bytes 262176 | tf_op jit(solution)/shard_map/ppermute | solution.py:131
  206.5 4.4 %collective-permute-start.23 = (bf16[64,2048]{1,0:T(8,128)(2,1)S(1)}, bf16[64,2048]{1,0:T(8,128)(2,1)S(1)}, u32[]{:S(2)}, u32[]{:S(2)}) collective-permute-start(bf16[64,2048]{1,0:T(8,128)(2,1)S(1)} %get-tuple-element.33), channel_id=1, source_target_pairs={{0,4},{4,8},{8,12},{1,5},{5,9},{9,13},{2,6},{6,10},{10,14},{3,7},{... | collective-permute-start | bytes 786440 | tf_op jit(solution)/shard_map/ppermute | solution.py:131
  210.9 7.4 %split_product.2 = (bf16[128,4096]{1,0:T(8,128)(2,1)S(1)}, f32[128,4096]{1,0:T(8,128)S(1)}) custom-call(bf16[256,2048]{1,0:T(8,128)(2,1)S(1)} %pad_maximum_fusion.x_ref, bf16[2048,4096]{1,0:T(8,128)(2,1)S(1)} %bitcast.188), custom_call_target="tpu_custom_call" | custom-call | flops 4294967296 | bytes 20971520 | tf_op jit(solution)/shard_map/split_product/pallas_call | solution.py:44
  219.8 5.1 %collective-permute-start.25 = (bf16[64,2048]{1,0:T(8,128)(2,1)S(1)}, bf16[64,2048]{1,0:T(8,128)(2,1)S(1)}, u32[]{:S(2)}, u32[]{:S(2)}) collective-permute-start(bf16[64,2048]{1,0:T(8,128)(2,1)S(1)} %dynamic-slice_select_fusion), channel_id=1, source_target_pairs={{0,4},{4,8},{8,12},{1,5},{5,9},{9,13},{2,6},{6,10},{10,14},{3,7},{... | collective-permute-start | bytes 786440 | tf_op jit(solution)/shard_map/ppermute | solution.py:131
  225.4 4.2 %collective-permute-done.24 = bf16[64,2048]{1,0:T(8,128)(2,1)S(1)} collective-permute-done((bf16[64,2048]{1,0:T(8,128)(2,1)S(1)}, bf16[64,2048]{1,0:T(8,128)(2,1)S(1)}, u32[]{:S(2)}, u32[]{:S(2)}) %collective-permute-start.24) | collective-permute-done | bytes 262176 | tf_op jit(solution)/shard_map/ppermute | solution.py:131
  231.5 7.2 %split_product.3 = (bf16[128,4096]{1,0:T(8,128)(2,1)S(1)}, f32[128,4096]{1,0:T(8,128)S(1)}) custom-call(bf16[256,2048]{1,0:T(8,128)(2,1)S(1)} %pad_maximum_fusion.1.x_ref, bf16[2048,4096]{1,0:T(8,128)(2,1)S(1)} %bitcast.188), custom_call_target="tpu_custom_call" | custom-call | flops 4294967296 | bytes 20971520 | tf_op jit(solution)/shard_map/split_product/pallas_call | solution.py:44
  243.4 3.2 %add_multiply_fusion = f32[4,64,4096]{2,1,0:T(8,128)} fusion(f32[64,4096]{1,0:T(8,128)S(1)} %get-tuple-element.47, f32[64,4096]{1,0:T(8,128)S(1)} %bitcast_convert_fusion, f32[64,4096]{1,0:T(8,128)S(1)} %get-tuple-element.46, f32[64,4096]{1,0:T(8,128)S(1)} %get-tuple-element.114, pred[4]{0:T(512)(128)(4,1)S(1)} %iota_compare_fusion.1, ...), kind=kLoop, calls=%fused_computation.5 | loop fusion | flops 8388608 | bytes 8388624 | tf_op jit(solution)/shard_map/mul | solution.py:203
  246.6 7.3 %collective-permute-done.17 = bf16[1,64,4096]{2,1,0:T(8,128)(2,1)S(1)} collective-permute-done((bf16[1,64,4096]{2,1,0:T(8,128)(2,1)S(1)}, bf16[1,64,4096]{2,1,0:T(8,128)(2,1)S(1)}, u32[]{:S(2)}, u32[]{:S(2)}) %collective-permute-start.17) | collective-permute-done | bytes 524320 | tf_op jit(solution)/shard_map/ppermute | solution.py:96
  254.3 10.4 %collective-permute-done.27 = bf16[1,64,4096]{2,1,0:T(8,128)(2,1)S(1)} collective-permute-done((bf16[1,64,4096]{2,1,0:T(8,128)(2,1)S(1)}, bf16[1,64,4096]{2,1,0:T(8,128)(2,1)S(1)}, u32[]{:S(2)}, u32[]{:S(2)}) %collective-permute-start.27) | collective-permute-done | bytes 524320 | tf_op jit(solution)/shard_map/ppermute | solution.py:96
  (160 shorter events, 79.6 us)
Async XLA Ops:
  6.9 31.4 %collective-permute-start = (bf16[64,2048]{1,0:T(8,128)(2,1)}, bf16[64,2048]{1,0:T(8,128)(2,1)S(1)}, u32[]{:S(2)}, u32[]{:S(2)}) collective-permute-start(bf16[64,2048]{1,0:T(8,128)(2,1)} %constant_dynamic-slice_fusion.1), channel_id=1, source_target_pairs={{4,0},{8,4},{12,8},{5,1},{9,5},{13,9},{6,2},{10,6},{14,10},{7,3},{... | collective-permute-start | bytes 786440 | tf_op jit(solution)/shard_map/ppermute | solution.py:131
  11.9 15.2 %collective-permute-start.13 = (f32[2,1,128,64]{2,3,1,0:T(8,128)}, f32[2,1,128,64]{2,3,1,0:T(8,128)}, u32[]{:S(2)}, u32[]{:S(2)}) collective-permute-start(f32[2,1,128,64]{2,3,1,0:T(8,128)} %slice_bitcast_fusion.2), channel_id=1, source_target_pairs={{0,1},{1,0},{2,3},{3,2},{4,5},{5,4},{6,7},{7,6},{8,9},{9,8},{10,11... | collective-permute-start | bytes 196616 | tf_op jit(solution)/shard_map/ppermute | solution.py:93
  35.7 8.9 %collective-permute-start.15 = (f32[1,128,128]{1,2,0:T(8,128)S(1)}, f32[1,128,128]{1,2,0:T(8,128)}, u32[]{:S(2)}, u32[]{:S(2)}) collective-permute-start(f32[1,128,128]{1,2,0:T(8,128)S(1)} %pad_maximum_fusion.3), channel_id=1, source_target_pairs={{0,4},{4,0},{8,12},{12,8},{1,5},{5,1},{9,13},{13,9},{2,6},{6,2},{1... | collective-permute-start | bytes 196616 | tf_op jit(solution)/shard_map/ppermute | solution.py:99
  40.2 10.4 %collective-permute-start.1 = (bf16[64,2048]{1,0:T(8,128)(2,1)}, bf16[64,2048]{1,0:T(8,128)(2,1)}, u32[]{:S(2)}, u32[]{:S(2)}) collective-permute-start(bf16[64,2048]{1,0:T(8,128)(2,1)} %dynamic-slice_select_fusion.16), channel_id=1, source_target_pairs={{4,0},{8,4},{12,8},{5,1},{9,5},{13,9},{6,2},{10,6},{14,10},{7,3},{... | collective-permute-start | bytes 786440 | tf_op jit(solution)/shard_map/ppermute | solution.py:131
  45.4 13.2 %collective-permute-start.16 = (f32[1,128,128]{1,2,0:T(8,128)S(1)}, f32[1,128,128]{1,2,0:T(8,128)}, u32[]{:S(2)}, u32[]{:S(2)}) collective-permute-start(f32[1,128,128]{1,2,0:T(8,128)S(1)} %fusion.34), channel_id=1, source_target_pairs={{0,8},{4,12},{8,0},{12,4},{1,9},{5,13},{9,1},{13,5},{2,10},{6,14},... | collective-permute-start | bytes 196616 | tf_op jit(solution)/shard_map/ppermute | solution.py:99
  52.4 9.4 %collective-permute-start.2 = (bf16[64,2048]{1,0:T(8,128)(2,1)}, bf16[64,2048]{1,0:T(8,128)(2,1)S(1)}, u32[]{:S(2)}, u32[]{:S(2)}) collective-permute-start(bf16[64,2048]{1,0:T(8,128)(2,1)} %dynamic-slice_select_fusion.17), channel_id=1, source_target_pairs={{4,0},{8,4},{12,8},{5,1},{9,5},{13,9},{6,2},{10,6},{14,10},{7,3},{... | collective-permute-start | bytes 786440 | tf_op jit(solution)/shard_map/ppermute | solution.py:131
  63.8 68.4 %collective-permute-start.3 = (bf16[64,2048]{1,0:T(8,128)(2,1)}, bf16[64,2048]{1,0:T(8,128)(2,1)}, u32[]{:S(2)}, u32[]{:S(2)}) collective-permute-start(bf16[64,2048]{1,0:T(8,128)(2,1)} %get-tuple-element.45), channel_id=1, source_target_pairs={{0,4},{4,8},{8,12},{1,5},{5,9},{9,13},{2,6},{6,10},{10,14},{3,7},{... | collective-permute-start | bytes 786440 | tf_op jit(solution)/shard_map/ppermute | solution.py:131
  68.2 64.0 %collective-permute-start.28 = (bf16[1,128,64]{1,2,0:T(8,128)(2,1)S(1)}, bf16[1,128,64]{1,2,0:T(8,128)(2,1)S(1)}, u32[]{:S(2)}, u32[]{:S(2)}) collective-permute-start(bf16[1,128,64]{1,2,0:T(8,128)(2,1)S(1)} %get-tuple-element.51), channel_id=1, source_target_pairs={{0,2},{1,3},{2,0},{3,1},{4,6},{5,7},{6,4},{7,5},{8,10},{9,11},{10,... | collective-permute-start | bytes 49160 | tf_op jit(solution)/shard_map/ppermute | solution.py:96
  136.4 22.1 %collective-permute-start.30 = (bf16[1,64,4096]{2,1,0:T(8,128)(2,1)S(1)}, bf16[1,64,4096]{2,1,0:T(8,128)(2,1)S(1)}, u32[]{:S(2)}, u32[]{:S(2)}) collective-permute-start(bf16[1,64,4096]{2,1,0:T(8,128)(2,1)S(1)} %bitcast.192), channel_id=1, source_target_pairs={{0,2},{1,3},{2,0},{3,1},{4,6},{5,7},{6,4},{7,5},{8,10},{9,11},{10,... | collective-permute-start | bytes 1572872 | tf_op jit(solution)/shard_map/ppermute | solution.py:96
  138.1 9.9 %collective-permute-start.6 = (bf16[64,2048]{1,0:T(8,128)(2,1)S(1)}, bf16[64,2048]{1,0:T(8,128)(2,1)S(1)}, u32[]{:S(2)}, u32[]{:S(2)}) collective-permute-start(bf16[64,2048]{1,0:T(8,128)(2,1)S(1)} %copy-done.7), channel_id=1, source_target_pairs={{4,0},{8,4},{12,8},{5,1},{9,5},{13,9},{6,2},{10,6},{14,10},{7,3},{... | collective-permute-start | bytes 786440 | tf_op jit(solution)/shard_map/ppermute | solution.py:131
  142.3 9.7 %collective-permute-start.5 = (bf16[64,2048]{1,0:T(8,128)(2,1)S(1)}, bf16[64,2048]{1,0:T(8,128)(2,1)S(1)}, u32[]{:S(2)}, u32[]{:S(2)}) collective-permute-start(bf16[64,2048]{1,0:T(8,128)(2,1)S(1)} %dynamic-slice_select_fusion.15), channel_id=1, source_target_pairs={{0,4},{4,8},{8,12},{1,5},{5,9},{9,13},{2,6},{6,10},{10,14},{3,7},{... | collective-permute-start | bytes 786440 | tf_op jit(solution)/shard_map/ppermute | solution.py:131
  152.1 9.5 %collective-permute-start.8 = (bf16[64,2048]{1,0:T(8,128)(2,1)S(1)}, bf16[64,2048]{1,0:T(8,128)(2,1)S(1)}, u32[]{:S(2)}, u32[]{:S(2)}) collective-permute-start(bf16[64,2048]{1,0:T(8,128)(2,1)S(1)} %get-tuple-element.42), channel_id=1, source_target_pairs={{4,0},{8,4},{12,8},{5,1},{9,5},{13,9},{6,2},{10,6},{14,10},{7,3},{... | collective-permute-start | bytes 786440 | tf_op jit(solution)/shard_map/ppermute | solution.py:131
  153.4 9.4 %collective-permute-start.7 = (bf16[64,2048]{1,0:T(8,128)(2,1)S(1)}, bf16[64,2048]{1,0:T(8,128)(2,1)S(1)}, u32[]{:S(2)}, u32[]{:S(2)}) collective-permute-start(bf16[64,2048]{1,0:T(8,128)(2,1)S(1)} %get-tuple-element.43), channel_id=1, source_target_pairs={{0,4},{4,8},{8,12},{1,5},{5,9},{9,13},{2,6},{6,10},{10,14},{3,7},{... | collective-permute-start | bytes 786440 | tf_op jit(solution)/shard_map/ppermute | solution.py:131
  158.6 21.4 %collective-permute-start.31 = (bf16[2,1,64,4096]{3,2,1,0:T(8,128)(2,1)S(1)}, bf16[2,1,64,4096]{3,2,1,0:T(8,128)(2,1)S(1)}, u32[]{:S(2)}, u32[]{:S(2)}) collective-permute-start(bf16[2,1,64,4096]{3,2,1,0:T(8,128)(2,1)S(1)} %pad_maximum_fusion.2), channel_id=1, source_target_pairs={{0,1},{1,0},{2,3},{3,2},{4,5},{5,4},{6,7},{7,6},{8,9},{9,8},{10,11... | collective-permute-start | bytes 3145736 | tf_op jit(solution)/shard_map/ppermute | solution.py:93
  164.3 8.9 %collective-permute-start.9 = (bf16[64,2048]{1,0:T(8,128)(2,1)S(1)}, bf16[64,2048]{1,0:T(8,128)(2,1)S(1)}, u32[]{:S(2)}, u32[]{:S(2)}) collective-permute-start(bf16[64,2048]{1,0:T(8,128)(2,1)S(1)} %get-tuple-element.41), channel_id=1, source_target_pairs={{0,4},{4,8},{8,12},{1,5},{5,9},{9,13},{2,6},{6,10},{10,14},{3,7},{... | collective-permute-start | bytes 786440 | tf_op jit(solution)/shard_map/ppermute | solution.py:131
  174.7 9.2 %collective-permute-start.11 = (bf16[64,2048]{1,0:T(8,128)(2,1)S(1)}, bf16[64,2048]{1,0:T(8,128)(2,1)S(1)}, u32[]{:S(2)}, u32[]{:S(2)}) collective-permute-start(bf16[64,2048]{1,0:T(8,128)(2,1)S(1)} %get-tuple-element.39), channel_id=1, source_target_pairs={{0,4},{4,8},{8,12},{1,5},{5,9},{9,13},{2,6},{6,10},{10,14},{3,7},{... | collective-permute-start | bytes 786440 | tf_op jit(solution)/shard_map/ppermute | solution.py:131
  185.4 8.9 %collective-permute-start.19 = (bf16[64,2048]{1,0:T(8,128)(2,1)S(1)}, bf16[64,2048]{1,0:T(8,128)(2,1)S(1)}, u32[]{:S(2)}, u32[]{:S(2)}) collective-permute-start(bf16[64,2048]{1,0:T(8,128)(2,1)S(1)} %get-tuple-element.37), channel_id=1, source_target_pairs={{0,4},{4,8},{8,12},{1,5},{5,9},{9,13},{2,6},{6,10},{10,14},{3,7},{... | collective-permute-start | bytes 786440 | tf_op jit(solution)/shard_map/ppermute | solution.py:131
  195.8 10.5 %collective-permute-start.21 = (bf16[64,2048]{1,0:T(8,128)(2,1)S(1)}, bf16[64,2048]{1,0:T(8,128)(2,1)S(1)}, u32[]{:S(2)}, u32[]{:S(2)}) collective-permute-start(bf16[64,2048]{1,0:T(8,128)(2,1)S(1)} %get-tuple-element.35), channel_id=1, source_target_pairs={{0,4},{4,8},{8,12},{1,5},{5,9},{9,13},{2,6},{6,10},{10,14},{3,7},{... | collective-permute-start | bytes 786440 | tf_op jit(solution)/shard_map/ppermute | solution.py:131
  206.5 13.2 %collective-permute-start.23 = (bf16[64,2048]{1,0:T(8,128)(2,1)S(1)}, bf16[64,2048]{1,0:T(8,128)(2,1)S(1)}, u32[]{:S(2)}, u32[]{:S(2)}) collective-permute-start(bf16[64,2048]{1,0:T(8,128)(2,1)S(1)} %get-tuple-element.33), channel_id=1, source_target_pairs={{0,4},{4,8},{8,12},{1,5},{5,9},{9,13},{2,6},{6,10},{10,14},{3,7},{... | collective-permute-start | bytes 786440 | tf_op jit(solution)/shard_map/ppermute | solution.py:131
  218.3 20.5 %collective-permute-start.12 = (bf16[128,4096]{1,0:T(8,128)(2,1)S(1)}, bf16[128,4096]{1,0:T(8,128)(2,1)S(1)}, u32[]{:S(2)}, u32[]{:S(2)}) collective-permute-start(bf16[128,4096]{1,0:T(8,128)(2,1)S(1)} %get-tuple-element.8), channel_id=1, source_target_pairs={{0,1},{1,0},{2,3},{3,2},{4,5},{5,4},{6,7},{7,6},{8,9},{9,8},{10,11... | collective-permute-start | bytes 3145736 | tf_op jit(solution)/shard_map/ppermute | solution.py:93
  218.4 11.2 %collective-permute-start.24 = (bf16[64,2048]{1,0:T(8,128)(2,1)S(1)}, bf16[64,2048]{1,0:T(8,128)(2,1)S(1)}, u32[]{:S(2)}, u32[]{:S(2)}) collective-permute-start(bf16[64,2048]{1,0:T(8,128)(2,1)S(1)} %get-tuple-element.32), channel_id=1, source_target_pairs={{4,0},{8,4},{12,8},{5,1},{9,5},{13,9},{6,2},{10,6},{14,10},{7,3},{... | collective-permute-start | bytes 786440 | tf_op jit(solution)/shard_map/ppermute | solution.py:131
  219.8 11.1 %collective-permute-start.25 = (bf16[64,2048]{1,0:T(8,128)(2,1)S(1)}, bf16[64,2048]{1,0:T(8,128)(2,1)S(1)}, u32[]{:S(2)}, u32[]{:S(2)}) collective-permute-start(bf16[64,2048]{1,0:T(8,128)(2,1)S(1)} %dynamic-slice_select_fusion), channel_id=1, source_target_pairs={{0,4},{4,8},{8,12},{1,5},{5,9},{9,13},{2,6},{6,10},{10,14},{3,7},{... | collective-permute-start | bytes 786440 | tf_op jit(solution)/shard_map/ppermute | solution.py:131
  239.1 14.8 %collective-permute-start.17 = (bf16[1,64,4096]{2,1,0:T(8,128)(2,1)S(1)}, bf16[1,64,4096]{2,1,0:T(8,128)(2,1)S(1)}, u32[]{:S(2)}, u32[]{:S(2)}) collective-permute-start(bf16[1,64,4096]{2,1,0:T(8,128)(2,1)S(1)} %fusion.10), channel_id=1, source_target_pairs={{0,2},{1,3},{2,0},{3,1},{4,6},{5,7},{6,4},{7,5},{8,10},{9,11},{10,... | collective-permute-start | bytes 1572872 | tf_op jit(solution)/shard_map/ppermute | solution.py:96
  241.7 23.0 %collective-permute-start.27 = (bf16[1,64,4096]{2,1,0:T(8,128)(2,1)S(1)}, bf16[1,64,4096]{2,1,0:T(8,128)(2,1)S(1)}, u32[]{:S(2)}, u32[]{:S(2)}) collective-permute-start(bf16[1,64,4096]{2,1,0:T(8,128)(2,1)S(1)} %fusion.11), channel_id=1, source_target_pairs={{0,2},{1,3},{2,0},{3,1},{4,6},{5,7},{6,4},{7,5},{8,10},{9,11},{10,... | collective-permute-start | bytes 1572872 | tf_op jit(solution)/shard_map/ppermute | solution.py:96
  (24 other events, 400.0 us)

commit v2 on v0

v2 whole, which is shorter than its diff:
```python
import functools

import jax
import jax.numpy as jnp
from jax import lax
from jax.experimental import pallas as pl
from jax.experimental.pallas import tpu as pltpu
from jax.sharding import PartitionSpec as P

BLK = 128
CAP = 3
CORES = 2
CHUNK_ROWS = (64, 64)
MIB = 2**20

adapter_scale = 0.5

LAST = (((1,), (1,)), ((), ()))


class Index:
    def __init__(self, ref, block_count, adapter_count, parts):
        self.ref = ref
        self.blocks, self.adapters, self.parts = block_count, adapter_count, parts
        self.chips = parts // CORES
        self.per_part = block_count // parts

    @staticmethod
    def pack(adapter_of_block, slot_of_block, tokens_per_adapter):
        place = jnp.stack([lax.axis_index("dp"), lax.axis_index("tensor")]).astype(jnp.int32)
        return jnp.concatenate([adapter_of_block, slot_of_block, tokens_per_adapter, place])

    def owner(self, block):
        return self.ref[block]

    def slot(self, block):
        return self.ref[self.blocks + block]

    def tokens(self, adapter):
        return self.ref[2 * self.blocks + adapter]

    @property
    def place(self):
        return self.ref[2 * self.blocks + self.adapters]

    @property
    def part(self):
        return self.ref[2 * self.blocks + self.adapters + 1]

    def block(self, core_bit, chip_bits, i):
        return (self.part ^ (chip_bits * CORES + core_bit)) * self.per_part + i

    def live_rows(self, block):
        adapter = self.owner(block)
        first = jnp.int32(0)
        for a in range(self.adapters):
            count = (self.tokens(a) + BLK - 1) // BLK
            first = first + jnp.where(a < adapter, count, 0)
        return self.tokens(adapter) - (block - first) * BLK


def whole(shape):
    return pl.BlockSpec(shape, lambda *_: (0,) * len(shape))


def shape_of(shape, dtype):
    return jax.ShapeDtypeStruct(shape, dtype)


def cost(flops, bytes_accessed):
    return pl.CostEstimate(flops=flops, bytes_accessed=bytes_accessed, transcendentals=0)


def copy_all(copies):
    for copy in copies:
        copy.start()
    for copy in copies:
        copy.wait()


def first_hop_kernel(index_of, starts, rows, index_ref, tokens_ref, *refs):
    outs, sems = refs[:-1], refs[-1]
    index = index_of(index_ref)
    place = index.place
    inward = jnp.where(place == 0, 2, 1)
    copies = []
    for c, (start, count) in enumerate(zip(starts, rows)):
        for j, block in enumerate((inward, 0)):
            at = pl.multiple_of(index.slot(block) * BLK + start, 16)
            copies.append(
                pltpu.make_async_copy(
                    tokens_ref.at[pl.ds(at, count)], outs[2 * c + j], sems.at[2 * c + j]
                )
            )
    copy_all(copies)


def pick_copy(choices, out_ref, sem):
    for condition, source in choices:

        @pl.when(condition)
        def _(source=source):
            copy = pltpu.make_async_copy(source, out_ref, sem)
            copy.start()
            copy.wait()


def second_hop_kernel(index_of, start, count, index_ref, tokens_ref, a_ref, b_ref, x_ref, y_ref, sems):
    index = index_of(index_ref)
    place = index.place

    def own(block):
        at = pl.multiple_of(index.slot(block) * BLK + start, 16)
        return tokens_ref.at[pl.ds(at, count)]

    outer = jnp.where(place == 0, 1, jnp.where(place == 1, 0, 2))
    passed = (place == 1) & (index.owner(0) != 1)
    pick_copy(
        [(jnp.logical_not(passed), own(outer)), (passed, b_ref)], x_ref, sems.at[0]
    )
    middle = jnp.where(place == 1, 2, 1)
    passed = ((place == 1) | (place == 2)) & (index.owner(middle) != place)
    pick_copy(
        [(jnp.logical_not(passed), own(middle)), (passed, a_ref)], y_ref, sems.at[1]
    )


def settle_kernel(index_of, start, count, index_ref, tokens_ref, x_ref, y_ref, out_ref, sems):
    index = index_of(index_ref)
    place = index.place
    owner = index.owner(place)
    mine = owner == place
    edge = (place == 0) | ((place == 1) & (owner == 0)) | ((place == 2) & (owner == 3))
    at = pl.multiple_of(index.slot(place) * BLK + start, 16)
    pick_copy(
        [
            (mine, tokens_ref.at[pl.ds(at, count)]),
            (jnp.logical_not(mine) & edge, x_ref),
            (jnp.logical_not(mine | edge), y_ref),
        ],
        out_ref,
        sems.at[0],
    )


def blocks_at_home(index_of, index, tokens):
    width = tokens.shape[1]
    starts = [sum(CHUNK_ROWS[:c]) for c in range(len(CHUNK_ROWS))]
    hbm = pl.BlockSpec(memory_space=pl.ANY)

    def call(kernel, outs, copies, operands, name):
        return pl.pallas_call(
            kernel,
            grid_spec=pltpu.PrefetchScalarGridSpec(
                num_scalar_prefetch=1,
                grid=(),
                in_specs=[hbm] * len(operands),
                out_specs=[hbm] * len(outs),
                scratch_shapes=[pltpu.SemaphoreType.DMA((copies,))],
            ),
            out_shape=outs,
            cost_estimate=cost(0, 4 * sum(o.size for o in outs)),
            name=name,
        )(index, *operands)

    sends = call(
        functools.partial(first_hop_kernel, index_of, starts, CHUNK_ROWS),
        [shape_of((count, width), tokens.dtype) for count in CHUNK_ROWS for _ in range(2)],
        2 * len(CHUNK_ROWS),
        (tokens,),
        "first_hop",
    )
    homes = []
    for c, (start, count) in enumerate(zip(starts, CHUNK_ROWS)):
        unit = shape_of((count, width), tokens.dtype)
        inward = lax.ppermute(sends[2 * c], "dp", [(3, 2), (0, 1)])
        left = lax.ppermute(sends[2 * c + 1], "dp", [(2, 1)])
        outer, middle = call(
            functools.partial(second_hop_kernel, index_of, start, count),
            [unit, unit],
            2,
            (tokens, inward, left),
            "second_hop",
        )
        outer = lax.ppermute(outer, "dp", [(1, 0), (0, 1), (3, 2)])
        middle = lax.ppermute(middle, "dp", [(2, 1), (1, 2)])
        (home,) = call(
            functools.partial(settle_kernel, index_of, start, count),
            [unit],
            1,
            (tokens, outer, middle),
            "settle",
        )
        homes.append(home)
    return homes


def split_product_kernel(index_of, index_ref, x_ref, w_ref, send_ref, other_ref, own_ref):
    index = index_of(index_ref)
    each = index.per_part * x_ref.shape[1]
    rows = [
        x_ref[index.block(core_bit, chip_bits, i)]
        for core_bit in (1, 0)
        for chip_bits in range(index.chips)
        for i in range(index.per_part)
    ]
    total = jnp.dot(
        jnp.concatenate(rows, axis=0), w_ref[...], preferred_element_type=jnp.float32
    )
    half = index.chips * each
    send_ref[...] = total[:half].astype(send_ref.dtype)
    own_ref[...] = total[half : half + each]
    other_ref[...] = total[half + each :]


def split_product(index_of, index, shape, rows, weight):
    block_count, count, depth = rows.shape
    width = weight.shape[1]
    tile = 512
    each = shape.per_part * count
    half = block_count * count // 2

    def columns(height):
        return pl.BlockSpec((height, tile), lambda n, _: (0, n))

    return pl.pallas_call(
        functools.partial(split_product_kernel, index_of),
        grid_spec=pltpu.PrefetchScalarGridSpec(
            num_scalar_prefetch=1,
            grid=(width // tile,),
            in_specs=[whole(rows.shape), columns(depth)],
            out_specs=[columns(half), columns(half - each), columns(each)],
        ),
        out_shape=[
            shape_of((half, width), jnp.bfloat16),
            shape_of((half - each, width), jnp.float32),
            shape_of((each, width), jnp.float32),
        ],
        compiler_params=pltpu.CompilerParams(vmem_limit_bytes=24 * MIB),
        cost_estimate=cost(
            4 * half * depth * width, 2 * depth * (2 * half + width) + 6 * half * width
        ),
        name="split_product",
    )(index, rows, weight)


def narrow_kernel(index_of, index_ref, tokens_ref, down_ref, cot_ref, up_ref, send_ref, keep_ref, back_ref, low):
    index = index_of(index_ref)
    for m in range(CAP):
        low[m] = lax.dot_general(
            down_ref[0],
            tokens_ref[m * BLK : (m + 1) * BLK],
            LAST,
            preferred_element_type=jnp.float32,
        )
    for core_bit, out_ref in ((1, send_ref), (0, keep_ref)):
        for chip_bits in range(index.chips):
            for i in range(index.per_part):
                block = index.block(core_bit, chip_bits, i)
                mine = index.owner(block) == index.place
                out_ref[chip_bits, i] = jnp.where(mine, low[index.slot(block)], 0.0)
    for i in range(index.per_part):
        adapter = index.owner(index.block(0, 0, i))
        back_ref[i] = lax.dot_general(
            up_ref[adapter],
            cot_ref[i * BLK : (i + 1) * BLK],
            LAST,
            preferred_element_type=jnp.float32,
        )


def narrow(index_of, index, shape, tokens, down, cotangent, up):
    rank = up.shape[1]
    one = (shape.per_part, rank, BLK)
    outs = [(shape.chips,) + one, (shape.chips,) + one, one]
    operands = (tokens, down, cotangent, up)
    return pl.pallas_call(
        functools.partial(narrow_kernel, index_of),
        grid_spec=pltpu.PrefetchScalarGridSpec(
            num_scalar_prefetch=1,
            grid=(1,),
            in_specs=[whole(o.shape) for o in operands],
            out_specs=[whole(o) for o in outs],
            scratch_shapes=[pltpu.VMEM((CAP, rank, BLK), jnp.float32)],
        ),
        out_shape=[shape_of(o, jnp.float32) for o in outs],
        compiler_params=pltpu.CompilerParams(vmem_limit_bytes=24 * MIB),
        cost_estimate=cost(2 * rank * (tokens.size + cotangent.size), 2 * sum(o.size for o in operands)),
        name="narrow",
    )(index, *operands)


def pieces_kernel(index_of, index_ref, sum_ref, more_ref, cot_ref, low_ref, back_ref, piece_ref):
    index = index_of(index_ref)
    for i in range(index.per_part):
        live = index.live_rows(index.block(0, 0, i))
        keep = lax.broadcasted_iota(jnp.int32, low_ref.shape[1:], 1) < live
        lowered = jnp.where(keep, sum_ref[0, i] + more_ref[0, i], 0.0).astype(low_ref.dtype)
        back = jnp.where(keep, sum_ref[1, i] + more_ref[1, i], 0.0)
        low_ref[i] = lowered
        back_ref[i] = back.astype(back_ref.dtype)
        piece_ref[i] = jnp.dot(
            lowered, cot_ref[i * BLK : (i + 1) * BLK], preferred_element_type=jnp.float32
        ).astype(piece_ref.dtype)


def make_pieces(index_of, index, shape, total, more, cotangent):
    _, per_part, rank, _ = total.shape
    width = cotangent.shape[1]
    outs = [(per_part, rank, BLK), (per_part, rank, BLK), (per_part, rank, width)]
    operands = (total, more, cotangent)
    return pl.pallas_call(
        functools.partial(pieces_kernel, index_of),
        grid_spec=pltpu.PrefetchScalarGridSpec(
            num_scalar_prefetch=1,
            grid=(1,),
            in_specs=[whole(o.shape) for o in operands],
            out_specs=[whole(o) for o in outs],
        ),
        out_shape=[shape_of(o, jnp.bfloat16) for o in outs],
        compiler_params=pltpu.CompilerParams(vmem_limit_bytes=24 * MIB),
        cost_estimate=cost(2 * rank * cotangent.size, 3 * cotangent.size),
        name="pieces",
    )(index, *operands)


def down_gradient_kernel(index_of, index_ref, tokens_ref, *refs):
    back_refs, out_ref = refs[:-1], refs[-1]
    index = index_of(index_ref)
    out_ref[...] = jnp.zeros_like(out_ref)
    for core_bit in range(CORES):
        for chip_bits in range(index.chips):
            for i in range(index.per_part):
                block = index.block(core_bit, chip_bits, i)
                back_ref = back_refs[core_bit * index.chips + chip_bits]

                @pl.when(index.owner(block) == index.place)
                def _(block=block, back_ref=back_ref, i=i):
                    at = pl.multiple_of(index.slot(block) * BLK, BLK)
                    out_ref[0] += adapter_scale * jnp.dot(
                        back_ref[i],
                        tokens_ref[pl.ds(at, BLK)],
                        preferred_element_type=jnp.float32,
                    )


def down_gradient(index_of, index, tokens, backs):
    out = (1, backs[0].shape[1], tokens.shape[1])
    operands = (tokens, *backs)
    return pl.pallas_call(
        functools.partial(down_gradient_kernel, index_of),
        grid_spec=pltpu.PrefetchScalarGridSpec(
            num_scalar_prefetch=1,
            grid=(1,),
            in_specs=[whole(o.shape) for o in operands],
            out_specs=whole(out),
        ),
        out_shape=shape_of(out, jnp.float32),
        compiler_params=pltpu.CompilerParams(vmem_limit_bytes=24 * MIB),
        cost_estimate=cost(2 * out[1] * tokens.size, 2 * tokens.size),
        name="down_gradient",
    )(index, *operands)


def up_gradient_kernel(index_of, index_ref, *refs):
    piece_refs, out_ref = refs[:-1], refs[-1]
    index = index_of(index_ref)

    def of_device(core_bit, chip_bits, adapter):
        total = None
        for i in range(index.per_part):
            mine = index.owner(index.block(core_bit, chip_bits, i)) == adapter
            piece = piece_refs[core_bit * index.chips + chip_bits][i].astype(jnp.float32)
            term = jnp.where(mine, piece, 0.0)
            total = term if total is None else total + term
        return total

    for adapter in range(index.adapters):
        level = [
            of_device(0, j, adapter) + of_device(1, j, adapter) for j in range(index.chips)
        ]
        while len(level) > 1:
            level = [level[j] + level[j + 1] for j in range(0, len(level), 2)]
        out_ref[adapter] = adapter_scale * level[0]


def up_gradient(index_of, index, adapter_count, pieces):
    per_part, rank, width = pieces[0].shape
    tile = 512
    out = (adapter_count, rank, width)
    return pl.pallas_call(
        functools.partial(up_gradient_kernel, index_of),
        grid_spec=pltpu.PrefetchScalarGridSpec(
            num_scalar_prefetch=1,
            grid=(width // tile,),
            in_specs=[pl.BlockSpec((per_part, rank, tile), lambda n, _: (0, 0, n))] * len(pieces),
            out_specs=pl.BlockSpec((adapter_count, rank, tile), lambda n, _: (0, 0, n)),
        ),
        out_shape=shape_of(out, jnp.float32),
        compiler_params=pltpu.CompilerParams(vmem_limit_bytes=24 * MIB),
        cost_estimate=cost(0, 4 * adapter_count * rank * width + 2 * len(pieces) * pieces[0].size),
        name="up_gradient",
    )(index, *pieces)


def finish_kernel(index_of, counts, index_ref, low_ref, up_ref, *refs):
    sum_refs, out_ref = refs[:-1], refs[-1]
    index = index_of(index_ref)
    per_chunk = len(sum_refs) // len(counts)
    for i in range(index.per_part):
        block = index.block(0, 0, i)
        live = index.live_rows(block)
        side = lax.dot_general(
            low_ref[i],
            up_ref[index.owner(block)],
            (((0,), (0,)), ((), ())),
            preferred_element_type=jnp.float32,
        )
        start = 0
        for c, count in enumerate(counts):
            total = adapter_scale * side[start : start + count]
            for ref in sum_refs[c * per_chunk : (c + 1) * per_chunk]:
                total = total + ref[i * count : (i + 1) * count].astype(jnp.float32)
            keep = start + lax.broadcasted_iota(jnp.int32, total.shape, 0) < live
            at = i * BLK + start
            out_ref[at : at + count] = jnp.where(keep, total, 0.0).astype(out_ref.dtype)
            start += count


def finish(index_of, index, lowered, up, sums):
    per_part = lowered.shape[0]
    adapter_count, rank, width = up.shape
    tile = 1024
    flat = [s for chunk in sums for s in chunk]
    heights = [per_part * count for chunk, count in zip(sums, CHUNK_ROWS) for _ in chunk]
    out = (per_part * BLK, width)
    return pl.pallas_call(
        functools.partial(finish_kernel, index_of, CHUNK_ROWS),
        grid_spec=pltpu.PrefetchScalarGridSpec(
            num_scalar_prefetch=1,
            grid=(width // tile,),
            in_specs=[
                whole(lowered.shape),
                pl.BlockSpec((adapter_count, rank, tile), lambda n, _: (0, 0, n)),
            ]
            + [pl.BlockSpec((height, tile), lambda n, _: (0, n)) for height in heights],
            out_specs=pl.BlockSpec((out[0], tile), lambda n, _: (0, n)),
        ),
        out_shape=shape_of(out, jnp.bfloat16),
        compiler_params=pltpu.CompilerParams(vmem_limit_bytes=24 * MIB),
        cost_estimate=cost(2 * rank * out[0] * width, 10 * out[0] * width + 2 * up.size),
        name="finish",
    )(index, lowered, up, *flat)


def per_device(
    tokens,
    cotangent,
    frozen_up_weight,
    adapter_down_factor,
    adapter_up_factor,
    tokens_per_adapter,
    adapter_of_block,
    slot_of_block,
):
    owners = lax.axis_size("dp")
    parts = lax.axis_size("tensor")
    chips = parts // CORES
    block_count = adapter_of_block.shape[0]
    adapter_count = adapter_up_factor.shape[0]
    width_dev = tokens.shape[1]
    index_of = functools.partial(
        Index, block_count=block_count, adapter_count=adapter_count, parts=parts
    )
    shape = index_of(None)
    index = Index.pack(adapter_of_block, slot_of_block, tokens_per_adapter)

    def to_other_core(value):
        return lax.ppermute(value, "tensor", [(i, i ^ 1) for i in range(parts)])

    def to_chip(value, k):
        return lax.ppermute(value, "tensor", [(i, i ^ (k * CORES)) for i in range(parts)])

    def across_dp(value, k):
        return lax.ppermute(value, "dp", [(i, i ^ k) for i in range(owners)])

    def every_part(value):
        same_core = [value] + [to_chip(value, k) for k in range(1, chips)]
        return same_core + [to_other_core(v) for v in same_core]

    if owners == 4 and block_count == 4:
        homes = blocks_at_home(index_of, index, tokens)
        chunks = [lax.all_gather(home, "dp", axis=0) for home in homes]
    else:
        every_slot = lax.all_gather(
            tokens.reshape(CAP, BLK, width_dev), "dp", axis=0, tiled=True
        )
        picked = every_slot[adapter_of_block * CAP + slot_of_block]
        starts = [sum(CHUNK_ROWS[:c]) for c in range(len(CHUNK_ROWS))]
        chunks = [picked[:, s : s + count] for s, count in zip(starts, CHUNK_ROWS)]

    send, keep, back = narrow(
        index_of,
        index,
        shape,
        tokens,
        jnp.swapaxes(adapter_down_factor, 1, 2),
        cotangent,
        adapter_up_factor,
    )
    low_chip = keep + to_other_core(send)
    low_part = low_chip[0]
    for k in range(1, chips):
        low_part = low_part + to_chip(low_chip[k], k)
    total = jnp.stack([low_part, back])
    k = 1
    while 2 * k < owners:
        total = total + across_dp(total, k)
        k *= 2
    more = across_dp(total, k)
    lowered, back_rows, pieces = make_pieces(index_of, index, shape, total, more, cotangent)
    up_grad = up_gradient(index_of, index, adapter_count, every_part(pieces))
    down_grad = down_gradient(index_of, index, tokens, every_part(back_rows))

    sums = []
    for rows in chunks:
        count = rows.shape[1]
        each = shape.per_part * count
        send, other, own = split_product(index_of, index, shape, rows, frozen_up_weight)
        arrived = to_other_core(send)
        outgoing = (other + arrived[each:].astype(jnp.float32)).astype(jnp.bfloat16)
        sums.append(
            [own, arrived]
            + [to_chip(outgoing[(k - 1) * each : k * each], k) for k in range(1, chips)]
        )
    projected = finish(index_of, index, lowered, adapter_up_factor, sums)
    return (projected, jnp.swapaxes(down_grad, 1, 2), up_grad)


def solution(mesh):
    return jax.shard_map(
        per_device,
        mesh=mesh,
        in_specs=(
            P(("groups", "dp"), "tensor"),
            P(("groups", "tensor"), "dp"),
            P("tensor", "dp"),
            P(("groups", "dp"), "tensor", None),
            P("groups", None, "dp"),
            P("groups"),
            P("groups"),
            P("groups"),
        ),
        out_specs=(
            P(("groups", "tensor"), "dp"),
            P(("groups", "dp"), "tensor", None),
            P("groups", None, "dp"),
        ),
        check_vma=False,
    )
```

time: 248 us -> 247 us (level)
  Pallas kernels: 0 us -> 120 us
  waiting for transfers between devices: 133 us -> 52.1 us
  blocking collectives: 48 us -> 0 us
  matrix products: 35.1 us -> 0 us
  starting transfers between devices: 0.11 us -> 34.6 us
  local copies, waits for them, and re-layouts: 12.5 us -> 23.8 us
    pallas_call x0 -> x12, Pallas kernels: none -> 120 us  [the longest x5 90.6 us: call(): pl.pallas_call(kernel, grid_spec=pltpu.PrefetchScalarGridSpec(num_scalar_...]
    all_gather x2, waiting for transfers between devices: 119 us -> 0.01 us  [per_device(): chunks = [lax.all_gather(home, 'dp', axis=0) for home in homes]]
    ppermute x0 -> x22, waiting for transfers between devices: none -> 52.1 us  [the longest x5 22.9 us: to_chip(): lax.ppermute(value, 'tensor', [(i, i ^ k * CORES) for i in range(parts)])]
    dot_general x8 -> x0, matrix products: 35.1 us -> none  [the longest x1 15.2 us: per_device(): jnp.dot(flat_rows, frozen_up_weight, preferred_element_type=jnp.float32)]
    ppermute x0 -> x22, starting transfers between devices: none -> 34.5 us  [the longest x2 9.85 us: blocks_at_home(): outer = lax.ppermute(outer, 'dp', [(1, 0), (0, 1), (3, 2)])]
    psum x2 -> x0, blocking collectives: 34.4 us -> none  [the longest x1 21.2 us: per_device(): returned_rows = lax.psum(partial_back, 'dp').astype(jnp.bfloat16)]
    unnamed x13 -> x44, local copies, waits for them, and re-layouts: 4.48 us -> 22.5 us
    all_gather x1 -> x0, blocking collectives: 13.6 us -> none  [per_device(): lax.all_gather(lowered, 'dp', axis=0, tiled=True)]
  transfers between devices with their start and end apart: 3 -> 24, of which waited for: 2 -> 11; matrix products, arithmetic and copies ran while one was open for 19% -> 1% of each run, Pallas kernels for 0% -> 22%
where the time goes in v2:
time: 247 us; the launch traced here: 246 us
  Pallas kernels  120 us (49%)
  waiting for transfers between devices  52.1 us (21%)
  starting transfers between devices  34.6 us (14%)
  local copies, waits for them, and re-layouts  23.8 us (10%)
  between operations  14.4 us (6%)
    pallas_call x5, Pallas kernels, call(): pl.pallas_call(kernel, grid_spec=pltpu.PrefetchScalarGridSpec(num_scalar_...  90.6 us
    ppermute x5, waiting for transfers between devices, to_chip(): lax.ppermute(value, 'tensor', [(i, i ^ k * CORES) for i in range(parts)])  22.9 us
    unnamed x44, local copies, waits for them, and re-layouts  22.5 us
    pallas_call x2, Pallas kernels, split_product(): pl.pallas_call(functools.partial(split_product_kernel, index_of), grid_sp...  16.4 us
    ppermute x2, starting transfers between devices, blocks_at_home(): outer = lax.ppermute(outer, 'dp', [(1, 0), (0, 1), (3, 2)])  9.85 us
    ppermute x2, starting transfers between devices, blocks_at_home(): inward = lax.ppermute(sends[2 * c], 'dp', [(3, 2), (0, 1)])  9.83 us
    ppermute x2, waiting for transfers between devices, blocks_at_home(): inward = lax.ppermute(sends[2 * c], 'dp', [(3, 2), (0, 1)])  8.94 us
    ppermute x2, waiting for transfers between devices, blocks_at_home(): outer = lax.ppermute(outer, 'dp', [(1, 0), (0, 1), (3, 2)])  8.8 us
  transfers between devices with their start and end apart: 24, of which 11 were waited for; matrix products, arithmetic and copies ran while one was open for 1% of the time, Pallas kernels for 22%

profile of v2, /device:TPU:0, one launch (start us, length us, event | category | flops | bytes accessed | tf_op | source)
XLA Modules:
  0.0 246.4 jit_solution(11260145263372066590)
XLA Ops:
  8.5 33.6 %first_hop.1 = (bf16[64,2048]{1,0:T(8,128)(2,1)}, bf16[64,2048]{1,0:T(8,128)(2,1)}, bf16[64,2048]{1,0:T(8,128)(2,1)}, bf16[64,2048]{1,0:T(8,128)(2,1)}) custom-call(s32[14]{0:T(128)} %concatenate.3.index_ref, bf16[384,2048]{1,0:T(8,128)(2,1)} %tokens_ref.13), custom_call_target="tpu_custom_call" | custom-call | bytes 2097152 | tf_op jit(solution)/shard_map/first_hop/pallas_call | solution.py:152
  42.1 4.9 %collective-permute-start.10 = (bf16[64,2048]{1,0:T(8,128)(2,1)}, bf16[64,2048]{1,0:T(8,128)(2,1)S(1)}, u32[]{:S(2)}, u32[]{:S(2)}) collective-permute-start(bf16[64,2048]{1,0:T(8,128)(2,1)} %get-tuple-element.34), channel_id=1, source_target_pairs={{12,8},{0,4},{13,9},{1,5},{14,10},{2,6},{15,11},{3,7},{28,24},{16,... | collective-permute-start | bytes 786440 | tf_op jit(solution)/shard_map/ppermute | solution.py:176
  47.7 5.2 %collective-permute-done.10.a_ref = bf16[64,2048]{1,0:T(8,128)(2,1)S(1)} collective-permute-done((bf16[64,2048]{1,0:T(8,128)(2,1)}, bf16[64,2048]{1,0:T(8,128)(2,1)S(1)}, u32[]{:S(2)}, u32[]{:S(2)}) %collective-permute-start.10) | collective-permute-done | bytes 262176 | tf_op jit(solution)/shard_map/ppermute | solution.py:176
  54.3 18.8 %second_hop.3 = (bf16[64,2048]{1,0:T(8,128)(2,1)}, bf16[64,2048]{1,0:T(8,128)(2,1)}) custom-call(s32[14]{0:T(128)} %concatenate.3.index_ref, bf16[384,2048]{1,0:T(8,128)(2,1)} %tokens_ref.13, bf16[64,2048]{1,0:T(8,128)(2,1)} %copy-done.15, bf16[64,2048]{1,0:T(8,128)(2,1)} %copy-done.18), custom_call_target="tpu_custom_call" | custom-call | bytes 1048576 | tf_op jit(solution)/shard_map/second_hop/pallas_call | solution.py:152
  73.1 5.1 %collective-permute-start.12 = (bf16[64,2048]{1,0:T(8,128)(2,1)}, bf16[64,2048]{1,0:T(8,128)(2,1)S(1)}, u32[]{:S(2)}, u32[]{:S(2)}) collective-permute-start(bf16[64,2048]{1,0:T(8,128)(2,1)} %get-tuple-element.36), channel_id=1, source_target_pairs={{4,0},{0,4},{12,8},{5,1},{1,5},{13,9},{6,2},{2,6},{14,10},{7,3},{3... | collective-permute-start | bytes 786440 | tf_op jit(solution)/shard_map/ppermute | solution.py:185
  79.0 4.9 %collective-permute-done.12.x_ref = bf16[64,2048]{1,0:T(8,128)(2,1)S(1)} collective-permute-done((bf16[64,2048]{1,0:T(8,128)(2,1)}, bf16[64,2048]{1,0:T(8,128)(2,1)S(1)}, u32[]{:S(2)}, u32[]{:S(2)}) %collective-permute-start.12) | collective-permute-done | bytes 262176 | tf_op jit(solution)/shard_map/ppermute | solution.py:185
  85.3 9.7 %settle.3 = bf16[64,2048]{1,0:T(8,128)(2,1)} custom-call(s32[14]{0:T(128)} %concatenate.3.index_ref, bf16[384,2048]{1,0:T(8,128)(2,1)} %tokens_ref.13, bf16[64,2048]{1,0:T(8,128)(2,1)} %copy-done.16, bf16[64,2048]{1,0:T(8,128)(2,1)} %copy-done.20), custom_call_target="tpu_custom_call" | custom-call | bytes 524288 | tf_op jit(solution)/shard_map/settle/pallas_call | solution.py:152
  95.1 4.9 %collective-permute-start.4 = (bf16[64,2048]{1,0:T(8,128)(2,1)}, bf16[64,2048]{1,0:T(8,128)(2,1)S(1)}, u32[]{:S(2)}, u32[]{:S(2)}) collective-permute-start(bf16[64,2048]{1,0:T(8,128)(2,1)} %get-tuple-element.27), channel_id=1, source_target_pairs={{12,8},{0,4},{13,9},{1,5},{14,10},{2,6},{15,11},{3,7},{28,24},{16,... | collective-permute-start | bytes 786440 | tf_op jit(solution)/shard_map/ppermute | solution.py:176
  100.7 3.8 %collective-permute-done.4.a_ref = bf16[64,2048]{1,0:T(8,128)(2,1)S(1)} collective-permute-done((bf16[64,2048]{1,0:T(8,128)(2,1)}, bf16[64,2048]{1,0:T(8,128)(2,1)S(1)}, u32[]{:S(2)}, u32[]{:S(2)}) %collective-permute-start.4) | collective-permute-done | bytes 262176 | tf_op jit(solution)/shard_map/ppermute | solution.py:176
  105.9 18.8 %second_hop.2 = (bf16[64,2048]{1,0:T(8,128)(2,1)}, bf16[64,2048]{1,0:T(8,128)(2,1)}) custom-call(s32[14]{0:T(128)} %concatenate.3.index_ref, bf16[384,2048]{1,0:T(8,128)(2,1)} %tokens_ref.13, bf16[64,2048]{1,0:T(8,128)(2,1)} %copy-done.14, bf16[64,2048]{1,0:T(8,128)(2,1)} %copy-done.19), custom_call_target="tpu_custom_call" | custom-call | bytes 1048576 | tf_op jit(solution)/shard_map/second_hop/pallas_call | solution.py:152
  124.7 4.7 %collective-permute-start.6 = (bf16[64,2048]{1,0:T(8,128)(2,1)}, bf16[64,2048]{1,0:T(8,128)(2,1)S(1)}, u32[]{:S(2)}, u32[]{:S(2)}) collective-permute-start(bf16[64,2048]{1,0:T(8,128)(2,1)} %get-tuple-element.29), channel_id=1, source_target_pairs={{4,0},{0,4},{12,8},{5,1},{1,5},{13,9},{6,2},{2,6},{14,10},{7,3},{3... | collective-permute-start | bytes 786440 | tf_op jit(solution)/shard_map/ppermute | solution.py:185
  130.1 3.9 %collective-permute-done.6.x_ref = bf16[64,2048]{1,0:T(8,128)(2,1)S(1)} collective-permute-done((bf16[64,2048]{1,0:T(8,128)(2,1)}, bf16[64,2048]{1,0:T(8,128)(2,1)S(1)}, u32[]{:S(2)}, u32[]{:S(2)}) %collective-permute-start.6) | collective-permute-done | bytes 262176 | tf_op jit(solution)/shard_map/ppermute | solution.py:185
  135.3 9.7 %settle.2 = bf16[64,2048]{1,0:T(8,128)(2,1)} custom-call(s32[14]{0:T(128)} %concatenate.3.index_ref, bf16[384,2048]{1,0:T(8,128)(2,1)} %tokens_ref.13, bf16[64,2048]{1,0:T(8,128)(2,1)} %copy-done.17, bf16[64,2048]{1,0:T(8,128)(2,1)} %copy-done.21), custom_call_target="tpu_custom_call" | custom-call | bytes 524288 | tf_op jit(solution)/shard_map/settle/pallas_call | solution.py:152
  151.2 6.0 %copy-done.1 = bf16[2048,4096]{1,0:T(8,128)(2,1)S(1)} copy-done((bf16[2048,4096]{1,0:T(8,128)(2,1)S(1)}, bf16[2048,4096]{1,0:T(8,128)(2,1)}, u32[]{:S(2)}) %copy-start.1) | copy-done | bytes 16777240
  158.5 8.5 %split_product.3 = (bf16[128,4096]{1,0:T(8,128)(2,1)}, f32[64,4096]{1,0:T(8,128)S(1)}, f32[64,4096]{1,0:T(8,128)S(1)}) custom-call(s32[14]{0:T(128)S(1)} %copy-done.13, bf16[4,64,2048]{2,1,0:T(8,128)(2,1)S(1)} %bitcast.17, bf16[2048,4096]{1,0:T(8,128)(2,1)S(1)} %copy-done.1), custom_call_target="tpu_custom_call" | custom-call | flops 4294967296 | bytes 20971520 | tf_op jit(solution)/shard_map/split_product/pallas_call | solution.py:226
  168.0 3.2 %collective-permute-start.2 = (f32[2,1,64,128]{3,2,1,0:T(8,128)S(1)}, f32[2,1,64,128]{3,2,1,0:T(8,128)S(1)}, u32[]{:S(2)}, u32[]{:S(2)}) collective-permute-start(f32[2,1,64,128]{3,2,1,0:T(8,128)S(1)} %pad_maximum_fusion), channel_id=1, source_target_pairs={{0,4},{4,0},{8,12},{12,8},{1,5},{5,1},{9,13},{13,9},{2,6},{6,2},{1... | collective-permute-start | bytes 196616 | tf_op jit(solution)/shard_map/ppermute | solution.py:485
  171.2 3.6 %collective-permute-done.2 = f32[2,1,64,128]{3,2,1,0:T(8,128)S(1)} collective-permute-done((f32[2,1,64,128]{3,2,1,0:T(8,128)S(1)}, f32[2,1,64,128]{3,2,1,0:T(8,128)S(1)}, u32[]{:S(2)}, u32[]{:S(2)}) %collective-permute-start.2) | collective-permute-done | bytes 65568 | tf_op jit(solution)/shard_map/ppermute | solution.py:485
  174.9 2.1 collective-permute-start.3
  177.0 4.3 %collective-permute-done.3.more_ref = f32[2,1,64,128]{3,2,1,0:T(8,128)S(1)} collective-permute-done((f32[2,1,64,128]{3,2,1,0:T(8,128)S(1)}, f32[2,1,64,128]{3,2,1,0:T(8,128)S(1)}, u32[]{:S(2)}, u32[]{:S(2)}) %collective-permute-start.3) | collective-permute-done | bytes 65568 | tf_op jit(solution)/shard_map/ppermute | solution.py:485
  183.6 5.8 %copy-done.2 = bf16[2048,4096]{1,0:T(8,128)(2,1)S(1)} copy-done((bf16[2048,4096]{1,0:T(8,128)(2,1)S(1)}, bf16[2048,4096]{1,0:T(8,128)(2,1)}, u32[]{:S(2)}) %copy-start.2) | copy-done | bytes 16777240
  190.6 7.9 %split_product.2 = (bf16[128,4096]{1,0:T(8,128)(2,1)S(1)}, f32[64,4096]{1,0:T(8,128)S(1)}, f32[64,4096]{1,0:T(8,128)S(1)}) custom-call(s32[14]{0:T(128)S(1)} %copy-done.13, bf16[4,64,2048]{2,1,0:T(8,128)(2,1)S(1)} %bitcast.18, bf16[2048,4096]{1,0:T(8,128)(2,1)S(1)} %copy-done.2), custom_call_target="tpu_custom_call" | custom-call | flops 4294967296 | bytes 20971520 | tf_op jit(solution)/shard_map/split_product/pallas_call | solution.py:226
  203.4 22.8 %collective-permute-done.16.refs_1_ = bf16[1,64,128]{2,1,0:T(8,128)(2,1)S(1)} collective-permute-done((bf16[1,64,128]{2,1,0:T(8,128)(2,1)S(1)}, bf16[1,64,128]{2,1,0:T(8,128)(2,1)S(1)}, u32[]{:S(2)}, u32[]{:S(2)}) %collective-permute-start.16) | collective-permute-done | bytes 16416 | tf_op jit(solution)/shard_map/ppermute | solution.py:482
  230.0 4.9 %up_gradient.1 = f32[4,64,4096]{2,1,0:T(8,128)} custom-call(s32[14]{0:T(128)S(1)} %copy-done.13, bf16[1,64,4096]{2,1,0:T(8,128)(2,1)S(1)} %get-tuple-element.42.refs_0_, bf16[1,64,4096]{2,1,0:T(8,128)(2,1)S(1)} %collective-permute-done.19.refs_1_, bf16[1,64,4096]{2,1,0:T(8,128)(2,1)S(1)} %collective-permute-done.20.refs_2_, ...), custom_call_target="tpu_custom_call" | custom-call | bytes 6291456 | tf_op jit(solution)/shard_map/up_gradient/pallas_call | solution.py:391
  235.0 4.6 %finish.1 = bf16[128,4096]{1,0:T(8,128)(2,1)} custom-call(s32[14]{0:T(128)S(1)} %copy-done.13, bf16[1,64,128]{2,1,0:T(8,128)(2,1)S(1)} %get-tuple-element.26.low_ref, bf16[4,64,4096]{2,1,0:T(8,128)(2,1)S(1)} %copy-done.4, f32[64,4096]{1,0:T(8,128)S(1)} %get-tuple-element.31.refs_0_, bf16[128,4096]{1,0:T(8,128)(2,1)S(1)} %collective-permute-done.8.refs_1_, ...), custom_call_target="tpu_custom_call" | custom-call | flops 67108864 | bytes 7340032 | tf_op jit(solution)/shard_map/finish/pallas_call | solution.py:437
  (90 shorter events, 30.2 us)
Async XLA Ops:
  7.2 144.1 %all-gather.7.cloned.1.call-start = ((), (), s32[]{:S(2)}) async-start(), calls=%async_computation.1 | async-start | bytes 1310720 | tf_op jit(solution)/shard_map/all_gather | solution.py:493
  42.1 10.8 %collective-permute-start.10 = (bf16[64,2048]{1,0:T(8,128)(2,1)}, bf16[64,2048]{1,0:T(8,128)(2,1)S(1)}, u32[]{:S(2)}, u32[]{:S(2)}) collective-permute-start(bf16[64,2048]{1,0:T(8,128)(2,1)} %get-tuple-element.34), channel_id=1, source_target_pairs={{12,8},{0,4},{13,9},{1,5},{14,10},{2,6},{15,11},{3,7},{28,24},{16,... | collective-permute-start | bytes 786440 | tf_op jit(solution)/shard_map/ppermute | solution.py:176
  47.0 5.9 %collective-permute-start.11 = (bf16[64,2048]{1,0:T(8,128)(2,1)}, bf16[64,2048]{1,0:T(8,128)(2,1)S(1)}, u32[]{:S(2)}, u32[]{:S(2)}) collective-permute-start(bf16[64,2048]{1,0:T(8,128)(2,1)} %get-tuple-element.35), channel_id=1, source_target_pairs={{8,4},{9,5},{10,6},{11,7},{24,20},{25,21},{26,22},{27,23}} | collective-permute-start | bytes 786440 | tf_op jit(solution)/shard_map/ppermute | solution.py:177
  73.1 10.8 %collective-permute-start.12 = (bf16[64,2048]{1,0:T(8,128)(2,1)}, bf16[64,2048]{1,0:T(8,128)(2,1)S(1)}, u32[]{:S(2)}, u32[]{:S(2)}) collective-permute-start(bf16[64,2048]{1,0:T(8,128)(2,1)} %get-tuple-element.36), channel_id=1, source_target_pairs={{4,0},{0,4},{12,8},{5,1},{1,5},{13,9},{6,2},{2,6},{14,10},{7,3},{3... | collective-permute-start | bytes 786440 | tf_op jit(solution)/shard_map/ppermute | solution.py:185
  78.3 5.6 %collective-permute-start.13 = (bf16[64,2048]{1,0:T(8,128)(2,1)}, bf16[64,2048]{1,0:T(8,128)(2,1)S(1)}, u32[]{:S(2)}, u32[]{:S(2)}) collective-permute-start(bf16[64,2048]{1,0:T(8,128)(2,1)} %get-tuple-element.37), channel_id=1, source_target_pairs={{8,4},{4,8},{9,5},{5,9},{10,6},{6,10},{11,7},{7,11},{24,20},{20,24... | collective-permute-start | bytes 786440 | tf_op jit(solution)/shard_map/ppermute | solution.py:186
  95.1 88.5 %all-gather.5.cloned.1.call-start = ((), (), s32[]{:S(2)}) async-start(), calls=%async_computation | async-start | bytes 1310720 | tf_op jit(solution)/shard_map/all_gather | solution.py:493
  95.1 9.4 %collective-permute-start.4 = (bf16[64,2048]{1,0:T(8,128)(2,1)}, bf16[64,2048]{1,0:T(8,128)(2,1)S(1)}, u32[]{:S(2)}, u32[]{:S(2)}) collective-permute-start(bf16[64,2048]{1,0:T(8,128)(2,1)} %get-tuple-element.27), channel_id=1, source_target_pairs={{12,8},{0,4},{13,9},{1,5},{14,10},{2,6},{15,11},{3,7},{28,24},{16,... | collective-permute-start | bytes 786440 | tf_op jit(solution)/shard_map/ppermute | solution.py:176
  100.0 4.5 %collective-permute-start.5 = (bf16[64,2048]{1,0:T(8,128)(2,1)}, bf16[64,2048]{1,0:T(8,128)(2,1)S(1)}, u32[]{:S(2)}, u32[]{:S(2)}) collective-permute-start(bf16[64,2048]{1,0:T(8,128)(2,1)} %get-tuple-element.28), channel_id=1, source_target_pairs={{8,4},{9,5},{10,6},{11,7},{24,20},{25,21},{26,22},{27,23}} | collective-permute-start | bytes 786440 | tf_op jit(solution)/shard_map/ppermute | solution.py:177
  124.7 9.3 %collective-permute-start.6 = (bf16[64,2048]{1,0:T(8,128)(2,1)}, bf16[64,2048]{1,0:T(8,128)(2,1)S(1)}, u32[]{:S(2)}, u32[]{:S(2)}) collective-permute-start(bf16[64,2048]{1,0:T(8,128)(2,1)} %get-tuple-element.29), channel_id=1, source_target_pairs={{4,0},{0,4},{12,8},{5,1},{1,5},{13,9},{6,2},{2,6},{14,10},{7,3},{3... | collective-permute-start | bytes 786440 | tf_op jit(solution)/shard_map/ppermute | solution.py:185
  129.4 4.6 %collective-permute-start.7 = (bf16[64,2048]{1,0:T(8,128)(2,1)}, bf16[64,2048]{1,0:T(8,128)(2,1)S(1)}, u32[]{:S(2)}, u32[]{:S(2)}) collective-permute-start(bf16[64,2048]{1,0:T(8,128)(2,1)} %get-tuple-element.30), channel_id=1, source_target_pairs={{8,4},{4,8},{9,5},{5,9},{10,6},{6,10},{11,7},{7,11},{24,20},{20,24... | collective-permute-start | bytes 786440 | tf_op jit(solution)/shard_map/ppermute | solution.py:186
  148.3 1.3 collective-permute-start
  149.6 18.3 %collective-permute-start.1 = (f32[1,64,128]{2,1,0:T(8,128)S(1)}, f32[1,64,128]{2,1,0:T(8,128)S(1)}, u32[]{:S(2)}, u32[]{:S(2)}) collective-permute-start(f32[1,64,128]{2,1,0:T(8,128)S(1)} %slice_bitcast_fusion), channel_id=1, source_target_pairs={{0,2},{1,3},{2,0},{3,1},{4,6},{5,7},{6,4},{7,5},{8,10},{9,11},{10,... | collective-permute-start | bytes 98312 | tf_op jit(solution)/shard_map/ppermute | solution.py:482
  168.0 31.2 %collective-permute-start.14 = (bf16[128,4096]{1,0:T(8,128)(2,1)}, bf16[128,4096]{1,0:T(8,128)(2,1)}, u32[]{:S(2)}, u32[]{:S(2)}) collective-permute-start(bf16[128,4096]{1,0:T(8,128)(2,1)} %get-tuple-element.39), channel_id=1, source_target_pairs={{0,1},{1,0},{2,3},{3,2},{4,5},{5,4},{6,7},{7,6},{8,9},{9,8},{10,11... | collective-permute-start | bytes 3145736 | tf_op jit(solution)/shard_map/ppermute | solution.py:479
  168.0 6.8 %collective-permute-start.2 = (f32[2,1,64,128]{3,2,1,0:T(8,128)S(1)}, f32[2,1,64,128]{3,2,1,0:T(8,128)S(1)}, u32[]{:S(2)}, u32[]{:S(2)}) collective-permute-start(f32[2,1,64,128]{3,2,1,0:T(8,128)S(1)} %pad_maximum_fusion), channel_id=1, source_target_pairs={{0,4},{4,0},{8,12},{12,8},{1,5},{5,1},{9,13},{13,9},{2,6},{6,2},{1... | collective-permute-start | bytes 196616 | tf_op jit(solution)/shard_map/ppermute | solution.py:485
  174.9 6.4 %collective-permute-start.3 = (f32[2,1,64,128]{3,2,1,0:T(8,128)S(1)}, f32[2,1,64,128]{3,2,1,0:T(8,128)S(1)}, u32[]{:S(2)}, u32[]{:S(2)}) collective-permute-start(f32[2,1,64,128]{3,2,1,0:T(8,128)S(1)} %fusion.2.sum_ref), channel_id=1, source_target_pairs={{0,8},{4,12},{8,0},{12,4},{1,9},{5,13},{9,1},{13,5},{2,10},{6,14},... | collective-permute-start | bytes 196616 | tf_op jit(solution)/shard_map/ppermute | solution.py:485
  182.1 16.9 %collective-permute-start.19 = (bf16[1,64,4096]{2,1,0:T(8,128)(2,1)S(1)}, bf16[1,64,4096]{2,1,0:T(8,128)(2,1)S(1)}, u32[]{:S(2)}, u32[]{:S(2)}) collective-permute-start(bf16[1,64,4096]{2,1,0:T(8,128)(2,1)S(1)} %get-tuple-element.42.refs_0_), channel_id=1, source_target_pairs={{0,2},{1,3},{2,0},{3,1},{4,6},{5,7},{6,4},{7,5},{8,10},{9,11},{10,... | collective-permute-start | bytes 1572872 | tf_op jit(solution)/shard_map/ppermute | solution.py:482
  198.4 2.7 %collective-permute-start.8 = (bf16[128,4096]{1,0:T(8,128)(2,1)S(1)}, bf16[128,4096]{1,0:T(8,128)(2,1)S(1)}, u32[]{:S(2)}, u32[]{:S(2)}) collective-permute-start(bf16[128,4096]{1,0:T(8,128)(2,1)S(1)} %get-tuple-element.32), channel_id=1, source_target_pairs={{0,1},{1,0},{2,3},{3,2},{4,5},{5,4},{6,7},{7,6},{8,9},{9,8},{10,11... | collective-permute-start | bytes 3145736 | tf_op jit(solution)/shard_map/ppermute | solution.py:479
  198.5 31.5 %collective-permute-start.20 = (bf16[1,64,4096]{2,1,0:T(8,128)(2,1)S(1)}, bf16[1,64,4096]{2,1,0:T(8,128)(2,1)S(1)}, u32[]{:S(2)}, u32[]{:S(2)}) collective-permute-start(bf16[1,64,4096]{2,1,0:T(8,128)(2,1)S(1)} %get-tuple-element.42.refs_0_), channel_id=1, source_target_pairs={{0,1},{1,0},{2,3},{3,2},{4,5},{5,4},{6,7},{7,6},{8,9},{9,8},{10,11... | collective-permute-start | bytes 1572872 | tf_op jit(solution)/shard_map/ppermute | solution.py:479
  199.0 31.0 %collective-permute-start.21 = (bf16[1,64,4096]{2,1,0:T(8,128)(2,1)S(1)}, bf16[1,64,4096]{2,1,0:T(8,128)(2,1)S(1)}, u32[]{:S(2)}, u32[]{:S(2)}) collective-permute-start(bf16[1,64,4096]{2,1,0:T(8,128)(2,1)S(1)} %collective-permute-done.19.refs_1_), channel_id=1, source_target_pairs={{0,1},{1,0},{2,3},{3,2},{4,5},{5,4},{6,7},{7,6},{8,9},{9,8},{10,11... | collective-permute-start | bytes 1572872 | tf_op jit(solution)/shard_map/ppermute | solution.py:479
  200.3 34.6 %collective-permute-start.15 = (bf16[64,4096]{1,0:T(8,128)(2,1)S(1)}, bf16[64,4096]{1,0:T(8,128)(2,1)S(1)}, u32[]{:S(2)}, u32[]{:S(2)}) collective-permute-start(bf16[64,4096]{1,0:T(8,128)(2,1)S(1)} %add_convert_fusion), channel_id=1, source_target_pairs={{0,2},{1,3},{2,0},{3,1},{4,6},{5,7},{6,4},{7,5},{8,10},{9,11},{10,... | collective-permute-start | bytes 1572872 | tf_op jit(solution)/shard_map/ppermute | solution.py:482
  201.3 33.7 %collective-permute-start.9 = (bf16[64,4096]{1,0:T(8,128)(2,1)S(1)}, bf16[64,4096]{1,0:T(8,128)(2,1)S(1)}, u32[]{:S(2)}, u32[]{:S(2)}) collective-permute-start(bf16[64,4096]{1,0:T(8,128)(2,1)S(1)} %add_convert_fusion.1), channel_id=1, source_target_pairs={{0,2},{1,3},{2,0},{3,1},{4,6},{5,7},{6,4},{7,5},{8,10},{9,11},{10,... | collective-permute-start | bytes 1572872 | tf_op jit(solution)/shard_map/ppermute | solution.py:482
  202.5 23.7 %collective-permute-start.16 = (bf16[1,64,128]{2,1,0:T(8,128)(2,1)S(1)}, bf16[1,64,128]{2,1,0:T(8,128)(2,1)S(1)}, u32[]{:S(2)}, u32[]{:S(2)}) collective-permute-start(bf16[1,64,128]{2,1,0:T(8,128)(2,1)S(1)} %get-tuple-element.41.refs_0_), channel_id=1, source_target_pairs={{0,2},{1,3},{2,0},{3,1},{4,6},{5,7},{6,4},{7,5},{8,10},{9,11},{10,... | collective-permute-start | bytes 49160 | tf_op jit(solution)/shard_map/ppermute | solution.py:482
  226.2 1.2 collective-permute-start.17
  227.4 1.2 collective-permute-start.18
  (22 other events, 398.0 us)
Sparse Core Ops, SparseCore 0:
  95.2 29.1 all-gather.6
  145.2 28.9 all-gather.4

commit v3 on v2

--- a/solution.py
+++ b/solution.py
@@ -71,103 +71,98 @@
     return pl.CostEstimate(flops=flops, bytes_accessed=bytes_accessed, transcendentals=0)
 
 
-def copy_all(copies):
+def own_copy(index, block, start, tokens_ref, out_ref, sem):
+    at = pl.multiple_of(index.slot(block) * BLK + start, 16)
+    return pltpu.make_async_copy(tokens_ref.at[pl.ds(at, out_ref.shape[0])], out_ref, sem)
+
+
+def run_all(copies):
     for copy in copies:
         copy.start()
     for copy in copies:
         copy.wait()
 
 
-def first_hop_kernel(index_of, starts, rows, index_ref, tokens_ref, *refs):
+def first_hop_kernel(index_of, starts, index_ref, tokens_ref, *refs):
     outs, sems = refs[:-1], refs[-1]
     index = index_of(index_ref)
+    inward = jnp.where(index.place == 0, 2, 1)
+    run_all(
+        [
+            own_copy(index, block, start, tokens_ref, outs[2 * c + j], sems.at[2 * c + j])
+            for c, start in enumerate(starts)
+            for j, block in enumerate((inward, 0))
+        ]
+    )
+
+
+def second_hop_kernel(index_of, start, index_ref, tokens_ref, a_ref, b_ref, *refs):
+    x_ref, y_ref, sems = refs[-3:]
+    index = index_of(index_ref)
     place = index.place
-    inward = jnp.where(place == 0, 2, 1)
-    copies = []
-    for c, (start, count) in enumerate(zip(starts, rows)):
-        for j, block in enumerate((inward, 0)):
-            at = pl.multiple_of(index.slot(block) * BLK + start, 16)
-            copies.append(
-                pltpu.make_async_copy(
-                    tokens_ref.at[pl.ds(at, count)], outs[2 * c + j], sems.at[2 * c + j]
-                )
-            )
-    copy_all(copies)
-
-
-def pick_copy(choices, out_ref, sem):
-    for condition, source in choices:
-
-        @pl.when(condition)
-        def _(source=source):
-            copy = pltpu.make_async_copy(source, out_ref, sem)
-            copy.start()
-            copy.wait()
-
-
-def second_hop_kernel(index_of, start, count, index_ref, tokens_ref, a_ref, b_ref, x_ref, y_ref, sems):
-    index = index_of(index_ref)
-    place = index.place
-
-    def own(block):
-        at = pl.multiple_of(index.slot(block) * BLK + start, 16)
-        return tokens_ref.at[pl.ds(at, count)]
-
     outer = jnp.where(place == 0, 1, jnp.where(place == 1, 0, 2))
-    passed = (place == 1) & (index.owner(0) != 1)
-    pick_copy(
-        [(jnp.logical_not(passed), own(outer)), (passed, b_ref)], x_ref, sems.at[0]
+    middle = jnp.where(place == 1, 2, 1)
+    run_all(
+        [
+            own_copy(index, outer, start, tokens_ref, x_ref, sems.at[0]),
+            own_copy(index, middle, start, tokens_ref, y_ref, sems.at[1]),
+        ]
     )
-    middle = jnp.where(place == 1, 2, 1)
-    passed = ((place == 1) | (place == 2)) & (index.owner(middle) != place)
-    pick_copy(
-        [(jnp.logical_not(passed), own(middle)), (passed, a_ref)], y_ref, sems.at[1]
-    )
-
-
-def settle_kernel(index_of, start, count, index_ref, tokens_ref, x_ref, y_ref, out_ref, sems):
+
+    @pl.when((place == 1) & (index.owner(0) != 1))
+    def _():
+        x_ref[...] = b_ref[...]
+
+    @pl.when(((place == 1) | (place == 2)) & (index.owner(middle) != place))
+    def _():
+        y_ref[...] = a_ref[...]
+
+
+def settle_kernel(index_of, start, index_ref, tokens_ref, x_ref, y_ref, *refs):
+    out_ref, sems = refs[-2:]
     index = index_of(index_ref)
     place = index.place
     owner = index.owner(place)
     mine = owner == place
     edge = (place == 0) | ((place == 1) & (owner == 0)) | ((place == 2) & (owner == 3))
-    at = pl.multiple_of(index.slot(place) * BLK + start, 16)
-    pick_copy(
-        [
-            (mine, tokens_ref.at[pl.ds(at, count)]),
-            (jnp.logical_not(mine) & edge, x_ref),
-            (jnp.logical_not(mine | edge), y_ref),
-        ],
-        out_ref,
-        sems.at[0],
-    )
-
-
-def blocks_at_home(index_of, index, tokens):
+    run_all([own_copy(index, place, start, tokens_ref, out_ref, sems.at[0])])
+
+    @pl.when(jnp.logical_not(mine) & edge)
+    def _():
+        out_ref[...] = x_ref[...]
+
+    @pl.when(jnp.logical_not(mine | edge))
+    def _():
+        out_ref[...] = y_ref[...]
+
+
+def blocks_at_home(index_of, index, tokens, beside):
     width = tokens.shape[1]
     starts = [sum(CHUNK_ROWS[:c]) for c in range(len(CHUNK_ROWS))]
     hbm = pl.BlockSpec(memory_space=pl.ANY)
-
-    def call(kernel, outs, copies, operands, name):
+    vmem = pl.BlockSpec(memory_space=pltpu.VMEM)
+    beside = list(beside)
+
+    def call(kernel, outs, received, name):
+        extra = tuple(beside.pop(0)()) if beside and received else ()
         return pl.pallas_call(
             kernel,
             grid_spec=pltpu.PrefetchScalarGridSpec(
                 num_scalar_prefetch=1,
                 grid=(),
-                in_specs=[hbm] * len(operands),
-                out_specs=[hbm] * len(outs),
-                scratch_shapes=[pltpu.SemaphoreType.DMA((copies,))],
+                in_specs=[hbm] + [vmem] * len(received) + [hbm] * len(extra),
+                out_specs=[vmem] * len(outs),
+                scratch_shapes=[pltpu.SemaphoreType.DMA((len(outs),))],
             ),
             out_shape=outs,
             cost_estimate=cost(0, 4 * sum(o.size for o in outs)),
             name=name,
-        )(index, *operands)
+        )(index, tokens, *received, *extra)
 
     sends = call(
-        functools.partial(first_hop_kernel, index_of, starts, CHUNK_ROWS),
+        functools.partial(first_hop_kernel, index_of, starts),
         [shape_of((count, width), tokens.dtype) for count in CHUNK_ROWS for _ in range(2)],
-        2 * len(CHUNK_ROWS),
-        (tokens,),
+        (),
         "first_hop",
     )
     homes = []
@@ -176,19 +171,17 @@
         inward = lax.ppermute(sends[2 * c], "dp", [(3, 2), (0, 1)])
         left = lax.ppermute(sends[2 * c + 1], "dp", [(2, 1)])
         outer, middle = call(
-            functools.partial(second_hop_kernel, index_of, start, count),
+            functools.partial(second_hop_kernel, index_of, start),
             [unit, unit],
-            2,
-            (tokens, inward, left),
+            (inward, left),
             "second_hop",
         )
         outer = lax.ppermute(outer, "dp", [(1, 0), (0, 1), (3, 2)])
         middle = lax.ppermute(middle, "dp", [(2, 1), (1, 2)])
         (home,) = call(
-            functools.partial(settle_kernel, index_of, start, count),
+            functools.partial(settle_kernel, index_of, start),
             [unit],
-            1,
-            (tokens, outer, middle),
+            (outer, middle),
             "settle",
         )
         homes.append(home)
@@ -236,7 +229,7 @@
             shape_of((half - each, width), jnp.float32),
             shape_of((each, width), jnp.float32),
         ],
-        compiler_params=pltpu.CompilerParams(vmem_limit_bytes=24 * MIB),
+        compiler_params=pltpu.CompilerParams(vmem_limit_bytes=48 * MIB),
         cost_estimate=cost(
             4 * half * depth * width, 2 * depth * (2 * half + width) + 6 * half * width
         ),
@@ -403,16 +396,16 @@
     )(index, *pieces)
 
 
-def finish_kernel(index_of, counts, index_ref, low_ref, up_ref, *refs):
-    sum_refs, out_ref = refs[:-1], refs[-1]
-    index = index_of(index_ref)
+def finish_kernel(index_of, counts, index_ref, low_ref, *refs):
+    index = index_of(index_ref)
+    up_refs, sum_refs, out_ref = refs[: index.per_part], refs[index.per_part : -1], refs[-1]
     per_chunk = len(sum_refs) // len(counts)
     for i in range(index.per_part):
         block = index.block(0, 0, i)
         live = index.live_rows(block)
         side = lax.dot_general(
             low_ref[i],
-            up_ref[index.owner(block)],
+            up_refs[i][0],
             (((0,), (0,)), ((), ())),
             preferred_element_type=jnp.float32,
         )
@@ -434,15 +427,21 @@
     flat = [s for chunk in sums for s in chunk]
     heights = [per_part * count for chunk, count in zip(sums, CHUNK_ROWS) for _ in chunk]
     out = (per_part * BLK, width)
+
+    def factor(i):
+        def at(n, index_ref):
+            index = index_of(index_ref)
+            return (index.owner(index.block(0, 0, i)), 0, n)
+
+        return pl.BlockSpec((1, rank, tile), at)
+
     return pl.pallas_call(
         functools.partial(finish_kernel, index_of, CHUNK_ROWS),
         grid_spec=pltpu.PrefetchScalarGridSpec(
             num_scalar_prefetch=1,
             grid=(width // tile,),
-            in_specs=[
-                whole(lowered.shape),
-                pl.BlockSpec((adapter_count, rank, tile), lambda n, _: (0, 0, n)),
-            ]
+            in_specs=[whole(lowered.shape)]
+            + [factor(i) for i in range(per_part)]
             + [pl.BlockSpec((height, tile), lambda n, _: (0, n)) for height in heights],
             out_specs=pl.BlockSpec((out[0], tile), lambda n, _: (0, n)),
         ),
@@ -450,7 +449,7 @@
         compiler_params=pltpu.CompilerParams(vmem_limit_bytes=24 * MIB),
         cost_estimate=cost(2 * rank * out[0] * width, 10 * out[0] * width + 2 * up.size),
         name="finish",
-    )(index, lowered, up, *flat)
+    )(index, lowered, *[up] * per_part, *flat)
 
 
 def per_device(
@@ -488,37 +487,50 @@
         same_core = [value] + [to_chip(value, k) for k in range(1, chips)]
         return same_core + [to_other_core(v) for v in same_core]
 
+    steps = {}
+
+    def first_step():
+        steps["send"], steps["keep"], steps["back"] = narrow(
+            index_of,
+            index,
+            shape,
+            tokens,
+            jnp.swapaxes(adapter_down_factor, 1, 2),
+            cotangent,
+            adapter_up_factor,
+        )
+        return [steps["send"]]
+
+    def second_step():
+        low_chip = steps["keep"] + to_other_core(steps["send"])
+        low_part = low_chip[0]
+        for k in range(1, chips):
+            low_part = low_part + to_chip(low_chip[k], k)
+        steps["total"] = jnp.stack([low_part, steps["back"]])
+        return [steps["total"]]
+
+    def third_step():
+        total, k = steps["total"], 1
+        while 2 * k < owners:
+            total = total + across_dp(total, k)
+            k *= 2
+        steps["small"] = make_pieces(
+            index_of, index, shape, total, across_dp(total, k), cotangent
+        )
+        return [steps["small"][0]]
+
     if owners == 4 and block_count == 4:
-        homes = blocks_at_home(index_of, index, tokens)
+        homes = blocks_at_home(index_of, index, tokens, [first_step, second_step, third_step])
         chunks = [lax.all_gather(home, "dp", axis=0) for home in homes]
     else:
+        first_step(), second_step(), third_step()
         every_slot = lax.all_gather(
             tokens.reshape(CAP, BLK, width_dev), "dp", axis=0, tiled=True
         )
         picked = every_slot[adapter_of_block * CAP + slot_of_block]
         starts = [sum(CHUNK_ROWS[:c]) for c in range(len(CHUNK_ROWS))]
         chunks = [picked[:, s : s + count] for s, count in zip(starts, CHUNK_ROWS)]
-
-    send, keep, back = narrow(
-        index_of,
-        index,
-        shape,
-        tokens,
-        jnp.swapaxes(adapter_down_factor, 1, 2),
-        cotangent,
-        adapter_up_factor,
-    )
-    low_chip = keep + to_other_core(send)
-    low_part = low_chip[0]
-    for k in range(1, chips):
-        low_part = low_part + to_chip(low_chip[k], k)
-    total = jnp.stack([low_part, back])
-    k = 1
-    while 2 * k < owners:
-        total = total + across_dp(total, k)
-        k *= 2
-    more = across_dp(total, k)
-    lowered, back_rows, pieces = make_pieces(index_of, index, shape, total, more, cotangent)
+    lowered, back_rows, pieces = steps["small"]
     up_grad = up_gradient(index_of, index, adapter_count, every_part(pieces))
     down_grad = down_gradient(index_of, index, tokens, every_part(back_rows))
 

time: 247 us -> 186 us (0.75)
  Pallas kernels: 120 us -> 54.5 us
  waiting for transfers between devices: 52.1 us -> 70.2 us
  local copies, waits for them, and re-layouts: 23.8 us -> 14.7 us
  starting transfers between devices: 34.6 us -> 31 us
    pallas_call x5, Pallas kernels: 90.6 us -> 16.7 us  [call(): pl.pallas_call(kernel, grid_spec=pltpu.PrefetchScalarGridSpec(num_scalar_...]
    all_gather x2, waiting for transfers between devices: 0.01 us -> 12 us  [per_device(): chunks = [lax.all_gather(home, 'dp', axis=0) for home in homes]]
    ppermute x2, waiting for transfers between devices: 8.8 us -> 19.7 us  [blocks_at_home(): outer = lax.ppermute(outer, 'dp', [(1, 0), (0, 1), (3, 2)])]
    unnamed x44 -> x52, local copies, waits for them, and re-layouts: 22.5 us -> 13.9 us
    pallas_call x2, Pallas kernels: 16.4 us -> 23 us  [split_product(): pl.pallas_call(functools.partial(split_product_kernel, index_of), grid_sp...]
    ppermute x2, waiting for transfers between devices: 8.94 us -> 3.16 us  [blocks_at_home(): inward = lax.ppermute(sends[2 * c], 'dp', [(3, 2), (0, 1)])]
    ppermute x2, starting transfers between devices: 9.85 us -> 6.96 us  [blocks_at_home(): outer = lax.ppermute(outer, 'dp', [(1, 0), (0, 1), (3, 2)])]
    ppermute x2, starting transfers between devices: 9.83 us -> 7.1 us  [blocks_at_home(): inward = lax.ppermute(sends[2 * c], 'dp', [(3, 2), (0, 1)])]
  transfers between devices with their start and end apart: 24 -> 24, of which waited for: 11 -> 11; matrix products, arithmetic and copies ran while one was open for 1% -> 0% of each run, Pallas kernels for 22% -> 23%
where the time goes in v3:
time: 186 us; the launch traced here: 185 us
  waiting for transfers between devices  70.2 us (38%)
  Pallas kernels  54.5 us (29%)
  starting transfers between devices  31 us (17%)
  local copies, waits for them, and re-layouts  14.7 us (8%)
  between operations  14.4 us (8%)
    pallas_call x2, Pallas kernels, split_product(): pl.pallas_call(functools.partial(split_product_kernel, index_of), grid_sp...  23 us
    ppermute x5, waiting for transfers between devices, to_chip(): lax.ppermute(value, 'tensor', [(i, i ^ k * CORES) for i in range(parts)])  23 us
    ppermute x2, waiting for transfers between devices, blocks_at_home(): outer = lax.ppermute(outer, 'dp', [(1, 0), (0, 1), (3, 2)])  19.7 us
    pallas_call x5, Pallas kernels, call(): pl.pallas_call(kernel, grid_spec=pltpu.PrefetchScalarGridSpec(num_scalar_...  16.7 us
    unnamed x52, local copies, waits for them, and re-layouts  13.9 us
    all_gather x2, waiting for transfers between devices, per_device(): chunks = [lax.all_gather(home, 'dp', axis=0) for home in homes]  12 us
    ppermute x2, waiting for transfers between devices, across_dp(): return lax.ppermute(value, 'dp', [(i, i ^ k) for i in range(owners)])  8.09 us
    ppermute x5, starting transfers between devices, to_chip(): lax.ppermute(value, 'tensor', [(i, i ^ k * CORES) for i in range(parts)])  7.98 us
  transfers between devices with their start and end apart: 24, of which 11 were waited for; matrix products, arithmetic and copies ran while one was open for 0% of the time, Pallas kernels for 23%

profile of v3, /device:TPU:0, one launch (start us, length us, event | category | flops | bytes accessed | tf_op | source)
XLA Modules:
  0.0 184.9 jit_solution(9949695862961588030)
XLA Ops:
  16.2 2.9 %collective-permute-start.1 = (f32[1,64,128]{2,1,0:T(8,128)S(1)}, f32[1,64,128]{2,1,0:T(8,128)S(1)}, u32[]{:S(2)}, u32[]{:S(2)}) collective-permute-start(f32[1,64,128]{2,1,0:T(8,128)S(1)} %slice_bitcast_fusion), channel_id=1, source_target_pairs={{0,2},{1,3},{2,0},{3,1},{4,6},{5,7},{6,4},{7,5},{8,10},{9,11},{10,... | collective-permute-start | bytes 98312 | tf_op jit(solution)/shard_map/ppermute | solution.py:481
  19.1 1.9 %collective-permute-done.1 = f32[1,64,128]{2,1,0:T(8,128)S(1)} collective-permute-done((f32[1,64,128]{2,1,0:T(8,128)S(1)}, f32[1,64,128]{2,1,0:T(8,128)S(1)}, u32[]{:S(2)}, u32[]{:S(2)}) %collective-permute-start.1) | collective-permute-done | bytes 32800 | tf_op jit(solution)/shard_map/ppermute | solution.py:481
  21.0 2.2 %collective-permute-start.2 = (f32[2,1,64,128]{3,2,1,0:T(8,128)S(1)}, f32[2,1,64,128]{3,2,1,0:T(8,128)S(1)}, u32[]{:S(2)}, u32[]{:S(2)}) collective-permute-start(f32[2,1,64,128]{3,2,1,0:T(8,128)S(1)} %pad_maximum_fusion.refs_0_), channel_id=1, source_target_pairs={{0,4},{4,0},{8,12},{12,8},{1,5},{5,1},{9,13},{13,9},{2,6},{6,2},{1... | collective-permute-start | bytes 196616 | tf_op jit(solution)/shard_map/ppermute | solution.py:484
  23.2 2.9 %first_hop.1 = (bf16[64,2048]{1,0:T(8,128)(2,1)}, bf16[64,2048]{1,0:T(8,128)(2,1)}, bf16[64,2048]{1,0:T(8,128)(2,1)}, bf16[64,2048]{1,0:T(8,128)(2,1)}) custom-call(s32[14]{0:T(128)} %copy-done.9, bf16[384,2048]{1,0:T(8,128)(2,1)} %tokens_ref.13), custom_call_target="tpu_custom_call" | custom-call | bytes 2097152 | tf_op jit(solution)/shard_map/first_hop/pallas_call | solution.py:148
  26.1 1.9 %collective-permute-start.10 = (bf16[64,2048]{1,0:T(8,128)(2,1)}, bf16[64,2048]{1,0:T(8,128)(2,1)S(1)}, u32[]{:S(2)}, u32[]{:S(2)}) collective-permute-start(bf16[64,2048]{1,0:T(8,128)(2,1)} %get-tuple-element.34), channel_id=1, source_target_pairs={{12,8},{0,4},{13,9},{1,5},{14,10},{2,6},{15,11},{3,7},{28,24},{16,... | collective-permute-start | bytes 786440 | tf_op jit(solution)/shard_map/ppermute | solution.py:171
  28.7 2.6 %collective-permute-start.3 = (f32[2,1,64,128]{3,2,1,0:T(8,128)S(1)}, f32[2,1,64,128]{3,2,1,0:T(8,128)S(1)}, u32[]{:S(2)}, u32[]{:S(2)}) collective-permute-start(f32[2,1,64,128]{3,2,1,0:T(8,128)S(1)} %fusion.2.sum_ref), channel_id=1, source_target_pairs={{0,8},{4,12},{8,0},{12,4},{1,9},{5,13},{9,1},{13,5},{2,10},{6,14},... | collective-permute-start | bytes 196616 | tf_op jit(solution)/shard_map/ppermute | solution.py:484
  31.4 8.1 %collective-permute-done.3.more_ref = f32[2,1,64,128]{3,2,1,0:T(8,128)S(1)} collective-permute-done((f32[2,1,64,128]{3,2,1,0:T(8,128)S(1)}, f32[2,1,64,128]{3,2,1,0:T(8,128)S(1)}, u32[]{:S(2)}, u32[]{:S(2)}) %collective-permute-start.3) | collective-permute-done | bytes 65568 | tf_op jit(solution)/shard_map/ppermute | solution.py:484
  40.1 1.7 pieces.1
  43.2 3.5 %second_hop.3 = (bf16[64,2048]{1,0:T(8,128)(2,1)}, bf16[64,2048]{1,0:T(8,128)(2,1)}) custom-call(s32[14]{0:T(128)} %copy-done.9, bf16[384,2048]{1,0:T(8,128)(2,1)} %tokens_ref.13, bf16[64,2048]{1,0:T(8,128)(2,1)} %copy-done.15, bf16[64,2048]{1,0:T(8,128)(2,1)} %copy-done.16, bf16[1,64,128]{2,1,0:T(8,128)(2,1)} %copy-done.12), custom_call_target="tpu_custom_call" | custom-call | bytes 1048576 | tf_op jit(solution)/shard_map/second_hop/pallas_call | solution.py:148
  46.7 1.9 %collective-permute-start.12 = (bf16[64,2048]{1,0:T(8,128)(2,1)}, bf16[64,2048]{1,0:T(8,128)(2,1)S(1)}, u32[]{:S(2)}, u32[]{:S(2)}) collective-permute-start(bf16[64,2048]{1,0:T(8,128)(2,1)} %get-tuple-element.36), channel_id=1, source_target_pairs={{4,0},{0,4},{12,8},{5,1},{1,5},{13,9},{6,2},{2,6},{14,10},{7,3},{3... | collective-permute-start | bytes 786440 | tf_op jit(solution)/shard_map/ppermute | solution.py:179
  49.3 5.9 %collective-permute-done.12.x_ref = bf16[64,2048]{1,0:T(8,128)(2,1)S(1)} collective-permute-done((bf16[64,2048]{1,0:T(8,128)(2,1)}, bf16[64,2048]{1,0:T(8,128)(2,1)S(1)}, u32[]{:S(2)}, u32[]{:S(2)}) %collective-permute-start.12) | collective-permute-done | bytes 262176 | tf_op jit(solution)/shard_map/ppermute | solution.py:179
  56.6 3.4 %settle.3 = bf16[64,2048]{1,0:T(8,128)(2,1)} custom-call(s32[14]{0:T(128)} %copy-done.9, bf16[384,2048]{1,0:T(8,128)(2,1)} %tokens_ref.13, bf16[64,2048]{1,0:T(8,128)(2,1)} %copy-done.18, bf16[64,2048]{1,0:T(8,128)(2,1)} %copy-done.20), custom_call_target="tpu_custom_call" | custom-call | bytes 524288 | tf_op jit(solution)/shard_map/settle/pallas_call | solution.py:148
  60.1 5.2 %collective-permute-start.4 = (bf16[64,2048]{1,0:T(8,128)(2,1)S(1)}, bf16[64,2048]{1,0:T(8,128)(2,1)S(1)}, u32[]{:S(2)}, u32[]{:S(2)}) collective-permute-start(bf16[64,2048]{1,0:T(8,128)(2,1)S(1)} %copy-done.25), channel_id=1, source_target_pairs={{12,8},{0,4},{13,9},{1,5},{14,10},{2,6},{15,11},{3,7},{28,24},{16,... | collective-permute-start | bytes 786440 | tf_op jit(solution)/shard_map/ppermute | solution.py:171
  66.0 3.2 %collective-permute-done.4.a_ref = bf16[64,2048]{1,0:T(8,128)(2,1)S(1)} collective-permute-done((bf16[64,2048]{1,0:T(8,128)(2,1)S(1)}, bf16[64,2048]{1,0:T(8,128)(2,1)S(1)}, u32[]{:S(2)}, u32[]{:S(2)}) %collective-permute-start.4) | collective-permute-done | bytes 262176 | tf_op jit(solution)/shard_map/ppermute | solution.py:171
  70.5 3.6 %second_hop.2 = (bf16[64,2048]{1,0:T(8,128)(2,1)}, bf16[64,2048]{1,0:T(8,128)(2,1)}) custom-call(s32[14]{0:T(128)} %copy-done.9, bf16[384,2048]{1,0:T(8,128)(2,1)} %tokens_ref.13, bf16[64,2048]{1,0:T(8,128)(2,1)} %copy-done.17, bf16[64,2048]{1,0:T(8,128)(2,1)} %copy-done.19, f32[2,1,64,128]{3,2,1,0:T(8,128)} %copy-done.14), custom_call_target="tpu_custom_call" | custom-call | bytes 1048576 | tf_op jit(solution)/shard_map/second_hop/pallas_call | solution.py:148
  74.1 5.0 %collective-permute-start.6 = (bf16[64,2048]{1,0:T(8,128)(2,1)}, bf16[64,2048]{1,0:T(8,128)(2,1)S(1)}, u32[]{:S(2)}, u32[]{:S(2)}) collective-permute-start(bf16[64,2048]{1,0:T(8,128)(2,1)} %get-tuple-element.29), channel_id=1, source_target_pairs={{4,0},{0,4},{12,8},{5,1},{1,5},{13,9},{6,2},{2,6},{14,10},{7,3},{3... | collective-permute-start | bytes 786440 | tf_op jit(solution)/shard_map/ppermute | solution.py:179
  79.8 13.8 %collective-permute-done.6.x_ref = bf16[64,2048]{1,0:T(8,128)(2,1)S(1)} collective-permute-done((bf16[64,2048]{1,0:T(8,128)(2,1)}, bf16[64,2048]{1,0:T(8,128)(2,1)S(1)}, u32[]{:S(2)}, u32[]{:S(2)}) %collective-permute-start.6) | collective-permute-done | bytes 262176 | tf_op jit(solution)/shard_map/ppermute | solution.py:179
  95.1 3.4 %settle.2 = bf16[64,2048]{1,0:T(8,128)(2,1)} custom-call(s32[14]{0:T(128)} %copy-done.9, bf16[384,2048]{1,0:T(8,128)(2,1)} %tokens_ref.13, bf16[64,2048]{1,0:T(8,128)(2,1)} %copy-done.21, bf16[64,2048]{1,0:T(8,128)(2,1)} %copy-done.22, f32[2,1,64,128]{3,2,1,0:T(8,128)} %copy-done.23), custom_call_target="tpu_custom_call" | custom-call | bytes 524288 | tf_op jit(solution)/shard_map/settle/pallas_call | solution.py:148
  99.7 11.9 %split_product.3 = (bf16[128,4096]{1,0:T(8,128)(2,1)}, f32[64,4096]{1,0:T(8,128)S(1)}, f32[64,4096]{1,0:T(8,128)S(1)}) custom-call(s32[14]{0:T(128)S(1)} %copy-done.11, bf16[4,64,2048]{2,1,0:T(8,128)(2,1)S(1)} %bitcast.17, bf16[2048,4096]{1,0:T(8,128)(2,1)} %w_ref.3), custom_call_target="tpu_custom_call" | custom-call | flops 4294967296 | bytes 20971520 | tf_op jit(solution)/shard_map/split_product/pallas_call | solution.py:219
  113.0 12.0 %all-gather.5.cloned.1.call-done = bf16[256,2048]{1,0:T(8,128)(2,1)} async-done(((bf16[64,2048]{1,0:T(8,128)(2,1)}), bf16[256,2048]{1,0:T(8,128)(2,1)}) %all-gather.5.cloned.1.call-update) | async-done | bytes 1048592 | tf_op jit(solution)/shard_map/all_gather | solution.py:524
  126.2 11.1 %split_product.2 = (bf16[128,4096]{1,0:T(8,128)(2,1)S(1)}, f32[64,4096]{1,0:T(8,128)S(1)}, f32[64,4096]{1,0:T(8,128)S(1)}) custom-call(s32[14]{0:T(128)S(1)} %copy-done.11, bf16[4,64,2048]{2,1,0:T(8,128)(2,1)S(1)} %bitcast.18, bf16[2048,4096]{1,0:T(8,128)(2,1)} %w_ref.3), custom_call_target="tpu_custom_call" | custom-call | flops 4294967296 | bytes 20971520 | tf_op jit(solution)/shard_map/split_product/pallas_call | solution.py:219
  143.0 21.1 %collective-permute-done.16.refs_1_ = bf16[1,64,128]{2,1,0:T(8,128)(2,1)S(1)} collective-permute-done((bf16[1,64,128]{2,1,0:T(8,128)(2,1)S(1)}, bf16[1,64,128]{2,1,0:T(8,128)(2,1)S(1)}, u32[]{:S(2)}, u32[]{:S(2)}) %collective-permute-start.16) | collective-permute-done | bytes 16416 | tf_op jit(solution)/shard_map/ppermute | solution.py:481
  167.9 6.9 %up_gradient.1 = f32[4,64,4096]{2,1,0:T(8,128)} custom-call(s32[14]{0:T(128)S(1)} %copy-done.11, bf16[1,64,4096]{2,1,0:T(8,128)(2,1)} %get-tuple-element.42.refs_0_, bf16[1,64,4096]{2,1,0:T(8,128)(2,1)} %collective-permute-done.19.refs_1_, bf16[1,64,4096]{2,1,0:T(8,128)(2,1)S(1)} %collective-permute-done.20.refs_2_, ...), custom_call_target="tpu_custom_call" | custom-call | bytes 6291456 | tf_op jit(solution)/shard_map/up_gradient/pallas_call | solution.py:384
  174.8 3.2 %finish.1 = bf16[128,4096]{1,0:T(8,128)(2,1)} custom-call(s32[14]{0:T(128)S(1)} %copy-done.11, bf16[1,64,128]{2,1,0:T(8,128)(2,1)S(1)} %copy-done.13, bf16[4,64,4096]{2,1,0:T(8,128)(2,1)S(1)} %copy-done.3, f32[64,4096]{1,0:T(8,128)S(1)} %get-tuple-element.31.refs_1_, bf16[128,4096]{1,0:T(8,128)(2,1)S(1)} %collective-permute-done.8.refs_2_, ...), custom_call_target="tpu_custom_call" | custom-call | flops 67108864 | bytes 7340032 | tf_op jit(solution)/shard_map/finish/pallas_call | solution.py:438
  (98 shorter events, 31.4 us)
Async XLA Ops:
  7.2 91.3 %all-gather.7.cloned.1.call-start = ((), (), s32[]{:S(2)}) async-start(), calls=%async_computation.1 | async-start | bytes 1310720 | tf_op jit(solution)/shard_map/all_gather | solution.py:524
  14.7 1.4 collective-permute-start
  16.2 4.8 %collective-permute-start.1 = (f32[1,64,128]{2,1,0:T(8,128)S(1)}, f32[1,64,128]{2,1,0:T(8,128)S(1)}, u32[]{:S(2)}, u32[]{:S(2)}) collective-permute-start(f32[1,64,128]{2,1,0:T(8,128)S(1)} %slice_bitcast_fusion), channel_id=1, source_target_pairs={{0,2},{1,3},{2,0},{3,1},{4,6},{5,7},{6,4},{7,5},{8,10},{9,11},{10,... | collective-permute-start | bytes 98312 | tf_op jit(solution)/shard_map/ppermute | solution.py:481
  21.0 7.7 %collective-permute-start.2 = (f32[2,1,64,128]{3,2,1,0:T(8,128)S(1)}, f32[2,1,64,128]{3,2,1,0:T(8,128)S(1)}, u32[]{:S(2)}, u32[]{:S(2)}) collective-permute-start(f32[2,1,64,128]{3,2,1,0:T(8,128)S(1)} %pad_maximum_fusion.refs_0_), channel_id=1, source_target_pairs={{0,4},{4,0},{8,12},{12,8},{1,5},{5,1},{9,13},{13,9},{2,6},{6,2},{1... | collective-permute-start | bytes 196616 | tf_op jit(solution)/shard_map/ppermute | solution.py:484
  26.1 16.3 %collective-permute-start.10 = (bf16[64,2048]{1,0:T(8,128)(2,1)}, bf16[64,2048]{1,0:T(8,128)(2,1)S(1)}, u32[]{:S(2)}, u32[]{:S(2)}) collective-permute-start(bf16[64,2048]{1,0:T(8,128)(2,1)} %get-tuple-element.34), channel_id=1, source_target_pairs={{12,8},{0,4},{13,9},{1,5},{14,10},{2,6},{15,11},{3,7},{28,24},{16,... | collective-permute-start | bytes 786440 | tf_op jit(solution)/shard_map/ppermute | solution.py:171
  28.0 14.4 %collective-permute-start.11 = (bf16[64,2048]{1,0:T(8,128)(2,1)}, bf16[64,2048]{1,0:T(8,128)(2,1)S(1)}, u32[]{:S(2)}, u32[]{:S(2)}) collective-permute-start(bf16[64,2048]{1,0:T(8,128)(2,1)} %get-tuple-element.35), channel_id=1, source_target_pairs={{8,4},{9,5},{10,6},{11,7},{24,20},{25,21},{26,22},{27,23}} | collective-permute-start | bytes 786440 | tf_op jit(solution)/shard_map/ppermute | solution.py:172
  28.7 10.7 %collective-permute-start.3 = (f32[2,1,64,128]{3,2,1,0:T(8,128)S(1)}, f32[2,1,64,128]{3,2,1,0:T(8,128)S(1)}, u32[]{:S(2)}, u32[]{:S(2)}) collective-permute-start(f32[2,1,64,128]{3,2,1,0:T(8,128)S(1)} %fusion.2.sum_ref), channel_id=1, source_target_pairs={{0,8},{4,12},{8,0},{12,4},{1,9},{5,13},{9,1},{13,5},{2,10},{6,14},... | collective-permute-start | bytes 196616 | tf_op jit(solution)/shard_map/ppermute | solution.py:484
  46.7 8.5 %collective-permute-start.12 = (bf16[64,2048]{1,0:T(8,128)(2,1)}, bf16[64,2048]{1,0:T(8,128)(2,1)S(1)}, u32[]{:S(2)}, u32[]{:S(2)}) collective-permute-start(bf16[64,2048]{1,0:T(8,128)(2,1)} %get-tuple-element.36), channel_id=1, source_target_pairs={{4,0},{0,4},{12,8},{5,1},{1,5},{13,9},{6,2},{2,6},{14,10},{7,3},{3... | collective-permute-start | bytes 786440 | tf_op jit(solution)/shard_map/ppermute | solution.py:179
  48.7 6.6 %collective-permute-start.13 = (bf16[64,2048]{1,0:T(8,128)(2,1)}, bf16[64,2048]{1,0:T(8,128)(2,1)S(1)}, u32[]{:S(2)}, u32[]{:S(2)}) collective-permute-start(bf16[64,2048]{1,0:T(8,128)(2,1)} %get-tuple-element.37), channel_id=1, source_target_pairs={{8,4},{4,8},{9,5},{5,9},{10,6},{6,10},{11,7},{7,11},{24,20},{20,24... | collective-permute-start | bytes 786440 | tf_op jit(solution)/shard_map/ppermute | solution.py:180
  60.0 65.0 %all-gather.5.cloned.1.call-start = ((), (), s32[]{:S(2)}) async-start(), calls=%async_computation | async-start | bytes 1310720 | tf_op jit(solution)/shard_map/all_gather | solution.py:524
  60.1 9.0 %collective-permute-start.4 = (bf16[64,2048]{1,0:T(8,128)(2,1)S(1)}, bf16[64,2048]{1,0:T(8,128)(2,1)S(1)}, u32[]{:S(2)}, u32[]{:S(2)}) collective-permute-start(bf16[64,2048]{1,0:T(8,128)(2,1)S(1)} %copy-done.25), channel_id=1, source_target_pairs={{12,8},{0,4},{13,9},{1,5},{14,10},{2,6},{15,11},{3,7},{28,24},{16,... | collective-permute-start | bytes 786440 | tf_op jit(solution)/shard_map/ppermute | solution.py:171
  65.3 3.9 %collective-permute-start.5 = (bf16[64,2048]{1,0:T(8,128)(2,1)S(1)}, bf16[64,2048]{1,0:T(8,128)(2,1)S(1)}, u32[]{:S(2)}, u32[]{:S(2)}) collective-permute-start(bf16[64,2048]{1,0:T(8,128)(2,1)S(1)} %copy-done.24), channel_id=1, source_target_pairs={{8,4},{9,5},{10,6},{11,7},{24,20},{25,21},{26,22},{27,23}} | collective-permute-start | bytes 786440 | tf_op jit(solution)/shard_map/ppermute | solution.py:172
  74.1 19.6 %collective-permute-start.6 = (bf16[64,2048]{1,0:T(8,128)(2,1)}, bf16[64,2048]{1,0:T(8,128)(2,1)S(1)}, u32[]{:S(2)}, u32[]{:S(2)}) collective-permute-start(bf16[64,2048]{1,0:T(8,128)(2,1)} %get-tuple-element.29), channel_id=1, source_target_pairs={{4,0},{0,4},{12,8},{5,1},{1,5},{13,9},{6,2},{2,6},{14,10},{7,3},{3... | collective-permute-start | bytes 786440 | tf_op jit(solution)/shard_map/ppermute | solution.py:179
  79.1 14.5 %collective-permute-start.7 = (bf16[64,2048]{1,0:T(8,128)(2,1)}, bf16[64,2048]{1,0:T(8,128)(2,1)S(1)}, u32[]{:S(2)}, u32[]{:S(2)}) collective-permute-start(bf16[64,2048]{1,0:T(8,128)(2,1)} %get-tuple-element.30), channel_id=1, source_target_pairs={{8,4},{4,8},{9,5},{5,9},{10,6},{6,10},{11,7},{7,11},{24,20},{20,24... | collective-permute-start | bytes 786440 | tf_op jit(solution)/shard_map/ppermute | solution.py:180
  111.6 26.5 %collective-permute-start.14 = (bf16[128,4096]{1,0:T(8,128)(2,1)}, bf16[128,4096]{1,0:T(8,128)(2,1)S(1)}, u32[]{:S(2)}, u32[]{:S(2)}) collective-permute-start(bf16[128,4096]{1,0:T(8,128)(2,1)} %get-tuple-element.39), channel_id=1, source_target_pairs={{0,1},{1,0},{2,3},{3,2},{4,5},{5,4},{6,7},{7,6},{8,9},{9,8},{10,11... | collective-permute-start | bytes 3145736 | tf_op jit(solution)/shard_map/ppermute | solution.py:478
  111.6 26.4 %collective-permute-start.19 = (bf16[1,64,4096]{2,1,0:T(8,128)(2,1)}, bf16[1,64,4096]{2,1,0:T(8,128)(2,1)}, u32[]{:S(2)}, u32[]{:S(2)}) collective-permute-start(bf16[1,64,4096]{2,1,0:T(8,128)(2,1)} %get-tuple-element.42.refs_0_), channel_id=1, source_target_pairs={{0,2},{1,3},{2,0},{3,1},{4,6},{5,7},{6,4},{7,5},{8,10},{9,11},{10,... | collective-permute-start | bytes 1572872 | tf_op jit(solution)/shard_map/ppermute | solution.py:481
  137.4 3.4 %collective-permute-start.8 = (bf16[128,4096]{1,0:T(8,128)(2,1)S(1)}, bf16[128,4096]{1,0:T(8,128)(2,1)S(1)}, u32[]{:S(2)}, u32[]{:S(2)}) collective-permute-start(bf16[128,4096]{1,0:T(8,128)(2,1)S(1)} %get-tuple-element.32), channel_id=1, source_target_pairs={{0,1},{1,0},{2,3},{3,2},{4,5},{5,4},{6,7},{7,6},{8,9},{9,8},{10,11... | collective-permute-start | bytes 3145736 | tf_op jit(solution)/shard_map/ppermute | solution.py:478
  137.5 30.4 %collective-permute-start.20 = (bf16[1,64,4096]{2,1,0:T(8,128)(2,1)}, bf16[1,64,4096]{2,1,0:T(8,128)(2,1)S(1)}, u32[]{:S(2)}, u32[]{:S(2)}) collective-permute-start(bf16[1,64,4096]{2,1,0:T(8,128)(2,1)} %get-tuple-element.42.refs_0_), channel_id=1, source_target_pairs={{0,1},{1,0},{2,3},{3,2},{4,5},{5,4},{6,7},{7,6},{8,9},{9,8},{10,11... | collective-permute-start | bytes 1572872 | tf_op jit(solution)/shard_map/ppermute | solution.py:478
  138.0 29.9 %collective-permute-start.21 = (bf16[1,64,4096]{2,1,0:T(8,128)(2,1)}, bf16[1,64,4096]{2,1,0:T(8,128)(2,1)S(1)}, u32[]{:S(2)}, u32[]{:S(2)}) collective-permute-start(bf16[1,64,4096]{2,1,0:T(8,128)(2,1)} %collective-permute-done.19.refs_1_), channel_id=1, source_target_pairs={{0,1},{1,0},{2,3},{3,2},{4,5},{5,4},{6,7},{7,6},{8,9},{9,8},{10,11... | collective-permute-start | bytes 1572872 | tf_op jit(solution)/shard_map/ppermute | solution.py:478
  138.2 36.6 %collective-permute-start.15 = (bf16[64,4096]{1,0:T(8,128)(2,1)S(1)}, bf16[64,4096]{1,0:T(8,128)(2,1)S(1)}, u32[]{:S(2)}, u32[]{:S(2)}) collective-permute-start(bf16[64,4096]{1,0:T(8,128)(2,1)S(1)} %add_convert_fusion), channel_id=1, source_target_pairs={{0,2},{1,3},{2,0},{3,1},{4,6},{5,7},{6,4},{7,5},{8,10},{9,11},{10,... | collective-permute-start | bytes 1572872 | tf_op jit(solution)/shard_map/ppermute | solution.py:481
  140.9 33.9 %collective-permute-start.9 = (bf16[64,4096]{1,0:T(8,128)(2,1)S(1)}, bf16[64,4096]{1,0:T(8,128)(2,1)S(1)}, u32[]{:S(2)}, u32[]{:S(2)}) collective-permute-start(bf16[64,4096]{1,0:T(8,128)(2,1)S(1)} %add_convert_fusion.1), channel_id=1, source_target_pairs={{0,2},{1,3},{2,0},{3,1},{4,6},{5,7},{6,4},{7,5},{8,10},{9,11},{10,... | collective-permute-start | bytes 1572872 | tf_op jit(solution)/shard_map/ppermute | solution.py:481
  142.5 21.6 %collective-permute-start.16 = (bf16[1,64,128]{2,1,0:T(8,128)(2,1)S(1)}, bf16[1,64,128]{2,1,0:T(8,128)(2,1)S(1)}, u32[]{:S(2)}, u32[]{:S(2)}) collective-permute-start(bf16[1,64,128]{2,1,0:T(8,128)(2,1)S(1)} %get-tuple-element.41.refs_0_), channel_id=1, source_target_pairs={{0,2},{1,3},{2,0},{3,1},{4,6},{5,7},{6,4},{7,5},{8,10},{9,11},{10,... | collective-permute-start | bytes 49160 | tf_op jit(solution)/shard_map/ppermute | solution.py:481
  164.1 1.2 collective-permute-start.17
  165.3 1.2 collective-permute-start.18
  (26 other events, 354.2 us)
Sparse Core Ops, SparseCore 0:
  60.2 34.0 all-gather.6
  98.6 26.3 all-gather.4

commit v4 on v3

--- a/solution.py
+++ b/solution.py
@@ -11,6 +11,7 @@
 CAP = 3
 CORES = 2
 CHUNK_ROWS = (64, 64)
+PARTS = 2
 MIB = 2**20
 
 adapter_scale = 0.5
@@ -83,15 +84,14 @@
         copy.wait()
 
 
-def first_hop_kernel(index_of, starts, index_ref, tokens_ref, *refs):
-    outs, sems = refs[:-1], refs[-1]
+def first_hop_kernel(index_of, start, index_ref, tokens_ref, *refs):
+    a_ref, b_ref, sems = refs[-3:]
     index = index_of(index_ref)
     inward = jnp.where(index.place == 0, 2, 1)
     run_all(
         [
-            own_copy(index, block, start, tokens_ref, outs[2 * c + j], sems.at[2 * c + j])
-            for c, start in enumerate(starts)
-            for j, block in enumerate((inward, 0))
+            own_copy(index, inward, start, tokens_ref, a_ref, sems.at[0]),
+            own_copy(index, 0, start, tokens_ref, b_ref, sems.at[1]),
         ]
     )
 
@@ -136,59 +136,75 @@
         out_ref[...] = y_ref[...]
 
 
-def blocks_at_home(index_of, index, tokens, beside):
-    width = tokens.shape[1]
-    starts = [sum(CHUNK_ROWS[:c]) for c in range(len(CHUNK_ROWS))]
-    hbm = pl.BlockSpec(memory_space=pl.ANY)
-    vmem = pl.BlockSpec(memory_space=pltpu.VMEM)
-    beside = list(beside)
-
-    def call(kernel, outs, received, name):
-        extra = tuple(beside.pop(0)()) if beside and received else ()
-        return pl.pallas_call(
-            kernel,
-            grid_spec=pltpu.PrefetchScalarGridSpec(
-                num_scalar_prefetch=1,
-                grid=(),
-                in_specs=[hbm] + [vmem] * len(received) + [hbm] * len(extra),
-                out_specs=[vmem] * len(outs),
-                scratch_shapes=[pltpu.SemaphoreType.DMA((len(outs),))],
-            ),
-            out_shape=outs,
-            cost_estimate=cost(0, 4 * sum(o.size for o in outs)),
-            name=name,
-        )(index, tokens, *received, *extra)
-
-    sends = call(
-        functools.partial(first_hop_kernel, index_of, starts),
-        [shape_of((count, width), tokens.dtype) for count in CHUNK_ROWS for _ in range(2)],
-        (),
-        "first_hop",
-    )
-    homes = []
-    for c, (start, count) in enumerate(zip(starts, CHUNK_ROWS)):
-        unit = shape_of((count, width), tokens.dtype)
-        inward = lax.ppermute(sends[2 * c], "dp", [(3, 2), (0, 1)])
-        left = lax.ppermute(sends[2 * c + 1], "dp", [(2, 1)])
-        outer, middle = call(
-            functools.partial(second_hop_kernel, index_of, start),
-            [unit, unit],
-            (inward, left),
-            "second_hop",
-        )
-        outer = lax.ppermute(outer, "dp", [(1, 0), (0, 1), (3, 2)])
-        middle = lax.ppermute(middle, "dp", [(2, 1), (1, 2)])
-        (home,) = call(
-            functools.partial(settle_kernel, index_of, start),
-            [unit],
-            (outer, middle),
-            "settle",
-        )
-        homes.append(home)
-    return homes
-
-
-def split_product_kernel(index_of, index_ref, x_ref, w_ref, send_ref, other_ref, own_ref):
+def after(values):
+    specs = [
+        pl.BlockSpec((1,) * (v.ndim - 2) + (16, 128), lambda *_, n=v.ndim: (0,) * n) for v in values
+    ]
+    return specs, list(values)
+
+
+def hop_call(kernel, index, tokens, outs, received, waits, name):
+    specs, extra = after(waits)
+    return pl.pallas_call(
+        kernel,
+        grid_spec=pltpu.PrefetchScalarGridSpec(
+            num_scalar_prefetch=1,
+            grid=(1,),
+            in_specs=[pl.BlockSpec(memory_space=pl.ANY)]
+            + [whole(r.shape) for r in received]
+            + specs,
+            out_specs=[whole(o.shape) for o in outs],
+            scratch_shapes=[pltpu.SemaphoreType.DMA((len(outs),))],
+        ),
+        out_shape=outs,
+        cost_estimate=cost(0, 4 * sum(o.size for o in outs)),
+        name=name,
+    )(index, tokens, *received, *extra)
+
+
+class Homing:
+    def __init__(self, index_of, index, tokens, chunk):
+        self.index_of, self.index, self.tokens = index_of, index, tokens
+        self.start = sum(CHUNK_ROWS[:chunk])
+        self.unit = shape_of((CHUNK_ROWS[chunk], tokens.shape[1]), tokens.dtype)
+
+    def call(self, kernel, count, received, waits, name):
+        return hop_call(
+            functools.partial(kernel, self.index_of, self.start),
+            self.index,
+            self.tokens,
+            [self.unit] * count,
+            received,
+            waits,
+            name,
+        )
+
+    def first(self, waits=()):
+        inward, left = self.call(first_hop_kernel, 2, (), waits, "first_hop")
+        self.sent = inward
+        self.received = (
+            lax.ppermute(inward, "dp", [(3, 2), (0, 1)]),
+            lax.ppermute(left, "dp", [(2, 1)]),
+        )
+
+    def second(self, waits=()):
+        outer, middle = self.call(second_hop_kernel, 2, self.received, waits, "second_hop")
+        self.sent = outer
+        self.received = (
+            lax.ppermute(outer, "dp", [(1, 0), (0, 1), (3, 2)]),
+            lax.ppermute(middle, "dp", [(2, 1), (1, 2)]),
+        )
+
+    def settle(self, waits=()):
+        (self.sent,) = self.call(settle_kernel, 1, self.received, waits, "settle")
+        return self.sent
+
+
+STREAMS = 4
+
+
+def split_product_kernel(index_of, index_ref, x_ref, *refs):
+    w_refs, (send_ref, other_ref, own_ref) = refs[:STREAMS], refs[-3:]
     index = index_of(index_ref)
     each = index.per_part * x_ref.shape[1]
     rows = [
@@ -198,7 +214,9 @@
         for i in range(index.per_part)
     ]
     total = jnp.dot(
-        jnp.concatenate(rows, axis=0), w_ref[...], preferred_element_type=jnp.float32
+        jnp.concatenate(rows, axis=0),
+        jnp.concatenate([w[...] for w in w_refs], axis=0),
+        preferred_element_type=jnp.float32,
     )
     half = index.chips * each
     send_ref[...] = total[:half].astype(send_ref.dtype)
@@ -206,22 +224,27 @@
     other_ref[...] = total[half + each :]
 
 
-def split_product(index_of, index, shape, rows, weight):
+def split_product(index_of, index, shape, rows, weight, part, part_count, waits):
     block_count, count, depth = rows.shape
-    width = weight.shape[1]
+    width = weight.shape[1] // part_count
     tile = 512
     each = shape.per_part * count
     half = block_count * count // 2
+    specs, extra = after(waits)
 
     def columns(height):
         return pl.BlockSpec((height, tile), lambda n, _: (0, n))
+
+    def stream(i):
+        first = part * (width // tile)
+        return pl.BlockSpec((depth // STREAMS, tile), lambda n, _: (i, first + n))
 
     return pl.pallas_call(
         functools.partial(split_product_kernel, index_of),
         grid_spec=pltpu.PrefetchScalarGridSpec(
             num_scalar_prefetch=1,
             grid=(width // tile,),
-            in_specs=[whole(rows.shape), columns(depth)],
+            in_specs=[whole(rows.shape)] + [stream(i) for i in range(STREAMS)] + specs,
             out_specs=[columns(half), columns(half - each), columns(each)],
         ),
         out_shape=[
@@ -234,10 +257,11 @@
             4 * half * depth * width, 2 * depth * (2 * half + width) + 6 * half * width
         ),
         name="split_product",
-    )(index, rows, weight)
-
-
-def narrow_kernel(index_of, index_ref, tokens_ref, down_ref, cot_ref, up_ref, send_ref, keep_ref, back_ref, low):
+    )(index, rows, *[weight] * STREAMS, *extra)
+
+
+def narrow_kernel(index_of, index_ref, tokens_ref, down_ref, cot_ref, up_ref, *refs):
+    send_ref, keep_ref, back_ref, low = refs[-4:]
     index = index_of(index_ref)
     for m in range(CAP):
         low[m] = lax.dot_general(
@@ -262,17 +286,18 @@
         )
 
 
-def narrow(index_of, index, shape, tokens, down, cotangent, up):
+def narrow(index_of, index, shape, tokens, down, cotangent, up, waits):
     rank = up.shape[1]
     one = (shape.per_part, rank, BLK)
     outs = [(shape.chips,) + one, (shape.chips,) + one, one]
     operands = (tokens, down, cotangent, up)
+    specs, extra = after(waits)
     return pl.pallas_call(
         functools.partial(narrow_kernel, index_of),
         grid_spec=pltpu.PrefetchScalarGridSpec(
             num_scalar_prefetch=1,
             grid=(1,),
-            in_specs=[whole(o.shape) for o in operands],
+            in_specs=[whole(o.shape) for o in operands] + specs,
             out_specs=[whole(o) for o in outs],
             scratch_shapes=[pltpu.VMEM((CAP, rank, BLK), jnp.float32)],
         ),
@@ -280,7 +305,7 @@
         compiler_params=pltpu.CompilerParams(vmem_limit_bytes=24 * MIB),
         cost_estimate=cost(2 * rank * (tokens.size + cotangent.size), 2 * sum(o.size for o in operands)),
         name="narrow",
-    )(index, *operands)
+    )(index, *operands, *extra)
 
 
 def pieces_kernel(index_of, index_ref, sum_ref, more_ref, cot_ref, low_ref, back_ref, piece_ref):
@@ -379,7 +404,7 @@
 
 def up_gradient(index_of, index, adapter_count, pieces):
     per_part, rank, width = pieces[0].shape
-    tile = 512
+    tile = 1024
     out = (adapter_count, rank, width)
     return pl.pallas_call(
         functools.partial(up_gradient_kernel, index_of),
@@ -420,36 +445,56 @@
             start += count
 
 
-def finish(index_of, index, lowered, up, sums):
+def finish(index_of, index, lowered, up, sums, part, part_count, projected):
     per_part = lowered.shape[0]
-    adapter_count, rank, width = up.shape
-    tile = 1024
-    flat = [s for chunk in sums for s in chunk]
-    heights = [per_part * count for chunk, count in zip(sums, CHUNK_ROWS) for _ in chunk]
+    _, rank, width = up.shape
+    tile = min(1024, width // part_count)
+    tiles = width // part_count // tile
+    first = part * tiles
     out = (per_part * BLK, width)
 
     def factor(i):
         def at(n, index_ref):
             index = index_of(index_ref)
-            return (index.owner(index.block(0, 0, i)), 0, n)
+            return (index.owner(index.block(0, 0, i)), 0, first + n)
 
         return pl.BlockSpec((1, rank, tile), at)
 
+    specs, flat = [], []
+    for chunk, count in zip(sums, CHUNK_ROWS):
+        for value in chunk:
+            begin = first if value.shape[1] == width else 0
+            specs.append(
+                pl.BlockSpec((per_part * count, tile), lambda n, _, begin=begin: (0, begin + n))
+            )
+            flat.append(value)
+    kernel = functools.partial(finish_kernel, index_of, CHUNK_ROWS)
+    operands = [index, lowered, *[up] * per_part, *flat]
+    aliases = {}
+    if projected is not None:
+        aliases = {len(operands): 0}
+        operands.append(projected)
+        specs.append(pl.BlockSpec(memory_space=pl.ANY))
+
+        def kernel(*refs):
+            finish_kernel(index_of, CHUNK_ROWS, *refs[:-2], refs[-1])
+
     return pl.pallas_call(
-        functools.partial(finish_kernel, index_of, CHUNK_ROWS),
+        kernel,
         grid_spec=pltpu.PrefetchScalarGridSpec(
             num_scalar_prefetch=1,
-            grid=(width // tile,),
-            in_specs=[whole(lowered.shape)]
-            + [factor(i) for i in range(per_part)]
-            + [pl.BlockSpec((height, tile), lambda n, _: (0, n)) for height in heights],
-            out_specs=pl.BlockSpec((out[0], tile), lambda n, _: (0, n)),
+            grid=(tiles,),
+            in_specs=[whole(lowered.shape)] + [factor(i) for i in range(per_part)] + specs,
+            out_specs=pl.BlockSpec((out[0], tile), lambda n, _: (0, first + n)),
         ),
         out_shape=shape_of(out, jnp.bfloat16),
+        input_output_aliases=aliases,
         compiler_params=pltpu.CompilerParams(vmem_limit_bytes=24 * MIB),
-        cost_estimate=cost(2 * rank * out[0] * width, 10 * out[0] * width + 2 * up.size),
+        cost_estimate=cost(
+            2 * rank * out[0] * tiles * tile, (10 * out[0] + 2 * rank) * tiles * tile
+        ),
         name="finish",
-    )(index, lowered, *[up] * per_part, *flat)
+    )(*operands)
 
 
 def per_device(
@@ -487,10 +532,8 @@
         same_core = [value] + [to_chip(value, k) for k in range(1, chips)]
         return same_core + [to_other_core(v) for v in same_core]
 
-    steps = {}
-
-    def first_step():
-        steps["send"], steps["keep"], steps["back"] = narrow(
+    def small_products(waits):
+        return narrow(
             index_of,
             index,
             shape,
@@ -498,54 +541,78 @@
             jnp.swapaxes(adapter_down_factor, 1, 2),
             cotangent,
             adapter_up_factor,
-        )
-        return [steps["send"]]
-
-    def second_step():
-        low_chip = steps["keep"] + to_other_core(steps["send"])
+            waits,
+        )
+
+    def over_parts(send, keep):
+        low_chip = keep + to_other_core(send)
         low_part = low_chip[0]
         for k in range(1, chips):
             low_part = low_part + to_chip(low_chip[k], k)
-        steps["total"] = jnp.stack([low_part, steps["back"]])
-        return [steps["total"]]
-
-    def third_step():
-        total, k = steps["total"], 1
+        return low_part
+
+    def over_dp(low_part, back):
+        total, k = jnp.stack([low_part, back]), 1
         while 2 * k < owners:
             total = total + across_dp(total, k)
             k *= 2
-        steps["small"] = make_pieces(
-            index_of, index, shape, total, across_dp(total, k), cotangent
-        )
-        return [steps["small"][0]]
+        return make_pieces(index_of, index, shape, total, across_dp(total, k), cotangent)
 
     if owners == 4 and block_count == 4:
-        homes = blocks_at_home(index_of, index, tokens, [first_step, second_step, third_step])
+        head = Homing(index_of, index, tokens, 0)
+        tail = [Homing(index_of, index, tokens, c) for c in range(1, len(CHUNK_ROWS))]
+        head.first()
+        send, keep, back = small_products([head.sent])
+        head.second([send])
+        low_part = over_parts(send, keep)
+        homes = [head.settle([low_part])]
+        for homing in tail:
+            homing.first([homes[-1]])
+            homing.second()
+            homes.append(homing.settle())
+        lowered, back_rows, pieces = over_dp(low_part, back)
         chunks = [lax.all_gather(home, "dp", axis=0) for home in homes]
     else:
-        first_step(), second_step(), third_step()
+        send, keep, back = small_products([])
+        lowered, back_rows, pieces = over_dp(over_parts(send, keep), back)
         every_slot = lax.all_gather(
             tokens.reshape(CAP, BLK, width_dev), "dp", axis=0, tiled=True
         )
         picked = every_slot[adapter_of_block * CAP + slot_of_block]
         starts = [sum(CHUNK_ROWS[:c]) for c in range(len(CHUNK_ROWS))]
         chunks = [picked[:, s : s + count] for s, count in zip(starts, CHUNK_ROWS)]
-    lowered, back_rows, pieces = steps["small"]
+
+    def summed(rows, part, part_count, waits):
+        each = shape.per_part * rows.shape[1]
+        send, other, own = split_product(
+            index_of, index, shape, rows, frozen_up_weight, part, part_count, waits
+        )
+        arrived = to_other_core(send)
+        outgoing = (other + arrived[each:].astype(jnp.float32)).astype(jnp.bfloat16)
+        return [own, arrived] + [
+            to_chip(outgoing[(k - 1) * each : k * each], k) for k in range(1, chips)
+        ]
+
+    sums = [summed(rows, 0, 1, [pieces]) for rows in chunks[:-1]]
     up_grad = up_gradient(index_of, index, adapter_count, every_part(pieces))
     down_grad = down_gradient(index_of, index, tokens, every_part(back_rows))
-
-    sums = []
-    for rows in chunks:
-        count = rows.shape[1]
-        each = shape.per_part * count
-        send, other, own = split_product(index_of, index, shape, rows, frozen_up_weight)
-        arrived = to_other_core(send)
-        outgoing = (other + arrived[each:].astype(jnp.float32)).astype(jnp.bfloat16)
-        sums.append(
-            [own, arrived]
-            + [to_chip(outgoing[(k - 1) * each : k * each], k) for k in range(1, chips)]
-        )
-    projected = finish(index_of, index, lowered, adapter_up_factor, sums)
+    waits = [up_grad, down_grad] + [chunk[-1] for chunk in sums]
+    last = []
+    for part in range(PARTS):
+        last.append(summed(chunks[-1], part, PARTS, waits))
+        waits = []
+    projected = None
+    for part in range(PARTS):
+        projected = finish(
+            index_of,
+            index,
+            lowered,
+            adapter_up_factor,
+            sums + [last[part]],
+            part,
+            PARTS,
+            projected,
+        )
     return (projected, jnp.swapaxes(down_grad, 1, 2), up_grad)
 
 

time: 186 us -> 192 us (1.032)
  waiting for transfers between devices: 70.2 us -> 64.1 us
  other arithmetic: 0.21 us -> 4.37 us
  local copies, waits for them, and re-layouts: 14.7 us -> 18.3 us
  Pallas kernels: 54.5 us -> 57.7 us
    ppermute x8, waiting for transfers between devices: 22.9 us -> 13 us  [the longest x2 8.87 us: second(): lax.ppermute(outer, 'dp', [(1, 0), (0, 1), (3, 2)])]
    all_gather x2, waiting for transfers between devices: 12 us -> 19.1 us  [per_device(): chunks = [lax.all_gather(home, 'dp', axis=0) for home in homes]]
    pallas_call x6 -> x8, Pallas kernels: 19.9 us -> 23.9 us  [the longest x6 19.7 us: hop_call(): pl.pallas_call(kernel, grid_spec=pltpu.PrefetchScalarGridSpec(num_scalar_...]
    unnamed x52, local copies, waits for them, and re-layouts: 13.9 us -> 16.9 us
    ppermute x2, waiting for transfers between devices: 8.09 us -> 5.75 us  [across_dp(): return lax.ppermute(value, 'dp', [(i, i ^ k) for i in range(owners)])]
    convert_element_type x2 -> x3, other arithmetic: 0.18 us -> 2.22 us  [summed(): outgoing = (other + arrived[each:].astype(jnp.float32)).astype(jnp.bfloat16)]
    ppermute x7 -> x8, waiting for transfers between devices: 4.26 us -> 2.53 us  [to_other_core(): return lax.ppermute(value, 'tensor', [(i, i ^ 1) for i in range(parts)])]
    pallas_call x2 -> x3, Pallas kernels: 23 us -> 23.9 us  [split_product(): pl.pallas_call(functools.partial(split_product_kernel, index_of), grid_sp...]
  transfers between devices with their start and end apart: 24 -> 26, of which waited for: 11 -> 14; matrix products, arithmetic and copies ran while one was open for 0% -> 2% of each run, Pallas kernels for 23% -> 15%
where the time goes in v4:
time: 192 us; the launch traced here: 191 us
  waiting for transfers between devices  64.1 us (33%)
  Pallas kernels  57.7 us (30%)
  starting transfers between devices  31.9 us (17%)
  local copies, waits for them, and re-layouts  18.3 us (10%)
  between operations  14.3 us (7%)
  other arithmetic  4.37 us (2%)
    pallas_call x3, Pallas kernels, split_product(): pl.pallas_call(functools.partial(split_product_kernel, index_of), grid_sp...  23.9 us
    ppermute x6, waiting for transfers between devices, to_chip(): lax.ppermute(value, 'tensor', [(i, i ^ k * CORES) for i in range(parts)])  23.7 us
    pallas_call x6, Pallas kernels, hop_call(): pl.pallas_call(kernel, grid_spec=pltpu.PrefetchScalarGridSpec(num_scalar_...  19.7 us
    all_gather x2, waiting for transfers between devices, per_device(): chunks = [lax.all_gather(home, 'dp', axis=0) for home in homes]  19.1 us
    unnamed x52, local copies, waits for them, and re-layouts  16.9 us
    ppermute x2, waiting for transfers between devices, second(): lax.ppermute(outer, 'dp', [(1, 0), (0, 1), (3, 2)])  8.87 us
    ppermute x2, starting transfers between devices, first(): lax.ppermute(inward, 'dp', [(3, 2), (0, 1)])  8.26 us
    ppermute x6, starting transfers between devices, to_chip(): lax.ppermute(value, 'tensor', [(i, i ^ k * CORES) for i in range(parts)])  8.21 us
  transfers between devices with their start and end apart: 26, of which 14 were waited for; matrix products, arithmetic and copies ran while one was open for 2% of the time, Pallas kernels for 15%

profile of v4, /device:TPU:0, one launch (start us, length us, event | category | flops | bytes accessed | tf_op | source)
XLA Modules:
  0.0 190.8 jit_solution(6252963499007420630)
XLA Ops:
  8.6 2.5 %first_hop.2 = (bf16[64,2048]{1,0:T(8,128)(2,1)}, bf16[64,2048]{1,0:T(8,128)(2,1)}) custom-call(s32[14]{0:T(128)} %concatenate.3.index_ref.refs_0_, bf16[384,2048]{1,0:T(8,128)(2,1)} %tokens_ref.15), custom_call_target="tpu_custom_call" | custom-call | bytes 1048576 | tf_op jit(solution)/shard_map/first_hop/pallas_call | solution.py:148
  11.1 4.9 %collective-permute-start.4 = (bf16[64,2048]{1,0:T(8,128)(2,1)}, bf16[64,2048]{1,0:T(8,128)(2,1)S(1)}, u32[]{:S(2)}, u32[]{:S(2)}) collective-permute-start(bf16[64,2048]{1,0:T(8,128)(2,1)} %get-tuple-element.26.refs_0_), channel_id=1, source_target_pairs={{12,8},{0,4},{13,9},{1,5},{14,10},{2,6},{15,11},{3,7},{28,24},{16,... | collective-permute-start | bytes 786440 | tf_op jit(solution)/shard_map/ppermute | solution.py:186
  27.9 3.5 %second_hop.2 = (bf16[64,2048]{1,0:T(8,128)(2,1)}, bf16[64,2048]{1,0:T(8,128)(2,1)}) custom-call(s32[14]{0:T(128)} %concatenate.3.index_ref.refs_0_, bf16[384,2048]{1,0:T(8,128)(2,1)} %tokens_ref.15, bf16[64,2048]{1,0:T(8,128)(2,1)} %copy-done.18, bf16[64,2048]{1,0:T(8,128)(2,1)} %copy-done.19, f32[2,1,64,128]{3,2,1,0:T(8,128)} %copy-done.17), custom_call_target="tpu_custom_call" | custom-call | bytes 1048576 | tf_op jit(solution)/shard_map/second_hop/pallas_call | solution.py:148
  35.6 2.4 %collective-permute-done.1 = f32[1,64,128]{2,1,0:T(8,128)S(1)} collective-permute-done((f32[1,64,128]{2,1,0:T(8,128)S(1)}, f32[1,64,128]{2,1,0:T(8,128)S(1)}, u32[]{:S(2)}, u32[]{:S(2)}) %collective-permute-start.1) | collective-permute-done | bytes 32800 | tf_op jit(solution)/shard_map/ppermute | solution.py:526
  38.6 3.2 %collective-permute-done.6.x_ref = bf16[64,2048]{1,0:T(8,128)(2,1)S(1)} collective-permute-done((bf16[64,2048]{1,0:T(8,128)(2,1)}, bf16[64,2048]{1,0:T(8,128)(2,1)S(1)}, u32[]{:S(2)}, u32[]{:S(2)}) %collective-permute-start.6) | collective-permute-done | bytes 262176 | tf_op jit(solution)/shard_map/ppermute | solution.py:194
  43.3 3.4 %settle.2.refs_0_ = bf16[64,2048]{1,0:T(8,128)(2,1)} custom-call(s32[14]{0:T(128)} %concatenate.3.index_ref.refs_0_, bf16[384,2048]{1,0:T(8,128)(2,1)} %tokens_ref.15, bf16[64,2048]{1,0:T(8,128)(2,1)} %copy-done.24, bf16[64,2048]{1,0:T(8,128)(2,1)} %copy-done.25, f32[1,64,128]{2,1,0:T(8,128)} %fusion.refs_0_), custom_call_target="tpu_custom_call" | custom-call | bytes 524288 | tf_op jit(solution)/shard_map/settle/pallas_call | solution.py:148
  47.5 3.0 %collective-permute-start.2 = (f32[2,1,64,128]{3,2,1,0:T(8,128)S(1)}, f32[2,1,64,128]{3,2,1,0:T(8,128)S(1)}, u32[]{:S(2)}, u32[]{:S(2)}) collective-permute-start(f32[2,1,64,128]{3,2,1,0:T(8,128)S(1)} %pad_maximum_fusion), channel_id=1, source_target_pairs={{0,4},{4,0},{8,12},{12,8},{1,5},{5,1},{9,13},{13,9},{2,6},{6,2},{1... | collective-permute-start | bytes 196616 | tf_op jit(solution)/shard_map/ppermute | solution.py:529
  55.3 3.5 %collective-permute-done.3.more_ref = f32[2,1,64,128]{3,2,1,0:T(8,128)S(1)} collective-permute-done((f32[2,1,64,128]{3,2,1,0:T(8,128)S(1)}, f32[2,1,64,128]{3,2,1,0:T(8,128)S(1)}, u32[]{:S(2)}, u32[]{:S(2)}) %collective-permute-start.3) | collective-permute-done | bytes 65568 | tf_op jit(solution)/shard_map/ppermute | solution.py:529
  60.5 15.5 %all-gather.5.cloned.1.call-done = bf16[256,2048]{1,0:T(8,128)(2,1)} async-done(((bf16[64,2048]{1,0:T(8,128)(2,1)}), bf16[256,2048]{1,0:T(8,128)(2,1)}) %all-gather.5.cloned.1.call-update) | async-done | bytes 1048592 | tf_op jit(solution)/shard_map/all_gather | solution.py:574
  77.3 11.6 %split_product.3 = (bf16[128,4096]{1,0:T(8,128)(2,1)}, f32[64,4096]{1,0:T(8,128)S(1)}, f32[64,4096]{1,0:T(8,128)S(1)}) custom-call(s32[14]{0:T(128)S(1)} %copy-done.15, bf16[4,64,2048]{2,1,0:T(8,128)(2,1)S(1)} %bitcast.17, bf16[2048,4096]{1,0:T(8,128)(2,1)} %refs_3_.5, bf16[2048,4096]{1,0:T(8,128)(2,1)} %refs_3_.5, bf16[2048,4096]{1,0:T(8,128)(2,1)} %refs_3_.5, ...), custom_call_target="tpu_custom_call" | custom-call | flops 4294967296 | bytes 20971520 | tf_op jit(solution)/shard_map/split_product/pallas_call | solution.py:242
  90.8 3.3 %first_hop.3 = (bf16[64,2048]{1,0:T(8,128)(2,1)}, bf16[64,2048]{1,0:T(8,128)(2,1)}) custom-call(s32[14]{0:T(128)} %concatenate.3.index_ref.refs_0_, bf16[384,2048]{1,0:T(8,128)(2,1)} %tokens_ref.15, bf16[64,2048]{1,0:T(8,128)(2,1)} %settle.2.refs_0_), custom_call_target="tpu_custom_call" | custom-call | bytes 1048576 | tf_op jit(solution)/shard_map/first_hop/pallas_call | solution.py:148
  94.1 3.3 %collective-permute-start.10 = (bf16[64,2048]{1,0:T(8,128)(2,1)}, bf16[64,2048]{1,0:T(8,128)(2,1)S(1)}, u32[]{:S(2)}, u32[]{:S(2)}) collective-permute-start(bf16[64,2048]{1,0:T(8,128)(2,1)} %get-tuple-element.38), channel_id=1, source_target_pairs={{12,8},{0,4},{13,9},{1,5},{14,10},{2,6},{15,11},{3,7},{28,24},{16,... | collective-permute-start | bytes 786440 | tf_op jit(solution)/shard_map/ppermute | solution.py:186
  99.7 4.1 %collective-permute-done.10.a_ref = bf16[64,2048]{1,0:T(8,128)(2,1)S(1)} collective-permute-done((bf16[64,2048]{1,0:T(8,128)(2,1)}, bf16[64,2048]{1,0:T(8,128)(2,1)S(1)}, u32[]{:S(2)}, u32[]{:S(2)}) %collective-permute-start.10) | collective-permute-done | bytes 262176 | tf_op jit(solution)/shard_map/ppermute | solution.py:186
  105.2 3.6 %second_hop.3 = (bf16[64,2048]{1,0:T(8,128)(2,1)}, bf16[64,2048]{1,0:T(8,128)(2,1)}) custom-call(s32[14]{0:T(128)} %concatenate.3.index_ref.refs_0_, bf16[384,2048]{1,0:T(8,128)(2,1)} %tokens_ref.15, bf16[64,2048]{1,0:T(8,128)(2,1)} %copy-done.20, bf16[64,2048]{1,0:T(8,128)(2,1)} %copy-done.21), custom_call_target="tpu_custom_call" | custom-call | bytes 1048576 | tf_op jit(solution)/shard_map/second_hop/pallas_call | solution.py:148
  108.8 4.9 %collective-permute-start.12 = (bf16[64,2048]{1,0:T(8,128)(2,1)}, bf16[64,2048]{1,0:T(8,128)(2,1)S(1)}, u32[]{:S(2)}, u32[]{:S(2)}) collective-permute-start(bf16[64,2048]{1,0:T(8,128)(2,1)} %get-tuple-element.40), channel_id=1, source_target_pairs={{4,0},{0,4},{12,8},{5,1},{1,5},{13,9},{6,2},{2,6},{14,10},{7,3},{3... | collective-permute-start | bytes 786440 | tf_op jit(solution)/shard_map/ppermute | solution.py:194
  114.4 5.6 %collective-permute-done.12.x_ref = bf16[64,2048]{1,0:T(8,128)(2,1)S(1)} collective-permute-done((bf16[64,2048]{1,0:T(8,128)(2,1)}, bf16[64,2048]{1,0:T(8,128)(2,1)S(1)}, u32[]{:S(2)}, u32[]{:S(2)}) %collective-permute-start.12) | collective-permute-done | bytes 262176 | tf_op jit(solution)/shard_map/ppermute | solution.py:194
  121.5 3.4 %settle.3 = bf16[64,2048]{1,0:T(8,128)(2,1)} custom-call(s32[14]{0:T(128)} %concatenate.3.index_ref.refs_0_, bf16[384,2048]{1,0:T(8,128)(2,1)} %tokens_ref.15, bf16[64,2048]{1,0:T(8,128)(2,1)} %copy-done.22, bf16[64,2048]{1,0:T(8,128)(2,1)} %copy-done.23), custom_call_target="tpu_custom_call" | custom-call | bytes 524288 | tf_op jit(solution)/shard_map/settle/pallas_call | solution.py:148
  129.6 12.4 %collective-permute-done.19.refs_1_ = bf16[1,64,128]{2,1,0:T(8,128)(2,1)S(1)} collective-permute-done((bf16[1,64,128]{2,1,0:T(8,128)(2,1)S(1)}, bf16[1,64,128]{2,1,0:T(8,128)(2,1)S(1)}, u32[]{:S(2)}, u32[]{:S(2)}) %collective-permute-start.19) | collective-permute-done | bytes 16416 | tf_op jit(solution)/shard_map/ppermute | solution.py:526
  144.7 5.3 %up_gradient.1.refs_4_ = f32[4,64,4096]{2,1,0:T(8,128)} custom-call(s32[14]{0:T(128)S(1)} %copy-done.16, bf16[1,64,4096]{2,1,0:T(8,128)(2,1)} %get-tuple-element.34.refs_4_.refs_0_, bf16[1,64,4096]{2,1,0:T(8,128)(2,1)} %collective-permute-done.16.refs_1_, bf16[1,64,4096]{2,1,0:T(8,128)(2,1)S(1)} %collective-permute-done.17.refs_2_, ...), custom_call_target="tpu_custom_call" | custom-call | bytes 6291456 | tf_op jit(solution)/shard_map/up_gradient/pallas_call | solution.py:409
  149.9 3.6 %all-gather.7.cloned.1.call-done = bf16[256,2048]{1,0:T(8,128)(2,1)} async-done(((bf16[64,2048]{1,0:T(8,128)(2,1)}), bf16[256,2048]{1,0:T(8,128)(2,1)}) %all-gather.7.cloned.1.call-update) | async-done | bytes 1048592 | tf_op jit(solution)/shard_map/all_gather | solution.py:574
  154.8 6.0 %split_product.5 = (bf16[128,2048]{1,0:T(8,128)(2,1)S(1)}, f32[64,2048]{1,0:T(8,128)S(1)}, f32[64,2048]{1,0:T(8,128)S(1)}) custom-call(s32[14]{0:T(128)S(1)} %copy-done.16, bf16[4,64,2048]{2,1,0:T(8,128)(2,1)S(1)} %bitcast.14, bf16[2048,4096]{1,0:T(8,128)(2,1)} %refs_3_.5, bf16[2048,4096]{1,0:T(8,128)(2,1)} %refs_3_.5, bf16[2048,4096]{1,0:T(8,128)(2,1)} %refs_3_.5, ...), custom_call_target="tpu_custom_call" | custom-call | flops 2147483648 | bytes 11010048 | tf_op jit(solution)/shard_map/split_product/pallas_call | solution.py:242
  160.9 6.3 %split_product.4 = (bf16[128,2048]{1,0:T(8,128)(2,1)S(1)}, f32[64,2048]{1,0:T(8,128)S(1)}, f32[64,2048]{1,0:T(8,128)S(1)}) custom-call(s32[14]{0:T(128)S(1)} %copy-done.16, bf16[4,64,2048]{2,1,0:T(8,128)(2,1)S(1)} %bitcast.15, bf16[2048,4096]{1,0:T(8,128)(2,1)} %refs_3_.5, bf16[2048,4096]{1,0:T(8,128)(2,1)} %refs_3_.5, bf16[2048,4096]{1,0:T(8,128)(2,1)} %refs_3_.5, ...), custom_call_target="tpu_custom_call" | custom-call | flops 2147483648 | bytes 11010048 | tf_op jit(solution)/shard_map/split_product/pallas_call | solution.py:242
  170.8 6.0 %collective-permute-done.23.refs_6_ = bf16[64,2048]{1,0:T(8,128)(2,1)S(1)} collective-permute-done((bf16[64,2048]{1,0:T(8,128)(2,1)S(1)}, bf16[64,2048]{1,0:T(8,128)(2,1)S(1)}, u32[]{:S(2)}, u32[]{:S(2)}) %collective-permute-start.23) | collective-permute-done | bytes 262176 | tf_op jit(solution)/shard_map/ppermute | solution.py:526
  178.9 2.9 %collective-permute-done.15.refs_8_ = bf16[64,2048]{1,0:T(8,128)(2,1)S(1)} collective-permute-done((bf16[64,2048]{1,0:T(8,128)(2,1)S(1)}, bf16[64,2048]{1,0:T(8,128)(2,1)S(1)}, u32[]{:S(2)}, u32[]{:S(2)}) %collective-permute-start.15) | collective-permute-done | bytes 262176 | tf_op jit(solution)/shard_map/ppermute | solution.py:526
  (106 shorter events, 52.1 us)
Async XLA Ops:
  7.2 68.9 %all-gather.5.cloned.1.call-start = ((), (), s32[]{:S(2)}) async-start(), calls=%async_computation | async-start | bytes 1310720 | tf_op jit(solution)/shard_map/all_gather | solution.py:574
  11.1 15.4 %collective-permute-start.4 = (bf16[64,2048]{1,0:T(8,128)(2,1)}, bf16[64,2048]{1,0:T(8,128)(2,1)S(1)}, u32[]{:S(2)}, u32[]{:S(2)}) collective-permute-start(bf16[64,2048]{1,0:T(8,128)(2,1)} %get-tuple-element.26.refs_0_), channel_id=1, source_target_pairs={{12,8},{0,4},{13,9},{1,5},{14,10},{2,6},{15,11},{3,7},{28,24},{16,... | collective-permute-start | bytes 786440 | tf_op jit(solution)/shard_map/ppermute | solution.py:186
  16.0 10.4 %collective-permute-start.5 = (bf16[64,2048]{1,0:T(8,128)(2,1)}, bf16[64,2048]{1,0:T(8,128)(2,1)S(1)}, u32[]{:S(2)}, u32[]{:S(2)}) collective-permute-start(bf16[64,2048]{1,0:T(8,128)(2,1)} %get-tuple-element.31), channel_id=1, source_target_pairs={{8,4},{9,5},{10,6},{11,7},{24,20},{25,21},{26,22},{27,23}} | collective-permute-start | bytes 786440 | tf_op jit(solution)/shard_map/ppermute | solution.py:187
  31.4 10.5 %collective-permute-start.6 = (bf16[64,2048]{1,0:T(8,128)(2,1)}, bf16[64,2048]{1,0:T(8,128)(2,1)S(1)}, u32[]{:S(2)}, u32[]{:S(2)}) collective-permute-start(bf16[64,2048]{1,0:T(8,128)(2,1)} %get-tuple-element.32), channel_id=1, source_target_pairs={{4,0},{0,4},{12,8},{5,1},{1,5},{13,9},{6,2},{2,6},{14,10},{7,3},{3... | collective-permute-start | bytes 786440 | tf_op jit(solution)/shard_map/ppermute | solution.py:194
  33.4 8.5 %collective-permute-start.7 = (bf16[64,2048]{1,0:T(8,128)(2,1)}, bf16[64,2048]{1,0:T(8,128)(2,1)S(1)}, u32[]{:S(2)}, u32[]{:S(2)}) collective-permute-start(bf16[64,2048]{1,0:T(8,128)(2,1)} %get-tuple-element.33), channel_id=1, source_target_pairs={{8,4},{4,8},{9,5},{5,9},{10,6},{6,10},{11,7},{7,11},{24,20},{20,24... | collective-permute-start | bytes 786440 | tf_op jit(solution)/shard_map/ppermute | solution.py:195
  34.1 4.0 %collective-permute-start.1 = (f32[1,64,128]{2,1,0:T(8,128)S(1)}, f32[1,64,128]{2,1,0:T(8,128)S(1)}, u32[]{:S(2)}, u32[]{:S(2)}) collective-permute-start(f32[1,64,128]{2,1,0:T(8,128)S(1)} %slice_bitcast_fusion), channel_id=1, source_target_pairs={{0,2},{1,3},{2,0},{3,1},{4,6},{5,7},{6,4},{7,5},{8,10},{9,11},{10,... | collective-permute-start | bytes 98312 | tf_op jit(solution)/shard_map/ppermute | solution.py:526
  46.7 106.8 %all-gather.7.cloned.1.call-start = ((), (), s32[]{:S(2)}) async-start(), calls=%async_computation.1 | async-start | bytes 1310720 | tf_op jit(solution)/shard_map/all_gather | solution.py:574
  47.5 5.2 %collective-permute-start.2 = (f32[2,1,64,128]{3,2,1,0:T(8,128)S(1)}, f32[2,1,64,128]{3,2,1,0:T(8,128)S(1)}, u32[]{:S(2)}, u32[]{:S(2)}) collective-permute-start(f32[2,1,64,128]{3,2,1,0:T(8,128)S(1)} %pad_maximum_fusion), channel_id=1, source_target_pairs={{0,4},{4,0},{8,12},{12,8},{1,5},{5,1},{9,13},{13,9},{2,6},{6,2},{1... | collective-permute-start | bytes 196616 | tf_op jit(solution)/shard_map/ppermute | solution.py:529
  53.5 5.3 %collective-permute-start.3 = (f32[2,1,64,128]{3,2,1,0:T(8,128)S(1)}, f32[2,1,64,128]{3,2,1,0:T(8,128)S(1)}, u32[]{:S(2)}, u32[]{:S(2)}) collective-permute-start(f32[2,1,64,128]{3,2,1,0:T(8,128)S(1)} %fusion.1.sum_ref), channel_id=1, source_target_pairs={{0,8},{4,12},{8,0},{12,4},{1,9},{5,13},{9,1},{13,5},{2,10},{6,14},... | collective-permute-start | bytes 196616 | tf_op jit(solution)/shard_map/ppermute | solution.py:529
  90.8 34.7 %collective-permute-start.8 = (bf16[128,4096]{1,0:T(8,128)(2,1)}, bf16[128,4096]{1,0:T(8,128)(2,1)S(1)}, u32[]{:S(2)}, u32[]{:S(2)}) collective-permute-start(bf16[128,4096]{1,0:T(8,128)(2,1)} %get-tuple-element.36), channel_id=1, source_target_pairs={{0,1},{1,0},{2,3},{3,2},{4,5},{5,4},{6,7},{7,6},{8,9},{9,8},{10,11... | collective-permute-start | bytes 3145736 | tf_op jit(solution)/shard_map/ppermute | solution.py:523
  94.1 9.7 %collective-permute-start.10 = (bf16[64,2048]{1,0:T(8,128)(2,1)}, bf16[64,2048]{1,0:T(8,128)(2,1)S(1)}, u32[]{:S(2)}, u32[]{:S(2)}) collective-permute-start(bf16[64,2048]{1,0:T(8,128)(2,1)} %get-tuple-element.38), channel_id=1, source_target_pairs={{12,8},{0,4},{13,9},{1,5},{14,10},{2,6},{15,11},{3,7},{28,24},{16,... | collective-permute-start | bytes 786440 | tf_op jit(solution)/shard_map/ppermute | solution.py:186
  97.5 6.4 %collective-permute-start.11 = (bf16[64,2048]{1,0:T(8,128)(2,1)}, bf16[64,2048]{1,0:T(8,128)(2,1)S(1)}, u32[]{:S(2)}, u32[]{:S(2)}) collective-permute-start(bf16[64,2048]{1,0:T(8,128)(2,1)} %get-tuple-element.39), channel_id=1, source_target_pairs={{8,4},{9,5},{10,6},{11,7},{24,20},{25,21},{26,22},{27,23}} | collective-permute-start | bytes 786440 | tf_op jit(solution)/shard_map/ppermute | solution.py:187
  98.1 26.8 %collective-permute-start.16 = (bf16[1,64,4096]{2,1,0:T(8,128)(2,1)}, bf16[1,64,4096]{2,1,0:T(8,128)(2,1)}, u32[]{:S(2)}, u32[]{:S(2)}) collective-permute-start(bf16[1,64,4096]{2,1,0:T(8,128)(2,1)} %get-tuple-element.34.refs_4_.refs_0_), channel_id=1, source_target_pairs={{0,2},{1,3},{2,0},{3,1},{4,6},{5,7},{6,4},{7,5},{8,10},{9,11},{10,... | collective-permute-start | bytes 1572872 | tf_op jit(solution)/shard_map/ppermute | solution.py:526
  108.8 11.2 %collective-permute-start.12 = (bf16[64,2048]{1,0:T(8,128)(2,1)}, bf16[64,2048]{1,0:T(8,128)(2,1)S(1)}, u32[]{:S(2)}, u32[]{:S(2)}) collective-permute-start(bf16[64,2048]{1,0:T(8,128)(2,1)} %get-tuple-element.40), channel_id=1, source_target_pairs={{4,0},{0,4},{12,8},{5,1},{1,5},{13,9},{6,2},{2,6},{14,10},{7,3},{3... | collective-permute-start | bytes 786440 | tf_op jit(solution)/shard_map/ppermute | solution.py:194
  113.7 6.3 %collective-permute-start.13 = (bf16[64,2048]{1,0:T(8,128)(2,1)}, bf16[64,2048]{1,0:T(8,128)(2,1)S(1)}, u32[]{:S(2)}, u32[]{:S(2)}) collective-permute-start(bf16[64,2048]{1,0:T(8,128)(2,1)} %get-tuple-element.41), channel_id=1, source_target_pairs={{8,4},{4,8},{9,5},{5,9},{10,6},{6,10},{11,7},{7,11},{24,20},{20,24... | collective-permute-start | bytes 786440 | tf_op jit(solution)/shard_map/ppermute | solution.py:195
  124.9 19.8 %collective-permute-start.17 = (bf16[1,64,4096]{2,1,0:T(8,128)(2,1)}, bf16[1,64,4096]{2,1,0:T(8,128)(2,1)S(1)}, u32[]{:S(2)}, u32[]{:S(2)}) collective-permute-start(bf16[1,64,4096]{2,1,0:T(8,128)(2,1)} %get-tuple-element.34.refs_4_.refs_0_), channel_id=1, source_target_pairs={{0,1},{1,0},{2,3},{3,2},{4,5},{5,4},{6,7},{7,6},{8,9},{9,8},{10,11... | collective-permute-start | bytes 1572872 | tf_op jit(solution)/shard_map/ppermute | solution.py:523
  125.0 19.7 %collective-permute-start.18 = (bf16[1,64,4096]{2,1,0:T(8,128)(2,1)}, bf16[1,64,4096]{2,1,0:T(8,128)(2,1)S(1)}, u32[]{:S(2)}, u32[]{:S(2)}) collective-permute-start(bf16[1,64,4096]{2,1,0:T(8,128)(2,1)} %collective-permute-done.16.refs_1_), channel_id=1, source_target_pairs={{0,1},{1,0},{2,3},{3,2},{4,5},{5,4},{6,7},{7,6},{8,9},{9,8},{10,11... | collective-permute-start | bytes 1572872 | tf_op jit(solution)/shard_map/ppermute | solution.py:523
  127.6 26.0 %collective-permute-start.9 = (bf16[64,4096]{1,0:T(8,128)(2,1)}, bf16[64,4096]{1,0:T(8,128)(2,1)S(1)}, u32[]{:S(2)}, u32[]{:S(2)}) collective-permute-start(bf16[64,4096]{1,0:T(8,128)(2,1)} %add_convert_fusion), channel_id=1, source_target_pairs={{0,2},{1,3},{2,0},{3,1},{4,6},{5,7},{6,4},{7,5},{8,10},{9,11},{10,... | collective-permute-start | bytes 1572872 | tf_op jit(solution)/shard_map/ppermute | solution.py:526
  129.1 13.0 %collective-permute-start.19 = (bf16[1,64,128]{2,1,0:T(8,128)(2,1)S(1)}, bf16[1,64,128]{2,1,0:T(8,128)(2,1)S(1)}, u32[]{:S(2)}, u32[]{:S(2)}) collective-permute-start(bf16[1,64,128]{2,1,0:T(8,128)(2,1)S(1)} %get-tuple-element.45.refs_0_), channel_id=1, source_target_pairs={{0,2},{1,3},{2,0},{3,1},{4,6},{5,7},{6,4},{7,5},{8,10},{9,11},{10,... | collective-permute-start | bytes 49160 | tf_op jit(solution)/shard_map/ppermute | solution.py:526
  129.6 12.5 %collective-permute-start.20 = (bf16[1,64,128]{2,1,0:T(8,128)(2,1)S(1)}, bf16[1,64,128]{2,1,0:T(8,128)(2,1)S(1)}, u32[]{:S(2)}, u32[]{:S(2)}) collective-permute-start(bf16[1,64,128]{2,1,0:T(8,128)(2,1)S(1)} %get-tuple-element.45.refs_0_), channel_id=1, source_target_pairs={{0,1},{1,0},{2,3},{3,2},{4,5},{5,4},{6,7},{7,6},{8,9},{9,8},{10,11... | collective-permute-start | bytes 49160 | tf_op jit(solution)/shard_map/ppermute | solution.py:523
  160.8 6.7 %collective-permute-start.22 = (bf16[128,2048]{1,0:T(8,128)(2,1)S(1)}, bf16[128,2048]{1,0:T(8,128)(2,1)S(1)}, u32[]{:S(2)}, u32[]{:S(2)}) collective-permute-start(bf16[128,2048]{1,0:T(8,128)(2,1)S(1)} %get-tuple-element.47), channel_id=1, source_target_pairs={{0,1},{1,0},{2,3},{3,2},{4,5},{5,4},{6,7},{7,6},{8,9},{9,8},{10,11... | collective-permute-start | bytes 1572872 | tf_op jit(solution)/shard_map/ppermute | solution.py:523
  167.2 2.0 %collective-permute-start.14 = (bf16[128,2048]{1,0:T(8,128)(2,1)S(1)}, bf16[128,2048]{1,0:T(8,128)(2,1)S(1)}, u32[]{:S(2)}, u32[]{:S(2)}) collective-permute-start(bf16[128,2048]{1,0:T(8,128)(2,1)S(1)} %get-tuple-element.43), channel_id=1, source_target_pairs={{0,1},{1,0},{2,3},{3,2},{4,5},{5,4},{6,7},{7,6},{8,9},{9,8},{10,11... | collective-permute-start | bytes 1572872 | tf_op jit(solution)/shard_map/ppermute | solution.py:523
  167.6 9.2 %collective-permute-start.23 = (bf16[64,2048]{1,0:T(8,128)(2,1)S(1)}, bf16[64,2048]{1,0:T(8,128)(2,1)S(1)}, u32[]{:S(2)}, u32[]{:S(2)}) collective-permute-start(bf16[64,2048]{1,0:T(8,128)(2,1)S(1)} %add_convert_fusion.1), channel_id=1, source_target_pairs={{0,2},{1,3},{2,0},{3,1},{4,6},{5,7},{6,4},{7,5},{8,10},{9,11},{10,... | collective-permute-start | bytes 786440 | tf_op jit(solution)/shard_map/ppermute | solution.py:526
  169.3 12.5 %collective-permute-start.15 = (bf16[64,2048]{1,0:T(8,128)(2,1)S(1)}, bf16[64,2048]{1,0:T(8,128)(2,1)S(1)}, u32[]{:S(2)}, u32[]{:S(2)}) collective-permute-start(bf16[64,2048]{1,0:T(8,128)(2,1)S(1)} %add_convert_fusion.2), channel_id=1, source_target_pairs={{0,2},{1,3},{2,0},{3,1},{4,6},{5,7},{6,4},{7,5},{8,10},{9,11},{10,... | collective-permute-start | bytes 786440 | tf_op jit(solution)/shard_map/ppermute | solution.py:526
  (28 other events, 237.2 us)
Sparse Core Ops, SparseCore 0:
  46.8 29.1 all-gather.4
  125.0 28.4 all-gather.6

commit v5 on v4

--- a/solution.py
+++ b/solution.py
@@ -11,8 +11,8 @@
 CAP = 3
 CORES = 2
 CHUNK_ROWS = (64, 64)
-PARTS = 2
-MIB = 2**20
+PARTS = 4
+SMALL = pltpu.CompilerParams(vmem_limit_bytes=12 * 2**20)
 
 adapter_scale = 0.5
 
@@ -60,6 +60,18 @@
         return self.tokens(adapter) - (block - first) * BLK
 
 
+def in_vmem(value):
+    return pltpu.with_memory_space_constraint(value, pltpu.VMEM)
+
+
+def in_hbm(value):
+    return pltpu.with_memory_space_constraint(value, pltpu.HBM)
+
+
+def held():
+    return pl.BlockSpec(memory_space=pltpu.VMEM)
+
+
 def whole(shape):
     return pl.BlockSpec(shape, lambda *_: (0,) * len(shape))
 
@@ -68,46 +80,29 @@
     return jax.ShapeDtypeStruct(shape, dtype)
 
 
-def cost(flops, bytes_accessed):
-    return pl.CostEstimate(flops=flops, bytes_accessed=bytes_accessed, transcendentals=0)
-
-
-def own_copy(index, block, start, tokens_ref, out_ref, sem):
+BRIEF = pl.CostEstimate(flops=1, bytes_accessed=1, transcendentals=0)
+
+
+def own_rows(index, block, start, tokens_ref, out_ref):
     at = pl.multiple_of(index.slot(block) * BLK + start, 16)
-    return pltpu.make_async_copy(tokens_ref.at[pl.ds(at, out_ref.shape[0])], out_ref, sem)
-
-
-def run_all(copies):
-    for copy in copies:
-        copy.start()
-    for copy in copies:
-        copy.wait()
+    out_ref[...] = tokens_ref[pl.ds(at, out_ref.shape[0])]
 
 
 def first_hop_kernel(index_of, start, index_ref, tokens_ref, *refs):
-    a_ref, b_ref, sems = refs[-3:]
-    index = index_of(index_ref)
-    inward = jnp.where(index.place == 0, 2, 1)
-    run_all(
-        [
-            own_copy(index, inward, start, tokens_ref, a_ref, sems.at[0]),
-            own_copy(index, 0, start, tokens_ref, b_ref, sems.at[1]),
-        ]
-    )
+    a_ref, b_ref = refs[-2:]
+    index = index_of(index_ref)
+    own_rows(index, jnp.where(index.place == 0, 2, 1), start, tokens_ref, a_ref)
+    own_rows(index, 0, start, tokens_ref, b_ref)
 
 
 def second_hop_kernel(index_of, start, index_ref, tokens_ref, a_ref, b_ref, *refs):
-    x_ref, y_ref, sems = refs[-3:]
+    x_ref, y_ref = refs[-2:]
     index = index_of(index_ref)
     place = index.place
     outer = jnp.where(place == 0, 1, jnp.where(place == 1, 0, 2))
     middle = jnp.where(place == 1, 2, 1)
-    run_all(
-        [
-            own_copy(index, outer, start, tokens_ref, x_ref, sems.at[0]),
-            own_copy(index, middle, start, tokens_ref, y_ref, sems.at[1]),
-        ]
-    )
+    own_rows(index, outer, start, tokens_ref, x_ref)
+    own_rows(index, middle, start, tokens_ref, y_ref)
 
     @pl.when((place == 1) & (index.owner(0) != 1))
     def _():
@@ -119,13 +114,13 @@
 
 
 def settle_kernel(index_of, start, index_ref, tokens_ref, x_ref, y_ref, *refs):
-    out_ref, sems = refs[-2:]
+    out_ref = refs[-1]
     index = index_of(index_ref)
     place = index.place
     owner = index.owner(place)
     mine = owner == place
     edge = (place == 0) | ((place == 1) & (owner == 0)) | ((place == 2) & (owner == 3))
-    run_all([own_copy(index, place, start, tokens_ref, out_ref, sems.at[0])])
+    own_rows(index, place, start, tokens_ref, out_ref)
 
     @pl.when(jnp.logical_not(mine) & edge)
     def _():
@@ -136,30 +131,29 @@
         out_ref[...] = y_ref[...]
 
 
-def after(values):
+def after(values, far=()):
     specs = [
         pl.BlockSpec((1,) * (v.ndim - 2) + (16, 128), lambda *_, n=v.ndim: (0,) * n) for v in values
-    ]
-    return specs, list(values)
-
-
-def hop_call(kernel, index, tokens, outs, received, waits, name):
-    specs, extra = after(waits)
+    ] + [pl.BlockSpec(memory_space=pl.ANY)] * len(far)
+    return specs, [*values, *(in_hbm(v) for v in far)]
+
+
+def hop_call(kernel, index, tokens, unit, count, stay, received, waits, name):
+    specs, extra = after((), waits) if waits and waits[0].shape == unit.shape else after(waits)
+    out = pltpu.VMEM(unit.shape, unit.dtype) if stay else unit
     return pl.pallas_call(
         kernel,
         grid_spec=pltpu.PrefetchScalarGridSpec(
             num_scalar_prefetch=1,
             grid=(1,),
-            in_specs=[pl.BlockSpec(memory_space=pl.ANY)]
-            + [whole(r.shape) for r in received]
-            + specs,
-            out_specs=[whole(o.shape) for o in outs],
-            scratch_shapes=[pltpu.SemaphoreType.DMA((len(outs),))],
-        ),
-        out_shape=outs,
-        cost_estimate=cost(0, 4 * sum(o.size for o in outs)),
+            in_specs=[held()] * (1 + len(received)) + specs,
+            out_specs=[held() if stay else whole(unit.shape)] * count,
+        ),
+        out_shape=[out] * count,
+        compiler_params=SMALL,
+        cost_estimate=BRIEF,
         name=name,
-    )(index, tokens, *received, *extra)
+    )(index, tokens, *[in_vmem(r) for r in received], *extra)
 
 
 class Homing:
@@ -168,19 +162,21 @@
         self.start = sum(CHUNK_ROWS[:chunk])
         self.unit = shape_of((CHUNK_ROWS[chunk], tokens.shape[1]), tokens.dtype)
 
-    def call(self, kernel, count, received, waits, name):
+    def call(self, kernel, count, stay, received, waits, name):
         return hop_call(
             functools.partial(kernel, self.index_of, self.start),
             self.index,
             self.tokens,
-            [self.unit] * count,
+            self.unit,
+            count,
+            stay,
             received,
             waits,
             name,
         )
 
     def first(self, waits=()):
-        inward, left = self.call(first_hop_kernel, 2, (), waits, "first_hop")
+        inward, left = self.call(first_hop_kernel, 2, True, (), waits, "first_hop")
         self.sent = inward
         self.received = (
             lax.ppermute(inward, "dp", [(3, 2), (0, 1)]),
@@ -188,7 +184,7 @@
         )
 
     def second(self, waits=()):
-        outer, middle = self.call(second_hop_kernel, 2, self.received, waits, "second_hop")
+        outer, middle = self.call(second_hop_kernel, 2, True, self.received, waits, "second_hop")
         self.sent = outer
         self.received = (
             lax.ppermute(outer, "dp", [(1, 0), (0, 1), (3, 2)]),
@@ -196,68 +192,78 @@
         )
 
     def settle(self, waits=()):
-        (self.sent,) = self.call(settle_kernel, 1, self.received, waits, "settle")
+        (self.sent,) = self.call(settle_kernel, 1, False, self.received, waits, "settle")
         return self.sent
 
 
-STREAMS = 4
-
-
-def split_product_kernel(index_of, index_ref, x_ref, *refs):
-    w_refs, (send_ref, other_ref, own_ref) = refs[:STREAMS], refs[-3:]
-    index = index_of(index_ref)
+def split_product_kernel(index_of, tile, index_ref, x_ref, w_ref, *refs):
+    send_ref, other_ref, own_ref, sent = refs[-4:]
+    index = index_of(index_ref)
+    step = pl.program_id(0)
     each = index.per_part * x_ref.shape[1]
-    rows = [
-        x_ref[index.block(core_bit, chip_bits, i)]
-        for core_bit in (1, 0)
-        for chip_bits in range(index.chips)
-        for i in range(index.per_part)
-    ]
-    total = jnp.dot(
-        jnp.concatenate(rows, axis=0),
-        jnp.concatenate([w[...] for w in w_refs], axis=0),
-        preferred_element_type=jnp.float32,
+    half = index.chips * each
+    rows = jnp.concatenate(
+        [
+            x_ref[index.block(core_bit, chip_bits, i)]
+            for core_bit in (1, 0)
+            for chip_bits in range(index.chips)
+            for i in range(index.per_part)
+        ],
+        axis=0,
     )
-    half = index.chips * each
-    send_ref[...] = total[:half].astype(send_ref.dtype)
-    own_ref[...] = total[half : half + each]
-    other_ref[...] = total[half + each :]
-
-
-def split_product(index_of, index, shape, rows, weight, part, part_count, waits):
+    for n in range(w_ref.shape[1] // tile):
+        columns = slice(n * tile, (n + 1) * tile)
+        total = jnp.dot(rows, w_ref[:, columns], preferred_element_type=jnp.float32)
+        parts = (
+            (sent, total[:half]),
+            (own_ref, total[half : half + each]),
+            (other_ref, total[half + each :]),
+        )
+
+        @pl.when(step == 0)
+        def _():
+            for ref, value in parts:
+                ref[:, columns] = value
+
+        @pl.when(step > 0)
+        def _():
+            for ref, value in parts:
+                ref[:, columns] += value
+
+    @pl.when(step == pl.num_programs(0) - 1)
+    def _():
+        send_ref[...] = sent[...].astype(send_ref.dtype)
+
+
+def split_product(index_of, index, shape, rows, weight, part, part_count, waits, far):
     block_count, count, depth = rows.shape
     width = weight.shape[1] // part_count
-    tile = 512
+    deep = min(512, depth)
     each = shape.per_part * count
     half = block_count * count // 2
-    specs, extra = after(waits)
-
-    def columns(height):
-        return pl.BlockSpec((height, tile), lambda n, _: (0, n))
-
-    def stream(i):
-        first = part * (width // tile)
-        return pl.BlockSpec((depth // STREAMS, tile), lambda n, _: (i, first + n))
-
-    return pl.pallas_call(
-        functools.partial(split_product_kernel, index_of),
+    specs, extra = after(waits, far)
+    return pl.pallas_call(
+        functools.partial(split_product_kernel, index_of, min(512, width)),
         grid_spec=pltpu.PrefetchScalarGridSpec(
             num_scalar_prefetch=1,
-            grid=(width // tile,),
-            in_specs=[whole(rows.shape)] + [stream(i) for i in range(STREAMS)] + specs,
-            out_specs=[columns(half), columns(half - each), columns(each)],
+            grid=(depth // deep,),
+            in_specs=[
+                pl.BlockSpec((block_count, count, deep), lambda k, _: (0, 0, k)),
+                pl.BlockSpec((deep, width), lambda k, _: (k, part)),
+            ]
+            + specs,
+            out_specs=[whole((half, width)), whole((half - each, width)), whole((each, width))],
+            scratch_shapes=[pltpu.VMEM((half, width), jnp.float32)],
         ),
         out_shape=[
             shape_of((half, width), jnp.bfloat16),
             shape_of((half - each, width), jnp.float32),
             shape_of((each, width), jnp.float32),
         ],
-        compiler_params=pltpu.CompilerParams(vmem_limit_bytes=48 * MIB),
-        cost_estimate=cost(
-            4 * half * depth * width, 2 * depth * (2 * half + width) + 6 * half * width
-        ),
+        compiler_params=pltpu.CompilerParams(vmem_limit_bytes=32 * 2**20),
+        cost_estimate=BRIEF,
         name="split_product",
-    )(index, rows, *[weight] * STREAMS, *extra)
+    )(index, in_hbm(rows), in_hbm(weight), *extra)
 
 
 def narrow_kernel(index_of, index_ref, tokens_ref, down_ref, cot_ref, up_ref, *refs):
@@ -297,15 +303,40 @@
         grid_spec=pltpu.PrefetchScalarGridSpec(
             num_scalar_prefetch=1,
             grid=(1,),
-            in_specs=[whole(o.shape) for o in operands] + specs,
+            in_specs=[held()] + [whole(o.shape) for o in operands[1:]] + specs,
             out_specs=[whole(o) for o in outs],
             scratch_shapes=[pltpu.VMEM((CAP, rank, BLK), jnp.float32)],
         ),
         out_shape=[shape_of(o, jnp.float32) for o in outs],
-        compiler_params=pltpu.CompilerParams(vmem_limit_bytes=24 * MIB),
-        cost_estimate=cost(2 * rank * (tokens.size + cotangent.size), 2 * sum(o.size for o in operands)),
+        compiler_params=SMALL,
+        cost_estimate=BRIEF,
         name="narrow",
     )(index, *operands, *extra)
+
+
+def merge_kernel(keep_ref, arrived_ref, back_ref, *refs):
+    out_ref = refs[-1]
+    total = keep_ref[0] + arrived_ref[0]
+    for ref in refs[:-1][: keep_ref.shape[0] - 1]:
+        total = total + ref[...]
+    out_ref[0] = total
+    out_ref[1] = back_ref[...]
+
+
+def merge(keep, arrived, back, others, waits):
+    specs, extra = after(waits)
+    operands = (keep, arrived, back, *others)
+    out = (2,) + back.shape
+    return pl.pallas_call(
+        merge_kernel,
+        grid=(1,),
+        in_specs=[whole(o.shape) for o in operands] + specs,
+        out_specs=whole(out),
+        out_shape=shape_of(out, jnp.float32),
+        compiler_params=SMALL,
+        cost_estimate=BRIEF,
+        name="merge",
+    )(*operands, *extra)
 
 
 def pieces_kernel(index_of, index_ref, sum_ref, more_ref, cot_ref, low_ref, back_ref, piece_ref):
@@ -336,8 +367,8 @@
             out_specs=[whole(o) for o in outs],
         ),
         out_shape=[shape_of(o, jnp.bfloat16) for o in outs],
-        compiler_params=pltpu.CompilerParams(vmem_limit_bytes=24 * MIB),
-        cost_estimate=cost(2 * rank * cotangent.size, 3 * cotangent.size),
+        compiler_params=SMALL,
+        cost_estimate=BRIEF,
         name="pieces",
     )(index, *operands)
 
@@ -370,12 +401,12 @@
         grid_spec=pltpu.PrefetchScalarGridSpec(
             num_scalar_prefetch=1,
             grid=(1,),
-            in_specs=[whole(o.shape) for o in operands],
+            in_specs=[held()] + [whole(o.shape) for o in backs],
             out_specs=whole(out),
         ),
         out_shape=shape_of(out, jnp.float32),
-        compiler_params=pltpu.CompilerParams(vmem_limit_bytes=24 * MIB),
-        cost_estimate=cost(2 * out[1] * tokens.size, 2 * tokens.size),
+        compiler_params=SMALL,
+        cost_estimate=BRIEF,
         name="down_gradient",
     )(index, *operands)
 
@@ -415,8 +446,8 @@
             out_specs=pl.BlockSpec((adapter_count, rank, tile), lambda n, _: (0, 0, n)),
         ),
         out_shape=shape_of(out, jnp.float32),
-        compiler_params=pltpu.CompilerParams(vmem_limit_bytes=24 * MIB),
-        cost_estimate=cost(0, 4 * adapter_count * rank * width + 2 * len(pieces) * pieces[0].size),
+        compiler_params=SMALL,
+        cost_estimate=BRIEF,
         name="up_gradient",
     )(index, *pieces)
 
@@ -445,7 +476,7 @@
             start += count
 
 
-def finish(index_of, index, lowered, up, sums, part, part_count, projected):
+def finish(index_of, index, lowered, up, sums, part, part_count, projected, far):
     per_part = lowered.shape[0]
     _, rank, width = up.shape
     tile = min(1024, width // part_count)
@@ -468,33 +499,32 @@
                 pl.BlockSpec((per_part * count, tile), lambda n, _, begin=begin: (0, begin + n))
             )
             flat.append(value)
-    kernel = functools.partial(finish_kernel, index_of, CHUNK_ROWS)
     operands = [index, lowered, *[up] * per_part, *flat]
     aliases = {}
     if projected is not None:
         aliases = {len(operands): 0}
-        operands.append(projected)
-        specs.append(pl.BlockSpec(memory_space=pl.ANY))
-
-        def kernel(*refs):
-            finish_kernel(index_of, CHUNK_ROWS, *refs[:-2], refs[-1])
+        far = [projected]
+    more, extra = after((), far)
+    if projected is not None:
+        extra = [projected]
+
+    def kernel(*refs):
+        finish_kernel(index_of, CHUNK_ROWS, *refs[: len(operands)], refs[-1])
 
     return pl.pallas_call(
         kernel,
         grid_spec=pltpu.PrefetchScalarGridSpec(
             num_scalar_prefetch=1,
             grid=(tiles,),
-            in_specs=[whole(lowered.shape)] + [factor(i) for i in range(per_part)] + specs,
+            in_specs=[whole(lowered.shape)] + [factor(i) for i in range(per_part)] + specs + more,
             out_specs=pl.BlockSpec((out[0], tile), lambda n, _: (0, first + n)),
         ),
         out_shape=shape_of(out, jnp.bfloat16),
         input_output_aliases=aliases,
-        compiler_params=pltpu.CompilerParams(vmem_limit_bytes=24 * MIB),
-        cost_estimate=cost(
-            2 * rank * out[0] * tiles * tile, (10 * out[0] + 2 * rank) * tiles * tile
-        ),
+        compiler_params=SMALL,
+        cost_estimate=BRIEF,
         name="finish",
-    )(*operands)
+    )(*operands, *extra)
 
 
 def per_device(
@@ -532,12 +562,14 @@
         same_core = [value] + [to_chip(value, k) for k in range(1, chips)]
         return same_core + [to_other_core(v) for v in same_core]
 
+    rows_here = in_vmem(tokens)
+
     def small_products(waits):
         return narrow(
             index_of,
             index,
             shape,
-            tokens,
+            rows_here,
             jnp.swapaxes(adapter_down_factor, 1, 2),
             cotangent,
             adapter_up_factor,
@@ -545,36 +577,39 @@
         )
 
     def over_parts(send, keep):
-        low_chip = keep + to_other_core(send)
-        low_part = low_chip[0]
-        for k in range(1, chips):
-            low_part = low_part + to_chip(low_chip[k], k)
-        return low_part
-
-    def over_dp(low_part, back):
-        total, k = jnp.stack([low_part, back]), 1
+        arrived = to_other_core(send)
+        return arrived, [to_chip(keep[k] + arrived[k], k) for k in range(1, chips)]
+
+    def over_dp(total):
+        k = 1
         while 2 * k < owners:
             total = total + across_dp(total, k)
             k *= 2
         return make_pieces(index_of, index, shape, total, across_dp(total, k), cotangent)
 
     if owners == 4 and block_count == 4:
-        head = Homing(index_of, index, tokens, 0)
-        tail = [Homing(index_of, index, tokens, c) for c in range(1, len(CHUNK_ROWS))]
+        head = Homing(index_of, index, rows_here, 0)
+        tail = [Homing(index_of, index, rows_here, c) for c in range(1, len(CHUNK_ROWS))]
         head.first()
         send, keep, back = small_products([head.sent])
         head.second([send])
-        low_part = over_parts(send, keep)
-        homes = [head.settle([low_part])]
-        for homing in tail:
+        arrived, others = over_parts(send, keep)
+        homes = [head.settle(others)]
+        tail[0].first([homes[-1]])
+        total = merge(keep, arrived, back, others, [tail[0].sent])
+        tail[0].second()
+        homes.append(tail[0].settle())
+        for homing in tail[1:]:
             homing.first([homes[-1]])
             homing.second()
             homes.append(homing.settle())
-        lowered, back_rows, pieces = over_dp(low_part, back)
+        lowered, back_rows, pieces = over_dp(total)
         chunks = [lax.all_gather(home, "dp", axis=0) for home in homes]
     else:
         send, keep, back = small_products([])
-        lowered, back_rows, pieces = over_dp(over_parts(send, keep), back)
+        arrived, others = over_parts(send, keep)
+        lowered, back_rows, pieces = over_dp(merge(keep, arrived, back, others, []))
+        homes = []
         every_slot = lax.all_gather(
             tokens.reshape(CAP, BLK, width_dev), "dp", axis=0, tiled=True
         )
@@ -582,10 +617,12 @@
         starts = [sum(CHUNK_ROWS[:c]) for c in range(len(CHUNK_ROWS))]
         chunks = [picked[:, s : s + count] for s, count in zip(starts, CHUNK_ROWS)]
 
-    def summed(rows, part, part_count, waits):
+    pieces_same_core = [pieces] + [to_chip(pieces, k) for k in range(1, chips)]
+
+    def summed(rows, part, waits, far):
         each = shape.per_part * rows.shape[1]
         send, other, own = split_product(
-            index_of, index, shape, rows, frozen_up_weight, part, part_count, waits
+            index_of, index, shape, rows, frozen_up_weight, part, PARTS, waits, far
         )
         arrived = to_other_core(send)
         outgoing = (other + arrived[each:].astype(jnp.float32)).astype(jnp.bfloat16)
@@ -593,14 +630,16 @@
             to_chip(outgoing[(k - 1) * each : k * each], k) for k in range(1, chips)
         ]
 
-    sums = [summed(rows, 0, 1, [pieces]) for rows in chunks[:-1]]
-    up_grad = up_gradient(index_of, index, adapter_count, every_part(pieces))
-    down_grad = down_gradient(index_of, index, tokens, every_part(back_rows))
-    waits = [up_grad, down_grad] + [chunk[-1] for chunk in sums]
-    last = []
-    for part in range(PARTS):
-        last.append(summed(chunks[-1], part, PARTS, waits))
-        waits = []
+    waits, far = pieces_same_core[1:], homes[1:]
+    sums = [[] for _ in range(PARTS)]
+    for rows in chunks:
+        for part in range(PARTS):
+            sums[part].append(summed(rows, part, waits, far))
+            waits, far = [], []
+        waits = [v for part in sums for v in part[-1][2:]]
+    pieces_all = pieces_same_core + [to_other_core(p) for p in pieces_same_core]
+    up_grad = up_gradient(index_of, index, adapter_count, pieces_all)
+    down_grad = down_gradient(index_of, index, rows_here, every_part(back_rows))
     projected = None
     for part in range(PARTS):
         projected = finish(
@@ -608,10 +647,11 @@
             index,
             lowered,
             adapter_up_factor,
-            sums + [last[part]],
+            sums[part],
             part,
             PARTS,
             projected,
+            [up_grad, down_grad],
         )
     return (projected, jnp.swapaxes(down_grad, 1, 2), up_grad)
 

time: 192 us -> 167 us (0.87)
  waiting for transfers between devices: 64.1 us -> 39.8 us
  local copies, waits for them, and re-layouts: 18.3 us -> 12.5 us
  Pallas kernels: 57.7 us -> 62.3 us
  other arithmetic: 4.37 us -> 0.25 us
  starting transfers between devices: 31.9 us -> 35.3 us
    pallas_call x3 -> x9, Pallas kernels: 23.9 us -> 43.2 us  [the longest x8 43.2 us: split_product(): pl.pallas_call(functools.partial(split_product_kernel, index_of, min(512,...]
    all_gather x2, waiting for transfers between devices: 19.1 us -> 0.02 us  [per_device(): chunks = [lax.all_gather(home, 'dp', axis=0) for home in homes]]
    pallas_call x6, Pallas kernels: 19.7 us -> 4.91 us  [hop_call(): pl.pallas_call(kernel, grid_spec=pltpu.PrefetchScalarGridSpec(num_scalar_...]
    ppermute x2, waiting for transfers between devices: 5.75 us -> 18.1 us  [across_dp(): return lax.ppermute(value, 'dp', [(i, i ^ k) for i in range(owners)])]
    ppermute x6 -> x11, waiting for transfers between devices: 23.7 us -> 13.6 us  [to_chip(): lax.ppermute(value, 'tensor', [(i, i ^ k * CORES) for i in range(parts)])]
    unnamed x52 -> x60, local copies, waits for them, and re-layouts: 16.9 us -> 11.8 us
    ppermute x2, starting transfers between devices: 4.78 us -> 0.14 us  [across_dp(): return lax.ppermute(value, 'dp', [(i, i ^ k) for i in range(owners)])]
    ppermute x2, waiting for transfers between devices: 4.11 us -> 0.01 us  [first(): lax.ppermute(inward, 'dp', [(3, 2), (0, 1)])]
  transfers between devices with their start and end apart: 26 -> 36, of which waited for: 14 -> 11; matrix products, arithmetic and copies ran while one was open for 2% -> 0% of each run, Pallas kernels for 15% -> 32%
where the time goes in v5:
time: 167 us; the launch traced here: 165 us
  Pallas kernels  62.3 us (37%)
  waiting for transfers between devices  39.8 us (24%)
  starting transfers between devices  35.3 us (21%)
  between operations  14.6 us (9%)
  local copies, waits for them, and re-layouts  12.5 us (7%)
    pallas_call x8, Pallas kernels, split_product(): pl.pallas_call(functools.partial(split_product_kernel, index_of, min(512,...  43.2 us
    ppermute x2, waiting for transfers between devices, across_dp(): return lax.ppermute(value, 'dp', [(i, i ^ k) for i in range(owners)])  18.1 us
    ppermute x11, waiting for transfers between devices, to_chip(): lax.ppermute(value, 'tensor', [(i, i ^ k * CORES) for i in range(parts)])  13.6 us
    ppermute x11, starting transfers between devices, to_chip(): lax.ppermute(value, 'tensor', [(i, i ^ k * CORES) for i in range(parts)])  12.1 us
    unnamed x60, local copies, waits for them, and re-layouts  11.8 us
    ppermute x2, starting transfers between devices, first(): lax.ppermute(inward, 'dp', [(3, 2), (0, 1)])  10.5 us
    ppermute x2, waiting for transfers between devices, second(): lax.ppermute(outer, 'dp', [(1, 0), (0, 1), (3, 2)])  6.96 us
    ppermute x2, starting transfers between devices, second(): lax.ppermute(outer, 'dp', [(1, 0), (0, 1), (3, 2)])  6.5 us
  transfers between devices with their start and end apart: 36, of which 11 were waited for; matrix products, arithmetic and copies ran while one was open for 0% of the time, Pallas kernels for 32%

profile of v5, /device:TPU:0, one launch (start us, length us, event | category | flops | bytes accessed | tf_op | source)
XLA Modules:
  0.0 164.7 jit_solution(9699587189867543098)
XLA Ops:
  10.0 4.9 %collective-permute-start.2 = (bf16[64,2048]{1,0:T(8,128)(2,1)S(1)}, bf16[64,2048]{1,0:T(8,128)(2,1)S(1)}, u32[]{:S(2)}, u32[]{:S(2)}) collective-permute-start(bf16[64,2048]{1,0:T(8,128)(2,1)S(1)} %get-tuple-element.41.refs_0_), channel_id=1, source_target_pairs={{12,8},{0,4},{13,9},{1,5},{14,10},{2,6},{15,11},{3,7},{28,24},{16,... | collective-permute-start | bytes 786440 | tf_op jit(solution)/shard_map/ppermute | solution.py:182
  15.6 1.6 copy-done.2
  19.4 1.6 narrow.1
  22.2 4.6 %collective-permute-start.4 = (bf16[64,2048]{1,0:T(8,128)(2,1)S(1)}, bf16[64,2048]{1,0:T(8,128)(2,1)S(1)}, u32[]{:S(2)}, u32[]{:S(2)}) collective-permute-start(bf16[64,2048]{1,0:T(8,128)(2,1)S(1)} %get-tuple-element.46), channel_id=1, source_target_pairs={{4,0},{0,4},{12,8},{5,1},{1,5},{13,9},{6,2},{2,6},{14,10},{7,3},{3... | collective-permute-start | bytes 786440 | tf_op jit(solution)/shard_map/ppermute | solution.py:190
  29.1 2.4 %collective-permute-done.1.refs_0_ = f32[1,64,128]{2,1,0:T(8,128)S(1)} collective-permute-done((f32[1,64,128]{2,1,0:T(8,128)S(1)}, f32[1,64,128]{2,1,0:T(8,128)S(1)}, u32[]{:S(2)}, u32[]{:S(2)}) %collective-permute-start.1) | collective-permute-done | bytes 32800 | tf_op jit(solution)/shard_map/ppermute | solution.py:556
  34.8 5.6 %collective-permute-start.10 = (bf16[64,2048]{1,0:T(8,128)(2,1)S(1)}, bf16[64,2048]{1,0:T(8,128)(2,1)S(1)}, u32[]{:S(2)}, u32[]{:S(2)}) collective-permute-start(bf16[64,2048]{1,0:T(8,128)(2,1)S(1)} %get-tuple-element.48.refs_1_), channel_id=1, source_target_pairs={{12,8},{0,4},{13,9},{1,5},{14,10},{2,6},{15,11},{3,7},{28,24},{16,... | collective-permute-start | bytes 786440 | tf_op jit(solution)/shard_map/ppermute | solution.py:182
  42.8 8.7 %collective-permute-done.6 = f32[2,1,64,128]{3,2,1,0:T(8,128)S(1)} collective-permute-done((f32[2,1,64,128]{3,2,1,0:T(8,128)S(1)}, f32[2,1,64,128]{3,2,1,0:T(8,128)S(1)}, u32[]{:S(2)}, u32[]{:S(2)}) %collective-permute-start.6) | collective-permute-done | bytes 65568 | tf_op jit(solution)/shard_map/ppermute | solution.py:559
  51.6 9.4 %collective-permute-done.7.more_ref = f32[2,1,64,128]{3,2,1,0:T(8,128)S(1)} collective-permute-done((f32[2,1,64,128]{3,2,1,0:T(8,128)S(1)}, f32[2,1,64,128]{3,2,1,0:T(8,128)S(1)}, u32[]{:S(2)}, u32[]{:S(2)}) %collective-permute-start.7) | collective-permute-done | bytes 65568 | tf_op jit(solution)/shard_map/ppermute | solution.py:559
  64.2 1.9 %collective-permute-start.12 = (bf16[64,2048]{1,0:T(8,128)(2,1)S(1)}, bf16[64,2048]{1,0:T(8,128)(2,1)S(1)}, u32[]{:S(2)}, u32[]{:S(2)}) collective-permute-start(bf16[64,2048]{1,0:T(8,128)(2,1)S(1)} %get-tuple-element.54), channel_id=1, source_target_pairs={{4,0},{0,4},{12,8},{5,1},{1,5},{13,9},{6,2},{2,6},{14,10},{7,3},{3... | collective-permute-start | bytes 786440 | tf_op jit(solution)/shard_map/ppermute | solution.py:190
  66.8 5.7 %collective-permute-done.12.x_ref = bf16[64,2048]{1,0:T(8,128)(2,1)S(1)} collective-permute-done((bf16[64,2048]{1,0:T(8,128)(2,1)S(1)}, bf16[64,2048]{1,0:T(8,128)(2,1)S(1)}, u32[]{:S(2)}, u32[]{:S(2)}) %collective-permute-start.12) | collective-permute-done | bytes 262176 | tf_op jit(solution)/shard_map/ppermute | solution.py:190
  73.8 5.4 %split_product.14 = (bf16[128,1024]{1,0:T(8,128)(2,1)S(1)}, f32[64,1024]{1,0:T(8,128)S(1)}, f32[64,1024]{1,0:T(8,128)S(1)}) custom-call(s32[14]{0:T(128)S(1)} %concatenate.3.index_ref.refs_0_, bf16[4,64,2048]{2,1,0:T(8,128)(2,1)} %bitcast.13, bf16[2048,4096]{1,0:T(8,128)(2,1)} %w_ref.15, bf16[1,64,4096]{2,1,0:T(8,128)(2,1)S(1)} %collective-permute-done.24.refs_0_.refs_1_, ...), custom_call_target="tpu_custom_call" | custom-call | flops 1 | bytes 1 | tf_op jit(solution)/shard_map/split_product/pallas_call | solution.py:245
  79.4 5.4 %split_product.10 = (bf16[128,1024]{1,0:T(8,128)(2,1)S(1)}, f32[64,1024]{1,0:T(8,128)S(1)}, f32[64,1024]{1,0:T(8,128)S(1)}) custom-call(s32[14]{0:T(128)S(1)} %concatenate.3.index_ref.refs_0_, bf16[4,64,2048]{2,1,0:T(8,128)(2,1)} %bitcast.14, bf16[2048,4096]{1,0:T(8,128)(2,1)} %w_ref.15), custom_call_target="tpu_custom_call" | custom-call | flops 1 | bytes 1 | tf_op jit(solution)/shard_map/split_product/pallas_call | solution.py:245
  86.0 5.4 %split_product.12 = (bf16[128,1024]{1,0:T(8,128)(2,1)S(1)}, f32[64,1024]{1,0:T(8,128)S(1)}, f32[64,1024]{1,0:T(8,128)S(1)}) custom-call(s32[14]{0:T(128)S(1)} %concatenate.3.index_ref.refs_0_, bf16[4,64,2048]{2,1,0:T(8,128)(2,1)} %bitcast.15, bf16[2048,4096]{1,0:T(8,128)(2,1)} %w_ref.15), custom_call_target="tpu_custom_call" | custom-call | flops 1 | bytes 1 | tf_op jit(solution)/shard_map/split_product/pallas_call | solution.py:245
  92.1 5.4 %split_product.8 = (bf16[128,1024]{1,0:T(8,128)(2,1)S(1)}, f32[64,1024]{1,0:T(8,128)S(1)}, f32[64,1024]{1,0:T(8,128)S(1)}) custom-call(s32[14]{0:T(128)S(1)} %concatenate.3.index_ref.refs_0_, bf16[4,64,2048]{2,1,0:T(8,128)(2,1)} %bitcast.16, bf16[2048,4096]{1,0:T(8,128)(2,1)} %w_ref.15), custom_call_target="tpu_custom_call" | custom-call | flops 1 | bytes 1 | tf_op jit(solution)/shard_map/split_product/pallas_call | solution.py:245
  103.2 2.0 %collective-permute-done.26.refs_0_.refs_5_ = bf16[64,1024]{1,0:T(8,128)(2,1)S(1)} collective-permute-done((bf16[64,1024]{1,0:T(8,128)(2,1)S(1)}, bf16[64,1024]{1,0:T(8,128)(2,1)S(1)}, u32[]{:S(2)}, u32[]{:S(2)}) %collective-permute-start.26) | collective-permute-done | bytes 131104 | tf_op jit(solution)/shard_map/ppermute | solution.py:556
  105.2 2.8 %collective-permute-done.17.refs_2_.refs_5_ = bf16[64,1024]{1,0:T(8,128)(2,1)S(1)} collective-permute-done((bf16[64,1024]{1,0:T(8,128)(2,1)S(1)}, bf16[64,1024]{1,0:T(8,128)(2,1)S(1)}, u32[]{:S(2)}, u32[]{:S(2)}) %collective-permute-start.17) | collective-permute-done | bytes 131104 | tf_op jit(solution)/shard_map/ppermute | solution.py:556
  108.0 2.8 %collective-permute-done.21.refs_1_.refs_5_ = bf16[64,1024]{1,0:T(8,128)(2,1)S(1)} collective-permute-done((bf16[64,1024]{1,0:T(8,128)(2,1)S(1)}, bf16[64,1024]{1,0:T(8,128)(2,1)S(1)}, u32[]{:S(2)}, u32[]{:S(2)}) %collective-permute-start.21) | collective-permute-done | bytes 131104 | tf_op jit(solution)/shard_map/ppermute | solution.py:556
  113.6 5.4 %split_product.15 = (bf16[128,1024]{1,0:T(8,128)(2,1)S(1)}, f32[64,1024]{1,0:T(8,128)S(1)}, f32[64,1024]{1,0:T(8,128)S(1)}) custom-call(s32[14]{0:T(128)S(1)} %concatenate.3.index_ref.refs_0_, bf16[4,64,2048]{2,1,0:T(8,128)(2,1)} %bitcast.9, bf16[2048,4096]{1,0:T(8,128)(2,1)} %w_ref.15, bf16[64,1024]{1,0:T(8,128)(2,1)S(1)} %collective-permute-done.26.refs_0_.refs_5_, ...), custom_call_target="tpu_custom_call" | custom-call | flops 1 | bytes 1 | tf_op jit(solution)/shard_map/split_product/pallas_call | solution.py:245
  119.1 5.4 %split_product.13 = (bf16[128,1024]{1,0:T(8,128)(2,1)S(1)}, f32[64,1024]{1,0:T(8,128)S(1)}, f32[64,1024]{1,0:T(8,128)S(1)}) custom-call(s32[14]{0:T(128)S(1)} %concatenate.3.index_ref.refs_0_, bf16[4,64,2048]{2,1,0:T(8,128)(2,1)} %bitcast.10, bf16[2048,4096]{1,0:T(8,128)(2,1)} %w_ref.15), custom_call_target="tpu_custom_call" | custom-call | flops 1 | bytes 1 | tf_op jit(solution)/shard_map/split_product/pallas_call | solution.py:245
  126.5 2.4 %collective-permute-done.31.refs_1_ = bf16[1,64,128]{2,1,0:T(8,128)(2,1)S(1)} collective-permute-done((bf16[1,64,128]{2,1,0:T(8,128)(2,1)S(1)}, bf16[1,64,128]{2,1,0:T(8,128)(2,1)S(1)}, u32[]{:S(2)}, u32[]{:S(2)}) %collective-permute-start.31) | collective-permute-done | bytes 16416 | tf_op jit(solution)/shard_map/ppermute | solution.py:556
  128.8 5.4 %split_product.11 = (bf16[128,1024]{1,0:T(8,128)(2,1)S(1)}, f32[64,1024]{1,0:T(8,128)S(1)}, f32[64,1024]{1,0:T(8,128)S(1)}) custom-call(s32[14]{0:T(128)S(1)} %concatenate.3.index_ref.refs_0_, bf16[4,64,2048]{2,1,0:T(8,128)(2,1)} %bitcast.11, bf16[2048,4096]{1,0:T(8,128)(2,1)} %w_ref.15), custom_call_target="tpu_custom_call" | custom-call | flops 1 | bytes 1 | tf_op jit(solution)/shard_map/split_product/pallas_call | solution.py:245
  134.2 5.4 %split_product.9 = (bf16[128,1024]{1,0:T(8,128)(2,1)S(1)}, f32[64,1024]{1,0:T(8,128)S(1)}, f32[64,1024]{1,0:T(8,128)S(1)}) custom-call(s32[14]{0:T(128)S(1)} %concatenate.3.index_ref.refs_0_, bf16[4,64,2048]{2,1,0:T(8,128)(2,1)} %bitcast.12, bf16[2048,4096]{1,0:T(8,128)(2,1)} %w_ref.15), custom_call_target="tpu_custom_call" | custom-call | flops 1 | bytes 1 | tf_op jit(solution)/shard_map/split_product/pallas_call | solution.py:245
  146.1 1.6 down_gradient.1.refs_10_
  147.7 3.9 %up_gradient.1.refs_9_ = f32[4,64,4096]{2,1,0:T(8,128)} custom-call(s32[14]{0:T(128)S(1)} %concatenate.3.index_ref.refs_0_, bf16[1,64,4096]{2,1,0:T(8,128)(2,1)S(1)} %copy-done.10, bf16[1,64,4096]{2,1,0:T(8,128)(2,1)S(1)} %collective-permute-done.24.refs_0_.refs_1_, bf16[1,64,4096]{2,1,0:T(8,128)(2,1)S(1)} %collective-permute-done.29.refs_2_, ...), custom_call_target="tpu_custom_call" | custom-call | flops 1 | bytes 1 | tf_op jit(solution)/shard_map/up_gradient/pallas_call | solution.py:440
  (144 shorter events, 45.1 us)
Async XLA Ops:
  7.2 66.7 %all-gather.5.cloned.1.call-start = ((), (), s32[]{:S(2)}) async-start(), calls=%async_computation | async-start | bytes 1310720 | tf_op jit(solution)/shard_map/all_gather | solution.py:607
  10.0 11.6 %collective-permute-start.2 = (bf16[64,2048]{1,0:T(8,128)(2,1)S(1)}, bf16[64,2048]{1,0:T(8,128)(2,1)S(1)}, u32[]{:S(2)}, u32[]{:S(2)}) collective-permute-start(bf16[64,2048]{1,0:T(8,128)(2,1)S(1)} %get-tuple-element.41.refs_0_), channel_id=1, source_target_pairs={{12,8},{0,4},{13,9},{1,5},{14,10},{2,6},{15,11},{3,7},{28,24},{16,... | collective-permute-start | bytes 786440 | tf_op jit(solution)/shard_map/ppermute | solution.py:182
  22.2 10.6 %collective-permute-start.4 = (bf16[64,2048]{1,0:T(8,128)(2,1)S(1)}, bf16[64,2048]{1,0:T(8,128)(2,1)S(1)}, u32[]{:S(2)}, u32[]{:S(2)}) collective-permute-start(bf16[64,2048]{1,0:T(8,128)(2,1)S(1)} %get-tuple-element.46), channel_id=1, source_target_pairs={{4,0},{0,4},{12,8},{5,1},{1,5},{13,9},{6,2},{2,6},{14,10},{7,3},{3... | collective-permute-start | bytes 786440 | tf_op jit(solution)/shard_map/ppermute | solution.py:190
  34.1 78.6 %all-gather.7.cloned.1.call-start = ((), (), s32[]{:S(2)}) async-start(), calls=%async_computation.1 | async-start | bytes 1310720 | tf_op jit(solution)/shard_map/all_gather | solution.py:607
  34.8 28.9 %collective-permute-start.10 = (bf16[64,2048]{1,0:T(8,128)(2,1)S(1)}, bf16[64,2048]{1,0:T(8,128)(2,1)S(1)}, u32[]{:S(2)}, u32[]{:S(2)}) collective-permute-start(bf16[64,2048]{1,0:T(8,128)(2,1)S(1)} %get-tuple-element.48.refs_1_), channel_id=1, source_target_pairs={{12,8},{0,4},{13,9},{1,5},{14,10},{2,6},{15,11},{3,7},{28,24},{16,... | collective-permute-start | bytes 786440 | tf_op jit(solution)/shard_map/ppermute | solution.py:182
  40.4 23.3 %collective-permute-start.11 = (bf16[64,2048]{1,0:T(8,128)(2,1)S(1)}, bf16[64,2048]{1,0:T(8,128)(2,1)S(1)}, u32[]{:S(2)}, u32[]{:S(2)}) collective-permute-start(bf16[64,2048]{1,0:T(8,128)(2,1)S(1)} %get-tuple-element.53), channel_id=1, source_target_pairs={{8,4},{9,5},{10,6},{11,7},{24,20},{25,21},{26,22},{27,23}} | collective-permute-start | bytes 786440 | tf_op jit(solution)/shard_map/ppermute | solution.py:183
  42.8 8.8 %collective-permute-start.6 = (f32[2,1,64,128]{3,2,1,0:T(8,128)S(1)}, f32[2,1,64,128]{3,2,1,0:T(8,128)S(1)}, u32[]{:S(2)}, u32[]{:S(2)}) collective-permute-start(f32[2,1,64,128]{3,2,1,0:T(8,128)S(1)} %merge.1), channel_id=1, source_target_pairs={{0,4},{4,0},{8,12},{12,8},{1,5},{5,1},{9,13},{13,9},{2,6},{6,2},{1... | collective-permute-start | bytes 196616 | tf_op jit(solution)/shard_map/ppermute | solution.py:559
  51.6 9.4 %collective-permute-start.7 = (f32[2,1,64,128]{3,2,1,0:T(8,128)S(1)}, f32[2,1,64,128]{3,2,1,0:T(8,128)S(1)}, u32[]{:S(2)}, u32[]{:S(2)}) collective-permute-start(f32[2,1,64,128]{3,2,1,0:T(8,128)S(1)} %add.43.sum_ref), channel_id=1, source_target_pairs={{0,8},{4,12},{8,0},{12,4},{1,9},{5,13},{9,1},{13,5},{2,10},{6,14},... | collective-permute-start | bytes 196616 | tf_op jit(solution)/shard_map/ppermute | solution.py:559
  62.5 11.3 %collective-permute-start.24 = (bf16[1,64,4096]{2,1,0:T(8,128)(2,1)S(1)}, bf16[1,64,4096]{2,1,0:T(8,128)(2,1)S(1)}, u32[]{:S(2)}, u32[]{:S(2)}) collective-permute-start(bf16[1,64,4096]{2,1,0:T(8,128)(2,1)S(1)} %get-tuple-element.71.refs_0_), channel_id=1, source_target_pairs={{0,2},{1,3},{2,0},{3,1},{4,6},{5,7},{6,4},{7,5},{8,10},{9,11},{10,... | collective-permute-start | bytes 1572872 | tf_op jit(solution)/shard_map/ppermute | solution.py:556
  64.2 8.3 %collective-permute-start.12 = (bf16[64,2048]{1,0:T(8,128)(2,1)S(1)}, bf16[64,2048]{1,0:T(8,128)(2,1)S(1)}, u32[]{:S(2)}, u32[]{:S(2)}) collective-permute-start(bf16[64,2048]{1,0:T(8,128)(2,1)S(1)} %get-tuple-element.54), channel_id=1, source_target_pairs={{4,0},{0,4},{12,8},{5,1},{1,5},{13,9},{6,2},{2,6},{14,10},{7,3},{3... | collective-permute-start | bytes 786440 | tf_op jit(solution)/shard_map/ppermute | solution.py:190
  79.3 19.5 %collective-permute-start.25 = (bf16[128,1024]{1,0:T(8,128)(2,1)S(1)}, bf16[128,1024]{1,0:T(8,128)(2,1)S(1)}, u32[]{:S(2)}, u32[]{:S(2)}) collective-permute-start(bf16[128,1024]{1,0:T(8,128)(2,1)S(1)} %get-tuple-element.73), channel_id=1, source_target_pairs={{0,1},{1,0},{2,3},{3,2},{4,5},{5,4},{6,7},{7,6},{8,9},{9,8},{10,11... | collective-permute-start | bytes 786440 | tf_op jit(solution)/shard_map/ppermute | solution.py:553
  85.5 14.2 %collective-permute-start.16 = (bf16[128,1024]{1,0:T(8,128)(2,1)S(1)}, bf16[128,1024]{1,0:T(8,128)(2,1)S(1)}, u32[]{:S(2)}, u32[]{:S(2)}) collective-permute-start(bf16[128,1024]{1,0:T(8,128)(2,1)S(1)} %get-tuple-element.60), channel_id=1, source_target_pairs={{0,1},{1,0},{2,3},{3,2},{4,5},{5,4},{6,7},{7,6},{8,9},{9,8},{10,11... | collective-permute-start | bytes 786440 | tf_op jit(solution)/shard_map/ppermute | solution.py:553
  99.8 8.2 %collective-permute-start.17 = (bf16[64,1024]{1,0:T(8,128)(2,1)S(1)}, bf16[64,1024]{1,0:T(8,128)(2,1)S(1)}, u32[]{:S(2)}, u32[]{:S(2)}) collective-permute-start(bf16[64,1024]{1,0:T(8,128)(2,1)S(1)} %add_convert_fusion.5), channel_id=1, source_target_pairs={{0,2},{1,3},{2,0},{3,1},{4,6},{5,7},{6,4},{7,5},{8,10},{9,11},{10,... | collective-permute-start | bytes 393224 | tf_op jit(solution)/shard_map/ppermute | solution.py:556
  101.0 9.8 %collective-permute-start.21 = (bf16[64,1024]{1,0:T(8,128)(2,1)S(1)}, bf16[64,1024]{1,0:T(8,128)(2,1)S(1)}, u32[]{:S(2)}, u32[]{:S(2)}) collective-permute-start(bf16[64,1024]{1,0:T(8,128)(2,1)S(1)} %add_convert_fusion.3), channel_id=1, source_target_pairs={{0,2},{1,3},{2,0},{3,1},{4,6},{5,7},{6,4},{7,5},{8,10},{9,11},{10,... | collective-permute-start | bytes 393224 | tf_op jit(solution)/shard_map/ppermute | solution.py:556
  102.0 10.7 %collective-permute-start.9 = (bf16[64,1024]{1,0:T(8,128)(2,1)S(1)}, bf16[64,1024]{1,0:T(8,128)(2,1)S(1)}, u32[]{:S(2)}, u32[]{:S(2)}) collective-permute-start(bf16[64,1024]{1,0:T(8,128)(2,1)S(1)} %add_convert_fusion.7), channel_id=1, source_target_pairs={{0,2},{1,3},{2,0},{3,1},{4,6},{5,7},{6,4},{7,5},{8,10},{9,11},{10,... | collective-permute-start | bytes 393224 | tf_op jit(solution)/shard_map/ppermute | solution.py:556
  119.0 20.6 %collective-permute-start.27 = (bf16[128,1024]{1,0:T(8,128)(2,1)S(1)}, bf16[128,1024]{1,0:T(8,128)(2,1)S(1)}, u32[]{:S(2)}, u32[]{:S(2)}) collective-permute-start(bf16[128,1024]{1,0:T(8,128)(2,1)S(1)} %get-tuple-element.76), channel_id=1, source_target_pairs={{0,1},{1,0},{2,3},{3,2},{4,5},{5,4},{6,7},{7,6},{8,9},{9,8},{10,11... | collective-permute-start | bytes 786440 | tf_op jit(solution)/shard_map/ppermute | solution.py:553
  124.5 15.7 %collective-permute-start.22 = (bf16[128,1024]{1,0:T(8,128)(2,1)S(1)}, bf16[128,1024]{1,0:T(8,128)(2,1)S(1)}, u32[]{:S(2)}, u32[]{:S(2)}) collective-permute-start(bf16[128,1024]{1,0:T(8,128)(2,1)S(1)} %get-tuple-element.69), channel_id=1, source_target_pairs={{0,1},{1,0},{2,3},{3,2},{4,5},{5,4},{6,7},{7,6},{8,9},{9,8},{10,11... | collective-permute-start | bytes 786440 | tf_op jit(solution)/shard_map/ppermute | solution.py:553
  126.0 18.9 %collective-permute-start.29 = (bf16[1,64,4096]{2,1,0:T(8,128)(2,1)S(1)}, bf16[1,64,4096]{2,1,0:T(8,128)(2,1)S(1)}, u32[]{:S(2)}, u32[]{:S(2)}) collective-permute-start(bf16[1,64,4096]{2,1,0:T(8,128)(2,1)S(1)} %copy-done.10), channel_id=1, source_target_pairs={{0,1},{1,0},{2,3},{3,2},{4,5},{5,4},{6,7},{7,6},{8,9},{9,8},{10,11... | collective-permute-start | bytes 1572872 | tf_op jit(solution)/shard_map/ppermute | solution.py:553
  126.0 15.8 %collective-permute-start.32 = (bf16[1,64,128]{2,1,0:T(8,128)(2,1)S(1)}, bf16[1,64,128]{2,1,0:T(8,128)(2,1)S(1)}, u32[]{:S(2)}, u32[]{:S(2)}) collective-permute-start(bf16[1,64,128]{2,1,0:T(8,128)(2,1)S(1)} %copy-done.29), channel_id=1, source_target_pairs={{0,1},{1,0},{2,3},{3,2},{4,5},{5,4},{6,7},{7,6},{8,9},{9,8},{10,11... | collective-permute-start | bytes 49160 | tf_op jit(solution)/shard_map/ppermute | solution.py:553
  128.8 13.9 %collective-permute-start.33 = (bf16[1,64,128]{2,1,0:T(8,128)(2,1)S(1)}, bf16[1,64,128]{2,1,0:T(8,128)(2,1)S(1)}, u32[]{:S(2)}, u32[]{:S(2)}) collective-permute-start(bf16[1,64,128]{2,1,0:T(8,128)(2,1)S(1)} %collective-permute-done.31.refs_1_), channel_id=1, source_target_pairs={{0,1},{1,0},{2,3},{3,2},{4,5},{5,4},{6,7},{7,6},{8,9},{9,8},{10,11... | collective-permute-start | bytes 49160 | tf_op jit(solution)/shard_map/ppermute | solution.py:553
  141.8 9.8 %collective-permute-start.28 = (bf16[64,1024]{1,0:T(8,128)(2,1)S(1)}, bf16[64,1024]{1,0:T(8,128)(2,1)S(1)}, u32[]{:S(2)}, u32[]{:S(2)}) collective-permute-start(bf16[64,1024]{1,0:T(8,128)(2,1)S(1)} %add_convert_fusion), channel_id=1, source_target_pairs={{0,2},{1,3},{2,0},{3,1},{4,6},{5,7},{6,4},{7,5},{8,10},{9,11},{10,... | collective-permute-start | bytes 393224 | tf_op jit(solution)/shard_map/ppermute | solution.py:556
  142.7 10.4 %collective-permute-start.23 = (bf16[64,1024]{1,0:T(8,128)(2,1)S(1)}, bf16[64,1024]{1,0:T(8,128)(2,1)S(1)}, u32[]{:S(2)}, u32[]{:S(2)}) collective-permute-start(bf16[64,1024]{1,0:T(8,128)(2,1)S(1)} %add_convert_fusion.2), channel_id=1, source_target_pairs={{0,2},{1,3},{2,0},{3,1},{4,6},{5,7},{6,4},{7,5},{8,10},{9,11},{10,... | collective-permute-start | bytes 393224 | tf_op jit(solution)/shard_map/ppermute | solution.py:556
  143.9 10.9 %collective-permute-start.19 = (bf16[64,1024]{1,0:T(8,128)(2,1)S(1)}, bf16[64,1024]{1,0:T(8,128)(2,1)S(1)}, u32[]{:S(2)}, u32[]{:S(2)}) collective-permute-start(bf16[64,1024]{1,0:T(8,128)(2,1)S(1)} %add_convert_fusion.4), channel_id=1, source_target_pairs={{0,2},{1,3},{2,0},{3,1},{4,6},{5,7},{6,4},{7,5},{8,10},{9,11},{10,... | collective-permute-start | bytes 393224 | tf_op jit(solution)/shard_map/ppermute | solution.py:556
  144.8 11.5 %collective-permute-start.15 = (bf16[64,1024]{1,0:T(8,128)(2,1)S(1)}, bf16[64,1024]{1,0:T(8,128)(2,1)S(1)}, u32[]{:S(2)}, u32[]{:S(2)}) collective-permute-start(bf16[64,1024]{1,0:T(8,128)(2,1)S(1)} %add_convert_fusion.6), channel_id=1, source_target_pairs={{0,2},{1,3},{2,0},{3,1},{4,6},{5,7},{6,4},{7,5},{8,10},{9,11},{10,... | collective-permute-start | bytes 393224 | tf_op jit(solution)/shard_map/ppermute | solution.py:556
  (42 other events, 234.0 us)
Sparse Core Ops, SparseCore 0:
  34.2 34.5 all-gather.4
  73.9 28.7 all-gather.6

commit v6 on v5

--- a/solution.py
+++ b/solution.py
@@ -11,7 +11,7 @@
 CAP = 3
 CORES = 2
 CHUNK_ROWS = (64, 64)
-PARTS = 4
+PARTS = (4, 2)
 SMALL = pltpu.CompilerParams(vmem_limit_bytes=12 * 2**20)
 
 adapter_scale = 0.5
@@ -138,7 +138,7 @@
     return specs, [*values, *(in_hbm(v) for v in far)]
 
 
-def hop_call(kernel, index, tokens, unit, count, stay, received, waits, name):
+def hop_call(kernel, index, tokens, unit, count, stay, received, waits, name, declared):
     specs, extra = after((), waits) if waits and waits[0].shape == unit.shape else after(waits)
     out = pltpu.VMEM(unit.shape, unit.dtype) if stay else unit
     return pl.pallas_call(
@@ -151,7 +151,7 @@
         ),
         out_shape=[out] * count,
         compiler_params=SMALL,
-        cost_estimate=BRIEF,
+        cost_estimate=declared,
         name=name,
     )(index, tokens, *[in_vmem(r) for r in received], *extra)
 
@@ -162,7 +162,7 @@
         self.start = sum(CHUNK_ROWS[:chunk])
         self.unit = shape_of((CHUNK_ROWS[chunk], tokens.shape[1]), tokens.dtype)
 
-    def call(self, kernel, count, stay, received, waits, name):
+    def call(self, kernel, count, stay, received, waits, name, declared=BRIEF):
         return hop_call(
             functools.partial(kernel, self.index_of, self.start),
             self.index,
@@ -173,6 +173,7 @@
             received,
             waits,
             name,
+            declared,
         )
 
     def first(self, waits=()):
@@ -191,76 +192,87 @@
             lax.ppermute(middle, "dp", [(2, 1), (1, 2)]),
         )
 
-    def settle(self, waits=()):
-        (self.sent,) = self.call(settle_kernel, 1, False, self.received, waits, "settle")
+    def settle(self, waits=(), declared=BRIEF):
+        (self.sent,) = self.call(
+            settle_kernel, 1, False, self.received, waits, "settle", declared
+        )
         return self.sent
 
 
-def split_product_kernel(index_of, tile, index_ref, x_ref, w_ref, *refs):
-    send_ref, other_ref, own_ref, sent = refs[-4:]
-    index = index_of(index_ref)
-    step = pl.program_id(0)
-    each = index.per_part * x_ref.shape[1]
+def split_product_kernel(index_of, first, index_ref, x_ref, w_ref, *refs):
+    send_ref, other_ref, own_ref, rows, tiles, rows_sems, tile_sems = refs[-7:]
+    index = index_of(index_ref)
+    count, tile = x_ref.shape[1], tiles.shape[2]
+    each = index.per_part * count
     half = index.chips * each
-    rows = jnp.concatenate(
-        [
-            x_ref[index.block(core_bit, chip_bits, i)]
-            for core_bit in (1, 0)
-            for chip_bits in range(index.chips)
-            for i in range(index.per_part)
-        ],
-        axis=0,
-    )
-    for n in range(w_ref.shape[1] // tile):
+    buffers, steps = tiles.shape[0], own_ref.shape[1] // tile
+
+    def weight_copy(n):
+        return pltpu.make_async_copy(
+            w_ref.at[:, pl.ds(first + n * tile, tile)],
+            tiles.at[n % buffers],
+            tile_sems.at[n % buffers],
+        )
+
+    order = [
+        index.block(core_bit, chip_bits, i)
+        for core_bit in (1, 0)
+        for chip_bits in range(index.chips)
+        for i in range(index.per_part)
+    ]
+    row_copies = [
+        pltpu.make_async_copy(
+            x_ref.at[block], rows.at[pl.ds(j * count, count)], rows_sems.at[j]
+        )
+        for j, block in enumerate(order)
+    ]
+    weight_copy(0).start()
+    for copy in row_copies:
+        copy.start()
+    for n in range(1, min(buffers, steps)):
+        weight_copy(n).start()
+    for copy in row_copies:
+        copy.wait()
+    for n in range(steps):
+        weight_copy(n).wait()
+        total = jnp.dot(rows[...], tiles[n % buffers], preferred_element_type=jnp.float32)
         columns = slice(n * tile, (n + 1) * tile)
-        total = jnp.dot(rows, w_ref[:, columns], preferred_element_type=jnp.float32)
-        parts = (
-            (sent, total[:half]),
-            (own_ref, total[half : half + each]),
-            (other_ref, total[half + each :]),
-        )
-
-        @pl.when(step == 0)
-        def _():
-            for ref, value in parts:
-                ref[:, columns] = value
-
-        @pl.when(step > 0)
-        def _():
-            for ref, value in parts:
-                ref[:, columns] += value
-
-    @pl.when(step == pl.num_programs(0) - 1)
-    def _():
-        send_ref[...] = sent[...].astype(send_ref.dtype)
+        send_ref[:, columns] = total[:half].astype(send_ref.dtype)
+        own_ref[:, columns] = total[half : half + each]
+        other_ref[:, columns] = total[half + each :]
+        if n + buffers < steps:
+            weight_copy(n + buffers).start()
 
 
 def split_product(index_of, index, shape, rows, weight, part, part_count, waits, far):
     block_count, count, depth = rows.shape
     width = weight.shape[1] // part_count
-    deep = min(512, depth)
+    tile = min(512, width)
+    buffers = min(4, width // tile)
     each = shape.per_part * count
     half = block_count * count // 2
     specs, extra = after(waits, far)
+    hbm = pl.BlockSpec(memory_space=pl.ANY)
     return pl.pallas_call(
-        functools.partial(split_product_kernel, index_of, min(512, width)),
+        functools.partial(split_product_kernel, index_of, part * width),
         grid_spec=pltpu.PrefetchScalarGridSpec(
             num_scalar_prefetch=1,
-            grid=(depth // deep,),
-            in_specs=[
-                pl.BlockSpec((block_count, count, deep), lambda k, _: (0, 0, k)),
-                pl.BlockSpec((deep, width), lambda k, _: (k, part)),
-            ]
-            + specs,
-            out_specs=[whole((half, width)), whole((half - each, width)), whole((each, width))],
-            scratch_shapes=[pltpu.VMEM((half, width), jnp.float32)],
+            grid=(1,),
+            in_specs=[hbm, hbm] + specs,
+            out_specs=[held()] * 3,
+            scratch_shapes=[
+                pltpu.VMEM((block_count * count, depth), rows.dtype),
+                pltpu.VMEM((buffers, depth, tile), weight.dtype),
+                pltpu.SemaphoreType.DMA((block_count,)),
+                pltpu.SemaphoreType.DMA((buffers,)),
+            ],
         ),
         out_shape=[
-            shape_of((half, width), jnp.bfloat16),
-            shape_of((half - each, width), jnp.float32),
-            shape_of((each, width), jnp.float32),
+            pltpu.VMEM((half, width), jnp.bfloat16),
+            pltpu.VMEM((half - each, width), jnp.float32),
+            pltpu.VMEM((each, width), jnp.float32),
         ],
-        compiler_params=pltpu.CompilerParams(vmem_limit_bytes=32 * 2**20),
+        compiler_params=pltpu.CompilerParams(vmem_limit_bytes=20 * 2**20),
         cost_estimate=BRIEF,
         name="split_product",
     )(index, in_hbm(rows), in_hbm(weight), *extra)
@@ -452,10 +464,10 @@
     )(index, *pieces)
 
 
-def finish_kernel(index_of, counts, index_ref, low_ref, *refs):
+def finish_kernel(index_of, layout, tiles, terms, index_ref, low_ref, *refs):
     index = index_of(index_ref)
     up_refs, sum_refs, out_ref = refs[: index.per_part], refs[index.per_part : -1], refs[-1]
-    per_chunk = len(sum_refs) // len(counts)
+    step = pl.program_id(0)
     for i in range(index.per_part):
         block = index.block(0, 0, i)
         live = index.live_rows(block)
@@ -465,21 +477,28 @@
             (((0,), (0,)), ((), ())),
             preferred_element_type=jnp.float32,
         )
-        start = 0
-        for c, count in enumerate(counts):
-            total = adapter_scale * side[start : start + count]
-            for ref in sum_refs[c * per_chunk : (c + 1) * per_chunk]:
-                total = total + ref[i * count : (i + 1) * count].astype(jnp.float32)
-            keep = start + lax.broadcasted_iota(jnp.int32, total.shape, 0) < live
-            at = i * BLK + start
-            out_ref[at : at + count] = jnp.where(keep, total, 0.0).astype(out_ref.dtype)
+        start, at_ref = 0, 0
+        for count, spans in layout:
+            for p in range(tiles // spans):
+                parts = sum_refs[at_ref : at_ref + terms]
+                at_ref += terms
+
+                @pl.when(step // spans == p)
+                def _(parts=parts, start=start, count=count):
+                    total = adapter_scale * side[start : start + count]
+                    for ref in parts:
+                        total = total + ref[i * count : (i + 1) * count].astype(jnp.float32)
+                    keep = start + lax.broadcasted_iota(jnp.int32, total.shape, 0) < live
+                    at = i * BLK + start
+                    out_ref[at : at + count] = jnp.where(keep, total, 0.0).astype(out_ref.dtype)
+
             start += count
 
 
 def finish(index_of, index, lowered, up, sums, part, part_count, projected, far):
     per_part = lowered.shape[0]
     _, rank, width = up.shape
-    tile = min(1024, width // part_count)
+    tile = width // max(PARTS)
     tiles = width // part_count // tile
     first = part * tiles
     out = (per_part * BLK, width)
@@ -491,14 +510,24 @@
 
         return pl.BlockSpec((1, rank, tile), at)
 
-    specs, flat = [], []
+    specs, flat, layout = [], [], []
     for chunk, count in zip(sums, CHUNK_ROWS):
-        for value in chunk:
-            begin = first if value.shape[1] == width else 0
-            specs.append(
-                pl.BlockSpec((per_part * count, tile), lambda n, _, begin=begin: (0, begin + n))
-            )
-            flat.append(value)
+        each = max(1, len(chunk) // part_count)
+        begin = part * len(chunk) // part_count
+        spans = tiles // each
+        layout.append((count, spans))
+        for p in range(each):
+            offset = first - begin * (width // len(chunk) // tile) - p * spans
+            limit = width // len(chunk) // tile - 1
+            for value in chunk[begin + p]:
+                specs.append(
+                    pl.BlockSpec(
+                        (per_part * count, tile),
+                        lambda n, _, o=offset, m=limit: (0, jnp.clip(o + n, 0, m)),
+                    )
+                )
+                flat.append(value)
+    terms = len(sums[0][0])
     operands = [index, lowered, *[up] * per_part, *flat]
     aliases = {}
     if projected is not None:
@@ -509,7 +538,7 @@
         extra = [projected]
 
     def kernel(*refs):
-        finish_kernel(index_of, CHUNK_ROWS, *refs[: len(operands)], refs[-1])
+        finish_kernel(index_of, layout, tiles, terms, *refs[: len(operands)], refs[-1])
 
     return pl.pallas_call(
         kernel,
@@ -596,8 +625,8 @@
         arrived, others = over_parts(send, keep)
         homes = [head.settle(others)]
         tail[0].first([homes[-1]])
+        tail[0].second()
         total = merge(keep, arrived, back, others, [tail[0].sent])
-        tail[0].second()
         homes.append(tail[0].settle())
         for homing in tail[1:]:
             homing.first([homes[-1]])
@@ -619,10 +648,10 @@
 
     pieces_same_core = [pieces] + [to_chip(pieces, k) for k in range(1, chips)]
 
-    def summed(rows, part, waits, far):
+    def summed(rows, part, part_count, waits, far):
         each = shape.per_part * rows.shape[1]
         send, other, own = split_product(
-            index_of, index, shape, rows, frozen_up_weight, part, PARTS, waits, far
+            index_of, index, shape, rows, frozen_up_weight, part, part_count, waits, far
         )
         arrived = to_other_core(send)
         outgoing = (other + arrived[each:].astype(jnp.float32)).astype(jnp.bfloat16)
@@ -630,26 +659,27 @@
             to_chip(outgoing[(k - 1) * each : k * each], k) for k in range(1, chips)
         ]
 
-    waits, far = pieces_same_core[1:], homes[1:]
-    sums = [[] for _ in range(PARTS)]
-    for rows in chunks:
-        for part in range(PARTS):
-            sums[part].append(summed(rows, part, waits, far))
+    waits, far = [lowered], homes[1:]
+    sums = []
+    for rows, part_count in zip(chunks, PARTS):
+        sums.append([])
+        for part in range(part_count):
+            sums[-1].append(summed(rows, part, part_count, waits, far))
             waits, far = [], []
-        waits = [v for part in sums for v in part[-1][2:]]
+        waits = pieces_same_core[1:] + [v for part in sums[-1] for v in part[2:]]
     pieces_all = pieces_same_core + [to_other_core(p) for p in pieces_same_core]
     up_grad = up_gradient(index_of, index, adapter_count, pieces_all)
     down_grad = down_gradient(index_of, index, rows_here, every_part(back_rows))
     projected = None
-    for part in range(PARTS):
+    for part in range(PARTS[-1]):
         projected = finish(
             index_of,
             index,
             lowered,
             adapter_up_factor,
-            sums[part],
+            sums,
             part,
-            PARTS,
+            PARTS[-1],
             projected,
             [up_grad, down_grad],
         )

time: 167 us -> 166 us (level)
  Pallas kernels: 62.3 us -> 47.8 us
  waiting for transfers between devices: 39.8 us -> 50 us
  starting transfers between devices: 35.3 us -> 43.2 us
  local copies, waits for them, and re-layouts: 12.5 us -> 9.6 us
    pallas_call x8 -> x6, Pallas kernels: 43.2 us -> 28.6 us  [split_product(): pl.pallas_call(functools.partial(split_product_kernel, index_of, part * w...]
    ppermute x2, waiting for transfers between devices: 18.1 us -> 5.49 us  [across_dp(): return lax.ppermute(value, 'dp', [(i, i ^ k) for i in range(owners)])]
    ppermute x2, waiting for transfers between devices: 6.96 us -> 15.7 us  [second(): lax.ppermute(outer, 'dp', [(1, 0), (0, 1), (3, 2)])]
    ppermute x11 -> x9, waiting for transfers between devices: 13.6 us -> 22.3 us  [to_chip(): lax.ppermute(value, 'tensor', [(i, i ^ k * CORES) for i in range(parts)])]
    ppermute x2, starting transfers between devices: 6.5 us -> 11.5 us  [second(): lax.ppermute(outer, 'dp', [(1, 0), (0, 1), (3, 2)])]
    ppermute x2, waiting for transfers between devices: 0.01 us -> 4.25 us  [first(): lax.ppermute(inward, 'dp', [(3, 2), (0, 1)])]
    ppermute x2, starting transfers between devices: 0.14 us -> 4.07 us  [across_dp(): return lax.ppermute(value, 'dp', [(i, i ^ k) for i in range(owners)])]
    unnamed x60 -> x44, local copies, waits for them, and re-layouts: 11.8 us -> 8.84 us
  transfers between devices with their start and end apart: 36 -> 32, of which waited for: 11 -> 13; matrix products, arithmetic and copies ran while one was open for 0% -> 0% of each run, Pallas kernels for 32% -> 22%
where the time goes in v6:
time: 166 us; the launch traced here: 165 us
  waiting for transfers between devices  50 us (30%)
  Pallas kernels  47.8 us (29%)
  starting transfers between devices  43.2 us (26%)
  between operations  14.5 us (9%)
  local copies, waits for them, and re-layouts  9.6 us (6%)
    pallas_call x6, Pallas kernels, split_product(): pl.pallas_call(functools.partial(split_product_kernel, index_of, part * w...  28.6 us
    ppermute x9, waiting for transfers between devices, to_chip(): lax.ppermute(value, 'tensor', [(i, i ^ k * CORES) for i in range(parts)])  22.3 us
    ppermute x2, waiting for transfers between devices, second(): lax.ppermute(outer, 'dp', [(1, 0), (0, 1), (3, 2)])  15.7 us
    ppermute x9, starting transfers between devices, to_chip(): lax.ppermute(value, 'tensor', [(i, i ^ k * CORES) for i in range(parts)])  11.9 us
    ppermute x2, starting transfers between devices, second(): lax.ppermute(outer, 'dp', [(1, 0), (0, 1), (3, 2)])  11.5 us
    ppermute x2, starting transfers between devices, first(): lax.ppermute(inward, 'dp', [(3, 2), (0, 1)])  10.5 us
    unnamed x44, local copies, waits for them, and re-layouts  8.84 us
    ppermute x2, waiting for transfers between devices, across_dp(): return lax.ppermute(value, 'dp', [(i, i ^ k) for i in range(owners)])  5.49 us
  transfers between devices with their start and end apart: 32, of which 13 were waited for; matrix products, arithmetic and copies ran while one was open for 0% of the time, Pallas kernels for 22%

profile of v6, /device:TPU:0, one launch (start us, length us, event | category | flops | bytes accessed | tf_op | source)
XLA Modules:
  0.0 165.3 jit_solution(7841081030185859122)
XLA Ops:
  10.0 4.9 %collective-permute-start.2 = (bf16[64,2048]{1,0:T(8,128)(2,1)S(1)}, bf16[64,2048]{1,0:T(8,128)(2,1)S(1)}, u32[]{:S(2)}, u32[]{:S(2)}) collective-permute-start(bf16[64,2048]{1,0:T(8,128)(2,1)S(1)} %get-tuple-element.35.refs_0_), channel_id=1, source_target_pairs={{12,8},{0,4},{13,9},{1,5},{14,10},{2,6},{15,11},{3,7},{28,24},{16,... | collective-permute-start | bytes 786440 | tf_op jit(solution)/shard_map/ppermute | solution.py:183
  21.7 5.1 %collective-permute-start.4 = (bf16[64,2048]{1,0:T(8,128)(2,1)S(1)}, bf16[64,2048]{1,0:T(8,128)(2,1)S(1)}, u32[]{:S(2)}, u32[]{:S(2)}) collective-permute-start(bf16[64,2048]{1,0:T(8,128)(2,1)S(1)} %get-tuple-element.40), channel_id=1, source_target_pairs={{4,0},{0,4},{12,8},{5,1},{1,5},{13,9},{6,2},{2,6},{14,10},{7,3},{3... | collective-permute-start | bytes 786440 | tf_op jit(solution)/shard_map/ppermute | solution.py:191
  29.0 2.4 %collective-permute-done.1.refs_0_ = f32[1,64,128]{2,1,0:T(8,128)S(1)} collective-permute-done((f32[1,64,128]{2,1,0:T(8,128)S(1)}, f32[1,64,128]{2,1,0:T(8,128)S(1)}, u32[]{:S(2)}, u32[]{:S(2)}) %collective-permute-start.1) | collective-permute-done | bytes 32800 | tf_op jit(solution)/shard_map/ppermute | solution.py:585
  34.2 5.6 %collective-permute-start.6 = (bf16[64,2048]{1,0:T(8,128)(2,1)S(1)}, bf16[64,2048]{1,0:T(8,128)(2,1)S(1)}, u32[]{:S(2)}, u32[]{:S(2)}) collective-permute-start(bf16[64,2048]{1,0:T(8,128)(2,1)S(1)} %get-tuple-element.42), channel_id=1, source_target_pairs={{12,8},{0,4},{13,9},{1,5},{14,10},{2,6},{15,11},{3,7},{28,24},{16,... | collective-permute-start | bytes 786440 | tf_op jit(solution)/shard_map/ppermute | solution.py:183
  40.5 4.2 %collective-permute-done.6.a_ref = bf16[64,2048]{1,0:T(8,128)(2,1)S(1)} collective-permute-done((bf16[64,2048]{1,0:T(8,128)(2,1)S(1)}, bf16[64,2048]{1,0:T(8,128)(2,1)S(1)}, u32[]{:S(2)}, u32[]{:S(2)}) %collective-permute-start.6) | collective-permute-done | bytes 262176 | tf_op jit(solution)/shard_map/ppermute | solution.py:183
  45.3 6.4 %collective-permute-start.14 = (bf16[64,2048]{1,0:T(8,128)(2,1)S(1)}, bf16[64,2048]{1,0:T(8,128)(2,1)S(1)}, u32[]{:S(2)}, u32[]{:S(2)}) collective-permute-start(bf16[64,2048]{1,0:T(8,128)(2,1)S(1)} %get-tuple-element.44.refs_1_), channel_id=1, source_target_pairs={{4,0},{0,4},{12,8},{5,1},{1,5},{13,9},{6,2},{2,6},{14,10},{7,3},{3... | collective-permute-start | bytes 786440 | tf_op jit(solution)/shard_map/ppermute | solution.py:191
  52.5 14.9 %collective-permute-done.14.x_ref = bf16[64,2048]{1,0:T(8,128)(2,1)S(1)} collective-permute-done((bf16[64,2048]{1,0:T(8,128)(2,1)S(1)}, bf16[64,2048]{1,0:T(8,128)(2,1)S(1)}, u32[]{:S(2)}, u32[]{:S(2)}) %collective-permute-start.14) | collective-permute-done | bytes 262176 | tf_op jit(solution)/shard_map/ppermute | solution.py:191
  70.7 2.3 %collective-permute-done.8 = f32[2,1,64,128]{3,2,1,0:T(8,128)S(1)} collective-permute-done((f32[2,1,64,128]{3,2,1,0:T(8,128)S(1)}, f32[2,1,64,128]{3,2,1,0:T(8,128)S(1)}, u32[]{:S(2)}, u32[]{:S(2)}) %collective-permute-start.8) | collective-permute-done | bytes 65568 | tf_op jit(solution)/shard_map/ppermute | solution.py:588
  75.1 3.2 %collective-permute-done.9.more_ref = f32[2,1,64,128]{3,2,1,0:T(8,128)S(1)} collective-permute-done((f32[2,1,64,128]{3,2,1,0:T(8,128)S(1)}, f32[2,1,64,128]{3,2,1,0:T(8,128)S(1)}, u32[]{:S(2)}, u32[]{:S(2)}) %collective-permute-start.9) | collective-permute-done | bytes 65568 | tf_op jit(solution)/shard_map/ppermute | solution.py:588
  79.9 3.9 %split_product.9 = (bf16[128,1024]{1,0:T(8,128)(2,1)S(1)}, f32[64,1024]{1,0:T(8,128)S(1)}, f32[64,1024]{1,0:T(8,128)S(1)}) custom-call(s32[14]{0:T(128)S(1)} %concatenate.3.index_ref.refs_0_, bf16[4,64,2048]{2,1,0:T(8,128)(2,1)} %bitcast.9, bf16[2048,4096]{1,0:T(8,128)(2,1)} %w_ref.11, bf16[1,64,128]{2,1,0:T(8,128)(2,1)S(1)} %get-tuple-element.45.refs_0_.refs_1_, ...), custom_call_target="tpu_custom_call" | custom-call | flops 1 | bytes 1 | tf_op jit(solution)/shard_map/split_product/pallas_call | solution.py:256
  83.9 3.9 %split_product.7 = (bf16[128,1024]{1,0:T(8,128)(2,1)S(1)}, f32[64,1024]{1,0:T(8,128)S(1)}, f32[64,1024]{1,0:T(8,128)S(1)}) custom-call(s32[14]{0:T(128)S(1)} %concatenate.3.index_ref.refs_0_, bf16[4,64,2048]{2,1,0:T(8,128)(2,1)} %bitcast.10, bf16[2048,4096]{1,0:T(8,128)(2,1)} %w_ref.11), custom_call_target="tpu_custom_call" | custom-call | flops 1 | bytes 1 | tf_op jit(solution)/shard_map/split_product/pallas_call | solution.py:256
  89.0 2.1 %collective-permute-start.22 = (bf16[1,64,4096]{2,1,0:T(8,128)(2,1)}, bf16[1,64,4096]{2,1,0:T(8,128)(2,1)S(1)}, u32[]{:S(2)}, u32[]{:S(2)}) collective-permute-start(bf16[1,64,4096]{2,1,0:T(8,128)(2,1)} %get-tuple-element.62.refs_0_), channel_id=1, source_target_pairs={{0,2},{1,3},{2,0},{3,1},{4,6},{5,7},{6,4},{7,5},{8,10},{9,11},{10,... | collective-permute-start | bytes 1572872 | tf_op jit(solution)/shard_map/ppermute | solution.py:585
  91.1 3.9 %split_product.10 = (bf16[128,1024]{1,0:T(8,128)(2,1)S(1)}, f32[64,1024]{1,0:T(8,128)S(1)}, f32[64,1024]{1,0:T(8,128)S(1)}) custom-call(s32[14]{0:T(128)S(1)} %concatenate.3.index_ref.refs_0_, bf16[4,64,2048]{2,1,0:T(8,128)(2,1)} %bitcast.11, bf16[2048,4096]{1,0:T(8,128)(2,1)} %w_ref.11), custom_call_target="tpu_custom_call" | custom-call | flops 1 | bytes 1 | tf_op jit(solution)/shard_map/split_product/pallas_call | solution.py:256
  95.7 3.9 %split_product.6 = (bf16[128,1024]{1,0:T(8,128)(2,1)S(1)}, f32[64,1024]{1,0:T(8,128)S(1)}, f32[64,1024]{1,0:T(8,128)S(1)}) custom-call(s32[14]{0:T(128)S(1)} %concatenate.3.index_ref.refs_0_, bf16[4,64,2048]{2,1,0:T(8,128)(2,1)} %bitcast.12, bf16[2048,4096]{1,0:T(8,128)(2,1)} %w_ref.11), custom_call_target="tpu_custom_call" | custom-call | flops 1 | bytes 1 | tf_op jit(solution)/shard_map/split_product/pallas_call | solution.py:256
  101.0 2.1 %collective-permute-start.13 = (bf16[64,1024]{1,0:T(8,128)(2,1)S(1)}, bf16[64,1024]{1,0:T(8,128)(2,1)S(1)}, u32[]{:S(2)}, u32[]{:S(2)}) collective-permute-start(bf16[64,1024]{1,0:T(8,128)(2,1)S(1)} %add_convert_fusion.4), channel_id=1, source_target_pairs={{0,2},{1,3},{2,0},{3,1},{4,6},{5,7},{6,4},{7,5},{8,10},{9,11},{10,... | collective-permute-start | bytes 393224 | tf_op jit(solution)/shard_map/ppermute | solution.py:585
  103.2 2.1 %collective-permute-start.11 = (bf16[64,1024]{1,0:T(8,128)(2,1)S(1)}, bf16[64,1024]{1,0:T(8,128)(2,1)S(1)}, u32[]{:S(2)}, u32[]{:S(2)}) collective-permute-start(bf16[64,1024]{1,0:T(8,128)(2,1)S(1)} %add_convert_fusion.5), channel_id=1, source_target_pairs={{0,2},{1,3},{2,0},{3,1},{4,6},{5,7},{6,4},{7,5},{8,10},{9,11},{10,... | collective-permute-start | bytes 393224 | tf_op jit(solution)/shard_map/ppermute | solution.py:585
  107.3 2.8 %collective-permute-done.13.refs_4_.refs_8_ = bf16[64,1024]{1,0:T(8,128)(2,1)S(1)} collective-permute-done((bf16[64,1024]{1,0:T(8,128)(2,1)S(1)}, bf16[64,1024]{1,0:T(8,128)(2,1)S(1)}, u32[]{:S(2)}, u32[]{:S(2)}) %collective-permute-start.13) | collective-permute-done | bytes 131104 | tf_op jit(solution)/shard_map/ppermute | solution.py:585
  110.1 2.8 %collective-permute-done.21.refs_2_.refs_8_ = bf16[64,1024]{1,0:T(8,128)(2,1)S(1)} collective-permute-done((bf16[64,1024]{1,0:T(8,128)(2,1)S(1)}, bf16[64,1024]{1,0:T(8,128)(2,1)S(1)}, u32[]{:S(2)}, u32[]{:S(2)}) %collective-permute-start.21) | collective-permute-done | bytes 131104 | tf_op jit(solution)/shard_map/ppermute | solution.py:585
  116.3 6.5 %split_product.11 = (bf16[128,2048]{1,0:T(8,128)(2,1)S(1)}, f32[64,2048]{1,0:T(8,128)S(1)}, f32[64,2048]{1,0:T(8,128)S(1)}) custom-call(s32[14]{0:T(128)S(1)} %concatenate.3.index_ref.refs_0_, bf16[4,64,2048]{2,1,0:T(8,128)(2,1)} %bitcast.13, bf16[2048,4096]{1,0:T(8,128)(2,1)} %w_ref.11, bf16[1,64,4096]{2,1,0:T(8,128)(2,1)S(1)} %collective-permute-done.22.refs_0_.refs_1_, ...), custom_call_target="tpu_custom_call" | custom-call | flops 1 | bytes 1 | tf_op jit(solution)/shard_map/split_product/pallas_call | solution.py:256
  122.9 6.5 %split_product.8 = (bf16[128,2048]{1,0:T(8,128)(2,1)S(1)}, f32[64,2048]{1,0:T(8,128)S(1)}, f32[64,2048]{1,0:T(8,128)S(1)}) custom-call(s32[14]{0:T(128)S(1)} %concatenate.3.index_ref.refs_0_, bf16[4,64,2048]{2,1,0:T(8,128)(2,1)} %bitcast.14, bf16[2048,4096]{1,0:T(8,128)(2,1)} %w_ref.11), custom_call_target="tpu_custom_call" | custom-call | flops 1 | bytes 1 | tf_op jit(solution)/shard_map/split_product/pallas_call | solution.py:256
  134.6 10.4 %collective-permute-done.27.refs_1_ = bf16[1,64,128]{2,1,0:T(8,128)(2,1)S(1)} collective-permute-done((bf16[1,64,128]{2,1,0:T(8,128)(2,1)S(1)}, bf16[1,64,128]{2,1,0:T(8,128)(2,1)S(1)}, u32[]{:S(2)}, u32[]{:S(2)}) %collective-permute-start.27) | collective-permute-done | bytes 16416 | tf_op jit(solution)/shard_map/ppermute | solution.py:585
  148.7 5.1 %up_gradient.1.refs_12_ = f32[4,64,4096]{2,1,0:T(8,128)} custom-call(s32[14]{0:T(128)S(1)} %concatenate.3.index_ref.refs_0_, bf16[1,64,4096]{2,1,0:T(8,128)(2,1)} %get-tuple-element.62.refs_0_, bf16[1,64,4096]{2,1,0:T(8,128)(2,1)S(1)} %collective-permute-done.22.refs_0_.refs_1_, bf16[1,64,4096]{2,1,0:T(8,128)(2,1)S(1)} %collective-permute-done.25.refs_2_, ...), custom_call_target="tpu_custom_call" | custom-call | flops 1 | bytes 1 | tf_op jit(solution)/shard_map/up_gradient/pallas_call | solution.py:452
  153.9 2.3 %finish.2.refs_12_ = bf16[128,4096]{1,0:T(8,128)(2,1)} custom-call(s32[14]{0:T(128)S(1)} %concatenate.3.index_ref.refs_0_, bf16[1,64,128]{2,1,0:T(8,128)(2,1)S(1)} %copy-done.19, bf16[4,64,4096]{2,1,0:T(8,128)(2,1)S(1)} %copy-done.3, f32[64,1024]{1,0:T(8,128)S(1)} %copy-done.15, bf16[128,1024]{1,0:T(8,128)(2,1)S(1)} %collective-permute-done.18.refs_4_, ...), custom_call_target="tpu_custom_call" | custom-call | flops 1 | bytes 1 | tf_op jit(solution)/shard_map/finish/pallas_call | solution.py:543
  156.2 2.3 %finish.3 = bf16[128,4096]{1,0:T(8,128)(2,1)} custom-call(s32[14]{0:T(128)S(1)} %concatenate.3.index_ref.refs_0_, bf16[1,64,128]{2,1,0:T(8,128)(2,1)S(1)} %copy-done.19, bf16[4,64,4096]{2,1,0:T(8,128)(2,1)S(1)} %copy-done.3, f32[64,1024]{1,0:T(8,128)S(1)} %copy-done.12, ...), custom_call_target="tpu_custom_call", output_to_operand_aliasing={{}: (12, {})} | custom-call | flops 1 | bytes 1 | tf_op jit(solution)/shard_map/finish/pallas_call | solution.py:543
  (114 shorter events, 41.2 us)
Async XLA Ops:
  7.2 72.8 %all-gather.5.cloned.1.call-start = ((), (), s32[]{:S(2)}) async-start(), calls=%async_computation | async-start | bytes 1310720 | tf_op jit(solution)/shard_map/all_gather | solution.py:636
  10.0 11.1 %collective-permute-start.2 = (bf16[64,2048]{1,0:T(8,128)(2,1)S(1)}, bf16[64,2048]{1,0:T(8,128)(2,1)S(1)}, u32[]{:S(2)}, u32[]{:S(2)}) collective-permute-start(bf16[64,2048]{1,0:T(8,128)(2,1)S(1)} %get-tuple-element.35.refs_0_), channel_id=1, source_target_pairs={{12,8},{0,4},{13,9},{1,5},{14,10},{2,6},{15,11},{3,7},{28,24},{16,... | collective-permute-start | bytes 786440 | tf_op jit(solution)/shard_map/ppermute | solution.py:183
  14.9 6.1 %collective-permute-start.3 = (bf16[64,2048]{1,0:T(8,128)(2,1)S(1)}, bf16[64,2048]{1,0:T(8,128)(2,1)S(1)}, u32[]{:S(2)}, u32[]{:S(2)}) collective-permute-start(bf16[64,2048]{1,0:T(8,128)(2,1)S(1)} %get-tuple-element.39), channel_id=1, source_target_pairs={{8,4},{9,5},{10,6},{11,7},{24,20},{25,21},{26,22},{27,23}} | collective-permute-start | bytes 786440 | tf_op jit(solution)/shard_map/ppermute | solution.py:184
  21.0 6.5 %collective-permute-start = (f32[2,1,64,128]{3,2,1,0:T(8,128)S(1)}, f32[2,1,64,128]{3,2,1,0:T(8,128)S(1)}, u32[]{:S(2)}, u32[]{:S(2)}) collective-permute-start(f32[2,1,64,128]{3,2,1,0:T(8,128)S(1)} %get-tuple-element.37.refs_0_), channel_id=1, source_target_pairs={{0,1},{1,0},{2,3},{3,2},{4,5},{5,4},{6,7},{7,6},{8,9},{9,8},{10,11... | collective-permute-start | bytes 196616 | tf_op jit(solution)/shard_map/ppermute | solution.py:582
  21.7 10.6 %collective-permute-start.4 = (bf16[64,2048]{1,0:T(8,128)(2,1)S(1)}, bf16[64,2048]{1,0:T(8,128)(2,1)S(1)}, u32[]{:S(2)}, u32[]{:S(2)}) collective-permute-start(bf16[64,2048]{1,0:T(8,128)(2,1)S(1)} %get-tuple-element.40), channel_id=1, source_target_pairs={{4,0},{0,4},{12,8},{5,1},{1,5},{13,9},{6,2},{2,6},{14,10},{7,3},{3... | collective-permute-start | bytes 786440 | tf_op jit(solution)/shard_map/ppermute | solution.py:191
  26.8 5.5 %collective-permute-start.5 = (bf16[64,2048]{1,0:T(8,128)(2,1)S(1)}, bf16[64,2048]{1,0:T(8,128)(2,1)S(1)}, u32[]{:S(2)}, u32[]{:S(2)}) collective-permute-start(bf16[64,2048]{1,0:T(8,128)(2,1)S(1)} %get-tuple-element.41), channel_id=1, source_target_pairs={{8,4},{4,8},{9,5},{5,9},{10,6},{6,10},{11,7},{7,11},{24,20},{20,24... | collective-permute-start | bytes 786440 | tf_op jit(solution)/shard_map/ppermute | solution.py:192
  33.6 81.8 %all-gather.7.cloned.1.call-start = ((), (), s32[]{:S(2)}) async-start(), calls=%async_computation.1 | async-start | bytes 1310720 | tf_op jit(solution)/shard_map/all_gather | solution.py:636
  34.2 10.5 %collective-permute-start.6 = (bf16[64,2048]{1,0:T(8,128)(2,1)S(1)}, bf16[64,2048]{1,0:T(8,128)(2,1)S(1)}, u32[]{:S(2)}, u32[]{:S(2)}) collective-permute-start(bf16[64,2048]{1,0:T(8,128)(2,1)S(1)} %get-tuple-element.42), channel_id=1, source_target_pairs={{12,8},{0,4},{13,9},{1,5},{14,10},{2,6},{15,11},{3,7},{28,24},{16,... | collective-permute-start | bytes 786440 | tf_op jit(solution)/shard_map/ppermute | solution.py:183
  45.3 22.0 %collective-permute-start.14 = (bf16[64,2048]{1,0:T(8,128)(2,1)S(1)}, bf16[64,2048]{1,0:T(8,128)(2,1)S(1)}, u32[]{:S(2)}, u32[]{:S(2)}) collective-permute-start(bf16[64,2048]{1,0:T(8,128)(2,1)S(1)} %get-tuple-element.44.refs_1_), channel_id=1, source_target_pairs={{4,0},{0,4},{12,8},{5,1},{1,5},{13,9},{6,2},{2,6},{14,10},{7,3},{3... | collective-permute-start | bytes 786440 | tf_op jit(solution)/shard_map/ppermute | solution.py:191
  51.8 15.6 %collective-permute-start.15 = (bf16[64,2048]{1,0:T(8,128)(2,1)S(1)}, bf16[64,2048]{1,0:T(8,128)(2,1)S(1)}, u32[]{:S(2)}, u32[]{:S(2)}) collective-permute-start(bf16[64,2048]{1,0:T(8,128)(2,1)S(1)} %get-tuple-element.52), channel_id=1, source_target_pairs={{8,4},{4,8},{9,5},{5,9},{10,6},{6,10},{11,7},{7,11},{24,20},{20,24... | collective-permute-start | bytes 786440 | tf_op jit(solution)/shard_map/ppermute | solution.py:192
  73.0 5.2 %collective-permute-start.9 = (f32[2,1,64,128]{3,2,1,0:T(8,128)S(1)}, f32[2,1,64,128]{3,2,1,0:T(8,128)S(1)}, u32[]{:S(2)}, u32[]{:S(2)}) collective-permute-start(f32[2,1,64,128]{3,2,1,0:T(8,128)S(1)} %add.37.sum_ref), channel_id=1, source_target_pairs={{0,8},{4,12},{8,0},{12,4},{1,9},{5,13},{9,1},{13,5},{2,10},{6,14},... | collective-permute-start | bytes 196616 | tf_op jit(solution)/shard_map/ppermute | solution.py:588
  83.8 17.0 %collective-permute-start.18 = (bf16[128,1024]{1,0:T(8,128)(2,1)S(1)}, bf16[128,1024]{1,0:T(8,128)(2,1)S(1)}, u32[]{:S(2)}, u32[]{:S(2)}) collective-permute-start(bf16[128,1024]{1,0:T(8,128)(2,1)S(1)} %get-tuple-element.57), channel_id=1, source_target_pairs={{0,1},{1,0},{2,3},{3,2},{4,5},{5,4},{6,7},{7,6},{8,9},{9,8},{10,11... | collective-permute-start | bytes 786440 | tf_op jit(solution)/shard_map/ppermute | solution.py:582
  88.5 12.4 %collective-permute-start.12 = (bf16[128,1024]{1,0:T(8,128)(2,1)S(1)}, bf16[128,1024]{1,0:T(8,128)(2,1)S(1)}, u32[]{:S(2)}, u32[]{:S(2)}) collective-permute-start(bf16[128,1024]{1,0:T(8,128)(2,1)S(1)} %get-tuple-element.50), channel_id=1, source_target_pairs={{0,1},{1,0},{2,3},{3,2},{4,5},{5,4},{6,7},{7,6},{8,9},{9,8},{10,11... | collective-permute-start | bytes 786440 | tf_op jit(solution)/shard_map/ppermute | solution.py:582
  89.0 16.3 %collective-permute-start.22 = (bf16[1,64,4096]{2,1,0:T(8,128)(2,1)}, bf16[1,64,4096]{2,1,0:T(8,128)(2,1)S(1)}, u32[]{:S(2)}, u32[]{:S(2)}) collective-permute-start(bf16[1,64,4096]{2,1,0:T(8,128)(2,1)} %get-tuple-element.62.refs_0_), channel_id=1, source_target_pairs={{0,2},{1,3},{2,0},{3,1},{4,6},{5,7},{6,4},{7,5},{8,10},{9,11},{10,... | collective-permute-start | bytes 1572872 | tf_op jit(solution)/shard_map/ppermute | solution.py:585
  100.9 6.4 %collective-permute-start.19 = (bf16[64,1024]{1,0:T(8,128)(2,1)S(1)}, bf16[64,1024]{1,0:T(8,128)(2,1)S(1)}, u32[]{:S(2)}, u32[]{:S(2)}) collective-permute-start(bf16[64,1024]{1,0:T(8,128)(2,1)S(1)} %add_convert_fusion.3), channel_id=1, source_target_pairs={{0,2},{1,3},{2,0},{3,1},{4,6},{5,7},{6,4},{7,5},{8,10},{9,11},{10,... | collective-permute-start | bytes 393224 | tf_op jit(solution)/shard_map/ppermute | solution.py:585
  101.0 9.1 %collective-permute-start.13 = (bf16[64,1024]{1,0:T(8,128)(2,1)S(1)}, bf16[64,1024]{1,0:T(8,128)(2,1)S(1)}, u32[]{:S(2)}, u32[]{:S(2)}) collective-permute-start(bf16[64,1024]{1,0:T(8,128)(2,1)S(1)} %add_convert_fusion.4), channel_id=1, source_target_pairs={{0,2},{1,3},{2,0},{3,1},{4,6},{5,7},{6,4},{7,5},{8,10},{9,11},{10,... | collective-permute-start | bytes 393224 | tf_op jit(solution)/shard_map/ppermute | solution.py:585
  103.1 9.8 %collective-permute-start.21 = (bf16[64,1024]{1,0:T(8,128)(2,1)S(1)}, bf16[64,1024]{1,0:T(8,128)(2,1)S(1)}, u32[]{:S(2)}, u32[]{:S(2)}) collective-permute-start(bf16[64,1024]{1,0:T(8,128)(2,1)S(1)} %add_convert_fusion.2), channel_id=1, source_target_pairs={{0,2},{1,3},{2,0},{3,1},{4,6},{5,7},{6,4},{7,5},{8,10},{9,11},{10,... | collective-permute-start | bytes 393224 | tf_op jit(solution)/shard_map/ppermute | solution.py:585
  103.2 11.5 %collective-permute-start.11 = (bf16[64,1024]{1,0:T(8,128)(2,1)S(1)}, bf16[64,1024]{1,0:T(8,128)(2,1)S(1)}, u32[]{:S(2)}, u32[]{:S(2)}) collective-permute-start(bf16[64,1024]{1,0:T(8,128)(2,1)S(1)} %add_convert_fusion.5), channel_id=1, source_target_pairs={{0,2},{1,3},{2,0},{3,1},{4,6},{5,7},{6,4},{7,5},{8,10},{9,11},{10,... | collective-permute-start | bytes 393224 | tf_op jit(solution)/shard_map/ppermute | solution.py:585
  122.9 7.7 %collective-permute-start.23 = (bf16[128,2048]{1,0:T(8,128)(2,1)S(1)}, bf16[128,2048]{1,0:T(8,128)(2,1)S(1)}, u32[]{:S(2)}, u32[]{:S(2)}) collective-permute-start(bf16[128,2048]{1,0:T(8,128)(2,1)S(1)} %get-tuple-element.64), channel_id=1, source_target_pairs={{0,1},{1,0},{2,3},{3,2},{4,5},{5,4},{6,7},{7,6},{8,9},{9,8},{10,11... | collective-permute-start | bytes 1572872 | tf_op jit(solution)/shard_map/ppermute | solution.py:582
  130.0 18.7 %collective-permute-start.25 = (bf16[1,64,4096]{2,1,0:T(8,128)(2,1)}, bf16[1,64,4096]{2,1,0:T(8,128)(2,1)S(1)}, u32[]{:S(2)}, u32[]{:S(2)}) collective-permute-start(bf16[1,64,4096]{2,1,0:T(8,128)(2,1)} %get-tuple-element.62.refs_0_), channel_id=1, source_target_pairs={{0,1},{1,0},{2,3},{3,2},{4,5},{5,4},{6,7},{7,6},{8,9},{9,8},{10,11... | collective-permute-start | bytes 1572872 | tf_op jit(solution)/shard_map/ppermute | solution.py:582
  130.1 18.6 %collective-permute-start.26 = (bf16[1,64,4096]{2,1,0:T(8,128)(2,1)S(1)}, bf16[1,64,4096]{2,1,0:T(8,128)(2,1)S(1)}, u32[]{:S(2)}, u32[]{:S(2)}) collective-permute-start(bf16[1,64,4096]{2,1,0:T(8,128)(2,1)S(1)} %collective-permute-done.22.refs_0_.refs_1_), channel_id=1, source_target_pairs={{0,1},{1,0},{2,3},{3,2},{4,5},{5,4},{6,7},{7,6},{8,9},{9,8},{10,11... | collective-permute-start | bytes 1572872 | tf_op jit(solution)/shard_map/ppermute | solution.py:582
  130.6 23.2 %collective-permute-start.24 = (bf16[64,2048]{1,0:T(8,128)(2,1)S(1)}, bf16[64,2048]{1,0:T(8,128)(2,1)S(1)}, u32[]{:S(2)}, u32[]{:S(2)}) collective-permute-start(bf16[64,2048]{1,0:T(8,128)(2,1)S(1)} %add_convert_fusion), channel_id=1, source_target_pairs={{0,2},{1,3},{2,0},{3,1},{4,6},{5,7},{6,4},{7,5},{8,10},{9,11},{10,... | collective-permute-start | bytes 786440 | tf_op jit(solution)/shard_map/ppermute | solution.py:585
  132.4 23.8 %collective-permute-start.17 = (bf16[64,2048]{1,0:T(8,128)(2,1)S(1)}, bf16[64,2048]{1,0:T(8,128)(2,1)S(1)}, u32[]{:S(2)}, u32[]{:S(2)}) collective-permute-start(bf16[64,2048]{1,0:T(8,128)(2,1)S(1)} %add_convert_fusion.1), channel_id=1, source_target_pairs={{0,2},{1,3},{2,0},{3,1},{4,6},{5,7},{6,4},{7,5},{8,10},{9,11},{10,... | collective-permute-start | bytes 786440 | tf_op jit(solution)/shard_map/ppermute | solution.py:585
  133.4 11.5 %collective-permute-start.27 = (bf16[1,64,128]{2,1,0:T(8,128)(2,1)S(1)}, bf16[1,64,128]{2,1,0:T(8,128)(2,1)S(1)}, u32[]{:S(2)}, u32[]{:S(2)}) collective-permute-start(bf16[1,64,128]{2,1,0:T(8,128)(2,1)S(1)} %copy-done.21), channel_id=1, source_target_pairs={{0,2},{1,3},{2,0},{3,1},{4,6},{5,7},{6,4},{7,5},{8,10},{9,11},{10,... | collective-permute-start | bytes 49160 | tf_op jit(solution)/shard_map/ppermute | solution.py:585
  (30 other events, 202.9 us)
Sparse Core Ops, SparseCore 0:
  33.7 34.8 all-gather.4
  70.8 28.1 all-gather.6

commit v7 on v6

--- a/solution.py
+++ b/solution.py
@@ -11,7 +11,7 @@
 CAP = 3
 CORES = 2
 CHUNK_ROWS = (64, 64)
-PARTS = (4, 2)
+PARTS = (2, 2)
 SMALL = pltpu.CompilerParams(vmem_limit_bytes=12 * 2**20)
 
 adapter_scale = 0.5
@@ -50,6 +50,11 @@
 
     def block(self, core_bit, chip_bits, i):
         return (self.part ^ (chip_bits * CORES + core_bit)) * self.per_part + i
+
+    def position(self, block):
+        bits = (block // self.per_part) ^ self.part
+        half = (1 - bits % CORES) * self.chips + bits // CORES
+        return half * self.per_part + block % self.per_part
 
     def live_rows(self, block):
         adapter = self.owner(block)
@@ -131,6 +136,30 @@
         out_ref[...] = y_ref[...]
 
 
+def collect_kernel(index_of, count, index_ref, home_ref, outer_ref, *refs):
+    inner_refs, outer_refs, out_ref = refs[:2], refs[2:4], refs[-1]
+    index = index_of(index_ref)
+    place = index.place
+
+    def put(block, ref):
+        at = pl.multiple_of(index.position(block) * count, 16)
+        out_ref[pl.ds(at, count)] = ref[...]
+
+    put(place, home_ref)
+    put(place ^ 1, outer_ref)
+    middle = (place == 1) | (place == 2)
+
+    @pl.when(middle)
+    def _():
+        put(3 - place, inner_refs[0])
+        put(place ^ 2, inner_refs[1])
+
+    @pl.when(jnp.logical_not(middle))
+    def _():
+        put(place ^ 2, outer_refs[0])
+        put(3 - place, outer_refs[1])
+
+
 def after(values, far=()):
     specs = [
         pl.BlockSpec((1,) * (v.ndim - 2) + (16, 128), lambda *_, n=v.ndim: (0,) * n) for v in values
@@ -139,7 +168,7 @@
 
 
 def hop_call(kernel, index, tokens, unit, count, stay, received, waits, name, declared):
-    specs, extra = after((), waits) if waits and waits[0].shape == unit.shape else after(waits)
+    specs, extra = after(waits)
     out = pltpu.VMEM(unit.shape, unit.dtype) if stay else unit
     return pl.pallas_call(
         kernel,
@@ -192,90 +221,98 @@
             lax.ppermute(middle, "dp", [(2, 1), (1, 2)]),
         )
 
-    def settle(self, waits=(), declared=BRIEF):
-        (self.sent,) = self.call(
-            settle_kernel, 1, False, self.received, waits, "settle", declared
-        )
-        return self.sent
-
-
-def split_product_kernel(index_of, first, index_ref, x_ref, w_ref, *refs):
-    send_ref, other_ref, own_ref, rows, tiles, rows_sems, tile_sems = refs[-7:]
-    index = index_of(index_ref)
-    count, tile = x_ref.shape[1], tiles.shape[2]
-    each = index.per_part * count
-    half = index.chips * each
-    buffers, steps = tiles.shape[0], own_ref.shape[1] // tile
-
-    def weight_copy(n):
-        return pltpu.make_async_copy(
-            w_ref.at[:, pl.ds(first + n * tile, tile)],
-            tiles.at[n % buffers],
-            tile_sems.at[n % buffers],
-        )
-
-    order = [
-        index.block(core_bit, chip_bits, i)
-        for core_bit in (1, 0)
-        for chip_bits in range(index.chips)
-        for i in range(index.per_part)
+    def settle(self, waits=()):
+        (home,) = self.call(settle_kernel, 1, True, self.received, waits, "settle")
+        self.sent = home
+        outer = lax.ppermute(home, "dp", [(0, 1), (1, 0), (2, 3), (3, 2)])
+        inner = lax.ppermute(home, "dp", [(1, 2), (2, 1)])
+        outer_2 = lax.ppermute(inner, "dp", [(1, 0), (2, 3)])
+        inner_2 = lax.ppermute(outer, "dp", [(1, 2), (2, 1)])
+        outer_3 = lax.ppermute(inner_2, "dp", [(1, 0), (2, 3)])
+        self.arrived = home, outer, inner, inner_2, outer_2, outer_3
+
+    def rows(self, waits=()):
+        count, width = self.unit.shape
+        specs, extra = after(waits)
+        return pl.pallas_call(
+            functools.partial(collect_kernel, self.index_of, count),
+            grid_spec=pltpu.PrefetchScalarGridSpec(
+                num_scalar_prefetch=1,
+                grid=(1,),
+                in_specs=[held()] * len(self.arrived) + specs,
+                out_specs=held(),
+            ),
+            out_shape=pltpu.VMEM((4 * count, width), self.unit.dtype),
+            compiler_params=SMALL,
+            cost_estimate=BRIEF,
+            name="collect",
+        )(self.index, *[in_vmem(a) for a in self.arrived], *extra)
+
+
+def load_weight_kernel(w_ref, *refs):
+    out_ref, sems = refs[-2:]
+    streams = sems.shape[0]
+    depth = w_ref.shape[0] // streams
+    copies = [
+        pltpu.make_async_copy(
+            w_ref.at[pl.ds(i * depth, depth)], out_ref.at[pl.ds(i * depth, depth)], sems.at[i]
+        )
+        for i in range(streams)
     ]
-    row_copies = [
-        pltpu.make_async_copy(
-            x_ref.at[block], rows.at[pl.ds(j * count, count)], rows_sems.at[j]
-        )
-        for j, block in enumerate(order)
-    ]
-    weight_copy(0).start()
-    for copy in row_copies:
+    for copy in copies:
         copy.start()
-    for n in range(1, min(buffers, steps)):
-        weight_copy(n).start()
-    for copy in row_copies:
+    for copy in copies:
         copy.wait()
-    for n in range(steps):
-        weight_copy(n).wait()
-        total = jnp.dot(rows[...], tiles[n % buffers], preferred_element_type=jnp.float32)
+
+
+def load_weight(weight, waits):
+    specs, extra = after(waits)
+    return pl.pallas_call(
+        load_weight_kernel,
+        grid=(1,),
+        in_specs=[pl.BlockSpec(memory_space=pl.ANY)] + specs,
+        out_specs=pl.BlockSpec(memory_space=pl.ANY),
+        out_shape=pltpu.VMEM(weight.shape, weight.dtype),
+        scratch_shapes=[pltpu.SemaphoreType.DMA((4,))],
+        compiler_params=SMALL,
+        cost_estimate=BRIEF,
+        name="load_weight",
+    )(in_hbm(weight), *extra)
+
+
+def split_product_kernel(each, half, first, tile, rows_ref, w_ref, *refs):
+    send_ref, other_ref, own_ref = refs[-3:]
+    for n in range(own_ref.shape[1] // tile):
+        total = jnp.dot(
+            rows_ref[...],
+            w_ref[:, first + n * tile : first + (n + 1) * tile],
+            preferred_element_type=jnp.float32,
+        )
         columns = slice(n * tile, (n + 1) * tile)
         send_ref[:, columns] = total[:half].astype(send_ref.dtype)
         own_ref[:, columns] = total[half : half + each]
         other_ref[:, columns] = total[half + each :]
-        if n + buffers < steps:
-            weight_copy(n + buffers).start()
-
-
-def split_product(index_of, index, shape, rows, weight, part, part_count, waits, far):
-    block_count, count, depth = rows.shape
+
+
+def split_product(shape, rows, weight, part, part_count, waits):
+    half = rows.shape[0] // 2
+    each = half // shape.chips
     width = weight.shape[1] // part_count
-    tile = min(512, width)
-    buffers = min(4, width // tile)
-    each = shape.per_part * count
-    half = block_count * count // 2
-    specs, extra = after(waits, far)
-    hbm = pl.BlockSpec(memory_space=pl.ANY)
-    return pl.pallas_call(
-        functools.partial(split_product_kernel, index_of, part * width),
-        grid_spec=pltpu.PrefetchScalarGridSpec(
-            num_scalar_prefetch=1,
-            grid=(1,),
-            in_specs=[hbm, hbm] + specs,
-            out_specs=[held()] * 3,
-            scratch_shapes=[
-                pltpu.VMEM((block_count * count, depth), rows.dtype),
-                pltpu.VMEM((buffers, depth, tile), weight.dtype),
-                pltpu.SemaphoreType.DMA((block_count,)),
-                pltpu.SemaphoreType.DMA((buffers,)),
-            ],
-        ),
+    specs, extra = after(waits)
+    return pl.pallas_call(
+        functools.partial(split_product_kernel, each, half, part * width, min(512, width)),
+        grid=(1,),
+        in_specs=[held(), held()] + specs,
+        out_specs=[held()] * 3,
         out_shape=[
             pltpu.VMEM((half, width), jnp.bfloat16),
             pltpu.VMEM((half - each, width), jnp.float32),
             pltpu.VMEM((each, width), jnp.float32),
         ],
-        compiler_params=pltpu.CompilerParams(vmem_limit_bytes=20 * 2**20),
+        compiler_params=SMALL,
         cost_estimate=BRIEF,
         name="split_product",
-    )(index, in_hbm(rows), in_hbm(weight), *extra)
+    )(in_vmem(rows), in_vmem(weight), *extra)
 
 
 def narrow_kernel(index_of, index_ref, tokens_ref, down_ref, cot_ref, up_ref, *refs):
@@ -617,56 +654,58 @@
         return make_pieces(index_of, index, shape, total, across_dp(total, k), cotangent)
 
     if owners == 4 and block_count == 4:
-        head = Homing(index_of, index, rows_here, 0)
-        tail = [Homing(index_of, index, rows_here, c) for c in range(1, len(CHUNK_ROWS))]
+        head, tail = [Homing(index_of, index, rows_here, c) for c in range(2)]
         head.first()
-        send, keep, back = small_products([head.sent])
+        tail.first([head.sent])
+        send, keep, back = small_products([tail.sent])
         head.second([send])
         arrived, others = over_parts(send, keep)
-        homes = [head.settle(others)]
-        tail[0].first([homes[-1]])
-        tail[0].second()
-        total = merge(keep, arrived, back, others, [tail[0].sent])
-        homes.append(tail[0].settle())
-        for homing in tail[1:]:
-            homing.first([homes[-1]])
-            homing.second()
-            homes.append(homing.settle())
+        tail.second([head.sent])
+        head.settle([tail.sent])
+        weight = load_weight(frozen_up_weight, [head.sent])
+        total = merge(keep, arrived, back, others, [])
+        tail.settle([total])
         lowered, back_rows, pieces = over_dp(total)
-        chunks = [lax.all_gather(home, "dp", axis=0) for home in homes]
+        chunks = [head.rows(), tail.rows()]
     else:
+        weight = load_weight(frozen_up_weight, [])
         send, keep, back = small_products([])
         arrived, others = over_parts(send, keep)
         lowered, back_rows, pieces = over_dp(merge(keep, arrived, back, others, []))
-        homes = []
         every_slot = lax.all_gather(
             tokens.reshape(CAP, BLK, width_dev), "dp", axis=0, tiled=True
         )
-        picked = every_slot[adapter_of_block * CAP + slot_of_block]
+        part = lax.axis_index("tensor")
+        devices = jnp.arange(parts, dtype=jnp.int32)
+        order = (devices // chips ^ 1) + (devices % chips) * CORES ^ part
+        blocks = (order[:, None] * shape.per_part + jnp.arange(shape.per_part)).reshape(-1)
+        picked = every_slot[adapter_of_block[blocks] * CAP + slot_of_block[blocks]]
         starts = [sum(CHUNK_ROWS[:c]) for c in range(len(CHUNK_ROWS))]
-        chunks = [picked[:, s : s + count] for s, count in zip(starts, CHUNK_ROWS)]
-
+        chunks = [
+            picked[:, s : s + count].reshape(-1, width_dev)
+            for s, count in zip(starts, CHUNK_ROWS)
+        ]
     pieces_same_core = [pieces] + [to_chip(pieces, k) for k in range(1, chips)]
 
-    def summed(rows, part, part_count, waits, far):
-        each = shape.per_part * rows.shape[1]
-        send, other, own = split_product(
-            index_of, index, shape, rows, frozen_up_weight, part, part_count, waits, far
-        )
+    def summed(rows, part, part_count, waits):
+        each = rows.shape[0] // parts
+        send, other, own = split_product(shape, rows, weight, part, part_count, waits)
         arrived = to_other_core(send)
         outgoing = (other + arrived[each:].astype(jnp.float32)).astype(jnp.bfloat16)
-        return [own, arrived] + [
-            to_chip(outgoing[(k - 1) * each : k * each], k) for k in range(1, chips)
-        ]
-
-    waits, far = [lowered], homes[1:]
+        across = [to_chip(outgoing[(k - 1) * each : k * each], k) for k in range(1, chips)]
+        return [own, arrived] + across, outgoing
+
+    waits = [lowered]
     sums = []
     for rows, part_count in zip(chunks, PARTS):
         sums.append([])
+        sent = []
         for part in range(part_count):
-            sums[-1].append(summed(rows, part, part_count, waits, far))
-            waits, far = [], []
-        waits = pieces_same_core[1:] + [v for part in sums[-1] for v in part[2:]]
+            terms, outgoing = summed(rows, part, part_count, waits)
+            sums[-1].append(terms)
+            sent.append(outgoing)
+            waits = []
+        waits = sent
     pieces_all = pieces_same_core + [to_other_core(p) for p in pieces_same_core]
     up_grad = up_gradient(index_of, index, adapter_count, pieces_all)
     down_grad = down_gradient(index_of, index, rows_here, every_part(back_rows))

time: 166 us -> 138 us (0.83)
  Pallas kernels: 47.8 us -> 31.5 us
  between operations: 14.5 us -> 1.11 us
  local copies, waits for them, and re-layouts: 9.6 us -> 4.36 us
  starting transfers between devices: 43.2 us -> 48.3 us
  waiting for transfers between devices: 50 us -> 51.7 us
    ppermute x0 -> x10, starting transfers between devices: none -> 15.6 us  [the longest x2 7.8 us: settle(): outer = lax.ppermute(home, 'dp', [(0, 1), (1, 0), (2, 3), (3, 2)])]
    ppermute x2, waiting for transfers between devices: 15.7 us -> 3.65 us  [second(): lax.ppermute(outer, 'dp', [(1, 0), (0, 1), (3, 2)])]
    pallas_call x6 -> x7, Pallas kernels: 28.6 us -> 16.7 us  [the longest x4 9.55 us: split_product(): pl.pallas_call(functools.partial(split_product_kernel, each, half, part *...]
    ppermute x2, waiting for transfers between devices: 5.49 us -> 16.8 us  [across_dp(): return lax.ppermute(value, 'dp', [(i, i ^ k) for i in range(owners)])]
    ppermute x0 -> x10, waiting for transfers between devices: none -> 6.32 us  [the longest x2 5.83 us: settle(): outer = lax.ppermute(home, 'dp', [(0, 1), (1, 0), (2, 3), (3, 2)])]
    unnamed x44 -> x12, local copies, waits for them, and re-layouts: 8.84 us -> 3.59 us
    ppermute x2, waiting for transfers between devices: 4.25 us -> 0.01 us  [first(): lax.ppermute(inward, 'dp', [(3, 2), (0, 1)])]
    ppermute x9 -> x7, starting transfers between devices: 11.9 us -> 7.77 us  [to_chip(): lax.ppermute(value, 'tensor', [(i, i ^ k * CORES) for i in range(parts)])]
  transfers between devices with their start and end apart: 32 -> 36, of which waited for: 13 -> 13; matrix products, arithmetic and copies ran while one was open for 0% -> 0% of each run, Pallas kernels for 22% -> 21%
where the time goes in v7:
time: 138 us; the launch traced here: 137 us
  waiting for transfers between devices  51.7 us (37%)
  starting transfers between devices  48.3 us (35%)
  Pallas kernels  31.5 us (23%)
  local copies, waits for them, and re-layouts  4.36 us (3%)
    ppermute x7, waiting for transfers between devices, to_chip(): lax.ppermute(value, 'tensor', [(i, i ^ k * CORES) for i in range(parts)])  23.2 us
    ppermute x2, waiting for transfers between devices, across_dp(): return lax.ppermute(value, 'dp', [(i, i ^ k) for i in range(owners)])  16.8 us
    ppermute x2, starting transfers between devices, second(): lax.ppermute(outer, 'dp', [(1, 0), (0, 1), (3, 2)])  10.2 us
    pallas_call x4, Pallas kernels, split_product(): pl.pallas_call(functools.partial(split_product_kernel, each, half, part *...  9.55 us
    ppermute x2, starting transfers between devices, settle(): outer = lax.ppermute(home, 'dp', [(0, 1), (1, 0), (2, 3), (3, 2)])  7.8 us
    ppermute x7, starting transfers between devices, to_chip(): lax.ppermute(value, 'tensor', [(i, i ^ k * CORES) for i in range(parts)])  7.77 us
    ppermute x2, starting transfers between devices, first(): lax.ppermute(inward, 'dp', [(3, 2), (0, 1)])  6.98 us
    pallas_call x1, Pallas kernels, load_weight(): pl.pallas_call(load_weight_kernel, grid=(1,), in_specs=[pl.BlockSpec(memo...  5.89 us
  transfers between devices with their start and end apart: 36, of which 13 were waited for; matrix products, arithmetic and copies ran while one was open for 0% of the time, Pallas kernels for 21%

profile of v7, /device:TPU:0, one launch (start us, length us, event | category | flops | bytes accessed | tf_op | source)
XLA Modules:
  0.0 137.3 jit_solution(16446935591951587664)
XLA Ops:
  3.4 5.1 %collective-permute-start.4 = (bf16[64,2048]{1,0:T(8,128)(2,1)S(1)}, bf16[64,2048]{1,0:T(8,128)(2,1)S(1)}, u32[]{:S(2)}, u32[]{:S(2)}) collective-permute-start(bf16[64,2048]{1,0:T(8,128)(2,1)S(1)} %get-tuple-element.29.refs_0_), channel_id=1, source_target_pairs={{12,8},{0,4},{13,9},{1,5},{14,10},{2,6},{15,11},{3,7},{28,24},{16,... | collective-permute-start | bytes 786440 | tf_op jit(solution)/shard_map/ppermute | solution.py:212
  9.8 1.9 %collective-permute-start.8 = (bf16[64,2048]{1,0:T(8,128)(2,1)S(1)}, bf16[64,2048]{1,0:T(8,128)(2,1)S(1)}, u32[]{:S(2)}, u32[]{:S(2)}) collective-permute-start(bf16[64,2048]{1,0:T(8,128)(2,1)S(1)} %get-tuple-element.30.refs_0_), channel_id=1, source_target_pairs={{12,8},{0,4},{13,9},{1,5},{14,10},{2,6},{15,11},{3,7},{28,24},{16,... | collective-permute-start | bytes 786440 | tf_op jit(solution)/shard_map/ppermute | solution.py:212
  16.8 4.7 %collective-permute-start.6 = (bf16[64,2048]{1,0:T(8,128)(2,1)S(1)}, bf16[64,2048]{1,0:T(8,128)(2,1)S(1)}, u32[]{:S(2)}, u32[]{:S(2)}) collective-permute-start(bf16[64,2048]{1,0:T(8,128)(2,1)S(1)} %get-tuple-element.36.refs_0_), channel_id=1, source_target_pairs={{4,0},{0,4},{12,8},{5,1},{1,5},{13,9},{6,2},{2,6},{14,10},{7,3},{3... | collective-permute-start | bytes 786440 | tf_op jit(solution)/shard_map/ppermute | solution.py:220
  22.8 3.6 %collective-permute-done.6.x_ref = bf16[64,2048]{1,0:T(8,128)(2,1)S(1)} collective-permute-done((bf16[64,2048]{1,0:T(8,128)(2,1)S(1)}, bf16[64,2048]{1,0:T(8,128)(2,1)S(1)}, u32[]{:S(2)}, u32[]{:S(2)}) %collective-permute-start.6) | collective-permute-done | bytes 262176 | tf_op jit(solution)/shard_map/ppermute | solution.py:220
  27.0 3.7 %collective-permute-start.10 = (bf16[64,2048]{1,0:T(8,128)(2,1)S(1)}, bf16[64,2048]{1,0:T(8,128)(2,1)S(1)}, u32[]{:S(2)}, u32[]{:S(2)}) collective-permute-start(bf16[64,2048]{1,0:T(8,128)(2,1)S(1)} %settle.2.home_ref.refs_0_), channel_id=1, source_target_pairs={{0,4},{4,0},{8,12},{12,8},{1,5},{5,1},{9,13},{13,9},{2,6},{6,2},{1... | collective-permute-start | bytes 786440 | tf_op jit(solution)/shard_map/ppermute | solution.py:227
  31.4 3.7 %collective-permute-done.10.outer_ref = bf16[64,2048]{1,0:T(8,128)(2,1)S(1)} collective-permute-done((bf16[64,2048]{1,0:T(8,128)(2,1)S(1)}, bf16[64,2048]{1,0:T(8,128)(2,1)S(1)}, u32[]{:S(2)}, u32[]{:S(2)}) %collective-permute-start.10) | collective-permute-done | bytes 262176 | tf_op jit(solution)/shard_map/ppermute | solution.py:227
  35.8 5.5 %collective-permute-start.17 = (bf16[64,2048]{1,0:T(8,128)(2,1)S(1)}, bf16[64,2048]{1,0:T(8,128)(2,1)S(1)}, u32[]{:S(2)}, u32[]{:S(2)}) collective-permute-start(bf16[64,2048]{1,0:T(8,128)(2,1)S(1)} %get-tuple-element.39.refs_0_), channel_id=1, source_target_pairs={{4,0},{0,4},{12,8},{5,1},{1,5},{13,9},{6,2},{2,6},{14,10},{7,3},{3... | collective-permute-start | bytes 786440 | tf_op jit(solution)/shard_map/ppermute | solution.py:220
  43.5 2.4 %collective-permute-done.1.refs_0_ = f32[1,64,128]{2,1,0:T(8,128)S(1)} collective-permute-done((f32[1,64,128]{2,1,0:T(8,128)S(1)}, f32[1,64,128]{2,1,0:T(8,128)S(1)}, u32[]{:S(2)}, u32[]{:S(2)}) %collective-permute-start.1) | collective-permute-done | bytes 32800 | tf_op jit(solution)/shard_map/ppermute | solution.py:622
  49.2 4.1 %collective-permute-start.19 = (bf16[64,2048]{1,0:T(8,128)(2,1)S(1)}, bf16[64,2048]{1,0:T(8,128)(2,1)S(1)}, u32[]{:S(2)}, u32[]{:S(2)}) collective-permute-start(bf16[64,2048]{1,0:T(8,128)(2,1)S(1)} %settle.3.home_ref), channel_id=1, source_target_pairs={{0,4},{4,0},{8,12},{12,8},{1,5},{5,1},{9,13},{13,9},{2,6},{6,2},{1... | collective-permute-start | bytes 786440 | tf_op jit(solution)/shard_map/ppermute | solution.py:227
  54.0 5.9 %load_weight.1.w_ref = bf16[2048,4096]{1,0:T(8,128)(2,1)S(1)} custom-call(bf16[2048,4096]{1,0:T(8,128)(2,1)} %w_ref.1, bf16[64,2048]{1,0:T(8,128)(2,1)S(1)} %settle.2.home_ref.refs_0_), custom_call_target="tpu_custom_call" | custom-call | flops 1 | bytes 1 | tf_op jit(solution)/shard_map/load_weight/pallas_call | solution.py:270
  61.0 2.2 %collective-permute-done.19.outer_ref = bf16[64,2048]{1,0:T(8,128)(2,1)S(1)} collective-permute-done((bf16[64,2048]{1,0:T(8,128)(2,1)S(1)}, bf16[64,2048]{1,0:T(8,128)(2,1)S(1)}, u32[]{:S(2)}, u32[]{:S(2)}) %collective-permute-start.19) | collective-permute-done | bytes 262176 | tf_op jit(solution)/shard_map/ppermute | solution.py:227
  63.8 2.4 %split_product.4 = (bf16[128,2048]{1,0:T(8,128)(2,1)S(1)}, f32[64,2048]{1,0:T(8,128)S(1)}, f32[64,2048]{1,0:T(8,128)S(1)}) custom-call(bf16[256,2048]{1,0:T(8,128)(2,1)S(1)} %collect.2.rows_ref, bf16[2048,4096]{1,0:T(8,128)(2,1)S(1)} %load_weight.1.w_ref), custom_call_target="tpu_custom_call" | custom-call | flops 1 | bytes 1 | tf_op jit(solution)/shard_map/split_product/pallas_call | solution.py:302
  68.9 3.5 %collective-permute-start.2 = (f32[2,1,64,128]{3,2,1,0:T(8,128)S(1)}, f32[2,1,64,128]{3,2,1,0:T(8,128)S(1)}, u32[]{:S(2)}, u32[]{:S(2)}) collective-permute-start(f32[2,1,64,128]{3,2,1,0:T(8,128)S(1)} %merge.1.refs_0_), channel_id=1, source_target_pairs={{0,4},{4,0},{8,12},{12,8},{1,5},{5,1},{9,13},{13,9},{2,6},{6,2},{1... | collective-permute-start | bytes 196616 | tf_op jit(solution)/shard_map/ppermute | solution.py:625
  72.4 11.5 %collective-permute-done.2 = f32[2,1,64,128]{3,2,1,0:T(8,128)S(1)} collective-permute-done((f32[2,1,64,128]{3,2,1,0:T(8,128)S(1)}, f32[2,1,64,128]{3,2,1,0:T(8,128)S(1)}, u32[]{:S(2)}, u32[]{:S(2)}) %collective-permute-start.2) | collective-permute-done | bytes 65568 | tf_op jit(solution)/shard_map/ppermute | solution.py:625
  84.2 5.3 %collective-permute-done.3.more_ref = f32[2,1,64,128]{3,2,1,0:T(8,128)S(1)} collective-permute-done((f32[2,1,64,128]{3,2,1,0:T(8,128)S(1)}, f32[2,1,64,128]{3,2,1,0:T(8,128)S(1)}, u32[]{:S(2)}, u32[]{:S(2)}) %collective-permute-start.3) | collective-permute-done | bytes 65568 | tf_op jit(solution)/shard_map/ppermute | solution.py:625
  90.3 2.4 %split_product.6 = (bf16[128,2048]{1,0:T(8,128)(2,1)S(1)}, f32[64,2048]{1,0:T(8,128)S(1)}, f32[64,2048]{1,0:T(8,128)S(1)}) custom-call(bf16[256,2048]{1,0:T(8,128)(2,1)S(1)} %collect.2.rows_ref, bf16[2048,4096]{1,0:T(8,128)(2,1)S(1)} %load_weight.1.w_ref, bf16[1,64,128]{2,1,0:T(8,128)(2,1)S(1)} %get-tuple-element.34.refs_0_.refs_1_), custom_call_target="tpu_custom_call" | custom-call | flops 1 | bytes 1 | tf_op jit(solution)/shard_map/split_product/pallas_call | solution.py:302
  96.3 2.4 %split_product.7 = (bf16[128,2048]{1,0:T(8,128)(2,1)S(1)}, f32[64,2048]{1,0:T(8,128)S(1)}, f32[64,2048]{1,0:T(8,128)S(1)}) custom-call(bf16[256,2048]{1,0:T(8,128)(2,1)S(1)} %collect.3.rows_ref, bf16[2048,4096]{1,0:T(8,128)(2,1)S(1)} %load_weight.1.w_ref, bf16[64,2048]{1,0:T(8,128)(2,1)S(1)} %add_convert_fusion.1.refs_0_, ...), custom_call_target="tpu_custom_call" | custom-call | flops 1 | bytes 1 | tf_op jit(solution)/shard_map/split_product/pallas_call | solution.py:302
  98.8 2.4 %split_product.5 = (bf16[128,2048]{1,0:T(8,128)(2,1)S(1)}, f32[64,2048]{1,0:T(8,128)S(1)}, f32[64,2048]{1,0:T(8,128)S(1)}) custom-call(bf16[256,2048]{1,0:T(8,128)(2,1)S(1)} %collect.3.rows_ref, bf16[2048,4096]{1,0:T(8,128)(2,1)S(1)} %load_weight.1.w_ref), custom_call_target="tpu_custom_call" | custom-call | flops 1 | bytes 1 | tf_op jit(solution)/shard_map/split_product/pallas_call | solution.py:302
  102.3 6.9 %collective-permute-done.33.refs_1_ = bf16[1,64,128]{2,1,0:T(8,128)(2,1)S(1)} collective-permute-done((bf16[1,64,128]{2,1,0:T(8,128)(2,1)S(1)}, bf16[1,64,128]{2,1,0:T(8,128)(2,1)S(1)}, u32[]{:S(2)}, u32[]{:S(2)}) %collective-permute-start.33) | collective-permute-done | bytes 16416 | tf_op jit(solution)/shard_map/ppermute | solution.py:622
  115.9 3.9 %up_gradient.1.refs_9_ = f32[4,64,4096]{2,1,0:T(8,128)} custom-call(s32[14]{0:T(128)S(1)} %concatenate.3.index_ref.refs_0_, bf16[1,64,4096]{2,1,0:T(8,128)(2,1)S(1)} %get-tuple-element.53.refs_0_, bf16[1,64,4096]{2,1,0:T(8,128)(2,1)S(1)} %collective-permute-done.30.refs_1_, bf16[1,64,4096]{2,1,0:T(8,128)(2,1)S(1)} %collective-permute-done.31.refs_2_, ...), custom_call_target="tpu_custom_call" | custom-call | flops 1 | bytes 1 | tf_op jit(solution)/shard_map/up_gradient/pallas_call | solution.py:489
  119.8 5.3 %collective-permute-done.29.refs_8_ = bf16[64,2048]{1,0:T(8,128)(2,1)S(1)} collective-permute-done((bf16[64,2048]{1,0:T(8,128)(2,1)S(1)}, bf16[64,2048]{1,0:T(8,128)(2,1)S(1)}, u32[]{:S(2)}, u32[]{:S(2)}) %collective-permute-start.29) | collective-permute-done | bytes 262176 | tf_op jit(solution)/shard_map/ppermute | solution.py:622
  125.1 1.8 %finish.2.refs_9_ = bf16[128,4096]{1,0:T(8,128)(2,1)} custom-call(s32[14]{0:T(128)S(1)} %concatenate.3.index_ref.refs_0_, bf16[1,64,128]{2,1,0:T(8,128)(2,1)S(1)} %get-tuple-element.34.refs_0_.refs_1_, bf16[4,64,4096]{2,1,0:T(8,128)(2,1)S(1)} %copy-done.2, f32[64,2048]{1,0:T(8,128)S(1)} %get-tuple-element.47.refs_3_, ...), custom_call_target="tpu_custom_call" | custom-call | flops 1 | bytes 1 | tf_op jit(solution)/shard_map/finish/pallas_call | solution.py:580
  126.9 3.8 %collective-permute-done.16.refs_5_ = bf16[64,2048]{1,0:T(8,128)(2,1)S(1)} collective-permute-done((bf16[64,2048]{1,0:T(8,128)(2,1)S(1)}, bf16[64,2048]{1,0:T(8,128)(2,1)S(1)}, u32[]{:S(2)}, u32[]{:S(2)}) %collective-permute-start.16) | collective-permute-done | bytes 262176 | tf_op jit(solution)/shard_map/ppermute | solution.py:622
  130.7 4.8 %collective-permute-done.25.refs_8_ = bf16[64,2048]{1,0:T(8,128)(2,1)S(1)} collective-permute-done((bf16[64,2048]{1,0:T(8,128)(2,1)S(1)}, bf16[64,2048]{1,0:T(8,128)(2,1)S(1)}, u32[]{:S(2)}, u32[]{:S(2)}) %collective-permute-start.25) | collective-permute-done | bytes 262176 | tf_op jit(solution)/shard_map/ppermute | solution.py:622
  (87 shorter events, 37.2 us)
Async XLA Ops:
  3.4 12.7 %collective-permute-start.4 = (bf16[64,2048]{1,0:T(8,128)(2,1)S(1)}, bf16[64,2048]{1,0:T(8,128)(2,1)S(1)}, u32[]{:S(2)}, u32[]{:S(2)}) collective-permute-start(bf16[64,2048]{1,0:T(8,128)(2,1)S(1)} %get-tuple-element.29.refs_0_), channel_id=1, source_target_pairs={{12,8},{0,4},{13,9},{1,5},{14,10},{2,6},{15,11},{3,7},{28,24},{16,... | collective-permute-start | bytes 786440 | tf_op jit(solution)/shard_map/ppermute | solution.py:212
  9.8 12.4 %collective-permute-start.8 = (bf16[64,2048]{1,0:T(8,128)(2,1)S(1)}, bf16[64,2048]{1,0:T(8,128)(2,1)S(1)}, u32[]{:S(2)}, u32[]{:S(2)}) collective-permute-start(bf16[64,2048]{1,0:T(8,128)(2,1)S(1)} %get-tuple-element.30.refs_0_), channel_id=1, source_target_pairs={{12,8},{0,4},{13,9},{1,5},{14,10},{2,6},{15,11},{3,7},{28,24},{16,... | collective-permute-start | bytes 786440 | tf_op jit(solution)/shard_map/ppermute | solution.py:212
  11.7 10.5 %collective-permute-start.9 = (bf16[64,2048]{1,0:T(8,128)(2,1)S(1)}, bf16[64,2048]{1,0:T(8,128)(2,1)S(1)}, u32[]{:S(2)}, u32[]{:S(2)}) collective-permute-start(bf16[64,2048]{1,0:T(8,128)(2,1)S(1)} %get-tuple-element.38), channel_id=1, source_target_pairs={{8,4},{9,5},{10,6},{11,7},{24,20},{25,21},{26,22},{27,23}} | collective-permute-start | bytes 786440 | tf_op jit(solution)/shard_map/ppermute | solution.py:213
  16.8 9.7 %collective-permute-start.6 = (bf16[64,2048]{1,0:T(8,128)(2,1)S(1)}, bf16[64,2048]{1,0:T(8,128)(2,1)S(1)}, u32[]{:S(2)}, u32[]{:S(2)}) collective-permute-start(bf16[64,2048]{1,0:T(8,128)(2,1)S(1)} %get-tuple-element.36.refs_0_), channel_id=1, source_target_pairs={{4,0},{0,4},{12,8},{5,1},{1,5},{13,9},{6,2},{2,6},{14,10},{7,3},{3... | collective-permute-start | bytes 786440 | tf_op jit(solution)/shard_map/ppermute | solution.py:220
  30.7 11.2 %collective-permute-start = (f32[2,1,64,128]{3,2,1,0:T(8,128)S(1)}, f32[2,1,64,128]{3,2,1,0:T(8,128)S(1)}, u32[]{:S(2)}, u32[]{:S(2)}) collective-permute-start(f32[2,1,64,128]{3,2,1,0:T(8,128)S(1)} %get-tuple-element.32.refs_0_), channel_id=1, source_target_pairs={{0,1},{1,0},{2,3},{3,2},{4,5},{5,4},{6,7},{7,6},{8,9},{9,8},{10,11... | collective-permute-start | bytes 196616 | tf_op jit(solution)/shard_map/ppermute | solution.py:619
  30.7 15.2 %collective-permute-start.11 = (bf16[64,2048]{1,0:T(8,128)(2,1)S(1)}, bf16[64,2048]{1,0:T(8,128)(2,1)S(1)}, u32[]{:S(2)}, u32[]{:S(2)}) collective-permute-start(bf16[64,2048]{1,0:T(8,128)(2,1)S(1)} %settle.2.home_ref.refs_0_), channel_id=1, source_target_pairs={{4,8},{8,4},{5,9},{9,5},{6,10},{10,6},{7,11},{11,7},{20,24},{24,20... | collective-permute-start | bytes 786440 | tf_op jit(solution)/shard_map/ppermute | solution.py:228
  35.1 12.2 %collective-permute-start.12 = (bf16[64,2048]{1,0:T(8,128)(2,1)S(1)}, bf16[64,2048]{1,0:T(8,128)(2,1)S(1)}, u32[]{:S(2)}, u32[]{:S(2)}) collective-permute-start(bf16[64,2048]{1,0:T(8,128)(2,1)S(1)} %collective-permute-done.10.outer_ref), channel_id=1, source_target_pairs={{4,8},{8,4},{5,9},{9,5},{6,10},{10,6},{7,11},{11,7},{20,24},{24,20... | collective-permute-start | bytes 786440 | tf_op jit(solution)/shard_map/ppermute | solution.py:230
  35.8 12.8 %collective-permute-start.17 = (bf16[64,2048]{1,0:T(8,128)(2,1)S(1)}, bf16[64,2048]{1,0:T(8,128)(2,1)S(1)}, u32[]{:S(2)}, u32[]{:S(2)}) collective-permute-start(bf16[64,2048]{1,0:T(8,128)(2,1)S(1)} %get-tuple-element.39.refs_0_), channel_id=1, source_target_pairs={{4,0},{0,4},{12,8},{5,1},{1,5},{13,9},{6,2},{2,6},{14,10},{7,3},{3... | collective-permute-start | bytes 786440 | tf_op jit(solution)/shard_map/ppermute | solution.py:220
  46.0 13.9 %collective-permute-start.13 = (bf16[64,2048]{1,0:T(8,128)(2,1)S(1)}, bf16[64,2048]{1,0:T(8,128)(2,1)S(1)}, u32[]{:S(2)}, u32[]{:S(2)}) collective-permute-start(bf16[64,2048]{1,0:T(8,128)(2,1)S(1)} %collective-permute-done.11.refs_0_), channel_id=1, source_target_pairs={{4,0},{8,12},{5,1},{9,13},{6,2},{10,14},{7,3},{11,15},{20,16},{24,... | collective-permute-start | bytes 786440 | tf_op jit(solution)/shard_map/ppermute | solution.py:229
  47.3 13.1 %collective-permute-start.14 = (bf16[64,2048]{1,0:T(8,128)(2,1)S(1)}, bf16[64,2048]{1,0:T(8,128)(2,1)S(1)}, u32[]{:S(2)}, u32[]{:S(2)}) collective-permute-start(bf16[64,2048]{1,0:T(8,128)(2,1)S(1)} %collective-permute-done.12.refs_1_), channel_id=1, source_target_pairs={{4,0},{8,12},{5,1},{9,13},{6,2},{10,14},{7,3},{11,15},{20,16},{24,... | collective-permute-start | bytes 786440 | tf_op jit(solution)/shard_map/ppermute | solution.py:231
  49.2 14.0 %collective-permute-start.19 = (bf16[64,2048]{1,0:T(8,128)(2,1)S(1)}, bf16[64,2048]{1,0:T(8,128)(2,1)S(1)}, u32[]{:S(2)}, u32[]{:S(2)}) collective-permute-start(bf16[64,2048]{1,0:T(8,128)(2,1)S(1)} %settle.3.home_ref), channel_id=1, source_target_pairs={{0,4},{4,0},{8,12},{12,8},{1,5},{5,1},{9,13},{13,9},{2,6},{6,2},{1... | collective-permute-start | bytes 786440 | tf_op jit(solution)/shard_map/ppermute | solution.py:227
  53.3 13.0 %collective-permute-start.20 = (bf16[64,2048]{1,0:T(8,128)(2,1)S(1)}, bf16[64,2048]{1,0:T(8,128)(2,1)S(1)}, u32[]{:S(2)}, u32[]{:S(2)}) collective-permute-start(bf16[64,2048]{1,0:T(8,128)(2,1)S(1)} %settle.3.home_ref), channel_id=1, source_target_pairs={{4,8},{8,4},{5,9},{9,5},{6,10},{10,6},{7,11},{11,7},{20,24},{24,20... | collective-permute-start | bytes 786440 | tf_op jit(solution)/shard_map/ppermute | solution.py:228
  66.2 27.2 %collective-permute-start.15 = (bf16[128,2048]{1,0:T(8,128)(2,1)S(1)}, bf16[128,2048]{1,0:T(8,128)(2,1)S(1)}, u32[]{:S(2)}, u32[]{:S(2)}) collective-permute-start(bf16[128,2048]{1,0:T(8,128)(2,1)S(1)} %get-tuple-element.41), channel_id=1, source_target_pairs={{0,1},{1,0},{2,3},{3,2},{4,5},{5,4},{6,7},{7,6},{8,9},{9,8},{10,11... | collective-permute-start | bytes 1572872 | tf_op jit(solution)/shard_map/ppermute | solution.py:619
  66.3 26.5 %collective-permute-start.22 = (bf16[64,2048]{1,0:T(8,128)(2,1)S(1)}, bf16[64,2048]{1,0:T(8,128)(2,1)S(1)}, u32[]{:S(2)}, u32[]{:S(2)}) collective-permute-start(bf16[64,2048]{1,0:T(8,128)(2,1)S(1)} %collective-permute-done.20.refs_0_), channel_id=1, source_target_pairs={{4,0},{8,12},{5,1},{9,13},{6,2},{10,14},{7,3},{11,15},{20,16},{24,... | collective-permute-start | bytes 786440 | tf_op jit(solution)/shard_map/ppermute | solution.py:229
  67.6 25.2 %collective-permute-start.23 = (bf16[64,2048]{1,0:T(8,128)(2,1)S(1)}, bf16[64,2048]{1,0:T(8,128)(2,1)S(1)}, u32[]{:S(2)}, u32[]{:S(2)}) collective-permute-start(bf16[64,2048]{1,0:T(8,128)(2,1)S(1)} %collective-permute-done.21.refs_1_), channel_id=1, source_target_pairs={{4,0},{8,12},{5,1},{9,13},{6,2},{10,14},{7,3},{11,15},{20,16},{24,... | collective-permute-start | bytes 786440 | tf_op jit(solution)/shard_map/ppermute | solution.py:231
  68.9 15.0 %collective-permute-start.2 = (f32[2,1,64,128]{3,2,1,0:T(8,128)S(1)}, f32[2,1,64,128]{3,2,1,0:T(8,128)S(1)}, u32[]{:S(2)}, u32[]{:S(2)}) collective-permute-start(f32[2,1,64,128]{3,2,1,0:T(8,128)S(1)} %merge.1.refs_0_), channel_id=1, source_target_pairs={{0,4},{4,0},{8,12},{12,8},{1,5},{5,1},{9,13},{13,9},{2,6},{6,2},{1... | collective-permute-start | bytes 196616 | tf_op jit(solution)/shard_map/ppermute | solution.py:625
  94.7 14.4 %collective-permute-start.30 = (bf16[1,64,4096]{2,1,0:T(8,128)(2,1)S(1)}, bf16[1,64,4096]{2,1,0:T(8,128)(2,1)S(1)}, u32[]{:S(2)}, u32[]{:S(2)}) collective-permute-start(bf16[1,64,4096]{2,1,0:T(8,128)(2,1)S(1)} %get-tuple-element.53.refs_0_), channel_id=1, source_target_pairs={{0,2},{1,3},{2,0},{3,1},{4,6},{5,7},{6,4},{7,5},{8,10},{9,11},{10,... | collective-permute-start | bytes 1572872 | tf_op jit(solution)/shard_map/ppermute | solution.py:622
  98.7 11.0 %collective-permute-start.28 = (bf16[128,2048]{1,0:T(8,128)(2,1)S(1)}, bf16[128,2048]{1,0:T(8,128)(2,1)S(1)}, u32[]{:S(2)}, u32[]{:S(2)}) collective-permute-start(bf16[128,2048]{1,0:T(8,128)(2,1)S(1)} %get-tuple-element.51), channel_id=1, source_target_pairs={{0,1},{1,0},{2,3},{3,2},{4,5},{5,4},{6,7},{7,6},{8,9},{9,8},{10,11... | collective-permute-start | bytes 1572872 | tf_op jit(solution)/shard_map/ppermute | solution.py:619
  101.2 10.6 %collective-permute-start.24 = (bf16[128,2048]{1,0:T(8,128)(2,1)S(1)}, bf16[128,2048]{1,0:T(8,128)(2,1)S(1)}, u32[]{:S(2)}, u32[]{:S(2)}) collective-permute-start(bf16[128,2048]{1,0:T(8,128)(2,1)S(1)} %get-tuple-element.45), channel_id=1, source_target_pairs={{0,1},{1,0},{2,3},{3,2},{4,5},{5,4},{6,7},{7,6},{8,9},{9,8},{10,11... | collective-permute-start | bytes 1572872 | tf_op jit(solution)/shard_map/ppermute | solution.py:619
  102.3 11.7 %collective-permute-start.31 = (bf16[1,64,4096]{2,1,0:T(8,128)(2,1)S(1)}, bf16[1,64,4096]{2,1,0:T(8,128)(2,1)S(1)}, u32[]{:S(2)}, u32[]{:S(2)}) collective-permute-start(bf16[1,64,4096]{2,1,0:T(8,128)(2,1)S(1)} %get-tuple-element.53.refs_0_), channel_id=1, source_target_pairs={{0,1},{1,0},{2,3},{3,2},{4,5},{5,4},{6,7},{7,6},{8,9},{9,8},{10,11... | collective-permute-start | bytes 1572872 | tf_op jit(solution)/shard_map/ppermute | solution.py:619
  110.3 9.5 %collective-permute-start.27 = (bf16[64,2048]{1,0:T(8,128)(2,1)S(1)}, bf16[64,2048]{1,0:T(8,128)(2,1)S(1)}, u32[]{:S(2)}, u32[]{:S(2)}) collective-permute-start(bf16[64,2048]{1,0:T(8,128)(2,1)S(1)} %add_convert_fusion.1.refs_0_), channel_id=1, source_target_pairs={{0,2},{1,3},{2,0},{3,1},{4,6},{5,7},{6,4},{7,5},{8,10},{9,11},{10,... | collective-permute-start | bytes 786440 | tf_op jit(solution)/shard_map/ppermute | solution.py:622
  111.8 13.3 %collective-permute-start.29 = (bf16[64,2048]{1,0:T(8,128)(2,1)S(1)}, bf16[64,2048]{1,0:T(8,128)(2,1)S(1)}, u32[]{:S(2)}, u32[]{:S(2)}) collective-permute-start(bf16[64,2048]{1,0:T(8,128)(2,1)S(1)} %add_convert_fusion), channel_id=1, source_target_pairs={{0,2},{1,3},{2,0},{3,1},{4,6},{5,7},{6,4},{7,5},{8,10},{9,11},{10,... | collective-permute-start | bytes 786440 | tf_op jit(solution)/shard_map/ppermute | solution.py:622
  112.4 18.3 %collective-permute-start.16 = (bf16[64,2048]{1,0:T(8,128)(2,1)S(1)}, bf16[64,2048]{1,0:T(8,128)(2,1)S(1)}, u32[]{:S(2)}, u32[]{:S(2)}) collective-permute-start(bf16[64,2048]{1,0:T(8,128)(2,1)S(1)} %add_convert_fusion.3.refs_1_), channel_id=1, source_target_pairs={{0,2},{1,3},{2,0},{3,1},{4,6},{5,7},{6,4},{7,5},{8,10},{9,11},{10,... | collective-permute-start | bytes 786440 | tf_op jit(solution)/shard_map/ppermute | solution.py:622
  114.0 21.6 %collective-permute-start.25 = (bf16[64,2048]{1,0:T(8,128)(2,1)S(1)}, bf16[64,2048]{1,0:T(8,128)(2,1)S(1)}, u32[]{:S(2)}, u32[]{:S(2)}) collective-permute-start(bf16[64,2048]{1,0:T(8,128)(2,1)S(1)} %add_convert_fusion.2), channel_id=1, source_target_pairs={{0,2},{1,3},{2,0},{3,1},{4,6},{5,7},{6,4},{7,5},{8,10},{9,11},{10,... | collective-permute-start | bytes 786440 | tf_op jit(solution)/shard_map/ppermute | solution.py:622
  (18 other events, 136.2 us)

commit v8 on v7

--- a/solution.py
+++ b/solution.py
@@ -88,26 +88,26 @@
 BRIEF = pl.CostEstimate(flops=1, bytes_accessed=1, transcendentals=0)
 
 
-def own_rows(index, block, start, tokens_ref, out_ref):
+def own_rows(index, block, tokens_ref, out_ref, start=0):
     at = pl.multiple_of(index.slot(block) * BLK + start, 16)
     out_ref[...] = tokens_ref[pl.ds(at, out_ref.shape[0])]
 
 
-def first_hop_kernel(index_of, start, index_ref, tokens_ref, *refs):
+def first_hop_kernel(index_of, index_ref, tokens_ref, *refs):
     a_ref, b_ref = refs[-2:]
     index = index_of(index_ref)
-    own_rows(index, jnp.where(index.place == 0, 2, 1), start, tokens_ref, a_ref)
-    own_rows(index, 0, start, tokens_ref, b_ref)
-
-
-def second_hop_kernel(index_of, start, index_ref, tokens_ref, a_ref, b_ref, *refs):
+    own_rows(index, jnp.where(index.place == 0, 2, 1), tokens_ref, a_ref)
+    own_rows(index, 0, tokens_ref, b_ref)
+
+
+def second_hop_kernel(index_of, index_ref, tokens_ref, a_ref, b_ref, *refs):
     x_ref, y_ref = refs[-2:]
     index = index_of(index_ref)
     place = index.place
     outer = jnp.where(place == 0, 1, jnp.where(place == 1, 0, 2))
     middle = jnp.where(place == 1, 2, 1)
-    own_rows(index, outer, start, tokens_ref, x_ref)
-    own_rows(index, middle, start, tokens_ref, y_ref)
+    own_rows(index, outer, tokens_ref, x_ref)
+    own_rows(index, middle, tokens_ref, y_ref)
 
     @pl.when((place == 1) & (index.owner(0) != 1))
     def _():
@@ -118,22 +118,27 @@
         y_ref[...] = a_ref[...]
 
 
-def settle_kernel(index_of, start, index_ref, tokens_ref, x_ref, y_ref, *refs):
-    out_ref = refs[-1]
+def settle_kernel(index_of, index_ref, tokens_ref, x_ref, y_ref, *refs):
+    out_refs = refs[-len(CHUNK_ROWS) :]
     index = index_of(index_ref)
     place = index.place
     owner = index.owner(place)
     mine = owner == place
     edge = (place == 0) | ((place == 1) & (owner == 0)) | ((place == 2) & (owner == 3))
-    own_rows(index, place, start, tokens_ref, out_ref)
-
-    @pl.when(jnp.logical_not(mine) & edge)
-    def _():
-        out_ref[...] = x_ref[...]
-
-    @pl.when(jnp.logical_not(mine | edge))
-    def _():
-        out_ref[...] = y_ref[...]
+    start = 0
+    for out_ref in out_refs:
+        rows = slice(start, start + out_ref.shape[0])
+        own_rows(index, place, tokens_ref, out_ref, start)
+
+        @pl.when(jnp.logical_not(mine) & edge)
+        def _(out_ref=out_ref, rows=rows):
+            out_ref[...] = x_ref[rows]
+
+        @pl.when(jnp.logical_not(mine | edge))
+        def _(out_ref=out_ref, rows=rows):
+            out_ref[...] = y_ref[rows]
+
+        start += out_ref.shape[0]
 
 
 def collect_kernel(index_of, count, index_ref, home_ref, outer_ref, *refs):
@@ -167,86 +172,80 @@
     return specs, [*values, *(in_hbm(v) for v in far)]
 
 
-def hop_call(kernel, index, tokens, unit, count, stay, received, waits, name, declared):
+def hop_call(kernel, index, tokens, heights, received, waits, name):
     specs, extra = after(waits)
-    out = pltpu.VMEM(unit.shape, unit.dtype) if stay else unit
+    width = tokens.shape[1]
     return pl.pallas_call(
         kernel,
         grid_spec=pltpu.PrefetchScalarGridSpec(
             num_scalar_prefetch=1,
             grid=(1,),
             in_specs=[held()] * (1 + len(received)) + specs,
-            out_specs=[held() if stay else whole(unit.shape)] * count,
+            out_specs=[held()] * len(heights),
         ),
-        out_shape=[out] * count,
-        compiler_params=SMALL,
-        cost_estimate=declared,
+        out_shape=[pltpu.VMEM((height, width), tokens.dtype) for height in heights],
+        compiler_params=SMALL,
+        cost_estimate=BRIEF,
         name=name,
     )(index, tokens, *[in_vmem(r) for r in received], *extra)
 
 
-class Homing:
-    def __init__(self, index_of, index, tokens, chunk):
+class Relay:
+    def __init__(self, index_of, index, tokens):
         self.index_of, self.index, self.tokens = index_of, index, tokens
-        self.start = sum(CHUNK_ROWS[:chunk])
-        self.unit = shape_of((CHUNK_ROWS[chunk], tokens.shape[1]), tokens.dtype)
-
-    def call(self, kernel, count, stay, received, waits, name, declared=BRIEF):
-        return hop_call(
-            functools.partial(kernel, self.index_of, self.start),
-            self.index,
-            self.tokens,
-            self.unit,
-            count,
-            stay,
-            received,
-            waits,
-            name,
-            declared,
-        )
+
+    def call(self, kernel, heights, received, waits, name):
+        kernel = functools.partial(kernel, self.index_of)
+        return hop_call(kernel, self.index, self.tokens, heights, received, waits, name)
 
     def first(self, waits=()):
-        inward, left = self.call(first_hop_kernel, 2, True, (), waits, "first_hop")
-        self.sent = inward
+        inward, left = self.call(first_hop_kernel, (BLK, BLK), (), waits, "first_hop")
         self.received = (
             lax.ppermute(inward, "dp", [(3, 2), (0, 1)]),
             lax.ppermute(left, "dp", [(2, 1)]),
         )
+        return inward
 
     def second(self, waits=()):
-        outer, middle = self.call(second_hop_kernel, 2, True, self.received, waits, "second_hop")
-        self.sent = outer
+        outer, middle = self.call(
+            second_hop_kernel, (BLK, BLK), self.received, waits, "second_hop"
+        )
         self.received = (
             lax.ppermute(outer, "dp", [(1, 0), (0, 1), (3, 2)]),
             lax.ppermute(middle, "dp", [(2, 1), (1, 2)]),
         )
+        return outer
 
     def settle(self, waits=()):
-        (home,) = self.call(settle_kernel, 1, True, self.received, waits, "settle")
-        self.sent = home
+        homes = self.call(settle_kernel, CHUNK_ROWS, self.received, waits, "settle")
+        self.arrived = [self.spread(home) for home in homes]
+        return homes[0]
+
+    def spread(self, home):
         outer = lax.ppermute(home, "dp", [(0, 1), (1, 0), (2, 3), (3, 2)])
         inner = lax.ppermute(home, "dp", [(1, 2), (2, 1)])
         outer_2 = lax.ppermute(inner, "dp", [(1, 0), (2, 3)])
         inner_2 = lax.ppermute(outer, "dp", [(1, 2), (2, 1)])
         outer_3 = lax.ppermute(inner_2, "dp", [(1, 0), (2, 3)])
-        self.arrived = home, outer, inner, inner_2, outer_2, outer_3
-
-    def rows(self, waits=()):
-        count, width = self.unit.shape
+        return home, outer, inner, inner_2, outer_2, outer_3
+
+    def rows(self, chunk, waits=()):
+        arrived = self.arrived[chunk]
+        count, width = arrived[0].shape
         specs, extra = after(waits)
         return pl.pallas_call(
             functools.partial(collect_kernel, self.index_of, count),
             grid_spec=pltpu.PrefetchScalarGridSpec(
                 num_scalar_prefetch=1,
                 grid=(1,),
-                in_specs=[held()] * len(self.arrived) + specs,
+                in_specs=[held()] * len(arrived) + specs,
                 out_specs=held(),
             ),
-            out_shape=pltpu.VMEM((4 * count, width), self.unit.dtype),
+            out_shape=pltpu.VMEM((4 * count, width), self.tokens.dtype),
             compiler_params=SMALL,
             cost_estimate=BRIEF,
             name="collect",
-        )(self.index, *[in_vmem(a) for a in self.arrived], *extra)
+        )(self.index, *[in_vmem(a) for a in arrived], *extra)
 
 
 def load_weight_kernel(w_ref, *refs):
@@ -624,9 +623,11 @@
     def across_dp(value, k):
         return lax.ppermute(value, "dp", [(i, i ^ k) for i in range(owners)])
 
-    def every_part(value):
-        same_core = [value] + [to_chip(value, k) for k in range(1, chips)]
-        return same_core + [to_other_core(v) for v in same_core]
+    def same_core(value):
+        return [value] + [to_chip(value, k) for k in range(1, chips)]
+
+    def with_other_core(values):
+        return values + [to_other_core(v) for v in values]
 
     rows_here = in_vmem(tokens)
 
@@ -646,32 +647,39 @@
         arrived = to_other_core(send)
         return arrived, [to_chip(keep[k] + arrived[k], k) for k in range(1, chips)]
 
-    def over_dp(total):
+    def halfway_over_dp(total):
         k = 1
         while 2 * k < owners:
             total = total + across_dp(total, k)
             k *= 2
-        return make_pieces(index_of, index, shape, total, across_dp(total, k), cotangent)
+        return total
+
+    def over_dp(total):
+        return make_pieces(
+            index_of, index, shape, total, across_dp(total, owners // 2), cotangent
+        )
 
     if owners == 4 and block_count == 4:
-        head, tail = [Homing(index_of, index, rows_here, c) for c in range(2)]
-        head.first()
-        tail.first([head.sent])
-        send, keep, back = small_products([tail.sent])
-        head.second([send])
+        relay = Relay(index_of, index, rows_here)
+        sent = relay.first()
+        send, keep, back = small_products([sent])
         arrived, others = over_parts(send, keep)
-        tail.second([head.sent])
-        head.settle([tail.sent])
-        weight = load_weight(frozen_up_weight, [head.sent])
-        total = merge(keep, arrived, back, others, [])
-        tail.settle([total])
+        sent = relay.second(others)
+        weight = load_weight(frozen_up_weight, [sent])
+        total = halfway_over_dp(merge(keep, arrived, back, others, [sent]))
+        relay.settle([weight, total])
         lowered, back_rows, pieces = over_dp(total)
-        chunks = [head.rows(), tail.rows()]
+        pieces_same_core = same_core(pieces)
+        ahead = [v for chunk in relay.arrived[1:] for v in chunk[3:5]]
+        chunks = [relay.rows(0, [lowered, *pieces_same_core[1:], *ahead])]
+        chunks += [relay.rows(c) for c in range(1, len(CHUNK_ROWS))]
     else:
         weight = load_weight(frozen_up_weight, [])
         send, keep, back = small_products([])
         arrived, others = over_parts(send, keep)
-        lowered, back_rows, pieces = over_dp(merge(keep, arrived, back, others, []))
+        total = halfway_over_dp(merge(keep, arrived, back, others, []))
+        lowered, back_rows, pieces = over_dp(total)
+        pieces_same_core = same_core(pieces)
         every_slot = lax.all_gather(
             tokens.reshape(CAP, BLK, width_dev), "dp", axis=0, tiled=True
         )
@@ -685,30 +693,24 @@
             picked[:, s : s + count].reshape(-1, width_dev)
             for s, count in zip(starts, CHUNK_ROWS)
         ]
-    pieces_same_core = [pieces] + [to_chip(pieces, k) for k in range(1, chips)]
-
     def summed(rows, part, part_count, waits):
         each = rows.shape[0] // parts
         send, other, own = split_product(shape, rows, weight, part, part_count, waits)
         arrived = to_other_core(send)
         outgoing = (other + arrived[each:].astype(jnp.float32)).astype(jnp.bfloat16)
-        across = [to_chip(outgoing[(k - 1) * each : k * each], k) for k in range(1, chips)]
-        return [own, arrived] + across, outgoing
-
-    waits = [lowered]
-    sums = []
+        return [own, arrived] + [
+            to_chip(outgoing[(k - 1) * each : k * each], k) for k in range(1, chips)
+        ]
+
+    sums, waits = [], []
     for rows, part_count in zip(chunks, PARTS):
         sums.append([])
-        sent = []
         for part in range(part_count):
-            terms, outgoing = summed(rows, part, part_count, waits)
-            sums[-1].append(terms)
-            sent.append(outgoing)
+            sums[-1].append(summed(rows, part, part_count, waits))
             waits = []
-        waits = sent
-    pieces_all = pieces_same_core + [to_other_core(p) for p in pieces_same_core]
-    up_grad = up_gradient(index_of, index, adapter_count, pieces_all)
-    down_grad = down_gradient(index_of, index, rows_here, every_part(back_rows))
+        waits = [v for terms in sums[-1] for v in terms[2:]]
+    up_grad = up_gradient(index_of, index, adapter_count, with_other_core(pieces_same_core))
+    down_grad = down_gradient(index_of, index, rows_here, with_other_core(same_core(back_rows)))
     projected = None
     for part in range(PARTS[-1]):
         projected = finish(

time: 138 us -> 131 us (0.949)
  starting transfers between devices: 48.3 us -> 39 us
  waiting for transfers between devices: 51.7 us -> 54.4 us
  local copies, waits for them, and re-layouts: 4.36 us -> 5.95 us
    ppermute x10, waiting for transfers between devices: 6.32 us -> 20.8 us  [the longest x2 11.2 us: spread(): outer_2 = lax.ppermute(inner, 'dp', [(1, 0), (2, 3)])]
    ppermute x2, waiting for transfers between devices: 16.8 us -> 9.77 us  [across_dp(): return lax.ppermute(value, 'dp', [(i, i ^ k) for i in range(owners)])]
    ppermute x2 -> x1, starting transfers between devices: 10.2 us -> 5.59 us  [second(): lax.ppermute(outer, 'dp', [(1, 0), (0, 1), (3, 2)])]
    ppermute x2 -> x1, waiting for transfers between devices: 3.65 us -> 0.01 us  [second(): lax.ppermute(outer, 'dp', [(1, 0), (0, 1), (3, 2)])]
    ppermute x7, waiting for transfers between devices: 23.2 us -> 20.4 us  [to_chip(): lax.ppermute(value, 'tensor', [(i, i ^ k * CORES) for i in range(parts)])]
    ppermute x2, starting transfers between devices: 3.71 us -> 1.31 us  [across_dp(): return lax.ppermute(value, 'dp', [(i, i ^ k) for i in range(owners)])]
    ppermute x2 -> x1, starting transfers between devices: 6.98 us -> 4.96 us  [first(): lax.ppermute(inward, 'dp', [(3, 2), (0, 1)])]
    ppermute x9, waiting for transfers between devices: 1.71 us -> 3.46 us  [to_other_core(): return lax.ppermute(value, 'tensor', [(i, i ^ 1) for i in range(parts)])]
  transfers between devices with their start and end apart: 36 -> 32, of which waited for: 13 -> 14; matrix products, arithmetic and copies ran while one was open for 0% -> 0% of each run, Pallas kernels for 21% -> 16%
where the time goes in v8:
time: 131 us
  waiting for transfers between devices  54.4 us (42%)
  starting transfers between devices  39 us (30%)
  Pallas kernels  30.2 us (23%)
  local copies, waits for them, and re-layouts  5.95 us (5%)
    ppermute x7, waiting for transfers between devices, to_chip(): lax.ppermute(value, 'tensor', [(i, i ^ k * CORES) for i in range(parts)])  20.4 us
    ppermute x2, waiting for transfers between devices, spread(): outer_2 = lax.ppermute(inner, 'dp', [(1, 0), (2, 3)])  11.2 us
    ppermute x2, waiting for transfers between devices, across_dp(): return lax.ppermute(value, 'dp', [(i, i ^ k) for i in range(owners)])  9.77 us
    ppermute x2, waiting for transfers between devices, spread(): outer_3 = lax.ppermute(inner_2, 'dp', [(1, 0), (2, 3)])  9.42 us
    pallas_call x4, Pallas kernels, split_product(): pl.pallas_call(functools.partial(split_product_kernel, each, half, part *...  9.3 us
    ppermute x7, starting transfers between devices, to_chip(): lax.ppermute(value, 'tensor', [(i, i ^ k * CORES) for i in range(parts)])  8.42 us
    ppermute x2, starting transfers between devices, spread(): outer = lax.ppermute(home, 'dp', [(0, 1), (1, 0), (2, 3), (3, 2)])  7.44 us
    pallas_call x1, Pallas kernels, load_weight(): pl.pallas_call(load_weight_kernel, grid=(1,), in_specs=[pl.BlockSpec(memo...  5.89 us
  transfers between devices with their start and end apart: 32, of which 14 were waited for; matrix products, arithmetic and copies ran while one was open for 0% of the time, Pallas kernels for 16%

profile of v8, /device:TPU:0, one launch (start us, length us, event | category | flops | bytes accessed | tf_op | source)
XLA Modules:
  0.0 130.8 jit_solution(14404809264180456032)
XLA Ops:
  3.4 5.0 %collective-permute-start.2 = (bf16[128,2048]{1,0:T(8,128)(2,1)S(1)}, bf16[128,2048]{1,0:T(8,128)(2,1)S(1)}, u32[]{:S(2)}, u32[]{:S(2)}) collective-permute-start(bf16[128,2048]{1,0:T(8,128)(2,1)S(1)} %get-tuple-element.27.refs_0_), channel_id=1, source_target_pairs={{12,8},{0,4},{13,9},{1,5},{14,10},{2,6},{15,11},{3,7},{28,24},{16,... | collective-permute-start | bytes 1572872 | tf_op jit(solution)/shard_map/ppermute | solution.py:204
  9.1 1.6 %copy-done.2 = bf16[4,64,4096]{2,1,0:T(8,128)(2,1)S(1)} copy-done((bf16[4,64,4096]{2,1,0:T(8,128)(2,1)S(1)}, bf16[4,64,4096]{2,1,0:T(8,128)(2,1)}, u32[]{:S(2)}) %copy-start.2) | copy-done | bytes 2097176
  17.3 2.4 %collective-permute-done.1.refs_0_ = f32[1,64,128]{2,1,0:T(8,128)S(1)} collective-permute-done((f32[1,64,128]{2,1,0:T(8,128)S(1)}, f32[1,64,128]{2,1,0:T(8,128)S(1)}, u32[]{:S(2)}, u32[]{:S(2)}) %collective-permute-start.1) | collective-permute-done | bytes 32800 | tf_op jit(solution)/shard_map/ppermute | solution.py:621
  20.3 5.6 %collective-permute-start.6 = (bf16[128,2048]{1,0:T(8,128)(2,1)S(1)}, bf16[128,2048]{1,0:T(8,128)(2,1)S(1)}, u32[]{:S(2)}, u32[]{:S(2)}) collective-permute-start(bf16[128,2048]{1,0:T(8,128)(2,1)S(1)} %get-tuple-element.32.refs_1_.refs_0_), channel_id=1, source_target_pairs={{4,0},{0,4},{12,8},{5,1},{1,5},{13,9},{6,2},{2,6},{14,10},{7,3},{3... | collective-permute-start | bytes 1572872 | tf_op jit(solution)/shard_map/ppermute | solution.py:214
  28.0 5.9 %load_weight.1.refs_0_.w_ref = bf16[2048,4096]{1,0:T(8,128)(2,1)S(1)} custom-call(bf16[2048,4096]{1,0:T(8,128)(2,1)} %w_ref.1, bf16[128,2048]{1,0:T(8,128)(2,1)S(1)} %get-tuple-element.32.refs_1_.refs_0_), custom_call_target="tpu_custom_call" | custom-call | flops 1 | bytes 1 | tf_op jit(solution)/shard_map/load_weight/pallas_call | solution.py:269
  33.9 4.5 %collective-permute-done.4 = f32[2,1,64,128]{3,2,1,0:T(8,128)S(1)} collective-permute-done((f32[2,1,64,128]{3,2,1,0:T(8,128)S(1)}, f32[2,1,64,128]{3,2,1,0:T(8,128)S(1)}, u32[]{:S(2)}, u32[]{:S(2)}) %collective-permute-start.4) | collective-permute-done | bytes 65568 | tf_op jit(solution)/shard_map/ppermute | solution.py:624
  39.0 2.3 %collective-permute-start.8 = (bf16[64,2048]{1,0:T(8,128)(2,1)S(1)}, bf16[64,2048]{1,0:T(8,128)(2,1)S(1)}, u32[]{:S(2)}, u32[]{:S(2)}) collective-permute-start(bf16[64,2048]{1,0:T(8,128)(2,1)S(1)} %get-tuple-element.35.home_ref), channel_id=1, source_target_pairs={{0,4},{4,0},{8,12},{12,8},{1,5},{5,1},{9,13},{13,9},{2,6},{6,2},{1... | collective-permute-start | bytes 786440 | tf_op jit(solution)/shard_map/ppermute | solution.py:225
  41.3 5.3 %collective-permute-done.5.more_ref = f32[2,1,64,128]{3,2,1,0:T(8,128)S(1)} collective-permute-done((f32[2,1,64,128]{3,2,1,0:T(8,128)S(1)}, f32[2,1,64,128]{3,2,1,0:T(8,128)S(1)}, u32[]{:S(2)}, u32[]{:S(2)}) %collective-permute-start.5) | collective-permute-done | bytes 65568 | tf_op jit(solution)/shard_map/ppermute | solution.py:624
  48.1 5.1 %collective-permute-start.14 = (bf16[64,2048]{1,0:T(8,128)(2,1)S(1)}, bf16[64,2048]{1,0:T(8,128)(2,1)S(1)}, u32[]{:S(2)}, u32[]{:S(2)}) collective-permute-start(bf16[64,2048]{1,0:T(8,128)(2,1)S(1)} %get-tuple-element.37.home_ref), channel_id=1, source_target_pairs={{0,4},{4,0},{8,12},{12,8},{1,5},{5,1},{9,13},{13,9},{2,6},{6,2},{1... | collective-permute-start | bytes 786440 | tf_op jit(solution)/shard_map/ppermute | solution.py:225
  60.9 2.5 %collective-permute-done.13.refs_5_.refs_1_ = bf16[1,64,4096]{2,1,0:T(8,128)(2,1)S(1)} collective-permute-done((bf16[1,64,4096]{2,1,0:T(8,128)(2,1)S(1)}, bf16[1,64,4096]{2,1,0:T(8,128)(2,1)S(1)}, u32[]{:S(2)}, u32[]{:S(2)}) %collective-permute-start.13) | collective-permute-done | bytes 524320 | tf_op jit(solution)/shard_map/ppermute | solution.py:621
  63.4 5.7 %collective-permute-done.11.refs_2_ = bf16[64,2048]{1,0:T(8,128)(2,1)S(1)} collective-permute-done((bf16[64,2048]{1,0:T(8,128)(2,1)S(1)}, bf16[64,2048]{1,0:T(8,128)(2,1)S(1)}, u32[]{:S(2)}, u32[]{:S(2)}) %collective-permute-start.11) | collective-permute-done | bytes 262176 | tf_op jit(solution)/shard_map/ppermute | solution.py:227
  69.1 5.5 %collective-permute-done.17.refs_7_.refs_2_ = bf16[64,2048]{1,0:T(8,128)(2,1)S(1)} collective-permute-done((bf16[64,2048]{1,0:T(8,128)(2,1)S(1)}, bf16[64,2048]{1,0:T(8,128)(2,1)S(1)}, u32[]{:S(2)}, u32[]{:S(2)}) %collective-permute-start.17) | collective-permute-done | bytes 262176 | tf_op jit(solution)/shard_map/ppermute | solution.py:227
  74.6 2.9 %collective-permute-done.12.refs_3_ = bf16[64,2048]{1,0:T(8,128)(2,1)S(1)} collective-permute-done((bf16[64,2048]{1,0:T(8,128)(2,1)S(1)}, bf16[64,2048]{1,0:T(8,128)(2,1)S(1)}, u32[]{:S(2)}, u32[]{:S(2)}) %collective-permute-start.12) | collective-permute-done | bytes 262176 | tf_op jit(solution)/shard_map/ppermute | solution.py:229
  78.1 2.3 %split_product.4 = (bf16[128,2048]{1,0:T(8,128)(2,1)S(1)}, f32[64,2048]{1,0:T(8,128)S(1)}, f32[64,2048]{1,0:T(8,128)S(1)}) custom-call(bf16[256,2048]{1,0:T(8,128)(2,1)S(1)} %collect.2.rows_ref, bf16[2048,4096]{1,0:T(8,128)(2,1)S(1)} %load_weight.1.refs_0_.w_ref), custom_call_target="tpu_custom_call" | custom-call | flops 1 | bytes 1 | tf_op jit(solution)/shard_map/split_product/pallas_call | solution.py:301
  80.5 2.3 %split_product.6 = (bf16[128,2048]{1,0:T(8,128)(2,1)S(1)}, f32[64,2048]{1,0:T(8,128)S(1)}, f32[64,2048]{1,0:T(8,128)S(1)}) custom-call(bf16[256,2048]{1,0:T(8,128)(2,1)S(1)} %collect.2.rows_ref, bf16[2048,4096]{1,0:T(8,128)(2,1)S(1)} %load_weight.1.refs_0_.w_ref), custom_call_target="tpu_custom_call" | custom-call | flops 1 | bytes 1 | tf_op jit(solution)/shard_map/split_product/pallas_call | solution.py:301
  87.0 6.5 %collective-permute-done.20.refs_3_ = bf16[64,2048]{1,0:T(8,128)(2,1)S(1)} collective-permute-done((bf16[64,2048]{1,0:T(8,128)(2,1)S(1)}, bf16[64,2048]{1,0:T(8,128)(2,1)S(1)}, u32[]{:S(2)}, u32[]{:S(2)}) %collective-permute-start.20) | collective-permute-done | bytes 262176 | tf_op jit(solution)/shard_map/ppermute | solution.py:229
  94.2 4.5 %collective-permute-done.24.refs_0_.refs_5_ = bf16[64,2048]{1,0:T(8,128)(2,1)S(1)} collective-permute-done((bf16[64,2048]{1,0:T(8,128)(2,1)S(1)}, bf16[64,2048]{1,0:T(8,128)(2,1)S(1)}, u32[]{:S(2)}, u32[]{:S(2)}) %collective-permute-start.24) | collective-permute-done | bytes 262176 | tf_op jit(solution)/shard_map/ppermute | solution.py:621
  98.7 2.3 %split_product.7 = (bf16[128,2048]{1,0:T(8,128)(2,1)S(1)}, f32[64,2048]{1,0:T(8,128)S(1)}, f32[64,2048]{1,0:T(8,128)S(1)}) custom-call(bf16[256,2048]{1,0:T(8,128)(2,1)S(1)} %collect.3.rows_ref, bf16[2048,4096]{1,0:T(8,128)(2,1)S(1)} %load_weight.1.refs_0_.w_ref, bf16[64,2048]{1,0:T(8,128)(2,1)S(1)} %collective-permute-done.24.refs_0_.refs_5_, ...), custom_call_target="tpu_custom_call" | custom-call | flops 1 | bytes 1 | tf_op jit(solution)/shard_map/split_product/pallas_call | solution.py:301
  101.1 2.3 %split_product.5 = (bf16[128,2048]{1,0:T(8,128)(2,1)S(1)}, f32[64,2048]{1,0:T(8,128)S(1)}, f32[64,2048]{1,0:T(8,128)S(1)}) custom-call(bf16[256,2048]{1,0:T(8,128)(2,1)S(1)} %collect.3.rows_ref, bf16[2048,4096]{1,0:T(8,128)(2,1)S(1)} %load_weight.1.refs_0_.w_ref), custom_call_target="tpu_custom_call" | custom-call | flops 1 | bytes 1 | tf_op jit(solution)/shard_map/split_product/pallas_call | solution.py:301
  107.9 11.0 %collective-permute-done.29.refs_1_ = bf16[1,64,128]{2,1,0:T(8,128)(2,1)S(1)} collective-permute-done((bf16[1,64,128]{2,1,0:T(8,128)(2,1)S(1)}, bf16[1,64,128]{2,1,0:T(8,128)(2,1)S(1)}, u32[]{:S(2)}, u32[]{:S(2)}) %collective-permute-start.29) | collective-permute-done | bytes 16416 | tf_op jit(solution)/shard_map/ppermute | solution.py:621
  121.3 2.0 %down_gradient.1.refs_10_ = f32[1,64,2048]{2,1,0:T(8,128)} custom-call(s32[14]{0:T(128)S(1)} %concatenate.3.index_ref.refs_0_, bf16[384,2048]{1,0:T(8,128)(2,1)S(1)} %copy-done.1, bf16[1,64,128]{2,1,0:T(8,128)(2,1)S(1)} %get-tuple-element.50.refs_0_, bf16[1,64,128]{2,1,0:T(8,128)(2,1)S(1)} %collective-permute-done.29.refs_1_, ...), custom_call_target="tpu_custom_call" | custom-call | flops 1 | bytes 1 | tf_op jit(solution)/shard_map/down_gradient/pallas_call | solution.py:447
  123.3 3.9 %up_gradient.1.refs_9_ = f32[4,64,4096]{2,1,0:T(8,128)} custom-call(s32[14]{0:T(128)S(1)} %concatenate.3.index_ref.refs_0_, bf16[1,64,4096]{2,1,0:T(8,128)(2,1)S(1)} %get-tuple-element.36.refs_0_, bf16[1,64,4096]{2,1,0:T(8,128)(2,1)S(1)} %collective-permute-done.13.refs_5_.refs_1_, bf16[1,64,4096]{2,1,0:T(8,128)(2,1)S(1)} %collective-permute-done.27.refs_2_, ...), custom_call_target="tpu_custom_call" | custom-call | flops 1 | bytes 1 | tf_op jit(solution)/shard_map/up_gradient/pallas_call | solution.py:488
  127.2 1.8 %finish.2.refs_9_ = bf16[128,4096]{1,0:T(8,128)(2,1)} custom-call(s32[14]{0:T(128)S(1)} %concatenate.3.index_ref.refs_0_, bf16[1,64,128]{2,1,0:T(8,128)(2,1)S(1)} %get-tuple-element.33.refs_4_.refs_1_, bf16[4,64,4096]{2,1,0:T(8,128)(2,1)S(1)} %copy-done.3, f32[64,2048]{1,0:T(8,128)S(1)} %get-tuple-element.44.refs_3_, ...), custom_call_target="tpu_custom_call" | custom-call | flops 1 | bytes 1 | tf_op jit(solution)/shard_map/finish/pallas_call | solution.py:579
  129.0 1.8 %finish.3 = bf16[128,4096]{1,0:T(8,128)(2,1)} custom-call(s32[14]{0:T(128)S(1)} %concatenate.3.index_ref.refs_0_, bf16[1,64,128]{2,1,0:T(8,128)(2,1)S(1)} %get-tuple-element.33.refs_4_.refs_1_, bf16[4,64,4096]{2,1,0:T(8,128)(2,1)S(1)} %copy-done.3, f32[64,2048]{1,0:T(8,128)S(1)} %get-tuple-element.38.refs_3_, ...), custom_call_target="tpu_custom_call", output_to_operand_aliasing={{}: (9, {})} | custom-call | flops 1 | bytes 1 | tf_op jit(solution)/shard_map/finish/pallas_call | solution.py:579
  (78 shorter events, 34.8 us)
Async XLA Ops:
  3.4 16.3 %collective-permute-start.2 = (bf16[128,2048]{1,0:T(8,128)(2,1)S(1)}, bf16[128,2048]{1,0:T(8,128)(2,1)S(1)}, u32[]{:S(2)}, u32[]{:S(2)}) collective-permute-start(bf16[128,2048]{1,0:T(8,128)(2,1)S(1)} %get-tuple-element.27.refs_0_), channel_id=1, source_target_pairs={{12,8},{0,4},{13,9},{1,5},{14,10},{2,6},{15,11},{3,7},{28,24},{16,... | collective-permute-start | bytes 1572872 | tf_op jit(solution)/shard_map/ppermute | solution.py:204
  8.4 11.3 %collective-permute-start.3 = (bf16[128,2048]{1,0:T(8,128)(2,1)S(1)}, bf16[128,2048]{1,0:T(8,128)(2,1)S(1)}, u32[]{:S(2)}, u32[]{:S(2)}) collective-permute-start(bf16[128,2048]{1,0:T(8,128)(2,1)S(1)} %get-tuple-element.31), channel_id=1, source_target_pairs={{8,4},{9,5},{10,6},{11,7},{24,20},{25,21},{26,22},{27,23}} | collective-permute-start | bytes 1572872 | tf_op jit(solution)/shard_map/ppermute | solution.py:205
  20.3 18.1 %collective-permute-start.6 = (bf16[128,2048]{1,0:T(8,128)(2,1)S(1)}, bf16[128,2048]{1,0:T(8,128)(2,1)S(1)}, u32[]{:S(2)}, u32[]{:S(2)}) collective-permute-start(bf16[128,2048]{1,0:T(8,128)(2,1)S(1)} %get-tuple-element.32.refs_1_.refs_0_), channel_id=1, source_target_pairs={{4,0},{0,4},{12,8},{5,1},{1,5},{13,9},{6,2},{2,6},{14,10},{7,3},{3... | collective-permute-start | bytes 1572872 | tf_op jit(solution)/shard_map/ppermute | solution.py:214
  25.9 12.5 %collective-permute-start.7 = (bf16[128,2048]{1,0:T(8,128)(2,1)S(1)}, bf16[128,2048]{1,0:T(8,128)(2,1)S(1)}, u32[]{:S(2)}, u32[]{:S(2)}) collective-permute-start(bf16[128,2048]{1,0:T(8,128)(2,1)S(1)} %get-tuple-element.34), channel_id=1, source_target_pairs={{8,4},{4,8},{9,5},{5,9},{10,6},{6,10},{11,7},{7,11},{24,20},{20,24... | collective-permute-start | bytes 1572872 | tf_op jit(solution)/shard_map/ppermute | solution.py:215
  26.7 11.7 %collective-permute-start.4 = (f32[2,1,64,128]{3,2,1,0:T(8,128)S(1)}, f32[2,1,64,128]{3,2,1,0:T(8,128)S(1)}, u32[]{:S(2)}, u32[]{:S(2)}) collective-permute-start(f32[2,1,64,128]{3,2,1,0:T(8,128)S(1)} %merge.1), channel_id=1, source_target_pairs={{0,4},{4,0},{8,12},{12,8},{1,5},{5,1},{9,13},{13,9},{2,6},{6,2},{1... | collective-permute-start | bytes 196616 | tf_op jit(solution)/shard_map/ppermute | solution.py:624
  39.0 16.4 %collective-permute-start.8 = (bf16[64,2048]{1,0:T(8,128)(2,1)S(1)}, bf16[64,2048]{1,0:T(8,128)(2,1)S(1)}, u32[]{:S(2)}, u32[]{:S(2)}) collective-permute-start(bf16[64,2048]{1,0:T(8,128)(2,1)S(1)} %get-tuple-element.35.home_ref), channel_id=1, source_target_pairs={{0,4},{4,0},{8,12},{12,8},{1,5},{5,1},{9,13},{13,9},{2,6},{6,2},{1... | collective-permute-start | bytes 786440 | tf_op jit(solution)/shard_map/ppermute | solution.py:225
  41.3 5.3 %collective-permute-start.5 = (f32[2,1,64,128]{3,2,1,0:T(8,128)S(1)}, f32[2,1,64,128]{3,2,1,0:T(8,128)S(1)}, u32[]{:S(2)}, u32[]{:S(2)}) collective-permute-start(f32[2,1,64,128]{3,2,1,0:T(8,128)S(1)} %add.31.sum_ref.refs_1_), channel_id=1, source_target_pairs={{0,8},{4,12},{8,0},{12,4},{1,9},{5,13},{9,1},{13,5},{2,10},{6,14},... | collective-permute-start | bytes 196616 | tf_op jit(solution)/shard_map/ppermute | solution.py:624
  47.5 8.7 %collective-permute-start.9 = (bf16[64,2048]{1,0:T(8,128)(2,1)S(1)}, bf16[64,2048]{1,0:T(8,128)(2,1)S(1)}, u32[]{:S(2)}, u32[]{:S(2)}) collective-permute-start(bf16[64,2048]{1,0:T(8,128)(2,1)S(1)} %get-tuple-element.35.home_ref), channel_id=1, source_target_pairs={{4,8},{8,4},{5,9},{9,5},{6,10},{10,6},{7,11},{11,7},{20,24},{24,20... | collective-permute-start | bytes 786440 | tf_op jit(solution)/shard_map/ppermute | solution.py:226
  48.1 9.5 %collective-permute-start.14 = (bf16[64,2048]{1,0:T(8,128)(2,1)S(1)}, bf16[64,2048]{1,0:T(8,128)(2,1)S(1)}, u32[]{:S(2)}, u32[]{:S(2)}) collective-permute-start(bf16[64,2048]{1,0:T(8,128)(2,1)S(1)} %get-tuple-element.37.home_ref), channel_id=1, source_target_pairs={{0,4},{4,0},{8,12},{12,8},{1,5},{5,1},{9,13},{13,9},{2,6},{6,2},{1... | collective-permute-start | bytes 786440 | tf_op jit(solution)/shard_map/ppermute | solution.py:225
  53.3 10.1 %collective-permute-start.13 = (bf16[1,64,4096]{2,1,0:T(8,128)(2,1)S(1)}, bf16[1,64,4096]{2,1,0:T(8,128)(2,1)S(1)}, u32[]{:S(2)}, u32[]{:S(2)}) collective-permute-start(bf16[1,64,4096]{2,1,0:T(8,128)(2,1)S(1)} %get-tuple-element.36.refs_0_), channel_id=1, source_target_pairs={{0,2},{1,3},{2,0},{3,1},{4,6},{5,7},{6,4},{7,5},{8,10},{9,11},{10,... | collective-permute-start | bytes 1572872 | tf_op jit(solution)/shard_map/ppermute | solution.py:621
  55.5 4.2 %collective-permute-start.10 = (bf16[64,2048]{1,0:T(8,128)(2,1)S(1)}, bf16[64,2048]{1,0:T(8,128)(2,1)S(1)}, u32[]{:S(2)}, u32[]{:S(2)}) collective-permute-start(bf16[64,2048]{1,0:T(8,128)(2,1)S(1)} %collective-permute-done.8.outer_ref), channel_id=1, source_target_pairs={{4,8},{8,4},{5,9},{9,5},{6,10},{10,6},{7,11},{11,7},{20,24},{24,20... | collective-permute-start | bytes 786440 | tf_op jit(solution)/shard_map/ppermute | solution.py:228
  56.2 12.9 %collective-permute-start.11 = (bf16[64,2048]{1,0:T(8,128)(2,1)S(1)}, bf16[64,2048]{1,0:T(8,128)(2,1)S(1)}, u32[]{:S(2)}, u32[]{:S(2)}) collective-permute-start(bf16[64,2048]{1,0:T(8,128)(2,1)S(1)} %collective-permute-done.9.refs_0_), channel_id=1, source_target_pairs={{4,0},{8,12},{5,1},{9,13},{6,2},{10,14},{7,3},{11,15},{20,16},{24,... | collective-permute-start | bytes 786440 | tf_op jit(solution)/shard_map/ppermute | solution.py:227
  57.6 11.4 %collective-permute-start.15 = (bf16[64,2048]{1,0:T(8,128)(2,1)S(1)}, bf16[64,2048]{1,0:T(8,128)(2,1)S(1)}, u32[]{:S(2)}, u32[]{:S(2)}) collective-permute-start(bf16[64,2048]{1,0:T(8,128)(2,1)S(1)} %collective-permute-done.14.outer_ref), channel_id=1, source_target_pairs={{4,8},{8,4},{5,9},{9,5},{6,10},{10,6},{7,11},{11,7},{20,24},{24,20... | collective-permute-start | bytes 786440 | tf_op jit(solution)/shard_map/ppermute | solution.py:228
  58.3 16.3 %collective-permute-start.17 = (bf16[64,2048]{1,0:T(8,128)(2,1)S(1)}, bf16[64,2048]{1,0:T(8,128)(2,1)S(1)}, u32[]{:S(2)}, u32[]{:S(2)}) collective-permute-start(bf16[64,2048]{1,0:T(8,128)(2,1)S(1)} %collective-permute-done.16.refs_0_), channel_id=1, source_target_pairs={{4,0},{8,12},{5,1},{9,13},{6,2},{10,14},{7,3},{11,15},{20,16},{24,... | collective-permute-start | bytes 786440 | tf_op jit(solution)/shard_map/ppermute | solution.py:227
  59.6 17.9 %collective-permute-start.12 = (bf16[64,2048]{1,0:T(8,128)(2,1)S(1)}, bf16[64,2048]{1,0:T(8,128)(2,1)S(1)}, u32[]{:S(2)}, u32[]{:S(2)}) collective-permute-start(bf16[64,2048]{1,0:T(8,128)(2,1)S(1)} %collective-permute-done.10.refs_1_), channel_id=1, source_target_pairs={{4,0},{8,12},{5,1},{9,13},{6,2},{10,14},{7,3},{11,15},{20,16},{24,... | collective-permute-start | bytes 786440 | tf_op jit(solution)/shard_map/ppermute | solution.py:229
  80.5 4.3 %collective-permute-start.18 = (bf16[128,2048]{1,0:T(8,128)(2,1)S(1)}, bf16[128,2048]{1,0:T(8,128)(2,1)S(1)}, u32[]{:S(2)}, u32[]{:S(2)}) collective-permute-start(bf16[128,2048]{1,0:T(8,128)(2,1)S(1)} %get-tuple-element.39), channel_id=1, source_target_pairs={{0,1},{1,0},{2,3},{3,2},{4,5},{5,4},{6,7},{7,6},{8,9},{9,8},{10,11... | collective-permute-start | bytes 1572872 | tf_op jit(solution)/shard_map/ppermute | solution.py:618
  83.4 10.1 %collective-permute-start.20 = (bf16[64,2048]{1,0:T(8,128)(2,1)S(1)}, bf16[64,2048]{1,0:T(8,128)(2,1)S(1)}, u32[]{:S(2)}, u32[]{:S(2)}) collective-permute-start(bf16[64,2048]{1,0:T(8,128)(2,1)S(1)} %collective-permute-done.15.refs_6_.refs_1_), channel_id=1, source_target_pairs={{4,0},{8,12},{5,1},{9,13},{6,2},{10,14},{7,3},{11,15},{20,16},{24,... | collective-permute-start | bytes 786440 | tf_op jit(solution)/shard_map/ppermute | solution.py:229
  84.8 9.4 %collective-permute-start.19 = (bf16[64,2048]{1,0:T(8,128)(2,1)S(1)}, bf16[64,2048]{1,0:T(8,128)(2,1)S(1)}, u32[]{:S(2)}, u32[]{:S(2)}) collective-permute-start(bf16[64,2048]{1,0:T(8,128)(2,1)S(1)} %add_convert_fusion.3), channel_id=1, source_target_pairs={{0,2},{1,3},{2,0},{3,1},{4,6},{5,7},{6,4},{7,5},{8,10},{9,11},{10,... | collective-permute-start | bytes 786440 | tf_op jit(solution)/shard_map/ppermute | solution.py:621
  86.0 12.7 %collective-permute-start.24 = (bf16[64,2048]{1,0:T(8,128)(2,1)S(1)}, bf16[64,2048]{1,0:T(8,128)(2,1)S(1)}, u32[]{:S(2)}, u32[]{:S(2)}) collective-permute-start(bf16[64,2048]{1,0:T(8,128)(2,1)S(1)} %add_convert_fusion.1), channel_id=1, source_target_pairs={{0,2},{1,3},{2,0},{3,1},{4,6},{5,7},{6,4},{7,5},{8,10},{9,11},{10,... | collective-permute-start | bytes 786440 | tf_op jit(solution)/shard_map/ppermute | solution.py:621
  104.0 19.3 %collective-permute-start.27 = (bf16[1,64,4096]{2,1,0:T(8,128)(2,1)S(1)}, bf16[1,64,4096]{2,1,0:T(8,128)(2,1)S(1)}, u32[]{:S(2)}, u32[]{:S(2)}) collective-permute-start(bf16[1,64,4096]{2,1,0:T(8,128)(2,1)S(1)} %get-tuple-element.36.refs_0_), channel_id=1, source_target_pairs={{0,1},{1,0},{2,3},{3,2},{4,5},{5,4},{6,7},{7,6},{8,9},{9,8},{10,11... | collective-permute-start | bytes 1572872 | tf_op jit(solution)/shard_map/ppermute | solution.py:618
  104.1 19.2 %collective-permute-start.28 = (bf16[1,64,4096]{2,1,0:T(8,128)(2,1)S(1)}, bf16[1,64,4096]{2,1,0:T(8,128)(2,1)S(1)}, u32[]{:S(2)}, u32[]{:S(2)}) collective-permute-start(bf16[1,64,4096]{2,1,0:T(8,128)(2,1)S(1)} %collective-permute-done.13.refs_5_.refs_1_), channel_id=1, source_target_pairs={{0,1},{1,0},{2,3},{3,2},{4,5},{5,4},{6,7},{7,6},{8,9},{9,8},{10,11... | collective-permute-start | bytes 1572872 | tf_op jit(solution)/shard_map/ppermute | solution.py:618
  104.6 22.6 %collective-permute-start.26 = (bf16[64,2048]{1,0:T(8,128)(2,1)S(1)}, bf16[64,2048]{1,0:T(8,128)(2,1)S(1)}, u32[]{:S(2)}, u32[]{:S(2)}) collective-permute-start(bf16[64,2048]{1,0:T(8,128)(2,1)S(1)} %add_convert_fusion), channel_id=1, source_target_pairs={{0,2},{1,3},{2,0},{3,1},{4,6},{5,7},{6,4},{7,5},{8,10},{9,11},{10,... | collective-permute-start | bytes 786440 | tf_op jit(solution)/shard_map/ppermute | solution.py:621
  105.8 23.2 %collective-permute-start.22 = (bf16[64,2048]{1,0:T(8,128)(2,1)S(1)}, bf16[64,2048]{1,0:T(8,128)(2,1)S(1)}, u32[]{:S(2)}, u32[]{:S(2)}) collective-permute-start(bf16[64,2048]{1,0:T(8,128)(2,1)S(1)} %add_convert_fusion.2), channel_id=1, source_target_pairs={{0,2},{1,3},{2,0},{3,1},{4,6},{5,7},{6,4},{7,5},{8,10},{9,11},{10,... | collective-permute-start | bytes 786440 | tf_op jit(solution)/shard_map/ppermute | solution.py:621
  106.8 12.1 %collective-permute-start.29 = (bf16[1,64,128]{2,1,0:T(8,128)(2,1)S(1)}, bf16[1,64,128]{2,1,0:T(8,128)(2,1)S(1)}, u32[]{:S(2)}, u32[]{:S(2)}) collective-permute-start(bf16[1,64,128]{2,1,0:T(8,128)(2,1)S(1)} %get-tuple-element.50.refs_0_), channel_id=1, source_target_pairs={{0,2},{1,3},{2,0},{3,1},{4,6},{5,7},{6,4},{7,5},{8,10},{9,11},{10,... | collective-permute-start | bytes 49160 | tf_op jit(solution)/shard_map/ppermute | solution.py:621
  (15 other events, 65.6 us)

commit v9 on v8

--- a/solution.py
+++ b/solution.py
@@ -11,7 +11,7 @@
 CAP = 3
 CORES = 2
 CHUNK_ROWS = (64, 64)
-PARTS = (2, 2)
+PARTS = 2
 SMALL = pltpu.CompilerParams(vmem_limit_bytes=12 * 2**20)
 
 adapter_scale = 0.5
@@ -94,10 +94,22 @@
 
 
 def first_hop_kernel(index_of, index_ref, tokens_ref, *refs):
-    a_ref, b_ref = refs[-2:]
-    index = index_of(index_ref)
-    own_rows(index, jnp.where(index.place == 0, 2, 1), tokens_ref, a_ref)
-    own_rows(index, 0, tokens_ref, b_ref)
+    a_ref, b_ref, sems = refs[-3:]
+    index = index_of(index_ref)
+    copies = [
+        pltpu.make_async_copy(
+            tokens_ref.at[pl.ds(pl.multiple_of(index.slot(block) * BLK, BLK), BLK)],
+            out_ref,
+            sems.at[i],
+        )
+        for i, (block, out_ref) in enumerate(
+            ((jnp.where(index.place == 0, 2, 1), a_ref), (0, b_ref))
+        )
+    ]
+    for copy in copies:
+        copy.start()
+    for copy in copies:
+        copy.wait()
 
 
 def second_hop_kernel(index_of, index_ref, tokens_ref, a_ref, b_ref, *refs):
@@ -175,19 +187,23 @@
 def hop_call(kernel, index, tokens, heights, received, waits, name):
     specs, extra = after(waits)
     width = tokens.shape[1]
+    first = not received
     return pl.pallas_call(
         kernel,
         grid_spec=pltpu.PrefetchScalarGridSpec(
             num_scalar_prefetch=1,
             grid=(1,),
-            in_specs=[held()] * (1 + len(received)) + specs,
+            in_specs=[pl.BlockSpec(memory_space=pl.ANY) if first else held()]
+            + [held()] * len(received)
+            + specs,
             out_specs=[held()] * len(heights),
+            scratch_shapes=[pltpu.SemaphoreType.DMA((len(heights),))] * first,
         ),
         out_shape=[pltpu.VMEM((height, width), tokens.dtype) for height in heights],
         compiler_params=SMALL,
         cost_estimate=BRIEF,
         name=name,
-    )(index, tokens, *[in_vmem(r) for r in received], *extra)
+    )(index, (in_hbm if first else in_vmem)(tokens), *[in_vmem(r) for r in received], *extra)
 
 
 class Relay:
@@ -219,7 +235,6 @@
     def settle(self, waits=()):
         homes = self.call(settle_kernel, CHUNK_ROWS, self.received, waits, "settle")
         self.arrived = [self.spread(home) for home in homes]
-        return homes[0]
 
     def spread(self, home):
         outer = lax.ppermute(home, "dp", [(0, 1), (1, 0), (2, 3), (3, 2)])
@@ -229,10 +244,10 @@
         outer_3 = lax.ppermute(inner_2, "dp", [(1, 0), (2, 3)])
         return home, outer, inner, inner_2, outer_2, outer_3
 
-    def rows(self, chunk, waits=()):
+    def rows(self, chunk, waits=(), far=()):
         arrived = self.arrived[chunk]
         count, width = arrived[0].shape
-        specs, extra = after(waits)
+        specs, extra = after(waits, far)
         return pl.pallas_call(
             functools.partial(collect_kernel, self.index_of, count),
             grid_spec=pltpu.PrefetchScalarGridSpec(
@@ -344,7 +359,7 @@
     rank = up.shape[1]
     one = (shape.per_part, rank, BLK)
     outs = [(shape.chips,) + one, (shape.chips,) + one, one]
-    operands = (tokens, down, cotangent, up)
+    operands = (in_vmem(tokens), down, cotangent, up)
     specs, extra = after(waits)
     return pl.pallas_call(
         functools.partial(narrow_kernel, index_of),
@@ -387,38 +402,42 @@
     )(*operands, *extra)
 
 
-def pieces_kernel(index_of, index_ref, sum_ref, more_ref, cot_ref, low_ref, back_ref, piece_ref):
-    index = index_of(index_ref)
+def pieces_kernel(index_of, count, index_ref, cot_ref, sum_ref, *refs):
+    more_refs, (low_ref, back_ref, piece_ref) = refs[:count], refs[-3:]
+    index = index_of(index_ref)
+    level = [sum_ref[...]] + [ref[...] for ref in more_refs]
+    while len(level) > 1:
+        level = [level[j] + level[j + 1] for j in range(0, len(level), 2)]
     for i in range(index.per_part):
         live = index.live_rows(index.block(0, 0, i))
         keep = lax.broadcasted_iota(jnp.int32, low_ref.shape[1:], 1) < live
-        lowered = jnp.where(keep, sum_ref[0, i] + more_ref[0, i], 0.0).astype(low_ref.dtype)
-        back = jnp.where(keep, sum_ref[1, i] + more_ref[1, i], 0.0)
+        lowered = jnp.where(keep, level[0][0, i], 0.0).astype(low_ref.dtype)
         low_ref[i] = lowered
-        back_ref[i] = back.astype(back_ref.dtype)
+        back_ref[i] = jnp.where(keep, level[0][1, i], 0.0).astype(back_ref.dtype)
         piece_ref[i] = jnp.dot(
             lowered, cot_ref[i * BLK : (i + 1) * BLK], preferred_element_type=jnp.float32
         ).astype(piece_ref.dtype)
 
 
-def make_pieces(index_of, index, shape, total, more, cotangent):
+def make_pieces(index_of, index, shape, total, more, cotangent, waits):
     _, per_part, rank, _ = total.shape
     width = cotangent.shape[1]
     outs = [(per_part, rank, BLK), (per_part, rank, BLK), (per_part, rank, width)]
-    operands = (total, more, cotangent)
-    return pl.pallas_call(
-        functools.partial(pieces_kernel, index_of),
+    operands = (cotangent, total, *more)
+    specs, extra = after(waits)
+    return pl.pallas_call(
+        functools.partial(pieces_kernel, index_of, len(more)),
         grid_spec=pltpu.PrefetchScalarGridSpec(
             num_scalar_prefetch=1,
             grid=(1,),
-            in_specs=[whole(o.shape) for o in operands],
+            in_specs=[whole(o.shape) for o in operands] + specs,
             out_specs=[whole(o) for o in outs],
         ),
         out_shape=[shape_of(o, jnp.bfloat16) for o in outs],
         compiler_params=SMALL,
         cost_estimate=BRIEF,
         name="pieces",
-    )(index, *operands)
+    )(index, *operands, *extra)
 
 
 def down_gradient_kernel(index_of, index_ref, tokens_ref, *refs):
@@ -443,7 +462,7 @@
 
 def down_gradient(index_of, index, tokens, backs):
     out = (1, backs[0].shape[1], tokens.shape[1])
-    operands = (tokens, *backs)
+    operands = (in_vmem(tokens), *backs)
     return pl.pallas_call(
         functools.partial(down_gradient_kernel, index_of),
         grid_spec=pltpu.PrefetchScalarGridSpec(
@@ -500,10 +519,10 @@
     )(index, *pieces)
 
 
-def finish_kernel(index_of, layout, tiles, terms, index_ref, low_ref, *refs):
+def finish_kernel(index_of, index_ref, low_ref, *refs):
     index = index_of(index_ref)
     up_refs, sum_refs, out_ref = refs[: index.per_part], refs[index.per_part : -1], refs[-1]
-    step = pl.program_id(0)
+    per_chunk = len(sum_refs) // len(CHUNK_ROWS)
     for i in range(index.per_part):
         block = index.block(0, 0, i)
         live = index.live_rows(block)
@@ -513,29 +532,22 @@
             (((0,), (0,)), ((), ())),
             preferred_element_type=jnp.float32,
         )
-        start, at_ref = 0, 0
-        for count, spans in layout:
-            for p in range(tiles // spans):
-                parts = sum_refs[at_ref : at_ref + terms]
-                at_ref += terms
-
-                @pl.when(step // spans == p)
-                def _(parts=parts, start=start, count=count):
-                    total = adapter_scale * side[start : start + count]
-                    for ref in parts:
-                        total = total + ref[i * count : (i + 1) * count].astype(jnp.float32)
-                    keep = start + lax.broadcasted_iota(jnp.int32, total.shape, 0) < live
-                    at = i * BLK + start
-                    out_ref[at : at + count] = jnp.where(keep, total, 0.0).astype(out_ref.dtype)
-
+        start = 0
+        for c, count in enumerate(CHUNK_ROWS):
+            total = adapter_scale * side[start : start + count]
+            for ref in sum_refs[c * per_chunk : (c + 1) * per_chunk]:
+                total = total + ref[i * count : (i + 1) * count].astype(jnp.float32)
+            keep = start + lax.broadcasted_iota(jnp.int32, total.shape, 0) < live
+            at = i * BLK + start
+            out_ref[at : at + count] = jnp.where(keep, total, 0.0).astype(out_ref.dtype)
             start += count
 
 
-def finish(index_of, index, lowered, up, sums, part, part_count, projected, far):
+def finish(index_of, index, lowered, up, sums, part, projected):
     per_part = lowered.shape[0]
     _, rank, width = up.shape
-    tile = width // max(PARTS)
-    tiles = width // part_count // tile
+    tile = min(1024, width // PARTS)
+    tiles = width // PARTS // tile
     first = part * tiles
     out = (per_part * BLK, width)
 
@@ -546,35 +558,20 @@
 
         return pl.BlockSpec((1, rank, tile), at)
 
-    specs, flat, layout = [], [], []
-    for chunk, count in zip(sums, CHUNK_ROWS):
-        each = max(1, len(chunk) // part_count)
-        begin = part * len(chunk) // part_count
-        spans = tiles // each
-        layout.append((count, spans))
-        for p in range(each):
-            offset = first - begin * (width // len(chunk) // tile) - p * spans
-            limit = width // len(chunk) // tile - 1
-            for value in chunk[begin + p]:
-                specs.append(
-                    pl.BlockSpec(
-                        (per_part * count, tile),
-                        lambda n, _, o=offset, m=limit: (0, jnp.clip(o + n, 0, m)),
-                    )
-                )
-                flat.append(value)
-    terms = len(sums[0][0])
+    flat = [term for chunk in sums for term in chunk]
+    specs = [
+        pl.BlockSpec((per_part * count, tile), lambda n, _: (0, n))
+        for chunk, count in zip(sums, CHUNK_ROWS)
+        for _ in chunk
+    ]
     operands = [index, lowered, *[up] * per_part, *flat]
-    aliases = {}
+    aliases, more, extra = {}, [], []
     if projected is not None:
         aliases = {len(operands): 0}
-        far = [projected]
-    more, extra = after((), far)
-    if projected is not None:
-        extra = [projected]
+        more, extra = [pl.BlockSpec(memory_space=pl.ANY)], [projected]
 
     def kernel(*refs):
-        finish_kernel(index_of, layout, tiles, terms, *refs[: len(operands)], refs[-1])
+        finish_kernel(index_of, *refs[: len(operands)], refs[-1])
 
     return pl.pallas_call(
         kernel,
@@ -629,14 +626,12 @@
     def with_other_core(values):
         return values + [to_other_core(v) for v in values]
 
-    rows_here = in_vmem(tokens)
-
     def small_products(waits):
         return narrow(
             index_of,
             index,
             shape,
-            rows_here,
+            tokens,
             jnp.swapaxes(adapter_down_factor, 1, 2),
             cotangent,
             adapter_up_factor,
@@ -647,39 +642,45 @@
         arrived = to_other_core(send)
         return arrived, [to_chip(keep[k] + arrived[k], k) for k in range(1, chips)]
 
-    def halfway_over_dp(total):
+    def over_dp(total):
         k = 1
-        while 2 * k < owners:
-            total = total + across_dp(total, k)
-            k *= 2
-        return total
-
-    def over_dp(total):
-        return make_pieces(
-            index_of, index, shape, total, across_dp(total, owners // 2), cotangent
+        while True:
+            more = [across_dp(total, j * k) for j in range(1, min(4, owners // k))]
+            if k * 4 >= owners:
+                return total, more
+            total = (total + more[0]) + (more[1] + more[2])
+            k *= 4
+
+    def gradients(total, more, waits):
+        lowered, back_rows, pieces = make_pieces(
+            index_of, index, shape, total, more, cotangent, waits
+        )
+        pieces, back_rows = same_core(pieces), same_core(back_rows)
+        return (
+            lowered,
+            up_gradient(index_of, index, adapter_count, with_other_core(pieces)),
+            down_gradient(index_of, index, tokens, with_other_core(back_rows)),
         )
 
     if owners == 4 and block_count == 4:
-        relay = Relay(index_of, index, rows_here)
+        relay = Relay(index_of, index, tokens)
         sent = relay.first()
         send, keep, back = small_products([sent])
         arrived, others = over_parts(send, keep)
         sent = relay.second(others)
         weight = load_weight(frozen_up_weight, [sent])
-        total = halfway_over_dp(merge(keep, arrived, back, others, [sent]))
-        relay.settle([weight, total])
-        lowered, back_rows, pieces = over_dp(total)
-        pieces_same_core = same_core(pieces)
+        total, more = over_dp(merge(keep, arrived, back, others, [sent]))
+        relay.settle([weight, *more])
+        lowered, up_grad, down_grad = gradients(total, more, relay.arrived[0][1:3])
         ahead = [v for chunk in relay.arrived[1:] for v in chunk[3:5]]
-        chunks = [relay.rows(0, [lowered, *pieces_same_core[1:], *ahead])]
-        chunks += [relay.rows(c) for c in range(1, len(CHUNK_ROWS))]
+        chunks = [lambda waits: relay.rows(0, ahead, [up_grad, down_grad])]
+        chunks += [functools.partial(relay.rows, c) for c in range(1, len(CHUNK_ROWS))]
     else:
         weight = load_weight(frozen_up_weight, [])
         send, keep, back = small_products([])
         arrived, others = over_parts(send, keep)
-        total = halfway_over_dp(merge(keep, arrived, back, others, []))
-        lowered, back_rows, pieces = over_dp(total)
-        pieces_same_core = same_core(pieces)
+        total, more = over_dp(merge(keep, arrived, back, others, []))
+        lowered, up_grad, down_grad = gradients(total, more, [])
         every_slot = lax.all_gather(
             tokens.reshape(CAP, BLK, width_dev), "dp", axis=0, tiled=True
         )
@@ -690,39 +691,35 @@
         picked = every_slot[adapter_of_block[blocks] * CAP + slot_of_block[blocks]]
         starts = [sum(CHUNK_ROWS[:c]) for c in range(len(CHUNK_ROWS))]
         chunks = [
-            picked[:, s : s + count].reshape(-1, width_dev)
+            lambda waits, s=s, count=count: picked[:, s : s + count].reshape(-1, width_dev)
             for s, count in zip(starts, CHUNK_ROWS)
         ]
-    def summed(rows, part, part_count, waits):
+    def summed(rows, part, waits):
         each = rows.shape[0] // parts
-        send, other, own = split_product(shape, rows, weight, part, part_count, waits)
+        send, other, own = split_product(shape, rows, weight, part, PARTS, waits)
         arrived = to_other_core(send)
         outgoing = (other + arrived[each:].astype(jnp.float32)).astype(jnp.bfloat16)
-        return [own, arrived] + [
-            to_chip(outgoing[(k - 1) * each : k * each], k) for k in range(1, chips)
-        ]
-
-    sums, waits = [], []
-    for rows, part_count in zip(chunks, PARTS):
-        sums.append([])
-        for part in range(part_count):
-            sums[-1].append(summed(rows, part, part_count, waits))
-            waits = []
-        waits = [v for terms in sums[-1] for v in terms[2:]]
-    up_grad = up_gradient(index_of, index, adapter_count, with_other_core(pieces_same_core))
-    down_grad = down_gradient(index_of, index, rows_here, with_other_core(same_core(back_rows)))
+        across = [to_chip(outgoing[(k - 1) * each : k * each], k) for k in range(1, chips)]
+        return [own, arrived] + across, outgoing
+
+    sums, rows, waits = [], [], []
+    for chunk in chunks:
+        rows.append(chunk(waits))
+        sums.append([summed(rows[-1], 0, ())])
+        waits = [sums[-1][0][1]]
+    for part in range(1, PARTS):
+        for chunk_rows, done in zip(rows, sums):
+            done.append(summed(chunk_rows, part, rows[-1:]))
     projected = None
-    for part in range(PARTS[-1]):
+    for part in range(PARTS):
         projected = finish(
             index_of,
             index,
             lowered,
             adapter_up_factor,
-            sums,
+            [done[part][0] for done in sums],
             part,
-            PARTS[-1],
             projected,
-            [up_grad, down_grad],
         )
     return (projected, jnp.swapaxes(down_grad, 1, 2), up_grad)
 

time: 131 us -> 142 us (1.084)
  waiting for transfers between devices: 54.4 us -> 64.6 us
  Pallas kernels: 30.2 us -> 31.9 us
  starting transfers between devices: 39 us -> 37.5 us
    ppermute x7, waiting for transfers between devices: 20.4 us -> 27.7 us  [to_chip(): lax.ppermute(value, 'tensor', [(i, i ^ k * CORES) for i in range(parts)])]
    ppermute x2, waiting for transfers between devices: 9.42 us -> 14.1 us  [spread(): outer_3 = lax.ppermute(inner_2, 'dp', [(1, 0), (2, 3)])]
    ppermute x2, waiting for transfers between devices: 0.18 us -> 4.51 us  [spread(): outer = lax.ppermute(home, 'dp', [(0, 1), (1, 0), (2, 3), (3, 2)])]
    ppermute x2 -> x3, starting transfers between devices: 1.31 us -> 4.45 us  [across_dp(): return lax.ppermute(value, 'dp', [(i, i ^ k) for i in range(owners)])]
    ppermute x2, waiting for transfers between devices: 11.2 us -> 8.45 us  [spread(): outer_2 = lax.ppermute(inner, 'dp', [(1, 0), (2, 3)])]
    ppermute x2, starting transfers between devices: 7.44 us -> 4.7 us  [spread(): outer = lax.ppermute(home, 'dp', [(0, 1), (1, 0), (2, 3), (3, 2)])]
    ppermute x2 -> x3, waiting for transfers between devices: 9.77 us -> 7.96 us  [across_dp(): return lax.ppermute(value, 'dp', [(i, i ^ k) for i in range(owners)])]
    ppermute x9, waiting for transfers between devices: 3.46 us -> 1.86 us  [to_other_core(): return lax.ppermute(value, 'tensor', [(i, i ^ 1) for i in range(parts)])]
  transfers between devices with their start and end apart: 32 -> 33, of which waited for: 14 -> 16; matrix products, arithmetic and copies ran while one was open for 0% -> 0% of each run, Pallas kernels for 16% -> 14%
where the time goes in v9:
time: 142 us; the launch traced here: 141 us
  waiting for transfers between devices  64.6 us (45%)
  starting transfers between devices  37.5 us (26%)
  Pallas kernels  31.9 us (22%)
  local copies, waits for them, and re-layouts  5.95 us (4%)
    ppermute x7, waiting for transfers between devices, to_chip(): lax.ppermute(value, 'tensor', [(i, i ^ k * CORES) for i in range(parts)])  27.7 us
    ppermute x2, waiting for transfers between devices, spread(): outer_3 = lax.ppermute(inner_2, 'dp', [(1, 0), (2, 3)])  14.1 us
    pallas_call x4, Pallas kernels, split_product(): pl.pallas_call(functools.partial(split_product_kernel, each, half, part *...  9.52 us
    ppermute x7, starting transfers between devices, to_chip(): lax.ppermute(value, 'tensor', [(i, i ^ k * CORES) for i in range(parts)])  8.85 us
    ppermute x2, waiting for transfers between devices, spread(): outer_2 = lax.ppermute(inner, 'dp', [(1, 0), (2, 3)])  8.45 us
    ppermute x3, waiting for transfers between devices, across_dp(): return lax.ppermute(value, 'dp', [(i, i ^ k) for i in range(owners)])  7.96 us
    pallas_call x1, Pallas kernels, load_weight(): pl.pallas_call(load_weight_kernel, grid=(1,), in_specs=[pl.BlockSpec(memo...  5.89 us
    unnamed x14, local copies, waits for them, and re-layouts  5.19 us
  transfers between devices with their start and end apart: 33, of which 16 were waited for; matrix products, arithmetic and copies ran while one was open for 0% of the time, Pallas kernels for 14%

profile of v9, /device:TPU:0, one launch (start us, length us, event | category | flops | bytes accessed | tf_op | source)
XLA Modules:
  0.0 141.1 jit_solution(1586074651121954923)
XLA Ops:
  3.2 5.0 %collective-permute-start.2 = (bf16[128,2048]{1,0:T(8,128)(2,1)S(1)}, bf16[128,2048]{1,0:T(8,128)(2,1)S(1)}, u32[]{:S(2)}, u32[]{:S(2)}) collective-permute-start(bf16[128,2048]{1,0:T(8,128)(2,1)S(1)} %get-tuple-element.27.refs_0_), channel_id=1, source_target_pairs={{12,8},{0,4},{13,9},{1,5},{14,10},{2,6},{15,11},{3,7},{28,24},{16,... | collective-permute-start | bytes 1572872 | tf_op jit(solution)/shard_map/ppermute | solution.py:220
  18.5 2.4 %collective-permute-done.1.refs_0_ = f32[1,64,128]{2,1,0:T(8,128)S(1)} collective-permute-done((f32[1,64,128]{2,1,0:T(8,128)S(1)}, f32[1,64,128]{2,1,0:T(8,128)S(1)}, u32[]{:S(2)}, u32[]{:S(2)}) %collective-permute-start.1) | collective-permute-done | bytes 32800 | tf_op jit(solution)/shard_map/ppermute | solution.py:618
  21.5 4.2 %collective-permute-start.7 = (bf16[128,2048]{1,0:T(8,128)(2,1)S(1)}, bf16[128,2048]{1,0:T(8,128)(2,1)S(1)}, u32[]{:S(2)}, u32[]{:S(2)}) collective-permute-start(bf16[128,2048]{1,0:T(8,128)(2,1)S(1)} %get-tuple-element.32.refs_1_.refs_0_), channel_id=1, source_target_pairs={{4,0},{0,4},{12,8},{5,1},{1,5},{13,9},{6,2},{2,6},{14,10},{7,3},{3... | collective-permute-start | bytes 1572872 | tf_op jit(solution)/shard_map/ppermute | solution.py:230
  30.9 5.9 %load_weight.1.refs_0_.w_ref = bf16[2048,4096]{1,0:T(8,128)(2,1)S(1)} custom-call(bf16[2048,4096]{1,0:T(8,128)(2,1)} %w_ref.1, bf16[128,2048]{1,0:T(8,128)(2,1)S(1)} %get-tuple-element.32.refs_1_.refs_0_), custom_call_target="tpu_custom_call" | custom-call | flops 1 | bytes 1 | tf_op jit(solution)/shard_map/load_weight/pallas_call | solution.py:284
  38.8 6.0 %collective-permute-done.5.refs_2_.refs_1_ = f32[2,1,64,128]{3,2,1,0:T(8,128)S(1)} collective-permute-done((f32[2,1,64,128]{3,2,1,0:T(8,128)S(1)}, f32[2,1,64,128]{3,2,1,0:T(8,128)S(1)}, u32[]{:S(2)}, u32[]{:S(2)}) %collective-permute-start.5) | collective-permute-done | bytes 65568 | tf_op jit(solution)/shard_map/ppermute | solution.py:621
  46.1 2.8 %collective-permute-start.9 = (bf16[64,2048]{1,0:T(8,128)(2,1)S(1)}, bf16[64,2048]{1,0:T(8,128)(2,1)S(1)}, u32[]{:S(2)}, u32[]{:S(2)}) collective-permute-start(bf16[64,2048]{1,0:T(8,128)(2,1)S(1)} %get-tuple-element.34.home_ref), channel_id=1, source_target_pairs={{0,4},{4,0},{8,12},{12,8},{1,5},{5,1},{9,13},{13,9},{2,6},{6,2},{1... | collective-permute-start | bytes 786440 | tf_op jit(solution)/shard_map/ppermute | solution.py:240
  49.0 4.5 %collective-permute-done.9.refs_3_.outer_ref = bf16[64,2048]{1,0:T(8,128)(2,1)S(1)} collective-permute-done((bf16[64,2048]{1,0:T(8,128)(2,1)S(1)}, bf16[64,2048]{1,0:T(8,128)(2,1)S(1)}, u32[]{:S(2)}, u32[]{:S(2)}) %collective-permute-start.9) | collective-permute-done | bytes 262176 | tf_op jit(solution)/shard_map/ppermute | solution.py:240
  58.4 7.2 %collective-permute-done.18.refs_1_ = bf16[1,64,4096]{2,1,0:T(8,128)(2,1)S(1)} collective-permute-done((bf16[1,64,4096]{2,1,0:T(8,128)(2,1)S(1)}, bf16[1,64,4096]{2,1,0:T(8,128)(2,1)S(1)}, u32[]{:S(2)}, u32[]{:S(2)}) %collective-permute-start.18) | collective-permute-done | bytes 524320 | tf_op jit(solution)/shard_map/ppermute | solution.py:618
  68.1 2.0 %collective-permute-done.21.refs_1_ = bf16[1,64,128]{2,1,0:T(8,128)(2,1)S(1)} collective-permute-done((bf16[1,64,128]{2,1,0:T(8,128)(2,1)S(1)}, bf16[1,64,128]{2,1,0:T(8,128)(2,1)S(1)}, u32[]{:S(2)}, u32[]{:S(2)}) %collective-permute-start.21) | collective-permute-done | bytes 16416 | tf_op jit(solution)/shard_map/ppermute | solution.py:618
  76.1 3.9 %up_gradient.1.refs_6_ = f32[4,64,4096]{2,1,0:T(8,128)} custom-call(s32[14]{0:T(128)S(1)} %concatenate.3.index_ref.refs_0_, bf16[1,64,4096]{2,1,0:T(8,128)(2,1)S(1)} %get-tuple-element.37.refs_0_, bf16[1,64,4096]{2,1,0:T(8,128)(2,1)S(1)} %collective-permute-done.18.refs_1_, bf16[1,64,4096]{2,1,0:T(8,128)(2,1)S(1)} %collective-permute-done.19.refs_2_, ...), custom_call_target="tpu_custom_call" | custom-call | flops 1 | bytes 1 | tf_op jit(solution)/shard_map/up_gradient/pallas_call | solution.py:507
  80.0 2.8 %collective-permute-done.12.refs_2_ = bf16[64,2048]{1,0:T(8,128)(2,1)S(1)} collective-permute-done((bf16[64,2048]{1,0:T(8,128)(2,1)S(1)}, bf16[64,2048]{1,0:T(8,128)(2,1)S(1)}, u32[]{:S(2)}, u32[]{:S(2)}) %collective-permute-start.12) | collective-permute-done | bytes 262176 | tf_op jit(solution)/shard_map/ppermute | solution.py:242
  82.9 5.6 %collective-permute-done.17.refs_5_.refs_2_ = bf16[64,2048]{1,0:T(8,128)(2,1)S(1)} collective-permute-done((bf16[64,2048]{1,0:T(8,128)(2,1)S(1)}, bf16[64,2048]{1,0:T(8,128)(2,1)S(1)}, u32[]{:S(2)}, u32[]{:S(2)}) %collective-permute-start.17) | collective-permute-done | bytes 262176 | tf_op jit(solution)/shard_map/ppermute | solution.py:242
  88.5 5.4 %collective-permute-done.13.refs_3_ = bf16[64,2048]{1,0:T(8,128)(2,1)S(1)} collective-permute-done((bf16[64,2048]{1,0:T(8,128)(2,1)S(1)}, bf16[64,2048]{1,0:T(8,128)(2,1)S(1)}, u32[]{:S(2)}, u32[]{:S(2)}) %collective-permute-start.13) | collective-permute-done | bytes 262176 | tf_op jit(solution)/shard_map/ppermute | solution.py:244
  94.6 2.4 %split_product.4 = (bf16[128,2048]{1,0:T(8,128)(2,1)S(1)}, f32[64,2048]{1,0:T(8,128)S(1)}, f32[64,2048]{1,0:T(8,128)S(1)}) custom-call(bf16[256,2048]{1,0:T(8,128)(2,1)S(1)} %collect.2.rows_ref, bf16[2048,4096]{1,0:T(8,128)(2,1)S(1)} %load_weight.1.refs_0_.w_ref), custom_call_target="tpu_custom_call" | custom-call | flops 1 | bytes 1 | tf_op jit(solution)/shard_map/split_product/pallas_call | solution.py:316
  99.0 8.6 %collective-permute-done.24.refs_3_ = bf16[64,2048]{1,0:T(8,128)(2,1)S(1)} collective-permute-done((bf16[64,2048]{1,0:T(8,128)(2,1)S(1)}, bf16[64,2048]{1,0:T(8,128)(2,1)S(1)}, u32[]{:S(2)}, u32[]{:S(2)}) %collective-permute-start.24) | collective-permute-done | bytes 262176 | tf_op jit(solution)/shard_map/ppermute | solution.py:244
  108.4 2.4 %split_product.7 = (bf16[128,2048]{1,0:T(8,128)(2,1)S(1)}, f32[64,2048]{1,0:T(8,128)S(1)}, f32[64,2048]{1,0:T(8,128)S(1)}) custom-call(bf16[256,2048]{1,0:T(8,128)(2,1)S(1)} %collect.3.refs_0_.rows_ref, bf16[2048,4096]{1,0:T(8,128)(2,1)S(1)} %load_weight.1.refs_0_.w_ref), custom_call_target="tpu_custom_call" | custom-call | flops 1 | bytes 1 | tf_op jit(solution)/shard_map/split_product/pallas_call | solution.py:316
  110.9 2.4 %split_product.6 = (bf16[128,2048]{1,0:T(8,128)(2,1)S(1)}, f32[64,2048]{1,0:T(8,128)S(1)}, f32[64,2048]{1,0:T(8,128)S(1)}) custom-call(bf16[256,2048]{1,0:T(8,128)(2,1)S(1)} %collect.3.refs_0_.rows_ref, bf16[2048,4096]{1,0:T(8,128)(2,1)S(1)} %load_weight.1.refs_0_.w_ref, bf16[256,2048]{1,0:T(8,128)(2,1)S(1)} %collect.3.refs_0_.rows_ref), custom_call_target="tpu_custom_call" | custom-call | flops 1 | bytes 1 | tf_op jit(solution)/shard_map/split_product/pallas_call | solution.py:316
  115.3 2.4 %split_product.5 = (bf16[128,2048]{1,0:T(8,128)(2,1)S(1)}, f32[64,2048]{1,0:T(8,128)S(1)}, f32[64,2048]{1,0:T(8,128)S(1)}) custom-call(bf16[256,2048]{1,0:T(8,128)(2,1)S(1)} %collect.2.rows_ref, bf16[2048,4096]{1,0:T(8,128)(2,1)S(1)} %load_weight.1.refs_0_.w_ref, bf16[256,2048]{1,0:T(8,128)(2,1)S(1)} %collect.3.refs_0_.rows_ref), custom_call_target="tpu_custom_call" | custom-call | flops 1 | bytes 1 | tf_op jit(solution)/shard_map/split_product/pallas_call | solution.py:316
  120.8 2.2 %collective-permute-done.30.refs_5_ = bf16[64,2048]{1,0:T(8,128)(2,1)S(1)} collective-permute-done((bf16[64,2048]{1,0:T(8,128)(2,1)S(1)}, bf16[64,2048]{1,0:T(8,128)(2,1)S(1)}, u32[]{:S(2)}, u32[]{:S(2)}) %collective-permute-start.30) | collective-permute-done | bytes 262176 | tf_op jit(solution)/shard_map/ppermute | solution.py:618
  123.0 5.6 %collective-permute-done.32.refs_8_ = bf16[64,2048]{1,0:T(8,128)(2,1)S(1)} collective-permute-done((bf16[64,2048]{1,0:T(8,128)(2,1)S(1)}, bf16[64,2048]{1,0:T(8,128)(2,1)S(1)}, u32[]{:S(2)}, u32[]{:S(2)}) %collective-permute-start.32) | collective-permute-done | bytes 262176 | tf_op jit(solution)/shard_map/ppermute | solution.py:618
  128.6 2.1 %finish.2.refs_9_ = bf16[128,4096]{1,0:T(8,128)(2,1)} custom-call(s32[14]{0:T(128)S(1)} %concatenate.3.index_ref.refs_0_, bf16[1,64,128]{2,1,0:T(8,128)(2,1)S(1)} %get-tuple-element.35.refs_1_, bf16[4,64,4096]{2,1,0:T(8,128)(2,1)S(1)} %copy-done.3, f32[64,2048]{1,0:T(8,128)S(1)} %get-tuple-element.47.refs_3_, ...), custom_call_target="tpu_custom_call" | custom-call | flops 1 | bytes 1 | tf_op jit(solution)/shard_map/finish/pallas_call | solution.py:576
  130.8 3.5 %collective-permute-done.29.refs_8_ = bf16[64,2048]{1,0:T(8,128)(2,1)S(1)} collective-permute-done((bf16[64,2048]{1,0:T(8,128)(2,1)S(1)}, bf16[64,2048]{1,0:T(8,128)(2,1)S(1)}, u32[]{:S(2)}, u32[]{:S(2)}) %collective-permute-start.29) | collective-permute-done | bytes 262176 | tf_op jit(solution)/shard_map/ppermute | solution.py:618
  134.2 4.7 %collective-permute-done.27.refs_5_ = bf16[64,2048]{1,0:T(8,128)(2,1)S(1)} collective-permute-done((bf16[64,2048]{1,0:T(8,128)(2,1)S(1)}, bf16[64,2048]{1,0:T(8,128)(2,1)S(1)}, u32[]{:S(2)}, u32[]{:S(2)}) %collective-permute-start.27) | collective-permute-done | bytes 262176 | tf_op jit(solution)/shard_map/ppermute | solution.py:618
  139.0 2.1 %finish.3 = bf16[128,4096]{1,0:T(8,128)(2,1)} custom-call(s32[14]{0:T(128)S(1)} %concatenate.3.index_ref.refs_0_, bf16[1,64,128]{2,1,0:T(8,128)(2,1)S(1)} %get-tuple-element.35.refs_1_, bf16[4,64,4096]{2,1,0:T(8,128)(2,1)S(1)} %copy-done.3, f32[64,2048]{1,0:T(8,128)S(1)} %get-tuple-element.41.refs_3_, ...), custom_call_target="tpu_custom_call", output_to_operand_aliasing={{}: (9, {})} | custom-call | flops 1 | bytes 1 | tf_op jit(solution)/shard_map/finish/pallas_call | solution.py:576
  (79 shorter events, 43.8 us)
Async XLA Ops:
  3.2 17.7 %collective-permute-start.2 = (bf16[128,2048]{1,0:T(8,128)(2,1)S(1)}, bf16[128,2048]{1,0:T(8,128)(2,1)S(1)}, u32[]{:S(2)}, u32[]{:S(2)}) collective-permute-start(bf16[128,2048]{1,0:T(8,128)(2,1)S(1)} %get-tuple-element.27.refs_0_), channel_id=1, source_target_pairs={{12,8},{0,4},{13,9},{1,5},{14,10},{2,6},{15,11},{3,7},{28,24},{16,... | collective-permute-start | bytes 1572872 | tf_op jit(solution)/shard_map/ppermute | solution.py:220
  8.2 12.7 %collective-permute-start.3 = (bf16[128,2048]{1,0:T(8,128)(2,1)S(1)}, bf16[128,2048]{1,0:T(8,128)(2,1)S(1)}, u32[]{:S(2)}, u32[]{:S(2)}) collective-permute-start(bf16[128,2048]{1,0:T(8,128)(2,1)S(1)} %get-tuple-element.31), channel_id=1, source_target_pairs={{8,4},{9,5},{10,6},{11,7},{24,20},{25,21},{26,22},{27,23}} | collective-permute-start | bytes 1572872 | tf_op jit(solution)/shard_map/ppermute | solution.py:221
  21.5 23.2 %collective-permute-start.7 = (bf16[128,2048]{1,0:T(8,128)(2,1)S(1)}, bf16[128,2048]{1,0:T(8,128)(2,1)S(1)}, u32[]{:S(2)}, u32[]{:S(2)}) collective-permute-start(bf16[128,2048]{1,0:T(8,128)(2,1)S(1)} %get-tuple-element.32.refs_1_.refs_0_), channel_id=1, source_target_pairs={{4,0},{0,4},{12,8},{5,1},{1,5},{13,9},{6,2},{2,6},{14,10},{7,3},{3... | collective-permute-start | bytes 1572872 | tf_op jit(solution)/shard_map/ppermute | solution.py:230
  25.7 19.1 %collective-permute-start.8 = (bf16[128,2048]{1,0:T(8,128)(2,1)S(1)}, bf16[128,2048]{1,0:T(8,128)(2,1)S(1)}, u32[]{:S(2)}, u32[]{:S(2)}) collective-permute-start(bf16[128,2048]{1,0:T(8,128)(2,1)S(1)} %get-tuple-element.33), channel_id=1, source_target_pairs={{8,4},{4,8},{9,5},{5,9},{10,6},{6,10},{11,7},{7,11},{24,20},{20,24... | collective-permute-start | bytes 1572872 | tf_op jit(solution)/shard_map/ppermute | solution.py:231
  26.4 12.4 %collective-permute-start.4 = (f32[2,1,64,128]{3,2,1,0:T(8,128)S(1)}, f32[2,1,64,128]{3,2,1,0:T(8,128)S(1)}, u32[]{:S(2)}, u32[]{:S(2)}) collective-permute-start(f32[2,1,64,128]{3,2,1,0:T(8,128)S(1)} %merge.1.sum_ref), channel_id=1, source_target_pairs={{0,4},{4,0},{8,12},{12,8},{1,5},{5,1},{9,13},{13,9},{2,6},{6,2},{1... | collective-permute-start | bytes 196616 | tf_op jit(solution)/shard_map/ppermute | solution.py:621
  27.8 17.0 %collective-permute-start.5 = (f32[2,1,64,128]{3,2,1,0:T(8,128)S(1)}, f32[2,1,64,128]{3,2,1,0:T(8,128)S(1)}, u32[]{:S(2)}, u32[]{:S(2)}) collective-permute-start(f32[2,1,64,128]{3,2,1,0:T(8,128)S(1)} %merge.1.sum_ref), channel_id=1, source_target_pairs={{0,8},{4,12},{8,0},{12,4},{1,9},{5,13},{9,1},{13,5},{2,10},{6,14},... | collective-permute-start | bytes 196616 | tf_op jit(solution)/shard_map/ppermute | solution.py:621
  29.3 15.5 %collective-permute-start.6 = (f32[2,1,64,128]{3,2,1,0:T(8,128)S(1)}, f32[2,1,64,128]{3,2,1,0:T(8,128)S(1)}, u32[]{:S(2)}, u32[]{:S(2)}) collective-permute-start(f32[2,1,64,128]{3,2,1,0:T(8,128)S(1)} %merge.1.sum_ref), channel_id=1, source_target_pairs={{0,12},{4,8},{8,4},{12,0},{1,13},{5,9},{9,5},{13,1},{2,14},{6,10},... | collective-permute-start | bytes 196616 | tf_op jit(solution)/shard_map/ppermute | solution.py:621
  46.1 7.4 %collective-permute-start.9 = (bf16[64,2048]{1,0:T(8,128)(2,1)S(1)}, bf16[64,2048]{1,0:T(8,128)(2,1)S(1)}, u32[]{:S(2)}, u32[]{:S(2)}) collective-permute-start(bf16[64,2048]{1,0:T(8,128)(2,1)S(1)} %get-tuple-element.34.home_ref), channel_id=1, source_target_pairs={{0,4},{4,0},{8,12},{12,8},{1,5},{5,1},{9,13},{13,9},{2,6},{6,2},{1... | collective-permute-start | bytes 786440 | tf_op jit(solution)/shard_map/ppermute | solution.py:240
  54.3 11.3 %collective-permute-start.18 = (bf16[1,64,4096]{2,1,0:T(8,128)(2,1)S(1)}, bf16[1,64,4096]{2,1,0:T(8,128)(2,1)S(1)}, u32[]{:S(2)}, u32[]{:S(2)}) collective-permute-start(bf16[1,64,4096]{2,1,0:T(8,128)(2,1)S(1)} %get-tuple-element.37.refs_0_), channel_id=1, source_target_pairs={{0,2},{1,3},{2,0},{3,1},{4,6},{5,7},{6,4},{7,5},{8,10},{9,11},{10,... | collective-permute-start | bytes 1572872 | tf_op jit(solution)/shard_map/ppermute | solution.py:618
  55.9 17.5 %collective-permute-start.19 = (bf16[1,64,4096]{2,1,0:T(8,128)(2,1)S(1)}, bf16[1,64,4096]{2,1,0:T(8,128)(2,1)S(1)}, u32[]{:S(2)}, u32[]{:S(2)}) collective-permute-start(bf16[1,64,4096]{2,1,0:T(8,128)(2,1)S(1)} %get-tuple-element.37.refs_0_), channel_id=1, source_target_pairs={{0,1},{1,0},{2,3},{3,2},{4,5},{5,4},{6,7},{7,6},{8,9},{9,8},{10,11... | collective-permute-start | bytes 1572872 | tf_op jit(solution)/shard_map/ppermute | solution.py:615
  55.9 10.4 %collective-permute-start.14 = (bf16[64,2048]{1,0:T(8,128)(2,1)S(1)}, bf16[64,2048]{1,0:T(8,128)(2,1)S(1)}, u32[]{:S(2)}, u32[]{:S(2)}) collective-permute-start(bf16[64,2048]{1,0:T(8,128)(2,1)S(1)} %get-tuple-element.36.home_ref), channel_id=1, source_target_pairs={{0,4},{4,0},{8,12},{12,8},{1,5},{5,1},{9,13},{13,9},{2,6},{6,2},{1... | collective-permute-start | bytes 786440 | tf_op jit(solution)/shard_map/ppermute | solution.py:240
  57.7 10.1 %collective-permute-start.16 = (bf16[64,2048]{1,0:T(8,128)(2,1)S(1)}, bf16[64,2048]{1,0:T(8,128)(2,1)S(1)}, u32[]{:S(2)}, u32[]{:S(2)}) collective-permute-start(bf16[64,2048]{1,0:T(8,128)(2,1)S(1)} %get-tuple-element.36.home_ref), channel_id=1, source_target_pairs={{4,8},{8,4},{5,9},{9,5},{6,10},{10,6},{7,11},{11,7},{20,24},{24,20... | collective-permute-start | bytes 786440 | tf_op jit(solution)/shard_map/ppermute | solution.py:241
  65.6 10.5 %collective-permute-start.20 = (bf16[1,64,4096]{2,1,0:T(8,128)(2,1)S(1)}, bf16[1,64,4096]{2,1,0:T(8,128)(2,1)S(1)}, u32[]{:S(2)}, u32[]{:S(2)}) collective-permute-start(bf16[1,64,4096]{2,1,0:T(8,128)(2,1)S(1)} %collective-permute-done.18.refs_1_), channel_id=1, source_target_pairs={{0,1},{1,0},{2,3},{3,2},{4,5},{5,4},{6,7},{7,6},{8,9},{9,8},{10,11... | collective-permute-start | bytes 1572872 | tf_op jit(solution)/shard_map/ppermute | solution.py:615
  65.6 6.5 %collective-permute-start.11 = (bf16[64,2048]{1,0:T(8,128)(2,1)S(1)}, bf16[64,2048]{1,0:T(8,128)(2,1)S(1)}, u32[]{:S(2)}, u32[]{:S(2)}) collective-permute-start(bf16[64,2048]{1,0:T(8,128)(2,1)S(1)} %collective-permute-done.9.refs_3_.outer_ref), channel_id=1, source_target_pairs={{4,8},{8,4},{5,9},{9,5},{6,10},{10,6},{7,11},{11,7},{20,24},{24,20... | collective-permute-start | bytes 786440 | tf_op jit(solution)/shard_map/ppermute | solution.py:243
  70.1 12.7 %collective-permute-start.12 = (bf16[64,2048]{1,0:T(8,128)(2,1)S(1)}, bf16[64,2048]{1,0:T(8,128)(2,1)S(1)}, u32[]{:S(2)}, u32[]{:S(2)}) collective-permute-start(bf16[64,2048]{1,0:T(8,128)(2,1)S(1)} %collective-permute-done.10.refs_4_.refs_0_), channel_id=1, source_target_pairs={{4,0},{8,12},{5,1},{9,13},{6,2},{10,14},{7,3},{11,15},{20,16},{24,... | collective-permute-start | bytes 786440 | tf_op jit(solution)/shard_map/ppermute | solution.py:242
  71.4 11.4 %collective-permute-start.15 = (bf16[64,2048]{1,0:T(8,128)(2,1)S(1)}, bf16[64,2048]{1,0:T(8,128)(2,1)S(1)}, u32[]{:S(2)}, u32[]{:S(2)}) collective-permute-start(bf16[64,2048]{1,0:T(8,128)(2,1)S(1)} %collective-permute-done.14.outer_ref), channel_id=1, source_target_pairs={{4,8},{8,4},{5,9},{9,5},{6,10},{10,6},{7,11},{11,7},{20,24},{24,20... | collective-permute-start | bytes 786440 | tf_op jit(solution)/shard_map/ppermute | solution.py:243
  72.1 16.4 %collective-permute-start.17 = (bf16[64,2048]{1,0:T(8,128)(2,1)S(1)}, bf16[64,2048]{1,0:T(8,128)(2,1)S(1)}, u32[]{:S(2)}, u32[]{:S(2)}) collective-permute-start(bf16[64,2048]{1,0:T(8,128)(2,1)S(1)} %collective-permute-done.16.refs_0_), channel_id=1, source_target_pairs={{4,0},{8,12},{5,1},{9,13},{6,2},{10,14},{7,3},{11,15},{20,16},{24,... | collective-permute-start | bytes 786440 | tf_op jit(solution)/shard_map/ppermute | solution.py:242
  73.4 20.5 %collective-permute-start.13 = (bf16[64,2048]{1,0:T(8,128)(2,1)S(1)}, bf16[64,2048]{1,0:T(8,128)(2,1)S(1)}, u32[]{:S(2)}, u32[]{:S(2)}) collective-permute-start(bf16[64,2048]{1,0:T(8,128)(2,1)S(1)} %collective-permute-done.11.refs_1_), channel_id=1, source_target_pairs={{4,0},{8,12},{5,1},{9,13},{6,2},{10,14},{7,3},{11,15},{20,16},{24,... | collective-permute-start | bytes 786440 | tf_op jit(solution)/shard_map/ppermute | solution.py:244
  97.0 10.6 %collective-permute-start.24 = (bf16[64,2048]{1,0:T(8,128)(2,1)S(1)}, bf16[64,2048]{1,0:T(8,128)(2,1)S(1)}, u32[]{:S(2)}, u32[]{:S(2)}) collective-permute-start(bf16[64,2048]{1,0:T(8,128)(2,1)S(1)} %collective-permute-done.15.refs_4_.refs_1_), channel_id=1, source_target_pairs={{4,0},{8,12},{5,1},{9,13},{6,2},{10,14},{7,3},{11,15},{20,16},{24,... | collective-permute-start | bytes 786440 | tf_op jit(solution)/shard_map/ppermute | solution.py:244
  110.8 7.0 %collective-permute-start.31 = (bf16[128,2048]{1,0:T(8,128)(2,1)S(1)}, bf16[128,2048]{1,0:T(8,128)(2,1)S(1)}, u32[]{:S(2)}, u32[]{:S(2)}) collective-permute-start(bf16[128,2048]{1,0:T(8,128)(2,1)S(1)} %get-tuple-element.49), channel_id=1, source_target_pairs={{0,1},{1,0},{2,3},{3,2},{4,5},{5,4},{6,7},{7,6},{8,9},{9,8},{10,11... | collective-permute-start | bytes 1572872 | tf_op jit(solution)/shard_map/ppermute | solution.py:615
  113.9 9.2 %collective-permute-start.30 = (bf16[64,2048]{1,0:T(8,128)(2,1)S(1)}, bf16[64,2048]{1,0:T(8,128)(2,1)S(1)}, u32[]{:S(2)}, u32[]{:S(2)}) collective-permute-start(bf16[64,2048]{1,0:T(8,128)(2,1)S(1)} %add_convert_fusion.3.refs_4_), channel_id=1, source_target_pairs={{0,2},{1,3},{2,0},{3,1},{4,6},{5,7},{6,4},{7,5},{8,10},{9,11},{10,... | collective-permute-start | bytes 786440 | tf_op jit(solution)/shard_map/ppermute | solution.py:618
  117.9 10.7 %collective-permute-start.32 = (bf16[64,2048]{1,0:T(8,128)(2,1)S(1)}, bf16[64,2048]{1,0:T(8,128)(2,1)S(1)}, u32[]{:S(2)}, u32[]{:S(2)}) collective-permute-start(bf16[64,2048]{1,0:T(8,128)(2,1)S(1)} %add_convert_fusion), channel_id=1, source_target_pairs={{0,2},{1,3},{2,0},{3,1},{4,6},{5,7},{6,4},{7,5},{8,10},{9,11},{10,... | collective-permute-start | bytes 786440 | tf_op jit(solution)/shard_map/ppermute | solution.py:618
  118.6 15.7 %collective-permute-start.29 = (bf16[64,2048]{1,0:T(8,128)(2,1)S(1)}, bf16[64,2048]{1,0:T(8,128)(2,1)S(1)}, u32[]{:S(2)}, u32[]{:S(2)}) collective-permute-start(bf16[64,2048]{1,0:T(8,128)(2,1)S(1)} %add_convert_fusion.1), channel_id=1, source_target_pairs={{0,2},{1,3},{2,0},{3,1},{4,6},{5,7},{6,4},{7,5},{8,10},{9,11},{10,... | collective-permute-start | bytes 786440 | tf_op jit(solution)/shard_map/ppermute | solution.py:618
  120.2 18.8 %collective-permute-start.27 = (bf16[64,2048]{1,0:T(8,128)(2,1)S(1)}, bf16[64,2048]{1,0:T(8,128)(2,1)S(1)}, u32[]{:S(2)}, u32[]{:S(2)}) collective-permute-start(bf16[64,2048]{1,0:T(8,128)(2,1)S(1)} %add_convert_fusion.2), channel_id=1, source_target_pairs={{0,2},{1,3},{2,0},{3,1},{4,6},{5,7},{6,4},{7,5},{8,10},{9,11},{10,... | collective-permute-start | bytes 786440 | tf_op jit(solution)/shard_map/ppermute | solution.py:618
  (16 other events, 76.8 us)

commit v10 on v9

--- a/solution.py
+++ b/solution.py
@@ -295,7 +295,7 @@
 
 
 def split_product_kernel(each, half, first, tile, rows_ref, w_ref, *refs):
-    send_ref, other_ref, own_ref = refs[-3:]
+    send_own_ref, send_ref, own_ref, other_ref = refs[-4:]
     for n in range(own_ref.shape[1] // tile):
         total = jnp.dot(
             rows_ref[...],
@@ -303,7 +303,8 @@
             preferred_element_type=jnp.float32,
         )
         columns = slice(n * tile, (n + 1) * tile)
-        send_ref[:, columns] = total[:half].astype(send_ref.dtype)
+        send_own_ref[:, columns] = total[:each].astype(send_own_ref.dtype)
+        send_ref[:, columns] = total[each:half].astype(send_ref.dtype)
         own_ref[:, columns] = total[half : half + each]
         other_ref[:, columns] = total[half + each :]
 
@@ -317,11 +318,12 @@
         functools.partial(split_product_kernel, each, half, part * width, min(512, width)),
         grid=(1,),
         in_specs=[held(), held()] + specs,
-        out_specs=[held()] * 3,
+        out_specs=[held()] * 4,
         out_shape=[
-            pltpu.VMEM((half, width), jnp.bfloat16),
+            pltpu.VMEM((each, width), jnp.bfloat16),
+            pltpu.VMEM((half - each, width), jnp.bfloat16),
+            pltpu.VMEM((each, width), jnp.float32),
             pltpu.VMEM((half - each, width), jnp.float32),
-            pltpu.VMEM((each, width), jnp.float32),
         ],
         compiler_params=SMALL,
         cost_estimate=BRIEF,
@@ -330,12 +332,24 @@
 
 
 def narrow_kernel(index_of, index_ref, tokens_ref, down_ref, cot_ref, up_ref, *refs):
-    send_ref, keep_ref, back_ref, low = refs[-4:]
-    index = index_of(index_ref)
+    send_ref, keep_ref, back_ref, low, tokens, down, cot, up, sems = refs[-9:]
+    index = index_of(index_ref)
+    pairs = [(tokens_ref, tokens), (down_ref, down), (cot_ref, cot)]
+    for i in range(index.per_part):
+        adapter = index.owner(index.block(0, 0, i))
+        pairs.append((up_ref.at[adapter], up.at[i]))
+    copies = [
+        pltpu.make_async_copy(source, target, sems.at[j])
+        for j, (source, target) in enumerate(pairs)
+    ]
+    for copy in copies:
+        copy.start()
+    for copy in copies[:2]:
+        copy.wait()
     for m in range(CAP):
         low[m] = lax.dot_general(
-            down_ref[0],
-            tokens_ref[m * BLK : (m + 1) * BLK],
+            down[0],
+            tokens[m * BLK : (m + 1) * BLK],
             LAST,
             preferred_element_type=jnp.float32,
         )
@@ -345,13 +359,11 @@
                 block = index.block(core_bit, chip_bits, i)
                 mine = index.owner(block) == index.place
                 out_ref[chip_bits, i] = jnp.where(mine, low[index.slot(block)], 0.0)
+    for copy in copies[2:]:
+        copy.wait()
     for i in range(index.per_part):
-        adapter = index.owner(index.block(0, 0, i))
         back_ref[i] = lax.dot_general(
-            up_ref[adapter],
-            cot_ref[i * BLK : (i + 1) * BLK],
-            LAST,
-            preferred_element_type=jnp.float32,
+            up[i], cot[i * BLK : (i + 1) * BLK], LAST, preferred_element_type=jnp.float32
         )
 
 
@@ -359,22 +371,29 @@
     rank = up.shape[1]
     one = (shape.per_part, rank, BLK)
     outs = [(shape.chips,) + one, (shape.chips,) + one, one]
-    operands = (in_vmem(tokens), down, cotangent, up)
+    operands = (tokens, down, cotangent, up)
     specs, extra = after(waits)
     return pl.pallas_call(
         functools.partial(narrow_kernel, index_of),
         grid_spec=pltpu.PrefetchScalarGridSpec(
             num_scalar_prefetch=1,
             grid=(1,),
-            in_specs=[held()] + [whole(o.shape) for o in operands[1:]] + specs,
-            out_specs=[whole(o) for o in outs],
-            scratch_shapes=[pltpu.VMEM((CAP, rank, BLK), jnp.float32)],
+            in_specs=[pl.BlockSpec(memory_space=pl.ANY)] * len(operands) + specs,
+            out_specs=[held()] * len(outs),
+            scratch_shapes=[
+                pltpu.VMEM((CAP, rank, BLK), jnp.float32),
+                pltpu.VMEM(tokens.shape, tokens.dtype),
+                pltpu.VMEM(down.shape, down.dtype),
+                pltpu.VMEM(cotangent.shape, cotangent.dtype),
+                pltpu.VMEM((shape.per_part,) + up.shape[1:], up.dtype),
+                pltpu.SemaphoreType.DMA((3 + shape.per_part,)),
+            ],
         ),
-        out_shape=[shape_of(o, jnp.float32) for o in outs],
+        out_shape=[pltpu.VMEM(o, jnp.float32) for o in outs],
         compiler_params=SMALL,
         cost_estimate=BRIEF,
         name="narrow",
-    )(index, *operands, *extra)
+    )(index, *[in_hbm(o) for o in operands], *extra)
 
 
 def merge_kernel(keep_ref, arrived_ref, back_ref, *refs):
@@ -651,13 +670,8 @@
             total = (total + more[0]) + (more[1] + more[2])
             k *= 4
 
-    def gradients(total, more, waits):
-        lowered, back_rows, pieces = make_pieces(
-            index_of, index, shape, total, more, cotangent, waits
-        )
-        pieces, back_rows = same_core(pieces), same_core(back_rows)
+    def gradients(pieces, back_rows):
         return (
-            lowered,
             up_gradient(index_of, index, adapter_count, with_other_core(pieces)),
             down_gradient(index_of, index, tokens, with_other_core(back_rows)),
         )
@@ -667,11 +681,15 @@
         sent = relay.first()
         send, keep, back = small_products([sent])
         arrived, others = over_parts(send, keep)
-        sent = relay.second(others)
+        total, more = over_dp(merge(keep, arrived, back, others, []))
+        lowered, back_rows, pieces = make_pieces(
+            index_of, index, shape, total, more, cotangent, []
+        )
+        sent = relay.second([lowered])
+        pieces, back_rows = same_core(pieces), same_core(back_rows)
         weight = load_weight(frozen_up_weight, [sent])
-        total, more = over_dp(merge(keep, arrived, back, others, [sent]))
-        relay.settle([weight, *more])
-        lowered, up_grad, down_grad = gradients(total, more, relay.arrived[0][1:3])
+        relay.settle([weight, *pieces[1:], *back_rows[1:]])
+        up_grad, down_grad = gradients(pieces, back_rows)
         ahead = [v for chunk in relay.arrived[1:] for v in chunk[3:5]]
         chunks = [lambda waits: relay.rows(0, ahead, [up_grad, down_grad])]
         chunks += [functools.partial(relay.rows, c) for c in range(1, len(CHUNK_ROWS))]
@@ -680,7 +698,10 @@
         send, keep, back = small_products([])
         arrived, others = over_parts(send, keep)
         total, more = over_dp(merge(keep, arrived, back, others, []))
-        lowered, up_grad, down_grad = gradients(total, more, [])
+        lowered, back_rows, pieces = make_pieces(
+            index_of, index, shape, total, more, cotangent, []
+        )
+        up_grad, down_grad = gradients(same_core(pieces), same_core(back_rows))
         every_slot = lax.all_gather(
             tokens.reshape(CAP, BLK, width_dev), "dp", axis=0, tiled=True
         )
@@ -696,11 +717,10 @@
         ]
     def summed(rows, part, waits):
         each = rows.shape[0] // parts
-        send, other, own = split_product(shape, rows, weight, part, PARTS, waits)
-        arrived = to_other_core(send)
-        outgoing = (other + arrived[each:].astype(jnp.float32)).astype(jnp.bfloat16)
+        send_own, send, own, other = split_product(shape, rows, weight, part, PARTS, waits)
+        outgoing = (other + to_other_core(send).astype(jnp.float32)).astype(jnp.bfloat16)
         across = [to_chip(outgoing[(k - 1) * each : k * each], k) for k in range(1, chips)]
-        return [own, arrived] + across, outgoing
+        return [own, to_other_core(send_own)] + across, outgoing
 
     sums, rows, waits = [], [], []
     for chunk in chunks:
@@ -708,8 +728,10 @@
         sums.append([summed(rows[-1], 0, ())])
         waits = [sums[-1][0][1]]
     for part in range(1, PARTS):
+        waits = rows[-1:]
         for chunk_rows, done in zip(rows, sums):
-            done.append(summed(chunk_rows, part, rows[-1:]))
+            done.append(summed(chunk_rows, part, waits))
+            waits = [*sums[0][part - 1][0][2:], sums[-1][part - 1][1]]
     projected = None
     for part in range(PARTS):
         projected = finish(

time: 142 us -> 126 us (0.89)
  waiting for transfers between devices: 64.6 us -> 51 us
  local copies, waits for them, and re-layouts: 5.95 us -> 0.87 us
  starting transfers between devices: 37.5 us -> 39.4 us
  Pallas kernels: 31.9 us -> 33.6 us
    ppermute x7, waiting for transfers between devices: 27.7 us -> 17 us  [to_chip(): lax.ppermute(value, 'tensor', [(i, i ^ k * CORES) for i in range(parts)])]
    unnamed x14 -> x6, local copies, waits for them, and re-layouts: 5.19 us -> 0.02 us
    ppermute x2, waiting for transfers between devices: 8.45 us -> 3.94 us  [spread(): outer_2 = lax.ppermute(inner, 'dp', [(1, 0), (2, 3)])]
    ppermute x1, waiting for transfers between devices: 0.01 us -> 3.55 us  [second(): lax.ppermute(outer, 'dp', [(1, 0), (0, 1), (3, 2)])]
    ppermute x3, waiting for transfers between devices: 7.96 us -> 5.48 us  [across_dp(): return lax.ppermute(value, 'dp', [(i, i ^ k) for i in range(owners)])]
    ppermute x7, starting transfers between devices: 8.85 us -> 6.81 us  [to_chip(): lax.ppermute(value, 'tensor', [(i, i ^ k * CORES) for i in range(parts)])]
    pallas_call x1, Pallas kernels: 1.57 us -> 3.52 us  [narrow(): pl.pallas_call(functools.partial(narrow_kernel, index_of), grid_spec=pltp...]
    ppermute x2, starting transfers between devices: 4.7 us -> 6.64 us  [spread(): outer = lax.ppermute(home, 'dp', [(0, 1), (1, 0), (2, 3), (3, 2)])]
  transfers between devices with their start and end apart: 33 -> 37, of which waited for: 16 -> 16; matrix products, arithmetic and copies ran while one was open for 0% -> 0% of each run, Pallas kernels for 14% -> 19%
where the time goes in v10:
time: 126 us
  waiting for transfers between devices  51 us (40%)
  starting transfers between devices  39.4 us (31%)
  Pallas kernels  33.6 us (27%)
    ppermute x7, waiting for transfers between devices, to_chip(): lax.ppermute(value, 'tensor', [(i, i ^ k * CORES) for i in range(parts)])  17 us
    ppermute x2, waiting for transfers between devices, spread(): outer_3 = lax.ppermute(inner_2, 'dp', [(1, 0), (2, 3)])  14.4 us
    pallas_call x4, Pallas kernels, split_product(): pl.pallas_call(functools.partial(split_product_kernel, each, half, part *...  9.3 us
    ppermute x7, starting transfers between devices, to_chip(): lax.ppermute(value, 'tensor', [(i, i ^ k * CORES) for i in range(parts)])  6.81 us
    ppermute x2, starting transfers between devices, spread(): outer = lax.ppermute(home, 'dp', [(0, 1), (1, 0), (2, 3), (3, 2)])  6.64 us
    pallas_call x1, Pallas kernels, load_weight(): pl.pallas_call(load_weight_kernel, grid=(1,), in_specs=[pl.BlockSpec(memo...  5.89 us
    ppermute x1, starting transfers between devices, first(): lax.ppermute(inward, 'dp', [(3, 2), (0, 1)])  5.56 us
    ppermute x3, waiting for transfers between devices, across_dp(): return lax.ppermute(value, 'dp', [(i, i ^ k) for i in range(owners)])  5.48 us
  transfers between devices with their start and end apart: 37, of which 16 were waited for; matrix products, arithmetic and copies ran while one was open for 0% of the time, Pallas kernels for 19%

profile of v10, /device:TPU:0, one launch (start us, length us, event | category | flops | bytes accessed | tf_op | source)
XLA Modules:
  0.0 126.1 jit_solution(5787552725052052571)
XLA Ops:
  1.5 1.8 %first_hop.1 = (bf16[128,2048]{1,0:T(8,128)(2,1)S(1)}, bf16[128,2048]{1,0:T(8,128)(2,1)S(1)}) custom-call(s32[14]{0:T(128)S(1)} %concatenate.3.index_ref.refs_0_, bf16[384,2048]{1,0:T(8,128)(2,1)} %tokens_ref.9), custom_call_target="tpu_custom_call" | custom-call | flops 1 | bytes 1 | tf_op jit(solution)/shard_map/first_hop/pallas_call | solution.py:191
  4.0 5.6 %collective-permute-start.5 = (bf16[128,2048]{1,0:T(8,128)(2,1)S(1)}, bf16[128,2048]{1,0:T(8,128)(2,1)S(1)}, u32[]{:S(2)}, u32[]{:S(2)}) collective-permute-start(bf16[128,2048]{1,0:T(8,128)(2,1)S(1)} %get-tuple-element.31.refs_0_), channel_id=1, source_target_pairs={{12,8},{0,4},{13,9},{1,5},{14,10},{2,6},{15,11},{3,7},{28,24},{16,... | collective-permute-start | bytes 1572872 | tf_op jit(solution)/shard_map/ppermute | solution.py:220
  9.5 3.5 %narrow.1 = (f32[2,1,64,128]{3,2,1,0:T(8,128)S(1)}, f32[2,1,64,128]{3,2,1,0:T(8,128)S(1)}, f32[1,64,128]{2,1,0:T(8,128)S(1)}) custom-call(s32[14]{0:T(128)S(1)} %concatenate.3.index_ref.refs_0_, bf16[384,2048]{1,0:T(8,128)(2,1)} %tokens_ref.9, bf16[1,64,2048]{2,1,0:T(8,128)(2,1)} %bitcast.7, bf16[128,4096]{1,0:T(8,128)(2,1)} %cot_ref.3, ...), custom_call_target="tpu_custom_call" | custom-call | flops 1 | bytes 1 | tf_op jit(solution)/shard_map/narrow/pallas_call | solution.py:376
  15.9 2.4 %collective-permute-done.1.refs_0_ = f32[1,64,128]{2,1,0:T(8,128)S(1)} collective-permute-done((f32[1,64,128]{2,1,0:T(8,128)S(1)}, f32[1,64,128]{2,1,0:T(8,128)S(1)}, u32[]{:S(2)}, u32[]{:S(2)}) %collective-permute-start.1) | collective-permute-done | bytes 32800 | tf_op jit(solution)/shard_map/ppermute | solution.py:637
  18.3 3.6 %collective-permute-start.4 = (f32[2,1,64,128]{3,2,1,0:T(8,128)S(1)}, f32[2,1,64,128]{3,2,1,0:T(8,128)S(1)}, u32[]{:S(2)}, u32[]{:S(2)}) collective-permute-start(f32[2,1,64,128]{3,2,1,0:T(8,128)S(1)} %merge.1.sum_ref), channel_id=1, source_target_pairs={{0,12},{4,8},{8,4},{12,0},{1,13},{5,9},{9,5},{13,1},{2,14},{6,10},... | collective-permute-start | bytes 196616 | tf_op jit(solution)/shard_map/ppermute | solution.py:640
  22.8 4.6 %collective-permute-done.4.refs_2_ = f32[2,1,64,128]{3,2,1,0:T(8,128)S(1)} collective-permute-done((f32[2,1,64,128]{3,2,1,0:T(8,128)S(1)}, f32[2,1,64,128]{3,2,1,0:T(8,128)S(1)}, u32[]{:S(2)}, u32[]{:S(2)}) %collective-permute-start.4) | collective-permute-done | bytes 65568 | tf_op jit(solution)/shard_map/ppermute | solution.py:640
  32.0 4.6 %collective-permute-start.7 = (bf16[128,2048]{1,0:T(8,128)(2,1)S(1)}, bf16[128,2048]{1,0:T(8,128)(2,1)S(1)}, u32[]{:S(2)}, u32[]{:S(2)}) collective-permute-start(bf16[128,2048]{1,0:T(8,128)(2,1)S(1)} %get-tuple-element.37.refs_0_), channel_id=1, source_target_pairs={{4,0},{0,4},{12,8},{5,1},{1,5},{13,9},{6,2},{2,6},{14,10},{7,3},{3... | collective-permute-start | bytes 1572872 | tf_op jit(solution)/shard_map/ppermute | solution.py:230
  37.4 5.9 %load_weight.1.refs_0_.w_ref = bf16[2048,4096]{1,0:T(8,128)(2,1)S(1)} custom-call(bf16[2048,4096]{1,0:T(8,128)(2,1)} %w_ref.1, bf16[128,2048]{1,0:T(8,128)(2,1)S(1)} %get-tuple-element.37.refs_0_), custom_call_target="tpu_custom_call" | custom-call | flops 1 | bytes 1 | tf_op jit(solution)/shard_map/load_weight/pallas_call | solution.py:284
  43.3 3.6 %collective-permute-done.7.x_ref = bf16[128,2048]{1,0:T(8,128)(2,1)S(1)} collective-permute-done((bf16[128,2048]{1,0:T(8,128)(2,1)S(1)}, bf16[128,2048]{1,0:T(8,128)(2,1)S(1)}, u32[]{:S(2)}, u32[]{:S(2)}) %collective-permute-start.7) | collective-permute-done | bytes 524320 | tf_op jit(solution)/shard_map/ppermute | solution.py:230
  51.8 4.9 %collective-permute-start.16 = (bf16[64,2048]{1,0:T(8,128)(2,1)S(1)}, bf16[64,2048]{1,0:T(8,128)(2,1)S(1)}, u32[]{:S(2)}, u32[]{:S(2)}) collective-permute-start(bf16[64,2048]{1,0:T(8,128)(2,1)S(1)} %get-tuple-element.42.home_ref), channel_id=1, source_target_pairs={{0,4},{4,0},{8,12},{12,8},{1,5},{5,1},{9,13},{13,9},{2,6},{6,2},{1... | collective-permute-start | bytes 786440 | tf_op jit(solution)/shard_map/ppermute | solution.py:240
  60.0 3.0 %collective-permute-done.16.outer_ref = bf16[64,2048]{1,0:T(8,128)(2,1)S(1)} collective-permute-done((bf16[64,2048]{1,0:T(8,128)(2,1)S(1)}, bf16[64,2048]{1,0:T(8,128)(2,1)S(1)}, u32[]{:S(2)}, u32[]{:S(2)}) %collective-permute-start.16) | collective-permute-done | bytes 262176 | tf_op jit(solution)/shard_map/ppermute | solution.py:240
  66.4 3.9 %up_gradient.1.refs_6_ = f32[4,64,4096]{2,1,0:T(8,128)} custom-call(s32[14]{0:T(128)S(1)} %concatenate.3.index_ref.refs_0_, bf16[1,64,4096]{2,1,0:T(8,128)(2,1)S(1)} %get-tuple-element.39.refs_0_, bf16[1,64,4096]{2,1,0:T(8,128)(2,1)S(1)} %collective-permute-done.9.refs_1_, bf16[1,64,4096]{2,1,0:T(8,128)(2,1)S(1)} %collective-permute-done.20.refs_2_, ...), custom_call_target="tpu_custom_call" | custom-call | flops 1 | bytes 1 | tf_op jit(solution)/shard_map/up_gradient/pallas_call | solution.py:526
  70.3 3.9 %collective-permute-done.19.refs_5_.refs_2_ = bf16[64,2048]{1,0:T(8,128)(2,1)S(1)} collective-permute-done((bf16[64,2048]{1,0:T(8,128)(2,1)S(1)}, bf16[64,2048]{1,0:T(8,128)(2,1)S(1)}, u32[]{:S(2)}, u32[]{:S(2)}) %collective-permute-start.19) | collective-permute-done | bytes 262176 | tf_op jit(solution)/shard_map/ppermute | solution.py:242
  74.2 5.4 %collective-permute-done.15.refs_3_ = bf16[64,2048]{1,0:T(8,128)(2,1)S(1)} collective-permute-done((bf16[64,2048]{1,0:T(8,128)(2,1)S(1)}, bf16[64,2048]{1,0:T(8,128)(2,1)S(1)}, u32[]{:S(2)}, u32[]{:S(2)}) %collective-permute-start.15) | collective-permute-done | bytes 262176 | tf_op jit(solution)/shard_map/ppermute | solution.py:244
  80.3 2.3 %split_product.4 = (bf16[64,2048]{1,0:T(8,128)(2,1)S(1)}, bf16[64,2048]{1,0:T(8,128)(2,1)S(1)}, f32[64,2048]{1,0:T(8,128)S(1)}, f32[64,2048]{1,0:T(8,128)S(1)}) custom-call(bf16[256,2048]{1,0:T(8,128)(2,1)S(1)} %collect.2.rows_ref, bf16[2048,4096]{1,0:T(8,128)(2,1)S(1)} %load_weight.1.refs_0_.w_ref), custom_call_target="tpu_custom_call" | custom-call | flops 1 | bytes 1 | tf_op jit(solution)/shard_map/split_product/pallas_call | solution.py:317
  84.3 9.0 %collective-permute-done.24.refs_3_ = bf16[64,2048]{1,0:T(8,128)(2,1)S(1)} collective-permute-done((bf16[64,2048]{1,0:T(8,128)(2,1)S(1)}, bf16[64,2048]{1,0:T(8,128)(2,1)S(1)}, u32[]{:S(2)}, u32[]{:S(2)}) %collective-permute-start.24) | collective-permute-done | bytes 262176 | tf_op jit(solution)/shard_map/ppermute | solution.py:244
  94.1 2.3 %split_product.6 = (bf16[64,2048]{1,0:T(8,128)(2,1)S(1)}, bf16[64,2048]{1,0:T(8,128)(2,1)S(1)}, f32[64,2048]{1,0:T(8,128)S(1)}, f32[64,2048]{1,0:T(8,128)S(1)}) custom-call(bf16[256,2048]{1,0:T(8,128)(2,1)S(1)} %collect.3.refs_0_.rows_ref, bf16[2048,4096]{1,0:T(8,128)(2,1)S(1)} %load_weight.1.refs_0_.w_ref), custom_call_target="tpu_custom_call" | custom-call | flops 1 | bytes 1 | tf_op jit(solution)/shard_map/split_product/pallas_call | solution.py:317
  97.5 2.3 %split_product.5 = (bf16[64,2048]{1,0:T(8,128)(2,1)S(1)}, bf16[64,2048]{1,0:T(8,128)(2,1)S(1)}, f32[64,2048]{1,0:T(8,128)S(1)}, f32[64,2048]{1,0:T(8,128)S(1)}) custom-call(bf16[256,2048]{1,0:T(8,128)(2,1)S(1)} %collect.2.rows_ref, bf16[2048,4096]{1,0:T(8,128)(2,1)S(1)} %load_weight.1.refs_0_.w_ref, bf16[256,2048]{1,0:T(8,128)(2,1)S(1)} %collect.3.refs_0_.rows_ref), custom_call_target="tpu_custom_call" | custom-call | flops 1 | bytes 1 | tf_op jit(solution)/shard_map/split_product/pallas_call | solution.py:317
  100.6 4.7 %collective-permute-done.29.refs_0_.refs_5_ = bf16[64,2048]{1,0:T(8,128)(2,1)S(1)} collective-permute-done((bf16[64,2048]{1,0:T(8,128)(2,1)S(1)}, bf16[64,2048]{1,0:T(8,128)(2,1)S(1)}, u32[]{:S(2)}, u32[]{:S(2)}) %collective-permute-start.29) | collective-permute-done | bytes 262176 | tf_op jit(solution)/shard_map/ppermute | solution.py:637
  105.8 2.3 %split_product.7 = (bf16[64,2048]{1,0:T(8,128)(2,1)S(1)}, bf16[64,2048]{1,0:T(8,128)(2,1)S(1)}, f32[64,2048]{1,0:T(8,128)S(1)}, f32[64,2048]{1,0:T(8,128)S(1)}) custom-call(bf16[256,2048]{1,0:T(8,128)(2,1)S(1)} %collect.3.refs_0_.rows_ref, bf16[2048,4096]{1,0:T(8,128)(2,1)S(1)} %load_weight.1.refs_0_.w_ref, ...), custom_call_target="tpu_custom_call" | custom-call | flops 1 | bytes 1 | tf_op jit(solution)/shard_map/split_product/pallas_call | solution.py:317
  112.9 2.1 %finish.2.refs_9_ = bf16[128,4096]{1,0:T(8,128)(2,1)} custom-call(s32[14]{0:T(128)S(1)} %concatenate.3.index_ref.refs_0_, bf16[1,64,128]{2,1,0:T(8,128)(2,1)S(1)} %get-tuple-element.35.refs_0_.refs_1_, bf16[4,64,4096]{2,1,0:T(8,128)(2,1)S(1)} %copy-done.1, f32[64,2048]{1,0:T(8,128)S(1)} %get-tuple-element.55.refs_3_, ...), custom_call_target="tpu_custom_call" | custom-call | flops 1 | bytes 1 | tf_op jit(solution)/shard_map/finish/pallas_call | solution.py:595
  115.0 3.9 %collective-permute-done.28.refs_5_ = bf16[64,2048]{1,0:T(8,128)(2,1)S(1)} collective-permute-done((bf16[64,2048]{1,0:T(8,128)(2,1)S(1)}, bf16[64,2048]{1,0:T(8,128)(2,1)S(1)}, u32[]{:S(2)}, u32[]{:S(2)}) %collective-permute-start.28) | collective-permute-done | bytes 262176 | tf_op jit(solution)/shard_map/ppermute | solution.py:637
  118.9 5.1 %collective-permute-done.33.refs_8_ = bf16[64,2048]{1,0:T(8,128)(2,1)S(1)} collective-permute-done((bf16[64,2048]{1,0:T(8,128)(2,1)S(1)}, bf16[64,2048]{1,0:T(8,128)(2,1)S(1)}, u32[]{:S(2)}, u32[]{:S(2)}) %collective-permute-start.33) | collective-permute-done | bytes 262176 | tf_op jit(solution)/shard_map/ppermute | solution.py:637
  124.0 2.1 %finish.3 = bf16[128,4096]{1,0:T(8,128)(2,1)} custom-call(s32[14]{0:T(128)S(1)} %concatenate.3.index_ref.refs_0_, bf16[1,64,128]{2,1,0:T(8,128)(2,1)S(1)} %get-tuple-element.35.refs_0_.refs_1_, bf16[4,64,4096]{2,1,0:T(8,128)(2,1)S(1)} %copy-done.1, f32[64,2048]{1,0:T(8,128)S(1)} %get-tuple-element.45.refs_3_, ...), custom_call_target="tpu_custom_call", output_to_operand_aliasing={{}: (9, {})} | custom-call | flops 1 | bytes 1 | tf_op jit(solution)/shard_map/finish/pallas_call | solution.py:595
  (79 shorter events, 32.2 us)
Async XLA Ops:
  3.3 27.4 %collective-permute-start.6 = (bf16[128,2048]{1,0:T(8,128)(2,1)S(1)}, bf16[128,2048]{1,0:T(8,128)(2,1)S(1)}, u32[]{:S(2)}, u32[]{:S(2)}) collective-permute-start(bf16[128,2048]{1,0:T(8,128)(2,1)S(1)} %get-tuple-element.36), channel_id=1, source_target_pairs={{8,4},{9,5},{10,6},{11,7},{24,20},{25,21},{26,22},{27,23}} | collective-permute-start | bytes 1572872 | tf_op jit(solution)/shard_map/ppermute | solution.py:221
  4.0 26.7 %collective-permute-start.5 = (bf16[128,2048]{1,0:T(8,128)(2,1)S(1)}, bf16[128,2048]{1,0:T(8,128)(2,1)S(1)}, u32[]{:S(2)}, u32[]{:S(2)}) collective-permute-start(bf16[128,2048]{1,0:T(8,128)(2,1)S(1)} %get-tuple-element.31.refs_0_), channel_id=1, source_target_pairs={{12,8},{0,4},{13,9},{1,5},{14,10},{2,6},{15,11},{3,7},{28,24},{16,... | collective-permute-start | bytes 1572872 | tf_op jit(solution)/shard_map/ppermute | solution.py:220
  18.3 9.1 %collective-permute-start.4 = (f32[2,1,64,128]{3,2,1,0:T(8,128)S(1)}, f32[2,1,64,128]{3,2,1,0:T(8,128)S(1)}, u32[]{:S(2)}, u32[]{:S(2)}) collective-permute-start(f32[2,1,64,128]{3,2,1,0:T(8,128)S(1)} %merge.1.sum_ref), channel_id=1, source_target_pairs={{0,12},{4,8},{8,4},{12,0},{1,13},{5,9},{9,5},{13,1},{2,14},{6,10},... | collective-permute-start | bytes 196616 | tf_op jit(solution)/shard_map/ppermute | solution.py:640
  29.1 14.1 %collective-permute-start.9 = (bf16[1,64,4096]{2,1,0:T(8,128)(2,1)S(1)}, bf16[1,64,4096]{2,1,0:T(8,128)(2,1)S(1)}, u32[]{:S(2)}, u32[]{:S(2)}) collective-permute-start(bf16[1,64,4096]{2,1,0:T(8,128)(2,1)S(1)} %get-tuple-element.39.refs_0_), channel_id=1, source_target_pairs={{0,2},{1,3},{2,0},{3,1},{4,6},{5,7},{6,4},{7,5},{8,10},{9,11},{10,... | collective-permute-start | bytes 1572872 | tf_op jit(solution)/shard_map/ppermute | solution.py:637
  31.3 11.9 %collective-permute-start.8 = (bf16[128,2048]{1,0:T(8,128)(2,1)S(1)}, bf16[128,2048]{1,0:T(8,128)(2,1)S(1)}, u32[]{:S(2)}, u32[]{:S(2)}) collective-permute-start(bf16[128,2048]{1,0:T(8,128)(2,1)S(1)} %get-tuple-element.38), channel_id=1, source_target_pairs={{8,4},{4,8},{9,5},{5,9},{10,6},{6,10},{11,7},{7,11},{24,20},{20,24... | collective-permute-start | bytes 1572872 | tf_op jit(solution)/shard_map/ppermute | solution.py:231
  32.0 14.8 %collective-permute-start.7 = (bf16[128,2048]{1,0:T(8,128)(2,1)S(1)}, bf16[128,2048]{1,0:T(8,128)(2,1)S(1)}, u32[]{:S(2)}, u32[]{:S(2)}) collective-permute-start(bf16[128,2048]{1,0:T(8,128)(2,1)S(1)} %get-tuple-element.37.refs_0_), channel_id=1, source_target_pairs={{4,0},{0,4},{12,8},{5,1},{1,5},{13,9},{6,2},{2,6},{14,10},{7,3},{3... | collective-permute-start | bytes 1572872 | tf_op jit(solution)/shard_map/ppermute | solution.py:230
  36.7 15.1 %collective-permute-start.20 = (bf16[1,64,4096]{2,1,0:T(8,128)(2,1)S(1)}, bf16[1,64,4096]{2,1,0:T(8,128)(2,1)S(1)}, u32[]{:S(2)}, u32[]{:S(2)}) collective-permute-start(bf16[1,64,4096]{2,1,0:T(8,128)(2,1)S(1)} %get-tuple-element.39.refs_0_), channel_id=1, source_target_pairs={{0,1},{1,0},{2,3},{3,2},{4,5},{5,4},{6,7},{7,6},{8,9},{9,8},{10,11... | collective-permute-start | bytes 1572872 | tf_op jit(solution)/shard_map/ppermute | solution.py:634
  47.5 9.2 %collective-permute-start.11 = (bf16[64,2048]{1,0:T(8,128)(2,1)S(1)}, bf16[64,2048]{1,0:T(8,128)(2,1)S(1)}, u32[]{:S(2)}, u32[]{:S(2)}) collective-permute-start(bf16[64,2048]{1,0:T(8,128)(2,1)S(1)} %get-tuple-element.41.home_ref), channel_id=1, source_target_pairs={{0,4},{4,0},{8,12},{12,8},{1,5},{5,1},{9,13},{13,9},{2,6},{6,2},{1... | collective-permute-start | bytes 786440 | tf_op jit(solution)/shard_map/ppermute | solution.py:240
  49.8 16.6 %collective-permute-start.21 = (bf16[1,64,4096]{2,1,0:T(8,128)(2,1)S(1)}, bf16[1,64,4096]{2,1,0:T(8,128)(2,1)S(1)}, u32[]{:S(2)}, u32[]{:S(2)}) collective-permute-start(bf16[1,64,4096]{2,1,0:T(8,128)(2,1)S(1)} %collective-permute-done.9.refs_1_), channel_id=1, source_target_pairs={{0,1},{1,0},{2,3},{3,2},{4,5},{5,4},{6,7},{7,6},{8,9},{9,8},{10,11... | collective-permute-start | bytes 1572872 | tf_op jit(solution)/shard_map/ppermute | solution.py:634
  51.8 11.2 %collective-permute-start.16 = (bf16[64,2048]{1,0:T(8,128)(2,1)S(1)}, bf16[64,2048]{1,0:T(8,128)(2,1)S(1)}, u32[]{:S(2)}, u32[]{:S(2)}) collective-permute-start(bf16[64,2048]{1,0:T(8,128)(2,1)S(1)} %get-tuple-element.42.home_ref), channel_id=1, source_target_pairs={{0,4},{4,0},{8,12},{12,8},{1,5},{5,1},{9,13},{13,9},{2,6},{6,2},{1... | collective-permute-start | bytes 786440 | tf_op jit(solution)/shard_map/ppermute | solution.py:240
  57.4 12.9 %collective-permute-start.14 = (bf16[64,2048]{1,0:T(8,128)(2,1)S(1)}, bf16[64,2048]{1,0:T(8,128)(2,1)S(1)}, u32[]{:S(2)}, u32[]{:S(2)}) collective-permute-start(bf16[64,2048]{1,0:T(8,128)(2,1)S(1)} %collective-permute-done.12.refs_0_), channel_id=1, source_target_pairs={{4,0},{8,12},{5,1},{9,13},{6,2},{10,14},{7,3},{11,15},{20,16},{24,... | collective-permute-start | bytes 786440 | tf_op jit(solution)/shard_map/ppermute | solution.py:242
  58.7 15.5 %collective-permute-start.19 = (bf16[64,2048]{1,0:T(8,128)(2,1)S(1)}, bf16[64,2048]{1,0:T(8,128)(2,1)S(1)}, u32[]{:S(2)}, u32[]{:S(2)}) collective-permute-start(bf16[64,2048]{1,0:T(8,128)(2,1)S(1)} %collective-permute-done.18.refs_0_), channel_id=1, source_target_pairs={{4,0},{8,12},{5,1},{9,13},{6,2},{10,14},{7,3},{11,15},{20,16},{24,... | collective-permute-start | bytes 786440 | tf_op jit(solution)/shard_map/ppermute | solution.py:242
  63.0 11.2 %collective-permute-start.17 = (bf16[64,2048]{1,0:T(8,128)(2,1)S(1)}, bf16[64,2048]{1,0:T(8,128)(2,1)S(1)}, u32[]{:S(2)}, u32[]{:S(2)}) collective-permute-start(bf16[64,2048]{1,0:T(8,128)(2,1)S(1)} %collective-permute-done.16.outer_ref), channel_id=1, source_target_pairs={{4,8},{8,4},{5,9},{9,5},{6,10},{10,6},{7,11},{11,7},{20,24},{24,20... | collective-permute-start | bytes 786440 | tf_op jit(solution)/shard_map/ppermute | solution.py:243
  63.7 15.9 %collective-permute-start.15 = (bf16[64,2048]{1,0:T(8,128)(2,1)S(1)}, bf16[64,2048]{1,0:T(8,128)(2,1)S(1)}, u32[]{:S(2)}, u32[]{:S(2)}) collective-permute-start(bf16[64,2048]{1,0:T(8,128)(2,1)S(1)} %collective-permute-done.13.refs_1_), channel_id=1, source_target_pairs={{4,0},{8,12},{5,1},{9,13},{6,2},{10,14},{7,3},{11,15},{20,16},{24,... | collective-permute-start | bytes 786440 | tf_op jit(solution)/shard_map/ppermute | solution.py:244
  82.7 10.6 %collective-permute-start.24 = (bf16[64,2048]{1,0:T(8,128)(2,1)S(1)}, bf16[64,2048]{1,0:T(8,128)(2,1)S(1)}, u32[]{:S(2)}, u32[]{:S(2)}) collective-permute-start(bf16[64,2048]{1,0:T(8,128)(2,1)S(1)} %collective-permute-done.17.refs_4_.refs_1_), channel_id=1, source_target_pairs={{4,0},{8,12},{5,1},{9,13},{6,2},{10,14},{7,3},{11,15},{20,16},{24,... | collective-permute-start | bytes 786440 | tf_op jit(solution)/shard_map/ppermute | solution.py:244
  96.5 14.8 %collective-permute-start.34 = (bf16[64,2048]{1,0:T(8,128)(2,1)S(1)}, bf16[64,2048]{1,0:T(8,128)(2,1)S(1)}, u32[]{:S(2)}, u32[]{:S(2)}) collective-permute-start(bf16[64,2048]{1,0:T(8,128)(2,1)S(1)} %get-tuple-element.56), channel_id=1, source_target_pairs={{0,1},{1,0},{2,3},{3,2},{4,5},{5,4},{6,7},{7,6},{8,9},{9,8},{10,11... | collective-permute-start | bytes 786440 | tf_op jit(solution)/shard_map/ppermute | solution.py:634
  97.0 8.3 %collective-permute-start.29 = (bf16[64,2048]{1,0:T(8,128)(2,1)S(1)}, bf16[64,2048]{1,0:T(8,128)(2,1)S(1)}, u32[]{:S(2)}, u32[]{:S(2)}) collective-permute-start(bf16[64,2048]{1,0:T(8,128)(2,1)S(1)} %add_convert_fusion.3.refs_4_), channel_id=1, source_target_pairs={{0,2},{1,3},{2,0},{3,1},{4,6},{5,7},{6,4},{7,5},{8,10},{9,11},{10,... | collective-permute-start | bytes 786440 | tf_op jit(solution)/shard_map/ppermute | solution.py:637
  99.9 15.2 %collective-permute-start.26 = (bf16[64,2048]{1,0:T(8,128)(2,1)S(1)}, bf16[64,2048]{1,0:T(8,128)(2,1)S(1)}, u32[]{:S(2)}, u32[]{:S(2)}) collective-permute-start(bf16[64,2048]{1,0:T(8,128)(2,1)S(1)} %get-tuple-element.46), channel_id=1, source_target_pairs={{0,1},{1,0},{2,3},{3,2},{4,5},{5,4},{6,7},{7,6},{8,9},{9,8},{10,11... | collective-permute-start | bytes 786440 | tf_op jit(solution)/shard_map/ppermute | solution.py:634
  99.9 8.2 %collective-permute-start.27 = (bf16[64,2048]{1,0:T(8,128)(2,1)S(1)}, bf16[64,2048]{1,0:T(8,128)(2,1)S(1)}, u32[]{:S(2)}, u32[]{:S(2)}) collective-permute-start(bf16[64,2048]{1,0:T(8,128)(2,1)S(1)} %get-tuple-element.48), channel_id=1, source_target_pairs={{0,1},{1,0},{2,3},{3,2},{4,5},{5,4},{6,7},{7,6},{8,9},{9,8},{10,11... | collective-permute-start | bytes 786440 | tf_op jit(solution)/shard_map/ppermute | solution.py:634
  100.4 11.0 %collective-permute-start.35 = (bf16[64,2048]{1,0:T(8,128)(2,1)S(1)}, bf16[64,2048]{1,0:T(8,128)(2,1)S(1)}, u32[]{:S(2)}, u32[]{:S(2)}) collective-permute-start(bf16[64,2048]{1,0:T(8,128)(2,1)S(1)} %get-tuple-element.58), channel_id=1, source_target_pairs={{0,1},{1,0},{2,3},{3,2},{4,5},{5,4},{6,7},{7,6},{8,9},{9,8},{10,11... | collective-permute-start | bytes 786440 | tf_op jit(solution)/shard_map/ppermute | solution.py:634
  105.3 7.6 %collective-permute-start.36 = (bf16[64,2048]{1,0:T(8,128)(2,1)S(1)}, bf16[64,2048]{1,0:T(8,128)(2,1)S(1)}, u32[]{:S(2)}, u32[]{:S(2)}) collective-permute-start(bf16[64,2048]{1,0:T(8,128)(2,1)S(1)} %add_convert_fusion.1.refs_1_), channel_id=1, source_target_pairs={{0,2},{1,3},{2,0},{3,1},{4,6},{5,7},{6,4},{7,5},{8,10},{9,11},{10,... | collective-permute-start | bytes 786440 | tf_op jit(solution)/shard_map/ppermute | solution.py:637
  109.8 9.2 %collective-permute-start.28 = (bf16[64,2048]{1,0:T(8,128)(2,1)S(1)}, bf16[64,2048]{1,0:T(8,128)(2,1)S(1)}, u32[]{:S(2)}, u32[]{:S(2)}) collective-permute-start(bf16[64,2048]{1,0:T(8,128)(2,1)S(1)} %add_convert_fusion.2), channel_id=1, source_target_pairs={{0,2},{1,3},{2,0},{3,1},{4,6},{5,7},{6,4},{7,5},{8,10},{9,11},{10,... | collective-permute-start | bytes 786440 | tf_op jit(solution)/shard_map/ppermute | solution.py:637
  111.3 7.6 %collective-permute-start.31 = (bf16[64,2048]{1,0:T(8,128)(2,1)S(1)}, bf16[64,2048]{1,0:T(8,128)(2,1)S(1)}, u32[]{:S(2)}, u32[]{:S(2)}) collective-permute-start(bf16[64,2048]{1,0:T(8,128)(2,1)S(1)} %get-tuple-element.52), channel_id=1, source_target_pairs={{0,1},{1,0},{2,3},{3,2},{4,5},{5,4},{6,7},{7,6},{8,9},{9,8},{10,11... | collective-permute-start | bytes 786440 | tf_op jit(solution)/shard_map/ppermute | solution.py:634
  111.4 12.6 %collective-permute-start.33 = (bf16[64,2048]{1,0:T(8,128)(2,1)S(1)}, bf16[64,2048]{1,0:T(8,128)(2,1)S(1)}, u32[]{:S(2)}, u32[]{:S(2)}) collective-permute-start(bf16[64,2048]{1,0:T(8,128)(2,1)S(1)} %add_convert_fusion), channel_id=1, source_target_pairs={{0,2},{1,3},{2,0},{3,1},{4,6},{5,7},{6,4},{7,5},{8,10},{9,11},{10,... | collective-permute-start | bytes 786440 | tf_op jit(solution)/shard_map/ppermute | solution.py:637
  (16 other events, 125.2 us)

commit v11 on v10

--- a/solution.py
+++ b/solution.py
@@ -10,8 +10,9 @@
 BLK = 128
 CAP = 3
 CORES = 2
-CHUNK_ROWS = (64, 64)
-PARTS = 2
+STREAM_ROWS = (64, 64)
+PARTS = 4
+WRITES = 2
 SMALL = pltpu.CompilerParams(vmem_limit_bytes=12 * 2**20)
 
 adapter_scale = 0.5
@@ -131,7 +132,7 @@
 
 
 def settle_kernel(index_of, index_ref, tokens_ref, x_ref, y_ref, *refs):
-    out_refs = refs[-len(CHUNK_ROWS) :]
+    out_refs = refs[-len(STREAM_ROWS) :]
     index = index_of(index_ref)
     place = index.place
     owner = index.owner(place)
@@ -153,28 +154,33 @@
         start += out_ref.shape[0]
 
 
-def collect_kernel(index_of, count, index_ref, home_ref, outer_ref, *refs):
-    inner_refs, outer_refs, out_ref = refs[:2], refs[2:4], refs[-1]
+def collect_kernel(index_of, index_ref, *refs):
+    out_ref = refs[-1]
     index = index_of(index_ref)
     place = index.place
-
-    def put(block, ref):
-        at = pl.multiple_of(index.position(block) * count, 16)
-        out_ref[pl.ds(at, count)] = ref[...]
-
-    put(place, home_ref)
-    put(place ^ 1, outer_ref)
     middle = (place == 1) | (place == 2)
-
-    @pl.when(middle)
-    def _():
-        put(3 - place, inner_refs[0])
-        put(place ^ 2, inner_refs[1])
-
-    @pl.when(jnp.logical_not(middle))
-    def _():
-        put(place ^ 2, outer_refs[0])
-        put(3 - place, outer_refs[1])
+    start = 0
+    for stream, count in enumerate(STREAM_ROWS):
+        home, outer, inner, inner_2, outer_2, outer_3 = refs[6 * stream : 6 * stream + 6]
+
+        def put(block, ref, start=start, count=count):
+            at = pl.multiple_of(index.position(block) * BLK + start, 16)
+            out_ref[pl.ds(at, count)] = ref[...]
+
+        put(place, home)
+        put(place ^ 1, outer)
+
+        @pl.when(middle)
+        def _(put=put, inner=inner, inner_2=inner_2):
+            put(3 - place, inner)
+            put(place ^ 2, inner_2)
+
+        @pl.when(jnp.logical_not(middle))
+        def _(put=put, outer_2=outer_2, outer_3=outer_3):
+            put(place ^ 2, outer_2)
+            put(3 - place, outer_3)
+
+        start += count
 
 
 def after(values, far=()):
@@ -233,7 +239,7 @@
         return outer
 
     def settle(self, waits=()):
-        homes = self.call(settle_kernel, CHUNK_ROWS, self.received, waits, "settle")
+        homes = self.call(settle_kernel, STREAM_ROWS, self.received, waits, "settle")
         self.arrived = [self.spread(home) for home in homes]
 
     def spread(self, home):
@@ -244,23 +250,22 @@
         outer_3 = lax.ppermute(inner_2, "dp", [(1, 0), (2, 3)])
         return home, outer, inner, inner_2, outer_2, outer_3
 
-    def rows(self, chunk, waits=(), far=()):
-        arrived = self.arrived[chunk]
-        count, width = arrived[0].shape
-        specs, extra = after(waits, far)
+    def rows(self, waits):
+        arrived = [in_vmem(a) for stream in self.arrived for a in stream]
+        specs, extra = after(waits)
         return pl.pallas_call(
-            functools.partial(collect_kernel, self.index_of, count),
+            functools.partial(collect_kernel, self.index_of),
             grid_spec=pltpu.PrefetchScalarGridSpec(
                 num_scalar_prefetch=1,
                 grid=(1,),
                 in_specs=[held()] * len(arrived) + specs,
                 out_specs=held(),
             ),
-            out_shape=pltpu.VMEM((4 * count, width), self.tokens.dtype),
+            out_shape=pltpu.VMEM((4 * BLK, self.tokens.shape[1]), self.tokens.dtype),
             compiler_params=SMALL,
             cost_estimate=BRIEF,
             name="collect",
-        )(self.index, *[in_vmem(a) for a in arrived], *extra)
+        )(self.index, *arrived, *extra)
 
 
 def load_weight_kernel(w_ref, *refs):
@@ -538,10 +543,10 @@
     )(index, *pieces)
 
 
-def finish_kernel(index_of, index_ref, low_ref, *refs):
+def finish_kernel(index_of, tiles, index_ref, low_ref, *refs):
     index = index_of(index_ref)
     up_refs, sum_refs, out_ref = refs[: index.per_part], refs[index.per_part : -1], refs[-1]
-    per_chunk = len(sum_refs) // len(CHUNK_ROWS)
+    terms = len(sum_refs) // tiles
     for i in range(index.per_part):
         block = index.block(0, 0, i)
         live = index.live_rows(block)
@@ -551,22 +556,23 @@
             (((0,), (0,)), ((), ())),
             preferred_element_type=jnp.float32,
         )
-        start = 0
-        for c, count in enumerate(CHUNK_ROWS):
-            total = adapter_scale * side[start : start + count]
-            for ref in sum_refs[c * per_chunk : (c + 1) * per_chunk]:
-                total = total + ref[i * count : (i + 1) * count].astype(jnp.float32)
-            keep = start + lax.broadcasted_iota(jnp.int32, total.shape, 0) < live
-            at = i * BLK + start
-            out_ref[at : at + count] = jnp.where(keep, total, 0.0).astype(out_ref.dtype)
-            start += count
-
-
-def finish(index_of, index, lowered, up, sums, part, projected):
+        keep = lax.broadcasted_iota(jnp.int32, side.shape, 0) < live
+        rows = slice(i * BLK, (i + 1) * BLK)
+        for n in range(tiles):
+
+            @pl.when(pl.program_id(0) == n)
+            def _(n=n):
+                total = adapter_scale * side
+                for ref in sum_refs[n * terms : (n + 1) * terms]:
+                    total = total + ref[rows].astype(jnp.float32)
+                out_ref[rows] = jnp.where(keep, total, 0.0).astype(out_ref.dtype)
+
+
+def finish(index_of, index, lowered, up, sums, part, projected, far):
     per_part = lowered.shape[0]
     _, rank, width = up.shape
-    tile = min(1024, width // PARTS)
-    tiles = width // PARTS // tile
+    tiles = len(sums)
+    tile = width // WRITES // tiles
     first = part * tiles
     out = (per_part * BLK, width)
 
@@ -577,27 +583,26 @@
 
         return pl.BlockSpec((1, rank, tile), at)
 
-    flat = [term for chunk in sums for term in chunk]
-    specs = [
-        pl.BlockSpec((per_part * count, tile), lambda n, _: (0, n))
-        for chunk, count in zip(sums, CHUNK_ROWS)
-        for _ in chunk
-    ]
+    flat = [term for terms in sums for term in terms]
     operands = [index, lowered, *[up] * per_part, *flat]
-    aliases, more, extra = {}, [], []
+    more, extra = after((), far)
+    aliases = {}
     if projected is not None:
         aliases = {len(operands): 0}
-        more, extra = [pl.BlockSpec(memory_space=pl.ANY)], [projected]
+        more, extra = [pl.BlockSpec(memory_space=pl.ANY)] + more, [projected] + extra
 
     def kernel(*refs):
-        finish_kernel(index_of, *refs[: len(operands)], refs[-1])
+        finish_kernel(index_of, tiles, *refs[: len(operands)], refs[-1])
 
     return pl.pallas_call(
         kernel,
         grid_spec=pltpu.PrefetchScalarGridSpec(
             num_scalar_prefetch=1,
             grid=(tiles,),
-            in_specs=[whole(lowered.shape)] + [factor(i) for i in range(per_part)] + specs + more,
+            in_specs=[whole(lowered.shape)]
+            + [factor(i) for i in range(per_part)]
+            + [whole((per_part * BLK, tile))] * len(flat)
+            + more,
             out_specs=pl.BlockSpec((out[0], tile), lambda n, _: (0, first + n)),
         ),
         out_shape=shape_of(out, jnp.bfloat16),
@@ -670,29 +675,21 @@
             total = (total + more[0]) + (more[1] + more[2])
             k *= 4
 
-    def gradients(pieces, back_rows):
-        return (
-            up_gradient(index_of, index, adapter_count, with_other_core(pieces)),
-            down_gradient(index_of, index, tokens, with_other_core(back_rows)),
-        )
-
     if owners == 4 and block_count == 4:
         relay = Relay(index_of, index, tokens)
         sent = relay.first()
         send, keep, back = small_products([sent])
         arrived, others = over_parts(send, keep)
-        total, more = over_dp(merge(keep, arrived, back, others, []))
+        sent = relay.second(others)
+        weight = load_weight(frozen_up_weight, [sent])
+        relay.settle([weight])
+        first_round = [v for stream in relay.arrived for v in stream[1:3]]
+        total, more = over_dp(merge(keep, arrived, back, others, first_round))
         lowered, back_rows, pieces = make_pieces(
             index_of, index, shape, total, more, cotangent, []
         )
-        sent = relay.second([lowered])
         pieces, back_rows = same_core(pieces), same_core(back_rows)
-        weight = load_weight(frozen_up_weight, [sent])
-        relay.settle([weight, *pieces[1:], *back_rows[1:]])
-        up_grad, down_grad = gradients(pieces, back_rows)
-        ahead = [v for chunk in relay.arrived[1:] for v in chunk[3:5]]
-        chunks = [lambda waits: relay.rows(0, ahead, [up_grad, down_grad])]
-        chunks += [functools.partial(relay.rows, c) for c in range(1, len(CHUNK_ROWS))]
+        rows = relay.rows([])
     else:
         weight = load_weight(frozen_up_weight, [])
         send, keep, back = small_products([])
@@ -701,7 +698,7 @@
         lowered, back_rows, pieces = make_pieces(
             index_of, index, shape, total, more, cotangent, []
         )
-        up_grad, down_grad = gradients(same_core(pieces), same_core(back_rows))
+        pieces, back_rows = same_core(pieces), same_core(back_rows)
         every_slot = lax.all_gather(
             tokens.reshape(CAP, BLK, width_dev), "dp", axis=0, tiled=True
         )
@@ -710,38 +707,45 @@
         order = (devices // chips ^ 1) + (devices % chips) * CORES ^ part
         blocks = (order[:, None] * shape.per_part + jnp.arange(shape.per_part)).reshape(-1)
         picked = every_slot[adapter_of_block[blocks] * CAP + slot_of_block[blocks]]
-        starts = [sum(CHUNK_ROWS[:c]) for c in range(len(CHUNK_ROWS))]
-        chunks = [
-            lambda waits, s=s, count=count: picked[:, s : s + count].reshape(-1, width_dev)
-            for s, count in zip(starts, CHUNK_ROWS)
-        ]
-    def summed(rows, part, waits):
+        rows = picked.reshape(-1, width_dev)
+
+    pieces, back_rows = with_other_core(pieces), with_other_core(back_rows)
+    up_grad = up_gradient(index_of, index, adapter_count, pieces)
+    down_grad = down_gradient(index_of, index, tokens, back_rows)
+
+    def summed(part, waits):
         each = rows.shape[0] // parts
         send_own, send, own, other = split_product(shape, rows, weight, part, PARTS, waits)
         outgoing = (other + to_other_core(send).astype(jnp.float32)).astype(jnp.bfloat16)
         across = [to_chip(outgoing[(k - 1) * each : k * each], k) for k in range(1, chips)]
         return [own, to_other_core(send_own)] + across, outgoing
 
-    sums, rows, waits = [], [], []
-    for chunk in chunks:
-        rows.append(chunk(waits))
-        sums.append([summed(rows[-1], 0, ())])
-        waits = [sums[-1][0][1]]
-    for part in range(1, PARTS):
-        waits = rows[-1:]
-        for chunk_rows, done in zip(rows, sums):
-            done.append(summed(chunk_rows, part, waits))
-            waits = [*sums[0][part - 1][0][2:], sums[-1][part - 1][1]]
+    sums, outgoing = [], []
+    for part in range(PARTS):
+        waits = []
+        if part == 1:
+            waits.extend([*pieces[1:chips], *back_rows[1:chips]])
+        if part == 2:
+            waits.extend([*pieces[chips:], *back_rows[chips:]])
+        if part >= 2:
+            waits.append(outgoing[part - 2])
+        if part >= 3:
+            waits.extend([sums[part - 1][0], *sums[part - 3][2:]])
+        terms, sent = summed(part, waits)
+        sums.append(terms)
+        outgoing.append(sent)
     projected = None
-    for part in range(PARTS):
+    for part in range(WRITES):
+        each = PARTS // WRITES
         projected = finish(
             index_of,
             index,
             lowered,
             adapter_up_factor,
-            [done[part][0] for done in sums],
+            sums[part * each : (part + 1) * each],
             part,
             projected,
+            [] if projected is not None else [up_grad, down_grad],
         )
     return (projected, jnp.swapaxes(down_grad, 1, 2), up_grad)
 

time: 126 us -> 131 us (1.040)
  waiting for transfers between devices: 51 us -> 54.6 us
  starting transfers between devices: 39.4 us -> 40.9 us
    ppermute x2, waiting for transfers between devices: 14.4 us -> 5.8 us  [spread(): outer_3 = lax.ppermute(inner_2, 'dp', [(1, 0), (2, 3)])]
    ppermute x2, waiting for transfers between devices: 3.94 us -> 11.5 us  [spread(): outer_2 = lax.ppermute(inner, 'dp', [(1, 0), (2, 3)])]
    ppermute x2, waiting for transfers between devices: 3.01 us -> 7.16 us  [spread(): outer = lax.ppermute(home, 'dp', [(0, 1), (1, 0), (2, 3), (3, 2)])]
    ppermute x7, waiting for transfers between devices: 17 us -> 19.5 us  [to_chip(): lax.ppermute(value, 'tensor', [(i, i ^ k * CORES) for i in range(parts)])]
    ppermute x3, waiting for transfers between devices: 5.48 us -> 3.05 us  [across_dp(): return lax.ppermute(value, 'dp', [(i, i ^ k) for i in range(owners)])]
    ppermute x13, waiting for transfers between devices: 3.61 us -> 1.51 us  [to_other_core(): return lax.ppermute(value, 'tensor', [(i, i ^ 1) for i in range(parts)])]
    ppermute x3, starting transfers between devices: 4.45 us -> 6.15 us  [across_dp(): return lax.ppermute(value, 'dp', [(i, i ^ k) for i in range(owners)])]
    ppermute x1, waiting for transfers between devices: 0.01 us -> 1.66 us  [first(): lax.ppermute(inward, 'dp', [(3, 2), (0, 1)])]
  transfers between devices with their start and end apart: 37 -> 37, of which waited for: 16 -> 18; matrix products, arithmetic and copies ran while one was open for 0% -> 0% of each run, Pallas kernels for 19% -> 21%
where the time goes in v11:
time: 131 us
  waiting for transfers between devices  54.6 us (42%)
  starting transfers between devices  40.9 us (31%)
  Pallas kernels  33.2 us (25%)
    ppermute x7, waiting for transfers between devices, to_chip(): lax.ppermute(value, 'tensor', [(i, i ^ k * CORES) for i in range(parts)])  19.5 us
    ppermute x2, waiting for transfers between devices, spread(): outer_2 = lax.ppermute(inner, 'dp', [(1, 0), (2, 3)])  11.5 us
    pallas_call x4, Pallas kernels, split_product(): pl.pallas_call(functools.partial(split_product_kernel, each, half, part *...  9.46 us
    ppermute x2, waiting for transfers between devices, spread(): outer = lax.ppermute(home, 'dp', [(0, 1), (1, 0), (2, 3), (3, 2)])  7.16 us
    ppermute x7, starting transfers between devices, to_chip(): lax.ppermute(value, 'tensor', [(i, i ^ k * CORES) for i in range(parts)])  6.76 us
    ppermute x3, starting transfers between devices, across_dp(): return lax.ppermute(value, 'dp', [(i, i ^ k) for i in range(owners)])  6.15 us
    pallas_call x1, Pallas kernels, load_weight(): pl.pallas_call(load_weight_kernel, grid=(1,), in_specs=[pl.BlockSpec(memo...  5.89 us
    ppermute x2, waiting for transfers between devices, spread(): outer_3 = lax.ppermute(inner_2, 'dp', [(1, 0), (2, 3)])  5.8 us
  transfers between devices with their start and end apart: 37, of which 18 were waited for; matrix products, arithmetic and copies ran while one was open for 0% of the time, Pallas kernels for 21%

profile of v11, /device:TPU:0, one launch (start us, length us, event | category | flops | bytes accessed | tf_op | source)
XLA Modules:
  0.0 130.8 jit_solution(3213861365644211852)
XLA Ops:
  3.3 5.0 %collective-permute-start.2 = (bf16[128,2048]{1,0:T(8,128)(2,1)S(1)}, bf16[128,2048]{1,0:T(8,128)(2,1)S(1)}, u32[]{:S(2)}, u32[]{:S(2)}) collective-permute-start(bf16[128,2048]{1,0:T(8,128)(2,1)S(1)} %get-tuple-element.31.refs_0_), channel_id=1, source_target_pairs={{12,8},{0,4},{13,9},{1,5},{14,10},{2,6},{15,11},{3,7},{28,24},{16,... | collective-permute-start | bytes 1572872 | tf_op jit(solution)/shard_map/ppermute | solution.py:226
  9.0 3.5 %narrow.1 = (f32[2,1,64,128]{3,2,1,0:T(8,128)S(1)}, f32[2,1,64,128]{3,2,1,0:T(8,128)S(1)}, f32[1,64,128]{2,1,0:T(8,128)S(1)}) custom-call(s32[14]{0:T(128)S(1)} %concatenate.3.index_ref.refs_0_, bf16[384,2048]{1,0:T(8,128)(2,1)} %tokens_ref.9, bf16[1,64,2048]{2,1,0:T(8,128)(2,1)} %bitcast.7, bf16[128,4096]{1,0:T(8,128)(2,1)} %cot_ref.3, ...), custom_call_target="tpu_custom_call" | custom-call | flops 1 | bytes 1 | tf_op jit(solution)/shard_map/narrow/pallas_call | solution.py:381
  15.3 2.4 %collective-permute-done.1.refs_0_ = f32[1,64,128]{2,1,0:T(8,128)S(1)} collective-permute-done((f32[1,64,128]{2,1,0:T(8,128)S(1)}, f32[1,64,128]{2,1,0:T(8,128)S(1)}, u32[]{:S(2)}, u32[]{:S(2)}) %collective-permute-start.1) | collective-permute-done | bytes 32800 | tf_op jit(solution)/shard_map/ppermute | solution.py:642
  20.0 5.7 %collective-permute-start.4 = (bf16[128,2048]{1,0:T(8,128)(2,1)S(1)}, bf16[128,2048]{1,0:T(8,128)(2,1)S(1)}, u32[]{:S(2)}, u32[]{:S(2)}) collective-permute-start(bf16[128,2048]{1,0:T(8,128)(2,1)S(1)} %get-tuple-element.36.refs_0_), channel_id=1, source_target_pairs={{4,0},{0,4},{12,8},{5,1},{1,5},{13,9},{6,2},{2,6},{14,10},{7,3},{3... | collective-permute-start | bytes 1572872 | tf_op jit(solution)/shard_map/ppermute | solution.py:236
  26.5 5.9 %load_weight.1.refs_0_.w_ref = bf16[2048,4096]{1,0:T(8,128)(2,1)S(1)} custom-call(bf16[2048,4096]{1,0:T(8,128)(2,1)} %w_ref.1, bf16[128,2048]{1,0:T(8,128)(2,1)S(1)} %get-tuple-element.36.refs_0_), custom_call_target="tpu_custom_call" | custom-call | flops 1 | bytes 1 | tf_op jit(solution)/shard_map/load_weight/pallas_call | solution.py:289
  32.4 4.4 %collective-permute-done.4.x_ref = bf16[128,2048]{1,0:T(8,128)(2,1)S(1)} collective-permute-done((bf16[128,2048]{1,0:T(8,128)(2,1)S(1)}, bf16[128,2048]{1,0:T(8,128)(2,1)S(1)}, u32[]{:S(2)}, u32[]{:S(2)}) %collective-permute-start.4) | collective-permute-done | bytes 524320 | tf_op jit(solution)/shard_map/ppermute | solution.py:236
  37.4 3.8 %collective-permute-start.6 = (bf16[64,2048]{1,0:T(8,128)(2,1)S(1)}, bf16[64,2048]{1,0:T(8,128)(2,1)S(1)}, u32[]{:S(2)}, u32[]{:S(2)}) collective-permute-start(bf16[64,2048]{1,0:T(8,128)(2,1)S(1)} %get-tuple-element.38.refs_0_), channel_id=1, source_target_pairs={{0,4},{4,0},{8,12},{12,8},{1,5},{5,1},{9,13},{13,9},{2,6},{6,2},{1... | collective-permute-start | bytes 786440 | tf_op jit(solution)/shard_map/ppermute | solution.py:246
  44.2 4.3 %collective-permute-done.6.refs_1_ = bf16[64,2048]{1,0:T(8,128)(2,1)S(1)} collective-permute-done((bf16[64,2048]{1,0:T(8,128)(2,1)S(1)}, bf16[64,2048]{1,0:T(8,128)(2,1)S(1)}, u32[]{:S(2)}, u32[]{:S(2)}) %collective-permute-start.6) | collective-permute-done | bytes 262176 | tf_op jit(solution)/shard_map/ppermute | solution.py:246
  48.4 2.9 %collective-permute-done.8.refs_3_.refs_7_ = bf16[64,2048]{1,0:T(8,128)(2,1)S(1)} collective-permute-done((bf16[64,2048]{1,0:T(8,128)(2,1)S(1)}, bf16[64,2048]{1,0:T(8,128)(2,1)S(1)}, u32[]{:S(2)}, u32[]{:S(2)}) %collective-permute-start.8) | collective-permute-done | bytes 262176 | tf_op jit(solution)/shard_map/ppermute | solution.py:246
  51.3 3.7 %collective-permute-start.10 = (f32[2,1,64,128]{3,2,1,0:T(8,128)S(1)}, f32[2,1,64,128]{3,2,1,0:T(8,128)S(1)}, u32[]{:S(2)}, u32[]{:S(2)}) collective-permute-start(f32[2,1,64,128]{3,2,1,0:T(8,128)S(1)} %merge.1.sum_ref), channel_id=1, source_target_pairs={{0,4},{4,0},{8,12},{12,8},{1,5},{5,1},{9,13},{13,9},{2,6},{6,2},{1... | collective-permute-start | bytes 196616 | tf_op jit(solution)/shard_map/ppermute | solution.py:645
  58.9 3.0 %collective-permute-done.11.refs_1_ = f32[2,1,64,128]{3,2,1,0:T(8,128)S(1)} collective-permute-done((f32[2,1,64,128]{3,2,1,0:T(8,128)S(1)}, f32[2,1,64,128]{3,2,1,0:T(8,128)S(1)}, u32[]{:S(2)}, u32[]{:S(2)}) %collective-permute-start.11) | collective-permute-done | bytes 65568 | tf_op jit(solution)/shard_map/ppermute | solution.py:645
  69.5 5.9 %collective-permute-done.14.refs_4_ = bf16[64,2048]{1,0:T(8,128)(2,1)S(1)} collective-permute-done((bf16[64,2048]{1,0:T(8,128)(2,1)S(1)}, bf16[64,2048]{1,0:T(8,128)(2,1)S(1)}, u32[]{:S(2)}, u32[]{:S(2)}) %collective-permute-start.14) | collective-permute-done | bytes 262176 | tf_op jit(solution)/shard_map/ppermute | solution.py:248
  75.5 5.6 %collective-permute-done.17.refs_10_ = bf16[64,2048]{1,0:T(8,128)(2,1)S(1)} collective-permute-done((bf16[64,2048]{1,0:T(8,128)(2,1)S(1)}, bf16[64,2048]{1,0:T(8,128)(2,1)S(1)}, u32[]{:S(2)}, u32[]{:S(2)}) %collective-permute-start.17) | collective-permute-done | bytes 262176 | tf_op jit(solution)/shard_map/ppermute | solution.py:248
  81.1 3.0 %collective-permute-done.15.refs_5_ = bf16[64,2048]{1,0:T(8,128)(2,1)S(1)} collective-permute-done((bf16[64,2048]{1,0:T(8,128)(2,1)S(1)}, bf16[64,2048]{1,0:T(8,128)(2,1)S(1)}, u32[]{:S(2)}, u32[]{:S(2)}) %collective-permute-start.15) | collective-permute-done | bytes 262176 | tf_op jit(solution)/shard_map/ppermute | solution.py:250
  84.1 2.8 %collective-permute-done.18.refs_11_ = bf16[64,2048]{1,0:T(8,128)(2,1)S(1)} collective-permute-done((bf16[64,2048]{1,0:T(8,128)(2,1)S(1)}, bf16[64,2048]{1,0:T(8,128)(2,1)S(1)}, u32[]{:S(2)}, u32[]{:S(2)}) %collective-permute-start.18) | collective-permute-done | bytes 262176 | tf_op jit(solution)/shard_map/ppermute | solution.py:250
  87.7 2.4 %split_product.4 = (bf16[128,1024]{1,0:T(8,128)(2,1)S(1)}, bf16[128,1024]{1,0:T(8,128)(2,1)S(1)}, f32[128,1024]{1,0:T(8,128)S(1)}, f32[128,1024]{1,0:T(8,128)S(1)}) custom-call(bf16[512,2048]{1,0:T(8,128)(2,1)S(1)} %collect.1.rows_ref, bf16[2048,4096]{1,0:T(8,128)(2,1)S(1)} %load_weight.1.refs_0_.w_ref), custom_call_target="tpu_custom_call" | custom-call | flops 1 | bytes 1 | tf_op jit(solution)/shard_map/split_product/pallas_call | solution.py:322
  91.4 3.0 %collective-permute-done.23.refs_1_ = bf16[1,64,128]{2,1,0:T(8,128)(2,1)S(1)} collective-permute-done((bf16[1,64,128]{2,1,0:T(8,128)(2,1)S(1)}, bf16[1,64,128]{2,1,0:T(8,128)(2,1)S(1)}, u32[]{:S(2)}, u32[]{:S(2)}) %collective-permute-start.23) | collective-permute-done | bytes 16416 | tf_op jit(solution)/shard_map/ppermute | solution.py:642
  94.4 2.4 %split_product.6 = (bf16[128,1024]{1,0:T(8,128)(2,1)S(1)}, bf16[128,1024]{1,0:T(8,128)(2,1)S(1)}, f32[128,1024]{1,0:T(8,128)S(1)}, f32[128,1024]{1,0:T(8,128)S(1)}) custom-call(bf16[512,2048]{1,0:T(8,128)(2,1)S(1)} %collect.1.rows_ref, bf16[2048,4096]{1,0:T(8,128)(2,1)S(1)} %load_weight.1.refs_0_.w_ref, ...), custom_call_target="tpu_custom_call" | custom-call | flops 1 | bytes 1 | tf_op jit(solution)/shard_map/split_product/pallas_call | solution.py:322
  98.1 2.4 %split_product.5 = (bf16[128,1024]{1,0:T(8,128)(2,1)S(1)}, bf16[128,1024]{1,0:T(8,128)(2,1)S(1)}, f32[128,1024]{1,0:T(8,128)S(1)}, f32[128,1024]{1,0:T(8,128)S(1)}) custom-call(bf16[512,2048]{1,0:T(8,128)(2,1)S(1)} %collect.1.rows_ref, bf16[2048,4096]{1,0:T(8,128)(2,1)S(1)} %load_weight.1.refs_0_.w_ref, ...), custom_call_target="tpu_custom_call" | custom-call | flops 1 | bytes 1 | tf_op jit(solution)/shard_map/split_product/pallas_call | solution.py:322
  100.6 5.2 %collective-permute-done.30.refs_2_.refs_5_ = bf16[128,1024]{1,0:T(8,128)(2,1)S(1)} collective-permute-done((bf16[128,1024]{1,0:T(8,128)(2,1)S(1)}, bf16[128,1024]{1,0:T(8,128)(2,1)S(1)}, u32[]{:S(2)}, u32[]{:S(2)}) %collective-permute-start.30) | collective-permute-done | bytes 262176 | tf_op jit(solution)/shard_map/ppermute | solution.py:642
  105.8 2.4 %split_product.7 = (bf16[128,1024]{1,0:T(8,128)(2,1)S(1)}, bf16[128,1024]{1,0:T(8,128)(2,1)S(1)}, f32[128,1024]{1,0:T(8,128)S(1)}, f32[128,1024]{1,0:T(8,128)S(1)}) custom-call(bf16[512,2048]{1,0:T(8,128)(2,1)S(1)} %collect.1.rows_ref, bf16[2048,4096]{1,0:T(8,128)(2,1)S(1)} %load_weight.1.refs_0_.w_ref, bf16[128,1024]{1,0:T(8,128)(2,1)S(1)} %add_convert_fusion.1.refs_0_, ...), custom_call_target="tpu_custom_call" | custom-call | flops 1 | bytes 1 | tf_op jit(solution)/shard_map/split_product/pallas_call | solution.py:322
  113.8 3.9 %up_gradient.1.refs_9_ = f32[4,64,4096]{2,1,0:T(8,128)} custom-call(s32[14]{0:T(128)S(1)} %concatenate.3.index_ref.refs_0_, bf16[1,64,4096]{2,1,0:T(8,128)(2,1)S(1)} %get-tuple-element.41.refs_0_, bf16[1,64,4096]{2,1,0:T(8,128)(2,1)S(1)} %collective-permute-done.20.refs_0_.refs_1_, bf16[1,64,4096]{2,1,0:T(8,128)(2,1)S(1)} %collective-permute-done.19.refs_0_.refs_2_, ...), custom_call_target="tpu_custom_call" | custom-call | flops 1 | bytes 1 | tf_op jit(solution)/shard_map/up_gradient/pallas_call | solution.py:531
  120.0 3.5 %collective-permute-done.28.refs_5_ = bf16[128,1024]{1,0:T(8,128)(2,1)S(1)} collective-permute-done((bf16[128,1024]{1,0:T(8,128)(2,1)S(1)}, bf16[128,1024]{1,0:T(8,128)(2,1)S(1)}, u32[]{:S(2)}, u32[]{:S(2)}) %collective-permute-start.28) | collective-permute-done | bytes 262176 | tf_op jit(solution)/shard_map/ppermute | solution.py:642
  123.5 5.2 %collective-permute-done.33.refs_8_ = bf16[128,1024]{1,0:T(8,128)(2,1)S(1)} collective-permute-done((bf16[128,1024]{1,0:T(8,128)(2,1)S(1)}, bf16[128,1024]{1,0:T(8,128)(2,1)S(1)}, u32[]{:S(2)}, u32[]{:S(2)}) %collective-permute-start.33) | collective-permute-done | bytes 262176 | tf_op jit(solution)/shard_map/ppermute | solution.py:642
  (78 shorter events, 37.7 us)
Async XLA Ops:
  3.3 16.1 %collective-permute-start.2 = (bf16[128,2048]{1,0:T(8,128)(2,1)S(1)}, bf16[128,2048]{1,0:T(8,128)(2,1)S(1)}, u32[]{:S(2)}, u32[]{:S(2)}) collective-permute-start(bf16[128,2048]{1,0:T(8,128)(2,1)S(1)} %get-tuple-element.31.refs_0_), channel_id=1, source_target_pairs={{12,8},{0,4},{13,9},{1,5},{14,10},{2,6},{15,11},{3,7},{28,24},{16,... | collective-permute-start | bytes 1572872 | tf_op jit(solution)/shard_map/ppermute | solution.py:226
  8.3 11.1 %collective-permute-start.3 = (bf16[128,2048]{1,0:T(8,128)(2,1)S(1)}, bf16[128,2048]{1,0:T(8,128)(2,1)S(1)}, u32[]{:S(2)}, u32[]{:S(2)}) collective-permute-start(bf16[128,2048]{1,0:T(8,128)(2,1)S(1)} %get-tuple-element.35), channel_id=1, source_target_pairs={{8,4},{9,5},{10,6},{11,7},{24,20},{25,21},{26,22},{27,23}} | collective-permute-start | bytes 1572872 | tf_op jit(solution)/shard_map/ppermute | solution.py:227
  20.0 16.8 %collective-permute-start.4 = (bf16[128,2048]{1,0:T(8,128)(2,1)S(1)}, bf16[128,2048]{1,0:T(8,128)(2,1)S(1)}, u32[]{:S(2)}, u32[]{:S(2)}) collective-permute-start(bf16[128,2048]{1,0:T(8,128)(2,1)S(1)} %get-tuple-element.36.refs_0_), channel_id=1, source_target_pairs={{4,0},{0,4},{12,8},{5,1},{1,5},{13,9},{6,2},{2,6},{14,10},{7,3},{3... | collective-permute-start | bytes 1572872 | tf_op jit(solution)/shard_map/ppermute | solution.py:236
  25.8 11.0 %collective-permute-start.5 = (bf16[128,2048]{1,0:T(8,128)(2,1)S(1)}, bf16[128,2048]{1,0:T(8,128)(2,1)S(1)}, u32[]{:S(2)}, u32[]{:S(2)}) collective-permute-start(bf16[128,2048]{1,0:T(8,128)(2,1)S(1)} %get-tuple-element.37), channel_id=1, source_target_pairs={{8,4},{4,8},{9,5},{5,9},{10,6},{6,10},{11,7},{7,11},{24,20},{20,24... | collective-permute-start | bytes 1572872 | tf_op jit(solution)/shard_map/ppermute | solution.py:237
  37.4 11.0 %collective-permute-start.6 = (bf16[64,2048]{1,0:T(8,128)(2,1)S(1)}, bf16[64,2048]{1,0:T(8,128)(2,1)S(1)}, u32[]{:S(2)}, u32[]{:S(2)}) collective-permute-start(bf16[64,2048]{1,0:T(8,128)(2,1)S(1)} %get-tuple-element.38.refs_0_), channel_id=1, source_target_pairs={{0,4},{4,0},{8,12},{12,8},{1,5},{5,1},{9,13},{13,9},{2,6},{6,2},{1... | collective-permute-start | bytes 786440 | tf_op jit(solution)/shard_map/ppermute | solution.py:246
  41.9 9.5 %collective-permute-start.8 = (bf16[64,2048]{1,0:T(8,128)(2,1)S(1)}, bf16[64,2048]{1,0:T(8,128)(2,1)S(1)}, u32[]{:S(2)}, u32[]{:S(2)}) collective-permute-start(bf16[64,2048]{1,0:T(8,128)(2,1)S(1)} %get-tuple-element.39.refs_6_), channel_id=1, source_target_pairs={{0,4},{4,0},{8,12},{12,8},{1,5},{5,1},{9,13},{13,9},{2,6},{6,2},{1... | collective-permute-start | bytes 786440 | tf_op jit(solution)/shard_map/ppermute | solution.py:246
  43.5 7.8 %collective-permute-start.9 = (bf16[64,2048]{1,0:T(8,128)(2,1)S(1)}, bf16[64,2048]{1,0:T(8,128)(2,1)S(1)}, u32[]{:S(2)}, u32[]{:S(2)}) collective-permute-start(bf16[64,2048]{1,0:T(8,128)(2,1)S(1)} %get-tuple-element.39.refs_6_), channel_id=1, source_target_pairs={{4,8},{8,4},{5,9},{9,5},{6,10},{10,6},{7,11},{11,7},{20,24},{24,20... | collective-permute-start | bytes 786440 | tf_op jit(solution)/shard_map/ppermute | solution.py:247
  51.3 7.5 %collective-permute-start.10 = (f32[2,1,64,128]{3,2,1,0:T(8,128)S(1)}, f32[2,1,64,128]{3,2,1,0:T(8,128)S(1)}, u32[]{:S(2)}, u32[]{:S(2)}) collective-permute-start(f32[2,1,64,128]{3,2,1,0:T(8,128)S(1)} %merge.1.sum_ref), channel_id=1, source_target_pairs={{0,4},{4,0},{8,12},{12,8},{1,5},{5,1},{9,13},{13,9},{2,6},{6,2},{1... | collective-permute-start | bytes 196616 | tf_op jit(solution)/shard_map/ppermute | solution.py:645
  57.5 9.4 %collective-permute-start.13 = (bf16[64,2048]{1,0:T(8,128)(2,1)S(1)}, bf16[64,2048]{1,0:T(8,128)(2,1)S(1)}, u32[]{:S(2)}, u32[]{:S(2)}) collective-permute-start(bf16[64,2048]{1,0:T(8,128)(2,1)S(1)} %collective-permute-done.6.refs_1_), channel_id=1, source_target_pairs={{4,8},{8,4},{5,9},{9,5},{6,10},{10,6},{7,11},{11,7},{20,24},{24,20... | collective-permute-start | bytes 786440 | tf_op jit(solution)/shard_map/ppermute | solution.py:249
  58.2 10.1 %collective-permute-start.16 = (bf16[64,2048]{1,0:T(8,128)(2,1)S(1)}, bf16[64,2048]{1,0:T(8,128)(2,1)S(1)}, u32[]{:S(2)}, u32[]{:S(2)}) collective-permute-start(bf16[64,2048]{1,0:T(8,128)(2,1)S(1)} %collective-permute-done.8.refs_3_.refs_7_), channel_id=1, source_target_pairs={{4,8},{8,4},{5,9},{9,5},{6,10},{10,6},{7,11},{11,7},{20,24},{24,20... | collective-permute-start | bytes 786440 | tf_op jit(solution)/shard_map/ppermute | solution.py:249
  62.8 27.3 %collective-permute-start.20 = (bf16[1,64,4096]{2,1,0:T(8,128)(2,1)S(1)}, bf16[1,64,4096]{2,1,0:T(8,128)(2,1)S(1)}, u32[]{:S(2)}, u32[]{:S(2)}) collective-permute-start(bf16[1,64,4096]{2,1,0:T(8,128)(2,1)S(1)} %get-tuple-element.41.refs_0_), channel_id=1, source_target_pairs={{0,2},{1,3},{2,0},{3,1},{4,6},{5,7},{6,4},{7,5},{8,10},{9,11},{10,... | collective-permute-start | bytes 1572872 | tf_op jit(solution)/shard_map/ppermute | solution.py:642
  64.3 11.1 %collective-permute-start.14 = (bf16[64,2048]{1,0:T(8,128)(2,1)S(1)}, bf16[64,2048]{1,0:T(8,128)(2,1)S(1)}, u32[]{:S(2)}, u32[]{:S(2)}) collective-permute-start(bf16[64,2048]{1,0:T(8,128)(2,1)S(1)} %collective-permute-done.7.refs_2_), channel_id=1, source_target_pairs={{4,0},{8,12},{5,1},{9,13},{6,2},{10,14},{7,3},{11,15},{20,16},{24,... | collective-permute-start | bytes 786440 | tf_op jit(solution)/shard_map/ppermute | solution.py:248
  65.6 15.5 %collective-permute-start.17 = (bf16[64,2048]{1,0:T(8,128)(2,1)S(1)}, bf16[64,2048]{1,0:T(8,128)(2,1)S(1)}, u32[]{:S(2)}, u32[]{:S(2)}) collective-permute-start(bf16[64,2048]{1,0:T(8,128)(2,1)S(1)} %collective-permute-done.9.refs_4_.refs_8_), channel_id=1, source_target_pairs={{4,0},{8,12},{5,1},{9,13},{6,2},{10,14},{7,3},{11,15},{20,16},{24,... | collective-permute-start | bytes 786440 | tf_op jit(solution)/shard_map/ppermute | solution.py:248
  66.9 17.1 %collective-permute-start.15 = (bf16[64,2048]{1,0:T(8,128)(2,1)S(1)}, bf16[64,2048]{1,0:T(8,128)(2,1)S(1)}, u32[]{:S(2)}, u32[]{:S(2)}) collective-permute-start(bf16[64,2048]{1,0:T(8,128)(2,1)S(1)} %collective-permute-done.13.refs_3_), channel_id=1, source_target_pairs={{4,0},{8,12},{5,1},{9,13},{6,2},{10,14},{7,3},{11,15},{20,16},{24,... | collective-permute-start | bytes 786440 | tf_op jit(solution)/shard_map/ppermute | solution.py:250
  68.2 18.6 %collective-permute-start.18 = (bf16[64,2048]{1,0:T(8,128)(2,1)S(1)}, bf16[64,2048]{1,0:T(8,128)(2,1)S(1)}, u32[]{:S(2)}, u32[]{:S(2)}) collective-permute-start(bf16[64,2048]{1,0:T(8,128)(2,1)S(1)} %collective-permute-done.16.refs_9_), channel_id=1, source_target_pairs={{4,0},{8,12},{5,1},{9,13},{6,2},{10,14},{7,3},{11,15},{20,16},{24,... | collective-permute-start | bytes 786440 | tf_op jit(solution)/shard_map/ppermute | solution.py:250
  87.6 10.5 %collective-permute-start.19 = (bf16[1,64,4096]{2,1,0:T(8,128)(2,1)S(1)}, bf16[1,64,4096]{2,1,0:T(8,128)(2,1)S(1)}, u32[]{:S(2)}, u32[]{:S(2)}) collective-permute-start(bf16[1,64,4096]{2,1,0:T(8,128)(2,1)S(1)} %get-tuple-element.41.refs_0_), channel_id=1, source_target_pairs={{0,1},{1,0},{2,3},{3,2},{4,5},{5,4},{6,7},{7,6},{8,9},{9,8},{10,11... | collective-permute-start | bytes 1572872 | tf_op jit(solution)/shard_map/ppermute | solution.py:639
  90.1 8.0 %collective-permute-start.21 = (bf16[1,64,4096]{2,1,0:T(8,128)(2,1)S(1)}, bf16[1,64,4096]{2,1,0:T(8,128)(2,1)S(1)}, u32[]{:S(2)}, u32[]{:S(2)}) collective-permute-start(bf16[1,64,4096]{2,1,0:T(8,128)(2,1)S(1)} %collective-permute-done.20.refs_0_.refs_1_), channel_id=1, source_target_pairs={{0,1},{1,0},{2,3},{3,2},{4,5},{5,4},{6,7},{7,6},{8,9},{9,8},{10,11... | collective-permute-start | bytes 1572872 | tf_op jit(solution)/shard_map/ppermute | solution.py:639
  97.5 8.3 %collective-permute-start.30 = (bf16[128,1024]{1,0:T(8,128)(2,1)S(1)}, bf16[128,1024]{1,0:T(8,128)(2,1)S(1)}, u32[]{:S(2)}, u32[]{:S(2)}) collective-permute-start(bf16[128,1024]{1,0:T(8,128)(2,1)S(1)} %add_convert_fusion.3.refs_4_), channel_id=1, source_target_pairs={{0,2},{1,3},{2,0},{3,1},{4,6},{5,7},{6,4},{7,5},{8,10},{9,11},{10,... | collective-permute-start | bytes 786440 | tf_op jit(solution)/shard_map/ppermute | solution.py:642
  100.5 8.9 %collective-permute-start.27 = (bf16[128,1024]{1,0:T(8,128)(2,1)S(1)}, bf16[128,1024]{1,0:T(8,128)(2,1)S(1)}, u32[]{:S(2)}, u32[]{:S(2)}) collective-permute-start(bf16[128,1024]{1,0:T(8,128)(2,1)S(1)} %get-tuple-element.48), channel_id=1, source_target_pairs={{0,1},{1,0},{2,3},{3,2},{4,5},{5,4},{6,7},{7,6},{8,9},{9,8},{10,11... | collective-permute-start | bytes 786440 | tf_op jit(solution)/shard_map/ppermute | solution.py:639
  108.8 9.1 %collective-permute-start.36 = (bf16[128,1024]{1,0:T(8,128)(2,1)S(1)}, bf16[128,1024]{1,0:T(8,128)(2,1)S(1)}, u32[]{:S(2)}, u32[]{:S(2)}) collective-permute-start(bf16[128,1024]{1,0:T(8,128)(2,1)S(1)} %add_convert_fusion.1.refs_0_), channel_id=1, source_target_pairs={{0,2},{1,3},{2,0},{3,1},{4,6},{5,7},{6,4},{7,5},{8,10},{9,11},{10,... | collective-permute-start | bytes 786440 | tf_op jit(solution)/shard_map/ppermute | solution.py:642
  109.3 10.7 %collective-permute-start.26 = (bf16[128,1024]{1,0:T(8,128)(2,1)S(1)}, bf16[128,1024]{1,0:T(8,128)(2,1)S(1)}, u32[]{:S(2)}, u32[]{:S(2)}) collective-permute-start(bf16[128,1024]{1,0:T(8,128)(2,1)S(1)} %get-tuple-element.46), channel_id=1, source_target_pairs={{0,1},{1,0},{2,3},{3,2},{4,5},{5,4},{6,7},{7,6},{8,9},{9,8},{10,11... | collective-permute-start | bytes 786440 | tf_op jit(solution)/shard_map/ppermute | solution.py:639
  109.7 10.3 %collective-permute-start.31 = (bf16[128,1024]{1,0:T(8,128)(2,1)S(1)}, bf16[128,1024]{1,0:T(8,128)(2,1)S(1)}, u32[]{:S(2)}, u32[]{:S(2)}) collective-permute-start(bf16[128,1024]{1,0:T(8,128)(2,1)S(1)} %get-tuple-element.52), channel_id=1, source_target_pairs={{0,1},{1,0},{2,3},{3,2},{4,5},{5,4},{6,7},{7,6},{8,9},{9,8},{10,11... | collective-permute-start | bytes 786440 | tf_op jit(solution)/shard_map/ppermute | solution.py:639
  110.1 13.4 %collective-permute-start.28 = (bf16[128,1024]{1,0:T(8,128)(2,1)S(1)}, bf16[128,1024]{1,0:T(8,128)(2,1)S(1)}, u32[]{:S(2)}, u32[]{:S(2)}) collective-permute-start(bf16[128,1024]{1,0:T(8,128)(2,1)S(1)} %add_convert_fusion.2), channel_id=1, source_target_pairs={{0,2},{1,3},{2,0},{3,1},{4,6},{5,7},{6,4},{7,5},{8,10},{9,11},{10,... | collective-permute-start | bytes 786440 | tf_op jit(solution)/shard_map/ppermute | solution.py:642
  111.6 17.1 %collective-permute-start.33 = (bf16[128,1024]{1,0:T(8,128)(2,1)S(1)}, bf16[128,1024]{1,0:T(8,128)(2,1)S(1)}, u32[]{:S(2)}, u32[]{:S(2)}) collective-permute-start(bf16[128,1024]{1,0:T(8,128)(2,1)S(1)} %add_convert_fusion), channel_id=1, source_target_pairs={{0,2},{1,3},{2,0},{3,1},{4,6},{5,7},{6,4},{7,5},{8,10},{9,11},{10,... | collective-permute-start | bytes 786440 | tf_op jit(solution)/shard_map/ppermute | solution.py:642
  (16 other events, 112.1 us)

commit v12 on v10

--- a/solution.py
+++ b/solution.py
@@ -562,7 +562,7 @@
             start += count
 
 
-def finish(index_of, index, lowered, up, sums, part, projected):
+def finish(index_of, index, lowered, up, sums, part, projected, far):
     per_part = lowered.shape[0]
     _, rank, width = up.shape
     tile = min(1024, width // PARTS)
@@ -584,10 +584,11 @@
         for _ in chunk
     ]
     operands = [index, lowered, *[up] * per_part, *flat]
-    aliases, more, extra = {}, [], []
+    more, extra = after((), far)
+    aliases = {}
     if projected is not None:
         aliases = {len(operands): 0}
-        more, extra = [pl.BlockSpec(memory_space=pl.ANY)], [projected]
+        more, extra = [pl.BlockSpec(memory_space=pl.ANY)] + more, [projected] + extra
 
     def kernel(*refs):
         finish_kernel(index_of, *refs[: len(operands)], refs[-1])
@@ -663,35 +664,28 @@
 
     def over_dp(total):
         k = 1
-        while True:
-            more = [across_dp(total, j * k) for j in range(1, min(4, owners // k))]
-            if k * 4 >= owners:
-                return total, more
-            total = (total + more[0]) + (more[1] + more[2])
-            k *= 4
-
-    def gradients(pieces, back_rows):
-        return (
-            up_gradient(index_of, index, adapter_count, with_other_core(pieces)),
-            down_gradient(index_of, index, tokens, with_other_core(back_rows)),
-        )
+        while 2 * k < owners:
+            total = total + across_dp(total, k)
+            k *= 2
+        return total, [across_dp(total, k)]
 
     if owners == 4 and block_count == 4:
         relay = Relay(index_of, index, tokens)
         sent = relay.first()
         send, keep, back = small_products([sent])
         arrived, others = over_parts(send, keep)
+        sent = relay.second(others)
         total, more = over_dp(merge(keep, arrived, back, others, []))
         lowered, back_rows, pieces = make_pieces(
             index_of, index, shape, total, more, cotangent, []
         )
-        sent = relay.second([lowered])
-        pieces, back_rows = same_core(pieces), same_core(back_rows)
-        weight = load_weight(frozen_up_weight, [sent])
-        relay.settle([weight, *pieces[1:], *back_rows[1:]])
-        up_grad, down_grad = gradients(pieces, back_rows)
+        relay.settle([lowered])
+        weight = load_weight(frozen_up_weight, relay.arrived[-1][1:3])
+        pieces = with_other_core(same_core(pieces))
+        back_rows = with_other_core(same_core(back_rows))
         ahead = [v for chunk in relay.arrived[1:] for v in chunk[3:5]]
-        chunks = [lambda waits: relay.rows(0, ahead, [up_grad, down_grad])]
+        ahead += [weight, *pieces[chips:]]
+        chunks = [lambda waits: relay.rows(0, ahead)]
         chunks += [functools.partial(relay.rows, c) for c in range(1, len(CHUNK_ROWS))]
     else:
         weight = load_weight(frozen_up_weight, [])
@@ -701,7 +695,8 @@
         lowered, back_rows, pieces = make_pieces(
             index_of, index, shape, total, more, cotangent, []
         )
-        up_grad, down_grad = gradients(same_core(pieces), same_core(back_rows))
+        pieces = with_other_core(same_core(pieces))
+        back_rows = with_other_core(same_core(back_rows))
         every_slot = lax.all_gather(
             tokens.reshape(CAP, BLK, width_dev), "dp", axis=0, tiled=True
         )
@@ -722,16 +717,15 @@
         across = [to_chip(outgoing[(k - 1) * each : k * each], k) for k in range(1, chips)]
         return [own, to_other_core(send_own)] + across, outgoing
 
-    sums, rows, waits = [], [], []
+    sums, waits, ready = [], [()] * PARTS, ()
     for chunk in chunks:
-        rows.append(chunk(waits))
-        sums.append([summed(rows[-1], 0, ())])
-        waits = [sums[-1][0][1]]
-    for part in range(1, PARTS):
-        waits = rows[-1:]
-        for chunk_rows, done in zip(rows, sums):
-            done.append(summed(chunk_rows, part, waits))
-            waits = [*sums[0][part - 1][0][2:], sums[-1][part - 1][1]]
+        rows = chunk(ready)
+        done = [summed(rows, part, waits[part]) for part in range(PARTS)]
+        sums.append([terms for terms, _ in done])
+        ready = [done[0][1]]
+        waits = [[*sums[-1][0][2:], *back_rows[1:chips]], [*sums[-1][1][2:], *back_rows[chips:]]]
+    up_grad = up_gradient(index_of, index, adapter_count, pieces)
+    down_grad = down_gradient(index_of, index, tokens, back_rows)
     projected = None
     for part in range(PARTS):
         projected = finish(
@@ -739,9 +733,10 @@
             index,
             lowered,
             adapter_up_factor,
-            [done[part][0] for done in sums],
+            [done[part] for done in sums],
             part,
             projected,
+            [] if projected is not None else [up_grad, down_grad],
         )
     return (projected, jnp.swapaxes(down_grad, 1, 2), up_grad)
 

time: 126 us -> 130 us (1.032)
  waiting for transfers between devices: 51 us -> 55.7 us
  starting transfers between devices: 39.4 us -> 37.9 us
    ppermute x3 -> x2, waiting for transfers between devices: 5.48 us -> 14.1 us  [across_dp(): return lax.ppermute(value, 'dp', [(i, i ^ k) for i in range(owners)])]
    ppermute x2, waiting for transfers between devices: 14.4 us -> 9.73 us  [spread(): outer_3 = lax.ppermute(inner_2, 'dp', [(1, 0), (2, 3)])]
    ppermute x1, waiting for transfers between devices: 3.55 us -> 0.01 us  [second(): lax.ppermute(outer, 'dp', [(1, 0), (0, 1), (3, 2)])]
    ppermute x2, starting transfers between devices: 6.64 us -> 4.83 us  [spread(): outer = lax.ppermute(home, 'dp', [(0, 1), (1, 0), (2, 3), (3, 2)])]
    ppermute x1, waiting for transfers between devices: 0.01 us -> 1.65 us  [first(): lax.ppermute(inward, 'dp', [(3, 2), (0, 1)])]
    ppermute x3 -> x2, starting transfers between devices: 4.45 us -> 2.85 us  [across_dp(): return lax.ppermute(value, 'dp', [(i, i ^ k) for i in range(owners)])]
    ppermute x2, waiting for transfers between devices: 3.94 us -> 5.48 us  [spread(): outer_2 = lax.ppermute(inner, 'dp', [(1, 0), (2, 3)])]
    ppermute x7, starting transfers between devices: 6.81 us -> 8.15 us  [to_chip(): lax.ppermute(value, 'tensor', [(i, i ^ k * CORES) for i in range(parts)])]
  transfers between devices with their start and end apart: 37 -> 36, of which waited for: 16 -> 17; matrix products, arithmetic and copies ran while one was open for 0% -> 0% of each run, Pallas kernels for 19% -> 20%
where the time goes in v12:
time: 130 us; the launch traced here: 129 us
  waiting for transfers between devices  55.7 us (43%)
  starting transfers between devices  37.9 us (29%)
  Pallas kernels  33.5 us (26%)
    ppermute x7, waiting for transfers between devices, to_chip(): lax.ppermute(value, 'tensor', [(i, i ^ k * CORES) for i in range(parts)])  17 us
    ppermute x2, waiting for transfers between devices, across_dp(): return lax.ppermute(value, 'dp', [(i, i ^ k) for i in range(owners)])  14.1 us
    ppermute x2, waiting for transfers between devices, spread(): outer_3 = lax.ppermute(inner_2, 'dp', [(1, 0), (2, 3)])  9.73 us
    pallas_call x4, Pallas kernels, split_product(): pl.pallas_call(functools.partial(split_product_kernel, each, half, part *...  9.4 us
    ppermute x7, starting transfers between devices, to_chip(): lax.ppermute(value, 'tensor', [(i, i ^ k * CORES) for i in range(parts)])  8.15 us
    pallas_call x1, Pallas kernels, load_weight(): pl.pallas_call(load_weight_kernel, grid=(1,), in_specs=[pl.BlockSpec(memo...  5.89 us
    ppermute x1, starting transfers between devices, second(): lax.ppermute(outer, 'dp', [(1, 0), (0, 1), (3, 2)])  5.69 us
    ppermute x2, waiting for transfers between devices, spread(): outer_2 = lax.ppermute(inner, 'dp', [(1, 0), (2, 3)])  5.48 us
  transfers between devices with their start and end apart: 36, of which 17 were waited for; matrix products, arithmetic and copies ran while one was open for 0% of the time, Pallas kernels for 20%

profile of v12, /device:TPU:0, one launch (start us, length us, event | category | flops | bytes accessed | tf_op | source)
XLA Modules:
  0.0 129.3 jit_solution(3714376339755955135)
XLA Ops:
  1.5 1.8 %first_hop.1 = (bf16[128,2048]{1,0:T(8,128)(2,1)S(1)}, bf16[128,2048]{1,0:T(8,128)(2,1)S(1)}) custom-call(s32[14]{0:T(128)S(1)} %concatenate.3.index_ref.refs_0_, bf16[384,2048]{1,0:T(8,128)(2,1)} %tokens_ref.9), custom_call_target="tpu_custom_call" | custom-call | flops 1 | bytes 1 | tf_op jit(solution)/shard_map/first_hop/pallas_call | solution.py:191
  3.3 5.0 %collective-permute-start.4 = (bf16[128,2048]{1,0:T(8,128)(2,1)S(1)}, bf16[128,2048]{1,0:T(8,128)(2,1)S(1)}, u32[]{:S(2)}, u32[]{:S(2)}) collective-permute-start(bf16[128,2048]{1,0:T(8,128)(2,1)S(1)} %get-tuple-element.31.refs_0_), channel_id=1, source_target_pairs={{12,8},{0,4},{13,9},{1,5},{14,10},{2,6},{15,11},{3,7},{28,24},{16,... | collective-permute-start | bytes 1572872 | tf_op jit(solution)/shard_map/ppermute | solution.py:220
  9.0 3.5 %narrow.1 = (f32[2,1,64,128]{3,2,1,0:T(8,128)S(1)}, f32[2,1,64,128]{3,2,1,0:T(8,128)S(1)}, f32[1,64,128]{2,1,0:T(8,128)S(1)}) custom-call(s32[14]{0:T(128)S(1)} %concatenate.3.index_ref.refs_0_, bf16[384,2048]{1,0:T(8,128)(2,1)} %tokens_ref.9, bf16[1,64,2048]{2,1,0:T(8,128)(2,1)} %bitcast.7, bf16[128,4096]{1,0:T(8,128)(2,1)} %cot_ref.3, ...), custom_call_target="tpu_custom_call" | custom-call | flops 1 | bytes 1 | tf_op jit(solution)/shard_map/narrow/pallas_call | solution.py:376
  15.3 2.4 %collective-permute-done.1.refs_0_ = f32[1,64,128]{2,1,0:T(8,128)S(1)} collective-permute-done((f32[1,64,128]{2,1,0:T(8,128)S(1)}, f32[1,64,128]{2,1,0:T(8,128)S(1)}, u32[]{:S(2)}, u32[]{:S(2)}) %collective-permute-start.1) | collective-permute-done | bytes 32800 | tf_op jit(solution)/shard_map/ppermute | solution.py:638
  20.0 5.7 %collective-permute-start.6 = (bf16[128,2048]{1,0:T(8,128)(2,1)S(1)}, bf16[128,2048]{1,0:T(8,128)(2,1)S(1)}, u32[]{:S(2)}, u32[]{:S(2)}) collective-permute-start(bf16[128,2048]{1,0:T(8,128)(2,1)S(1)} %get-tuple-element.37), channel_id=1, source_target_pairs={{4,0},{0,4},{12,8},{5,1},{1,5},{13,9},{6,2},{2,6},{14,10},{7,3},{3... | collective-permute-start | bytes 1572872 | tf_op jit(solution)/shard_map/ppermute | solution.py:230
  27.8 10.4 %collective-permute-done.2 = f32[2,1,64,128]{3,2,1,0:T(8,128)S(1)} collective-permute-done((f32[2,1,64,128]{3,2,1,0:T(8,128)S(1)}, f32[2,1,64,128]{3,2,1,0:T(8,128)S(1)}, u32[]{:S(2)}, u32[]{:S(2)}) %collective-permute-start.2) | collective-permute-done | bytes 65568 | tf_op jit(solution)/shard_map/ppermute | solution.py:641
  39.7 3.7 %collective-permute-done.3.refs_0_ = f32[2,1,64,128]{3,2,1,0:T(8,128)S(1)} collective-permute-done((f32[2,1,64,128]{3,2,1,0:T(8,128)S(1)}, f32[2,1,64,128]{3,2,1,0:T(8,128)S(1)}, u32[]{:S(2)}, u32[]{:S(2)}) %collective-permute-start.3) | collective-permute-done | bytes 65568 | tf_op jit(solution)/shard_map/ppermute | solution.py:641
  46.5 1.8 %collective-permute-start.8 = (bf16[64,2048]{1,0:T(8,128)(2,1)S(1)}, bf16[64,2048]{1,0:T(8,128)(2,1)S(1)}, u32[]{:S(2)}, u32[]{:S(2)}) collective-permute-start(bf16[64,2048]{1,0:T(8,128)(2,1)S(1)} %get-tuple-element.39.home_ref), channel_id=1, source_target_pairs={{0,4},{4,0},{8,12},{12,8},{1,5},{5,1},{9,13},{13,9},{2,6},{6,2},{1... | collective-permute-start | bytes 786440 | tf_op jit(solution)/shard_map/ppermute | solution.py:240
  48.3 7.1 %collective-permute-done.18.refs_1_ = bf16[1,64,4096]{2,1,0:T(8,128)(2,1)S(1)} collective-permute-done((bf16[1,64,4096]{2,1,0:T(8,128)(2,1)S(1)}, bf16[1,64,4096]{2,1,0:T(8,128)(2,1)S(1)}, u32[]{:S(2)}, u32[]{:S(2)}) %collective-permute-start.18) | collective-permute-done | bytes 524320 | tf_op jit(solution)/shard_map/ppermute | solution.py:638
  56.0 3.1 %collective-permute-start.13 = (bf16[64,2048]{1,0:T(8,128)(2,1)S(1)}, bf16[64,2048]{1,0:T(8,128)(2,1)S(1)}, u32[]{:S(2)}, u32[]{:S(2)}) collective-permute-start(bf16[64,2048]{1,0:T(8,128)(2,1)S(1)} %get-tuple-element.40.home_ref), channel_id=1, source_target_pairs={{0,4},{4,0},{8,12},{12,8},{1,5},{5,1},{9,13},{13,9},{2,6},{6,2},{1... | collective-permute-start | bytes 786440 | tf_op jit(solution)/shard_map/ppermute | solution.py:240
  61.8 4.0 %collective-permute-done.13.refs_0_.outer_ref = bf16[64,2048]{1,0:T(8,128)(2,1)S(1)} collective-permute-done((bf16[64,2048]{1,0:T(8,128)(2,1)S(1)}, bf16[64,2048]{1,0:T(8,128)(2,1)S(1)}, u32[]{:S(2)}, u32[]{:S(2)}) %collective-permute-start.13) | collective-permute-done | bytes 262176 | tf_op jit(solution)/shard_map/ppermute | solution.py:240
  69.1 5.9 %load_weight.1.refs_6_.w_ref = bf16[2048,4096]{1,0:T(8,128)(2,1)S(1)} custom-call(bf16[2048,4096]{1,0:T(8,128)(2,1)} %w_ref.1, bf16[64,2048]{1,0:T(8,128)(2,1)S(1)} %collective-permute-done.13.refs_0_.outer_ref, bf16[64,2048]{1,0:T(8,128)(2,1)S(1)} %collective-permute-done.15.refs_1_.refs_0_), custom_call_target="tpu_custom_call" | custom-call | flops 1 | bytes 1 | tf_op jit(solution)/shard_map/load_weight/pallas_call | solution.py:284
  75.0 5.5 %collective-permute-done.16.refs_5_.refs_2_ = bf16[64,2048]{1,0:T(8,128)(2,1)S(1)} collective-permute-done((bf16[64,2048]{1,0:T(8,128)(2,1)S(1)}, bf16[64,2048]{1,0:T(8,128)(2,1)S(1)}, u32[]{:S(2)}, u32[]{:S(2)}) %collective-permute-start.16) | collective-permute-done | bytes 262176 | tf_op jit(solution)/shard_map/ppermute | solution.py:242
  80.5 5.6 %collective-permute-done.12.refs_3_ = bf16[64,2048]{1,0:T(8,128)(2,1)S(1)} collective-permute-done((bf16[64,2048]{1,0:T(8,128)(2,1)S(1)}, bf16[64,2048]{1,0:T(8,128)(2,1)S(1)}, u32[]{:S(2)}, u32[]{:S(2)}) %collective-permute-start.12) | collective-permute-done | bytes 262176 | tf_op jit(solution)/shard_map/ppermute | solution.py:244
  86.7 2.3 %split_product.5 = (bf16[64,2048]{1,0:T(8,128)(2,1)S(1)}, bf16[64,2048]{1,0:T(8,128)(2,1)S(1)}, f32[64,2048]{1,0:T(8,128)S(1)}, f32[64,2048]{1,0:T(8,128)S(1)}) custom-call(bf16[256,2048]{1,0:T(8,128)(2,1)S(1)} %collect.2.rows_ref, bf16[2048,4096]{1,0:T(8,128)(2,1)S(1)} %load_weight.1.refs_6_.w_ref), custom_call_target="tpu_custom_call" | custom-call | flops 1 | bytes 1 | tf_op jit(solution)/shard_map/split_product/pallas_call | solution.py:317
  92.0 2.3 %split_product.4 = (bf16[64,2048]{1,0:T(8,128)(2,1)S(1)}, bf16[64,2048]{1,0:T(8,128)(2,1)S(1)}, f32[64,2048]{1,0:T(8,128)S(1)}, f32[64,2048]{1,0:T(8,128)S(1)}) custom-call(bf16[256,2048]{1,0:T(8,128)(2,1)S(1)} %collect.2.rows_ref, bf16[2048,4096]{1,0:T(8,128)(2,1)S(1)} %load_weight.1.refs_6_.w_ref), custom_call_target="tpu_custom_call" | custom-call | flops 1 | bytes 1 | tf_op jit(solution)/shard_map/split_product/pallas_call | solution.py:317
  96.8 4.1 %collective-permute-done.23.refs_3_ = bf16[64,2048]{1,0:T(8,128)(2,1)S(1)} collective-permute-done((bf16[64,2048]{1,0:T(8,128)(2,1)S(1)}, bf16[64,2048]{1,0:T(8,128)(2,1)S(1)}, u32[]{:S(2)}, u32[]{:S(2)}) %collective-permute-start.23) | collective-permute-done | bytes 262176 | tf_op jit(solution)/shard_map/ppermute | solution.py:244
  101.6 2.2 %collective-permute-done.32.refs_0_.refs_5_ = bf16[64,2048]{1,0:T(8,128)(2,1)S(1)} collective-permute-done((bf16[64,2048]{1,0:T(8,128)(2,1)S(1)}, bf16[64,2048]{1,0:T(8,128)(2,1)S(1)}, u32[]{:S(2)}, u32[]{:S(2)}) %collective-permute-start.32) | collective-permute-done | bytes 262176 | tf_op jit(solution)/shard_map/ppermute | solution.py:638
  103.8 2.4 %split_product.7 = (bf16[64,2048]{1,0:T(8,128)(2,1)S(1)}, bf16[64,2048]{1,0:T(8,128)(2,1)S(1)}, f32[64,2048]{1,0:T(8,128)S(1)}, f32[64,2048]{1,0:T(8,128)S(1)}) custom-call(bf16[256,2048]{1,0:T(8,128)(2,1)S(1)} %collect.3.rows_ref, bf16[2048,4096]{1,0:T(8,128)(2,1)S(1)} %load_weight.1.refs_6_.w_ref, ...), custom_call_target="tpu_custom_call" | custom-call | flops 1 | bytes 1 | tf_op jit(solution)/shard_map/split_product/pallas_call | solution.py:317
  108.9 2.4 %split_product.6 = (bf16[64,2048]{1,0:T(8,128)(2,1)S(1)}, bf16[64,2048]{1,0:T(8,128)(2,1)S(1)}, f32[64,2048]{1,0:T(8,128)S(1)}, f32[64,2048]{1,0:T(8,128)S(1)}) custom-call(bf16[256,2048]{1,0:T(8,128)(2,1)S(1)} %collect.3.rows_ref, bf16[2048,4096]{1,0:T(8,128)(2,1)S(1)} %load_weight.1.refs_6_.w_ref, ...), custom_call_target="tpu_custom_call" | custom-call | flops 1 | bytes 1 | tf_op jit(solution)/shard_map/split_product/pallas_call | solution.py:317
  116.8 3.9 %up_gradient.1.refs_9_ = f32[4,64,4096]{2,1,0:T(8,128)} custom-call(s32[14]{0:T(128)S(1)} %concatenate.3.index_ref.refs_0_, bf16[1,64,4096]{2,1,0:T(8,128)(2,1)S(1)} %get-tuple-element.41.refs_0_, bf16[1,64,4096]{2,1,0:T(8,128)(2,1)S(1)} %collective-permute-done.18.refs_1_, bf16[1,64,4096]{2,1,0:T(8,128)(2,1)S(1)} %collective-permute-done.17.refs_7_.refs_2_, ...), custom_call_target="tpu_custom_call" | custom-call | flops 1 | bytes 1 | tf_op jit(solution)/shard_map/up_gradient/pallas_call | solution.py:526
  122.4 2.1 %finish.2.refs_9_ = bf16[128,4096]{1,0:T(8,128)(2,1)} custom-call(s32[14]{0:T(128)S(1)} %concatenate.3.index_ref.refs_0_, bf16[1,64,128]{2,1,0:T(8,128)(2,1)S(1)} %get-tuple-element.35.refs_0_.refs_1_, bf16[4,64,4096]{2,1,0:T(8,128)(2,1)S(1)} %copy-done.1, f32[64,2048]{1,0:T(8,128)S(1)} %get-tuple-element.53.refs_3_, ...), custom_call_target="tpu_custom_call" | custom-call | flops 1 | bytes 1 | tf_op jit(solution)/shard_map/finish/pallas_call | solution.py:596
  124.5 2.7 %collective-permute-done.30.refs_8_ = bf16[64,2048]{1,0:T(8,128)(2,1)S(1)} collective-permute-done((bf16[64,2048]{1,0:T(8,128)(2,1)S(1)}, bf16[64,2048]{1,0:T(8,128)(2,1)S(1)}, u32[]{:S(2)}, u32[]{:S(2)}) %collective-permute-start.30) | collective-permute-done | bytes 262176 | tf_op jit(solution)/shard_map/ppermute | solution.py:638
  127.2 2.1 %finish.3 = bf16[128,4096]{1,0:T(8,128)(2,1)} custom-call(s32[14]{0:T(128)S(1)} %concatenate.3.index_ref.refs_0_, bf16[1,64,128]{2,1,0:T(8,128)(2,1)S(1)} %get-tuple-element.35.refs_0_.refs_1_, bf16[4,64,4096]{2,1,0:T(8,128)(2,1)S(1)} %copy-done.1, f32[64,2048]{1,0:T(8,128)S(1)} %get-tuple-element.42.refs_3_, ...), custom_call_target="tpu_custom_call", output_to_operand_aliasing={{}: (9, {})} | custom-call | flops 1 | bytes 1 | tf_op jit(solution)/shard_map/finish/pallas_call | solution.py:596
  (78 shorter events, 36.4 us)
Async XLA Ops:
  3.3 16.1 %collective-permute-start.4 = (bf16[128,2048]{1,0:T(8,128)(2,1)S(1)}, bf16[128,2048]{1,0:T(8,128)(2,1)S(1)}, u32[]{:S(2)}, u32[]{:S(2)}) collective-permute-start(bf16[128,2048]{1,0:T(8,128)(2,1)S(1)} %get-tuple-element.31.refs_0_), channel_id=1, source_target_pairs={{12,8},{0,4},{13,9},{1,5},{14,10},{2,6},{15,11},{3,7},{28,24},{16,... | collective-permute-start | bytes 1572872 | tf_op jit(solution)/shard_map/ppermute | solution.py:220
  8.3 11.1 %collective-permute-start.5 = (bf16[128,2048]{1,0:T(8,128)(2,1)S(1)}, bf16[128,2048]{1,0:T(8,128)(2,1)S(1)}, u32[]{:S(2)}, u32[]{:S(2)}) collective-permute-start(bf16[128,2048]{1,0:T(8,128)(2,1)S(1)} %get-tuple-element.36), channel_id=1, source_target_pairs={{8,4},{9,5},{10,6},{11,7},{24,20},{25,21},{26,22},{27,23}} | collective-permute-start | bytes 1572872 | tf_op jit(solution)/shard_map/ppermute | solution.py:221
  20.0 25.8 %collective-permute-start.6 = (bf16[128,2048]{1,0:T(8,128)(2,1)S(1)}, bf16[128,2048]{1,0:T(8,128)(2,1)S(1)}, u32[]{:S(2)}, u32[]{:S(2)}) collective-permute-start(bf16[128,2048]{1,0:T(8,128)(2,1)S(1)} %get-tuple-element.37), channel_id=1, source_target_pairs={{4,0},{0,4},{12,8},{5,1},{1,5},{13,9},{6,2},{2,6},{14,10},{7,3},{3... | collective-permute-start | bytes 1572872 | tf_op jit(solution)/shard_map/ppermute | solution.py:230
  25.7 20.1 %collective-permute-start.7 = (bf16[128,2048]{1,0:T(8,128)(2,1)S(1)}, bf16[128,2048]{1,0:T(8,128)(2,1)S(1)}, u32[]{:S(2)}, u32[]{:S(2)}) collective-permute-start(bf16[128,2048]{1,0:T(8,128)(2,1)S(1)} %get-tuple-element.38), channel_id=1, source_target_pairs={{8,4},{4,8},{9,5},{5,9},{10,6},{6,10},{11,7},{7,11},{24,20},{20,24... | collective-permute-start | bytes 1572872 | tf_op jit(solution)/shard_map/ppermute | solution.py:231
  26.5 11.7 %collective-permute-start.2 = (f32[2,1,64,128]{3,2,1,0:T(8,128)S(1)}, f32[2,1,64,128]{3,2,1,0:T(8,128)S(1)}, u32[]{:S(2)}, u32[]{:S(2)}) collective-permute-start(f32[2,1,64,128]{3,2,1,0:T(8,128)S(1)} %merge.1), channel_id=1, source_target_pairs={{0,4},{4,0},{8,12},{12,8},{1,5},{5,1},{9,13},{13,9},{2,6},{6,2},{1... | collective-permute-start | bytes 196616 | tf_op jit(solution)/shard_map/ppermute | solution.py:641
  44.3 11.1 %collective-permute-start.18 = (bf16[1,64,4096]{2,1,0:T(8,128)(2,1)S(1)}, bf16[1,64,4096]{2,1,0:T(8,128)(2,1)S(1)}, u32[]{:S(2)}, u32[]{:S(2)}) collective-permute-start(bf16[1,64,4096]{2,1,0:T(8,128)(2,1)S(1)} %get-tuple-element.41.refs_0_), channel_id=1, source_target_pairs={{0,2},{1,3},{2,0},{3,1},{4,6},{5,7},{6,4},{7,5},{8,10},{9,11},{10,... | collective-permute-start | bytes 1572872 | tf_op jit(solution)/shard_map/ppermute | solution.py:638
  45.8 13.3 %collective-permute-start.17 = (bf16[1,64,4096]{2,1,0:T(8,128)(2,1)S(1)}, bf16[1,64,4096]{2,1,0:T(8,128)(2,1)S(1)}, u32[]{:S(2)}, u32[]{:S(2)}) collective-permute-start(bf16[1,64,4096]{2,1,0:T(8,128)(2,1)S(1)} %get-tuple-element.41.refs_0_), channel_id=1, source_target_pairs={{0,1},{1,0},{2,3},{3,2},{4,5},{5,4},{6,7},{7,6},{8,9},{9,8},{10,11... | collective-permute-start | bytes 1572872 | tf_op jit(solution)/shard_map/ppermute | solution.py:635
  46.5 13.3 %collective-permute-start.8 = (bf16[64,2048]{1,0:T(8,128)(2,1)S(1)}, bf16[64,2048]{1,0:T(8,128)(2,1)S(1)}, u32[]{:S(2)}, u32[]{:S(2)}) collective-permute-start(bf16[64,2048]{1,0:T(8,128)(2,1)S(1)} %get-tuple-element.39.home_ref), channel_id=1, source_target_pairs={{0,4},{4,0},{8,12},{12,8},{1,5},{5,1},{9,13},{13,9},{2,6},{6,2},{1... | collective-permute-start | bytes 786440 | tf_op jit(solution)/shard_map/ppermute | solution.py:240
  55.3 19.6 %collective-permute-start.19 = (bf16[1,64,4096]{2,1,0:T(8,128)(2,1)S(1)}, bf16[1,64,4096]{2,1,0:T(8,128)(2,1)S(1)}, u32[]{:S(2)}, u32[]{:S(2)}) collective-permute-start(bf16[1,64,4096]{2,1,0:T(8,128)(2,1)S(1)} %collective-permute-done.18.refs_1_), channel_id=1, source_target_pairs={{0,1},{1,0},{2,3},{3,2},{4,5},{5,4},{6,7},{7,6},{8,9},{9,8},{10,11... | collective-permute-start | bytes 1572872 | tf_op jit(solution)/shard_map/ppermute | solution.py:635
  56.0 9.8 %collective-permute-start.13 = (bf16[64,2048]{1,0:T(8,128)(2,1)S(1)}, bf16[64,2048]{1,0:T(8,128)(2,1)S(1)}, u32[]{:S(2)}, u32[]{:S(2)}) collective-permute-start(bf16[64,2048]{1,0:T(8,128)(2,1)S(1)} %get-tuple-element.40.home_ref), channel_id=1, source_target_pairs={{0,4},{4,0},{8,12},{12,8},{1,5},{5,1},{9,13},{13,9},{2,6},{6,2},{1... | collective-permute-start | bytes 786440 | tf_op jit(solution)/shard_map/ppermute | solution.py:240
  59.8 8.0 %collective-permute-start.10 = (bf16[64,2048]{1,0:T(8,128)(2,1)S(1)}, bf16[64,2048]{1,0:T(8,128)(2,1)S(1)}, u32[]{:S(2)}, u32[]{:S(2)}) collective-permute-start(bf16[64,2048]{1,0:T(8,128)(2,1)S(1)} %collective-permute-done.8.outer_ref), channel_id=1, source_target_pairs={{4,8},{8,4},{5,9},{9,5},{6,10},{10,6},{7,11},{11,7},{20,24},{24,20... | collective-permute-start | bytes 786440 | tf_op jit(solution)/shard_map/ppermute | solution.py:243
  60.5 14.5 %collective-permute-start.11 = (bf16[64,2048]{1,0:T(8,128)(2,1)S(1)}, bf16[64,2048]{1,0:T(8,128)(2,1)S(1)}, u32[]{:S(2)}, u32[]{:S(2)}) collective-permute-start(bf16[64,2048]{1,0:T(8,128)(2,1)S(1)} %collective-permute-done.9.refs_0_), channel_id=1, source_target_pairs={{4,0},{8,12},{5,1},{9,13},{6,2},{10,14},{7,3},{11,15},{20,16},{24,... | collective-permute-start | bytes 786440 | tf_op jit(solution)/shard_map/ppermute | solution.py:242
  65.8 9.2 %collective-permute-start.14 = (bf16[64,2048]{1,0:T(8,128)(2,1)S(1)}, bf16[64,2048]{1,0:T(8,128)(2,1)S(1)}, u32[]{:S(2)}, u32[]{:S(2)}) collective-permute-start(bf16[64,2048]{1,0:T(8,128)(2,1)S(1)} %collective-permute-done.13.refs_0_.outer_ref), channel_id=1, source_target_pairs={{4,8},{8,4},{5,9},{9,5},{6,10},{10,6},{7,11},{11,7},{20,24},{24,20... | collective-permute-start | bytes 786440 | tf_op jit(solution)/shard_map/ppermute | solution.py:243
  66.5 14.0 %collective-permute-start.16 = (bf16[64,2048]{1,0:T(8,128)(2,1)S(1)}, bf16[64,2048]{1,0:T(8,128)(2,1)S(1)}, u32[]{:S(2)}, u32[]{:S(2)}) collective-permute-start(bf16[64,2048]{1,0:T(8,128)(2,1)S(1)} %collective-permute-done.15.refs_1_.refs_0_), channel_id=1, source_target_pairs={{4,0},{8,12},{5,1},{9,13},{6,2},{10,14},{7,3},{11,15},{20,16},{24,... | collective-permute-start | bytes 786440 | tf_op jit(solution)/shard_map/ppermute | solution.py:242
  67.8 18.3 %collective-permute-start.12 = (bf16[64,2048]{1,0:T(8,128)(2,1)S(1)}, bf16[64,2048]{1,0:T(8,128)(2,1)S(1)}, u32[]{:S(2)}, u32[]{:S(2)}) collective-permute-start(bf16[64,2048]{1,0:T(8,128)(2,1)S(1)} %collective-permute-done.10.refs_1_), channel_id=1, source_target_pairs={{4,0},{8,12},{5,1},{9,13},{6,2},{10,14},{7,3},{11,15},{20,16},{24,... | collective-permute-start | bytes 786440 | tf_op jit(solution)/shard_map/ppermute | solution.py:244
  89.1 12.5 %collective-permute-start.26 = (bf16[1,64,128]{2,1,0:T(8,128)(2,1)S(1)}, bf16[1,64,128]{2,1,0:T(8,128)(2,1)S(1)}, u32[]{:S(2)}, u32[]{:S(2)}) collective-permute-start(bf16[1,64,128]{2,1,0:T(8,128)(2,1)S(1)} %get-tuple-element.48.refs_0_), channel_id=1, source_target_pairs={{0,2},{1,3},{2,0},{3,1},{4,6},{5,7},{6,4},{7,5},{8,10},{9,11},{10,... | collective-permute-start | bytes 49160 | tf_op jit(solution)/shard_map/ppermute | solution.py:638
  90.7 10.3 %collective-permute-start.23 = (bf16[64,2048]{1,0:T(8,128)(2,1)S(1)}, bf16[64,2048]{1,0:T(8,128)(2,1)S(1)}, u32[]{:S(2)}, u32[]{:S(2)}) collective-permute-start(bf16[64,2048]{1,0:T(8,128)(2,1)S(1)} %collective-permute-done.14.refs_4_.refs_1_), channel_id=1, source_target_pairs={{4,0},{8,12},{5,1},{9,13},{6,2},{10,14},{7,3},{11,15},{20,16},{24,... | collective-permute-start | bytes 786440 | tf_op jit(solution)/shard_map/ppermute | solution.py:244
  94.6 9.2 %collective-permute-start.32 = (bf16[64,2048]{1,0:T(8,128)(2,1)S(1)}, bf16[64,2048]{1,0:T(8,128)(2,1)S(1)}, u32[]{:S(2)}, u32[]{:S(2)}) collective-permute-start(bf16[64,2048]{1,0:T(8,128)(2,1)S(1)} %add_convert_fusion.2.refs_4_), channel_id=1, source_target_pairs={{0,2},{1,3},{2,0},{3,1},{4,6},{5,7},{6,4},{7,5},{8,10},{9,11},{10,... | collective-permute-start | bytes 786440 | tf_op jit(solution)/shard_map/ppermute | solution.py:638
  96.0 12.9 %collective-permute-start.22 = (bf16[64,2048]{1,0:T(8,128)(2,1)S(1)}, bf16[64,2048]{1,0:T(8,128)(2,1)S(1)}, u32[]{:S(2)}, u32[]{:S(2)}) collective-permute-start(bf16[64,2048]{1,0:T(8,128)(2,1)S(1)} %add_convert_fusion.3), channel_id=1, source_target_pairs={{0,2},{1,3},{2,0},{3,1},{4,6},{5,7},{6,4},{7,5},{8,10},{9,11},{10,... | collective-permute-start | bytes 786440 | tf_op jit(solution)/shard_map/ppermute | solution.py:638
  106.8 17.6 %collective-permute-start.20 = (bf16[64,2048]{1,0:T(8,128)(2,1)S(1)}, bf16[64,2048]{1,0:T(8,128)(2,1)S(1)}, u32[]{:S(2)}, u32[]{:S(2)}) collective-permute-start(bf16[64,2048]{1,0:T(8,128)(2,1)S(1)} %get-tuple-element.43), channel_id=1, source_target_pairs={{0,1},{1,0},{2,3},{3,2},{4,5},{5,4},{6,7},{7,6},{8,9},{9,8},{10,11... | collective-permute-start | bytes 786440 | tf_op jit(solution)/shard_map/ppermute | solution.py:635
  111.2 13.3 %collective-permute-start.28 = (bf16[64,2048]{1,0:T(8,128)(2,1)S(1)}, bf16[64,2048]{1,0:T(8,128)(2,1)S(1)}, u32[]{:S(2)}, u32[]{:S(2)}) collective-permute-start(bf16[64,2048]{1,0:T(8,128)(2,1)S(1)} %get-tuple-element.50), channel_id=1, source_target_pairs={{0,1},{1,0},{2,3},{3,2},{4,5},{5,4},{6,7},{7,6},{8,9},{9,8},{10,11... | collective-permute-start | bytes 786440 | tf_op jit(solution)/shard_map/ppermute | solution.py:635
  111.8 8.9 %collective-permute-start.33 = (bf16[64,2048]{1,0:T(8,128)(2,1)S(1)}, bf16[64,2048]{1,0:T(8,128)(2,1)S(1)}, u32[]{:S(2)}, u32[]{:S(2)}) collective-permute-start(bf16[64,2048]{1,0:T(8,128)(2,1)S(1)} %get-tuple-element.56), channel_id=1, source_target_pairs={{0,1},{1,0},{2,3},{3,2},{4,5},{5,4},{6,7},{7,6},{8,9},{9,8},{10,11... | collective-permute-start | bytes 786440 | tf_op jit(solution)/shard_map/ppermute | solution.py:635
  113.2 9.1 %collective-permute-start.35 = (bf16[64,2048]{1,0:T(8,128)(2,1)S(1)}, bf16[64,2048]{1,0:T(8,128)(2,1)S(1)}, u32[]{:S(2)}, u32[]{:S(2)}) collective-permute-start(bf16[64,2048]{1,0:T(8,128)(2,1)S(1)} %add_convert_fusion), channel_id=1, source_target_pairs={{0,2},{1,3},{2,0},{3,1},{4,6},{5,7},{6,4},{7,5},{8,10},{9,11},{10,... | collective-permute-start | bytes 786440 | tf_op jit(solution)/shard_map/ppermute | solution.py:638
  113.8 13.3 %collective-permute-start.30 = (bf16[64,2048]{1,0:T(8,128)(2,1)S(1)}, bf16[64,2048]{1,0:T(8,128)(2,1)S(1)}, u32[]{:S(2)}, u32[]{:S(2)}) collective-permute-start(bf16[64,2048]{1,0:T(8,128)(2,1)S(1)} %add_convert_fusion.1), channel_id=1, source_target_pairs={{0,2},{1,3},{2,0},{3,1},{4,6},{5,7},{6,4},{7,5},{8,10},{9,11},{10,... | collective-permute-start | bytes 786440 | tf_op jit(solution)/shard_map/ppermute | solution.py:638
  (15 other events, 108.1 us)

commit v13 on v12

--- a/solution.py
+++ b/solution.py
@@ -674,8 +674,8 @@
         sent = relay.first()
         send, keep, back = small_products([sent])
         arrived, others = over_parts(send, keep)
-        sent = relay.second(others)
         total, more = over_dp(merge(keep, arrived, back, others, []))
+        relay.second([total])
         lowered, back_rows, pieces = make_pieces(
             index_of, index, shape, total, more, cotangent, []
         )
@@ -684,7 +684,7 @@
         pieces = with_other_core(same_core(pieces))
         back_rows = with_other_core(same_core(back_rows))
         ahead = [v for chunk in relay.arrived[1:] for v in chunk[3:5]]
-        ahead += [weight, *pieces[chips:]]
+        ahead.append(weight)
         chunks = [lambda waits: relay.rows(0, ahead)]
         chunks += [functools.partial(relay.rows, c) for c in range(1, len(CHUNK_ROWS))]
     else:
@@ -717,13 +717,17 @@
         across = [to_chip(outgoing[(k - 1) * each : k * each], k) for k in range(1, chips)]
         return [own, to_other_core(send_own)] + across, outgoing
 
-    sums, waits, ready = [], [()] * PARTS, ()
+    sums, ready = [], ()
+    waits = [pieces[1:chips], ()]
     for chunk in chunks:
         rows = chunk(ready)
         done = [summed(rows, part, waits[part]) for part in range(PARTS)]
         sums.append([terms for terms, _ in done])
         ready = [done[0][1]]
-        waits = [[*sums[-1][0][2:], *back_rows[1:chips]], [*sums[-1][1][2:], *back_rows[chips:]]]
+        waits = [
+            [*sums[-1][0][2:], *back_rows[1:chips]],
+            [*sums[-1][1][2:], *back_rows[chips:], *pieces[chips:]],
+        ]
     up_grad = up_gradient(index_of, index, adapter_count, pieces)
     down_grad = down_gradient(index_of, index, tokens, back_rows)
     projected = None

time: 130 us -> 120 us (0.923)
  waiting for transfers between devices: 55.7 us -> 47.6 us
  starting transfers between devices: 37.9 us -> 36.1 us
    ppermute x7, waiting for transfers between devices: 17 us -> 9.53 us  [to_chip(): lax.ppermute(value, 'tensor', [(i, i ^ k * CORES) for i in range(parts)])]
    ppermute x2, waiting for transfers between devices: 14.1 us -> 17 us  [across_dp(): return lax.ppermute(value, 'dp', [(i, i ^ k) for i in range(owners)])]
    ppermute x1, starting transfers between devices: 5.69 us -> 3.16 us  [second(): lax.ppermute(outer, 'dp', [(1, 0), (0, 1), (3, 2)])]
    ppermute x13, waiting for transfers between devices: 3.76 us -> 5.65 us  [to_other_core(): return lax.ppermute(value, 'tensor', [(i, i ^ 1) for i in range(parts)])]
    ppermute x2, waiting for transfers between devices: 9.73 us -> 8.02 us  [spread(): outer_3 = lax.ppermute(inner_2, 'dp', [(1, 0), (2, 3)])]
    ppermute x1, waiting for transfers between devices: 1.65 us -> 0.01 us  [first(): lax.ppermute(inward, 'dp', [(3, 2), (0, 1)])]
  transfers between devices with their start and end apart: 36 -> 36, of which waited for: 17 -> 15; matrix products, arithmetic and copies ran while one was open for 0% -> 0% of each run, Pallas kernels for 20% -> 22%
where the time goes in v13:
time: 120 us; the launch traced here: 119 us
  waiting for transfers between devices  47.6 us (40%)
  starting transfers between devices  36.1 us (30%)
  Pallas kernels  33.4 us (28%)
    ppermute x2, waiting for transfers between devices, across_dp(): return lax.ppermute(value, 'dp', [(i, i ^ k) for i in range(owners)])  17 us
    ppermute x7, waiting for transfers between devices, to_chip(): lax.ppermute(value, 'tensor', [(i, i ^ k * CORES) for i in range(parts)])  9.53 us
    pallas_call x4, Pallas kernels, split_product(): pl.pallas_call(functools.partial(split_product_kernel, each, half, part *...  9.3 us
    ppermute x2, waiting for transfers between devices, spread(): outer_3 = lax.ppermute(inner_2, 'dp', [(1, 0), (2, 3)])  8.02 us
    ppermute x7, starting transfers between devices, to_chip(): lax.ppermute(value, 'tensor', [(i, i ^ k * CORES) for i in range(parts)])  7.71 us
    pallas_call x1, Pallas kernels, load_weight(): pl.pallas_call(load_weight_kernel, grid=(1,), in_specs=[pl.BlockSpec(memo...  5.89 us
    ppermute x13, waiting for transfers between devices, to_other_core(): return lax.ppermute(value, 'tensor', [(i, i ^ 1) for i in range(parts)])  5.65 us
    ppermute x1, starting transfers between devices, first(): lax.ppermute(inward, 'dp', [(3, 2), (0, 1)])  4.96 us
  transfers between devices with their start and end apart: 36, of which 15 were waited for; matrix products, arithmetic and copies ran while one was open for 0% of the time, Pallas kernels for 22%

profile of v13, /device:TPU:0, one launch (start us, length us, event | category | flops | bytes accessed | tf_op | source)
XLA Modules:
  0.0 119.3 jit_solution(1019121391528515959)
XLA Ops:
  1.5 1.8 %first_hop.1 = (bf16[128,2048]{1,0:T(8,128)(2,1)S(1)}, bf16[128,2048]{1,0:T(8,128)(2,1)S(1)}) custom-call(s32[14]{0:T(128)S(1)} %concatenate.3.index_ref.refs_0_, bf16[384,2048]{1,0:T(8,128)(2,1)} %tokens_ref.9), custom_call_target="tpu_custom_call" | custom-call | flops 1 | bytes 1 | tf_op jit(solution)/shard_map/first_hop/pallas_call | solution.py:191
  3.3 5.0 %collective-permute-start.4 = (bf16[128,2048]{1,0:T(8,128)(2,1)S(1)}, bf16[128,2048]{1,0:T(8,128)(2,1)S(1)}, u32[]{:S(2)}, u32[]{:S(2)}) collective-permute-start(bf16[128,2048]{1,0:T(8,128)(2,1)S(1)} %get-tuple-element.31.refs_0_), channel_id=1, source_target_pairs={{12,8},{0,4},{13,9},{1,5},{14,10},{2,6},{15,11},{3,7},{28,24},{16,... | collective-permute-start | bytes 1572872 | tf_op jit(solution)/shard_map/ppermute | solution.py:220
  9.0 3.5 %narrow.1 = (f32[2,1,64,128]{3,2,1,0:T(8,128)S(1)}, f32[2,1,64,128]{3,2,1,0:T(8,128)S(1)}, f32[1,64,128]{2,1,0:T(8,128)S(1)}) custom-call(s32[14]{0:T(128)S(1)} %concatenate.3.index_ref.refs_0_, bf16[384,2048]{1,0:T(8,128)(2,1)} %tokens_ref.9, bf16[1,64,2048]{2,1,0:T(8,128)(2,1)} %bitcast.7, bf16[128,4096]{1,0:T(8,128)(2,1)} %cot_ref.3, ...), custom_call_target="tpu_custom_call" | custom-call | flops 1 | bytes 1 | tf_op jit(solution)/shard_map/narrow/pallas_call | solution.py:376
  15.3 2.4 %collective-permute-done.1.refs_0_ = f32[1,64,128]{2,1,0:T(8,128)S(1)} collective-permute-done((f32[1,64,128]{2,1,0:T(8,128)S(1)}, f32[1,64,128]{2,1,0:T(8,128)S(1)}, u32[]{:S(2)}, u32[]{:S(2)}) %collective-permute-start.1) | collective-permute-done | bytes 32800 | tf_op jit(solution)/shard_map/ppermute | solution.py:638
  17.8 4.3 %collective-permute-done.2 = f32[2,1,64,128]{3,2,1,0:T(8,128)S(1)} collective-permute-done((f32[2,1,64,128]{3,2,1,0:T(8,128)S(1)}, f32[2,1,64,128]{3,2,1,0:T(8,128)S(1)}, u32[]{:S(2)}, u32[]{:S(2)}) %collective-permute-start.2) | collective-permute-done | bytes 65568 | tf_op jit(solution)/shard_map/ppermute | solution.py:641
  22.8 3.2 %collective-permute-start.6 = (bf16[128,2048]{1,0:T(8,128)(2,1)S(1)}, bf16[128,2048]{1,0:T(8,128)(2,1)S(1)}, u32[]{:S(2)}, u32[]{:S(2)}) collective-permute-start(bf16[128,2048]{1,0:T(8,128)(2,1)S(1)} %get-tuple-element.37), channel_id=1, source_target_pairs={{4,0},{0,4},{12,8},{5,1},{1,5},{13,9},{6,2},{2,6},{14,10},{7,3},{3... | collective-permute-start | bytes 1572872 | tf_op jit(solution)/shard_map/ppermute | solution.py:230
  26.7 3.5 %collective-permute-start.3 = (f32[2,1,64,128]{3,2,1,0:T(8,128)S(1)}, f32[2,1,64,128]{3,2,1,0:T(8,128)S(1)}, u32[]{:S(2)}, u32[]{:S(2)}) collective-permute-start(f32[2,1,64,128]{3,2,1,0:T(8,128)S(1)} %add.31.sum_ref.refs_0_), channel_id=1, source_target_pairs={{0,8},{4,12},{8,0},{12,4},{1,9},{5,13},{9,1},{13,5},{2,10},{6,14},... | collective-permute-start | bytes 196616 | tf_op jit(solution)/shard_map/ppermute | solution.py:641
  30.2 12.7 %collective-permute-done.3.refs_0_ = f32[2,1,64,128]{3,2,1,0:T(8,128)S(1)} collective-permute-done((f32[2,1,64,128]{3,2,1,0:T(8,128)S(1)}, f32[2,1,64,128]{3,2,1,0:T(8,128)S(1)}, u32[]{:S(2)}, u32[]{:S(2)}) %collective-permute-start.3) | collective-permute-done | bytes 65568 | tf_op jit(solution)/shard_map/ppermute | solution.py:641
  45.2 4.3 %collective-permute-start.13 = (bf16[64,2048]{1,0:T(8,128)(2,1)S(1)}, bf16[64,2048]{1,0:T(8,128)(2,1)S(1)}, u32[]{:S(2)}, u32[]{:S(2)}) collective-permute-start(bf16[64,2048]{1,0:T(8,128)(2,1)S(1)} %get-tuple-element.40.home_ref), channel_id=1, source_target_pairs={{0,4},{4,0},{8,12},{12,8},{1,5},{5,1},{9,13},{13,9},{2,6},{6,2},{1... | collective-permute-start | bytes 786440 | tf_op jit(solution)/shard_map/ppermute | solution.py:240
  50.1 3.1 %collective-permute-done.8.outer_ref = bf16[64,2048]{1,0:T(8,128)(2,1)S(1)} collective-permute-done((bf16[64,2048]{1,0:T(8,128)(2,1)S(1)}, bf16[64,2048]{1,0:T(8,128)(2,1)S(1)}, u32[]{:S(2)}, u32[]{:S(2)}) %collective-permute-start.8) | collective-permute-done | bytes 262176 | tf_op jit(solution)/shard_map/ppermute | solution.py:240
  60.0 5.9 %load_weight.1.refs_6_.w_ref = bf16[2048,4096]{1,0:T(8,128)(2,1)S(1)} custom-call(bf16[2048,4096]{1,0:T(8,128)(2,1)} %w_ref.1, bf16[64,2048]{1,0:T(8,128)(2,1)S(1)} %collective-permute-done.13.refs_0_.outer_ref, bf16[64,2048]{1,0:T(8,128)(2,1)S(1)} %collective-permute-done.15.refs_1_.refs_0_), custom_call_target="tpu_custom_call" | custom-call | flops 1 | bytes 1 | tf_op jit(solution)/shard_map/load_weight/pallas_call | solution.py:284
  66.0 4.3 %collective-permute-done.16.refs_5_.refs_2_ = bf16[64,2048]{1,0:T(8,128)(2,1)S(1)} collective-permute-done((bf16[64,2048]{1,0:T(8,128)(2,1)S(1)}, bf16[64,2048]{1,0:T(8,128)(2,1)S(1)}, u32[]{:S(2)}, u32[]{:S(2)}) %collective-permute-start.16) | collective-permute-done | bytes 262176 | tf_op jit(solution)/shard_map/ppermute | solution.py:242
  70.3 3.4 %collective-permute-done.12.refs_3_ = bf16[64,2048]{1,0:T(8,128)(2,1)S(1)} collective-permute-done((bf16[64,2048]{1,0:T(8,128)(2,1)S(1)}, bf16[64,2048]{1,0:T(8,128)(2,1)S(1)}, u32[]{:S(2)}, u32[]{:S(2)}) %collective-permute-start.12) | collective-permute-done | bytes 262176 | tf_op jit(solution)/shard_map/ppermute | solution.py:244
  74.4 2.3 %split_product.5 = (bf16[64,2048]{1,0:T(8,128)(2,1)S(1)}, bf16[64,2048]{1,0:T(8,128)(2,1)S(1)}, f32[64,2048]{1,0:T(8,128)S(1)}, f32[64,2048]{1,0:T(8,128)S(1)}) custom-call(bf16[256,2048]{1,0:T(8,128)(2,1)S(1)} %collect.2.rows_ref, bf16[2048,4096]{1,0:T(8,128)(2,1)S(1)} %load_weight.1.refs_6_.w_ref, ...), custom_call_target="tpu_custom_call" | custom-call | flops 1 | bytes 1 | tf_op jit(solution)/shard_map/split_product/pallas_call | solution.py:317
  80.0 2.3 %split_product.4 = (bf16[64,2048]{1,0:T(8,128)(2,1)S(1)}, bf16[64,2048]{1,0:T(8,128)(2,1)S(1)}, f32[64,2048]{1,0:T(8,128)S(1)}, f32[64,2048]{1,0:T(8,128)S(1)}) custom-call(bf16[256,2048]{1,0:T(8,128)(2,1)S(1)} %collect.2.rows_ref, bf16[2048,4096]{1,0:T(8,128)(2,1)S(1)} %load_weight.1.refs_6_.w_ref), custom_call_target="tpu_custom_call" | custom-call | flops 1 | bytes 1 | tf_op jit(solution)/shard_map/split_product/pallas_call | solution.py:317
  84.7 4.6 %collective-permute-done.20.refs_3_ = bf16[64,2048]{1,0:T(8,128)(2,1)S(1)} collective-permute-done((bf16[64,2048]{1,0:T(8,128)(2,1)S(1)}, bf16[64,2048]{1,0:T(8,128)(2,1)S(1)}, u32[]{:S(2)}, u32[]{:S(2)}) %collective-permute-start.20) | collective-permute-done | bytes 262176 | tf_op jit(solution)/shard_map/ppermute | solution.py:244
  90.5 2.7 %collective-permute-done.32.refs_0_.refs_5_ = bf16[64,2048]{1,0:T(8,128)(2,1)S(1)} collective-permute-done((bf16[64,2048]{1,0:T(8,128)(2,1)S(1)}, bf16[64,2048]{1,0:T(8,128)(2,1)S(1)}, u32[]{:S(2)}, u32[]{:S(2)}) %collective-permute-start.32) | collective-permute-done | bytes 262176 | tf_op jit(solution)/shard_map/ppermute | solution.py:638
  93.3 2.3 %split_product.7 = (bf16[64,2048]{1,0:T(8,128)(2,1)S(1)}, bf16[64,2048]{1,0:T(8,128)(2,1)S(1)}, f32[64,2048]{1,0:T(8,128)S(1)}, f32[64,2048]{1,0:T(8,128)S(1)}) custom-call(bf16[256,2048]{1,0:T(8,128)(2,1)S(1)} %collect.3.rows_ref, bf16[2048,4096]{1,0:T(8,128)(2,1)S(1)} %load_weight.1.refs_6_.w_ref, ...), custom_call_target="tpu_custom_call" | custom-call | flops 1 | bytes 1 | tf_op jit(solution)/shard_map/split_product/pallas_call | solution.py:317
  98.9 2.3 %split_product.6 = (bf16[64,2048]{1,0:T(8,128)(2,1)S(1)}, bf16[64,2048]{1,0:T(8,128)(2,1)S(1)}, f32[64,2048]{1,0:T(8,128)S(1)}, f32[64,2048]{1,0:T(8,128)S(1)}) custom-call(bf16[256,2048]{1,0:T(8,128)(2,1)S(1)} %collect.3.rows_ref, bf16[2048,4096]{1,0:T(8,128)(2,1)S(1)} %load_weight.1.refs_6_.w_ref, ...), custom_call_target="tpu_custom_call" | custom-call | flops 1 | bytes 1 | tf_op jit(solution)/shard_map/split_product/pallas_call | solution.py:317
  106.8 3.9 %up_gradient.1.refs_9_ = f32[4,64,4096]{2,1,0:T(8,128)} custom-call(s32[14]{0:T(128)S(1)} %concatenate.3.index_ref.refs_0_, bf16[1,64,4096]{2,1,0:T(8,128)(2,1)S(1)} %get-tuple-element.45.refs_0_, bf16[1,64,4096]{2,1,0:T(8,128)(2,1)S(1)} %collective-permute-done.21.refs_0_.refs_1_, bf16[1,64,4096]{2,1,0:T(8,128)(2,1)S(1)} %collective-permute-done.26.refs_3_.refs_2_, ...), custom_call_target="tpu_custom_call" | custom-call | flops 1 | bytes 1 | tf_op jit(solution)/shard_map/up_gradient/pallas_call | solution.py:526
  110.7 1.7 %collective-permute-done.35.refs_8_ = bf16[64,2048]{1,0:T(8,128)(2,1)S(1)} collective-permute-done((bf16[64,2048]{1,0:T(8,128)(2,1)S(1)}, bf16[64,2048]{1,0:T(8,128)(2,1)S(1)}, u32[]{:S(2)}, u32[]{:S(2)}) %collective-permute-start.35) | collective-permute-done | bytes 262176 | tf_op jit(solution)/shard_map/ppermute | solution.py:638
  112.4 2.1 %finish.2.refs_9_ = bf16[128,4096]{1,0:T(8,128)(2,1)} custom-call(s32[14]{0:T(128)S(1)} %concatenate.3.index_ref.refs_0_, bf16[1,64,128]{2,1,0:T(8,128)(2,1)S(1)} %get-tuple-element.35.refs_0_.refs_1_, bf16[4,64,4096]{2,1,0:T(8,128)(2,1)S(1)} %copy-done.1, f32[64,2048]{1,0:T(8,128)S(1)} %get-tuple-element.53.refs_3_, ...), custom_call_target="tpu_custom_call" | custom-call | flops 1 | bytes 1 | tf_op jit(solution)/shard_map/finish/pallas_call | solution.py:596
  114.5 2.7 %collective-permute-done.30.refs_8_ = bf16[64,2048]{1,0:T(8,128)(2,1)S(1)} collective-permute-done((bf16[64,2048]{1,0:T(8,128)(2,1)S(1)}, bf16[64,2048]{1,0:T(8,128)(2,1)S(1)}, u32[]{:S(2)}, u32[]{:S(2)}) %collective-permute-start.30) | collective-permute-done | bytes 262176 | tf_op jit(solution)/shard_map/ppermute | solution.py:638
  117.2 2.1 %finish.3 = bf16[128,4096]{1,0:T(8,128)(2,1)} custom-call(s32[14]{0:T(128)S(1)} %concatenate.3.index_ref.refs_0_, bf16[1,64,128]{2,1,0:T(8,128)(2,1)S(1)} %get-tuple-element.35.refs_0_.refs_1_, bf16[4,64,4096]{2,1,0:T(8,128)(2,1)S(1)} %copy-done.1, f32[64,2048]{1,0:T(8,128)S(1)} %get-tuple-element.41.refs_3_, ...), custom_call_target="tpu_custom_call", output_to_operand_aliasing={{}: (9, {})} | custom-call | flops 1 | bytes 1 | tf_op jit(solution)/shard_map/finish/pallas_call | solution.py:596
  (78 shorter events, 31.8 us)
Async XLA Ops:
  3.3 18.8 %collective-permute-start.4 = (bf16[128,2048]{1,0:T(8,128)(2,1)S(1)}, bf16[128,2048]{1,0:T(8,128)(2,1)S(1)}, u32[]{:S(2)}, u32[]{:S(2)}) collective-permute-start(bf16[128,2048]{1,0:T(8,128)(2,1)S(1)} %get-tuple-element.31.refs_0_), channel_id=1, source_target_pairs={{12,8},{0,4},{13,9},{1,5},{14,10},{2,6},{15,11},{3,7},{28,24},{16,... | collective-permute-start | bytes 1572872 | tf_op jit(solution)/shard_map/ppermute | solution.py:220
  8.3 13.9 %collective-permute-start.5 = (bf16[128,2048]{1,0:T(8,128)(2,1)S(1)}, bf16[128,2048]{1,0:T(8,128)(2,1)S(1)}, u32[]{:S(2)}, u32[]{:S(2)}) collective-permute-start(bf16[128,2048]{1,0:T(8,128)(2,1)S(1)} %get-tuple-element.36), channel_id=1, source_target_pairs={{8,4},{9,5},{10,6},{11,7},{24,20},{25,21},{26,22},{27,23}} | collective-permute-start | bytes 1572872 | tf_op jit(solution)/shard_map/ppermute | solution.py:221
  22.8 21.0 %collective-permute-start.6 = (bf16[128,2048]{1,0:T(8,128)(2,1)S(1)}, bf16[128,2048]{1,0:T(8,128)(2,1)S(1)}, u32[]{:S(2)}, u32[]{:S(2)}) collective-permute-start(bf16[128,2048]{1,0:T(8,128)(2,1)S(1)} %get-tuple-element.37), channel_id=1, source_target_pairs={{4,0},{0,4},{12,8},{5,1},{1,5},{13,9},{6,2},{2,6},{14,10},{7,3},{3... | collective-permute-start | bytes 1572872 | tf_op jit(solution)/shard_map/ppermute | solution.py:230
  25.9 17.8 %collective-permute-start.7 = (bf16[128,2048]{1,0:T(8,128)(2,1)S(1)}, bf16[128,2048]{1,0:T(8,128)(2,1)S(1)}, u32[]{:S(2)}, u32[]{:S(2)}) collective-permute-start(bf16[128,2048]{1,0:T(8,128)(2,1)S(1)} %get-tuple-element.38), channel_id=1, source_target_pairs={{8,4},{4,8},{9,5},{5,9},{10,6},{6,10},{11,7},{7,11},{24,20},{20,24... | collective-permute-start | bytes 1572872 | tf_op jit(solution)/shard_map/ppermute | solution.py:231
  26.7 16.2 %collective-permute-start.3 = (f32[2,1,64,128]{3,2,1,0:T(8,128)S(1)}, f32[2,1,64,128]{3,2,1,0:T(8,128)S(1)}, u32[]{:S(2)}, u32[]{:S(2)}) collective-permute-start(f32[2,1,64,128]{3,2,1,0:T(8,128)S(1)} %add.31.sum_ref.refs_0_), channel_id=1, source_target_pairs={{0,8},{4,12},{8,0},{12,4},{1,9},{5,13},{9,1},{13,5},{2,10},{6,14},... | collective-permute-start | bytes 196616 | tf_op jit(solution)/shard_map/ppermute | solution.py:641
  44.4 8.8 %collective-permute-start.8 = (bf16[64,2048]{1,0:T(8,128)(2,1)S(1)}, bf16[64,2048]{1,0:T(8,128)(2,1)S(1)}, u32[]{:S(2)}, u32[]{:S(2)}) collective-permute-start(bf16[64,2048]{1,0:T(8,128)(2,1)S(1)} %get-tuple-element.39.home_ref), channel_id=1, source_target_pairs={{0,4},{4,0},{8,12},{12,8},{1,5},{5,1},{9,13},{13,9},{2,6},{6,2},{1... | collective-permute-start | bytes 786440 | tf_op jit(solution)/shard_map/ppermute | solution.py:240
  44.5 10.9 %collective-permute-start.9 = (bf16[64,2048]{1,0:T(8,128)(2,1)S(1)}, bf16[64,2048]{1,0:T(8,128)(2,1)S(1)}, u32[]{:S(2)}, u32[]{:S(2)}) collective-permute-start(bf16[64,2048]{1,0:T(8,128)(2,1)S(1)} %get-tuple-element.39.home_ref), channel_id=1, source_target_pairs={{4,8},{8,4},{5,9},{9,5},{6,10},{10,6},{7,11},{11,7},{20,24},{24,20... | collective-permute-start | bytes 786440 | tf_op jit(solution)/shard_map/ppermute | solution.py:241
  45.2 11.6 %collective-permute-start.13 = (bf16[64,2048]{1,0:T(8,128)(2,1)S(1)}, bf16[64,2048]{1,0:T(8,128)(2,1)S(1)}, u32[]{:S(2)}, u32[]{:S(2)}) collective-permute-start(bf16[64,2048]{1,0:T(8,128)(2,1)S(1)} %get-tuple-element.40.home_ref), channel_id=1, source_target_pairs={{0,4},{4,0},{8,12},{12,8},{1,5},{5,1},{9,13},{13,9},{2,6},{6,2},{1... | collective-permute-start | bytes 786440 | tf_op jit(solution)/shard_map/ppermute | solution.py:240
  53.9 20.5 %collective-permute-start.21 = (bf16[1,64,4096]{2,1,0:T(8,128)(2,1)S(1)}, bf16[1,64,4096]{2,1,0:T(8,128)(2,1)S(1)}, u32[]{:S(2)}, u32[]{:S(2)}) collective-permute-start(bf16[1,64,4096]{2,1,0:T(8,128)(2,1)S(1)} %get-tuple-element.45.refs_0_), channel_id=1, source_target_pairs={{0,2},{1,3},{2,0},{3,1},{4,6},{5,7},{6,4},{7,5},{8,10},{9,11},{10,... | collective-permute-start | bytes 1572872 | tf_op jit(solution)/shard_map/ppermute | solution.py:638
  55.4 10.5 %collective-permute-start.11 = (bf16[64,2048]{1,0:T(8,128)(2,1)S(1)}, bf16[64,2048]{1,0:T(8,128)(2,1)S(1)}, u32[]{:S(2)}, u32[]{:S(2)}) collective-permute-start(bf16[64,2048]{1,0:T(8,128)(2,1)S(1)} %collective-permute-done.9.refs_0_), channel_id=1, source_target_pairs={{4,0},{8,12},{5,1},{9,13},{6,2},{10,14},{7,3},{11,15},{20,16},{24,... | collective-permute-start | bytes 786440 | tf_op jit(solution)/shard_map/ppermute | solution.py:242
  56.7 9.2 %collective-permute-start.14 = (bf16[64,2048]{1,0:T(8,128)(2,1)S(1)}, bf16[64,2048]{1,0:T(8,128)(2,1)S(1)}, u32[]{:S(2)}, u32[]{:S(2)}) collective-permute-start(bf16[64,2048]{1,0:T(8,128)(2,1)S(1)} %collective-permute-done.13.refs_0_.outer_ref), channel_id=1, source_target_pairs={{4,8},{8,4},{5,9},{9,5},{6,10},{10,6},{7,11},{11,7},{20,24},{24,20... | collective-permute-start | bytes 786440 | tf_op jit(solution)/shard_map/ppermute | solution.py:243
  57.4 12.9 %collective-permute-start.16 = (bf16[64,2048]{1,0:T(8,128)(2,1)S(1)}, bf16[64,2048]{1,0:T(8,128)(2,1)S(1)}, u32[]{:S(2)}, u32[]{:S(2)}) collective-permute-start(bf16[64,2048]{1,0:T(8,128)(2,1)S(1)} %collective-permute-done.15.refs_1_.refs_0_), channel_id=1, source_target_pairs={{4,0},{8,12},{5,1},{9,13},{6,2},{10,14},{7,3},{11,15},{20,16},{24,... | collective-permute-start | bytes 786440 | tf_op jit(solution)/shard_map/ppermute | solution.py:242
  58.7 15.0 %collective-permute-start.12 = (bf16[64,2048]{1,0:T(8,128)(2,1)S(1)}, bf16[64,2048]{1,0:T(8,128)(2,1)S(1)}, u32[]{:S(2)}, u32[]{:S(2)}) collective-permute-start(bf16[64,2048]{1,0:T(8,128)(2,1)S(1)} %collective-permute-done.10.refs_1_), channel_id=1, source_target_pairs={{4,0},{8,12},{5,1},{9,13},{6,2},{10,14},{7,3},{11,15},{20,16},{24,... | collective-permute-start | bytes 786440 | tf_op jit(solution)/shard_map/ppermute | solution.py:244
  76.8 21.8 %collective-permute-start.26 = (bf16[1,64,4096]{2,1,0:T(8,128)(2,1)S(1)}, bf16[1,64,4096]{2,1,0:T(8,128)(2,1)S(1)}, u32[]{:S(2)}, u32[]{:S(2)}) collective-permute-start(bf16[1,64,4096]{2,1,0:T(8,128)(2,1)S(1)} %get-tuple-element.45.refs_0_), channel_id=1, source_target_pairs={{0,1},{1,0},{2,3},{3,2},{4,5},{5,4},{6,7},{7,6},{8,9},{9,8},{10,11... | collective-permute-start | bytes 1572872 | tf_op jit(solution)/shard_map/ppermute | solution.py:635
  77.3 13.3 %collective-permute-start.24 = (bf16[1,64,128]{2,1,0:T(8,128)(2,1)S(1)}, bf16[1,64,128]{2,1,0:T(8,128)(2,1)S(1)}, u32[]{:S(2)}, u32[]{:S(2)}) collective-permute-start(bf16[1,64,128]{2,1,0:T(8,128)(2,1)S(1)} %get-tuple-element.48.refs_0_), channel_id=1, source_target_pairs={{0,2},{1,3},{2,0},{3,1},{4,6},{5,7},{6,4},{7,5},{8,10},{9,11},{10,... | collective-permute-start | bytes 49160 | tf_op jit(solution)/shard_map/ppermute | solution.py:638
  78.7 20.2 %collective-permute-start.27 = (bf16[1,64,4096]{2,1,0:T(8,128)(2,1)S(1)}, bf16[1,64,4096]{2,1,0:T(8,128)(2,1)S(1)}, u32[]{:S(2)}, u32[]{:S(2)}) collective-permute-start(bf16[1,64,4096]{2,1,0:T(8,128)(2,1)S(1)} %collective-permute-done.21.refs_0_.refs_1_), channel_id=1, source_target_pairs={{0,1},{1,0},{2,3},{3,2},{4,5},{5,4},{6,7},{7,6},{8,9},{9,8},{10,11... | collective-permute-start | bytes 1572872 | tf_op jit(solution)/shard_map/ppermute | solution.py:635
  78.8 10.6 %collective-permute-start.20 = (bf16[64,2048]{1,0:T(8,128)(2,1)S(1)}, bf16[64,2048]{1,0:T(8,128)(2,1)S(1)}, u32[]{:S(2)}, u32[]{:S(2)}) collective-permute-start(bf16[64,2048]{1,0:T(8,128)(2,1)S(1)} %collective-permute-done.14.refs_4_.refs_1_), channel_id=1, source_target_pairs={{4,0},{8,12},{5,1},{9,13},{6,2},{10,14},{7,3},{11,15},{20,16},{24,... | collective-permute-start | bytes 786440 | tf_op jit(solution)/shard_map/ppermute | solution.py:244
  84.1 9.1 %collective-permute-start.32 = (bf16[64,2048]{1,0:T(8,128)(2,1)S(1)}, bf16[64,2048]{1,0:T(8,128)(2,1)S(1)}, u32[]{:S(2)}, u32[]{:S(2)}) collective-permute-start(bf16[64,2048]{1,0:T(8,128)(2,1)S(1)} %add_convert_fusion.2.refs_4_), channel_id=1, source_target_pairs={{0,2},{1,3},{2,0},{3,1},{4,6},{5,7},{6,4},{7,5},{8,10},{9,11},{10,... | collective-permute-start | bytes 786440 | tf_op jit(solution)/shard_map/ppermute | solution.py:638
  89.4 9.6 %collective-permute-start.19 = (bf16[64,2048]{1,0:T(8,128)(2,1)S(1)}, bf16[64,2048]{1,0:T(8,128)(2,1)S(1)}, u32[]{:S(2)}, u32[]{:S(2)}) collective-permute-start(bf16[64,2048]{1,0:T(8,128)(2,1)S(1)} %add_convert_fusion.3), channel_id=1, source_target_pairs={{0,2},{1,3},{2,0},{3,1},{4,6},{5,7},{6,4},{7,5},{8,10},{9,11},{10,... | collective-permute-start | bytes 786440 | tf_op jit(solution)/shard_map/ppermute | solution.py:638
  98.4 16.1 %collective-permute-start.17 = (bf16[64,2048]{1,0:T(8,128)(2,1)S(1)}, bf16[64,2048]{1,0:T(8,128)(2,1)S(1)}, u32[]{:S(2)}, u32[]{:S(2)}) collective-permute-start(bf16[64,2048]{1,0:T(8,128)(2,1)S(1)} %get-tuple-element.42), channel_id=1, source_target_pairs={{0,1},{1,0},{2,3},{3,2},{4,5},{5,4},{6,7},{7,6},{8,9},{9,8},{10,11... | collective-permute-start | bytes 786440 | tf_op jit(solution)/shard_map/ppermute | solution.py:635
  101.2 13.3 %collective-permute-start.28 = (bf16[64,2048]{1,0:T(8,128)(2,1)S(1)}, bf16[64,2048]{1,0:T(8,128)(2,1)S(1)}, u32[]{:S(2)}, u32[]{:S(2)}) collective-permute-start(bf16[64,2048]{1,0:T(8,128)(2,1)S(1)} %get-tuple-element.50), channel_id=1, source_target_pairs={{0,1},{1,0},{2,3},{3,2},{4,5},{5,4},{6,7},{7,6},{8,9},{9,8},{10,11... | collective-permute-start | bytes 786440 | tf_op jit(solution)/shard_map/ppermute | solution.py:635
  101.8 8.9 %collective-permute-start.33 = (bf16[64,2048]{1,0:T(8,128)(2,1)S(1)}, bf16[64,2048]{1,0:T(8,128)(2,1)S(1)}, u32[]{:S(2)}, u32[]{:S(2)}) collective-permute-start(bf16[64,2048]{1,0:T(8,128)(2,1)S(1)} %get-tuple-element.56), channel_id=1, source_target_pairs={{0,1},{1,0},{2,3},{3,2},{4,5},{5,4},{6,7},{7,6},{8,9},{9,8},{10,11... | collective-permute-start | bytes 786440 | tf_op jit(solution)/shard_map/ppermute | solution.py:635
  103.2 9.1 %collective-permute-start.35 = (bf16[64,2048]{1,0:T(8,128)(2,1)S(1)}, bf16[64,2048]{1,0:T(8,128)(2,1)S(1)}, u32[]{:S(2)}, u32[]{:S(2)}) collective-permute-start(bf16[64,2048]{1,0:T(8,128)(2,1)S(1)} %add_convert_fusion), channel_id=1, source_target_pairs={{0,2},{1,3},{2,0},{3,1},{4,6},{5,7},{6,4},{7,5},{8,10},{9,11},{10,... | collective-permute-start | bytes 786440 | tf_op jit(solution)/shard_map/ppermute | solution.py:638
  103.8 13.4 %collective-permute-start.30 = (bf16[64,2048]{1,0:T(8,128)(2,1)S(1)}, bf16[64,2048]{1,0:T(8,128)(2,1)S(1)}, u32[]{:S(2)}, u32[]{:S(2)}) collective-permute-start(bf16[64,2048]{1,0:T(8,128)(2,1)S(1)} %add_convert_fusion.1), channel_id=1, source_target_pairs={{0,2},{1,3},{2,0},{3,1},{4,6},{5,7},{6,4},{7,5},{8,10},{9,11},{10,... | collective-permute-start | bytes 786440 | tf_op jit(solution)/shard_map/ppermute | solution.py:638
  (15 other events, 110.5 us)

commit v14 on v13

--- a/solution.py
+++ b/solution.py
@@ -295,7 +295,7 @@
 
 
 def split_product_kernel(each, half, first, tile, rows_ref, w_ref, *refs):
-    send_own_ref, send_ref, own_ref, other_ref = refs[-4:]
+    send_ref, own_ref, other_ref = refs[-3:]
     for n in range(own_ref.shape[1] // tile):
         total = jnp.dot(
             rows_ref[...],
@@ -303,8 +303,7 @@
             preferred_element_type=jnp.float32,
         )
         columns = slice(n * tile, (n + 1) * tile)
-        send_own_ref[:, columns] = total[:each].astype(send_own_ref.dtype)
-        send_ref[:, columns] = total[each:half].astype(send_ref.dtype)
+        send_ref[:, columns] = total[:half].astype(send_ref.dtype)
         own_ref[:, columns] = total[half : half + each]
         other_ref[:, columns] = total[half + each :]
 
@@ -318,10 +317,9 @@
         functools.partial(split_product_kernel, each, half, part * width, min(512, width)),
         grid=(1,),
         in_specs=[held(), held()] + specs,
-        out_specs=[held()] * 4,
+        out_specs=[held()] * 3,
         out_shape=[
-            pltpu.VMEM((each, width), jnp.bfloat16),
-            pltpu.VMEM((half - each, width), jnp.bfloat16),
+            pltpu.VMEM((half, width), jnp.bfloat16),
             pltpu.VMEM((each, width), jnp.float32),
             pltpu.VMEM((half - each, width), jnp.float32),
         ],
@@ -712,22 +710,19 @@
         ]
     def summed(rows, part, waits):
         each = rows.shape[0] // parts
-        send_own, send, own, other = split_product(shape, rows, weight, part, PARTS, waits)
-        outgoing = (other + to_other_core(send).astype(jnp.float32)).astype(jnp.bfloat16)
+        send, own, other = split_product(shape, rows, weight, part, PARTS, waits)
+        arrived = to_other_core(send)
+        outgoing = (other + arrived[each:].astype(jnp.float32)).astype(jnp.bfloat16)
         across = [to_chip(outgoing[(k - 1) * each : k * each], k) for k in range(1, chips)]
-        return [own, to_other_core(send_own)] + across, outgoing
-
-    sums, ready = [], ()
-    waits = [pieces[1:chips], ()]
-    for chunk in chunks:
-        rows = chunk(ready)
-        done = [summed(rows, part, waits[part]) for part in range(PARTS)]
-        sums.append([terms for terms, _ in done])
-        ready = [done[0][1]]
-        waits = [
-            [*sums[-1][0][2:], *back_rows[1:chips]],
-            [*sums[-1][1][2:], *back_rows[chips:], *pieces[chips:]],
-        ]
+        return [own, arrived] + across, outgoing
+
+    first = chunks[0](())
+    first_0 = summed(first, 0, pieces[1:chips])
+    first_1 = summed(first, 1, ())
+    second = chunks[1]([first_0[1], first_1[1]])
+    second_0 = summed(second, 0, first_0[0][2:])
+    second_1 = summed(second, 1, first_1[0][2:])
+    sums = [[first_0[0], first_1[0]], [second_0[0], second_1[0]]]
     up_grad = up_gradient(index_of, index, adapter_count, pieces)
     down_grad = down_gradient(index_of, index, tokens, back_rows)
     projected = None

time: 120 us -> 132 us (1.10)
  waiting for transfers between devices: 47.6 us -> 59 us
    ppermute x7, waiting for transfers between devices: 9.53 us -> 20.6 us  [to_chip(): lax.ppermute(value, 'tensor', [(i, i ^ k * CORES) for i in range(parts)])]
    ppermute x2, waiting for transfers between devices: 8.02 us -> 10.6 us  [spread(): outer_3 = lax.ppermute(inner_2, 'dp', [(1, 0), (2, 3)])]
    ppermute x13 -> x9, waiting for transfers between devices: 5.65 us -> 3.46 us  [to_other_core(): return lax.ppermute(value, 'tensor', [(i, i ^ 1) for i in range(parts)])]
    ppermute x7, starting transfers between devices: 7.71 us -> 9.8 us  [to_chip(): lax.ppermute(value, 'tensor', [(i, i ^ k * CORES) for i in range(parts)])]
    ppermute x13 -> x9, starting transfers between devices: 3.17 us -> 1.59 us  [to_other_core(): return lax.ppermute(value, 'tensor', [(i, i ^ 1) for i in range(parts)])]
  transfers between devices with their start and end apart: 36 -> 32, of which waited for: 15 -> 12; matrix products, arithmetic and copies ran while one was open for 0% -> 0% of each run, Pallas kernels for 22% -> 18%
where the time goes in v14:
time: 132 us; the launch traced here: 131 us
  waiting for transfers between devices  59 us (45%)
  starting transfers between devices  36.7 us (28%)
  Pallas kernels  33.6 us (25%)
    ppermute x7, waiting for transfers between devices, to_chip(): lax.ppermute(value, 'tensor', [(i, i ^ k * CORES) for i in range(parts)])  20.6 us
    ppermute x2, waiting for transfers between devices, across_dp(): return lax.ppermute(value, 'dp', [(i, i ^ k) for i in range(owners)])  17 us
    ppermute x2, waiting for transfers between devices, spread(): outer_3 = lax.ppermute(inner_2, 'dp', [(1, 0), (2, 3)])  10.6 us
    ppermute x7, starting transfers between devices, to_chip(): lax.ppermute(value, 'tensor', [(i, i ^ k * CORES) for i in range(parts)])  9.8 us
    pallas_call x4, Pallas kernels, split_product(): pl.pallas_call(functools.partial(split_product_kernel, each, half, part *...  9.3 us
    pallas_call x1, Pallas kernels, load_weight(): pl.pallas_call(load_weight_kernel, grid=(1,), in_specs=[pl.BlockSpec(memo...  5.89 us
    ppermute x1, starting transfers between devices, first(): lax.ppermute(inward, 'dp', [(3, 2), (0, 1)])  4.96 us
    ppermute x2, starting transfers between devices, spread(): outer = lax.ppermute(home, 'dp', [(0, 1), (1, 0), (2, 3), (3, 2)])  4.39 us
  transfers between devices with their start and end apart: 32, of which 12 were waited for; matrix products, arithmetic and copies ran while one was open for 0% of the time, Pallas kernels for 18%

profile of v14, /device:TPU:0, one launch (start us, length us, event | category | flops | bytes accessed | tf_op | source)
XLA Modules:
  0.0 131.5 jit_solution(12581478881995070728)
XLA Ops:
  1.5 1.8 %first_hop.1 = (bf16[128,2048]{1,0:T(8,128)(2,1)S(1)}, bf16[128,2048]{1,0:T(8,128)(2,1)S(1)}) custom-call(s32[14]{0:T(128)S(1)} %concatenate.3.index_ref.refs_0_, bf16[384,2048]{1,0:T(8,128)(2,1)} %tokens_ref.9), custom_call_target="tpu_custom_call" | custom-call | flops 1 | bytes 1 | tf_op jit(solution)/shard_map/first_hop/pallas_call | solution.py:191
  3.3 5.0 %collective-permute-start.4 = (bf16[128,2048]{1,0:T(8,128)(2,1)S(1)}, bf16[128,2048]{1,0:T(8,128)(2,1)S(1)}, u32[]{:S(2)}, u32[]{:S(2)}) collective-permute-start(bf16[128,2048]{1,0:T(8,128)(2,1)S(1)} %get-tuple-element.27.refs_0_), channel_id=1, source_target_pairs={{12,8},{0,4},{13,9},{1,5},{14,10},{2,6},{15,11},{3,7},{28,24},{16,... | collective-permute-start | bytes 1572872 | tf_op jit(solution)/shard_map/ppermute | solution.py:220
  9.0 3.5 %narrow.1 = (f32[2,1,64,128]{3,2,1,0:T(8,128)S(1)}, f32[2,1,64,128]{3,2,1,0:T(8,128)S(1)}, f32[1,64,128]{2,1,0:T(8,128)S(1)}) custom-call(s32[14]{0:T(128)S(1)} %concatenate.3.index_ref.refs_0_, bf16[384,2048]{1,0:T(8,128)(2,1)} %tokens_ref.9, bf16[1,64,2048]{2,1,0:T(8,128)(2,1)} %bitcast.7, bf16[128,4096]{1,0:T(8,128)(2,1)} %cot_ref.3, ...), custom_call_target="tpu_custom_call" | custom-call | flops 1 | bytes 1 | tf_op jit(solution)/shard_map/narrow/pallas_call | solution.py:374
  15.3 2.4 %collective-permute-done.1.refs_0_ = f32[1,64,128]{2,1,0:T(8,128)S(1)} collective-permute-done((f32[1,64,128]{2,1,0:T(8,128)S(1)}, f32[1,64,128]{2,1,0:T(8,128)S(1)}, u32[]{:S(2)}, u32[]{:S(2)}) %collective-permute-start.1) | collective-permute-done | bytes 32800 | tf_op jit(solution)/shard_map/ppermute | solution.py:636
  17.8 4.3 %collective-permute-done.2 = f32[2,1,64,128]{3,2,1,0:T(8,128)S(1)} collective-permute-done((f32[2,1,64,128]{3,2,1,0:T(8,128)S(1)}, f32[2,1,64,128]{3,2,1,0:T(8,128)S(1)}, u32[]{:S(2)}, u32[]{:S(2)}) %collective-permute-start.2) | collective-permute-done | bytes 65568 | tf_op jit(solution)/shard_map/ppermute | solution.py:639
  22.8 3.2 %collective-permute-start.6 = (bf16[128,2048]{1,0:T(8,128)(2,1)S(1)}, bf16[128,2048]{1,0:T(8,128)(2,1)S(1)}, u32[]{:S(2)}, u32[]{:S(2)}) collective-permute-start(bf16[128,2048]{1,0:T(8,128)(2,1)S(1)} %get-tuple-element.33), channel_id=1, source_target_pairs={{4,0},{0,4},{12,8},{5,1},{1,5},{13,9},{6,2},{2,6},{14,10},{7,3},{3... | collective-permute-start | bytes 1572872 | tf_op jit(solution)/shard_map/ppermute | solution.py:230
  26.7 3.5 %collective-permute-start.3 = (f32[2,1,64,128]{3,2,1,0:T(8,128)S(1)}, f32[2,1,64,128]{3,2,1,0:T(8,128)S(1)}, u32[]{:S(2)}, u32[]{:S(2)}) collective-permute-start(f32[2,1,64,128]{3,2,1,0:T(8,128)S(1)} %add.31.sum_ref.refs_0_), channel_id=1, source_target_pairs={{0,8},{4,12},{8,0},{12,4},{1,9},{5,13},{9,1},{13,5},{2,10},{6,14},... | collective-permute-start | bytes 196616 | tf_op jit(solution)/shard_map/ppermute | solution.py:639
  30.2 12.7 %collective-permute-done.3.refs_0_ = f32[2,1,64,128]{3,2,1,0:T(8,128)S(1)} collective-permute-done((f32[2,1,64,128]{3,2,1,0:T(8,128)S(1)}, f32[2,1,64,128]{3,2,1,0:T(8,128)S(1)}, u32[]{:S(2)}, u32[]{:S(2)}) %collective-permute-start.3) | collective-permute-done | bytes 65568 | tf_op jit(solution)/shard_map/ppermute | solution.py:639
  45.1 4.3 %collective-permute-start.13 = (bf16[64,2048]{1,0:T(8,128)(2,1)S(1)}, bf16[64,2048]{1,0:T(8,128)(2,1)S(1)}, u32[]{:S(2)}, u32[]{:S(2)}) collective-permute-start(bf16[64,2048]{1,0:T(8,128)(2,1)S(1)} %get-tuple-element.36.home_ref), channel_id=1, source_target_pairs={{0,4},{4,0},{8,12},{12,8},{1,5},{5,1},{9,13},{13,9},{2,6},{6,2},{1... | collective-permute-start | bytes 786440 | tf_op jit(solution)/shard_map/ppermute | solution.py:240
  50.1 3.1 %collective-permute-done.8.outer_ref = bf16[64,2048]{1,0:T(8,128)(2,1)S(1)} collective-permute-done((bf16[64,2048]{1,0:T(8,128)(2,1)S(1)}, bf16[64,2048]{1,0:T(8,128)(2,1)S(1)}, u32[]{:S(2)}, u32[]{:S(2)}) %collective-permute-start.8) | collective-permute-done | bytes 262176 | tf_op jit(solution)/shard_map/ppermute | solution.py:240
  60.1 5.9 %load_weight.1.refs_6_.w_ref = bf16[2048,4096]{1,0:T(8,128)(2,1)S(1)} custom-call(bf16[2048,4096]{1,0:T(8,128)(2,1)} %w_ref.1, bf16[64,2048]{1,0:T(8,128)(2,1)S(1)} %collective-permute-done.13.refs_0_.outer_ref, bf16[64,2048]{1,0:T(8,128)(2,1)S(1)} %collective-permute-done.15.refs_1_.refs_0_), custom_call_target="tpu_custom_call" | custom-call | flops 1 | bytes 1 | tf_op jit(solution)/shard_map/load_weight/pallas_call | solution.py:284
  66.0 4.3 %collective-permute-done.16.refs_5_.refs_2_ = bf16[64,2048]{1,0:T(8,128)(2,1)S(1)} collective-permute-done((bf16[64,2048]{1,0:T(8,128)(2,1)S(1)}, bf16[64,2048]{1,0:T(8,128)(2,1)S(1)}, u32[]{:S(2)}, u32[]{:S(2)}) %collective-permute-start.16) | collective-permute-done | bytes 262176 | tf_op jit(solution)/shard_map/ppermute | solution.py:242
  70.3 3.4 %collective-permute-done.12.refs_3_ = bf16[64,2048]{1,0:T(8,128)(2,1)S(1)} collective-permute-done((bf16[64,2048]{1,0:T(8,128)(2,1)S(1)}, bf16[64,2048]{1,0:T(8,128)(2,1)S(1)}, u32[]{:S(2)}, u32[]{:S(2)}) %collective-permute-start.12) | collective-permute-done | bytes 262176 | tf_op jit(solution)/shard_map/ppermute | solution.py:244
  74.4 2.3 %split_product.5 = (bf16[128,2048]{1,0:T(8,128)(2,1)S(1)}, f32[64,2048]{1,0:T(8,128)S(1)}, f32[64,2048]{1,0:T(8,128)S(1)}) custom-call(bf16[256,2048]{1,0:T(8,128)(2,1)S(1)} %collect.2.rows_ref, bf16[2048,4096]{1,0:T(8,128)(2,1)S(1)} %load_weight.1.refs_6_.w_ref, bf16[1,64,4096]{2,1,0:T(8,128)(2,1)S(1)} %collective-permute-done.20.refs_0_.refs_1_), custom_call_target="tpu_custom_call" | custom-call | flops 1 | bytes 1 | tf_op jit(solution)/shard_map/split_product/pallas_call | solution.py:316
  76.8 2.3 %split_product.4 = (bf16[128,2048]{1,0:T(8,128)(2,1)S(1)}, f32[64,2048]{1,0:T(8,128)S(1)}, f32[64,2048]{1,0:T(8,128)S(1)}) custom-call(bf16[256,2048]{1,0:T(8,128)(2,1)S(1)} %collect.2.rows_ref, bf16[2048,4096]{1,0:T(8,128)(2,1)S(1)} %load_weight.1.refs_6_.w_ref), custom_call_target="tpu_custom_call" | custom-call | flops 1 | bytes 1 | tf_op jit(solution)/shard_map/split_product/pallas_call | solution.py:316
  82.6 7.2 %collective-permute-done.19.refs_3_ = bf16[64,2048]{1,0:T(8,128)(2,1)S(1)} collective-permute-done((bf16[64,2048]{1,0:T(8,128)(2,1)S(1)}, bf16[64,2048]{1,0:T(8,128)(2,1)S(1)}, u32[]{:S(2)}, u32[]{:S(2)}) %collective-permute-start.19) | collective-permute-done | bytes 262176 | tf_op jit(solution)/shard_map/ppermute | solution.py:244
  90.5 2.3 %split_product.7 = (bf16[128,2048]{1,0:T(8,128)(2,1)S(1)}, f32[64,2048]{1,0:T(8,128)S(1)}, f32[64,2048]{1,0:T(8,128)S(1)}) custom-call(bf16[256,2048]{1,0:T(8,128)(2,1)S(1)} %collect.3.rows_ref, bf16[2048,4096]{1,0:T(8,128)(2,1)S(1)} %load_weight.1.refs_6_.w_ref, bf16[64,2048]{1,0:T(8,128)(2,1)S(1)} %collective-permute-done.24.refs_0_.refs_5_), custom_call_target="tpu_custom_call" | custom-call | flops 1 | bytes 1 | tf_op jit(solution)/shard_map/split_product/pallas_call | solution.py:316
  94.4 7.2 %collective-permute-done.18.refs_0_.refs_5_ = bf16[64,2048]{1,0:T(8,128)(2,1)S(1)} collective-permute-done((bf16[64,2048]{1,0:T(8,128)(2,1)S(1)}, bf16[64,2048]{1,0:T(8,128)(2,1)S(1)}, u32[]{:S(2)}, u32[]{:S(2)}) %collective-permute-start.18) | collective-permute-done | bytes 262176 | tf_op jit(solution)/shard_map/ppermute | solution.py:636
  101.6 2.3 %split_product.6 = (bf16[128,2048]{1,0:T(8,128)(2,1)S(1)}, f32[64,2048]{1,0:T(8,128)S(1)}, f32[64,2048]{1,0:T(8,128)S(1)}) custom-call(bf16[256,2048]{1,0:T(8,128)(2,1)S(1)} %collect.3.rows_ref, bf16[2048,4096]{1,0:T(8,128)(2,1)S(1)} %load_weight.1.refs_6_.w_ref, bf16[64,2048]{1,0:T(8,128)(2,1)S(1)} %collective-permute-done.18.refs_0_.refs_5_), custom_call_target="tpu_custom_call" | custom-call | flops 1 | bytes 1 | tf_op jit(solution)/shard_map/split_product/pallas_call | solution.py:316
  108.3 11.0 %collective-permute-done.29.refs_1_ = bf16[1,64,128]{2,1,0:T(8,128)(2,1)S(1)} collective-permute-done((bf16[1,64,128]{2,1,0:T(8,128)(2,1)S(1)}, bf16[1,64,128]{2,1,0:T(8,128)(2,1)S(1)}, u32[]{:S(2)}, u32[]{:S(2)}) %collective-permute-start.29) | collective-permute-done | bytes 16416 | tf_op jit(solution)/shard_map/ppermute | solution.py:636
  121.7 1.6 %down_gradient.1.refs_10_ = f32[1,64,2048]{2,1,0:T(8,128)} custom-call(s32[14]{0:T(128)S(1)} %concatenate.3.index_ref.refs_0_, bf16[384,2048]{1,0:T(8,128)(2,1)S(1)} %copy-done, bf16[1,64,128]{2,1,0:T(8,128)(2,1)S(1)} %get-tuple-element.50.refs_0_, bf16[1,64,128]{2,1,0:T(8,128)(2,1)S(1)} %collective-permute-done.29.refs_1_, ...), custom_call_target="tpu_custom_call" | custom-call | flops 1 | bytes 1 | tf_op jit(solution)/shard_map/down_gradient/pallas_call | solution.py:483
  123.3 3.9 %up_gradient.1.refs_9_ = f32[4,64,4096]{2,1,0:T(8,128)} custom-call(s32[14]{0:T(128)S(1)} %concatenate.3.index_ref.refs_0_, bf16[1,64,4096]{2,1,0:T(8,128)(2,1)S(1)} %get-tuple-element.40.refs_0_, bf16[1,64,4096]{2,1,0:T(8,128)(2,1)S(1)} %collective-permute-done.20.refs_0_.refs_1_, bf16[1,64,4096]{2,1,0:T(8,128)(2,1)S(1)} %collective-permute-done.27.refs_2_, ...), custom_call_target="tpu_custom_call" | custom-call | flops 1 | bytes 1 | tf_op jit(solution)/shard_map/up_gradient/pallas_call | solution.py:524
  127.2 2.1 %finish.2.refs_9_ = bf16[128,4096]{1,0:T(8,128)(2,1)} custom-call(s32[14]{0:T(128)S(1)} %concatenate.3.index_ref.refs_0_, bf16[1,64,128]{2,1,0:T(8,128)(2,1)S(1)} %get-tuple-element.31.refs_0_.refs_1_, bf16[4,64,4096]{2,1,0:T(8,128)(2,1)S(1)} %copy-done.1, f32[64,2048]{1,0:T(8,128)S(1)} %get-tuple-element.46.refs_3_, ...), custom_call_target="tpu_custom_call" | custom-call | flops 1 | bytes 1 | tf_op jit(solution)/shard_map/finish/pallas_call | solution.py:594
  129.3 2.1 %finish.3 = bf16[128,4096]{1,0:T(8,128)(2,1)} custom-call(s32[14]{0:T(128)S(1)} %concatenate.3.index_ref.refs_0_, bf16[1,64,128]{2,1,0:T(8,128)(2,1)S(1)} %get-tuple-element.31.refs_0_.refs_1_, bf16[4,64,4096]{2,1,0:T(8,128)(2,1)S(1)} %copy-done.1, f32[64,2048]{1,0:T(8,128)S(1)} %get-tuple-element.37.refs_3_, ...), custom_call_target="tpu_custom_call", output_to_operand_aliasing={{}: (9, {})} | custom-call | flops 1 | bytes 1 | tf_op jit(solution)/shard_map/finish/pallas_call | solution.py:594
  (70 shorter events, 28.7 us)
Async XLA Ops:
  3.3 18.8 %collective-permute-start.4 = (bf16[128,2048]{1,0:T(8,128)(2,1)S(1)}, bf16[128,2048]{1,0:T(8,128)(2,1)S(1)}, u32[]{:S(2)}, u32[]{:S(2)}) collective-permute-start(bf16[128,2048]{1,0:T(8,128)(2,1)S(1)} %get-tuple-element.27.refs_0_), channel_id=1, source_target_pairs={{12,8},{0,4},{13,9},{1,5},{14,10},{2,6},{15,11},{3,7},{28,24},{16,... | collective-permute-start | bytes 1572872 | tf_op jit(solution)/shard_map/ppermute | solution.py:220
  8.3 13.9 %collective-permute-start.5 = (bf16[128,2048]{1,0:T(8,128)(2,1)S(1)}, bf16[128,2048]{1,0:T(8,128)(2,1)S(1)}, u32[]{:S(2)}, u32[]{:S(2)}) collective-permute-start(bf16[128,2048]{1,0:T(8,128)(2,1)S(1)} %get-tuple-element.32), channel_id=1, source_target_pairs={{8,4},{9,5},{10,6},{11,7},{24,20},{25,21},{26,22},{27,23}} | collective-permute-start | bytes 1572872 | tf_op jit(solution)/shard_map/ppermute | solution.py:221
  22.8 21.0 %collective-permute-start.6 = (bf16[128,2048]{1,0:T(8,128)(2,1)S(1)}, bf16[128,2048]{1,0:T(8,128)(2,1)S(1)}, u32[]{:S(2)}, u32[]{:S(2)}) collective-permute-start(bf16[128,2048]{1,0:T(8,128)(2,1)S(1)} %get-tuple-element.33), channel_id=1, source_target_pairs={{4,0},{0,4},{12,8},{5,1},{1,5},{13,9},{6,2},{2,6},{14,10},{7,3},{3... | collective-permute-start | bytes 1572872 | tf_op jit(solution)/shard_map/ppermute | solution.py:230
  25.9 17.8 %collective-permute-start.7 = (bf16[128,2048]{1,0:T(8,128)(2,1)S(1)}, bf16[128,2048]{1,0:T(8,128)(2,1)S(1)}, u32[]{:S(2)}, u32[]{:S(2)}) collective-permute-start(bf16[128,2048]{1,0:T(8,128)(2,1)S(1)} %get-tuple-element.34), channel_id=1, source_target_pairs={{8,4},{4,8},{9,5},{5,9},{10,6},{6,10},{11,7},{7,11},{24,20},{20,24... | collective-permute-start | bytes 1572872 | tf_op jit(solution)/shard_map/ppermute | solution.py:231
  26.7 16.2 %collective-permute-start.3 = (f32[2,1,64,128]{3,2,1,0:T(8,128)S(1)}, f32[2,1,64,128]{3,2,1,0:T(8,128)S(1)}, u32[]{:S(2)}, u32[]{:S(2)}) collective-permute-start(f32[2,1,64,128]{3,2,1,0:T(8,128)S(1)} %add.31.sum_ref.refs_0_), channel_id=1, source_target_pairs={{0,8},{4,12},{8,0},{12,4},{1,9},{5,13},{9,1},{13,5},{2,10},{6,14},... | collective-permute-start | bytes 196616 | tf_op jit(solution)/shard_map/ppermute | solution.py:639
  44.4 8.9 %collective-permute-start.8 = (bf16[64,2048]{1,0:T(8,128)(2,1)S(1)}, bf16[64,2048]{1,0:T(8,128)(2,1)S(1)}, u32[]{:S(2)}, u32[]{:S(2)}) collective-permute-start(bf16[64,2048]{1,0:T(8,128)(2,1)S(1)} %get-tuple-element.35.home_ref), channel_id=1, source_target_pairs={{0,4},{4,0},{8,12},{12,8},{1,5},{5,1},{9,13},{13,9},{2,6},{6,2},{1... | collective-permute-start | bytes 786440 | tf_op jit(solution)/shard_map/ppermute | solution.py:240
  44.5 11.0 %collective-permute-start.9 = (bf16[64,2048]{1,0:T(8,128)(2,1)S(1)}, bf16[64,2048]{1,0:T(8,128)(2,1)S(1)}, u32[]{:S(2)}, u32[]{:S(2)}) collective-permute-start(bf16[64,2048]{1,0:T(8,128)(2,1)S(1)} %get-tuple-element.35.home_ref), channel_id=1, source_target_pairs={{4,8},{8,4},{5,9},{9,5},{6,10},{10,6},{7,11},{11,7},{20,24},{24,20... | collective-permute-start | bytes 786440 | tf_op jit(solution)/shard_map/ppermute | solution.py:241
  45.1 11.6 %collective-permute-start.13 = (bf16[64,2048]{1,0:T(8,128)(2,1)S(1)}, bf16[64,2048]{1,0:T(8,128)(2,1)S(1)}, u32[]{:S(2)}, u32[]{:S(2)}) collective-permute-start(bf16[64,2048]{1,0:T(8,128)(2,1)S(1)} %get-tuple-element.36.home_ref), channel_id=1, source_target_pairs={{0,4},{4,0},{8,12},{12,8},{1,5},{5,1},{9,13},{13,9},{2,6},{6,2},{1... | collective-permute-start | bytes 786440 | tf_op jit(solution)/shard_map/ppermute | solution.py:240
  49.5 8.0 %collective-permute-start.15 = (bf16[64,2048]{1,0:T(8,128)(2,1)S(1)}, bf16[64,2048]{1,0:T(8,128)(2,1)S(1)}, u32[]{:S(2)}, u32[]{:S(2)}) collective-permute-start(bf16[64,2048]{1,0:T(8,128)(2,1)S(1)} %get-tuple-element.36.home_ref), channel_id=1, source_target_pairs={{4,8},{8,4},{5,9},{9,5},{6,10},{10,6},{7,11},{11,7},{20,24},{24,20... | collective-permute-start | bytes 786440 | tf_op jit(solution)/shard_map/ppermute | solution.py:241
  53.2 5.5 %collective-permute-start.10 = (bf16[64,2048]{1,0:T(8,128)(2,1)S(1)}, bf16[64,2048]{1,0:T(8,128)(2,1)S(1)}, u32[]{:S(2)}, u32[]{:S(2)}) collective-permute-start(bf16[64,2048]{1,0:T(8,128)(2,1)S(1)} %collective-permute-done.8.outer_ref), channel_id=1, source_target_pairs={{4,8},{8,4},{5,9},{9,5},{6,10},{10,6},{7,11},{11,7},{20,24},{24,20... | collective-permute-start | bytes 786440 | tf_op jit(solution)/shard_map/ppermute | solution.py:243
  53.9 20.5 %collective-permute-start.20 = (bf16[1,64,4096]{2,1,0:T(8,128)(2,1)S(1)}, bf16[1,64,4096]{2,1,0:T(8,128)(2,1)S(1)}, u32[]{:S(2)}, u32[]{:S(2)}) collective-permute-start(bf16[1,64,4096]{2,1,0:T(8,128)(2,1)S(1)} %get-tuple-element.40.refs_0_), channel_id=1, source_target_pairs={{0,2},{1,3},{2,0},{3,1},{4,6},{5,7},{6,4},{7,5},{8,10},{9,11},{10,... | collective-permute-start | bytes 1572872 | tf_op jit(solution)/shard_map/ppermute | solution.py:636
  55.5 10.5 %collective-permute-start.11 = (bf16[64,2048]{1,0:T(8,128)(2,1)S(1)}, bf16[64,2048]{1,0:T(8,128)(2,1)S(1)}, u32[]{:S(2)}, u32[]{:S(2)}) collective-permute-start(bf16[64,2048]{1,0:T(8,128)(2,1)S(1)} %collective-permute-done.9.refs_0_), channel_id=1, source_target_pairs={{4,0},{8,12},{5,1},{9,13},{6,2},{10,14},{7,3},{11,15},{20,16},{24,... | collective-permute-start | bytes 786440 | tf_op jit(solution)/shard_map/ppermute | solution.py:242
  56.8 9.2 %collective-permute-start.14 = (bf16[64,2048]{1,0:T(8,128)(2,1)S(1)}, bf16[64,2048]{1,0:T(8,128)(2,1)S(1)}, u32[]{:S(2)}, u32[]{:S(2)}) collective-permute-start(bf16[64,2048]{1,0:T(8,128)(2,1)S(1)} %collective-permute-done.13.refs_0_.outer_ref), channel_id=1, source_target_pairs={{4,8},{8,4},{5,9},{9,5},{6,10},{10,6},{7,11},{11,7},{20,24},{24,20... | collective-permute-start | bytes 786440 | tf_op jit(solution)/shard_map/ppermute | solution.py:243
  57.5 12.9 %collective-permute-start.16 = (bf16[64,2048]{1,0:T(8,128)(2,1)S(1)}, bf16[64,2048]{1,0:T(8,128)(2,1)S(1)}, u32[]{:S(2)}, u32[]{:S(2)}) collective-permute-start(bf16[64,2048]{1,0:T(8,128)(2,1)S(1)} %collective-permute-done.15.refs_1_.refs_0_), channel_id=1, source_target_pairs={{4,0},{8,12},{5,1},{9,13},{6,2},{10,14},{7,3},{11,15},{20,16},{24,... | collective-permute-start | bytes 786440 | tf_op jit(solution)/shard_map/ppermute | solution.py:242
  58.8 15.0 %collective-permute-start.12 = (bf16[64,2048]{1,0:T(8,128)(2,1)S(1)}, bf16[64,2048]{1,0:T(8,128)(2,1)S(1)}, u32[]{:S(2)}, u32[]{:S(2)}) collective-permute-start(bf16[64,2048]{1,0:T(8,128)(2,1)S(1)} %collective-permute-done.10.refs_1_), channel_id=1, source_target_pairs={{4,0},{8,12},{5,1},{9,13},{6,2},{10,14},{7,3},{11,15},{20,16},{24,... | collective-permute-start | bytes 786440 | tf_op jit(solution)/shard_map/ppermute | solution.py:244
  79.7 10.1 %collective-permute-start.19 = (bf16[64,2048]{1,0:T(8,128)(2,1)S(1)}, bf16[64,2048]{1,0:T(8,128)(2,1)S(1)}, u32[]{:S(2)}, u32[]{:S(2)}) collective-permute-start(bf16[64,2048]{1,0:T(8,128)(2,1)S(1)} %collective-permute-done.14.refs_4_.refs_1_), channel_id=1, source_target_pairs={{4,0},{8,12},{5,1},{9,13},{6,2},{10,14},{7,3},{11,15},{20,16},{24,... | collective-permute-start | bytes 786440 | tf_op jit(solution)/shard_map/ppermute | solution.py:244
  81.0 9.4 %collective-permute-start.24 = (bf16[64,2048]{1,0:T(8,128)(2,1)S(1)}, bf16[64,2048]{1,0:T(8,128)(2,1)S(1)}, u32[]{:S(2)}, u32[]{:S(2)}) collective-permute-start(bf16[64,2048]{1,0:T(8,128)(2,1)S(1)} %add_convert_fusion.2.refs_4_), channel_id=1, source_target_pairs={{0,2},{1,3},{2,0},{3,1},{4,6},{5,7},{6,4},{7,5},{8,10},{9,11},{10,... | collective-permute-start | bytes 786440 | tf_op jit(solution)/shard_map/ppermute | solution.py:636
  92.8 11.8 %collective-permute-start.25 = (bf16[128,2048]{1,0:T(8,128)(2,1)S(1)}, bf16[128,2048]{1,0:T(8,128)(2,1)S(1)}, u32[]{:S(2)}, u32[]{:S(2)}) collective-permute-start(bf16[128,2048]{1,0:T(8,128)(2,1)S(1)} %get-tuple-element.48), channel_id=1, source_target_pairs={{0,1},{1,0},{2,3},{3,2},{4,5},{5,4},{6,7},{7,6},{8,9},{9,8},{10,11... | collective-permute-start | bytes 1572872 | tf_op jit(solution)/shard_map/ppermute | solution.py:633
  92.9 8.7 %collective-permute-start.18 = (bf16[64,2048]{1,0:T(8,128)(2,1)S(1)}, bf16[64,2048]{1,0:T(8,128)(2,1)S(1)}, u32[]{:S(2)}, u32[]{:S(2)}) collective-permute-start(bf16[64,2048]{1,0:T(8,128)(2,1)S(1)} %add_convert_fusion.3.refs_5_), channel_id=1, source_target_pairs={{0,2},{1,3},{2,0},{3,1},{4,6},{5,7},{6,4},{7,5},{8,10},{9,11},{10,... | collective-permute-start | bytes 786440 | tf_op jit(solution)/shard_map/ppermute | solution.py:636
  104.0 19.3 %collective-permute-start.27 = (bf16[1,64,4096]{2,1,0:T(8,128)(2,1)S(1)}, bf16[1,64,4096]{2,1,0:T(8,128)(2,1)S(1)}, u32[]{:S(2)}, u32[]{:S(2)}) collective-permute-start(bf16[1,64,4096]{2,1,0:T(8,128)(2,1)S(1)} %get-tuple-element.40.refs_0_), channel_id=1, source_target_pairs={{0,1},{1,0},{2,3},{3,2},{4,5},{5,4},{6,7},{7,6},{8,9},{9,8},{10,11... | collective-permute-start | bytes 1572872 | tf_op jit(solution)/shard_map/ppermute | solution.py:633
  104.5 18.8 %collective-permute-start.28 = (bf16[1,64,4096]{2,1,0:T(8,128)(2,1)S(1)}, bf16[1,64,4096]{2,1,0:T(8,128)(2,1)S(1)}, u32[]{:S(2)}, u32[]{:S(2)}) collective-permute-start(bf16[1,64,4096]{2,1,0:T(8,128)(2,1)S(1)} %collective-permute-done.20.refs_0_.refs_1_), channel_id=1, source_target_pairs={{0,1},{1,0},{2,3},{3,2},{4,5},{5,4},{6,7},{7,6},{8,9},{9,8},{10,11... | collective-permute-start | bytes 1572872 | tf_op jit(solution)/shard_map/ppermute | solution.py:633
  104.6 22.6 %collective-permute-start.26 = (bf16[64,2048]{1,0:T(8,128)(2,1)S(1)}, bf16[64,2048]{1,0:T(8,128)(2,1)S(1)}, u32[]{:S(2)}, u32[]{:S(2)}) collective-permute-start(bf16[64,2048]{1,0:T(8,128)(2,1)S(1)} %add_convert_fusion), channel_id=1, source_target_pairs={{0,2},{1,3},{2,0},{3,1},{4,6},{5,7},{6,4},{7,5},{8,10},{9,11},{10,... | collective-permute-start | bytes 786440 | tf_op jit(solution)/shard_map/ppermute | solution.py:636
  106.2 23.1 %collective-permute-start.23 = (bf16[64,2048]{1,0:T(8,128)(2,1)S(1)}, bf16[64,2048]{1,0:T(8,128)(2,1)S(1)}, u32[]{:S(2)}, u32[]{:S(2)}) collective-permute-start(bf16[64,2048]{1,0:T(8,128)(2,1)S(1)} %add_convert_fusion.1), channel_id=1, source_target_pairs={{0,2},{1,3},{2,0},{3,1},{4,6},{5,7},{6,4},{7,5},{8,10},{9,11},{10,... | collective-permute-start | bytes 786440 | tf_op jit(solution)/shard_map/ppermute | solution.py:636
  107.5 11.8 %collective-permute-start.29 = (bf16[1,64,128]{2,1,0:T(8,128)(2,1)S(1)}, bf16[1,64,128]{2,1,0:T(8,128)(2,1)S(1)}, u32[]{:S(2)}, u32[]{:S(2)}) collective-permute-start(bf16[1,64,128]{2,1,0:T(8,128)(2,1)S(1)} %get-tuple-element.50.refs_0_), channel_id=1, source_target_pairs={{0,2},{1,3},{2,0},{3,1},{4,6},{5,7},{6,4},{7,5},{8,10},{9,11},{10,... | collective-permute-start | bytes 49160 | tf_op jit(solution)/shard_map/ppermute | solution.py:636
  (11 other events, 97.1 us)

commit v15 on v13

--- a/solution.py
+++ b/solution.py
@@ -726,7 +726,7 @@
         ready = [done[0][1]]
         waits = [
             [*sums[-1][0][2:], *back_rows[1:chips]],
-            [*sums[-1][1][2:], *back_rows[chips:], *pieces[chips:]],
+            [*back_rows[chips:], *pieces[chips:]],
         ]
     up_grad = up_gradient(index_of, index, adapter_count, pieces)
     down_grad = down_gradient(index_of, index, tokens, back_rows)

time: 120 us -> 117 us (0.975)
  waiting for transfers between devices: 47.6 us -> 42.9 us
  starting transfers between devices: 36.1 us -> 37.7 us
    ppermute x13, waiting for transfers between devices: 5.65 us -> 2.46 us  [to_other_core(): return lax.ppermute(value, 'tensor', [(i, i ^ 1) for i in range(parts)])]
    ppermute x7, starting transfers between devices: 7.71 us -> 9.67 us  [to_chip(): lax.ppermute(value, 'tensor', [(i, i ^ k * CORES) for i in range(parts)])]
    ppermute x7, waiting for transfers between devices: 9.53 us -> 8.16 us  [to_chip(): lax.ppermute(value, 'tensor', [(i, i ^ k * CORES) for i in range(parts)])]
  transfers between devices with their start and end apart: 36 -> 36, of which waited for: 15 -> 13; matrix products, arithmetic and copies ran while one was open for 0% -> 0% of each run, Pallas kernels for 22% -> 23%
where the time goes in v15:
time: 117 us
  waiting for transfers between devices  42.9 us (37%)
  starting transfers between devices  37.7 us (32%)
  Pallas kernels  34 us (29%)
    ppermute x2, waiting for transfers between devices, across_dp(): return lax.ppermute(value, 'dp', [(i, i ^ k) for i in range(owners)])  17 us
    ppermute x7, starting transfers between devices, to_chip(): lax.ppermute(value, 'tensor', [(i, i ^ k * CORES) for i in range(parts)])  9.67 us
    pallas_call x4, Pallas kernels, split_product(): pl.pallas_call(functools.partial(split_product_kernel, each, half, part *...  9.29 us
    ppermute x7, waiting for transfers between devices, to_chip(): lax.ppermute(value, 'tensor', [(i, i ^ k * CORES) for i in range(parts)])  8.16 us
    ppermute x2, waiting for transfers between devices, spread(): outer_3 = lax.ppermute(inner_2, 'dp', [(1, 0), (2, 3)])  7.88 us
    pallas_call x1, Pallas kernels, load_weight(): pl.pallas_call(load_weight_kernel, grid=(1,), in_specs=[pl.BlockSpec(memo...  5.89 us
    ppermute x1, starting transfers between devices, first(): lax.ppermute(inward, 'dp', [(3, 2), (0, 1)])  4.96 us
    ppermute x2, starting transfers between devices, spread(): outer = lax.ppermute(home, 'dp', [(0, 1), (1, 0), (2, 3), (3, 2)])  4.39 us
  transfers between devices with their start and end apart: 36, of which 13 were waited for; matrix products, arithmetic and copies ran while one was open for 0% of the time, Pallas kernels for 23%

profile of v15, /device:TPU:0, one launch (start us, length us, event | category | flops | bytes accessed | tf_op | source)
XLA Modules:
  0.0 116.8 jit_solution(1195842932053530159)
XLA Ops:
  1.5 1.8 %first_hop.1 = (bf16[128,2048]{1,0:T(8,128)(2,1)S(1)}, bf16[128,2048]{1,0:T(8,128)(2,1)S(1)}) custom-call(s32[14]{0:T(128)S(1)} %concatenate.3.index_ref.refs_0_, bf16[384,2048]{1,0:T(8,128)(2,1)} %tokens_ref.9), custom_call_target="tpu_custom_call" | custom-call | flops 1 | bytes 1 | tf_op jit(solution)/shard_map/first_hop/pallas_call | solution.py:191
  3.3 5.0 %collective-permute-start.4 = (bf16[128,2048]{1,0:T(8,128)(2,1)S(1)}, bf16[128,2048]{1,0:T(8,128)(2,1)S(1)}, u32[]{:S(2)}, u32[]{:S(2)}) collective-permute-start(bf16[128,2048]{1,0:T(8,128)(2,1)S(1)} %get-tuple-element.31.refs_0_), channel_id=1, source_target_pairs={{12,8},{0,4},{13,9},{1,5},{14,10},{2,6},{15,11},{3,7},{28,24},{16,... | collective-permute-start | bytes 1572872 | tf_op jit(solution)/shard_map/ppermute | solution.py:220
  9.0 3.5 %narrow.1 = (f32[2,1,64,128]{3,2,1,0:T(8,128)S(1)}, f32[2,1,64,128]{3,2,1,0:T(8,128)S(1)}, f32[1,64,128]{2,1,0:T(8,128)S(1)}) custom-call(s32[14]{0:T(128)S(1)} %concatenate.3.index_ref.refs_0_, bf16[384,2048]{1,0:T(8,128)(2,1)} %tokens_ref.9, bf16[1,64,2048]{2,1,0:T(8,128)(2,1)} %bitcast.7, bf16[128,4096]{1,0:T(8,128)(2,1)} %cot_ref.3, ...), custom_call_target="tpu_custom_call" | custom-call | flops 1 | bytes 1 | tf_op jit(solution)/shard_map/narrow/pallas_call | solution.py:376
  15.3 2.4 %collective-permute-done.1.refs_0_ = f32[1,64,128]{2,1,0:T(8,128)S(1)} collective-permute-done((f32[1,64,128]{2,1,0:T(8,128)S(1)}, f32[1,64,128]{2,1,0:T(8,128)S(1)}, u32[]{:S(2)}, u32[]{:S(2)}) %collective-permute-start.1) | collective-permute-done | bytes 32800 | tf_op jit(solution)/shard_map/ppermute | solution.py:638
  17.8 4.3 %collective-permute-done.2 = f32[2,1,64,128]{3,2,1,0:T(8,128)S(1)} collective-permute-done((f32[2,1,64,128]{3,2,1,0:T(8,128)S(1)}, f32[2,1,64,128]{3,2,1,0:T(8,128)S(1)}, u32[]{:S(2)}, u32[]{:S(2)}) %collective-permute-start.2) | collective-permute-done | bytes 65568 | tf_op jit(solution)/shard_map/ppermute | solution.py:641
  22.8 3.2 %collective-permute-start.6 = (bf16[128,2048]{1,0:T(8,128)(2,1)S(1)}, bf16[128,2048]{1,0:T(8,128)(2,1)S(1)}, u32[]{:S(2)}, u32[]{:S(2)}) collective-permute-start(bf16[128,2048]{1,0:T(8,128)(2,1)S(1)} %get-tuple-element.37), channel_id=1, source_target_pairs={{4,0},{0,4},{12,8},{5,1},{1,5},{13,9},{6,2},{2,6},{14,10},{7,3},{3... | collective-permute-start | bytes 1572872 | tf_op jit(solution)/shard_map/ppermute | solution.py:230
  26.7 3.5 %collective-permute-start.3 = (f32[2,1,64,128]{3,2,1,0:T(8,128)S(1)}, f32[2,1,64,128]{3,2,1,0:T(8,128)S(1)}, u32[]{:S(2)}, u32[]{:S(2)}) collective-permute-start(f32[2,1,64,128]{3,2,1,0:T(8,128)S(1)} %add.31.sum_ref.refs_0_), channel_id=1, source_target_pairs={{0,8},{4,12},{8,0},{12,4},{1,9},{5,13},{9,1},{13,5},{2,10},{6,14},... | collective-permute-start | bytes 196616 | tf_op jit(solution)/shard_map/ppermute | solution.py:641
  30.2 12.7 %collective-permute-done.3.refs_0_ = f32[2,1,64,128]{3,2,1,0:T(8,128)S(1)} collective-permute-done((f32[2,1,64,128]{3,2,1,0:T(8,128)S(1)}, f32[2,1,64,128]{3,2,1,0:T(8,128)S(1)}, u32[]{:S(2)}, u32[]{:S(2)}) %collective-permute-start.3) | collective-permute-done | bytes 65568 | tf_op jit(solution)/shard_map/ppermute | solution.py:641
  45.1 4.3 %collective-permute-start.13 = (bf16[64,2048]{1,0:T(8,128)(2,1)S(1)}, bf16[64,2048]{1,0:T(8,128)(2,1)S(1)}, u32[]{:S(2)}, u32[]{:S(2)}) collective-permute-start(bf16[64,2048]{1,0:T(8,128)(2,1)S(1)} %get-tuple-element.40.home_ref), channel_id=1, source_target_pairs={{0,4},{4,0},{8,12},{12,8},{1,5},{5,1},{9,13},{13,9},{2,6},{6,2},{1... | collective-permute-start | bytes 786440 | tf_op jit(solution)/shard_map/ppermute | solution.py:240
  50.1 3.1 %collective-permute-done.8.outer_ref = bf16[64,2048]{1,0:T(8,128)(2,1)S(1)} collective-permute-done((bf16[64,2048]{1,0:T(8,128)(2,1)S(1)}, bf16[64,2048]{1,0:T(8,128)(2,1)S(1)}, u32[]{:S(2)}, u32[]{:S(2)}) %collective-permute-start.8) | collective-permute-done | bytes 262176 | tf_op jit(solution)/shard_map/ppermute | solution.py:240
  60.1 5.9 %load_weight.1.refs_6_.w_ref = bf16[2048,4096]{1,0:T(8,128)(2,1)S(1)} custom-call(bf16[2048,4096]{1,0:T(8,128)(2,1)} %w_ref.1, bf16[64,2048]{1,0:T(8,128)(2,1)S(1)} %collective-permute-done.13.refs_0_.outer_ref, bf16[64,2048]{1,0:T(8,128)(2,1)S(1)} %collective-permute-done.15.refs_1_.refs_0_), custom_call_target="tpu_custom_call" | custom-call | flops 1 | bytes 1 | tf_op jit(solution)/shard_map/load_weight/pallas_call | solution.py:284
  66.0 4.3 %collective-permute-done.16.refs_5_.refs_2_ = bf16[64,2048]{1,0:T(8,128)(2,1)S(1)} collective-permute-done((bf16[64,2048]{1,0:T(8,128)(2,1)S(1)}, bf16[64,2048]{1,0:T(8,128)(2,1)S(1)}, u32[]{:S(2)}, u32[]{:S(2)}) %collective-permute-start.16) | collective-permute-done | bytes 262176 | tf_op jit(solution)/shard_map/ppermute | solution.py:242
  70.3 3.4 %collective-permute-done.12.refs_3_ = bf16[64,2048]{1,0:T(8,128)(2,1)S(1)} collective-permute-done((bf16[64,2048]{1,0:T(8,128)(2,1)S(1)}, bf16[64,2048]{1,0:T(8,128)(2,1)S(1)}, u32[]{:S(2)}, u32[]{:S(2)}) %collective-permute-start.12) | collective-permute-done | bytes 262176 | tf_op jit(solution)/shard_map/ppermute | solution.py:244
  74.4 2.3 %split_product.5 = (bf16[64,2048]{1,0:T(8,128)(2,1)S(1)}, bf16[64,2048]{1,0:T(8,128)(2,1)S(1)}, f32[64,2048]{1,0:T(8,128)S(1)}, f32[64,2048]{1,0:T(8,128)S(1)}) custom-call(bf16[256,2048]{1,0:T(8,128)(2,1)S(1)} %collect.2.rows_ref, bf16[2048,4096]{1,0:T(8,128)(2,1)S(1)} %load_weight.1.refs_6_.w_ref, ...), custom_call_target="tpu_custom_call" | custom-call | flops 1 | bytes 1 | tf_op jit(solution)/shard_map/split_product/pallas_call | solution.py:317
  79.9 2.3 %split_product.4 = (bf16[64,2048]{1,0:T(8,128)(2,1)S(1)}, bf16[64,2048]{1,0:T(8,128)(2,1)S(1)}, f32[64,2048]{1,0:T(8,128)S(1)}, f32[64,2048]{1,0:T(8,128)S(1)}) custom-call(bf16[256,2048]{1,0:T(8,128)(2,1)S(1)} %collect.2.rows_ref, bf16[2048,4096]{1,0:T(8,128)(2,1)S(1)} %load_weight.1.refs_6_.w_ref), custom_call_target="tpu_custom_call" | custom-call | flops 1 | bytes 1 | tf_op jit(solution)/shard_map/split_product/pallas_call | solution.py:317
  82.9 4.5 %collective-permute-done.20.refs_3_ = bf16[64,2048]{1,0:T(8,128)(2,1)S(1)} collective-permute-done((bf16[64,2048]{1,0:T(8,128)(2,1)S(1)}, bf16[64,2048]{1,0:T(8,128)(2,1)S(1)}, u32[]{:S(2)}, u32[]{:S(2)}) %collective-permute-start.20) | collective-permute-done | bytes 262176 | tf_op jit(solution)/shard_map/ppermute | solution.py:244
  89.5 1.6 %collective-permute-done.24.refs_1_ = bf16[1,64,128]{2,1,0:T(8,128)(2,1)S(1)} collective-permute-done((bf16[1,64,128]{2,1,0:T(8,128)(2,1)S(1)}, bf16[1,64,128]{2,1,0:T(8,128)(2,1)S(1)}, u32[]{:S(2)}, u32[]{:S(2)}) %collective-permute-start.24) | collective-permute-done | bytes 16416 | tf_op jit(solution)/shard_map/ppermute | solution.py:638
  91.6 2.3 %split_product.7 = (bf16[64,2048]{1,0:T(8,128)(2,1)S(1)}, bf16[64,2048]{1,0:T(8,128)(2,1)S(1)}, f32[64,2048]{1,0:T(8,128)S(1)}, f32[64,2048]{1,0:T(8,128)S(1)}) custom-call(bf16[256,2048]{1,0:T(8,128)(2,1)S(1)} %collect.3.rows_ref, bf16[2048,4096]{1,0:T(8,128)(2,1)S(1)} %load_weight.1.refs_6_.w_ref, ...), custom_call_target="tpu_custom_call" | custom-call | flops 1 | bytes 1 | tf_op jit(solution)/shard_map/split_product/pallas_call | solution.py:317
  96.3 2.3 %split_product.6 = (bf16[64,2048]{1,0:T(8,128)(2,1)S(1)}, bf16[64,2048]{1,0:T(8,128)(2,1)S(1)}, f32[64,2048]{1,0:T(8,128)S(1)}, f32[64,2048]{1,0:T(8,128)S(1)}) custom-call(bf16[256,2048]{1,0:T(8,128)(2,1)S(1)} %collect.3.rows_ref, bf16[2048,4096]{1,0:T(8,128)(2,1)S(1)} %load_weight.1.refs_6_.w_ref, ...), custom_call_target="tpu_custom_call" | custom-call | flops 1 | bytes 1 | tf_op jit(solution)/shard_map/split_product/pallas_call | solution.py:317
  102.5 2.0 %down_gradient.1.refs_10_ = f32[1,64,2048]{2,1,0:T(8,128)} custom-call(s32[14]{0:T(128)S(1)} %concatenate.3.index_ref.refs_0_, bf16[384,2048]{1,0:T(8,128)(2,1)S(1)} %copy-done, bf16[1,64,128]{2,1,0:T(8,128)(2,1)S(1)} %get-tuple-element.48.refs_0_, bf16[1,64,128]{2,1,0:T(8,128)(2,1)S(1)} %collective-permute-done.24.refs_1_, ...), custom_call_target="tpu_custom_call" | custom-call | flops 1 | bytes 1 | tf_op jit(solution)/shard_map/down_gradient/pallas_call | solution.py:485
  104.5 3.9 %up_gradient.1.refs_9_ = f32[4,64,4096]{2,1,0:T(8,128)} custom-call(s32[14]{0:T(128)S(1)} %concatenate.3.index_ref.refs_0_, bf16[1,64,4096]{2,1,0:T(8,128)(2,1)S(1)} %get-tuple-element.45.refs_0_, bf16[1,64,4096]{2,1,0:T(8,128)(2,1)S(1)} %collective-permute-done.21.refs_0_.refs_1_, bf16[1,64,4096]{2,1,0:T(8,128)(2,1)S(1)} %collective-permute-done.26.refs_2_, ...), custom_call_target="tpu_custom_call" | custom-call | flops 1 | bytes 1 | tf_op jit(solution)/shard_map/up_gradient/pallas_call | solution.py:526
  109.5 2.1 %finish.2.refs_9_ = bf16[128,4096]{1,0:T(8,128)(2,1)} custom-call(s32[14]{0:T(128)S(1)} %concatenate.3.index_ref.refs_0_, bf16[1,64,128]{2,1,0:T(8,128)(2,1)S(1)} %get-tuple-element.35.refs_0_.refs_1_, bf16[4,64,4096]{2,1,0:T(8,128)(2,1)S(1)} %copy-done.1, f32[64,2048]{1,0:T(8,128)S(1)} %get-tuple-element.53.refs_3_, ...), custom_call_target="tpu_custom_call" | custom-call | flops 1 | bytes 1 | tf_op jit(solution)/shard_map/finish/pallas_call | solution.py:596
  111.6 3.0 %collective-permute-done.30.refs_8_ = bf16[64,2048]{1,0:T(8,128)(2,1)S(1)} collective-permute-done((bf16[64,2048]{1,0:T(8,128)(2,1)S(1)}, bf16[64,2048]{1,0:T(8,128)(2,1)S(1)}, u32[]{:S(2)}, u32[]{:S(2)}) %collective-permute-start.30) | collective-permute-done | bytes 262176 | tf_op jit(solution)/shard_map/ppermute | solution.py:638
  114.7 2.1 %finish.3 = bf16[128,4096]{1,0:T(8,128)(2,1)} custom-call(s32[14]{0:T(128)S(1)} %concatenate.3.index_ref.refs_0_, bf16[1,64,128]{2,1,0:T(8,128)(2,1)S(1)} %get-tuple-element.35.refs_0_.refs_1_, bf16[4,64,4096]{2,1,0:T(8,128)(2,1)S(1)} %copy-done.1, f32[64,2048]{1,0:T(8,128)S(1)} %get-tuple-element.41.refs_3_, ...), custom_call_target="tpu_custom_call", output_to_operand_aliasing={{}: (9, {})} | custom-call | flops 1 | bytes 1 | tf_op jit(solution)/shard_map/finish/pallas_call | solution.py:596
  (78 shorter events, 29.8 us)
Async XLA Ops:
  3.3 18.8 %collective-permute-start.4 = (bf16[128,2048]{1,0:T(8,128)(2,1)S(1)}, bf16[128,2048]{1,0:T(8,128)(2,1)S(1)}, u32[]{:S(2)}, u32[]{:S(2)}) collective-permute-start(bf16[128,2048]{1,0:T(8,128)(2,1)S(1)} %get-tuple-element.31.refs_0_), channel_id=1, source_target_pairs={{12,8},{0,4},{13,9},{1,5},{14,10},{2,6},{15,11},{3,7},{28,24},{16,... | collective-permute-start | bytes 1572872 | tf_op jit(solution)/shard_map/ppermute | solution.py:220
  8.3 13.9 %collective-permute-start.5 = (bf16[128,2048]{1,0:T(8,128)(2,1)S(1)}, bf16[128,2048]{1,0:T(8,128)(2,1)S(1)}, u32[]{:S(2)}, u32[]{:S(2)}) collective-permute-start(bf16[128,2048]{1,0:T(8,128)(2,1)S(1)} %get-tuple-element.36), channel_id=1, source_target_pairs={{8,4},{9,5},{10,6},{11,7},{24,20},{25,21},{26,22},{27,23}} | collective-permute-start | bytes 1572872 | tf_op jit(solution)/shard_map/ppermute | solution.py:221
  22.8 21.0 %collective-permute-start.6 = (bf16[128,2048]{1,0:T(8,128)(2,1)S(1)}, bf16[128,2048]{1,0:T(8,128)(2,1)S(1)}, u32[]{:S(2)}, u32[]{:S(2)}) collective-permute-start(bf16[128,2048]{1,0:T(8,128)(2,1)S(1)} %get-tuple-element.37), channel_id=1, source_target_pairs={{4,0},{0,4},{12,8},{5,1},{1,5},{13,9},{6,2},{2,6},{14,10},{7,3},{3... | collective-permute-start | bytes 1572872 | tf_op jit(solution)/shard_map/ppermute | solution.py:230
  25.9 17.8 %collective-permute-start.7 = (bf16[128,2048]{1,0:T(8,128)(2,1)S(1)}, bf16[128,2048]{1,0:T(8,128)(2,1)S(1)}, u32[]{:S(2)}, u32[]{:S(2)}) collective-permute-start(bf16[128,2048]{1,0:T(8,128)(2,1)S(1)} %get-tuple-element.38), channel_id=1, source_target_pairs={{8,4},{4,8},{9,5},{5,9},{10,6},{6,10},{11,7},{7,11},{24,20},{20,24... | collective-permute-start | bytes 1572872 | tf_op jit(solution)/shard_map/ppermute | solution.py:231
  26.7 16.2 %collective-permute-start.3 = (f32[2,1,64,128]{3,2,1,0:T(8,128)S(1)}, f32[2,1,64,128]{3,2,1,0:T(8,128)S(1)}, u32[]{:S(2)}, u32[]{:S(2)}) collective-permute-start(f32[2,1,64,128]{3,2,1,0:T(8,128)S(1)} %add.31.sum_ref.refs_0_), channel_id=1, source_target_pairs={{0,8},{4,12},{8,0},{12,4},{1,9},{5,13},{9,1},{13,5},{2,10},{6,14},... | collective-permute-start | bytes 196616 | tf_op jit(solution)/shard_map/ppermute | solution.py:641
  44.4 8.9 %collective-permute-start.8 = (bf16[64,2048]{1,0:T(8,128)(2,1)S(1)}, bf16[64,2048]{1,0:T(8,128)(2,1)S(1)}, u32[]{:S(2)}, u32[]{:S(2)}) collective-permute-start(bf16[64,2048]{1,0:T(8,128)(2,1)S(1)} %get-tuple-element.39.home_ref), channel_id=1, source_target_pairs={{0,4},{4,0},{8,12},{12,8},{1,5},{5,1},{9,13},{13,9},{2,6},{6,2},{1... | collective-permute-start | bytes 786440 | tf_op jit(solution)/shard_map/ppermute | solution.py:240
  44.5 11.0 %collective-permute-start.9 = (bf16[64,2048]{1,0:T(8,128)(2,1)S(1)}, bf16[64,2048]{1,0:T(8,128)(2,1)S(1)}, u32[]{:S(2)}, u32[]{:S(2)}) collective-permute-start(bf16[64,2048]{1,0:T(8,128)(2,1)S(1)} %get-tuple-element.39.home_ref), channel_id=1, source_target_pairs={{4,8},{8,4},{5,9},{9,5},{6,10},{10,6},{7,11},{11,7},{20,24},{24,20... | collective-permute-start | bytes 786440 | tf_op jit(solution)/shard_map/ppermute | solution.py:241
  45.1 11.6 %collective-permute-start.13 = (bf16[64,2048]{1,0:T(8,128)(2,1)S(1)}, bf16[64,2048]{1,0:T(8,128)(2,1)S(1)}, u32[]{:S(2)}, u32[]{:S(2)}) collective-permute-start(bf16[64,2048]{1,0:T(8,128)(2,1)S(1)} %get-tuple-element.40.home_ref), channel_id=1, source_target_pairs={{0,4},{4,0},{8,12},{12,8},{1,5},{5,1},{9,13},{13,9},{2,6},{6,2},{1... | collective-permute-start | bytes 786440 | tf_op jit(solution)/shard_map/ppermute | solution.py:240
  49.5 8.0 %collective-permute-start.15 = (bf16[64,2048]{1,0:T(8,128)(2,1)S(1)}, bf16[64,2048]{1,0:T(8,128)(2,1)S(1)}, u32[]{:S(2)}, u32[]{:S(2)}) collective-permute-start(bf16[64,2048]{1,0:T(8,128)(2,1)S(1)} %get-tuple-element.40.home_ref), channel_id=1, source_target_pairs={{4,8},{8,4},{5,9},{9,5},{6,10},{10,6},{7,11},{11,7},{20,24},{24,20... | collective-permute-start | bytes 786440 | tf_op jit(solution)/shard_map/ppermute | solution.py:241
  53.9 20.5 %collective-permute-start.21 = (bf16[1,64,4096]{2,1,0:T(8,128)(2,1)S(1)}, bf16[1,64,4096]{2,1,0:T(8,128)(2,1)S(1)}, u32[]{:S(2)}, u32[]{:S(2)}) collective-permute-start(bf16[1,64,4096]{2,1,0:T(8,128)(2,1)S(1)} %get-tuple-element.45.refs_0_), channel_id=1, source_target_pairs={{0,2},{1,3},{2,0},{3,1},{4,6},{5,7},{6,4},{7,5},{8,10},{9,11},{10,... | collective-permute-start | bytes 1572872 | tf_op jit(solution)/shard_map/ppermute | solution.py:638
  55.5 10.5 %collective-permute-start.11 = (bf16[64,2048]{1,0:T(8,128)(2,1)S(1)}, bf16[64,2048]{1,0:T(8,128)(2,1)S(1)}, u32[]{:S(2)}, u32[]{:S(2)}) collective-permute-start(bf16[64,2048]{1,0:T(8,128)(2,1)S(1)} %collective-permute-done.9.refs_0_), channel_id=1, source_target_pairs={{4,0},{8,12},{5,1},{9,13},{6,2},{10,14},{7,3},{11,15},{20,16},{24,... | collective-permute-start | bytes 786440 | tf_op jit(solution)/shard_map/ppermute | solution.py:242
  56.8 9.2 %collective-permute-start.14 = (bf16[64,2048]{1,0:T(8,128)(2,1)S(1)}, bf16[64,2048]{1,0:T(8,128)(2,1)S(1)}, u32[]{:S(2)}, u32[]{:S(2)}) collective-permute-start(bf16[64,2048]{1,0:T(8,128)(2,1)S(1)} %collective-permute-done.13.refs_0_.outer_ref), channel_id=1, source_target_pairs={{4,8},{8,4},{5,9},{9,5},{6,10},{10,6},{7,11},{11,7},{20,24},{24,20... | collective-permute-start | bytes 786440 | tf_op jit(solution)/shard_map/ppermute | solution.py:243
  57.5 12.9 %collective-permute-start.16 = (bf16[64,2048]{1,0:T(8,128)(2,1)S(1)}, bf16[64,2048]{1,0:T(8,128)(2,1)S(1)}, u32[]{:S(2)}, u32[]{:S(2)}) collective-permute-start(bf16[64,2048]{1,0:T(8,128)(2,1)S(1)} %collective-permute-done.15.refs_1_.refs_0_), channel_id=1, source_target_pairs={{4,0},{8,12},{5,1},{9,13},{6,2},{10,14},{7,3},{11,15},{20,16},{24,... | collective-permute-start | bytes 786440 | tf_op jit(solution)/shard_map/ppermute | solution.py:242
  58.8 15.0 %collective-permute-start.12 = (bf16[64,2048]{1,0:T(8,128)(2,1)S(1)}, bf16[64,2048]{1,0:T(8,128)(2,1)S(1)}, u32[]{:S(2)}, u32[]{:S(2)}) collective-permute-start(bf16[64,2048]{1,0:T(8,128)(2,1)S(1)} %collective-permute-done.10.refs_1_), channel_id=1, source_target_pairs={{4,0},{8,12},{5,1},{9,13},{6,2},{10,14},{7,3},{11,15},{20,16},{24,... | collective-permute-start | bytes 786440 | tf_op jit(solution)/shard_map/ppermute | solution.py:244
  76.8 10.6 %collective-permute-start.20 = (bf16[64,2048]{1,0:T(8,128)(2,1)S(1)}, bf16[64,2048]{1,0:T(8,128)(2,1)S(1)}, u32[]{:S(2)}, u32[]{:S(2)}) collective-permute-start(bf16[64,2048]{1,0:T(8,128)(2,1)S(1)} %collective-permute-done.14.refs_4_.refs_1_), channel_id=1, source_target_pairs={{4,0},{8,12},{5,1},{9,13},{6,2},{10,14},{7,3},{11,15},{20,16},{24,... | collective-permute-start | bytes 786440 | tf_op jit(solution)/shard_map/ppermute | solution.py:244
  78.4 12.7 %collective-permute-start.32 = (bf16[64,2048]{1,0:T(8,128)(2,1)S(1)}, bf16[64,2048]{1,0:T(8,128)(2,1)S(1)}, u32[]{:S(2)}, u32[]{:S(2)}) collective-permute-start(bf16[64,2048]{1,0:T(8,128)(2,1)S(1)} %add_convert_fusion.2.refs_4_), channel_id=1, source_target_pairs={{0,2},{1,3},{2,0},{3,1},{4,6},{5,7},{6,4},{7,5},{8,10},{9,11},{10,... | collective-permute-start | bytes 786440 | tf_op jit(solution)/shard_map/ppermute | solution.py:638
  82.3 11.7 %collective-permute-start.18 = (bf16[64,2048]{1,0:T(8,128)(2,1)S(1)}, bf16[64,2048]{1,0:T(8,128)(2,1)S(1)}, u32[]{:S(2)}, u32[]{:S(2)}) collective-permute-start(bf16[64,2048]{1,0:T(8,128)(2,1)S(1)} %get-tuple-element.44), channel_id=1, source_target_pairs={{0,1},{1,0},{2,3},{3,2},{4,5},{5,4},{6,7},{7,6},{8,9},{9,8},{10,11... | collective-permute-start | bytes 786440 | tf_op jit(solution)/shard_map/ppermute | solution.py:635
  82.3 12.4 %collective-permute-start.26 = (bf16[1,64,4096]{2,1,0:T(8,128)(2,1)S(1)}, bf16[1,64,4096]{2,1,0:T(8,128)(2,1)S(1)}, u32[]{:S(2)}, u32[]{:S(2)}) collective-permute-start(bf16[1,64,4096]{2,1,0:T(8,128)(2,1)S(1)} %get-tuple-element.45.refs_0_), channel_id=1, source_target_pairs={{0,1},{1,0},{2,3},{3,2},{4,5},{5,4},{6,7},{7,6},{8,9},{9,8},{10,11... | collective-permute-start | bytes 1572872 | tf_op jit(solution)/shard_map/ppermute | solution.py:635
  82.8 13.4 %collective-permute-start.27 = (bf16[1,64,4096]{2,1,0:T(8,128)(2,1)S(1)}, bf16[1,64,4096]{2,1,0:T(8,128)(2,1)S(1)}, u32[]{:S(2)}, u32[]{:S(2)}) collective-permute-start(bf16[1,64,4096]{2,1,0:T(8,128)(2,1)S(1)} %collective-permute-done.21.refs_0_.refs_1_), channel_id=1, source_target_pairs={{0,1},{1,0},{2,3},{3,2},{4,5},{5,4},{6,7},{7,6},{8,9},{9,8},{10,11... | collective-permute-start | bytes 1572872 | tf_op jit(solution)/shard_map/ppermute | solution.py:635
  94.1 17.5 %collective-permute-start.17 = (bf16[64,2048]{1,0:T(8,128)(2,1)S(1)}, bf16[64,2048]{1,0:T(8,128)(2,1)S(1)}, u32[]{:S(2)}, u32[]{:S(2)}) collective-permute-start(bf16[64,2048]{1,0:T(8,128)(2,1)S(1)} %get-tuple-element.42), channel_id=1, source_target_pairs={{0,1},{1,0},{2,3},{3,2},{4,5},{5,4},{6,7},{7,6},{8,9},{9,8},{10,11... | collective-permute-start | bytes 786440 | tf_op jit(solution)/shard_map/ppermute | solution.py:635
  94.8 16.9 %collective-permute-start.19 = (bf16[64,2048]{1,0:T(8,128)(2,1)S(1)}, bf16[64,2048]{1,0:T(8,128)(2,1)S(1)}, u32[]{:S(2)}, u32[]{:S(2)}) collective-permute-start(bf16[64,2048]{1,0:T(8,128)(2,1)S(1)} %add_convert_fusion.3), channel_id=1, source_target_pairs={{0,2},{1,3},{2,0},{3,1},{4,6},{5,7},{6,4},{7,5},{8,10},{9,11},{10,... | collective-permute-start | bytes 786440 | tf_op jit(solution)/shard_map/ppermute | solution.py:638
  100.2 9.3 %collective-permute-start.35 = (bf16[64,2048]{1,0:T(8,128)(2,1)S(1)}, bf16[64,2048]{1,0:T(8,128)(2,1)S(1)}, u32[]{:S(2)}, u32[]{:S(2)}) collective-permute-start(bf16[64,2048]{1,0:T(8,128)(2,1)S(1)} %add_convert_fusion), channel_id=1, source_target_pairs={{0,2},{1,3},{2,0},{3,1},{4,6},{5,7},{6,4},{7,5},{8,10},{9,11},{10,... | collective-permute-start | bytes 786440 | tf_op jit(solution)/shard_map/ppermute | solution.py:638
  100.8 10.8 %collective-permute-start.28 = (bf16[64,2048]{1,0:T(8,128)(2,1)S(1)}, bf16[64,2048]{1,0:T(8,128)(2,1)S(1)}, u32[]{:S(2)}, u32[]{:S(2)}) collective-permute-start(bf16[64,2048]{1,0:T(8,128)(2,1)S(1)} %get-tuple-element.50), channel_id=1, source_target_pairs={{0,1},{1,0},{2,3},{3,2},{4,5},{5,4},{6,7},{7,6},{8,9},{9,8},{10,11... | collective-permute-start | bytes 786440 | tf_op jit(solution)/shard_map/ppermute | solution.py:635
  100.9 13.7 %collective-permute-start.30 = (bf16[64,2048]{1,0:T(8,128)(2,1)S(1)}, bf16[64,2048]{1,0:T(8,128)(2,1)S(1)}, u32[]{:S(2)}, u32[]{:S(2)}) collective-permute-start(bf16[64,2048]{1,0:T(8,128)(2,1)S(1)} %add_convert_fusion.1), channel_id=1, source_target_pairs={{0,2},{1,3},{2,0},{3,1},{4,6},{5,7},{6,4},{7,5},{8,10},{9,11},{10,... | collective-permute-start | bytes 786440 | tf_op jit(solution)/shard_map/ppermute | solution.py:638
  (15 other events, 105.7 us)

commit v16 on v15

--- a/solution.py
+++ b/solution.py
@@ -457,6 +457,25 @@
         cost_estimate=BRIEF,
         name="pieces",
     )(index, *operands, *extra)
+
+
+def hand_on_kernel(count, *refs):
+    for source, target in zip(refs[:count], refs[-count:]):
+        target[...] = source[...]
+
+
+def hand_on(values, waits):
+    specs, extra = after(waits)
+    return pl.pallas_call(
+        functools.partial(hand_on_kernel, len(values)),
+        grid=(1,),
+        in_specs=[held()] * len(values) + specs,
+        out_specs=[held()] * len(values),
+        out_shape=[pltpu.VMEM(v.shape, v.dtype) for v in values],
+        compiler_params=SMALL,
+        cost_estimate=BRIEF,
+        name="hand_on",
+    )(*[in_vmem(v) for v in values], *extra)
 
 
 def down_gradient_kernel(index_of, index_ref, tokens_ref, *refs):
@@ -682,7 +701,7 @@
         relay.settle([lowered])
         weight = load_weight(frozen_up_weight, relay.arrived[-1][1:3])
         pieces = with_other_core(same_core(pieces))
-        back_rows = with_other_core(same_core(back_rows))
+        back_rows = same_core(back_rows)
         ahead = [v for chunk in relay.arrived[1:] for v in chunk[3:5]]
         ahead.append(weight)
         chunks = [lambda waits: relay.rows(0, ahead)]
@@ -696,7 +715,7 @@
             index_of, index, shape, total, more, cotangent, []
         )
         pieces = with_other_core(same_core(pieces))
-        back_rows = with_other_core(same_core(back_rows))
+        back_rows = same_core(back_rows)
         every_slot = lax.all_gather(
             tokens.reshape(CAP, BLK, width_dev), "dp", axis=0, tiled=True
         )
@@ -717,17 +736,14 @@
         across = [to_chip(outgoing[(k - 1) * each : k * each], k) for k in range(1, chips)]
         return [own, to_other_core(send_own)] + across, outgoing
 
-    sums, ready = [], ()
-    waits = [pieces[1:chips], ()]
-    for chunk in chunks:
-        rows = chunk(ready)
-        done = [summed(rows, part, waits[part]) for part in range(PARTS)]
-        sums.append([terms for terms, _ in done])
-        ready = [done[0][1]]
-        waits = [
-            [*sums[-1][0][2:], *back_rows[1:chips]],
-            [*back_rows[chips:], *pieces[chips:]],
-        ]
+    first = chunks[0](())
+    first_0 = summed(first, 0, pieces[1:chips])
+    first_1 = summed(first, 1, ())
+    back_rows = with_other_core(list(hand_on(back_rows, first_1[0][2:])))
+    second = chunks[1]([first_0[1]])
+    second_0 = summed(second, 0, back_rows[1:chips])
+    second_1 = summed(second, 1, [*first_0[0][2:], *back_rows[chips:]])
+    sums = [[first_0[0], first_1[0]], [second_0[0], second_1[0]]]
     up_grad = up_gradient(index_of, index, adapter_count, pieces)
     down_grad = down_gradient(index_of, index, tokens, back_rows)
     projected = None

time: 117 us -> 118 us (level)
  waiting for transfers between devices: 42.9 us -> 45.2 us
  starting transfers between devices: 37.7 us -> 36.5 us
    ppermute x7, waiting for transfers between devices: 8.16 us -> 10.2 us  [to_chip(): lax.ppermute(value, 'tensor', [(i, i ^ k * CORES) for i in range(parts)])]
    ppermute x7, starting transfers between devices: 9.67 us -> 8.09 us  [to_chip(): lax.ppermute(value, 'tensor', [(i, i ^ k * CORES) for i in range(parts)])]
  transfers between devices with their start and end apart: 36 -> 36, of which waited for: 13 -> 14; matrix products, arithmetic and copies ran while one was open for 0% -> 0% of each run, Pallas kernels for 23% -> 24%
where the time goes in v16:
time: 118 us; the launch traced here: 117 us
  waiting for transfers between devices  45.2 us (38%)
  starting transfers between devices  36.5 us (31%)
  Pallas kernels  33.6 us (28%)
    ppermute x2, waiting for transfers between devices, across_dp(): return lax.ppermute(value, 'dp', [(i, i ^ k) for i in range(owners)])  17 us
    ppermute x7, waiting for transfers between devices, to_chip(): lax.ppermute(value, 'tensor', [(i, i ^ k * CORES) for i in range(parts)])  10.2 us
    pallas_call x4, Pallas kernels, split_product(): pl.pallas_call(functools.partial(split_product_kernel, each, half, part *...  9.3 us
    ppermute x7, starting transfers between devices, to_chip(): lax.ppermute(value, 'tensor', [(i, i ^ k * CORES) for i in range(parts)])  8.09 us
    ppermute x2, waiting for transfers between devices, spread(): outer_3 = lax.ppermute(inner_2, 'dp', [(1, 0), (2, 3)])  7.53 us
    pallas_call x1, Pallas kernels, load_weight(): pl.pallas_call(load_weight_kernel, grid=(1,), in_specs=[pl.BlockSpec(memo...  5.89 us
    ppermute x1, starting transfers between devices, first(): lax.ppermute(inward, 'dp', [(3, 2), (0, 1)])  5 us
    ppermute x2, starting transfers between devices, spread(): outer = lax.ppermute(home, 'dp', [(0, 1), (1, 0), (2, 3), (3, 2)])  4.36 us
  transfers between devices with their start and end apart: 36, of which 14 were waited for; matrix products, arithmetic and copies ran while one was open for 0% of the time, Pallas kernels for 24%

profile of v16, /device:TPU:0, one launch (start us, length us, event | category | flops | bytes accessed | tf_op | source)
XLA Modules:
  0.0 117.5 jit_solution(14337807627622388772)
XLA Ops:
  1.5 1.8 %first_hop.1 = (bf16[128,2048]{1,0:T(8,128)(2,1)S(1)}, bf16[128,2048]{1,0:T(8,128)(2,1)S(1)}) custom-call(s32[14]{0:T(128)S(1)} %concatenate.3.index_ref.refs_0_, bf16[384,2048]{1,0:T(8,128)(2,1)} %tokens_ref.9), custom_call_target="tpu_custom_call" | custom-call | flops 1 | bytes 1 | tf_op jit(solution)/shard_map/first_hop/pallas_call | solution.py:191
  3.3 5.0 %collective-permute-start.4 = (bf16[128,2048]{1,0:T(8,128)(2,1)S(1)}, bf16[128,2048]{1,0:T(8,128)(2,1)S(1)}, u32[]{:S(2)}, u32[]{:S(2)}) collective-permute-start(bf16[128,2048]{1,0:T(8,128)(2,1)S(1)} %get-tuple-element.33.refs_0_), channel_id=1, source_target_pairs={{12,8},{0,4},{13,9},{1,5},{14,10},{2,6},{15,11},{3,7},{28,24},{16,... | collective-permute-start | bytes 1572872 | tf_op jit(solution)/shard_map/ppermute | solution.py:220
  9.0 3.5 %narrow.1 = (f32[2,1,64,128]{3,2,1,0:T(8,128)S(1)}, f32[2,1,64,128]{3,2,1,0:T(8,128)S(1)}, f32[1,64,128]{2,1,0:T(8,128)S(1)}) custom-call(s32[14]{0:T(128)S(1)} %concatenate.3.index_ref.refs_0_, bf16[384,2048]{1,0:T(8,128)(2,1)} %tokens_ref.9, bf16[1,64,2048]{2,1,0:T(8,128)(2,1)} %bitcast.7, bf16[128,4096]{1,0:T(8,128)(2,1)} %cot_ref.3, ...), custom_call_target="tpu_custom_call" | custom-call | flops 1 | bytes 1 | tf_op jit(solution)/shard_map/narrow/pallas_call | solution.py:376
  15.4 2.4 %collective-permute-done.1.refs_0_ = f32[1,64,128]{2,1,0:T(8,128)S(1)} collective-permute-done((f32[1,64,128]{2,1,0:T(8,128)S(1)}, f32[1,64,128]{2,1,0:T(8,128)S(1)}, u32[]{:S(2)}, u32[]{:S(2)}) %collective-permute-start.1) | collective-permute-done | bytes 32800 | tf_op jit(solution)/shard_map/ppermute | solution.py:657
  17.9 4.3 %collective-permute-done.2 = f32[2,1,64,128]{3,2,1,0:T(8,128)S(1)} collective-permute-done((f32[2,1,64,128]{3,2,1,0:T(8,128)S(1)}, f32[2,1,64,128]{3,2,1,0:T(8,128)S(1)}, u32[]{:S(2)}, u32[]{:S(2)}) %collective-permute-start.2) | collective-permute-done | bytes 65568 | tf_op jit(solution)/shard_map/ppermute | solution.py:660
  22.8 3.2 %collective-permute-start.6 = (bf16[128,2048]{1,0:T(8,128)(2,1)S(1)}, bf16[128,2048]{1,0:T(8,128)(2,1)S(1)}, u32[]{:S(2)}, u32[]{:S(2)}) collective-permute-start(bf16[128,2048]{1,0:T(8,128)(2,1)S(1)} %get-tuple-element.39), channel_id=1, source_target_pairs={{4,0},{0,4},{12,8},{5,1},{1,5},{13,9},{6,2},{2,6},{14,10},{7,3},{3... | collective-permute-start | bytes 1572872 | tf_op jit(solution)/shard_map/ppermute | solution.py:230
  26.7 3.5 %collective-permute-start.3 = (f32[2,1,64,128]{3,2,1,0:T(8,128)S(1)}, f32[2,1,64,128]{3,2,1,0:T(8,128)S(1)}, u32[]{:S(2)}, u32[]{:S(2)}) collective-permute-start(f32[2,1,64,128]{3,2,1,0:T(8,128)S(1)} %add.31.sum_ref.refs_0_), channel_id=1, source_target_pairs={{0,8},{4,12},{8,0},{12,4},{1,9},{5,13},{9,1},{13,5},{2,10},{6,14},... | collective-permute-start | bytes 196616 | tf_op jit(solution)/shard_map/ppermute | solution.py:660
  30.2 12.7 %collective-permute-done.3.refs_0_ = f32[2,1,64,128]{3,2,1,0:T(8,128)S(1)} collective-permute-done((f32[2,1,64,128]{3,2,1,0:T(8,128)S(1)}, f32[2,1,64,128]{3,2,1,0:T(8,128)S(1)}, u32[]{:S(2)}, u32[]{:S(2)}) %collective-permute-start.3) | collective-permute-done | bytes 65568 | tf_op jit(solution)/shard_map/ppermute | solution.py:660
  45.2 4.3 %collective-permute-start.13 = (bf16[64,2048]{1,0:T(8,128)(2,1)S(1)}, bf16[64,2048]{1,0:T(8,128)(2,1)S(1)}, u32[]{:S(2)}, u32[]{:S(2)}) collective-permute-start(bf16[64,2048]{1,0:T(8,128)(2,1)S(1)} %get-tuple-element.42.home_ref), channel_id=1, source_target_pairs={{0,4},{4,0},{8,12},{12,8},{1,5},{5,1},{9,13},{13,9},{2,6},{6,2},{1... | collective-permute-start | bytes 786440 | tf_op jit(solution)/shard_map/ppermute | solution.py:240
  50.2 3.1 %collective-permute-done.8.outer_ref = bf16[64,2048]{1,0:T(8,128)(2,1)S(1)} collective-permute-done((bf16[64,2048]{1,0:T(8,128)(2,1)S(1)}, bf16[64,2048]{1,0:T(8,128)(2,1)S(1)}, u32[]{:S(2)}, u32[]{:S(2)}) %collective-permute-start.8) | collective-permute-done | bytes 262176 | tf_op jit(solution)/shard_map/ppermute | solution.py:240
  60.1 5.9 %load_weight.1.refs_6_.w_ref = bf16[2048,4096]{1,0:T(8,128)(2,1)S(1)} custom-call(bf16[2048,4096]{1,0:T(8,128)(2,1)} %w_ref.1, bf16[64,2048]{1,0:T(8,128)(2,1)S(1)} %collective-permute-done.13.refs_0_.outer_ref, bf16[64,2048]{1,0:T(8,128)(2,1)S(1)} %collective-permute-done.15.refs_1_.refs_0_), custom_call_target="tpu_custom_call" | custom-call | flops 1 | bytes 1 | tf_op jit(solution)/shard_map/load_weight/pallas_call | solution.py:284
  66.0 4.3 %collective-permute-done.16.refs_5_.refs_2_ = bf16[64,2048]{1,0:T(8,128)(2,1)S(1)} collective-permute-done((bf16[64,2048]{1,0:T(8,128)(2,1)S(1)}, bf16[64,2048]{1,0:T(8,128)(2,1)S(1)}, u32[]{:S(2)}, u32[]{:S(2)}) %collective-permute-start.16) | collective-permute-done | bytes 262176 | tf_op jit(solution)/shard_map/ppermute | solution.py:242
  70.4 3.4 %collective-permute-done.12.refs_3_ = bf16[64,2048]{1,0:T(8,128)(2,1)S(1)} collective-permute-done((bf16[64,2048]{1,0:T(8,128)(2,1)S(1)}, bf16[64,2048]{1,0:T(8,128)(2,1)S(1)}, u32[]{:S(2)}, u32[]{:S(2)}) %collective-permute-start.12) | collective-permute-done | bytes 262176 | tf_op jit(solution)/shard_map/ppermute | solution.py:244
  74.4 2.3 %split_product.4 = (bf16[64,2048]{1,0:T(8,128)(2,1)S(1)}, bf16[64,2048]{1,0:T(8,128)(2,1)S(1)}, f32[64,2048]{1,0:T(8,128)S(1)}, f32[64,2048]{1,0:T(8,128)S(1)}) custom-call(bf16[256,2048]{1,0:T(8,128)(2,1)S(1)} %collect.2.rows_ref, bf16[2048,4096]{1,0:T(8,128)(2,1)S(1)} %load_weight.1.refs_6_.w_ref), custom_call_target="tpu_custom_call" | custom-call | flops 1 | bytes 1 | tf_op jit(solution)/shard_map/split_product/pallas_call | solution.py:317
  79.7 2.3 %split_product.5 = (bf16[64,2048]{1,0:T(8,128)(2,1)S(1)}, bf16[64,2048]{1,0:T(8,128)(2,1)S(1)}, f32[64,2048]{1,0:T(8,128)S(1)}, f32[64,2048]{1,0:T(8,128)S(1)}) custom-call(bf16[256,2048]{1,0:T(8,128)(2,1)S(1)} %collect.2.rows_ref, bf16[2048,4096]{1,0:T(8,128)(2,1)S(1)} %load_weight.1.refs_6_.w_ref, ...), custom_call_target="tpu_custom_call" | custom-call | flops 1 | bytes 1 | tf_op jit(solution)/shard_map/split_product/pallas_call | solution.py:317
  84.5 4.1 %collective-permute-done.20.refs_3_ = bf16[64,2048]{1,0:T(8,128)(2,1)S(1)} collective-permute-done((bf16[64,2048]{1,0:T(8,128)(2,1)S(1)}, bf16[64,2048]{1,0:T(8,128)(2,1)S(1)}, u32[]{:S(2)}, u32[]{:S(2)}) %collective-permute-start.20) | collective-permute-done | bytes 262176 | tf_op jit(solution)/shard_map/ppermute | solution.py:244
  89.5 2.0 %collective-permute-done.19.refs_2_.refs_5_ = bf16[64,2048]{1,0:T(8,128)(2,1)S(1)} collective-permute-done((bf16[64,2048]{1,0:T(8,128)(2,1)S(1)}, bf16[64,2048]{1,0:T(8,128)(2,1)S(1)}, u32[]{:S(2)}, u32[]{:S(2)}) %collective-permute-start.19) | collective-permute-done | bytes 262176 | tf_op jit(solution)/shard_map/ppermute | solution.py:657
  91.5 2.3 %split_product.7 = (bf16[64,2048]{1,0:T(8,128)(2,1)S(1)}, bf16[64,2048]{1,0:T(8,128)(2,1)S(1)}, f32[64,2048]{1,0:T(8,128)S(1)}, f32[64,2048]{1,0:T(8,128)S(1)}) custom-call(bf16[256,2048]{1,0:T(8,128)(2,1)S(1)} %collect.3.rows_ref, bf16[2048,4096]{1,0:T(8,128)(2,1)S(1)} %load_weight.1.refs_6_.w_ref, bf16[1,64,128]{2,1,0:T(8,128)(2,1)S(1)} %get-tuple-element.52.refs_0_.refs_1_), custom_call_target="tpu_custom_call" | custom-call | flops 1 | bytes 1 | tf_op jit(solution)/shard_map/split_product/pallas_call | solution.py:317
  94.9 1.6 %collective-permute-done.23.refs_0_.refs_5_ = bf16[64,2048]{1,0:T(8,128)(2,1)S(1)} collective-permute-done((bf16[64,2048]{1,0:T(8,128)(2,1)S(1)}, bf16[64,2048]{1,0:T(8,128)(2,1)S(1)}, u32[]{:S(2)}, u32[]{:S(2)}) %collective-permute-start.23) | collective-permute-done | bytes 262176 | tf_op jit(solution)/shard_map/ppermute | solution.py:657
  97.1 2.3 %split_product.6 = (bf16[64,2048]{1,0:T(8,128)(2,1)S(1)}, bf16[64,2048]{1,0:T(8,128)(2,1)S(1)}, f32[64,2048]{1,0:T(8,128)S(1)}, f32[64,2048]{1,0:T(8,128)S(1)}) custom-call(bf16[256,2048]{1,0:T(8,128)(2,1)S(1)} %collect.3.rows_ref, bf16[2048,4096]{1,0:T(8,128)(2,1)S(1)} %load_weight.1.refs_6_.w_ref, ...), custom_call_target="tpu_custom_call" | custom-call | flops 1 | bytes 1 | tf_op jit(solution)/shard_map/split_product/pallas_call | solution.py:317
  103.8 3.9 %up_gradient.1.refs_9_ = f32[4,64,4096]{2,1,0:T(8,128)} custom-call(s32[14]{0:T(128)S(1)} %concatenate.3.index_ref.refs_0_, bf16[1,64,4096]{2,1,0:T(8,128)(2,1)S(1)} %get-tuple-element.47.refs_0_, bf16[1,64,4096]{2,1,0:T(8,128)(2,1)S(1)} %collective-permute-done.21.refs_0_.refs_1_, bf16[1,64,4096]{2,1,0:T(8,128)(2,1)S(1)} %collective-permute-done.34.refs_2_, ...), custom_call_target="tpu_custom_call" | custom-call | flops 1 | bytes 1 | tf_op jit(solution)/shard_map/up_gradient/pallas_call | solution.py:545
  110.3 2.1 %finish.2.refs_9_ = bf16[128,4096]{1,0:T(8,128)(2,1)} custom-call(s32[14]{0:T(128)S(1)} %concatenate.3.index_ref.refs_0_, bf16[1,64,128]{2,1,0:T(8,128)(2,1)S(1)} %get-tuple-element.37.refs_0_.refs_1_, bf16[4,64,4096]{2,1,0:T(8,128)(2,1)S(1)} %copy-done.1, f32[64,2048]{1,0:T(8,128)S(1)} %get-tuple-element.57.refs_3_, ...), custom_call_target="tpu_custom_call" | custom-call | flops 1 | bytes 1 | tf_op jit(solution)/shard_map/finish/pallas_call | solution.py:615
  112.4 2.9 %collective-permute-done.29.refs_8_ = bf16[64,2048]{1,0:T(8,128)(2,1)S(1)} collective-permute-done((bf16[64,2048]{1,0:T(8,128)(2,1)S(1)}, bf16[64,2048]{1,0:T(8,128)(2,1)S(1)}, u32[]{:S(2)}, u32[]{:S(2)}) %collective-permute-start.29) | collective-permute-done | bytes 262176 | tf_op jit(solution)/shard_map/ppermute | solution.py:657
  115.3 2.1 %finish.3 = bf16[128,4096]{1,0:T(8,128)(2,1)} custom-call(s32[14]{0:T(128)S(1)} %concatenate.3.index_ref.refs_0_, bf16[1,64,128]{2,1,0:T(8,128)(2,1)S(1)} %get-tuple-element.37.refs_0_.refs_1_, bf16[4,64,4096]{2,1,0:T(8,128)(2,1)S(1)} %copy-done.1, f32[64,2048]{1,0:T(8,128)S(1)} %get-tuple-element.43.refs_3_, ...), custom_call_target="tpu_custom_call", output_to_operand_aliasing={{}: (9, {})} | custom-call | flops 1 | bytes 1 | tf_op jit(solution)/shard_map/finish/pallas_call | solution.py:615
  (79 shorter events, 30.9 us)
Async XLA Ops:
  3.3 18.9 %collective-permute-start.4 = (bf16[128,2048]{1,0:T(8,128)(2,1)S(1)}, bf16[128,2048]{1,0:T(8,128)(2,1)S(1)}, u32[]{:S(2)}, u32[]{:S(2)}) collective-permute-start(bf16[128,2048]{1,0:T(8,128)(2,1)S(1)} %get-tuple-element.33.refs_0_), channel_id=1, source_target_pairs={{12,8},{0,4},{13,9},{1,5},{14,10},{2,6},{15,11},{3,7},{28,24},{16,... | collective-permute-start | bytes 1572872 | tf_op jit(solution)/shard_map/ppermute | solution.py:220
  8.3 13.9 %collective-permute-start.5 = (bf16[128,2048]{1,0:T(8,128)(2,1)S(1)}, bf16[128,2048]{1,0:T(8,128)(2,1)S(1)}, u32[]{:S(2)}, u32[]{:S(2)}) collective-permute-start(bf16[128,2048]{1,0:T(8,128)(2,1)S(1)} %get-tuple-element.38), channel_id=1, source_target_pairs={{8,4},{9,5},{10,6},{11,7},{24,20},{25,21},{26,22},{27,23}} | collective-permute-start | bytes 1572872 | tf_op jit(solution)/shard_map/ppermute | solution.py:221
  22.8 21.0 %collective-permute-start.6 = (bf16[128,2048]{1,0:T(8,128)(2,1)S(1)}, bf16[128,2048]{1,0:T(8,128)(2,1)S(1)}, u32[]{:S(2)}, u32[]{:S(2)}) collective-permute-start(bf16[128,2048]{1,0:T(8,128)(2,1)S(1)} %get-tuple-element.39), channel_id=1, source_target_pairs={{4,0},{0,4},{12,8},{5,1},{1,5},{13,9},{6,2},{2,6},{14,10},{7,3},{3... | collective-permute-start | bytes 1572872 | tf_op jit(solution)/shard_map/ppermute | solution.py:230
  26.0 17.8 %collective-permute-start.7 = (bf16[128,2048]{1,0:T(8,128)(2,1)S(1)}, bf16[128,2048]{1,0:T(8,128)(2,1)S(1)}, u32[]{:S(2)}, u32[]{:S(2)}) collective-permute-start(bf16[128,2048]{1,0:T(8,128)(2,1)S(1)} %get-tuple-element.40), channel_id=1, source_target_pairs={{8,4},{4,8},{9,5},{5,9},{10,6},{6,10},{11,7},{7,11},{24,20},{20,24... | collective-permute-start | bytes 1572872 | tf_op jit(solution)/shard_map/ppermute | solution.py:231
  26.7 16.2 %collective-permute-start.3 = (f32[2,1,64,128]{3,2,1,0:T(8,128)S(1)}, f32[2,1,64,128]{3,2,1,0:T(8,128)S(1)}, u32[]{:S(2)}, u32[]{:S(2)}) collective-permute-start(f32[2,1,64,128]{3,2,1,0:T(8,128)S(1)} %add.31.sum_ref.refs_0_), channel_id=1, source_target_pairs={{0,8},{4,12},{8,0},{12,4},{1,9},{5,13},{9,1},{13,5},{2,10},{6,14},... | collective-permute-start | bytes 196616 | tf_op jit(solution)/shard_map/ppermute | solution.py:660
  44.5 8.8 %collective-permute-start.8 = (bf16[64,2048]{1,0:T(8,128)(2,1)S(1)}, bf16[64,2048]{1,0:T(8,128)(2,1)S(1)}, u32[]{:S(2)}, u32[]{:S(2)}) collective-permute-start(bf16[64,2048]{1,0:T(8,128)(2,1)S(1)} %get-tuple-element.41.home_ref), channel_id=1, source_target_pairs={{0,4},{4,0},{8,12},{12,8},{1,5},{5,1},{9,13},{13,9},{2,6},{6,2},{1... | collective-permute-start | bytes 786440 | tf_op jit(solution)/shard_map/ppermute | solution.py:240
  44.5 11.0 %collective-permute-start.9 = (bf16[64,2048]{1,0:T(8,128)(2,1)S(1)}, bf16[64,2048]{1,0:T(8,128)(2,1)S(1)}, u32[]{:S(2)}, u32[]{:S(2)}) collective-permute-start(bf16[64,2048]{1,0:T(8,128)(2,1)S(1)} %get-tuple-element.41.home_ref), channel_id=1, source_target_pairs={{4,8},{8,4},{5,9},{9,5},{6,10},{10,6},{7,11},{11,7},{20,24},{24,20... | collective-permute-start | bytes 786440 | tf_op jit(solution)/shard_map/ppermute | solution.py:241
  45.2 11.6 %collective-permute-start.13 = (bf16[64,2048]{1,0:T(8,128)(2,1)S(1)}, bf16[64,2048]{1,0:T(8,128)(2,1)S(1)}, u32[]{:S(2)}, u32[]{:S(2)}) collective-permute-start(bf16[64,2048]{1,0:T(8,128)(2,1)S(1)} %get-tuple-element.42.home_ref), channel_id=1, source_target_pairs={{0,4},{4,0},{8,12},{12,8},{1,5},{5,1},{9,13},{13,9},{2,6},{6,2},{1... | collective-permute-start | bytes 786440 | tf_op jit(solution)/shard_map/ppermute | solution.py:240
  49.5 8.0 %collective-permute-start.15 = (bf16[64,2048]{1,0:T(8,128)(2,1)S(1)}, bf16[64,2048]{1,0:T(8,128)(2,1)S(1)}, u32[]{:S(2)}, u32[]{:S(2)}) collective-permute-start(bf16[64,2048]{1,0:T(8,128)(2,1)S(1)} %get-tuple-element.42.home_ref), channel_id=1, source_target_pairs={{4,8},{8,4},{5,9},{9,5},{6,10},{10,6},{7,11},{11,7},{20,24},{24,20... | collective-permute-start | bytes 786440 | tf_op jit(solution)/shard_map/ppermute | solution.py:241
  54.0 25.7 %collective-permute-start.21 = (bf16[1,64,4096]{2,1,0:T(8,128)(2,1)S(1)}, bf16[1,64,4096]{2,1,0:T(8,128)(2,1)S(1)}, u32[]{:S(2)}, u32[]{:S(2)}) collective-permute-start(bf16[1,64,4096]{2,1,0:T(8,128)(2,1)S(1)} %get-tuple-element.47.refs_0_), channel_id=1, source_target_pairs={{0,2},{1,3},{2,0},{3,1},{4,6},{5,7},{6,4},{7,5},{8,10},{9,11},{10,... | collective-permute-start | bytes 1572872 | tf_op jit(solution)/shard_map/ppermute | solution.py:657
  55.5 10.5 %collective-permute-start.11 = (bf16[64,2048]{1,0:T(8,128)(2,1)S(1)}, bf16[64,2048]{1,0:T(8,128)(2,1)S(1)}, u32[]{:S(2)}, u32[]{:S(2)}) collective-permute-start(bf16[64,2048]{1,0:T(8,128)(2,1)S(1)} %collective-permute-done.9.refs_0_), channel_id=1, source_target_pairs={{4,0},{8,12},{5,1},{9,13},{6,2},{10,14},{7,3},{11,15},{20,16},{24,... | collective-permute-start | bytes 786440 | tf_op jit(solution)/shard_map/ppermute | solution.py:242
  56.8 9.2 %collective-permute-start.14 = (bf16[64,2048]{1,0:T(8,128)(2,1)S(1)}, bf16[64,2048]{1,0:T(8,128)(2,1)S(1)}, u32[]{:S(2)}, u32[]{:S(2)}) collective-permute-start(bf16[64,2048]{1,0:T(8,128)(2,1)S(1)} %collective-permute-done.13.refs_0_.outer_ref), channel_id=1, source_target_pairs={{4,8},{8,4},{5,9},{9,5},{6,10},{10,6},{7,11},{11,7},{20,24},{24,20... | collective-permute-start | bytes 786440 | tf_op jit(solution)/shard_map/ppermute | solution.py:243
  57.5 12.9 %collective-permute-start.16 = (bf16[64,2048]{1,0:T(8,128)(2,1)S(1)}, bf16[64,2048]{1,0:T(8,128)(2,1)S(1)}, u32[]{:S(2)}, u32[]{:S(2)}) collective-permute-start(bf16[64,2048]{1,0:T(8,128)(2,1)S(1)} %collective-permute-done.15.refs_1_.refs_0_), channel_id=1, source_target_pairs={{4,0},{8,12},{5,1},{9,13},{6,2},{10,14},{7,3},{11,15},{20,16},{24,... | collective-permute-start | bytes 786440 | tf_op jit(solution)/shard_map/ppermute | solution.py:242
  58.8 15.0 %collective-permute-start.12 = (bf16[64,2048]{1,0:T(8,128)(2,1)S(1)}, bf16[64,2048]{1,0:T(8,128)(2,1)S(1)}, u32[]{:S(2)}, u32[]{:S(2)}) collective-permute-start(bf16[64,2048]{1,0:T(8,128)(2,1)S(1)} %collective-permute-done.10.refs_1_), channel_id=1, source_target_pairs={{4,0},{8,12},{5,1},{9,13},{6,2},{10,14},{7,3},{11,15},{20,16},{24,... | collective-permute-start | bytes 786440 | tf_op jit(solution)/shard_map/ppermute | solution.py:244
  76.8 12.6 %collective-permute-start.24 = (bf16[1,64,128]{2,1,0:T(8,128)(2,1)S(1)}, bf16[1,64,128]{2,1,0:T(8,128)(2,1)S(1)}, u32[]{:S(2)}, u32[]{:S(2)}) collective-permute-start(bf16[1,64,128]{2,1,0:T(8,128)(2,1)S(1)} %get-tuple-element.50.refs_0_), channel_id=1, source_target_pairs={{0,2},{1,3},{2,0},{3,1},{4,6},{5,7},{6,4},{7,5},{8,10},{9,11},{10,... | collective-permute-start | bytes 49160 | tf_op jit(solution)/shard_map/ppermute | solution.py:657
  78.4 10.3 %collective-permute-start.20 = (bf16[64,2048]{1,0:T(8,128)(2,1)S(1)}, bf16[64,2048]{1,0:T(8,128)(2,1)S(1)}, u32[]{:S(2)}, u32[]{:S(2)}) collective-permute-start(bf16[64,2048]{1,0:T(8,128)(2,1)S(1)} %collective-permute-done.14.refs_4_.refs_1_), channel_id=1, source_target_pairs={{4,0},{8,12},{5,1},{9,13},{6,2},{10,14},{7,3},{11,15},{20,16},{24,... | collective-permute-start | bytes 786440 | tf_op jit(solution)/shard_map/ppermute | solution.py:244
  82.3 9.2 %collective-permute-start.19 = (bf16[64,2048]{1,0:T(8,128)(2,1)S(1)}, bf16[64,2048]{1,0:T(8,128)(2,1)S(1)}, u32[]{:S(2)}, u32[]{:S(2)}) collective-permute-start(bf16[64,2048]{1,0:T(8,128)(2,1)S(1)} %add_convert_fusion.3), channel_id=1, source_target_pairs={{0,2},{1,3},{2,0},{3,1},{4,6},{5,7},{6,4},{7,5},{8,10},{9,11},{10,... | collective-permute-start | bytes 786440 | tf_op jit(solution)/shard_map/ppermute | solution.py:657
  83.7 12.9 %collective-permute-start.23 = (bf16[64,2048]{1,0:T(8,128)(2,1)S(1)}, bf16[64,2048]{1,0:T(8,128)(2,1)S(1)}, u32[]{:S(2)}, u32[]{:S(2)}) collective-permute-start(bf16[64,2048]{1,0:T(8,128)(2,1)S(1)} %add_convert_fusion.2.refs_4_), channel_id=1, source_target_pairs={{0,2},{1,3},{2,0},{3,1},{4,6},{5,7},{6,4},{7,5},{8,10},{9,11},{10,... | collective-permute-start | bytes 786440 | tf_op jit(solution)/shard_map/ppermute | solution.py:657
  94.5 7.3 %collective-permute-start.34 = (bf16[1,64,4096]{2,1,0:T(8,128)(2,1)S(1)}, bf16[1,64,4096]{2,1,0:T(8,128)(2,1)S(1)}, u32[]{:S(2)}, u32[]{:S(2)}) collective-permute-start(bf16[1,64,4096]{2,1,0:T(8,128)(2,1)S(1)} %get-tuple-element.47.refs_0_), channel_id=1, source_target_pairs={{0,1},{1,0},{2,3},{3,2},{4,5},{5,4},{6,7},{7,6},{8,9},{9,8},{10,11... | collective-permute-start | bytes 1572872 | tf_op jit(solution)/shard_map/ppermute | solution.py:654
  97.1 12.1 %collective-permute-start.31 = (bf16[64,2048]{1,0:T(8,128)(2,1)S(1)}, bf16[64,2048]{1,0:T(8,128)(2,1)S(1)}, u32[]{:S(2)}, u32[]{:S(2)}) collective-permute-start(bf16[64,2048]{1,0:T(8,128)(2,1)S(1)} %get-tuple-element.60), channel_id=1, source_target_pairs={{0,1},{1,0},{2,3},{3,2},{4,5},{5,4},{6,7},{7,6},{8,9},{9,8},{10,11... | collective-permute-start | bytes 786440 | tf_op jit(solution)/shard_map/ppermute | solution.py:654
  101.1 9.1 %collective-permute-start.33 = (bf16[64,2048]{1,0:T(8,128)(2,1)S(1)}, bf16[64,2048]{1,0:T(8,128)(2,1)S(1)}, u32[]{:S(2)}, u32[]{:S(2)}) collective-permute-start(bf16[64,2048]{1,0:T(8,128)(2,1)S(1)} %add_convert_fusion), channel_id=1, source_target_pairs={{0,2},{1,3},{2,0},{3,1},{4,6},{5,7},{6,4},{7,5},{8,10},{9,11},{10,... | collective-permute-start | bytes 786440 | tf_op jit(solution)/shard_map/ppermute | solution.py:657
  101.8 10.6 %collective-permute-start.17 = (bf16[64,2048]{1,0:T(8,128)(2,1)S(1)}, bf16[64,2048]{1,0:T(8,128)(2,1)S(1)}, u32[]{:S(2)}, u32[]{:S(2)}) collective-permute-start(bf16[64,2048]{1,0:T(8,128)(2,1)S(1)} %get-tuple-element.44), channel_id=1, source_target_pairs={{0,1},{1,0},{2,3},{3,2},{4,5},{5,4},{6,7},{7,6},{8,9},{9,8},{10,11... | collective-permute-start | bytes 786440 | tf_op jit(solution)/shard_map/ppermute | solution.py:654
  101.9 10.5 %collective-permute-start.27 = (bf16[64,2048]{1,0:T(8,128)(2,1)S(1)}, bf16[64,2048]{1,0:T(8,128)(2,1)S(1)}, u32[]{:S(2)}, u32[]{:S(2)}) collective-permute-start(bf16[64,2048]{1,0:T(8,128)(2,1)S(1)} %get-tuple-element.54), channel_id=1, source_target_pairs={{0,1},{1,0},{2,3},{3,2},{4,5},{5,4},{6,7},{7,6},{8,9},{9,8},{10,11... | collective-permute-start | bytes 786440 | tf_op jit(solution)/shard_map/ppermute | solution.py:654
  102.3 13.0 %collective-permute-start.29 = (bf16[64,2048]{1,0:T(8,128)(2,1)S(1)}, bf16[64,2048]{1,0:T(8,128)(2,1)S(1)}, u32[]{:S(2)}, u32[]{:S(2)}) collective-permute-start(bf16[64,2048]{1,0:T(8,128)(2,1)S(1)} %add_convert_fusion.1), channel_id=1, source_target_pairs={{0,2},{1,3},{2,0},{3,1},{4,6},{5,7},{6,4},{7,5},{8,10},{9,11},{10,... | collective-permute-start | bytes 786440 | tf_op jit(solution)/shard_map/ppermute | solution.py:657
  (15 other events, 109.8 us)

commit v17 on v15

--- a/solution.py
+++ b/solution.py
@@ -663,11 +663,11 @@
         return arrived, [to_chip(keep[k] + arrived[k], k) for k in range(1, chips)]
 
     def over_dp(total):
-        k = 1
-        while 2 * k < owners:
+        k = owners // 2
+        while k > 1:
             total = total + across_dp(total, k)
-            k *= 2
-        return total, [across_dp(total, k)]
+            k //= 2
+        return total, [across_dp(total, 1)]
 
     if owners == 4 and block_count == 4:
         relay = Relay(index_of, index, tokens)
@@ -679,7 +679,7 @@
         lowered, back_rows, pieces = make_pieces(
             index_of, index, shape, total, more, cotangent, []
         )
-        relay.settle([lowered])
+        relay.settle(more)
         weight = load_weight(frozen_up_weight, relay.arrived[-1][1:3])
         pieces = with_other_core(same_core(pieces))
         back_rows = with_other_core(same_core(back_rows))

time: 117 us -> 116 us (level)
  starting transfers between devices: 37.7 us -> 36.3 us
    ppermute x2, starting transfers between devices: 3.59 us -> 5.43 us  [across_dp(): return lax.ppermute(value, 'dp', [(i, i ^ k) for i in range(owners)])]
    ppermute x2, waiting for transfers between devices: 17 us -> 15.4 us  [across_dp(): return lax.ppermute(value, 'dp', [(i, i ^ k) for i in range(owners)])]
    ppermute x7, starting transfers between devices: 9.67 us -> 8.13 us  [to_chip(): lax.ppermute(value, 'tensor', [(i, i ^ k * CORES) for i in range(parts)])]
    ppermute x1, starting transfers between devices: 3.16 us -> 1.92 us  [second(): lax.ppermute(outer, 'dp', [(1, 0), (0, 1), (3, 2)])]
  transfers between devices with their start and end apart: 36 -> 36, of which waited for: 13 -> 14; matrix products, arithmetic and copies ran while one was open for 0% -> 0% of each run, Pallas kernels for 23% -> 23%
where the time goes in v17:
time: 116 us
  waiting for transfers between devices  43.3 us (37%)
  starting transfers between devices  36.3 us (31%)
  Pallas kernels  34 us (29%)
    ppermute x2, waiting for transfers between devices, across_dp(): return lax.ppermute(value, 'dp', [(i, i ^ k) for i in range(owners)])  15.4 us
    pallas_call x4, Pallas kernels, split_product(): pl.pallas_call(functools.partial(split_product_kernel, each, half, part *...  9.29 us
    ppermute x7, waiting for transfers between devices, to_chip(): lax.ppermute(value, 'tensor', [(i, i ^ k * CORES) for i in range(parts)])  9.2 us
    ppermute x7, starting transfers between devices, to_chip(): lax.ppermute(value, 'tensor', [(i, i ^ k * CORES) for i in range(parts)])  8.13 us
    ppermute x2, waiting for transfers between devices, spread(): outer_3 = lax.ppermute(inner_2, 'dp', [(1, 0), (2, 3)])  7.79 us
    pallas_call x1, Pallas kernels, load_weight(): pl.pallas_call(load_weight_kernel, grid=(1,), in_specs=[pl.BlockSpec(memo...  5.89 us
    ppermute x2, starting transfers between devices, across_dp(): return lax.ppermute(value, 'dp', [(i, i ^ k) for i in range(owners)])  5.43 us
    ppermute x1, starting transfers between devices, first(): lax.ppermute(inward, 'dp', [(3, 2), (0, 1)])  4.96 us
  transfers between devices with their start and end apart: 36, of which 14 were waited for; matrix products, arithmetic and copies ran while one was open for 0% of the time, Pallas kernels for 23%

profile of v17, /device:TPU:0, one launch (start us, length us, event | category | flops | bytes accessed | tf_op | source)
XLA Modules:
  0.0 115.7 jit_solution(17043569452357279099)
XLA Ops:
  3.3 5.0 %collective-permute-start.4 = (bf16[128,2048]{1,0:T(8,128)(2,1)S(1)}, bf16[128,2048]{1,0:T(8,128)(2,1)S(1)}, u32[]{:S(2)}, u32[]{:S(2)}) collective-permute-start(bf16[128,2048]{1,0:T(8,128)(2,1)S(1)} %get-tuple-element.31.refs_0_), channel_id=1, source_target_pairs={{12,8},{0,4},{13,9},{1,5},{14,10},{2,6},{15,11},{3,7},{28,24},{16,... | collective-permute-start | bytes 1572872 | tf_op jit(solution)/shard_map/ppermute | solution.py:220
  9.0 3.5 %narrow.1 = (f32[2,1,64,128]{3,2,1,0:T(8,128)S(1)}, f32[2,1,64,128]{3,2,1,0:T(8,128)S(1)}, f32[1,64,128]{2,1,0:T(8,128)S(1)}) custom-call(s32[14]{0:T(128)S(1)} %concatenate.3.index_ref.refs_0_, bf16[384,2048]{1,0:T(8,128)(2,1)} %tokens_ref.9, bf16[1,64,2048]{2,1,0:T(8,128)(2,1)} %bitcast.7, bf16[128,4096]{1,0:T(8,128)(2,1)} %cot_ref.3, ...), custom_call_target="tpu_custom_call" | custom-call | flops 1 | bytes 1 | tf_op jit(solution)/shard_map/narrow/pallas_call | solution.py:376
  15.3 2.4 %collective-permute-done.1.refs_0_ = f32[1,64,128]{2,1,0:T(8,128)S(1)} collective-permute-done((f32[1,64,128]{2,1,0:T(8,128)S(1)}, f32[1,64,128]{2,1,0:T(8,128)S(1)}, u32[]{:S(2)}, u32[]{:S(2)}) %collective-permute-start.1) | collective-permute-done | bytes 32800 | tf_op jit(solution)/shard_map/ppermute | solution.py:638
  17.8 2.1 %collective-permute-start.2 = (f32[2,1,64,128]{3,2,1,0:T(8,128)S(1)}, f32[2,1,64,128]{3,2,1,0:T(8,128)S(1)}, u32[]{:S(2)}, u32[]{:S(2)}) collective-permute-start(f32[2,1,64,128]{3,2,1,0:T(8,128)S(1)} %merge.1), channel_id=1, source_target_pairs={{0,8},{4,12},{8,0},{12,4},{1,9},{5,13},{9,1},{13,5},{2,10},{6,14},... | collective-permute-start | bytes 196616 | tf_op jit(solution)/shard_map/ppermute | solution.py:641
  19.9 5.5 %collective-permute-done.2 = f32[2,1,64,128]{3,2,1,0:T(8,128)S(1)} collective-permute-done((f32[2,1,64,128]{3,2,1,0:T(8,128)S(1)}, f32[2,1,64,128]{3,2,1,0:T(8,128)S(1)}, u32[]{:S(2)}, u32[]{:S(2)}) %collective-permute-start.2) | collective-permute-done | bytes 65568 | tf_op jit(solution)/shard_map/ppermute | solution.py:641
  26.1 1.9 %collective-permute-start.6 = (bf16[128,2048]{1,0:T(8,128)(2,1)S(1)}, bf16[128,2048]{1,0:T(8,128)(2,1)S(1)}, u32[]{:S(2)}, u32[]{:S(2)}) collective-permute-start(bf16[128,2048]{1,0:T(8,128)(2,1)S(1)} %get-tuple-element.37), channel_id=1, source_target_pairs={{4,0},{0,4},{12,8},{5,1},{1,5},{13,9},{6,2},{2,6},{14,10},{7,3},{3... | collective-permute-start | bytes 1572872 | tf_op jit(solution)/shard_map/ppermute | solution.py:230
  28.7 3.3 %collective-permute-start.3 = (f32[2,1,64,128]{3,2,1,0:T(8,128)S(1)}, f32[2,1,64,128]{3,2,1,0:T(8,128)S(1)}, u32[]{:S(2)}, u32[]{:S(2)}) collective-permute-start(f32[2,1,64,128]{3,2,1,0:T(8,128)S(1)} %add.31.sum_ref.refs_0_), channel_id=1, source_target_pairs={{0,4},{4,0},{8,12},{12,8},{1,5},{5,1},{9,13},{13,9},{2,6},{6,2},{1... | collective-permute-start | bytes 196616 | tf_op jit(solution)/shard_map/ppermute | solution.py:641
  32.0 9.9 %collective-permute-done.3.refs_0_ = f32[2,1,64,128]{3,2,1,0:T(8,128)S(1)} collective-permute-done((f32[2,1,64,128]{3,2,1,0:T(8,128)S(1)}, f32[2,1,64,128]{3,2,1,0:T(8,128)S(1)}, u32[]{:S(2)}, u32[]{:S(2)}) %collective-permute-start.3) | collective-permute-done | bytes 65568 | tf_op jit(solution)/shard_map/ppermute | solution.py:641
  42.5 2.3 %collective-permute-start.8 = (bf16[64,2048]{1,0:T(8,128)(2,1)S(1)}, bf16[64,2048]{1,0:T(8,128)(2,1)S(1)}, u32[]{:S(2)}, u32[]{:S(2)}) collective-permute-start(bf16[64,2048]{1,0:T(8,128)(2,1)S(1)} %get-tuple-element.39.home_ref), channel_id=1, source_target_pairs={{0,4},{4,0},{8,12},{12,8},{1,5},{5,1},{9,13},{13,9},{2,6},{6,2},{1... | collective-permute-start | bytes 786440 | tf_op jit(solution)/shard_map/ppermute | solution.py:240
  47.8 3.8 %collective-permute-done.8.outer_ref = bf16[64,2048]{1,0:T(8,128)(2,1)S(1)} collective-permute-done((bf16[64,2048]{1,0:T(8,128)(2,1)S(1)}, bf16[64,2048]{1,0:T(8,128)(2,1)S(1)}, u32[]{:S(2)}, u32[]{:S(2)}) %collective-permute-start.8) | collective-permute-done | bytes 262176 | tf_op jit(solution)/shard_map/ppermute | solution.py:240
  59.3 5.9 %load_weight.1.refs_6_.w_ref = bf16[2048,4096]{1,0:T(8,128)(2,1)S(1)} custom-call(bf16[2048,4096]{1,0:T(8,128)(2,1)} %w_ref.1, bf16[64,2048]{1,0:T(8,128)(2,1)S(1)} %collective-permute-done.13.refs_0_.outer_ref, bf16[64,2048]{1,0:T(8,128)(2,1)S(1)} %collective-permute-done.15.refs_1_.refs_0_), custom_call_target="tpu_custom_call" | custom-call | flops 1 | bytes 1 | tf_op jit(solution)/shard_map/load_weight/pallas_call | solution.py:284
  66.2 3.7 %collective-permute-done.16.refs_5_.refs_2_ = bf16[64,2048]{1,0:T(8,128)(2,1)S(1)} collective-permute-done((bf16[64,2048]{1,0:T(8,128)(2,1)S(1)}, bf16[64,2048]{1,0:T(8,128)(2,1)S(1)}, u32[]{:S(2)}, u32[]{:S(2)}) %collective-permute-start.16) | collective-permute-done | bytes 262176 | tf_op jit(solution)/shard_map/ppermute | solution.py:242
  69.9 2.8 %collective-permute-done.12.refs_3_ = bf16[64,2048]{1,0:T(8,128)(2,1)S(1)} collective-permute-done((bf16[64,2048]{1,0:T(8,128)(2,1)S(1)}, bf16[64,2048]{1,0:T(8,128)(2,1)S(1)}, u32[]{:S(2)}, u32[]{:S(2)}) %collective-permute-start.12) | collective-permute-done | bytes 262176 | tf_op jit(solution)/shard_map/ppermute | solution.py:244
  73.3 2.3 %split_product.5 = (bf16[64,2048]{1,0:T(8,128)(2,1)S(1)}, bf16[64,2048]{1,0:T(8,128)(2,1)S(1)}, f32[64,2048]{1,0:T(8,128)S(1)}, f32[64,2048]{1,0:T(8,128)S(1)}) custom-call(bf16[256,2048]{1,0:T(8,128)(2,1)S(1)} %collect.2.rows_ref, bf16[2048,4096]{1,0:T(8,128)(2,1)S(1)} %load_weight.1.refs_6_.w_ref, ...), custom_call_target="tpu_custom_call" | custom-call | flops 1 | bytes 1 | tf_op jit(solution)/shard_map/split_product/pallas_call | solution.py:317
  78.4 2.3 %split_product.4 = (bf16[64,2048]{1,0:T(8,128)(2,1)S(1)}, bf16[64,2048]{1,0:T(8,128)(2,1)S(1)}, f32[64,2048]{1,0:T(8,128)S(1)}, f32[64,2048]{1,0:T(8,128)S(1)}) custom-call(bf16[256,2048]{1,0:T(8,128)(2,1)S(1)} %collect.2.rows_ref, bf16[2048,4096]{1,0:T(8,128)(2,1)S(1)} %load_weight.1.refs_6_.w_ref), custom_call_target="tpu_custom_call" | custom-call | flops 1 | bytes 1 | tf_op jit(solution)/shard_map/split_product/pallas_call | solution.py:317
  81.3 5.0 %collective-permute-done.20.refs_3_ = bf16[64,2048]{1,0:T(8,128)(2,1)S(1)} collective-permute-done((bf16[64,2048]{1,0:T(8,128)(2,1)S(1)}, bf16[64,2048]{1,0:T(8,128)(2,1)S(1)}, u32[]{:S(2)}, u32[]{:S(2)}) %collective-permute-start.20) | collective-permute-done | bytes 262176 | tf_op jit(solution)/shard_map/ppermute | solution.py:244
  87.9 2.1 %collective-permute-done.24.refs_1_ = bf16[1,64,128]{2,1,0:T(8,128)(2,1)S(1)} collective-permute-done((bf16[1,64,128]{2,1,0:T(8,128)(2,1)S(1)}, bf16[1,64,128]{2,1,0:T(8,128)(2,1)S(1)}, u32[]{:S(2)}, u32[]{:S(2)}) %collective-permute-start.24) | collective-permute-done | bytes 16416 | tf_op jit(solution)/shard_map/ppermute | solution.py:638
  90.6 2.3 %split_product.7 = (bf16[64,2048]{1,0:T(8,128)(2,1)S(1)}, bf16[64,2048]{1,0:T(8,128)(2,1)S(1)}, f32[64,2048]{1,0:T(8,128)S(1)}, f32[64,2048]{1,0:T(8,128)S(1)}) custom-call(bf16[256,2048]{1,0:T(8,128)(2,1)S(1)} %collect.3.rows_ref, bf16[2048,4096]{1,0:T(8,128)(2,1)S(1)} %load_weight.1.refs_6_.w_ref, ...), custom_call_target="tpu_custom_call" | custom-call | flops 1 | bytes 1 | tf_op jit(solution)/shard_map/split_product/pallas_call | solution.py:317
  94.7 2.3 %split_product.6 = (bf16[64,2048]{1,0:T(8,128)(2,1)S(1)}, bf16[64,2048]{1,0:T(8,128)(2,1)S(1)}, f32[64,2048]{1,0:T(8,128)S(1)}, f32[64,2048]{1,0:T(8,128)S(1)}) custom-call(bf16[256,2048]{1,0:T(8,128)(2,1)S(1)} %collect.3.rows_ref, bf16[2048,4096]{1,0:T(8,128)(2,1)S(1)} %load_weight.1.refs_6_.w_ref, ...), custom_call_target="tpu_custom_call" | custom-call | flops 1 | bytes 1 | tf_op jit(solution)/shard_map/split_product/pallas_call | solution.py:317
  100.9 2.0 %down_gradient.1.refs_10_ = f32[1,64,2048]{2,1,0:T(8,128)} custom-call(s32[14]{0:T(128)S(1)} %concatenate.3.index_ref.refs_0_, bf16[384,2048]{1,0:T(8,128)(2,1)S(1)} %copy-done, bf16[1,64,128]{2,1,0:T(8,128)(2,1)S(1)} %get-tuple-element.48.refs_0_, bf16[1,64,128]{2,1,0:T(8,128)(2,1)S(1)} %collective-permute-done.24.refs_1_, ...), custom_call_target="tpu_custom_call" | custom-call | flops 1 | bytes 1 | tf_op jit(solution)/shard_map/down_gradient/pallas_call | solution.py:485
  102.9 3.9 %up_gradient.1.refs_9_ = f32[4,64,4096]{2,1,0:T(8,128)} custom-call(s32[14]{0:T(128)S(1)} %concatenate.3.index_ref.refs_0_, bf16[1,64,4096]{2,1,0:T(8,128)(2,1)S(1)} %get-tuple-element.45.refs_0_, bf16[1,64,4096]{2,1,0:T(8,128)(2,1)S(1)} %collective-permute-done.21.refs_0_.refs_1_, bf16[1,64,4096]{2,1,0:T(8,128)(2,1)S(1)} %collective-permute-done.26.refs_2_, ...), custom_call_target="tpu_custom_call" | custom-call | flops 1 | bytes 1 | tf_op jit(solution)/shard_map/up_gradient/pallas_call | solution.py:526
  108.4 2.1 %finish.2.refs_9_ = bf16[128,4096]{1,0:T(8,128)(2,1)} custom-call(s32[14]{0:T(128)S(1)} %concatenate.3.index_ref.refs_0_, bf16[1,64,128]{2,1,0:T(8,128)(2,1)S(1)} %get-tuple-element.35.refs_1_, bf16[4,64,4096]{2,1,0:T(8,128)(2,1)S(1)} %copy-done.1, f32[64,2048]{1,0:T(8,128)S(1)} %get-tuple-element.53.refs_3_, ...), custom_call_target="tpu_custom_call" | custom-call | flops 1 | bytes 1 | tf_op jit(solution)/shard_map/finish/pallas_call | solution.py:596
  110.6 3.0 %collective-permute-done.30.refs_8_ = bf16[64,2048]{1,0:T(8,128)(2,1)S(1)} collective-permute-done((bf16[64,2048]{1,0:T(8,128)(2,1)S(1)}, bf16[64,2048]{1,0:T(8,128)(2,1)S(1)}, u32[]{:S(2)}, u32[]{:S(2)}) %collective-permute-start.30) | collective-permute-done | bytes 262176 | tf_op jit(solution)/shard_map/ppermute | solution.py:638
  113.6 2.1 %finish.3 = bf16[128,4096]{1,0:T(8,128)(2,1)} custom-call(s32[14]{0:T(128)S(1)} %concatenate.3.index_ref.refs_0_, bf16[1,64,128]{2,1,0:T(8,128)(2,1)S(1)} %get-tuple-element.35.refs_1_, bf16[4,64,4096]{2,1,0:T(8,128)(2,1)S(1)} %copy-done.1, f32[64,2048]{1,0:T(8,128)S(1)} %get-tuple-element.41.refs_3_, ...), custom_call_target="tpu_custom_call", output_to_operand_aliasing={{}: (9, {})} | custom-call | flops 1 | bytes 1 | tf_op jit(solution)/shard_map/finish/pallas_call | solution.py:596
  (78 shorter events, 32.9 us)
Async XLA Ops:
  3.3 22.1 %collective-permute-start.4 = (bf16[128,2048]{1,0:T(8,128)(2,1)S(1)}, bf16[128,2048]{1,0:T(8,128)(2,1)S(1)}, u32[]{:S(2)}, u32[]{:S(2)}) collective-permute-start(bf16[128,2048]{1,0:T(8,128)(2,1)S(1)} %get-tuple-element.31.refs_0_), channel_id=1, source_target_pairs={{12,8},{0,4},{13,9},{1,5},{14,10},{2,6},{15,11},{3,7},{28,24},{16,... | collective-permute-start | bytes 1572872 | tf_op jit(solution)/shard_map/ppermute | solution.py:220
  8.3 17.2 %collective-permute-start.5 = (bf16[128,2048]{1,0:T(8,128)(2,1)S(1)}, bf16[128,2048]{1,0:T(8,128)(2,1)S(1)}, u32[]{:S(2)}, u32[]{:S(2)}) collective-permute-start(bf16[128,2048]{1,0:T(8,128)(2,1)S(1)} %get-tuple-element.36), channel_id=1, source_target_pairs={{8,4},{9,5},{10,6},{11,7},{24,20},{25,21},{26,22},{27,23}} | collective-permute-start | bytes 1572872 | tf_op jit(solution)/shard_map/ppermute | solution.py:221
  26.1 15.8 %collective-permute-start.6 = (bf16[128,2048]{1,0:T(8,128)(2,1)S(1)}, bf16[128,2048]{1,0:T(8,128)(2,1)S(1)}, u32[]{:S(2)}, u32[]{:S(2)}) collective-permute-start(bf16[128,2048]{1,0:T(8,128)(2,1)S(1)} %get-tuple-element.37), channel_id=1, source_target_pairs={{4,0},{0,4},{12,8},{5,1},{1,5},{13,9},{6,2},{2,6},{14,10},{7,3},{3... | collective-permute-start | bytes 1572872 | tf_op jit(solution)/shard_map/ppermute | solution.py:230
  28.0 13.9 %collective-permute-start.7 = (bf16[128,2048]{1,0:T(8,128)(2,1)S(1)}, bf16[128,2048]{1,0:T(8,128)(2,1)S(1)}, u32[]{:S(2)}, u32[]{:S(2)}) collective-permute-start(bf16[128,2048]{1,0:T(8,128)(2,1)S(1)} %get-tuple-element.38), channel_id=1, source_target_pairs={{8,4},{4,8},{9,5},{5,9},{10,6},{6,10},{11,7},{7,11},{24,20},{20,24... | collective-permute-start | bytes 1572872 | tf_op jit(solution)/shard_map/ppermute | solution.py:231
  28.7 13.2 %collective-permute-start.3 = (f32[2,1,64,128]{3,2,1,0:T(8,128)S(1)}, f32[2,1,64,128]{3,2,1,0:T(8,128)S(1)}, u32[]{:S(2)}, u32[]{:S(2)}) collective-permute-start(f32[2,1,64,128]{3,2,1,0:T(8,128)S(1)} %add.31.sum_ref.refs_0_), channel_id=1, source_target_pairs={{0,4},{4,0},{8,12},{12,8},{1,5},{5,1},{9,13},{13,9},{2,6},{6,2},{1... | collective-permute-start | bytes 196616 | tf_op jit(solution)/shard_map/ppermute | solution.py:641
  42.5 9.1 %collective-permute-start.8 = (bf16[64,2048]{1,0:T(8,128)(2,1)S(1)}, bf16[64,2048]{1,0:T(8,128)(2,1)S(1)}, u32[]{:S(2)}, u32[]{:S(2)}) collective-permute-start(bf16[64,2048]{1,0:T(8,128)(2,1)S(1)} %get-tuple-element.39.home_ref), channel_id=1, source_target_pairs={{0,4},{4,0},{8,12},{12,8},{1,5},{5,1},{9,13},{13,9},{2,6},{6,2},{1... | collective-permute-start | bytes 786440 | tf_op jit(solution)/shard_map/ppermute | solution.py:240
  44.9 9.8 %collective-permute-start.9 = (bf16[64,2048]{1,0:T(8,128)(2,1)S(1)}, bf16[64,2048]{1,0:T(8,128)(2,1)S(1)}, u32[]{:S(2)}, u32[]{:S(2)}) collective-permute-start(bf16[64,2048]{1,0:T(8,128)(2,1)S(1)} %get-tuple-element.39.home_ref), channel_id=1, source_target_pairs={{4,8},{8,4},{5,9},{9,5},{6,10},{10,6},{7,11},{11,7},{20,24},{24,20... | collective-permute-start | bytes 786440 | tf_op jit(solution)/shard_map/ppermute | solution.py:241
  45.5 10.5 %collective-permute-start.13 = (bf16[64,2048]{1,0:T(8,128)(2,1)S(1)}, bf16[64,2048]{1,0:T(8,128)(2,1)S(1)}, u32[]{:S(2)}, u32[]{:S(2)}) collective-permute-start(bf16[64,2048]{1,0:T(8,128)(2,1)S(1)} %get-tuple-element.40.home_ref), channel_id=1, source_target_pairs={{0,4},{4,0},{8,12},{12,8},{1,5},{5,1},{9,13},{13,9},{2,6},{6,2},{1... | collective-permute-start | bytes 786440 | tf_op jit(solution)/shard_map/ppermute | solution.py:240
  47.2 9.5 %collective-permute-start.15 = (bf16[64,2048]{1,0:T(8,128)(2,1)S(1)}, bf16[64,2048]{1,0:T(8,128)(2,1)S(1)}, u32[]{:S(2)}, u32[]{:S(2)}) collective-permute-start(bf16[64,2048]{1,0:T(8,128)(2,1)S(1)} %get-tuple-element.40.home_ref), channel_id=1, source_target_pairs={{4,8},{8,4},{5,9},{9,5},{6,10},{10,6},{7,11},{11,7},{20,24},{24,20... | collective-permute-start | bytes 786440 | tf_op jit(solution)/shard_map/ppermute | solution.py:241
  53.2 20.2 %collective-permute-start.21 = (bf16[1,64,4096]{2,1,0:T(8,128)(2,1)S(1)}, bf16[1,64,4096]{2,1,0:T(8,128)(2,1)S(1)}, u32[]{:S(2)}, u32[]{:S(2)}) collective-permute-start(bf16[1,64,4096]{2,1,0:T(8,128)(2,1)S(1)} %get-tuple-element.45.refs_0_), channel_id=1, source_target_pairs={{0,2},{1,3},{2,0},{3,1},{4,6},{5,7},{6,4},{7,5},{8,10},{9,11},{10,... | collective-permute-start | bytes 1572872 | tf_op jit(solution)/shard_map/ppermute | solution.py:638
  54.7 11.4 %collective-permute-start.11 = (bf16[64,2048]{1,0:T(8,128)(2,1)S(1)}, bf16[64,2048]{1,0:T(8,128)(2,1)S(1)}, u32[]{:S(2)}, u32[]{:S(2)}) collective-permute-start(bf16[64,2048]{1,0:T(8,128)(2,1)S(1)} %collective-permute-done.9.refs_0_), channel_id=1, source_target_pairs={{4,0},{8,12},{5,1},{9,13},{6,2},{10,14},{7,3},{11,15},{20,16},{24,... | collective-permute-start | bytes 786440 | tf_op jit(solution)/shard_map/ppermute | solution.py:242
  56.0 10.2 %collective-permute-start.14 = (bf16[64,2048]{1,0:T(8,128)(2,1)S(1)}, bf16[64,2048]{1,0:T(8,128)(2,1)S(1)}, u32[]{:S(2)}, u32[]{:S(2)}) collective-permute-start(bf16[64,2048]{1,0:T(8,128)(2,1)S(1)} %collective-permute-done.13.refs_0_.outer_ref), channel_id=1, source_target_pairs={{4,8},{8,4},{5,9},{9,5},{6,10},{10,6},{7,11},{11,7},{20,24},{24,20... | collective-permute-start | bytes 786440 | tf_op jit(solution)/shard_map/ppermute | solution.py:243
  56.7 13.2 %collective-permute-start.16 = (bf16[64,2048]{1,0:T(8,128)(2,1)S(1)}, bf16[64,2048]{1,0:T(8,128)(2,1)S(1)}, u32[]{:S(2)}, u32[]{:S(2)}) collective-permute-start(bf16[64,2048]{1,0:T(8,128)(2,1)S(1)} %collective-permute-done.15.refs_1_.refs_0_), channel_id=1, source_target_pairs={{4,0},{8,12},{5,1},{9,13},{6,2},{10,14},{7,3},{11,15},{20,16},{24,... | collective-permute-start | bytes 786440 | tf_op jit(solution)/shard_map/ppermute | solution.py:242
  58.0 14.7 %collective-permute-start.12 = (bf16[64,2048]{1,0:T(8,128)(2,1)S(1)}, bf16[64,2048]{1,0:T(8,128)(2,1)S(1)}, u32[]{:S(2)}, u32[]{:S(2)}) collective-permute-start(bf16[64,2048]{1,0:T(8,128)(2,1)S(1)} %collective-permute-done.10.refs_1_), channel_id=1, source_target_pairs={{4,0},{8,12},{5,1},{9,13},{6,2},{10,14},{7,3},{11,15},{20,16},{24,... | collective-permute-start | bytes 786440 | tf_op jit(solution)/shard_map/ppermute | solution.py:244
  75.7 10.6 %collective-permute-start.20 = (bf16[64,2048]{1,0:T(8,128)(2,1)S(1)}, bf16[64,2048]{1,0:T(8,128)(2,1)S(1)}, u32[]{:S(2)}, u32[]{:S(2)}) collective-permute-start(bf16[64,2048]{1,0:T(8,128)(2,1)S(1)} %collective-permute-done.14.refs_4_.refs_1_), channel_id=1, source_target_pairs={{4,0},{8,12},{5,1},{9,13},{6,2},{10,14},{7,3},{11,15},{20,16},{24,... | collective-permute-start | bytes 786440 | tf_op jit(solution)/shard_map/ppermute | solution.py:244
  77.3 12.7 %collective-permute-start.32 = (bf16[64,2048]{1,0:T(8,128)(2,1)S(1)}, bf16[64,2048]{1,0:T(8,128)(2,1)S(1)}, u32[]{:S(2)}, u32[]{:S(2)}) collective-permute-start(bf16[64,2048]{1,0:T(8,128)(2,1)S(1)} %add_convert_fusion.2.refs_4_), channel_id=1, source_target_pairs={{0,2},{1,3},{2,0},{3,1},{4,6},{5,7},{6,4},{7,5},{8,10},{9,11},{10,... | collective-permute-start | bytes 786440 | tf_op jit(solution)/shard_map/ppermute | solution.py:638
  80.7 12.2 %collective-permute-start.18 = (bf16[64,2048]{1,0:T(8,128)(2,1)S(1)}, bf16[64,2048]{1,0:T(8,128)(2,1)S(1)}, u32[]{:S(2)}, u32[]{:S(2)}) collective-permute-start(bf16[64,2048]{1,0:T(8,128)(2,1)S(1)} %get-tuple-element.44), channel_id=1, source_target_pairs={{0,1},{1,0},{2,3},{3,2},{4,5},{5,4},{6,7},{7,6},{8,9},{9,8},{10,11... | collective-permute-start | bytes 786440 | tf_op jit(solution)/shard_map/ppermute | solution.py:635
  80.8 12.9 %collective-permute-start.26 = (bf16[1,64,4096]{2,1,0:T(8,128)(2,1)S(1)}, bf16[1,64,4096]{2,1,0:T(8,128)(2,1)S(1)}, u32[]{:S(2)}, u32[]{:S(2)}) collective-permute-start(bf16[1,64,4096]{2,1,0:T(8,128)(2,1)S(1)} %get-tuple-element.45.refs_0_), channel_id=1, source_target_pairs={{0,1},{1,0},{2,3},{3,2},{4,5},{5,4},{6,7},{7,6},{8,9},{9,8},{10,11... | collective-permute-start | bytes 1572872 | tf_op jit(solution)/shard_map/ppermute | solution.py:635
  81.3 13.4 %collective-permute-start.27 = (bf16[1,64,4096]{2,1,0:T(8,128)(2,1)S(1)}, bf16[1,64,4096]{2,1,0:T(8,128)(2,1)S(1)}, u32[]{:S(2)}, u32[]{:S(2)}) collective-permute-start(bf16[1,64,4096]{2,1,0:T(8,128)(2,1)S(1)} %collective-permute-done.21.refs_0_.refs_1_), channel_id=1, source_target_pairs={{0,1},{1,0},{2,3},{3,2},{4,5},{5,4},{6,7},{7,6},{8,9},{9,8},{10,11... | collective-permute-start | bytes 1572872 | tf_op jit(solution)/shard_map/ppermute | solution.py:635
  93.1 17.5 %collective-permute-start.17 = (bf16[64,2048]{1,0:T(8,128)(2,1)S(1)}, bf16[64,2048]{1,0:T(8,128)(2,1)S(1)}, u32[]{:S(2)}, u32[]{:S(2)}) collective-permute-start(bf16[64,2048]{1,0:T(8,128)(2,1)S(1)} %get-tuple-element.42), channel_id=1, source_target_pairs={{0,1},{1,0},{2,3},{3,2},{4,5},{5,4},{6,7},{7,6},{8,9},{9,8},{10,11... | collective-permute-start | bytes 786440 | tf_op jit(solution)/shard_map/ppermute | solution.py:635
  93.7 16.9 %collective-permute-start.19 = (bf16[64,2048]{1,0:T(8,128)(2,1)S(1)}, bf16[64,2048]{1,0:T(8,128)(2,1)S(1)}, u32[]{:S(2)}, u32[]{:S(2)}) collective-permute-start(bf16[64,2048]{1,0:T(8,128)(2,1)S(1)} %add_convert_fusion.3), channel_id=1, source_target_pairs={{0,2},{1,3},{2,0},{3,1},{4,6},{5,7},{6,4},{7,5},{8,10},{9,11},{10,... | collective-permute-start | bytes 786440 | tf_op jit(solution)/shard_map/ppermute | solution.py:638
  98.6 9.8 %collective-permute-start.35 = (bf16[64,2048]{1,0:T(8,128)(2,1)S(1)}, bf16[64,2048]{1,0:T(8,128)(2,1)S(1)}, u32[]{:S(2)}, u32[]{:S(2)}) collective-permute-start(bf16[64,2048]{1,0:T(8,128)(2,1)S(1)} %add_convert_fusion), channel_id=1, source_target_pairs={{0,2},{1,3},{2,0},{3,1},{4,6},{5,7},{6,4},{7,5},{8,10},{9,11},{10,... | collective-permute-start | bytes 786440 | tf_op jit(solution)/shard_map/ppermute | solution.py:638
  99.8 10.8 %collective-permute-start.28 = (bf16[64,2048]{1,0:T(8,128)(2,1)S(1)}, bf16[64,2048]{1,0:T(8,128)(2,1)S(1)}, u32[]{:S(2)}, u32[]{:S(2)}) collective-permute-start(bf16[64,2048]{1,0:T(8,128)(2,1)S(1)} %get-tuple-element.50), channel_id=1, source_target_pairs={{0,1},{1,0},{2,3},{3,2},{4,5},{5,4},{6,7},{7,6},{8,9},{9,8},{10,11... | collective-permute-start | bytes 786440 | tf_op jit(solution)/shard_map/ppermute | solution.py:635
  99.9 13.8 %collective-permute-start.30 = (bf16[64,2048]{1,0:T(8,128)(2,1)S(1)}, bf16[64,2048]{1,0:T(8,128)(2,1)S(1)}, u32[]{:S(2)}, u32[]{:S(2)}) collective-permute-start(bf16[64,2048]{1,0:T(8,128)(2,1)S(1)} %add_convert_fusion.1), channel_id=1, source_target_pairs={{0,2},{1,3},{2,0},{3,1},{4,6},{5,7},{6,4},{7,5},{8,10},{9,11},{10,... | collective-permute-start | bytes 786440 | tf_op jit(solution)/shard_map/ppermute | solution.py:638
  (15 other events, 119.1 us)

commit v18 on v17

--- a/solution.py
+++ b/solution.py
@@ -717,17 +717,13 @@
         across = [to_chip(outgoing[(k - 1) * each : k * each], k) for k in range(1, chips)]
         return [own, to_other_core(send_own)] + across, outgoing
 
-    sums, ready = [], ()
-    waits = [pieces[1:chips], ()]
-    for chunk in chunks:
-        rows = chunk(ready)
-        done = [summed(rows, part, waits[part]) for part in range(PARTS)]
-        sums.append([terms for terms, _ in done])
-        ready = [done[0][1]]
-        waits = [
-            [*sums[-1][0][2:], *back_rows[1:chips]],
-            [*back_rows[chips:], *pieces[chips:]],
-        ]
+    first = chunks[0](())
+    first_0 = summed(first, 0, pieces[1:chips])
+    second = chunks[1](())
+    first_1 = summed(first, 1, [second])
+    second_0 = summed(second, 0, [*first_0[0][2:], *back_rows[1:chips]])
+    second_1 = summed(second, 1, [*first_1[0][2:], *back_rows[chips:], *pieces[chips:]])
+    sums = [[first_0[0], first_1[0]], [second_0[0], second_1[0]]]
     up_grad = up_gradient(index_of, index, adapter_count, pieces)
     down_grad = down_gradient(index_of, index, tokens, back_rows)
     projected = None

time: 116 us -> 119 us (1.026)
  waiting for transfers between devices: 43.3 us -> 46.1 us
    ppermute x7, waiting for transfers between devices: 9.2 us -> 13.4 us  [to_chip(): lax.ppermute(value, 'tensor', [(i, i ^ k * CORES) for i in range(parts)])]
    ppermute x2, waiting for transfers between devices: 7.79 us -> 5.39 us  [spread(): outer_3 = lax.ppermute(inner_2, 'dp', [(1, 0), (2, 3)])]
    ppermute x13, waiting for transfers between devices: 2.46 us -> 4.54 us  [to_other_core(): return lax.ppermute(value, 'tensor', [(i, i ^ 1) for i in range(parts)])]
  transfers between devices with their start and end apart: 36 -> 36, of which waited for: 14 -> 13; matrix products, arithmetic and copies ran while one was open for 0% -> 0% of each run, Pallas kernels for 23% -> 24%
where the time goes in v18:
time: 119 us
  waiting for transfers between devices  46.1 us (39%)
  starting transfers between devices  37 us (31%)
  Pallas kernels  33.5 us (28%)
    ppermute x2, waiting for transfers between devices, across_dp(): return lax.ppermute(value, 'dp', [(i, i ^ k) for i in range(owners)])  15.4 us
    ppermute x7, waiting for transfers between devices, to_chip(): lax.ppermute(value, 'tensor', [(i, i ^ k * CORES) for i in range(parts)])  13.4 us
    pallas_call x4, Pallas kernels, split_product(): pl.pallas_call(functools.partial(split_product_kernel, each, half, part *...  9.3 us
    ppermute x7, starting transfers between devices, to_chip(): lax.ppermute(value, 'tensor', [(i, i ^ k * CORES) for i in range(parts)])  8.34 us
    pallas_call x1, Pallas kernels, load_weight(): pl.pallas_call(load_weight_kernel, grid=(1,), in_specs=[pl.BlockSpec(memo...  5.89 us
    ppermute x2, starting transfers between devices, across_dp(): return lax.ppermute(value, 'dp', [(i, i ^ k) for i in range(owners)])  5.43 us
    ppermute x2, waiting for transfers between devices, spread(): outer_3 = lax.ppermute(inner_2, 'dp', [(1, 0), (2, 3)])  5.39 us
    ppermute x1, starting transfers between devices, first(): lax.ppermute(inward, 'dp', [(3, 2), (0, 1)])  4.92 us
  transfers between devices with their start and end apart: 36, of which 13 were waited for; matrix products, arithmetic and copies ran while one was open for 0% of the time, Pallas kernels for 24%

profile of v18, /device:TPU:0, one launch (start us, length us, event | category | flops | bytes accessed | tf_op | source)
XLA Modules:
  0.0 118.7 jit_solution(8517507094073148049)
XLA Ops:
  1.5 1.8 %first_hop.1 = (bf16[128,2048]{1,0:T(8,128)(2,1)S(1)}, bf16[128,2048]{1,0:T(8,128)(2,1)S(1)}) custom-call(s32[14]{0:T(128)S(1)} %concatenate.3.index_ref.refs_0_, bf16[384,2048]{1,0:T(8,128)(2,1)} %tokens_ref.9), custom_call_target="tpu_custom_call" | custom-call | flops 1 | bytes 1 | tf_op jit(solution)/shard_map/first_hop/pallas_call | solution.py:191
  3.3 4.9 %collective-permute-start.4 = (bf16[128,2048]{1,0:T(8,128)(2,1)S(1)}, bf16[128,2048]{1,0:T(8,128)(2,1)S(1)}, u32[]{:S(2)}, u32[]{:S(2)}) collective-permute-start(bf16[128,2048]{1,0:T(8,128)(2,1)S(1)} %get-tuple-element.31.refs_0_), channel_id=1, source_target_pairs={{12,8},{0,4},{13,9},{1,5},{14,10},{2,6},{15,11},{3,7},{28,24},{16,... | collective-permute-start | bytes 1572872 | tf_op jit(solution)/shard_map/ppermute | solution.py:220
  9.0 3.5 %narrow.1 = (f32[2,1,64,128]{3,2,1,0:T(8,128)S(1)}, f32[2,1,64,128]{3,2,1,0:T(8,128)S(1)}, f32[1,64,128]{2,1,0:T(8,128)S(1)}) custom-call(s32[14]{0:T(128)S(1)} %concatenate.3.index_ref.refs_0_, bf16[384,2048]{1,0:T(8,128)(2,1)} %tokens_ref.9, bf16[1,64,2048]{2,1,0:T(8,128)(2,1)} %bitcast.7, bf16[128,4096]{1,0:T(8,128)(2,1)} %cot_ref.3, ...), custom_call_target="tpu_custom_call" | custom-call | flops 1 | bytes 1 | tf_op jit(solution)/shard_map/narrow/pallas_call | solution.py:376
  15.3 2.4 %collective-permute-done.1.refs_0_ = f32[1,64,128]{2,1,0:T(8,128)S(1)} collective-permute-done((f32[1,64,128]{2,1,0:T(8,128)S(1)}, f32[1,64,128]{2,1,0:T(8,128)S(1)}, u32[]{:S(2)}, u32[]{:S(2)}) %collective-permute-start.1) | collective-permute-done | bytes 32800 | tf_op jit(solution)/shard_map/ppermute | solution.py:638
  17.8 2.1 %collective-permute-start.2 = (f32[2,1,64,128]{3,2,1,0:T(8,128)S(1)}, f32[2,1,64,128]{3,2,1,0:T(8,128)S(1)}, u32[]{:S(2)}, u32[]{:S(2)}) collective-permute-start(f32[2,1,64,128]{3,2,1,0:T(8,128)S(1)} %merge.1), channel_id=1, source_target_pairs={{0,8},{4,12},{8,0},{12,4},{1,9},{5,13},{9,1},{13,5},{2,10},{6,14},... | collective-permute-start | bytes 196616 | tf_op jit(solution)/shard_map/ppermute | solution.py:641
  19.9 5.5 %collective-permute-done.2 = f32[2,1,64,128]{3,2,1,0:T(8,128)S(1)} collective-permute-done((f32[2,1,64,128]{3,2,1,0:T(8,128)S(1)}, f32[2,1,64,128]{3,2,1,0:T(8,128)S(1)}, u32[]{:S(2)}, u32[]{:S(2)}) %collective-permute-start.2) | collective-permute-done | bytes 65568 | tf_op jit(solution)/shard_map/ppermute | solution.py:641
  26.1 1.9 %collective-permute-start.6 = (bf16[128,2048]{1,0:T(8,128)(2,1)S(1)}, bf16[128,2048]{1,0:T(8,128)(2,1)S(1)}, u32[]{:S(2)}, u32[]{:S(2)}) collective-permute-start(bf16[128,2048]{1,0:T(8,128)(2,1)S(1)} %get-tuple-element.37), channel_id=1, source_target_pairs={{4,0},{0,4},{12,8},{5,1},{1,5},{13,9},{6,2},{2,6},{14,10},{7,3},{3... | collective-permute-start | bytes 1572872 | tf_op jit(solution)/shard_map/ppermute | solution.py:230
  28.7 3.3 %collective-permute-start.3 = (f32[2,1,64,128]{3,2,1,0:T(8,128)S(1)}, f32[2,1,64,128]{3,2,1,0:T(8,128)S(1)}, u32[]{:S(2)}, u32[]{:S(2)}) collective-permute-start(f32[2,1,64,128]{3,2,1,0:T(8,128)S(1)} %add.31.sum_ref.refs_0_), channel_id=1, source_target_pairs={{0,4},{4,0},{8,12},{12,8},{1,5},{5,1},{9,13},{13,9},{2,6},{6,2},{1... | collective-permute-start | bytes 196616 | tf_op jit(solution)/shard_map/ppermute | solution.py:641
  32.0 9.9 %collective-permute-done.3.refs_0_ = f32[2,1,64,128]{3,2,1,0:T(8,128)S(1)} collective-permute-done((f32[2,1,64,128]{3,2,1,0:T(8,128)S(1)}, f32[2,1,64,128]{3,2,1,0:T(8,128)S(1)}, u32[]{:S(2)}, u32[]{:S(2)}) %collective-permute-start.3) | collective-permute-done | bytes 65568 | tf_op jit(solution)/shard_map/ppermute | solution.py:641
  42.6 2.3 %collective-permute-start.8 = (bf16[64,2048]{1,0:T(8,128)(2,1)S(1)}, bf16[64,2048]{1,0:T(8,128)(2,1)S(1)}, u32[]{:S(2)}, u32[]{:S(2)}) collective-permute-start(bf16[64,2048]{1,0:T(8,128)(2,1)S(1)} %get-tuple-element.39.home_ref), channel_id=1, source_target_pairs={{0,4},{4,0},{8,12},{12,8},{1,5},{5,1},{9,13},{13,9},{2,6},{6,2},{1... | collective-permute-start | bytes 786440 | tf_op jit(solution)/shard_map/ppermute | solution.py:240
  47.8 3.8 %collective-permute-done.8.outer_ref = bf16[64,2048]{1,0:T(8,128)(2,1)S(1)} collective-permute-done((bf16[64,2048]{1,0:T(8,128)(2,1)S(1)}, bf16[64,2048]{1,0:T(8,128)(2,1)S(1)}, u32[]{:S(2)}, u32[]{:S(2)}) %collective-permute-start.8) | collective-permute-done | bytes 262176 | tf_op jit(solution)/shard_map/ppermute | solution.py:240
  59.3 5.9 %load_weight.1.refs_6_.w_ref = bf16[2048,4096]{1,0:T(8,128)(2,1)S(1)} custom-call(bf16[2048,4096]{1,0:T(8,128)(2,1)} %w_ref.1, bf16[64,2048]{1,0:T(8,128)(2,1)S(1)} %collective-permute-done.13.refs_0_.outer_ref, bf16[64,2048]{1,0:T(8,128)(2,1)S(1)} %collective-permute-done.15.refs_1_.refs_0_), custom_call_target="tpu_custom_call" | custom-call | flops 1 | bytes 1 | tf_op jit(solution)/shard_map/load_weight/pallas_call | solution.py:284
  66.5 3.6 %collective-permute-done.16.refs_5_.refs_2_ = bf16[64,2048]{1,0:T(8,128)(2,1)S(1)} collective-permute-done((bf16[64,2048]{1,0:T(8,128)(2,1)S(1)}, bf16[64,2048]{1,0:T(8,128)(2,1)S(1)}, u32[]{:S(2)}, u32[]{:S(2)}) %collective-permute-start.16) | collective-permute-done | bytes 262176 | tf_op jit(solution)/shard_map/ppermute | solution.py:242
  70.1 5.4 %collective-permute-done.12.refs_3_ = bf16[64,2048]{1,0:T(8,128)(2,1)S(1)} collective-permute-done((bf16[64,2048]{1,0:T(8,128)(2,1)S(1)}, bf16[64,2048]{1,0:T(8,128)(2,1)S(1)}, u32[]{:S(2)}, u32[]{:S(2)}) %collective-permute-start.12) | collective-permute-done | bytes 262176 | tf_op jit(solution)/shard_map/ppermute | solution.py:244
  76.1 2.3 %split_product.6 = (bf16[64,2048]{1,0:T(8,128)(2,1)S(1)}, bf16[64,2048]{1,0:T(8,128)(2,1)S(1)}, f32[64,2048]{1,0:T(8,128)S(1)}, f32[64,2048]{1,0:T(8,128)S(1)}) custom-call(bf16[256,2048]{1,0:T(8,128)(2,1)S(1)} %collect.2.rows_ref, bf16[2048,4096]{1,0:T(8,128)(2,1)S(1)} %load_weight.1.refs_6_.w_ref, ...), custom_call_target="tpu_custom_call" | custom-call | flops 1 | bytes 1 | tf_op jit(solution)/shard_map/split_product/pallas_call | solution.py:317
  80.4 2.3 %split_product.4 = (bf16[64,2048]{1,0:T(8,128)(2,1)S(1)}, bf16[64,2048]{1,0:T(8,128)(2,1)S(1)}, f32[64,2048]{1,0:T(8,128)S(1)}, f32[64,2048]{1,0:T(8,128)S(1)}) custom-call(bf16[256,2048]{1,0:T(8,128)(2,1)S(1)} %collect.2.rows_ref, bf16[2048,4096]{1,0:T(8,128)(2,1)S(1)} %load_weight.1.refs_6_.w_ref, bf16[256,2048]{1,0:T(8,128)(2,1)S(1)} %collect.3.refs_0_.rows_ref), custom_call_target="tpu_custom_call" | custom-call | flops 1 | bytes 1 | tf_op jit(solution)/shard_map/split_product/pallas_call | solution.py:317
  86.0 6.6 %collective-permute-done.32.refs_0_.refs_5_ = bf16[64,2048]{1,0:T(8,128)(2,1)S(1)} collective-permute-done((bf16[64,2048]{1,0:T(8,128)(2,1)S(1)}, bf16[64,2048]{1,0:T(8,128)(2,1)S(1)}, u32[]{:S(2)}, u32[]{:S(2)}) %collective-permute-start.32) | collective-permute-done | bytes 262176 | tf_op jit(solution)/shard_map/ppermute | solution.py:638
  92.6 2.3 %split_product.7 = (bf16[64,2048]{1,0:T(8,128)(2,1)S(1)}, bf16[64,2048]{1,0:T(8,128)(2,1)S(1)}, f32[64,2048]{1,0:T(8,128)S(1)}, f32[64,2048]{1,0:T(8,128)S(1)}) custom-call(bf16[256,2048]{1,0:T(8,128)(2,1)S(1)} %collect.3.refs_0_.rows_ref, bf16[2048,4096]{1,0:T(8,128)(2,1)S(1)} %load_weight.1.refs_6_.w_ref, ...), custom_call_target="tpu_custom_call" | custom-call | flops 1 | bytes 1 | tf_op jit(solution)/shard_map/split_product/pallas_call | solution.py:317
  98.3 2.3 %split_product.5 = (bf16[64,2048]{1,0:T(8,128)(2,1)S(1)}, bf16[64,2048]{1,0:T(8,128)(2,1)S(1)}, f32[64,2048]{1,0:T(8,128)S(1)}, f32[64,2048]{1,0:T(8,128)S(1)}) custom-call(bf16[256,2048]{1,0:T(8,128)(2,1)S(1)} %collect.3.refs_0_.rows_ref, bf16[2048,4096]{1,0:T(8,128)(2,1)S(1)} %load_weight.1.refs_6_.w_ref, ...), custom_call_target="tpu_custom_call" | custom-call | flops 1 | bytes 1 | tf_op jit(solution)/shard_map/split_product/pallas_call | solution.py:317
  106.1 3.9 %up_gradient.1.refs_9_ = f32[4,64,4096]{2,1,0:T(8,128)} custom-call(s32[14]{0:T(128)S(1)} %concatenate.3.index_ref.refs_0_, bf16[1,64,4096]{2,1,0:T(8,128)(2,1)S(1)} %get-tuple-element.46.refs_0_, bf16[1,64,4096]{2,1,0:T(8,128)(2,1)S(1)} %collective-permute-done.25.refs_0_.refs_1_, bf16[1,64,4096]{2,1,0:T(8,128)(2,1)S(1)} %collective-permute-done.24.refs_3_.refs_2_, ...), custom_call_target="tpu_custom_call" | custom-call | flops 1 | bytes 1 | tf_op jit(solution)/shard_map/up_gradient/pallas_call | solution.py:526
  110.0 1.7 %collective-permute-done.35.refs_8_ = bf16[64,2048]{1,0:T(8,128)(2,1)S(1)} collective-permute-done((bf16[64,2048]{1,0:T(8,128)(2,1)S(1)}, bf16[64,2048]{1,0:T(8,128)(2,1)S(1)}, u32[]{:S(2)}, u32[]{:S(2)}) %collective-permute-start.35) | collective-permute-done | bytes 262176 | tf_op jit(solution)/shard_map/ppermute | solution.py:638
  111.7 2.1 %finish.2.refs_9_ = bf16[128,4096]{1,0:T(8,128)(2,1)} custom-call(s32[14]{0:T(128)S(1)} %concatenate.3.index_ref.refs_0_, bf16[1,64,128]{2,1,0:T(8,128)(2,1)S(1)} %get-tuple-element.35.refs_1_, bf16[4,64,4096]{2,1,0:T(8,128)(2,1)S(1)} %copy-done.1, f32[64,2048]{1,0:T(8,128)S(1)} %get-tuple-element.51.refs_3_, ...), custom_call_target="tpu_custom_call" | custom-call | flops 1 | bytes 1 | tf_op jit(solution)/shard_map/finish/pallas_call | solution.py:596
  113.8 2.7 %collective-permute-done.29.refs_8_ = bf16[64,2048]{1,0:T(8,128)(2,1)S(1)} collective-permute-done((bf16[64,2048]{1,0:T(8,128)(2,1)S(1)}, bf16[64,2048]{1,0:T(8,128)(2,1)S(1)}, u32[]{:S(2)}, u32[]{:S(2)}) %collective-permute-start.29) | collective-permute-done | bytes 262176 | tf_op jit(solution)/shard_map/ppermute | solution.py:638
  116.6 2.1 %finish.3 = bf16[128,4096]{1,0:T(8,128)(2,1)} custom-call(s32[14]{0:T(128)S(1)} %concatenate.3.index_ref.refs_0_, bf16[1,64,128]{2,1,0:T(8,128)(2,1)S(1)} %get-tuple-element.35.refs_1_, bf16[4,64,4096]{2,1,0:T(8,128)(2,1)S(1)} %copy-done.1, f32[64,2048]{1,0:T(8,128)S(1)} %get-tuple-element.41.refs_3_, ...), custom_call_target="tpu_custom_call", output_to_operand_aliasing={{}: (9, {})} | custom-call | flops 1 | bytes 1 | tf_op jit(solution)/shard_map/finish/pallas_call | solution.py:596
  (78 shorter events, 32.9 us)
Async XLA Ops:
  3.3 22.1 %collective-permute-start.4 = (bf16[128,2048]{1,0:T(8,128)(2,1)S(1)}, bf16[128,2048]{1,0:T(8,128)(2,1)S(1)}, u32[]{:S(2)}, u32[]{:S(2)}) collective-permute-start(bf16[128,2048]{1,0:T(8,128)(2,1)S(1)} %get-tuple-element.31.refs_0_), channel_id=1, source_target_pairs={{12,8},{0,4},{13,9},{1,5},{14,10},{2,6},{15,11},{3,7},{28,24},{16,... | collective-permute-start | bytes 1572872 | tf_op jit(solution)/shard_map/ppermute | solution.py:220
  8.3 17.2 %collective-permute-start.5 = (bf16[128,2048]{1,0:T(8,128)(2,1)S(1)}, bf16[128,2048]{1,0:T(8,128)(2,1)S(1)}, u32[]{:S(2)}, u32[]{:S(2)}) collective-permute-start(bf16[128,2048]{1,0:T(8,128)(2,1)S(1)} %get-tuple-element.36), channel_id=1, source_target_pairs={{8,4},{9,5},{10,6},{11,7},{24,20},{25,21},{26,22},{27,23}} | collective-permute-start | bytes 1572872 | tf_op jit(solution)/shard_map/ppermute | solution.py:221
  26.1 15.8 %collective-permute-start.6 = (bf16[128,2048]{1,0:T(8,128)(2,1)S(1)}, bf16[128,2048]{1,0:T(8,128)(2,1)S(1)}, u32[]{:S(2)}, u32[]{:S(2)}) collective-permute-start(bf16[128,2048]{1,0:T(8,128)(2,1)S(1)} %get-tuple-element.37), channel_id=1, source_target_pairs={{4,0},{0,4},{12,8},{5,1},{1,5},{13,9},{6,2},{2,6},{14,10},{7,3},{3... | collective-permute-start | bytes 1572872 | tf_op jit(solution)/shard_map/ppermute | solution.py:230
  28.0 13.9 %collective-permute-start.7 = (bf16[128,2048]{1,0:T(8,128)(2,1)S(1)}, bf16[128,2048]{1,0:T(8,128)(2,1)S(1)}, u32[]{:S(2)}, u32[]{:S(2)}) collective-permute-start(bf16[128,2048]{1,0:T(8,128)(2,1)S(1)} %get-tuple-element.38), channel_id=1, source_target_pairs={{8,4},{4,8},{9,5},{5,9},{10,6},{6,10},{11,7},{7,11},{24,20},{20,24... | collective-permute-start | bytes 1572872 | tf_op jit(solution)/shard_map/ppermute | solution.py:231
  28.7 13.2 %collective-permute-start.3 = (f32[2,1,64,128]{3,2,1,0:T(8,128)S(1)}, f32[2,1,64,128]{3,2,1,0:T(8,128)S(1)}, u32[]{:S(2)}, u32[]{:S(2)}) collective-permute-start(f32[2,1,64,128]{3,2,1,0:T(8,128)S(1)} %add.31.sum_ref.refs_0_), channel_id=1, source_target_pairs={{0,4},{4,0},{8,12},{12,8},{1,5},{5,1},{9,13},{13,9},{2,6},{6,2},{1... | collective-permute-start | bytes 196616 | tf_op jit(solution)/shard_map/ppermute | solution.py:641
  42.6 9.1 %collective-permute-start.8 = (bf16[64,2048]{1,0:T(8,128)(2,1)S(1)}, bf16[64,2048]{1,0:T(8,128)(2,1)S(1)}, u32[]{:S(2)}, u32[]{:S(2)}) collective-permute-start(bf16[64,2048]{1,0:T(8,128)(2,1)S(1)} %get-tuple-element.39.home_ref), channel_id=1, source_target_pairs={{0,4},{4,0},{8,12},{12,8},{1,5},{5,1},{9,13},{13,9},{2,6},{6,2},{1... | collective-permute-start | bytes 786440 | tf_op jit(solution)/shard_map/ppermute | solution.py:240
  44.9 9.8 %collective-permute-start.9 = (bf16[64,2048]{1,0:T(8,128)(2,1)S(1)}, bf16[64,2048]{1,0:T(8,128)(2,1)S(1)}, u32[]{:S(2)}, u32[]{:S(2)}) collective-permute-start(bf16[64,2048]{1,0:T(8,128)(2,1)S(1)} %get-tuple-element.39.home_ref), channel_id=1, source_target_pairs={{4,8},{8,4},{5,9},{9,5},{6,10},{10,6},{7,11},{11,7},{20,24},{24,20... | collective-permute-start | bytes 786440 | tf_op jit(solution)/shard_map/ppermute | solution.py:241
  45.5 10.5 %collective-permute-start.13 = (bf16[64,2048]{1,0:T(8,128)(2,1)S(1)}, bf16[64,2048]{1,0:T(8,128)(2,1)S(1)}, u32[]{:S(2)}, u32[]{:S(2)}) collective-permute-start(bf16[64,2048]{1,0:T(8,128)(2,1)S(1)} %get-tuple-element.40.home_ref), channel_id=1, source_target_pairs={{0,4},{4,0},{8,12},{12,8},{1,5},{5,1},{9,13},{13,9},{2,6},{6,2},{1... | collective-permute-start | bytes 786440 | tf_op jit(solution)/shard_map/ppermute | solution.py:240
  47.2 9.5 %collective-permute-start.15 = (bf16[64,2048]{1,0:T(8,128)(2,1)S(1)}, bf16[64,2048]{1,0:T(8,128)(2,1)S(1)}, u32[]{:S(2)}, u32[]{:S(2)}) collective-permute-start(bf16[64,2048]{1,0:T(8,128)(2,1)S(1)} %get-tuple-element.40.home_ref), channel_id=1, source_target_pairs={{4,8},{8,4},{5,9},{9,5},{6,10},{10,6},{7,11},{11,7},{20,24},{24,20... | collective-permute-start | bytes 786440 | tf_op jit(solution)/shard_map/ppermute | solution.py:241
  53.1 23.0 %collective-permute-start.25 = (bf16[1,64,4096]{2,1,0:T(8,128)(2,1)S(1)}, bf16[1,64,4096]{2,1,0:T(8,128)(2,1)S(1)}, u32[]{:S(2)}, u32[]{:S(2)}) collective-permute-start(bf16[1,64,4096]{2,1,0:T(8,128)(2,1)S(1)} %get-tuple-element.46.refs_0_), channel_id=1, source_target_pairs={{0,2},{1,3},{2,0},{3,1},{4,6},{5,7},{6,4},{7,5},{8,10},{9,11},{10,... | collective-permute-start | bytes 1572872 | tf_op jit(solution)/shard_map/ppermute | solution.py:638
  54.7 11.8 %collective-permute-start.11 = (bf16[64,2048]{1,0:T(8,128)(2,1)S(1)}, bf16[64,2048]{1,0:T(8,128)(2,1)S(1)}, u32[]{:S(2)}, u32[]{:S(2)}) collective-permute-start(bf16[64,2048]{1,0:T(8,128)(2,1)S(1)} %collective-permute-done.9.refs_0_), channel_id=1, source_target_pairs={{4,0},{8,12},{5,1},{9,13},{6,2},{10,14},{7,3},{11,15},{20,16},{24,... | collective-permute-start | bytes 786440 | tf_op jit(solution)/shard_map/ppermute | solution.py:242
  56.0 9.2 %collective-permute-start.14 = (bf16[64,2048]{1,0:T(8,128)(2,1)S(1)}, bf16[64,2048]{1,0:T(8,128)(2,1)S(1)}, u32[]{:S(2)}, u32[]{:S(2)}) collective-permute-start(bf16[64,2048]{1,0:T(8,128)(2,1)S(1)} %collective-permute-done.13.refs_0_.outer_ref), channel_id=1, source_target_pairs={{4,8},{8,4},{5,9},{9,5},{6,10},{10,6},{7,11},{11,7},{20,24},{24,20... | collective-permute-start | bytes 786440 | tf_op jit(solution)/shard_map/ppermute | solution.py:243
  56.7 13.4 %collective-permute-start.16 = (bf16[64,2048]{1,0:T(8,128)(2,1)S(1)}, bf16[64,2048]{1,0:T(8,128)(2,1)S(1)}, u32[]{:S(2)}, u32[]{:S(2)}) collective-permute-start(bf16[64,2048]{1,0:T(8,128)(2,1)S(1)} %collective-permute-done.15.refs_1_.refs_0_), channel_id=1, source_target_pairs={{4,0},{8,12},{5,1},{9,13},{6,2},{10,14},{7,3},{11,15},{20,16},{24,... | collective-permute-start | bytes 786440 | tf_op jit(solution)/shard_map/ppermute | solution.py:242
  58.0 17.5 %collective-permute-start.12 = (bf16[64,2048]{1,0:T(8,128)(2,1)S(1)}, bf16[64,2048]{1,0:T(8,128)(2,1)S(1)}, u32[]{:S(2)}, u32[]{:S(2)}) collective-permute-start(bf16[64,2048]{1,0:T(8,128)(2,1)S(1)} %collective-permute-done.10.refs_1_), channel_id=1, source_target_pairs={{4,0},{8,12},{5,1},{9,13},{6,2},{10,14},{7,3},{11,15},{20,16},{24,... | collective-permute-start | bytes 786440 | tf_op jit(solution)/shard_map/ppermute | solution.py:244
  65.2 14.5 %collective-permute-start.17 = (bf16[64,2048]{1,0:T(8,128)(2,1)S(1)}, bf16[64,2048]{1,0:T(8,128)(2,1)S(1)}, u32[]{:S(2)}, u32[]{:S(2)}) collective-permute-start(bf16[64,2048]{1,0:T(8,128)(2,1)S(1)} %collective-permute-done.14.refs_4_.refs_1_), channel_id=1, source_target_pairs={{4,0},{8,12},{5,1},{9,13},{6,2},{10,14},{7,3},{11,15},{20,16},{24,... | collective-permute-start | bytes 786440 | tf_op jit(solution)/shard_map/ppermute | solution.py:244
  78.5 19.4 %collective-permute-start.24 = (bf16[1,64,4096]{2,1,0:T(8,128)(2,1)S(1)}, bf16[1,64,4096]{2,1,0:T(8,128)(2,1)S(1)}, u32[]{:S(2)}, u32[]{:S(2)}) collective-permute-start(bf16[1,64,4096]{2,1,0:T(8,128)(2,1)S(1)} %get-tuple-element.46.refs_0_), channel_id=1, source_target_pairs={{0,1},{1,0},{2,3},{3,2},{4,5},{5,4},{6,7},{7,6},{8,9},{9,8},{10,11... | collective-permute-start | bytes 1572872 | tf_op jit(solution)/shard_map/ppermute | solution.py:635
  80.3 17.9 %collective-permute-start.26 = (bf16[1,64,4096]{2,1,0:T(8,128)(2,1)S(1)}, bf16[1,64,4096]{2,1,0:T(8,128)(2,1)S(1)}, u32[]{:S(2)}, u32[]{:S(2)}) collective-permute-start(bf16[1,64,4096]{2,1,0:T(8,128)(2,1)S(1)} %collective-permute-done.25.refs_0_.refs_1_), channel_id=1, source_target_pairs={{0,1},{1,0},{2,3},{3,2},{4,5},{5,4},{6,7},{7,6},{8,9},{9,8},{10,11... | collective-permute-start | bytes 1572872 | tf_op jit(solution)/shard_map/ppermute | solution.py:635
  83.4 9.2 %collective-permute-start.32 = (bf16[64,2048]{1,0:T(8,128)(2,1)S(1)}, bf16[64,2048]{1,0:T(8,128)(2,1)S(1)}, u32[]{:S(2)}, u32[]{:S(2)}) collective-permute-start(bf16[64,2048]{1,0:T(8,128)(2,1)S(1)} %add_convert_fusion.1), channel_id=1, source_target_pairs={{0,2},{1,3},{2,0},{3,1},{4,6},{5,7},{6,4},{7,5},{8,10},{9,11},{10,... | collective-permute-start | bytes 786440 | tf_op jit(solution)/shard_map/ppermute | solution.py:638
  84.9 13.4 %collective-permute-start.20 = (bf16[64,2048]{1,0:T(8,128)(2,1)S(1)}, bf16[64,2048]{1,0:T(8,128)(2,1)S(1)}, u32[]{:S(2)}, u32[]{:S(2)}) collective-permute-start(bf16[64,2048]{1,0:T(8,128)(2,1)S(1)} %add_convert_fusion.3), channel_id=1, source_target_pairs={{0,2},{1,3},{2,0},{3,1},{4,6},{5,7},{6,4},{7,5},{8,10},{9,11},{10,... | collective-permute-start | bytes 786440 | tf_op jit(solution)/shard_map/ppermute | solution.py:638
  97.7 16.1 %collective-permute-start.18 = (bf16[64,2048]{1,0:T(8,128)(2,1)S(1)}, bf16[64,2048]{1,0:T(8,128)(2,1)S(1)}, u32[]{:S(2)}, u32[]{:S(2)}) collective-permute-start(bf16[64,2048]{1,0:T(8,128)(2,1)S(1)} %get-tuple-element.42), channel_id=1, source_target_pairs={{0,1},{1,0},{2,3},{3,2},{4,5},{5,4},{6,7},{7,6},{8,9},{9,8},{10,11... | collective-permute-start | bytes 786440 | tf_op jit(solution)/shard_map/ppermute | solution.py:635
  100.6 13.3 %collective-permute-start.27 = (bf16[64,2048]{1,0:T(8,128)(2,1)S(1)}, bf16[64,2048]{1,0:T(8,128)(2,1)S(1)}, u32[]{:S(2)}, u32[]{:S(2)}) collective-permute-start(bf16[64,2048]{1,0:T(8,128)(2,1)S(1)} %get-tuple-element.48), channel_id=1, source_target_pairs={{0,1},{1,0},{2,3},{3,2},{4,5},{5,4},{6,7},{7,6},{8,9},{9,8},{10,11... | collective-permute-start | bytes 786440 | tf_op jit(solution)/shard_map/ppermute | solution.py:635
  101.2 8.9 %collective-permute-start.33 = (bf16[64,2048]{1,0:T(8,128)(2,1)S(1)}, bf16[64,2048]{1,0:T(8,128)(2,1)S(1)}, u32[]{:S(2)}, u32[]{:S(2)}) collective-permute-start(bf16[64,2048]{1,0:T(8,128)(2,1)S(1)} %get-tuple-element.56), channel_id=1, source_target_pairs={{0,1},{1,0},{2,3},{3,2},{4,5},{5,4},{6,7},{7,6},{8,9},{9,8},{10,11... | collective-permute-start | bytes 786440 | tf_op jit(solution)/shard_map/ppermute | solution.py:635
  102.6 9.1 %collective-permute-start.35 = (bf16[64,2048]{1,0:T(8,128)(2,1)S(1)}, bf16[64,2048]{1,0:T(8,128)(2,1)S(1)}, u32[]{:S(2)}, u32[]{:S(2)}) collective-permute-start(bf16[64,2048]{1,0:T(8,128)(2,1)S(1)} %add_convert_fusion), channel_id=1, source_target_pairs={{0,2},{1,3},{2,0},{3,1},{4,6},{5,7},{6,4},{7,5},{8,10},{9,11},{10,... | collective-permute-start | bytes 786440 | tf_op jit(solution)/shard_map/ppermute | solution.py:638
  104.0 12.5 %collective-permute-start.29 = (bf16[64,2048]{1,0:T(8,128)(2,1)S(1)}, bf16[64,2048]{1,0:T(8,128)(2,1)S(1)}, u32[]{:S(2)}, u32[]{:S(2)}) collective-permute-start(bf16[64,2048]{1,0:T(8,128)(2,1)S(1)} %add_convert_fusion.2), channel_id=1, source_target_pairs={{0,2},{1,3},{2,0},{3,1},{4,6},{5,7},{6,4},{7,5},{8,10},{9,11},{10,... | collective-permute-start | bytes 786440 | tf_op jit(solution)/shard_map/ppermute | solution.py:638
  (15 other events, 122.3 us)

commit v19 on v18

--- a/solution.py
+++ b/solution.py
@@ -329,6 +329,25 @@
         cost_estimate=BRIEF,
         name="split_product",
     )(in_vmem(rows), in_vmem(weight), *extra)
+
+
+def leaving_kernel(other_ref, arrived_ref, *refs):
+    total = other_ref[...] + arrived_ref[...].astype(jnp.float32)
+    refs[-1][...] = total.astype(refs[-1].dtype)
+
+
+def leaving(other, arrived, waits):
+    specs, extra = after(waits)
+    return pl.pallas_call(
+        leaving_kernel,
+        grid=(1,),
+        in_specs=[held(), held()] + specs,
+        out_specs=held(),
+        out_shape=pltpu.VMEM(other.shape, arrived.dtype),
+        compiler_params=SMALL,
+        cost_estimate=BRIEF,
+        name="leaving",
+    )(in_vmem(other), in_vmem(arrived), *extra)
 
 
 def narrow_kernel(index_of, index_ref, tokens_ref, down_ref, cot_ref, up_ref, *refs):
@@ -710,10 +729,10 @@
             lambda waits, s=s, count=count: picked[:, s : s + count].reshape(-1, width_dev)
             for s, count in zip(starts, CHUNK_ROWS)
         ]
-    def summed(rows, part, waits):
+    def summed(rows, part, waits, late=()):
         each = rows.shape[0] // parts
         send_own, send, own, other = split_product(shape, rows, weight, part, PARTS, waits)
-        outgoing = (other + to_other_core(send).astype(jnp.float32)).astype(jnp.bfloat16)
+        outgoing = leaving(other, to_other_core(send), late)
         across = [to_chip(outgoing[(k - 1) * each : k * each], k) for k in range(1, chips)]
         return [own, to_other_core(send_own)] + across, outgoing
 
@@ -721,8 +740,8 @@
     first_0 = summed(first, 0, pieces[1:chips])
     second = chunks[1](())
     first_1 = summed(first, 1, [second])
-    second_0 = summed(second, 0, [*first_0[0][2:], *back_rows[1:chips]])
-    second_1 = summed(second, 1, [*first_1[0][2:], *back_rows[chips:], *pieces[chips:]])
+    second_0 = summed(second, 0, back_rows[1:chips], first_0[0][2:])
+    second_1 = summed(second, 1, [*back_rows[chips:], *pieces[chips:]], first_1[0][2:])
     sums = [[first_0[0], first_1[0]], [second_0[0], second_1[0]]]
     up_grad = up_gradient(index_of, index, adapter_count, pieces)
     down_grad = down_gradient(index_of, index, tokens, back_rows)

time: 119 us -> 118 us (level)
  starting transfers between devices: 37 us -> 34 us
  waiting for transfers between devices: 46.1 us -> 47.8 us
    ppermute x7, waiting for transfers between devices: 13.4 us -> 17.1 us  [to_chip(): lax.ppermute(value, 'tensor', [(i, i ^ k * CORES) for i in range(parts)])]
    ppermute x13, waiting for transfers between devices: 4.54 us -> 1.27 us  [to_other_core(): return lax.ppermute(value, 'tensor', [(i, i ^ 1) for i in range(parts)])]
    ppermute x2, waiting for transfers between devices: 3.55 us -> 6.34 us  [spread(): outer_2 = lax.ppermute(inner, 'dp', [(1, 0), (2, 3)])]
    ppermute x13, starting transfers between devices: 3.22 us -> 1.61 us  [to_other_core(): return lax.ppermute(value, 'tensor', [(i, i ^ 1) for i in range(parts)])]
    ppermute x7, starting transfers between devices: 8.34 us -> 7 us  [to_chip(): lax.ppermute(value, 'tensor', [(i, i ^ k * CORES) for i in range(parts)])]
where the time goes in v19:
time: 118 us; the launch traced here: 117 us
  waiting for transfers between devices  47.8 us (41%)
  starting transfers between devices  34 us (29%)
  Pallas kernels  33.6 us (28%)
    ppermute x7, waiting for transfers between devices, to_chip(): lax.ppermute(value, 'tensor', [(i, i ^ k * CORES) for i in range(parts)])  17.1 us
    ppermute x2, waiting for transfers between devices, across_dp(): return lax.ppermute(value, 'dp', [(i, i ^ k) for i in range(owners)])  15.4 us
    pallas_call x4, Pallas kernels, split_product(): pl.pallas_call(functools.partial(split_product_kernel, each, half, part *...  9.3 us
    ppermute x7, starting transfers between devices, to_chip(): lax.ppermute(value, 'tensor', [(i, i ^ k * CORES) for i in range(parts)])  7 us
    ppermute x2, waiting for transfers between devices, spread(): outer_2 = lax.ppermute(inner, 'dp', [(1, 0), (2, 3)])  6.34 us
    pallas_call x1, Pallas kernels, load_weight(): pl.pallas_call(load_weight_kernel, grid=(1,), in_specs=[pl.BlockSpec(memo...  5.89 us
    ppermute x2, starting transfers between devices, across_dp(): return lax.ppermute(value, 'dp', [(i, i ^ k) for i in range(owners)])  5.43 us
    ppermute x1, starting transfers between devices, first(): lax.ppermute(inward, 'dp', [(3, 2), (0, 1)])  4.96 us
  transfers between devices with their start and end apart: 36, of which 13 were waited for; matrix products, arithmetic and copies ran while one was open for 0% of the time, Pallas kernels for 24%

profile of v19, /device:TPU:0, one launch (start us, length us, event | category | flops | bytes accessed | tf_op | source)
XLA Modules:
  0.0 117.4 jit_solution(11331578461670988675)
XLA Ops:
  3.3 5.0 %collective-permute-start.4 = (bf16[128,2048]{1,0:T(8,128)(2,1)S(1)}, bf16[128,2048]{1,0:T(8,128)(2,1)S(1)}, u32[]{:S(2)}, u32[]{:S(2)}) collective-permute-start(bf16[128,2048]{1,0:T(8,128)(2,1)S(1)} %get-tuple-element.31.refs_0_), channel_id=1, source_target_pairs={{12,8},{0,4},{13,9},{1,5},{14,10},{2,6},{15,11},{3,7},{28,24},{16,... | collective-permute-start | bytes 1572872 | tf_op jit(solution)/shard_map/ppermute | solution.py:220
  9.0 3.5 %narrow.1 = (f32[2,1,64,128]{3,2,1,0:T(8,128)S(1)}, f32[2,1,64,128]{3,2,1,0:T(8,128)S(1)}, f32[1,64,128]{2,1,0:T(8,128)S(1)}) custom-call(s32[14]{0:T(128)S(1)} %concatenate.3.index_ref.refs_0_, bf16[384,2048]{1,0:T(8,128)(2,1)} %tokens_ref.9, bf16[1,64,2048]{2,1,0:T(8,128)(2,1)} %bitcast.7, bf16[128,4096]{1,0:T(8,128)(2,1)} %cot_ref.3, ...), custom_call_target="tpu_custom_call" | custom-call | flops 1 | bytes 1 | tf_op jit(solution)/shard_map/narrow/pallas_call | solution.py:395
  15.3 2.4 %collective-permute-done.1.refs_0_ = f32[1,64,128]{2,1,0:T(8,128)S(1)} collective-permute-done((f32[1,64,128]{2,1,0:T(8,128)S(1)}, f32[1,64,128]{2,1,0:T(8,128)S(1)}, u32[]{:S(2)}, u32[]{:S(2)}) %collective-permute-start.1) | collective-permute-done | bytes 32800 | tf_op jit(solution)/shard_map/ppermute | solution.py:657
  17.8 2.1 %collective-permute-start.2 = (f32[2,1,64,128]{3,2,1,0:T(8,128)S(1)}, f32[2,1,64,128]{3,2,1,0:T(8,128)S(1)}, u32[]{:S(2)}, u32[]{:S(2)}) collective-permute-start(f32[2,1,64,128]{3,2,1,0:T(8,128)S(1)} %merge.1), channel_id=1, source_target_pairs={{0,8},{4,12},{8,0},{12,4},{1,9},{5,13},{9,1},{13,5},{2,10},{6,14},... | collective-permute-start | bytes 196616 | tf_op jit(solution)/shard_map/ppermute | solution.py:660
  19.9 5.5 %collective-permute-done.2 = f32[2,1,64,128]{3,2,1,0:T(8,128)S(1)} collective-permute-done((f32[2,1,64,128]{3,2,1,0:T(8,128)S(1)}, f32[2,1,64,128]{3,2,1,0:T(8,128)S(1)}, u32[]{:S(2)}, u32[]{:S(2)}) %collective-permute-start.2) | collective-permute-done | bytes 65568 | tf_op jit(solution)/shard_map/ppermute | solution.py:660
  26.1 1.9 %collective-permute-start.6 = (bf16[128,2048]{1,0:T(8,128)(2,1)S(1)}, bf16[128,2048]{1,0:T(8,128)(2,1)S(1)}, u32[]{:S(2)}, u32[]{:S(2)}) collective-permute-start(bf16[128,2048]{1,0:T(8,128)(2,1)S(1)} %get-tuple-element.37), channel_id=1, source_target_pairs={{4,0},{0,4},{12,8},{5,1},{1,5},{13,9},{6,2},{2,6},{14,10},{7,3},{3... | collective-permute-start | bytes 1572872 | tf_op jit(solution)/shard_map/ppermute | solution.py:230
  28.7 3.3 %collective-permute-start.3 = (f32[2,1,64,128]{3,2,1,0:T(8,128)S(1)}, f32[2,1,64,128]{3,2,1,0:T(8,128)S(1)}, u32[]{:S(2)}, u32[]{:S(2)}) collective-permute-start(f32[2,1,64,128]{3,2,1,0:T(8,128)S(1)} %add.19.sum_ref.refs_0_), channel_id=1, source_target_pairs={{0,4},{4,0},{8,12},{12,8},{1,5},{5,1},{9,13},{13,9},{2,6},{6,2},{1... | collective-permute-start | bytes 196616 | tf_op jit(solution)/shard_map/ppermute | solution.py:660
  32.0 9.9 %collective-permute-done.3.refs_0_ = f32[2,1,64,128]{3,2,1,0:T(8,128)S(1)} collective-permute-done((f32[2,1,64,128]{3,2,1,0:T(8,128)S(1)}, f32[2,1,64,128]{3,2,1,0:T(8,128)S(1)}, u32[]{:S(2)}, u32[]{:S(2)}) %collective-permute-start.3) | collective-permute-done | bytes 65568 | tf_op jit(solution)/shard_map/ppermute | solution.py:660
  42.6 2.3 %collective-permute-start.8 = (bf16[64,2048]{1,0:T(8,128)(2,1)S(1)}, bf16[64,2048]{1,0:T(8,128)(2,1)S(1)}, u32[]{:S(2)}, u32[]{:S(2)}) collective-permute-start(bf16[64,2048]{1,0:T(8,128)(2,1)S(1)} %get-tuple-element.39.home_ref), channel_id=1, source_target_pairs={{0,4},{4,0},{8,12},{12,8},{1,5},{5,1},{9,13},{13,9},{2,6},{6,2},{1... | collective-permute-start | bytes 786440 | tf_op jit(solution)/shard_map/ppermute | solution.py:240
  52.8 2.6 %collective-permute-done.13.refs_0_.outer_ref = bf16[64,2048]{1,0:T(8,128)(2,1)S(1)} collective-permute-done((bf16[64,2048]{1,0:T(8,128)(2,1)S(1)}, bf16[64,2048]{1,0:T(8,128)(2,1)S(1)}, u32[]{:S(2)}, u32[]{:S(2)}) %collective-permute-start.13) | collective-permute-done | bytes 262176 | tf_op jit(solution)/shard_map/ppermute | solution.py:240
  58.8 6.3 %collective-permute-done.11.refs_2_ = bf16[64,2048]{1,0:T(8,128)(2,1)S(1)} collective-permute-done((bf16[64,2048]{1,0:T(8,128)(2,1)S(1)}, bf16[64,2048]{1,0:T(8,128)(2,1)S(1)}, u32[]{:S(2)}, u32[]{:S(2)}) %collective-permute-start.11) | collective-permute-done | bytes 262176 | tf_op jit(solution)/shard_map/ppermute | solution.py:242
  66.4 5.9 %load_weight.1.refs_6_.w_ref = bf16[2048,4096]{1,0:T(8,128)(2,1)S(1)} custom-call(bf16[2048,4096]{1,0:T(8,128)(2,1)} %w_ref.1, bf16[64,2048]{1,0:T(8,128)(2,1)S(1)} %collective-permute-done.13.refs_0_.outer_ref, bf16[64,2048]{1,0:T(8,128)(2,1)S(1)} %collective-permute-done.15.refs_1_.refs_0_), custom_call_target="tpu_custom_call" | custom-call | flops 1 | bytes 1 | tf_op jit(solution)/shard_map/load_weight/pallas_call | solution.py:284
  72.3 3.4 %collective-permute-done.12.refs_3_ = bf16[64,2048]{1,0:T(8,128)(2,1)S(1)} collective-permute-done((bf16[64,2048]{1,0:T(8,128)(2,1)S(1)}, bf16[64,2048]{1,0:T(8,128)(2,1)S(1)}, u32[]{:S(2)}, u32[]{:S(2)}) %collective-permute-start.12) | collective-permute-done | bytes 262176 | tf_op jit(solution)/shard_map/ppermute | solution.py:244
  76.4 2.3 %split_product.6 = (bf16[64,2048]{1,0:T(8,128)(2,1)S(1)}, bf16[64,2048]{1,0:T(8,128)(2,1)S(1)}, f32[64,2048]{1,0:T(8,128)S(1)}, f32[64,2048]{1,0:T(8,128)S(1)}) custom-call(bf16[256,2048]{1,0:T(8,128)(2,1)S(1)} %collect.2.rows_ref, bf16[2048,4096]{1,0:T(8,128)(2,1)S(1)} %load_weight.1.refs_6_.w_ref, ...), custom_call_target="tpu_custom_call" | custom-call | flops 1 | bytes 1 | tf_op jit(solution)/shard_map/split_product/pallas_call | solution.py:317
  80.5 2.3 %split_product.4 = (bf16[64,2048]{1,0:T(8,128)(2,1)S(1)}, bf16[64,2048]{1,0:T(8,128)(2,1)S(1)}, f32[64,2048]{1,0:T(8,128)S(1)}, f32[64,2048]{1,0:T(8,128)S(1)}) custom-call(bf16[256,2048]{1,0:T(8,128)(2,1)S(1)} %collect.2.rows_ref, bf16[2048,4096]{1,0:T(8,128)(2,1)S(1)} %load_weight.1.refs_6_.w_ref, bf16[256,2048]{1,0:T(8,128)(2,1)S(1)} %collect.3.refs_0_.rows_ref), custom_call_target="tpu_custom_call" | custom-call | flops 1 | bytes 1 | tf_op jit(solution)/shard_map/split_product/pallas_call | solution.py:317
  83.5 3.2 %collective-permute-done.22.refs_0_.refs_1_ = bf16[1,64,128]{2,1,0:T(8,128)(2,1)S(1)} collective-permute-done((bf16[1,64,128]{2,1,0:T(8,128)(2,1)S(1)}, bf16[1,64,128]{2,1,0:T(8,128)(2,1)S(1)}, u32[]{:S(2)}, u32[]{:S(2)}) %collective-permute-start.22) | collective-permute-done | bytes 16416 | tf_op jit(solution)/shard_map/ppermute | solution.py:657
  87.2 2.3 %split_product.7 = (bf16[64,2048]{1,0:T(8,128)(2,1)S(1)}, bf16[64,2048]{1,0:T(8,128)(2,1)S(1)}, f32[64,2048]{1,0:T(8,128)S(1)}, f32[64,2048]{1,0:T(8,128)S(1)}) custom-call(bf16[256,2048]{1,0:T(8,128)(2,1)S(1)} %collect.3.refs_0_.rows_ref, bf16[2048,4096]{1,0:T(8,128)(2,1)S(1)} %load_weight.1.refs_6_.w_ref, ...), custom_call_target="tpu_custom_call" | custom-call | flops 1 | bytes 1 | tf_op jit(solution)/shard_map/split_product/pallas_call | solution.py:317
  90.3 2.3 %split_product.5 = (bf16[64,2048]{1,0:T(8,128)(2,1)S(1)}, bf16[64,2048]{1,0:T(8,128)(2,1)S(1)}, f32[64,2048]{1,0:T(8,128)S(1)}, f32[64,2048]{1,0:T(8,128)S(1)}) custom-call(bf16[256,2048]{1,0:T(8,128)(2,1)S(1)} %collect.3.refs_0_.rows_ref, bf16[2048,4096]{1,0:T(8,128)(2,1)S(1)} %load_weight.1.refs_6_.w_ref, ...), custom_call_target="tpu_custom_call" | custom-call | flops 1 | bytes 1 | tf_op jit(solution)/shard_map/split_product/pallas_call | solution.py:317
  95.0 3.9 %collective-permute-done.32.refs_0_.refs_5_ = bf16[64,2048]{1,0:T(8,128)(2,1)S(1)} collective-permute-done((bf16[64,2048]{1,0:T(8,128)(2,1)S(1)}, bf16[64,2048]{1,0:T(8,128)(2,1)S(1)}, u32[]{:S(2)}, u32[]{:S(2)}) %collective-permute-start.32) | collective-permute-done | bytes 262176 | tf_op jit(solution)/shard_map/ppermute | solution.py:657
  99.6 4.9 %collective-permute-done.20.refs_0_.refs_5_ = bf16[64,2048]{1,0:T(8,128)(2,1)S(1)} collective-permute-done((bf16[64,2048]{1,0:T(8,128)(2,1)S(1)}, bf16[64,2048]{1,0:T(8,128)(2,1)S(1)}, u32[]{:S(2)}, u32[]{:S(2)}) %collective-permute-start.20) | collective-permute-done | bytes 262176 | tf_op jit(solution)/shard_map/ppermute | solution.py:657
  106.6 3.9 %up_gradient.1.refs_9_ = f32[4,64,4096]{2,1,0:T(8,128)} custom-call(s32[14]{0:T(128)S(1)} %concatenate.3.index_ref.refs_0_, bf16[1,64,4096]{2,1,0:T(8,128)(2,1)S(1)} %get-tuple-element.46.refs_0_, bf16[1,64,4096]{2,1,0:T(8,128)(2,1)S(1)} %collective-permute-done.25.refs_0_.refs_1_, bf16[1,64,4096]{2,1,0:T(8,128)(2,1)S(1)} %collective-permute-done.24.refs_2_, ...), custom_call_target="tpu_custom_call" | custom-call | flops 1 | bytes 1 | tf_op jit(solution)/shard_map/up_gradient/pallas_call | solution.py:545
  110.5 2.1 %finish.2.refs_9_ = bf16[128,4096]{1,0:T(8,128)(2,1)} custom-call(s32[14]{0:T(128)S(1)} %concatenate.3.index_ref.refs_0_, bf16[1,64,128]{2,1,0:T(8,128)(2,1)S(1)} %get-tuple-element.35.refs_1_, bf16[4,64,4096]{2,1,0:T(8,128)(2,1)S(1)} %copy-done.1, f32[64,2048]{1,0:T(8,128)S(1)} %get-tuple-element.51.refs_3_, ...), custom_call_target="tpu_custom_call" | custom-call | flops 1 | bytes 1 | tf_op jit(solution)/shard_map/finish/pallas_call | solution.py:615
  112.6 2.6 %collective-permute-done.29.refs_8_ = bf16[64,2048]{1,0:T(8,128)(2,1)S(1)} collective-permute-done((bf16[64,2048]{1,0:T(8,128)(2,1)S(1)}, bf16[64,2048]{1,0:T(8,128)(2,1)S(1)}, u32[]{:S(2)}, u32[]{:S(2)}) %collective-permute-start.29) | collective-permute-done | bytes 262176 | tf_op jit(solution)/shard_map/ppermute | solution.py:657
  115.3 2.1 %finish.3 = bf16[128,4096]{1,0:T(8,128)(2,1)} custom-call(s32[14]{0:T(128)S(1)} %concatenate.3.index_ref.refs_0_, bf16[1,64,128]{2,1,0:T(8,128)(2,1)S(1)} %get-tuple-element.35.refs_1_, bf16[4,64,4096]{2,1,0:T(8,128)(2,1)S(1)} %copy-done.1, f32[64,2048]{1,0:T(8,128)S(1)} %get-tuple-element.41.refs_3_, ...), custom_call_target="tpu_custom_call", output_to_operand_aliasing={{}: (9, {})} | custom-call | flops 1 | bytes 1 | tf_op jit(solution)/shard_map/finish/pallas_call | solution.py:615
  (78 shorter events, 30.1 us)
Async XLA Ops:
  3.3 22.1 %collective-permute-start.4 = (bf16[128,2048]{1,0:T(8,128)(2,1)S(1)}, bf16[128,2048]{1,0:T(8,128)(2,1)S(1)}, u32[]{:S(2)}, u32[]{:S(2)}) collective-permute-start(bf16[128,2048]{1,0:T(8,128)(2,1)S(1)} %get-tuple-element.31.refs_0_), channel_id=1, source_target_pairs={{12,8},{0,4},{13,9},{1,5},{14,10},{2,6},{15,11},{3,7},{28,24},{16,... | collective-permute-start | bytes 1572872 | tf_op jit(solution)/shard_map/ppermute | solution.py:220
  8.3 17.2 %collective-permute-start.5 = (bf16[128,2048]{1,0:T(8,128)(2,1)S(1)}, bf16[128,2048]{1,0:T(8,128)(2,1)S(1)}, u32[]{:S(2)}, u32[]{:S(2)}) collective-permute-start(bf16[128,2048]{1,0:T(8,128)(2,1)S(1)} %get-tuple-element.36), channel_id=1, source_target_pairs={{8,4},{9,5},{10,6},{11,7},{24,20},{25,21},{26,22},{27,23}} | collective-permute-start | bytes 1572872 | tf_op jit(solution)/shard_map/ppermute | solution.py:221
  26.1 15.8 %collective-permute-start.6 = (bf16[128,2048]{1,0:T(8,128)(2,1)S(1)}, bf16[128,2048]{1,0:T(8,128)(2,1)S(1)}, u32[]{:S(2)}, u32[]{:S(2)}) collective-permute-start(bf16[128,2048]{1,0:T(8,128)(2,1)S(1)} %get-tuple-element.37), channel_id=1, source_target_pairs={{4,0},{0,4},{12,8},{5,1},{1,5},{13,9},{6,2},{2,6},{14,10},{7,3},{3... | collective-permute-start | bytes 1572872 | tf_op jit(solution)/shard_map/ppermute | solution.py:230
  28.0 13.9 %collective-permute-start.7 = (bf16[128,2048]{1,0:T(8,128)(2,1)S(1)}, bf16[128,2048]{1,0:T(8,128)(2,1)S(1)}, u32[]{:S(2)}, u32[]{:S(2)}) collective-permute-start(bf16[128,2048]{1,0:T(8,128)(2,1)S(1)} %get-tuple-element.38), channel_id=1, source_target_pairs={{8,4},{4,8},{9,5},{5,9},{10,6},{6,10},{11,7},{7,11},{24,20},{20,24... | collective-permute-start | bytes 1572872 | tf_op jit(solution)/shard_map/ppermute | solution.py:231
  28.7 13.2 %collective-permute-start.3 = (f32[2,1,64,128]{3,2,1,0:T(8,128)S(1)}, f32[2,1,64,128]{3,2,1,0:T(8,128)S(1)}, u32[]{:S(2)}, u32[]{:S(2)}) collective-permute-start(f32[2,1,64,128]{3,2,1,0:T(8,128)S(1)} %add.19.sum_ref.refs_0_), channel_id=1, source_target_pairs={{0,4},{4,0},{8,12},{12,8},{1,5},{5,1},{9,13},{13,9},{2,6},{6,2},{1... | collective-permute-start | bytes 196616 | tf_op jit(solution)/shard_map/ppermute | solution.py:660
  42.6 8.3 %collective-permute-start.8 = (bf16[64,2048]{1,0:T(8,128)(2,1)S(1)}, bf16[64,2048]{1,0:T(8,128)(2,1)S(1)}, u32[]{:S(2)}, u32[]{:S(2)}) collective-permute-start(bf16[64,2048]{1,0:T(8,128)(2,1)S(1)} %get-tuple-element.39.home_ref), channel_id=1, source_target_pairs={{0,4},{4,0},{8,12},{12,8},{1,5},{5,1},{9,13},{13,9},{2,6},{6,2},{1... | collective-permute-start | bytes 786440 | tf_op jit(solution)/shard_map/ppermute | solution.py:240
  45.7 13.0 %collective-permute-start.25 = (bf16[1,64,4096]{2,1,0:T(8,128)(2,1)S(1)}, bf16[1,64,4096]{2,1,0:T(8,128)(2,1)S(1)}, u32[]{:S(2)}, u32[]{:S(2)}) collective-permute-start(bf16[1,64,4096]{2,1,0:T(8,128)(2,1)S(1)} %get-tuple-element.46.refs_0_), channel_id=1, source_target_pairs={{0,2},{1,3},{2,0},{3,1},{4,6},{5,7},{6,4},{7,5},{8,10},{9,11},{10,... | collective-permute-start | bytes 1572872 | tf_op jit(solution)/shard_map/ppermute | solution.py:657
  51.5 13.6 %collective-permute-start.11 = (bf16[64,2048]{1,0:T(8,128)(2,1)S(1)}, bf16[64,2048]{1,0:T(8,128)(2,1)S(1)}, u32[]{:S(2)}, u32[]{:S(2)}) collective-permute-start(bf16[64,2048]{1,0:T(8,128)(2,1)S(1)} %collective-permute-done.9.refs_0_), channel_id=1, source_target_pairs={{4,0},{8,12},{5,1},{9,13},{6,2},{10,14},{7,3},{11,15},{20,16},{24,... | collective-permute-start | bytes 786440 | tf_op jit(solution)/shard_map/ppermute | solution.py:242
  55.4 9.7 %collective-permute-start.14 = (bf16[64,2048]{1,0:T(8,128)(2,1)S(1)}, bf16[64,2048]{1,0:T(8,128)(2,1)S(1)}, u32[]{:S(2)}, u32[]{:S(2)}) collective-permute-start(bf16[64,2048]{1,0:T(8,128)(2,1)S(1)} %collective-permute-done.13.refs_0_.outer_ref), channel_id=1, source_target_pairs={{4,8},{8,4},{5,9},{9,5},{6,10},{10,6},{7,11},{11,7},{20,24},{24,20... | collective-permute-start | bytes 786440 | tf_op jit(solution)/shard_map/ppermute | solution.py:243
  56.1 16.2 %collective-permute-start.16 = (bf16[64,2048]{1,0:T(8,128)(2,1)S(1)}, bf16[64,2048]{1,0:T(8,128)(2,1)S(1)}, u32[]{:S(2)}, u32[]{:S(2)}) collective-permute-start(bf16[64,2048]{1,0:T(8,128)(2,1)S(1)} %collective-permute-done.15.refs_1_.refs_0_), channel_id=1, source_target_pairs={{4,0},{8,12},{5,1},{9,13},{6,2},{10,14},{7,3},{11,15},{20,16},{24,... | collective-permute-start | bytes 786440 | tf_op jit(solution)/shard_map/ppermute | solution.py:242
  57.4 18.3 %collective-permute-start.12 = (bf16[64,2048]{1,0:T(8,128)(2,1)S(1)}, bf16[64,2048]{1,0:T(8,128)(2,1)S(1)}, u32[]{:S(2)}, u32[]{:S(2)}) collective-permute-start(bf16[64,2048]{1,0:T(8,128)(2,1)S(1)} %collective-permute-done.10.refs_1_), channel_id=1, source_target_pairs={{4,0},{8,12},{5,1},{9,13},{6,2},{10,14},{7,3},{11,15},{20,16},{24,... | collective-permute-start | bytes 786440 | tf_op jit(solution)/shard_map/ppermute | solution.py:244
  58.7 31.6 %collective-permute-start.24 = (bf16[1,64,4096]{2,1,0:T(8,128)(2,1)S(1)}, bf16[1,64,4096]{2,1,0:T(8,128)(2,1)S(1)}, u32[]{:S(2)}, u32[]{:S(2)}) collective-permute-start(bf16[1,64,4096]{2,1,0:T(8,128)(2,1)S(1)} %get-tuple-element.46.refs_0_), channel_id=1, source_target_pairs={{0,1},{1,0},{2,3},{3,2},{4,5},{5,4},{6,7},{7,6},{8,9},{9,8},{10,11... | collective-permute-start | bytes 1572872 | tf_op jit(solution)/shard_map/ppermute | solution.py:654
  65.1 25.2 %collective-permute-start.26 = (bf16[1,64,4096]{2,1,0:T(8,128)(2,1)S(1)}, bf16[1,64,4096]{2,1,0:T(8,128)(2,1)S(1)}, u32[]{:S(2)}, u32[]{:S(2)}) collective-permute-start(bf16[1,64,4096]{2,1,0:T(8,128)(2,1)S(1)} %collective-permute-done.25.refs_0_.refs_1_), channel_id=1, source_target_pairs={{0,1},{1,0},{2,3},{3,2},{4,5},{5,4},{6,7},{7,6},{8,9},{9,8},{10,11... | collective-permute-start | bytes 1572872 | tf_op jit(solution)/shard_map/ppermute | solution.py:654
  65.1 14.7 %collective-permute-start.17 = (bf16[64,2048]{1,0:T(8,128)(2,1)S(1)}, bf16[64,2048]{1,0:T(8,128)(2,1)S(1)}, u32[]{:S(2)}, u32[]{:S(2)}) collective-permute-start(bf16[64,2048]{1,0:T(8,128)(2,1)S(1)} %collective-permute-done.14.refs_4_.refs_1_), channel_id=1, source_target_pairs={{4,0},{8,12},{5,1},{9,13},{6,2},{10,14},{7,3},{11,15},{20,16},{24,... | collective-permute-start | bytes 786440 | tf_op jit(solution)/shard_map/ppermute | solution.py:244
  78.7 8.0 %collective-permute-start.31 = (bf16[64,2048]{1,0:T(8,128)(2,1)S(1)}, bf16[64,2048]{1,0:T(8,128)(2,1)S(1)}, u32[]{:S(2)}, u32[]{:S(2)}) collective-permute-start(bf16[64,2048]{1,0:T(8,128)(2,1)S(1)} %get-tuple-element.54), channel_id=1, source_target_pairs={{0,1},{1,0},{2,3},{3,2},{4,5},{5,4},{6,7},{7,6},{8,9},{9,8},{10,11... | collective-permute-start | bytes 786440 | tf_op jit(solution)/shard_map/ppermute | solution.py:654
  82.8 10.0 %collective-permute-start.19 = (bf16[64,2048]{1,0:T(8,128)(2,1)S(1)}, bf16[64,2048]{1,0:T(8,128)(2,1)S(1)}, u32[]{:S(2)}, u32[]{:S(2)}) collective-permute-start(bf16[64,2048]{1,0:T(8,128)(2,1)S(1)} %get-tuple-element.44), channel_id=1, source_target_pairs={{0,1},{1,0},{2,3},{3,2},{4,5},{5,4},{6,7},{7,6},{8,9},{9,8},{10,11... | collective-permute-start | bytes 786440 | tf_op jit(solution)/shard_map/ppermute | solution.py:654
  89.7 9.2 %collective-permute-start.32 = (bf16[64,2048]{1,0:T(8,128)(2,1)S(1)}, bf16[64,2048]{1,0:T(8,128)(2,1)S(1)}, u32[]{:S(2)}, u32[]{:S(2)}) collective-permute-start(bf16[64,2048]{1,0:T(8,128)(2,1)S(1)} %leaving.6), channel_id=1, source_target_pairs={{0,2},{1,3},{2,0},{3,1},{4,6},{5,7},{6,4},{7,5},{8,10},{9,11},{10,... | collective-permute-start | bytes 786440 | tf_op jit(solution)/shard_map/ppermute | solution.py:657
  92.9 11.6 %collective-permute-start.20 = (bf16[64,2048]{1,0:T(8,128)(2,1)S(1)}, bf16[64,2048]{1,0:T(8,128)(2,1)S(1)}, u32[]{:S(2)}, u32[]{:S(2)}) collective-permute-start(bf16[64,2048]{1,0:T(8,128)(2,1)S(1)} %leaving.4), channel_id=1, source_target_pairs={{0,2},{1,3},{2,0},{3,1},{4,6},{5,7},{6,4},{7,5},{8,10},{9,11},{10,... | collective-permute-start | bytes 786440 | tf_op jit(solution)/shard_map/ppermute | solution.py:657
  94.5 10.1 %collective-permute-start.30 = (bf16[64,2048]{1,0:T(8,128)(2,1)S(1)}, bf16[64,2048]{1,0:T(8,128)(2,1)S(1)}, u32[]{:S(2)}, u32[]{:S(2)}) collective-permute-start(bf16[64,2048]{1,0:T(8,128)(2,1)S(1)} %get-tuple-element.52), channel_id=1, source_target_pairs={{0,1},{1,0},{2,3},{3,2},{4,5},{5,4},{6,7},{7,6},{8,9},{9,8},{10,11... | collective-permute-start | bytes 786440 | tf_op jit(solution)/shard_map/ppermute | solution.py:654
  94.5 18.1 %collective-permute-start.18 = (bf16[64,2048]{1,0:T(8,128)(2,1)S(1)}, bf16[64,2048]{1,0:T(8,128)(2,1)S(1)}, u32[]{:S(2)}, u32[]{:S(2)}) collective-permute-start(bf16[64,2048]{1,0:T(8,128)(2,1)S(1)} %get-tuple-element.42), channel_id=1, source_target_pairs={{0,1},{1,0},{2,3},{3,2},{4,5},{5,4},{6,7},{7,6},{8,9},{9,8},{10,11... | collective-permute-start | bytes 786440 | tf_op jit(solution)/shard_map/ppermute | solution.py:654
  98.9 11.6 %collective-permute-start.33 = (bf16[64,2048]{1,0:T(8,128)(2,1)S(1)}, bf16[64,2048]{1,0:T(8,128)(2,1)S(1)}, u32[]{:S(2)}, u32[]{:S(2)}) collective-permute-start(bf16[64,2048]{1,0:T(8,128)(2,1)S(1)} %get-tuple-element.56), channel_id=1, source_target_pairs={{0,1},{1,0},{2,3},{3,2},{4,5},{5,4},{6,7},{7,6},{8,9},{9,8},{10,11... | collective-permute-start | bytes 786440 | tf_op jit(solution)/shard_map/ppermute | solution.py:654
  99.0 11.5 %collective-permute-start.35 = (bf16[64,2048]{1,0:T(8,128)(2,1)S(1)}, bf16[64,2048]{1,0:T(8,128)(2,1)S(1)}, u32[]{:S(2)}, u32[]{:S(2)}) collective-permute-start(bf16[64,2048]{1,0:T(8,128)(2,1)S(1)} %leaving.7), channel_id=1, source_target_pairs={{0,2},{1,3},{2,0},{3,1},{4,6},{5,7},{6,4},{7,5},{8,10},{9,11},{10,... | collective-permute-start | bytes 786440 | tf_op jit(solution)/shard_map/ppermute | solution.py:657
  104.5 8.1 %collective-permute-start.27 = (bf16[64,2048]{1,0:T(8,128)(2,1)S(1)}, bf16[64,2048]{1,0:T(8,128)(2,1)S(1)}, u32[]{:S(2)}, u32[]{:S(2)}) collective-permute-start(bf16[64,2048]{1,0:T(8,128)(2,1)S(1)} %get-tuple-element.48), channel_id=1, source_target_pairs={{0,1},{1,0},{2,3},{3,2},{4,5},{5,4},{6,7},{7,6},{8,9},{9,8},{10,11... | collective-permute-start | bytes 786440 | tf_op jit(solution)/shard_map/ppermute | solution.py:654
  104.6 10.7 %collective-permute-start.29 = (bf16[64,2048]{1,0:T(8,128)(2,1)S(1)}, bf16[64,2048]{1,0:T(8,128)(2,1)S(1)}, u32[]{:S(2)}, u32[]{:S(2)}) collective-permute-start(bf16[64,2048]{1,0:T(8,128)(2,1)S(1)} %leaving.5), channel_id=1, source_target_pairs={{0,2},{1,3},{2,0},{3,1},{4,6},{5,7},{6,4},{7,5},{8,10},{9,11},{10,... | collective-permute-start | bytes 786440 | tf_op jit(solution)/shard_map/ppermute | solution.py:657
  (15 other events, 121.8 us)

commit v20 on v17

--- a/solution.py
+++ b/solution.py
@@ -331,21 +331,21 @@
     )(in_vmem(rows), in_vmem(weight), *extra)
 
 
-def narrow_kernel(index_of, index_ref, tokens_ref, down_ref, cot_ref, up_ref, *refs):
-    send_ref, keep_ref, back_ref, low, tokens, down, cot, up, sems = refs[-9:]
-    index = index_of(index_ref)
-    pairs = [(tokens_ref, tokens), (down_ref, down), (cot_ref, cot)]
-    for i in range(index.per_part):
-        adapter = index.owner(index.block(0, 0, i))
-        pairs.append((up_ref.at[adapter], up.at[i]))
+def run_copies(pairs, sems):
     copies = [
         pltpu.make_async_copy(source, target, sems.at[j])
         for j, (source, target) in enumerate(pairs)
     ]
     for copy in copies:
         copy.start()
-    for copy in copies[:2]:
+    for copy in copies:
         copy.wait()
+
+
+def narrow_kernel(index_of, index_ref, tokens_ref, down_ref, *refs):
+    send_ref, keep_ref, low, tokens, down, sems = refs[-6:]
+    index = index_of(index_ref)
+    run_copies([(tokens_ref, tokens), (down_ref, down)], sems)
     for m in range(CAP):
         low[m] = lax.dot_general(
             down[0],
@@ -359,41 +359,65 @@
                 block = index.block(core_bit, chip_bits, i)
                 mine = index.owner(block) == index.place
                 out_ref[chip_bits, i] = jnp.where(mine, low[index.slot(block)], 0.0)
-    for copy in copies[2:]:
-        copy.wait()
-    for i in range(index.per_part):
-        back_ref[i] = lax.dot_general(
-            up[i], cot[i * BLK : (i + 1) * BLK], LAST, preferred_element_type=jnp.float32
-        )
-
-
-def narrow(index_of, index, shape, tokens, down, cotangent, up, waits):
-    rank = up.shape[1]
-    one = (shape.per_part, rank, BLK)
-    outs = [(shape.chips,) + one, (shape.chips,) + one, one]
-    operands = (tokens, down, cotangent, up)
+
+
+def narrow(index_of, index, shape, tokens, down, rank, waits):
+    out = (shape.chips, shape.per_part, rank, BLK)
     specs, extra = after(waits)
     return pl.pallas_call(
         functools.partial(narrow_kernel, index_of),
         grid_spec=pltpu.PrefetchScalarGridSpec(
             num_scalar_prefetch=1,
             grid=(1,),
-            in_specs=[pl.BlockSpec(memory_space=pl.ANY)] * len(operands) + specs,
-            out_specs=[held()] * len(outs),
+            in_specs=[pl.BlockSpec(memory_space=pl.ANY)] * 2 + specs,
+            out_specs=[held()] * 2,
             scratch_shapes=[
                 pltpu.VMEM((CAP, rank, BLK), jnp.float32),
                 pltpu.VMEM(tokens.shape, tokens.dtype),
                 pltpu.VMEM(down.shape, down.dtype),
+                pltpu.SemaphoreType.DMA((2,)),
+            ],
+        ),
+        out_shape=[pltpu.VMEM(out, jnp.float32)] * 2,
+        compiler_params=SMALL,
+        cost_estimate=BRIEF,
+        name="narrow",
+    )(index, in_hbm(tokens), in_hbm(down), *extra)
+
+
+def backward_kernel(index_of, index_ref, cot_ref, up_ref, *refs):
+    back_ref, cot, up, sems = refs[-4:]
+    index = index_of(index_ref)
+    pairs = [(cot_ref, cot)]
+    for i in range(index.per_part):
+        pairs.append((up_ref.at[index.owner(index.block(0, 0, i))], up.at[i]))
+    run_copies(pairs, sems)
+    for i in range(index.per_part):
+        back_ref[i] = lax.dot_general(
+            up[i], cot[i * BLK : (i + 1) * BLK], LAST, preferred_element_type=jnp.float32
+        )
+
+
+def backward(index_of, index, shape, cotangent, up, waits):
+    specs, extra = after(waits)
+    return pl.pallas_call(
+        functools.partial(backward_kernel, index_of),
+        grid_spec=pltpu.PrefetchScalarGridSpec(
+            num_scalar_prefetch=1,
+            grid=(1,),
+            in_specs=[pl.BlockSpec(memory_space=pl.ANY)] * 2 + specs,
+            out_specs=held(),
+            scratch_shapes=[
                 pltpu.VMEM(cotangent.shape, cotangent.dtype),
                 pltpu.VMEM((shape.per_part,) + up.shape[1:], up.dtype),
-                pltpu.SemaphoreType.DMA((3 + shape.per_part,)),
+                pltpu.SemaphoreType.DMA((1 + shape.per_part,)),
             ],
         ),
-        out_shape=[pltpu.VMEM(o, jnp.float32) for o in outs],
-        compiler_params=SMALL,
-        cost_estimate=BRIEF,
-        name="narrow",
-    )(index, *[in_hbm(o) for o in operands], *extra)
+        out_shape=pltpu.VMEM((shape.per_part, up.shape[1], BLK), jnp.float32),
+        compiler_params=SMALL,
+        cost_estimate=BRIEF,
+        name="backward",
+    )(index, in_hbm(cotangent), in_hbm(up), *extra)
 
 
 def merge_kernel(keep_ref, arrived_ref, back_ref, *refs):
@@ -647,16 +671,11 @@
         return values + [to_other_core(v) for v in values]
 
     def small_products(waits):
-        return narrow(
-            index_of,
-            index,
-            shape,
-            tokens,
-            jnp.swapaxes(adapter_down_factor, 1, 2),
-            cotangent,
-            adapter_up_factor,
-            waits,
-        )
+        down = jnp.swapaxes(adapter_down_factor, 1, 2)
+        rank = adapter_up_factor.shape[1]
+        send, keep = narrow(index_of, index, shape, tokens, down, rank, waits)
+        back = backward(index_of, index, shape, cotangent, adapter_up_factor, [send])
+        return send, keep, back
 
     def over_parts(send, keep):
         arrived = to_other_core(send)

time: 116 us -> 116 us (level)
    pallas_call x0 -> x1, Pallas kernels: none -> 2.39 us  [backward(): pl.pallas_call(functools.partial(backward_kernel, index_of), grid_spec=pl...]
    ppermute x7, waiting for transfers between devices: 9.2 us -> 7.5 us  [to_chip(): lax.ppermute(value, 'tensor', [(i, i ^ k * CORES) for i in range(parts)])]
  transfers between devices with their start and end apart: 36 -> 36, of which waited for: 14 -> 13; matrix products, arithmetic and copies ran while one was open for 0% -> 0% of each run, Pallas kernels for 23% -> 24%
where the time goes in v20:
time: 116 us
  waiting for transfers between devices  42.4 us (37%)
  starting transfers between devices  36.2 us (31%)
  Pallas kernels  34.9 us (30%)
    ppermute x2, waiting for transfers between devices, across_dp(): return lax.ppermute(value, 'dp', [(i, i ^ k) for i in range(owners)])  16.2 us
    pallas_call x4, Pallas kernels, split_product(): pl.pallas_call(functools.partial(split_product_kernel, each, half, part *...  9.29 us
    ppermute x7, starting transfers between devices, to_chip(): lax.ppermute(value, 'tensor', [(i, i ^ k * CORES) for i in range(parts)])  8.08 us
    ppermute x2, waiting for transfers between devices, spread(): outer_3 = lax.ppermute(inner_2, 'dp', [(1, 0), (2, 3)])  7.83 us
    ppermute x7, waiting for transfers between devices, to_chip(): lax.ppermute(value, 'tensor', [(i, i ^ k * CORES) for i in range(parts)])  7.5 us
    pallas_call x1, Pallas kernels, load_weight(): pl.pallas_call(load_weight_kernel, grid=(1,), in_specs=[pl.BlockSpec(memo...  5.89 us
    ppermute x2, starting transfers between devices, across_dp(): return lax.ppermute(value, 'dp', [(i, i ^ k) for i in range(owners)])  5.43 us
    ppermute x1, starting transfers between devices, first(): lax.ppermute(inward, 'dp', [(3, 2), (0, 1)])  4.96 us
  transfers between devices with their start and end apart: 36, of which 13 were waited for; matrix products, arithmetic and copies ran while one was open for 0% of the time, Pallas kernels for 24%

profile of v20, /device:TPU:0, one launch (start us, length us, event | category | flops | bytes accessed | tf_op | source)
XLA Modules:
  0.0 115.7 jit_solution(7147952976681561527)
XLA Ops:
  3.3 5.0 %collective-permute-start.4 = (bf16[128,2048]{1,0:T(8,128)(2,1)S(1)}, bf16[128,2048]{1,0:T(8,128)(2,1)S(1)}, u32[]{:S(2)}, u32[]{:S(2)}) collective-permute-start(bf16[128,2048]{1,0:T(8,128)(2,1)S(1)} %get-tuple-element.30.refs_0_), channel_id=1, source_target_pairs={{12,8},{0,4},{13,9},{1,5},{14,10},{2,6},{15,11},{3,7},{28,24},{16,... | collective-permute-start | bytes 1572872 | tf_op jit(solution)/shard_map/ppermute | solution.py:220
  9.0 2.7 %narrow.1 = (f32[2,1,64,128]{3,2,1,0:T(8,128)S(1)}, f32[2,1,64,128]{3,2,1,0:T(8,128)S(1)}) custom-call(s32[14]{0:T(128)S(1)} %concatenate.3.index_ref.refs_0_, bf16[384,2048]{1,0:T(8,128)(2,1)} %tokens_ref.9, bf16[1,64,2048]{2,1,0:T(8,128)(2,1)} %bitcast.7, bf16[128,2048]{1,0:T(8,128)(2,1)S(1)} %get-tuple-element.30.refs_0_), custom_call_target="tpu_custom_call" | custom-call | flops 1 | bytes 1 | tf_op jit(solution)/shard_map/narrow/pallas_call | solution.py:367
  14.5 2.4 %backward.1.back_ref = f32[1,64,128]{2,1,0:T(8,128)S(1)} custom-call(s32[14]{0:T(128)S(1)} %concatenate.3.index_ref.refs_0_, bf16[128,4096]{1,0:T(8,128)(2,1)} %cot_ref.3, bf16[4,64,4096]{2,1,0:T(8,128)(2,1)} %refs_2_.3, f32[2,1,64,128]{3,2,1,0:T(8,128)S(1)} %get-tuple-element.32.refs_0_), custom_call_target="tpu_custom_call" | custom-call | flops 1 | bytes 1 | tf_op jit(solution)/shard_map/backward/pallas_call | solution.py:403
  17.0 2.1 %collective-permute-start.2 = (f32[2,1,64,128]{3,2,1,0:T(8,128)S(1)}, f32[2,1,64,128]{3,2,1,0:T(8,128)S(1)}, u32[]{:S(2)}, u32[]{:S(2)}) collective-permute-start(f32[2,1,64,128]{3,2,1,0:T(8,128)S(1)} %merge.1), channel_id=1, source_target_pairs={{0,8},{4,12},{8,0},{12,4},{1,9},{5,13},{9,1},{13,5},{2,10},{6,14},... | collective-permute-start | bytes 196616 | tf_op jit(solution)/shard_map/ppermute | solution.py:665
  19.1 6.3 %collective-permute-done.2 = f32[2,1,64,128]{3,2,1,0:T(8,128)S(1)} collective-permute-done((f32[2,1,64,128]{3,2,1,0:T(8,128)S(1)}, f32[2,1,64,128]{3,2,1,0:T(8,128)S(1)}, u32[]{:S(2)}, u32[]{:S(2)}) %collective-permute-start.2) | collective-permute-done | bytes 65568 | tf_op jit(solution)/shard_map/ppermute | solution.py:665
  26.1 1.9 %collective-permute-start.6 = (bf16[128,2048]{1,0:T(8,128)(2,1)S(1)}, bf16[128,2048]{1,0:T(8,128)(2,1)S(1)}, u32[]{:S(2)}, u32[]{:S(2)}) collective-permute-start(bf16[128,2048]{1,0:T(8,128)(2,1)S(1)} %get-tuple-element.35), channel_id=1, source_target_pairs={{4,0},{0,4},{12,8},{5,1},{1,5},{13,9},{6,2},{2,6},{14,10},{7,3},{3... | collective-permute-start | bytes 1572872 | tf_op jit(solution)/shard_map/ppermute | solution.py:230
  28.7 3.3 %collective-permute-start.3 = (f32[2,1,64,128]{3,2,1,0:T(8,128)S(1)}, f32[2,1,64,128]{3,2,1,0:T(8,128)S(1)}, u32[]{:S(2)}, u32[]{:S(2)}) collective-permute-start(f32[2,1,64,128]{3,2,1,0:T(8,128)S(1)} %add.31.sum_ref.refs_0_), channel_id=1, source_target_pairs={{0,4},{4,0},{8,12},{12,8},{1,5},{5,1},{9,13},{13,9},{2,6},{6,2},{1... | collective-permute-start | bytes 196616 | tf_op jit(solution)/shard_map/ppermute | solution.py:665
  32.0 9.9 %collective-permute-done.3.refs_0_ = f32[2,1,64,128]{3,2,1,0:T(8,128)S(1)} collective-permute-done((f32[2,1,64,128]{3,2,1,0:T(8,128)S(1)}, f32[2,1,64,128]{3,2,1,0:T(8,128)S(1)}, u32[]{:S(2)}, u32[]{:S(2)}) %collective-permute-start.3) | collective-permute-done | bytes 65568 | tf_op jit(solution)/shard_map/ppermute | solution.py:665
  42.6 2.3 %collective-permute-start.8 = (bf16[64,2048]{1,0:T(8,128)(2,1)S(1)}, bf16[64,2048]{1,0:T(8,128)(2,1)S(1)}, u32[]{:S(2)}, u32[]{:S(2)}) collective-permute-start(bf16[64,2048]{1,0:T(8,128)(2,1)S(1)} %get-tuple-element.37.home_ref), channel_id=1, source_target_pairs={{0,4},{4,0},{8,12},{12,8},{1,5},{5,1},{9,13},{13,9},{2,6},{6,2},{1... | collective-permute-start | bytes 786440 | tf_op jit(solution)/shard_map/ppermute | solution.py:240
  47.8 3.8 %collective-permute-done.8.outer_ref = bf16[64,2048]{1,0:T(8,128)(2,1)S(1)} collective-permute-done((bf16[64,2048]{1,0:T(8,128)(2,1)S(1)}, bf16[64,2048]{1,0:T(8,128)(2,1)S(1)}, u32[]{:S(2)}, u32[]{:S(2)}) %collective-permute-start.8) | collective-permute-done | bytes 262176 | tf_op jit(solution)/shard_map/ppermute | solution.py:240
  59.3 5.9 %load_weight.1.refs_6_.w_ref = bf16[2048,4096]{1,0:T(8,128)(2,1)S(1)} custom-call(bf16[2048,4096]{1,0:T(8,128)(2,1)} %w_ref.1, bf16[64,2048]{1,0:T(8,128)(2,1)S(1)} %collective-permute-done.13.refs_0_.outer_ref, bf16[64,2048]{1,0:T(8,128)(2,1)S(1)} %collective-permute-done.15.refs_1_.refs_0_), custom_call_target="tpu_custom_call" | custom-call | flops 1 | bytes 1 | tf_op jit(solution)/shard_map/load_weight/pallas_call | solution.py:284
  66.1 3.7 %collective-permute-done.16.refs_5_.refs_2_ = bf16[64,2048]{1,0:T(8,128)(2,1)S(1)} collective-permute-done((bf16[64,2048]{1,0:T(8,128)(2,1)S(1)}, bf16[64,2048]{1,0:T(8,128)(2,1)S(1)}, u32[]{:S(2)}, u32[]{:S(2)}) %collective-permute-start.16) | collective-permute-done | bytes 262176 | tf_op jit(solution)/shard_map/ppermute | solution.py:242
  69.8 2.8 %collective-permute-done.12.refs_3_ = bf16[64,2048]{1,0:T(8,128)(2,1)S(1)} collective-permute-done((bf16[64,2048]{1,0:T(8,128)(2,1)S(1)}, bf16[64,2048]{1,0:T(8,128)(2,1)S(1)}, u32[]{:S(2)}, u32[]{:S(2)}) %collective-permute-start.12) | collective-permute-done | bytes 262176 | tf_op jit(solution)/shard_map/ppermute | solution.py:244
  73.3 2.3 %split_product.5 = (bf16[64,2048]{1,0:T(8,128)(2,1)S(1)}, bf16[64,2048]{1,0:T(8,128)(2,1)S(1)}, f32[64,2048]{1,0:T(8,128)S(1)}, f32[64,2048]{1,0:T(8,128)S(1)}) custom-call(bf16[256,2048]{1,0:T(8,128)(2,1)S(1)} %collect.2.rows_ref, bf16[2048,4096]{1,0:T(8,128)(2,1)S(1)} %load_weight.1.refs_6_.w_ref, ...), custom_call_target="tpu_custom_call" | custom-call | flops 1 | bytes 1 | tf_op jit(solution)/shard_map/split_product/pallas_call | solution.py:317
  78.3 2.3 %split_product.4 = (bf16[64,2048]{1,0:T(8,128)(2,1)S(1)}, bf16[64,2048]{1,0:T(8,128)(2,1)S(1)}, f32[64,2048]{1,0:T(8,128)S(1)}, f32[64,2048]{1,0:T(8,128)S(1)}) custom-call(bf16[256,2048]{1,0:T(8,128)(2,1)S(1)} %collect.2.rows_ref, bf16[2048,4096]{1,0:T(8,128)(2,1)S(1)} %load_weight.1.refs_6_.w_ref), custom_call_target="tpu_custom_call" | custom-call | flops 1 | bytes 1 | tf_op jit(solution)/shard_map/split_product/pallas_call | solution.py:317
  81.3 5.0 %collective-permute-done.20.refs_3_ = bf16[64,2048]{1,0:T(8,128)(2,1)S(1)} collective-permute-done((bf16[64,2048]{1,0:T(8,128)(2,1)S(1)}, bf16[64,2048]{1,0:T(8,128)(2,1)S(1)}, u32[]{:S(2)}, u32[]{:S(2)}) %collective-permute-start.20) | collective-permute-done | bytes 262176 | tf_op jit(solution)/shard_map/ppermute | solution.py:244
  87.9 2.2 %collective-permute-done.24.refs_1_ = bf16[1,64,128]{2,1,0:T(8,128)(2,1)S(1)} collective-permute-done((bf16[1,64,128]{2,1,0:T(8,128)(2,1)S(1)}, bf16[1,64,128]{2,1,0:T(8,128)(2,1)S(1)}, u32[]{:S(2)}, u32[]{:S(2)}) %collective-permute-start.24) | collective-permute-done | bytes 16416 | tf_op jit(solution)/shard_map/ppermute | solution.py:662
  90.5 2.3 %split_product.7 = (bf16[64,2048]{1,0:T(8,128)(2,1)S(1)}, bf16[64,2048]{1,0:T(8,128)(2,1)S(1)}, f32[64,2048]{1,0:T(8,128)S(1)}, f32[64,2048]{1,0:T(8,128)S(1)}) custom-call(bf16[256,2048]{1,0:T(8,128)(2,1)S(1)} %collect.3.rows_ref, bf16[2048,4096]{1,0:T(8,128)(2,1)S(1)} %load_weight.1.refs_6_.w_ref, ...), custom_call_target="tpu_custom_call" | custom-call | flops 1 | bytes 1 | tf_op jit(solution)/shard_map/split_product/pallas_call | solution.py:317
  94.6 2.3 %split_product.6 = (bf16[64,2048]{1,0:T(8,128)(2,1)S(1)}, bf16[64,2048]{1,0:T(8,128)(2,1)S(1)}, f32[64,2048]{1,0:T(8,128)S(1)}, f32[64,2048]{1,0:T(8,128)S(1)}) custom-call(bf16[256,2048]{1,0:T(8,128)(2,1)S(1)} %collect.3.rows_ref, bf16[2048,4096]{1,0:T(8,128)(2,1)S(1)} %load_weight.1.refs_6_.w_ref, ...), custom_call_target="tpu_custom_call" | custom-call | flops 1 | bytes 1 | tf_op jit(solution)/shard_map/split_product/pallas_call | solution.py:317
  102.2 3.9 %up_gradient.1.refs_9_ = f32[4,64,4096]{2,1,0:T(8,128)} custom-call(s32[14]{0:T(128)S(1)} %concatenate.3.index_ref.refs_0_, bf16[1,64,4096]{2,1,0:T(8,128)(2,1)S(1)} %get-tuple-element.43.refs_0_, bf16[1,64,4096]{2,1,0:T(8,128)(2,1)S(1)} %collective-permute-done.21.refs_0_.refs_1_, bf16[1,64,4096]{2,1,0:T(8,128)(2,1)S(1)} %collective-permute-done.26.refs_2_, ...), custom_call_target="tpu_custom_call" | custom-call | flops 1 | bytes 1 | tf_op jit(solution)/shard_map/up_gradient/pallas_call | solution.py:550
  106.1 2.3 %collective-permute-done.35.refs_8_ = bf16[64,2048]{1,0:T(8,128)(2,1)S(1)} collective-permute-done((bf16[64,2048]{1,0:T(8,128)(2,1)S(1)}, bf16[64,2048]{1,0:T(8,128)(2,1)S(1)}, u32[]{:S(2)}, u32[]{:S(2)}) %collective-permute-start.35) | collective-permute-done | bytes 262176 | tf_op jit(solution)/shard_map/ppermute | solution.py:662
  108.4 2.1 %finish.2.refs_9_ = bf16[128,4096]{1,0:T(8,128)(2,1)} custom-call(s32[14]{0:T(128)S(1)} %concatenate.3.index_ref.refs_0_, bf16[1,64,128]{2,1,0:T(8,128)(2,1)S(1)} %get-tuple-element.33.refs_1_, bf16[4,64,4096]{2,1,0:T(8,128)(2,1)S(1)} %copy-done.1, f32[64,2048]{1,0:T(8,128)S(1)} %get-tuple-element.51.refs_3_, ...), custom_call_target="tpu_custom_call" | custom-call | flops 1 | bytes 1 | tf_op jit(solution)/shard_map/finish/pallas_call | solution.py:620
  110.5 3.0 %collective-permute-done.30.refs_8_ = bf16[64,2048]{1,0:T(8,128)(2,1)S(1)} collective-permute-done((bf16[64,2048]{1,0:T(8,128)(2,1)S(1)}, bf16[64,2048]{1,0:T(8,128)(2,1)S(1)}, u32[]{:S(2)}, u32[]{:S(2)}) %collective-permute-start.30) | collective-permute-done | bytes 262176 | tf_op jit(solution)/shard_map/ppermute | solution.py:662
  113.6 2.1 %finish.3 = bf16[128,4096]{1,0:T(8,128)(2,1)} custom-call(s32[14]{0:T(128)S(1)} %concatenate.3.index_ref.refs_0_, bf16[1,64,128]{2,1,0:T(8,128)(2,1)S(1)} %get-tuple-element.33.refs_1_, bf16[4,64,4096]{2,1,0:T(8,128)(2,1)S(1)} %copy-done.1, f32[64,2048]{1,0:T(8,128)S(1)} %get-tuple-element.39.refs_3_, ...), custom_call_target="tpu_custom_call", output_to_operand_aliasing={{}: (9, {})} | custom-call | flops 1 | bytes 1 | tf_op jit(solution)/shard_map/finish/pallas_call | solution.py:620
  (79 shorter events, 32.7 us)
Async XLA Ops:
  3.3 22.1 %collective-permute-start.4 = (bf16[128,2048]{1,0:T(8,128)(2,1)S(1)}, bf16[128,2048]{1,0:T(8,128)(2,1)S(1)}, u32[]{:S(2)}, u32[]{:S(2)}) collective-permute-start(bf16[128,2048]{1,0:T(8,128)(2,1)S(1)} %get-tuple-element.30.refs_0_), channel_id=1, source_target_pairs={{12,8},{0,4},{13,9},{1,5},{14,10},{2,6},{15,11},{3,7},{28,24},{16,... | collective-permute-start | bytes 1572872 | tf_op jit(solution)/shard_map/ppermute | solution.py:220
  8.3 17.2 %collective-permute-start.5 = (bf16[128,2048]{1,0:T(8,128)(2,1)S(1)}, bf16[128,2048]{1,0:T(8,128)(2,1)S(1)}, u32[]{:S(2)}, u32[]{:S(2)}) collective-permute-start(bf16[128,2048]{1,0:T(8,128)(2,1)S(1)} %get-tuple-element.34), channel_id=1, source_target_pairs={{8,4},{9,5},{10,6},{11,7},{24,20},{25,21},{26,22},{27,23}} | collective-permute-start | bytes 1572872 | tf_op jit(solution)/shard_map/ppermute | solution.py:221
  26.1 15.8 %collective-permute-start.6 = (bf16[128,2048]{1,0:T(8,128)(2,1)S(1)}, bf16[128,2048]{1,0:T(8,128)(2,1)S(1)}, u32[]{:S(2)}, u32[]{:S(2)}) collective-permute-start(bf16[128,2048]{1,0:T(8,128)(2,1)S(1)} %get-tuple-element.35), channel_id=1, source_target_pairs={{4,0},{0,4},{12,8},{5,1},{1,5},{13,9},{6,2},{2,6},{14,10},{7,3},{3... | collective-permute-start | bytes 1572872 | tf_op jit(solution)/shard_map/ppermute | solution.py:230
  28.0 13.9 %collective-permute-start.7 = (bf16[128,2048]{1,0:T(8,128)(2,1)S(1)}, bf16[128,2048]{1,0:T(8,128)(2,1)S(1)}, u32[]{:S(2)}, u32[]{:S(2)}) collective-permute-start(bf16[128,2048]{1,0:T(8,128)(2,1)S(1)} %get-tuple-element.36), channel_id=1, source_target_pairs={{8,4},{4,8},{9,5},{5,9},{10,6},{6,10},{11,7},{7,11},{24,20},{20,24... | collective-permute-start | bytes 1572872 | tf_op jit(solution)/shard_map/ppermute | solution.py:231
  28.7 13.2 %collective-permute-start.3 = (f32[2,1,64,128]{3,2,1,0:T(8,128)S(1)}, f32[2,1,64,128]{3,2,1,0:T(8,128)S(1)}, u32[]{:S(2)}, u32[]{:S(2)}) collective-permute-start(f32[2,1,64,128]{3,2,1,0:T(8,128)S(1)} %add.31.sum_ref.refs_0_), channel_id=1, source_target_pairs={{0,4},{4,0},{8,12},{12,8},{1,5},{5,1},{9,13},{13,9},{2,6},{6,2},{1... | collective-permute-start | bytes 196616 | tf_op jit(solution)/shard_map/ppermute | solution.py:665
  42.6 9.0 %collective-permute-start.8 = (bf16[64,2048]{1,0:T(8,128)(2,1)S(1)}, bf16[64,2048]{1,0:T(8,128)(2,1)S(1)}, u32[]{:S(2)}, u32[]{:S(2)}) collective-permute-start(bf16[64,2048]{1,0:T(8,128)(2,1)S(1)} %get-tuple-element.37.home_ref), channel_id=1, source_target_pairs={{0,4},{4,0},{8,12},{12,8},{1,5},{5,1},{9,13},{13,9},{2,6},{6,2},{1... | collective-permute-start | bytes 786440 | tf_op jit(solution)/shard_map/ppermute | solution.py:240
  44.8 9.8 %collective-permute-start.9 = (bf16[64,2048]{1,0:T(8,128)(2,1)S(1)}, bf16[64,2048]{1,0:T(8,128)(2,1)S(1)}, u32[]{:S(2)}, u32[]{:S(2)}) collective-permute-start(bf16[64,2048]{1,0:T(8,128)(2,1)S(1)} %get-tuple-element.37.home_ref), channel_id=1, source_target_pairs={{4,8},{8,4},{5,9},{9,5},{6,10},{10,6},{7,11},{11,7},{20,24},{24,20... | collective-permute-start | bytes 786440 | tf_op jit(solution)/shard_map/ppermute | solution.py:241
  45.5 10.5 %collective-permute-start.13 = (bf16[64,2048]{1,0:T(8,128)(2,1)S(1)}, bf16[64,2048]{1,0:T(8,128)(2,1)S(1)}, u32[]{:S(2)}, u32[]{:S(2)}) collective-permute-start(bf16[64,2048]{1,0:T(8,128)(2,1)S(1)} %get-tuple-element.38.home_ref), channel_id=1, source_target_pairs={{0,4},{4,0},{8,12},{12,8},{1,5},{5,1},{9,13},{13,9},{2,6},{6,2},{1... | collective-permute-start | bytes 786440 | tf_op jit(solution)/shard_map/ppermute | solution.py:240
  47.2 9.5 %collective-permute-start.15 = (bf16[64,2048]{1,0:T(8,128)(2,1)S(1)}, bf16[64,2048]{1,0:T(8,128)(2,1)S(1)}, u32[]{:S(2)}, u32[]{:S(2)}) collective-permute-start(bf16[64,2048]{1,0:T(8,128)(2,1)S(1)} %get-tuple-element.38.home_ref), channel_id=1, source_target_pairs={{4,8},{8,4},{5,9},{9,5},{6,10},{10,6},{7,11},{11,7},{20,24},{24,20... | collective-permute-start | bytes 786440 | tf_op jit(solution)/shard_map/ppermute | solution.py:241
  53.1 20.2 %collective-permute-start.21 = (bf16[1,64,4096]{2,1,0:T(8,128)(2,1)S(1)}, bf16[1,64,4096]{2,1,0:T(8,128)(2,1)S(1)}, u32[]{:S(2)}, u32[]{:S(2)}) collective-permute-start(bf16[1,64,4096]{2,1,0:T(8,128)(2,1)S(1)} %get-tuple-element.43.refs_0_), channel_id=1, source_target_pairs={{0,2},{1,3},{2,0},{3,1},{4,6},{5,7},{6,4},{7,5},{8,10},{9,11},{10,... | collective-permute-start | bytes 1572872 | tf_op jit(solution)/shard_map/ppermute | solution.py:662
  54.7 11.4 %collective-permute-start.11 = (bf16[64,2048]{1,0:T(8,128)(2,1)S(1)}, bf16[64,2048]{1,0:T(8,128)(2,1)S(1)}, u32[]{:S(2)}, u32[]{:S(2)}) collective-permute-start(bf16[64,2048]{1,0:T(8,128)(2,1)S(1)} %collective-permute-done.9.refs_0_), channel_id=1, source_target_pairs={{4,0},{8,12},{5,1},{9,13},{6,2},{10,14},{7,3},{11,15},{20,16},{24,... | collective-permute-start | bytes 786440 | tf_op jit(solution)/shard_map/ppermute | solution.py:242
  56.0 10.2 %collective-permute-start.14 = (bf16[64,2048]{1,0:T(8,128)(2,1)S(1)}, bf16[64,2048]{1,0:T(8,128)(2,1)S(1)}, u32[]{:S(2)}, u32[]{:S(2)}) collective-permute-start(bf16[64,2048]{1,0:T(8,128)(2,1)S(1)} %collective-permute-done.13.refs_0_.outer_ref), channel_id=1, source_target_pairs={{4,8},{8,4},{5,9},{9,5},{6,10},{10,6},{7,11},{11,7},{20,24},{24,20... | collective-permute-start | bytes 786440 | tf_op jit(solution)/shard_map/ppermute | solution.py:243
  56.7 13.2 %collective-permute-start.16 = (bf16[64,2048]{1,0:T(8,128)(2,1)S(1)}, bf16[64,2048]{1,0:T(8,128)(2,1)S(1)}, u32[]{:S(2)}, u32[]{:S(2)}) collective-permute-start(bf16[64,2048]{1,0:T(8,128)(2,1)S(1)} %collective-permute-done.15.refs_1_.refs_0_), channel_id=1, source_target_pairs={{4,0},{8,12},{5,1},{9,13},{6,2},{10,14},{7,3},{11,15},{20,16},{24,... | collective-permute-start | bytes 786440 | tf_op jit(solution)/shard_map/ppermute | solution.py:242
  58.0 14.7 %collective-permute-start.12 = (bf16[64,2048]{1,0:T(8,128)(2,1)S(1)}, bf16[64,2048]{1,0:T(8,128)(2,1)S(1)}, u32[]{:S(2)}, u32[]{:S(2)}) collective-permute-start(bf16[64,2048]{1,0:T(8,128)(2,1)S(1)} %collective-permute-done.10.refs_1_), channel_id=1, source_target_pairs={{4,0},{8,12},{5,1},{9,13},{6,2},{10,14},{7,3},{11,15},{20,16},{24,... | collective-permute-start | bytes 786440 | tf_op jit(solution)/shard_map/ppermute | solution.py:244
  75.7 10.6 %collective-permute-start.20 = (bf16[64,2048]{1,0:T(8,128)(2,1)S(1)}, bf16[64,2048]{1,0:T(8,128)(2,1)S(1)}, u32[]{:S(2)}, u32[]{:S(2)}) collective-permute-start(bf16[64,2048]{1,0:T(8,128)(2,1)S(1)} %collective-permute-done.14.refs_4_.refs_1_), channel_id=1, source_target_pairs={{4,0},{8,12},{5,1},{9,13},{6,2},{10,14},{7,3},{11,15},{20,16},{24,... | collective-permute-start | bytes 786440 | tf_op jit(solution)/shard_map/ppermute | solution.py:244
  77.3 12.7 %collective-permute-start.32 = (bf16[64,2048]{1,0:T(8,128)(2,1)S(1)}, bf16[64,2048]{1,0:T(8,128)(2,1)S(1)}, u32[]{:S(2)}, u32[]{:S(2)}) collective-permute-start(bf16[64,2048]{1,0:T(8,128)(2,1)S(1)} %add_convert_fusion.2.refs_4_), channel_id=1, source_target_pairs={{0,2},{1,3},{2,0},{3,1},{4,6},{5,7},{6,4},{7,5},{8,10},{9,11},{10,... | collective-permute-start | bytes 786440 | tf_op jit(solution)/shard_map/ppermute | solution.py:662
  80.6 12.3 %collective-permute-start.18 = (bf16[64,2048]{1,0:T(8,128)(2,1)S(1)}, bf16[64,2048]{1,0:T(8,128)(2,1)S(1)}, u32[]{:S(2)}, u32[]{:S(2)}) collective-permute-start(bf16[64,2048]{1,0:T(8,128)(2,1)S(1)} %get-tuple-element.42), channel_id=1, source_target_pairs={{0,1},{1,0},{2,3},{3,2},{4,5},{5,4},{6,7},{7,6},{8,9},{9,8},{10,11... | collective-permute-start | bytes 786440 | tf_op jit(solution)/shard_map/ppermute | solution.py:659
  80.7 13.0 %collective-permute-start.26 = (bf16[1,64,4096]{2,1,0:T(8,128)(2,1)S(1)}, bf16[1,64,4096]{2,1,0:T(8,128)(2,1)S(1)}, u32[]{:S(2)}, u32[]{:S(2)}) collective-permute-start(bf16[1,64,4096]{2,1,0:T(8,128)(2,1)S(1)} %get-tuple-element.43.refs_0_), channel_id=1, source_target_pairs={{0,1},{1,0},{2,3},{3,2},{4,5},{5,4},{6,7},{7,6},{8,9},{9,8},{10,11... | collective-permute-start | bytes 1572872 | tf_op jit(solution)/shard_map/ppermute | solution.py:659
  81.2 13.4 %collective-permute-start.27 = (bf16[1,64,4096]{2,1,0:T(8,128)(2,1)S(1)}, bf16[1,64,4096]{2,1,0:T(8,128)(2,1)S(1)}, u32[]{:S(2)}, u32[]{:S(2)}) collective-permute-start(bf16[1,64,4096]{2,1,0:T(8,128)(2,1)S(1)} %collective-permute-done.21.refs_0_.refs_1_), channel_id=1, source_target_pairs={{0,1},{1,0},{2,3},{3,2},{4,5},{5,4},{6,7},{7,6},{8,9},{9,8},{10,11... | collective-permute-start | bytes 1572872 | tf_op jit(solution)/shard_map/ppermute | solution.py:659
  93.0 17.5 %collective-permute-start.17 = (bf16[64,2048]{1,0:T(8,128)(2,1)S(1)}, bf16[64,2048]{1,0:T(8,128)(2,1)S(1)}, u32[]{:S(2)}, u32[]{:S(2)}) collective-permute-start(bf16[64,2048]{1,0:T(8,128)(2,1)S(1)} %get-tuple-element.40), channel_id=1, source_target_pairs={{0,1},{1,0},{2,3},{3,2},{4,5},{5,4},{6,7},{7,6},{8,9},{9,8},{10,11... | collective-permute-start | bytes 786440 | tf_op jit(solution)/shard_map/ppermute | solution.py:659
  93.7 16.9 %collective-permute-start.19 = (bf16[64,2048]{1,0:T(8,128)(2,1)S(1)}, bf16[64,2048]{1,0:T(8,128)(2,1)S(1)}, u32[]{:S(2)}, u32[]{:S(2)}) collective-permute-start(bf16[64,2048]{1,0:T(8,128)(2,1)S(1)} %add_convert_fusion.3), channel_id=1, source_target_pairs={{0,2},{1,3},{2,0},{3,1},{4,6},{5,7},{6,4},{7,5},{8,10},{9,11},{10,... | collective-permute-start | bytes 786440 | tf_op jit(solution)/shard_map/ppermute | solution.py:662
  98.6 9.9 %collective-permute-start.35 = (bf16[64,2048]{1,0:T(8,128)(2,1)S(1)}, bf16[64,2048]{1,0:T(8,128)(2,1)S(1)}, u32[]{:S(2)}, u32[]{:S(2)}) collective-permute-start(bf16[64,2048]{1,0:T(8,128)(2,1)S(1)} %add_convert_fusion), channel_id=1, source_target_pairs={{0,2},{1,3},{2,0},{3,1},{4,6},{5,7},{6,4},{7,5},{8,10},{9,11},{10,... | collective-permute-start | bytes 786440 | tf_op jit(solution)/shard_map/ppermute | solution.py:662
  99.7 10.8 %collective-permute-start.28 = (bf16[64,2048]{1,0:T(8,128)(2,1)S(1)}, bf16[64,2048]{1,0:T(8,128)(2,1)S(1)}, u32[]{:S(2)}, u32[]{:S(2)}) collective-permute-start(bf16[64,2048]{1,0:T(8,128)(2,1)S(1)} %get-tuple-element.48), channel_id=1, source_target_pairs={{0,1},{1,0},{2,3},{3,2},{4,5},{5,4},{6,7},{7,6},{8,9},{9,8},{10,11... | collective-permute-start | bytes 786440 | tf_op jit(solution)/shard_map/ppermute | solution.py:659
  99.8 13.8 %collective-permute-start.30 = (bf16[64,2048]{1,0:T(8,128)(2,1)S(1)}, bf16[64,2048]{1,0:T(8,128)(2,1)S(1)}, u32[]{:S(2)}, u32[]{:S(2)}) collective-permute-start(bf16[64,2048]{1,0:T(8,128)(2,1)S(1)} %add_convert_fusion.1), channel_id=1, source_target_pairs={{0,2},{1,3},{2,0},{3,1},{4,6},{5,7},{6,4},{7,5},{8,10},{9,11},{10,... | collective-permute-start | bytes 786440 | tf_op jit(solution)/shard_map/ppermute | solution.py:662
  (15 other events, 119.5 us)

commit v21 on v17

--- a/solution.py
+++ b/solution.py
@@ -542,6 +542,8 @@
     index = index_of(index_ref)
     up_refs, sum_refs, out_ref = refs[: index.per_part], refs[index.per_part : -1], refs[-1]
     per_chunk = len(sum_refs) // len(CHUNK_ROWS)
+    tile = out_ref.shape[1]
+    columns = pl.ds(pl.multiple_of(pl.program_id(0) * tile, tile), tile)
     for i in range(index.per_part):
         block = index.block(0, 0, i)
         live = index.live_rows(block)
@@ -555,7 +557,7 @@
         for c, count in enumerate(CHUNK_ROWS):
             total = adapter_scale * side[start : start + count]
             for ref in sum_refs[c * per_chunk : (c + 1) * per_chunk]:
-                total = total + ref[i * count : (i + 1) * count].astype(jnp.float32)
+                total = total + ref[i * count : (i + 1) * count, columns].astype(jnp.float32)
             keep = start + lax.broadcasted_iota(jnp.int32, total.shape, 0) < live
             at = i * BLK + start
             out_ref[at : at + count] = jnp.where(keep, total, 0.0).astype(out_ref.dtype)
@@ -578,12 +580,8 @@
         return pl.BlockSpec((1, rank, tile), at)
 
     flat = [term for chunk in sums for term in chunk]
-    specs = [
-        pl.BlockSpec((per_part * count, tile), lambda n, _: (0, n))
-        for chunk, count in zip(sums, CHUNK_ROWS)
-        for _ in chunk
-    ]
-    operands = [index, lowered, *[up] * per_part, *flat]
+    specs = [held()] * len(flat)
+    operands = [index, lowered, *[up] * per_part, *[in_vmem(term) for term in flat]]
     more, extra = after((), far)
     aliases = {}
     if projected is not None:

time: 116 us -> 116 us (level)
  transfers between devices with their start and end apart: 36 -> 36, of which waited for: 14 -> 14; matrix products, arithmetic and copies ran while one was open for 0% -> 0% of each run, Pallas kernels for 23% -> 22%
where the time goes in v21:
time: 116 us
  waiting for transfers between devices  44.1 us (38%)
  starting transfers between devices  36.2 us (31%)
  Pallas kernels  33.1 us (29%)
    ppermute x2, waiting for transfers between devices, across_dp(): return lax.ppermute(value, 'dp', [(i, i ^ k) for i in range(owners)])  15.4 us
    ppermute x7, waiting for transfers between devices, to_chip(): lax.ppermute(value, 'tensor', [(i, i ^ k * CORES) for i in range(parts)])  10 us
    pallas_call x4, Pallas kernels, split_product(): pl.pallas_call(functools.partial(split_product_kernel, each, half, part *...  9.29 us
    ppermute x7, starting transfers between devices, to_chip(): lax.ppermute(value, 'tensor', [(i, i ^ k * CORES) for i in range(parts)])  8.08 us
    ppermute x2, waiting for transfers between devices, spread(): outer_3 = lax.ppermute(inner_2, 'dp', [(1, 0), (2, 3)])  7.8 us
    pallas_call x1, Pallas kernels, load_weight(): pl.pallas_call(load_weight_kernel, grid=(1,), in_specs=[pl.BlockSpec(memo...  5.89 us
    ppermute x2, starting transfers between devices, across_dp(): return lax.ppermute(value, 'dp', [(i, i ^ k) for i in range(owners)])  5.43 us
    ppermute x1, starting transfers between devices, first(): lax.ppermute(inward, 'dp', [(3, 2), (0, 1)])  4.96 us
  transfers between devices with their start and end apart: 36, of which 14 were waited for; matrix products, arithmetic and copies ran while one was open for 0% of the time, Pallas kernels for 22%

profile of v21, /device:TPU:0, one launch (start us, length us, event | category | flops | bytes accessed | tf_op | source)
XLA Modules:
  0.0 115.6 jit_solution(53873417735662858)
XLA Ops:
  3.3 5.0 %collective-permute-start.4 = (bf16[128,2048]{1,0:T(8,128)(2,1)S(1)}, bf16[128,2048]{1,0:T(8,128)(2,1)S(1)}, u32[]{:S(2)}, u32[]{:S(2)}) collective-permute-start(bf16[128,2048]{1,0:T(8,128)(2,1)S(1)} %get-tuple-element.31.refs_0_), channel_id=1, source_target_pairs={{12,8},{0,4},{13,9},{1,5},{14,10},{2,6},{15,11},{3,7},{28,24},{16,... | collective-permute-start | bytes 1572872 | tf_op jit(solution)/shard_map/ppermute | solution.py:220
  9.0 3.5 %narrow.1 = (f32[2,1,64,128]{3,2,1,0:T(8,128)S(1)}, f32[2,1,64,128]{3,2,1,0:T(8,128)S(1)}, f32[1,64,128]{2,1,0:T(8,128)S(1)}) custom-call(s32[14]{0:T(128)S(1)} %concatenate.3.index_ref.refs_0_, bf16[384,2048]{1,0:T(8,128)(2,1)} %tokens_ref.9, bf16[1,64,2048]{2,1,0:T(8,128)(2,1)} %bitcast.7, bf16[128,4096]{1,0:T(8,128)(2,1)} %cot_ref.3, ...), custom_call_target="tpu_custom_call" | custom-call | flops 1 | bytes 1 | tf_op jit(solution)/shard_map/narrow/pallas_call | solution.py:376
  15.3 2.4 %collective-permute-done.1.refs_0_ = f32[1,64,128]{2,1,0:T(8,128)S(1)} collective-permute-done((f32[1,64,128]{2,1,0:T(8,128)S(1)}, f32[1,64,128]{2,1,0:T(8,128)S(1)}, u32[]{:S(2)}, u32[]{:S(2)}) %collective-permute-start.1) | collective-permute-done | bytes 32800 | tf_op jit(solution)/shard_map/ppermute | solution.py:636
  17.8 2.1 %collective-permute-start.2 = (f32[2,1,64,128]{3,2,1,0:T(8,128)S(1)}, f32[2,1,64,128]{3,2,1,0:T(8,128)S(1)}, u32[]{:S(2)}, u32[]{:S(2)}) collective-permute-start(f32[2,1,64,128]{3,2,1,0:T(8,128)S(1)} %merge.1), channel_id=1, source_target_pairs={{0,8},{4,12},{8,0},{12,4},{1,9},{5,13},{9,1},{13,5},{2,10},{6,14},... | collective-permute-start | bytes 196616 | tf_op jit(solution)/shard_map/ppermute | solution.py:639
  19.9 5.5 %collective-permute-done.2 = f32[2,1,64,128]{3,2,1,0:T(8,128)S(1)} collective-permute-done((f32[2,1,64,128]{3,2,1,0:T(8,128)S(1)}, f32[2,1,64,128]{3,2,1,0:T(8,128)S(1)}, u32[]{:S(2)}, u32[]{:S(2)}) %collective-permute-start.2) | collective-permute-done | bytes 65568 | tf_op jit(solution)/shard_map/ppermute | solution.py:639
  26.1 1.9 %collective-permute-start.6 = (bf16[128,2048]{1,0:T(8,128)(2,1)S(1)}, bf16[128,2048]{1,0:T(8,128)(2,1)S(1)}, u32[]{:S(2)}, u32[]{:S(2)}) collective-permute-start(bf16[128,2048]{1,0:T(8,128)(2,1)S(1)} %get-tuple-element.37), channel_id=1, source_target_pairs={{4,0},{0,4},{12,8},{5,1},{1,5},{13,9},{6,2},{2,6},{14,10},{7,3},{3... | collective-permute-start | bytes 1572872 | tf_op jit(solution)/shard_map/ppermute | solution.py:230
  28.7 3.3 %collective-permute-start.3 = (f32[2,1,64,128]{3,2,1,0:T(8,128)S(1)}, f32[2,1,64,128]{3,2,1,0:T(8,128)S(1)}, u32[]{:S(2)}, u32[]{:S(2)}) collective-permute-start(f32[2,1,64,128]{3,2,1,0:T(8,128)S(1)} %add.31.sum_ref.refs_0_), channel_id=1, source_target_pairs={{0,4},{4,0},{8,12},{12,8},{1,5},{5,1},{9,13},{13,9},{2,6},{6,2},{1... | collective-permute-start | bytes 196616 | tf_op jit(solution)/shard_map/ppermute | solution.py:639
  32.0 9.9 %collective-permute-done.3.refs_0_ = f32[2,1,64,128]{3,2,1,0:T(8,128)S(1)} collective-permute-done((f32[2,1,64,128]{3,2,1,0:T(8,128)S(1)}, f32[2,1,64,128]{3,2,1,0:T(8,128)S(1)}, u32[]{:S(2)}, u32[]{:S(2)}) %collective-permute-start.3) | collective-permute-done | bytes 65568 | tf_op jit(solution)/shard_map/ppermute | solution.py:639
  42.6 2.3 %collective-permute-start.8 = (bf16[64,2048]{1,0:T(8,128)(2,1)S(1)}, bf16[64,2048]{1,0:T(8,128)(2,1)S(1)}, u32[]{:S(2)}, u32[]{:S(2)}) collective-permute-start(bf16[64,2048]{1,0:T(8,128)(2,1)S(1)} %get-tuple-element.39.home_ref), channel_id=1, source_target_pairs={{0,4},{4,0},{8,12},{12,8},{1,5},{5,1},{9,13},{13,9},{2,6},{6,2},{1... | collective-permute-start | bytes 786440 | tf_op jit(solution)/shard_map/ppermute | solution.py:240
  47.8 3.8 %collective-permute-done.8.outer_ref = bf16[64,2048]{1,0:T(8,128)(2,1)S(1)} collective-permute-done((bf16[64,2048]{1,0:T(8,128)(2,1)S(1)}, bf16[64,2048]{1,0:T(8,128)(2,1)S(1)}, u32[]{:S(2)}, u32[]{:S(2)}) %collective-permute-start.8) | collective-permute-done | bytes 262176 | tf_op jit(solution)/shard_map/ppermute | solution.py:240
  59.3 5.9 %load_weight.1.refs_6_.w_ref = bf16[2048,4096]{1,0:T(8,128)(2,1)S(1)} custom-call(bf16[2048,4096]{1,0:T(8,128)(2,1)} %w_ref.1, bf16[64,2048]{1,0:T(8,128)(2,1)S(1)} %collective-permute-done.13.refs_0_.outer_ref, bf16[64,2048]{1,0:T(8,128)(2,1)S(1)} %collective-permute-done.15.refs_1_.refs_0_), custom_call_target="tpu_custom_call" | custom-call | flops 1 | bytes 1 | tf_op jit(solution)/shard_map/load_weight/pallas_call | solution.py:284
  66.2 3.7 %collective-permute-done.16.refs_5_.refs_2_ = bf16[64,2048]{1,0:T(8,128)(2,1)S(1)} collective-permute-done((bf16[64,2048]{1,0:T(8,128)(2,1)S(1)}, bf16[64,2048]{1,0:T(8,128)(2,1)S(1)}, u32[]{:S(2)}, u32[]{:S(2)}) %collective-permute-start.16) | collective-permute-done | bytes 262176 | tf_op jit(solution)/shard_map/ppermute | solution.py:242
  69.9 2.8 %collective-permute-done.12.refs_3_ = bf16[64,2048]{1,0:T(8,128)(2,1)S(1)} collective-permute-done((bf16[64,2048]{1,0:T(8,128)(2,1)S(1)}, bf16[64,2048]{1,0:T(8,128)(2,1)S(1)}, u32[]{:S(2)}, u32[]{:S(2)}) %collective-permute-start.12) | collective-permute-done | bytes 262176 | tf_op jit(solution)/shard_map/ppermute | solution.py:244
  73.3 2.3 %split_product.5 = (bf16[64,2048]{1,0:T(8,128)(2,1)S(1)}, bf16[64,2048]{1,0:T(8,128)(2,1)S(1)}, f32[64,2048]{1,0:T(8,128)S(1)}, f32[64,2048]{1,0:T(8,128)S(1)}) custom-call(bf16[256,2048]{1,0:T(8,128)(2,1)S(1)} %collect.2.rows_ref, bf16[2048,4096]{1,0:T(8,128)(2,1)S(1)} %load_weight.1.refs_6_.w_ref, ...), custom_call_target="tpu_custom_call" | custom-call | flops 1 | bytes 1 | tf_op jit(solution)/shard_map/split_product/pallas_call | solution.py:317
  78.3 2.3 %split_product.4 = (bf16[64,2048]{1,0:T(8,128)(2,1)S(1)}, bf16[64,2048]{1,0:T(8,128)(2,1)S(1)}, f32[64,2048]{1,0:T(8,128)S(1)}, f32[64,2048]{1,0:T(8,128)S(1)}) custom-call(bf16[256,2048]{1,0:T(8,128)(2,1)S(1)} %collect.2.rows_ref, bf16[2048,4096]{1,0:T(8,128)(2,1)S(1)} %load_weight.1.refs_6_.w_ref), custom_call_target="tpu_custom_call" | custom-call | flops 1 | bytes 1 | tf_op jit(solution)/shard_map/split_product/pallas_call | solution.py:317
  81.3 5.0 %collective-permute-done.20.refs_3_ = bf16[64,2048]{1,0:T(8,128)(2,1)S(1)} collective-permute-done((bf16[64,2048]{1,0:T(8,128)(2,1)S(1)}, bf16[64,2048]{1,0:T(8,128)(2,1)S(1)}, u32[]{:S(2)}, u32[]{:S(2)}) %collective-permute-start.20) | collective-permute-done | bytes 262176 | tf_op jit(solution)/shard_map/ppermute | solution.py:244
  87.9 2.1 %collective-permute-done.24.refs_1_ = bf16[1,64,128]{2,1,0:T(8,128)(2,1)S(1)} collective-permute-done((bf16[1,64,128]{2,1,0:T(8,128)(2,1)S(1)}, bf16[1,64,128]{2,1,0:T(8,128)(2,1)S(1)}, u32[]{:S(2)}, u32[]{:S(2)}) %collective-permute-start.24) | collective-permute-done | bytes 16416 | tf_op jit(solution)/shard_map/ppermute | solution.py:636
  90.6 2.3 %split_product.7 = (bf16[64,2048]{1,0:T(8,128)(2,1)S(1)}, bf16[64,2048]{1,0:T(8,128)(2,1)S(1)}, f32[64,2048]{1,0:T(8,128)S(1)}, f32[64,2048]{1,0:T(8,128)S(1)}) custom-call(bf16[256,2048]{1,0:T(8,128)(2,1)S(1)} %collect.3.rows_ref, bf16[2048,4096]{1,0:T(8,128)(2,1)S(1)} %load_weight.1.refs_6_.w_ref, ...), custom_call_target="tpu_custom_call" | custom-call | flops 1 | bytes 1 | tf_op jit(solution)/shard_map/split_product/pallas_call | solution.py:317
  94.7 2.3 %split_product.6 = (bf16[64,2048]{1,0:T(8,128)(2,1)S(1)}, bf16[64,2048]{1,0:T(8,128)(2,1)S(1)}, f32[64,2048]{1,0:T(8,128)S(1)}, f32[64,2048]{1,0:T(8,128)S(1)}) custom-call(bf16[256,2048]{1,0:T(8,128)(2,1)S(1)} %collect.3.rows_ref, bf16[2048,4096]{1,0:T(8,128)(2,1)S(1)} %load_weight.1.refs_6_.w_ref, ...), custom_call_target="tpu_custom_call" | custom-call | flops 1 | bytes 1 | tf_op jit(solution)/shard_map/split_product/pallas_call | solution.py:317
  102.3 3.9 %up_gradient.1.refs_9_ = f32[4,64,4096]{2,1,0:T(8,128)} custom-call(s32[14]{0:T(128)S(1)} %concatenate.3.index_ref.refs_0_, bf16[1,64,4096]{2,1,0:T(8,128)(2,1)S(1)} %get-tuple-element.45.refs_0_, bf16[1,64,4096]{2,1,0:T(8,128)(2,1)S(1)} %collective-permute-done.21.refs_0_.refs_1_, bf16[1,64,4096]{2,1,0:T(8,128)(2,1)S(1)} %collective-permute-done.26.refs_2_, ...), custom_call_target="tpu_custom_call" | custom-call | flops 1 | bytes 1 | tf_op jit(solution)/shard_map/up_gradient/pallas_call | solution.py:526
  106.2 2.3 %collective-permute-done.35.refs_8_ = bf16[64,2048]{1,0:T(8,128)(2,1)S(1)} collective-permute-done((bf16[64,2048]{1,0:T(8,128)(2,1)S(1)}, bf16[64,2048]{1,0:T(8,128)(2,1)S(1)}, u32[]{:S(2)}, u32[]{:S(2)}) %collective-permute-start.35) | collective-permute-done | bytes 262176 | tf_op jit(solution)/shard_map/ppermute | solution.py:636
  108.4 2.0 %finish.2.refs_9_ = bf16[128,4096]{1,0:T(8,128)(2,1)} custom-call(s32[14]{0:T(128)S(1)} %concatenate.3.index_ref.refs_0_, bf16[1,64,128]{2,1,0:T(8,128)(2,1)S(1)} %get-tuple-element.35.refs_1_, bf16[4,64,4096]{2,1,0:T(8,128)(2,1)S(1)} %copy-done.1, f32[64,2048]{1,0:T(8,128)S(1)} %get-tuple-element.53.refs_3_, ...), custom_call_target="tpu_custom_call" | custom-call | flops 1 | bytes 1 | tf_op jit(solution)/shard_map/finish/pallas_call | solution.py:594
  110.4 3.2 %collective-permute-done.30.refs_8_ = bf16[64,2048]{1,0:T(8,128)(2,1)S(1)} collective-permute-done((bf16[64,2048]{1,0:T(8,128)(2,1)S(1)}, bf16[64,2048]{1,0:T(8,128)(2,1)S(1)}, u32[]{:S(2)}, u32[]{:S(2)}) %collective-permute-start.30) | collective-permute-done | bytes 262176 | tf_op jit(solution)/shard_map/ppermute | solution.py:636
  113.6 2.0 %finish.3 = bf16[128,4096]{1,0:T(8,128)(2,1)} custom-call(s32[14]{0:T(128)S(1)} %concatenate.3.index_ref.refs_0_, bf16[1,64,128]{2,1,0:T(8,128)(2,1)S(1)} %get-tuple-element.35.refs_1_, bf16[4,64,4096]{2,1,0:T(8,128)(2,1)S(1)} %copy-done.1, f32[64,2048]{1,0:T(8,128)S(1)} %get-tuple-element.41.refs_3_, ...), custom_call_target="tpu_custom_call", output_to_operand_aliasing={{}: (9, {})} | custom-call | flops 1 | bytes 1 | tf_op jit(solution)/shard_map/finish/pallas_call | solution.py:594
  (78 shorter events, 32.7 us)
Async XLA Ops:
  3.3 22.1 %collective-permute-start.4 = (bf16[128,2048]{1,0:T(8,128)(2,1)S(1)}, bf16[128,2048]{1,0:T(8,128)(2,1)S(1)}, u32[]{:S(2)}, u32[]{:S(2)}) collective-permute-start(bf16[128,2048]{1,0:T(8,128)(2,1)S(1)} %get-tuple-element.31.refs_0_), channel_id=1, source_target_pairs={{12,8},{0,4},{13,9},{1,5},{14,10},{2,6},{15,11},{3,7},{28,24},{16,... | collective-permute-start | bytes 1572872 | tf_op jit(solution)/shard_map/ppermute | solution.py:220
  8.3 17.2 %collective-permute-start.5 = (bf16[128,2048]{1,0:T(8,128)(2,1)S(1)}, bf16[128,2048]{1,0:T(8,128)(2,1)S(1)}, u32[]{:S(2)}, u32[]{:S(2)}) collective-permute-start(bf16[128,2048]{1,0:T(8,128)(2,1)S(1)} %get-tuple-element.36), channel_id=1, source_target_pairs={{8,4},{9,5},{10,6},{11,7},{24,20},{25,21},{26,22},{27,23}} | collective-permute-start | bytes 1572872 | tf_op jit(solution)/shard_map/ppermute | solution.py:221
  26.1 15.8 %collective-permute-start.6 = (bf16[128,2048]{1,0:T(8,128)(2,1)S(1)}, bf16[128,2048]{1,0:T(8,128)(2,1)S(1)}, u32[]{:S(2)}, u32[]{:S(2)}) collective-permute-start(bf16[128,2048]{1,0:T(8,128)(2,1)S(1)} %get-tuple-element.37), channel_id=1, source_target_pairs={{4,0},{0,4},{12,8},{5,1},{1,5},{13,9},{6,2},{2,6},{14,10},{7,3},{3... | collective-permute-start | bytes 1572872 | tf_op jit(solution)/shard_map/ppermute | solution.py:230
  28.0 13.9 %collective-permute-start.7 = (bf16[128,2048]{1,0:T(8,128)(2,1)S(1)}, bf16[128,2048]{1,0:T(8,128)(2,1)S(1)}, u32[]{:S(2)}, u32[]{:S(2)}) collective-permute-start(bf16[128,2048]{1,0:T(8,128)(2,1)S(1)} %get-tuple-element.38), channel_id=1, source_target_pairs={{8,4},{4,8},{9,5},{5,9},{10,6},{6,10},{11,7},{7,11},{24,20},{20,24... | collective-permute-start | bytes 1572872 | tf_op jit(solution)/shard_map/ppermute | solution.py:231
  28.7 13.2 %collective-permute-start.3 = (f32[2,1,64,128]{3,2,1,0:T(8,128)S(1)}, f32[2,1,64,128]{3,2,1,0:T(8,128)S(1)}, u32[]{:S(2)}, u32[]{:S(2)}) collective-permute-start(f32[2,1,64,128]{3,2,1,0:T(8,128)S(1)} %add.31.sum_ref.refs_0_), channel_id=1, source_target_pairs={{0,4},{4,0},{8,12},{12,8},{1,5},{5,1},{9,13},{13,9},{2,6},{6,2},{1... | collective-permute-start | bytes 196616 | tf_op jit(solution)/shard_map/ppermute | solution.py:639
  42.6 9.1 %collective-permute-start.8 = (bf16[64,2048]{1,0:T(8,128)(2,1)S(1)}, bf16[64,2048]{1,0:T(8,128)(2,1)S(1)}, u32[]{:S(2)}, u32[]{:S(2)}) collective-permute-start(bf16[64,2048]{1,0:T(8,128)(2,1)S(1)} %get-tuple-element.39.home_ref), channel_id=1, source_target_pairs={{0,4},{4,0},{8,12},{12,8},{1,5},{5,1},{9,13},{13,9},{2,6},{6,2},{1... | collective-permute-start | bytes 786440 | tf_op jit(solution)/shard_map/ppermute | solution.py:240
  44.9 9.8 %collective-permute-start.9 = (bf16[64,2048]{1,0:T(8,128)(2,1)S(1)}, bf16[64,2048]{1,0:T(8,128)(2,1)S(1)}, u32[]{:S(2)}, u32[]{:S(2)}) collective-permute-start(bf16[64,2048]{1,0:T(8,128)(2,1)S(1)} %get-tuple-element.39.home_ref), channel_id=1, source_target_pairs={{4,8},{8,4},{5,9},{9,5},{6,10},{10,6},{7,11},{11,7},{20,24},{24,20... | collective-permute-start | bytes 786440 | tf_op jit(solution)/shard_map/ppermute | solution.py:241
  45.5 10.5 %collective-permute-start.13 = (bf16[64,2048]{1,0:T(8,128)(2,1)S(1)}, bf16[64,2048]{1,0:T(8,128)(2,1)S(1)}, u32[]{:S(2)}, u32[]{:S(2)}) collective-permute-start(bf16[64,2048]{1,0:T(8,128)(2,1)S(1)} %get-tuple-element.40.home_ref), channel_id=1, source_target_pairs={{0,4},{4,0},{8,12},{12,8},{1,5},{5,1},{9,13},{13,9},{2,6},{6,2},{1... | collective-permute-start | bytes 786440 | tf_op jit(solution)/shard_map/ppermute | solution.py:240
  47.2 9.5 %collective-permute-start.15 = (bf16[64,2048]{1,0:T(8,128)(2,1)S(1)}, bf16[64,2048]{1,0:T(8,128)(2,1)S(1)}, u32[]{:S(2)}, u32[]{:S(2)}) collective-permute-start(bf16[64,2048]{1,0:T(8,128)(2,1)S(1)} %get-tuple-element.40.home_ref), channel_id=1, source_target_pairs={{4,8},{8,4},{5,9},{9,5},{6,10},{10,6},{7,11},{11,7},{20,24},{24,20... | collective-permute-start | bytes 786440 | tf_op jit(solution)/shard_map/ppermute | solution.py:241
  53.1 20.2 %collective-permute-start.21 = (bf16[1,64,4096]{2,1,0:T(8,128)(2,1)S(1)}, bf16[1,64,4096]{2,1,0:T(8,128)(2,1)S(1)}, u32[]{:S(2)}, u32[]{:S(2)}) collective-permute-start(bf16[1,64,4096]{2,1,0:T(8,128)(2,1)S(1)} %get-tuple-element.45.refs_0_), channel_id=1, source_target_pairs={{0,2},{1,3},{2,0},{3,1},{4,6},{5,7},{6,4},{7,5},{8,10},{9,11},{10,... | collective-permute-start | bytes 1572872 | tf_op jit(solution)/shard_map/ppermute | solution.py:636
  54.7 11.4 %collective-permute-start.11 = (bf16[64,2048]{1,0:T(8,128)(2,1)S(1)}, bf16[64,2048]{1,0:T(8,128)(2,1)S(1)}, u32[]{:S(2)}, u32[]{:S(2)}) collective-permute-start(bf16[64,2048]{1,0:T(8,128)(2,1)S(1)} %collective-permute-done.9.refs_0_), channel_id=1, source_target_pairs={{4,0},{8,12},{5,1},{9,13},{6,2},{10,14},{7,3},{11,15},{20,16},{24,... | collective-permute-start | bytes 786440 | tf_op jit(solution)/shard_map/ppermute | solution.py:242
  56.0 10.1 %collective-permute-start.14 = (bf16[64,2048]{1,0:T(8,128)(2,1)S(1)}, bf16[64,2048]{1,0:T(8,128)(2,1)S(1)}, u32[]{:S(2)}, u32[]{:S(2)}) collective-permute-start(bf16[64,2048]{1,0:T(8,128)(2,1)S(1)} %collective-permute-done.13.refs_0_.outer_ref), channel_id=1, source_target_pairs={{4,8},{8,4},{5,9},{9,5},{6,10},{10,6},{7,11},{11,7},{20,24},{24,20... | collective-permute-start | bytes 786440 | tf_op jit(solution)/shard_map/ppermute | solution.py:243
  56.7 13.2 %collective-permute-start.16 = (bf16[64,2048]{1,0:T(8,128)(2,1)S(1)}, bf16[64,2048]{1,0:T(8,128)(2,1)S(1)}, u32[]{:S(2)}, u32[]{:S(2)}) collective-permute-start(bf16[64,2048]{1,0:T(8,128)(2,1)S(1)} %collective-permute-done.15.refs_1_.refs_0_), channel_id=1, source_target_pairs={{4,0},{8,12},{5,1},{9,13},{6,2},{10,14},{7,3},{11,15},{20,16},{24,... | collective-permute-start | bytes 786440 | tf_op jit(solution)/shard_map/ppermute | solution.py:242
  58.0 14.7 %collective-permute-start.12 = (bf16[64,2048]{1,0:T(8,128)(2,1)S(1)}, bf16[64,2048]{1,0:T(8,128)(2,1)S(1)}, u32[]{:S(2)}, u32[]{:S(2)}) collective-permute-start(bf16[64,2048]{1,0:T(8,128)(2,1)S(1)} %collective-permute-done.10.refs_1_), channel_id=1, source_target_pairs={{4,0},{8,12},{5,1},{9,13},{6,2},{10,14},{7,3},{11,15},{20,16},{24,... | collective-permute-start | bytes 786440 | tf_op jit(solution)/shard_map/ppermute | solution.py:244
  75.7 10.6 %collective-permute-start.20 = (bf16[64,2048]{1,0:T(8,128)(2,1)S(1)}, bf16[64,2048]{1,0:T(8,128)(2,1)S(1)}, u32[]{:S(2)}, u32[]{:S(2)}) collective-permute-start(bf16[64,2048]{1,0:T(8,128)(2,1)S(1)} %collective-permute-done.14.refs_4_.refs_1_), channel_id=1, source_target_pairs={{4,0},{8,12},{5,1},{9,13},{6,2},{10,14},{7,3},{11,15},{20,16},{24,... | collective-permute-start | bytes 786440 | tf_op jit(solution)/shard_map/ppermute | solution.py:244
  77.3 12.7 %collective-permute-start.32 = (bf16[64,2048]{1,0:T(8,128)(2,1)S(1)}, bf16[64,2048]{1,0:T(8,128)(2,1)S(1)}, u32[]{:S(2)}, u32[]{:S(2)}) collective-permute-start(bf16[64,2048]{1,0:T(8,128)(2,1)S(1)} %add_convert_fusion.2.refs_4_), channel_id=1, source_target_pairs={{0,2},{1,3},{2,0},{3,1},{4,6},{5,7},{6,4},{7,5},{8,10},{9,11},{10,... | collective-permute-start | bytes 786440 | tf_op jit(solution)/shard_map/ppermute | solution.py:636
  80.7 12.2 %collective-permute-start.18 = (bf16[64,2048]{1,0:T(8,128)(2,1)S(1)}, bf16[64,2048]{1,0:T(8,128)(2,1)S(1)}, u32[]{:S(2)}, u32[]{:S(2)}) collective-permute-start(bf16[64,2048]{1,0:T(8,128)(2,1)S(1)} %get-tuple-element.44), channel_id=1, source_target_pairs={{0,1},{1,0},{2,3},{3,2},{4,5},{5,4},{6,7},{7,6},{8,9},{9,8},{10,11... | collective-permute-start | bytes 786440 | tf_op jit(solution)/shard_map/ppermute | solution.py:633
  80.7 13.0 %collective-permute-start.26 = (bf16[1,64,4096]{2,1,0:T(8,128)(2,1)S(1)}, bf16[1,64,4096]{2,1,0:T(8,128)(2,1)S(1)}, u32[]{:S(2)}, u32[]{:S(2)}) collective-permute-start(bf16[1,64,4096]{2,1,0:T(8,128)(2,1)S(1)} %get-tuple-element.45.refs_0_), channel_id=1, source_target_pairs={{0,1},{1,0},{2,3},{3,2},{4,5},{5,4},{6,7},{7,6},{8,9},{9,8},{10,11... | collective-permute-start | bytes 1572872 | tf_op jit(solution)/shard_map/ppermute | solution.py:633
  81.2 13.4 %collective-permute-start.27 = (bf16[1,64,4096]{2,1,0:T(8,128)(2,1)S(1)}, bf16[1,64,4096]{2,1,0:T(8,128)(2,1)S(1)}, u32[]{:S(2)}, u32[]{:S(2)}) collective-permute-start(bf16[1,64,4096]{2,1,0:T(8,128)(2,1)S(1)} %collective-permute-done.21.refs_0_.refs_1_), channel_id=1, source_target_pairs={{0,1},{1,0},{2,3},{3,2},{4,5},{5,4},{6,7},{7,6},{8,9},{9,8},{10,11... | collective-permute-start | bytes 1572872 | tf_op jit(solution)/shard_map/ppermute | solution.py:633
  93.1 17.4 %collective-permute-start.17 = (bf16[64,2048]{1,0:T(8,128)(2,1)S(1)}, bf16[64,2048]{1,0:T(8,128)(2,1)S(1)}, u32[]{:S(2)}, u32[]{:S(2)}) collective-permute-start(bf16[64,2048]{1,0:T(8,128)(2,1)S(1)} %get-tuple-element.42), channel_id=1, source_target_pairs={{0,1},{1,0},{2,3},{3,2},{4,5},{5,4},{6,7},{7,6},{8,9},{9,8},{10,11... | collective-permute-start | bytes 786440 | tf_op jit(solution)/shard_map/ppermute | solution.py:633
  93.7 16.7 %collective-permute-start.19 = (bf16[64,2048]{1,0:T(8,128)(2,1)S(1)}, bf16[64,2048]{1,0:T(8,128)(2,1)S(1)}, u32[]{:S(2)}, u32[]{:S(2)}) collective-permute-start(bf16[64,2048]{1,0:T(8,128)(2,1)S(1)} %add_convert_fusion.3), channel_id=1, source_target_pairs={{0,2},{1,3},{2,0},{3,1},{4,6},{5,7},{6,4},{7,5},{8,10},{9,11},{10,... | collective-permute-start | bytes 786440 | tf_op jit(solution)/shard_map/ppermute | solution.py:636
  98.6 9.8 %collective-permute-start.35 = (bf16[64,2048]{1,0:T(8,128)(2,1)S(1)}, bf16[64,2048]{1,0:T(8,128)(2,1)S(1)}, u32[]{:S(2)}, u32[]{:S(2)}) collective-permute-start(bf16[64,2048]{1,0:T(8,128)(2,1)S(1)} %add_convert_fusion), channel_id=1, source_target_pairs={{0,2},{1,3},{2,0},{3,1},{4,6},{5,7},{6,4},{7,5},{8,10},{9,11},{10,... | collective-permute-start | bytes 786440 | tf_op jit(solution)/shard_map/ppermute | solution.py:636
  99.8 10.7 %collective-permute-start.28 = (bf16[64,2048]{1,0:T(8,128)(2,1)S(1)}, bf16[64,2048]{1,0:T(8,128)(2,1)S(1)}, u32[]{:S(2)}, u32[]{:S(2)}) collective-permute-start(bf16[64,2048]{1,0:T(8,128)(2,1)S(1)} %get-tuple-element.50), channel_id=1, source_target_pairs={{0,1},{1,0},{2,3},{3,2},{4,5},{5,4},{6,7},{7,6},{8,9},{9,8},{10,11... | collective-permute-start | bytes 786440 | tf_op jit(solution)/shard_map/ppermute | solution.py:633
  99.8 13.8 %collective-permute-start.30 = (bf16[64,2048]{1,0:T(8,128)(2,1)S(1)}, bf16[64,2048]{1,0:T(8,128)(2,1)S(1)}, u32[]{:S(2)}, u32[]{:S(2)}) collective-permute-start(bf16[64,2048]{1,0:T(8,128)(2,1)S(1)} %add_convert_fusion.1), channel_id=1, source_target_pairs={{0,2},{1,3},{2,0},{3,1},{4,6},{5,7},{6,4},{7,5},{8,10},{9,11},{10,... | collective-permute-start | bytes 786440 | tf_op jit(solution)/shard_map/ppermute | solution.py:636
  (15 other events, 119.1 us)

commit v22 on v20

--- a/solution.py
+++ b/solution.py
@@ -682,11 +682,11 @@
         return arrived, [to_chip(keep[k] + arrived[k], k) for k in range(1, chips)]
 
     def over_dp(total):
-        k = owners // 2
-        while k > 1:
+        k = 1
+        while 2 * k < owners:
             total = total + across_dp(total, k)
-            k //= 2
-        return total, [across_dp(total, 1)]
+            k *= 2
+        return total, [across_dp(total, k)]
 
     if owners == 4 and block_count == 4:
         relay = Relay(index_of, index, tokens)

time: 116 us -> 117 us (level)
    ppermute x2, starting transfers between devices: 5.43 us -> 2.82 us  [across_dp(): return lax.ppermute(value, 'dp', [(i, i ^ k) for i in range(owners)])]
    ppermute x1, starting transfers between devices: 1.92 us -> 3.97 us  [second(): lax.ppermute(outer, 'dp', [(1, 0), (0, 1), (3, 2)])]
    ppermute x2, waiting for transfers between devices: 16.2 us -> 17.7 us  [across_dp(): return lax.ppermute(value, 'dp', [(i, i ^ k) for i in range(owners)])]
where the time goes in v22:
time: 117 us; the launch traced here: 116 us
  waiting for transfers between devices  43.4 us (37%)
  starting transfers between devices  35.9 us (31%)
  Pallas kernels  34.9 us (30%)
    ppermute x2, waiting for transfers between devices, across_dp(): return lax.ppermute(value, 'dp', [(i, i ^ k) for i in range(owners)])  17.7 us
    pallas_call x4, Pallas kernels, split_product(): pl.pallas_call(functools.partial(split_product_kernel, each, half, part *...  9.29 us
    ppermute x7, starting transfers between devices, to_chip(): lax.ppermute(value, 'tensor', [(i, i ^ k * CORES) for i in range(parts)])  8.07 us
    ppermute x2, waiting for transfers between devices, spread(): outer_3 = lax.ppermute(inner_2, 'dp', [(1, 0), (2, 3)])  7.83 us
    ppermute x7, waiting for transfers between devices, to_chip(): lax.ppermute(value, 'tensor', [(i, i ^ k * CORES) for i in range(parts)])  7.51 us
    pallas_call x1, Pallas kernels, load_weight(): pl.pallas_call(load_weight_kernel, grid=(1,), in_specs=[pl.BlockSpec(memo...  5.89 us
    ppermute x1, starting transfers between devices, first(): lax.ppermute(inward, 'dp', [(3, 2), (0, 1)])  4.96 us
    ppermute x2, waiting for transfers between devices, spread(): outer_2 = lax.ppermute(inner, 'dp', [(1, 0), (2, 3)])  4.62 us
  transfers between devices with their start and end apart: 36, of which 13 were waited for; matrix products, arithmetic and copies ran while one was open for 0% of the time, Pallas kernels for 24%

profile of v22, /device:TPU:0, one launch (start us, length us, event | category | flops | bytes accessed | tf_op | source)
XLA Modules:
  0.0 116.5 jit_solution(7206585276370779749)
XLA Ops:
  1.5 1.8 %first_hop.1 = (bf16[128,2048]{1,0:T(8,128)(2,1)S(1)}, bf16[128,2048]{1,0:T(8,128)(2,1)S(1)}) custom-call(s32[14]{0:T(128)S(1)} %concatenate.3.index_ref.refs_0_, bf16[384,2048]{1,0:T(8,128)(2,1)} %tokens_ref.9), custom_call_target="tpu_custom_call" | custom-call | flops 1 | bytes 1 | tf_op jit(solution)/shard_map/first_hop/pallas_call | solution.py:191
  3.3 5.0 %collective-permute-start.4 = (bf16[128,2048]{1,0:T(8,128)(2,1)S(1)}, bf16[128,2048]{1,0:T(8,128)(2,1)S(1)}, u32[]{:S(2)}, u32[]{:S(2)}) collective-permute-start(bf16[128,2048]{1,0:T(8,128)(2,1)S(1)} %get-tuple-element.30.refs_0_), channel_id=1, source_target_pairs={{12,8},{0,4},{13,9},{1,5},{14,10},{2,6},{15,11},{3,7},{28,24},{16,... | collective-permute-start | bytes 1572872 | tf_op jit(solution)/shard_map/ppermute | solution.py:220
  9.0 2.7 %narrow.1 = (f32[2,1,64,128]{3,2,1,0:T(8,128)S(1)}, f32[2,1,64,128]{3,2,1,0:T(8,128)S(1)}) custom-call(s32[14]{0:T(128)S(1)} %concatenate.3.index_ref.refs_0_, bf16[384,2048]{1,0:T(8,128)(2,1)} %tokens_ref.9, bf16[1,64,2048]{2,1,0:T(8,128)(2,1)} %bitcast.7, bf16[128,2048]{1,0:T(8,128)(2,1)S(1)} %get-tuple-element.30.refs_0_), custom_call_target="tpu_custom_call" | custom-call | flops 1 | bytes 1 | tf_op jit(solution)/shard_map/narrow/pallas_call | solution.py:367
  14.5 2.4 %backward.1.back_ref = f32[1,64,128]{2,1,0:T(8,128)S(1)} custom-call(s32[14]{0:T(128)S(1)} %concatenate.3.index_ref.refs_0_, bf16[128,4096]{1,0:T(8,128)(2,1)} %cot_ref.3, bf16[4,64,4096]{2,1,0:T(8,128)(2,1)} %refs_2_.3, f32[2,1,64,128]{3,2,1,0:T(8,128)S(1)} %get-tuple-element.32.refs_0_), custom_call_target="tpu_custom_call" | custom-call | flops 1 | bytes 1 | tf_op jit(solution)/shard_map/backward/pallas_call | solution.py:403
  17.0 4.3 %collective-permute-done.2 = f32[2,1,64,128]{3,2,1,0:T(8,128)S(1)} collective-permute-done((f32[2,1,64,128]{3,2,1,0:T(8,128)S(1)}, f32[2,1,64,128]{3,2,1,0:T(8,128)S(1)}, u32[]{:S(2)}, u32[]{:S(2)}) %collective-permute-start.2) | collective-permute-done | bytes 65568 | tf_op jit(solution)/shard_map/ppermute | solution.py:665
  22.0 4.0 %collective-permute-start.6 = (bf16[128,2048]{1,0:T(8,128)(2,1)S(1)}, bf16[128,2048]{1,0:T(8,128)(2,1)S(1)}, u32[]{:S(2)}, u32[]{:S(2)}) collective-permute-start(bf16[128,2048]{1,0:T(8,128)(2,1)S(1)} %get-tuple-element.35), channel_id=1, source_target_pairs={{4,0},{0,4},{12,8},{5,1},{1,5},{13,9},{6,2},{2,6},{14,10},{7,3},{3... | collective-permute-start | bytes 1572872 | tf_op jit(solution)/shard_map/ppermute | solution.py:230
  26.7 2.8 %collective-permute-start.3 = (f32[2,1,64,128]{3,2,1,0:T(8,128)S(1)}, f32[2,1,64,128]{3,2,1,0:T(8,128)S(1)}, u32[]{:S(2)}, u32[]{:S(2)}) collective-permute-start(f32[2,1,64,128]{3,2,1,0:T(8,128)S(1)} %add.31.sum_ref.refs_0_), channel_id=1, source_target_pairs={{0,8},{4,12},{8,0},{12,4},{1,9},{5,13},{9,1},{13,5},{2,10},{6,14},... | collective-permute-start | bytes 196616 | tf_op jit(solution)/shard_map/ppermute | solution.py:665
  29.4 13.5 %collective-permute-done.3.refs_0_ = f32[2,1,64,128]{3,2,1,0:T(8,128)S(1)} collective-permute-done((f32[2,1,64,128]{3,2,1,0:T(8,128)S(1)}, f32[2,1,64,128]{3,2,1,0:T(8,128)S(1)}, u32[]{:S(2)}, u32[]{:S(2)}) %collective-permute-start.3) | collective-permute-done | bytes 65568 | tf_op jit(solution)/shard_map/ppermute | solution.py:665
  44.3 4.2 %collective-permute-start.13 = (bf16[64,2048]{1,0:T(8,128)(2,1)S(1)}, bf16[64,2048]{1,0:T(8,128)(2,1)S(1)}, u32[]{:S(2)}, u32[]{:S(2)}) collective-permute-start(bf16[64,2048]{1,0:T(8,128)(2,1)S(1)} %get-tuple-element.38.home_ref), channel_id=1, source_target_pairs={{0,4},{4,0},{8,12},{12,8},{1,5},{5,1},{9,13},{13,9},{2,6},{6,2},{1... | collective-permute-start | bytes 786440 | tf_op jit(solution)/shard_map/ppermute | solution.py:240
  49.1 3.2 %collective-permute-done.8.outer_ref = bf16[64,2048]{1,0:T(8,128)(2,1)S(1)} collective-permute-done((bf16[64,2048]{1,0:T(8,128)(2,1)S(1)}, bf16[64,2048]{1,0:T(8,128)(2,1)S(1)}, u32[]{:S(2)}, u32[]{:S(2)}) %collective-permute-start.8) | collective-permute-done | bytes 262176 | tf_op jit(solution)/shard_map/ppermute | solution.py:240
  60.1 5.9 %load_weight.1.refs_6_.w_ref = bf16[2048,4096]{1,0:T(8,128)(2,1)S(1)} custom-call(bf16[2048,4096]{1,0:T(8,128)(2,1)} %w_ref.1, bf16[64,2048]{1,0:T(8,128)(2,1)S(1)} %collective-permute-done.13.refs_0_.outer_ref, bf16[64,2048]{1,0:T(8,128)(2,1)S(1)} %collective-permute-done.15.refs_1_.refs_0_), custom_call_target="tpu_custom_call" | custom-call | flops 1 | bytes 1 | tf_op jit(solution)/shard_map/load_weight/pallas_call | solution.py:284
  66.6 4.0 %collective-permute-done.16.refs_5_.refs_2_ = bf16[64,2048]{1,0:T(8,128)(2,1)S(1)} collective-permute-done((bf16[64,2048]{1,0:T(8,128)(2,1)S(1)}, bf16[64,2048]{1,0:T(8,128)(2,1)S(1)}, u32[]{:S(2)}, u32[]{:S(2)}) %collective-permute-start.16) | collective-permute-done | bytes 262176 | tf_op jit(solution)/shard_map/ppermute | solution.py:242
  70.6 2.8 %collective-permute-done.12.refs_3_ = bf16[64,2048]{1,0:T(8,128)(2,1)S(1)} collective-permute-done((bf16[64,2048]{1,0:T(8,128)(2,1)S(1)}, bf16[64,2048]{1,0:T(8,128)(2,1)S(1)}, u32[]{:S(2)}, u32[]{:S(2)}) %collective-permute-start.12) | collective-permute-done | bytes 262176 | tf_op jit(solution)/shard_map/ppermute | solution.py:244
  74.1 2.3 %split_product.5 = (bf16[64,2048]{1,0:T(8,128)(2,1)S(1)}, bf16[64,2048]{1,0:T(8,128)(2,1)S(1)}, f32[64,2048]{1,0:T(8,128)S(1)}, f32[64,2048]{1,0:T(8,128)S(1)}) custom-call(bf16[256,2048]{1,0:T(8,128)(2,1)S(1)} %collect.2.rows_ref, bf16[2048,4096]{1,0:T(8,128)(2,1)S(1)} %load_weight.1.refs_6_.w_ref, ...), custom_call_target="tpu_custom_call" | custom-call | flops 1 | bytes 1 | tf_op jit(solution)/shard_map/split_product/pallas_call | solution.py:317
  79.1 2.3 %split_product.4 = (bf16[64,2048]{1,0:T(8,128)(2,1)S(1)}, bf16[64,2048]{1,0:T(8,128)(2,1)S(1)}, f32[64,2048]{1,0:T(8,128)S(1)}, f32[64,2048]{1,0:T(8,128)S(1)}) custom-call(bf16[256,2048]{1,0:T(8,128)(2,1)S(1)} %collect.2.rows_ref, bf16[2048,4096]{1,0:T(8,128)(2,1)S(1)} %load_weight.1.refs_6_.w_ref), custom_call_target="tpu_custom_call" | custom-call | flops 1 | bytes 1 | tf_op jit(solution)/shard_map/split_product/pallas_call | solution.py:317
  82.0 5.0 %collective-permute-done.20.refs_3_ = bf16[64,2048]{1,0:T(8,128)(2,1)S(1)} collective-permute-done((bf16[64,2048]{1,0:T(8,128)(2,1)S(1)}, bf16[64,2048]{1,0:T(8,128)(2,1)S(1)}, u32[]{:S(2)}, u32[]{:S(2)}) %collective-permute-start.20) | collective-permute-done | bytes 262176 | tf_op jit(solution)/shard_map/ppermute | solution.py:244
  88.6 2.2 %collective-permute-done.24.refs_1_ = bf16[1,64,128]{2,1,0:T(8,128)(2,1)S(1)} collective-permute-done((bf16[1,64,128]{2,1,0:T(8,128)(2,1)S(1)}, bf16[1,64,128]{2,1,0:T(8,128)(2,1)S(1)}, u32[]{:S(2)}, u32[]{:S(2)}) %collective-permute-start.24) | collective-permute-done | bytes 16416 | tf_op jit(solution)/shard_map/ppermute | solution.py:662
  91.3 2.3 %split_product.7 = (bf16[64,2048]{1,0:T(8,128)(2,1)S(1)}, bf16[64,2048]{1,0:T(8,128)(2,1)S(1)}, f32[64,2048]{1,0:T(8,128)S(1)}, f32[64,2048]{1,0:T(8,128)S(1)}) custom-call(bf16[256,2048]{1,0:T(8,128)(2,1)S(1)} %collect.3.rows_ref, bf16[2048,4096]{1,0:T(8,128)(2,1)S(1)} %load_weight.1.refs_6_.w_ref, ...), custom_call_target="tpu_custom_call" | custom-call | flops 1 | bytes 1 | tf_op jit(solution)/shard_map/split_product/pallas_call | solution.py:317
  95.4 2.3 %split_product.6 = (bf16[64,2048]{1,0:T(8,128)(2,1)S(1)}, bf16[64,2048]{1,0:T(8,128)(2,1)S(1)}, f32[64,2048]{1,0:T(8,128)S(1)}, f32[64,2048]{1,0:T(8,128)S(1)}) custom-call(bf16[256,2048]{1,0:T(8,128)(2,1)S(1)} %collect.3.rows_ref, bf16[2048,4096]{1,0:T(8,128)(2,1)S(1)} %load_weight.1.refs_6_.w_ref, ...), custom_call_target="tpu_custom_call" | custom-call | flops 1 | bytes 1 | tf_op jit(solution)/shard_map/split_product/pallas_call | solution.py:317
  103.0 3.9 %up_gradient.1.refs_9_ = f32[4,64,4096]{2,1,0:T(8,128)} custom-call(s32[14]{0:T(128)S(1)} %concatenate.3.index_ref.refs_0_, bf16[1,64,4096]{2,1,0:T(8,128)(2,1)S(1)} %get-tuple-element.43.refs_0_, bf16[1,64,4096]{2,1,0:T(8,128)(2,1)S(1)} %collective-permute-done.21.refs_0_.refs_1_, bf16[1,64,4096]{2,1,0:T(8,128)(2,1)S(1)} %collective-permute-done.26.refs_2_, ...), custom_call_target="tpu_custom_call" | custom-call | flops 1 | bytes 1 | tf_op jit(solution)/shard_map/up_gradient/pallas_call | solution.py:550
  106.9 2.3 %collective-permute-done.35.refs_8_ = bf16[64,2048]{1,0:T(8,128)(2,1)S(1)} collective-permute-done((bf16[64,2048]{1,0:T(8,128)(2,1)S(1)}, bf16[64,2048]{1,0:T(8,128)(2,1)S(1)}, u32[]{:S(2)}, u32[]{:S(2)}) %collective-permute-start.35) | collective-permute-done | bytes 262176 | tf_op jit(solution)/shard_map/ppermute | solution.py:662
  109.2 2.1 %finish.2.refs_9_ = bf16[128,4096]{1,0:T(8,128)(2,1)} custom-call(s32[14]{0:T(128)S(1)} %concatenate.3.index_ref.refs_0_, bf16[1,64,128]{2,1,0:T(8,128)(2,1)S(1)} %get-tuple-element.33.refs_1_, bf16[4,64,4096]{2,1,0:T(8,128)(2,1)S(1)} %copy-done.1, f32[64,2048]{1,0:T(8,128)S(1)} %get-tuple-element.51.refs_3_, ...), custom_call_target="tpu_custom_call" | custom-call | flops 1 | bytes 1 | tf_op jit(solution)/shard_map/finish/pallas_call | solution.py:620
  111.3 3.0 %collective-permute-done.30.refs_8_ = bf16[64,2048]{1,0:T(8,128)(2,1)S(1)} collective-permute-done((bf16[64,2048]{1,0:T(8,128)(2,1)S(1)}, bf16[64,2048]{1,0:T(8,128)(2,1)S(1)}, u32[]{:S(2)}, u32[]{:S(2)}) %collective-permute-start.30) | collective-permute-done | bytes 262176 | tf_op jit(solution)/shard_map/ppermute | solution.py:662
  114.3 2.1 %finish.3 = bf16[128,4096]{1,0:T(8,128)(2,1)} custom-call(s32[14]{0:T(128)S(1)} %concatenate.3.index_ref.refs_0_, bf16[1,64,128]{2,1,0:T(8,128)(2,1)S(1)} %get-tuple-element.33.refs_1_, bf16[4,64,4096]{2,1,0:T(8,128)(2,1)S(1)} %copy-done.1, f32[64,2048]{1,0:T(8,128)S(1)} %get-tuple-element.39.refs_3_, ...), custom_call_target="tpu_custom_call", output_to_operand_aliasing={{}: (9, {})} | custom-call | flops 1 | bytes 1 | tf_op jit(solution)/shard_map/finish/pallas_call | solution.py:620
  (79 shorter events, 29.1 us)
Async XLA Ops:
  3.3 18.0 %collective-permute-start.4 = (bf16[128,2048]{1,0:T(8,128)(2,1)S(1)}, bf16[128,2048]{1,0:T(8,128)(2,1)S(1)}, u32[]{:S(2)}, u32[]{:S(2)}) collective-permute-start(bf16[128,2048]{1,0:T(8,128)(2,1)S(1)} %get-tuple-element.30.refs_0_), channel_id=1, source_target_pairs={{12,8},{0,4},{13,9},{1,5},{14,10},{2,6},{15,11},{3,7},{28,24},{16,... | collective-permute-start | bytes 1572872 | tf_op jit(solution)/shard_map/ppermute | solution.py:220
  8.3 13.0 %collective-permute-start.5 = (bf16[128,2048]{1,0:T(8,128)(2,1)S(1)}, bf16[128,2048]{1,0:T(8,128)(2,1)S(1)}, u32[]{:S(2)}, u32[]{:S(2)}) collective-permute-start(bf16[128,2048]{1,0:T(8,128)(2,1)S(1)} %get-tuple-element.34), channel_id=1, source_target_pairs={{8,4},{9,5},{10,6},{11,7},{24,20},{25,21},{26,22},{27,23}} | collective-permute-start | bytes 1572872 | tf_op jit(solution)/shard_map/ppermute | solution.py:221
  22.0 20.9 %collective-permute-start.6 = (bf16[128,2048]{1,0:T(8,128)(2,1)S(1)}, bf16[128,2048]{1,0:T(8,128)(2,1)S(1)}, u32[]{:S(2)}, u32[]{:S(2)}) collective-permute-start(bf16[128,2048]{1,0:T(8,128)(2,1)S(1)} %get-tuple-element.35), channel_id=1, source_target_pairs={{4,0},{0,4},{12,8},{5,1},{1,5},{13,9},{6,2},{2,6},{14,10},{7,3},{3... | collective-permute-start | bytes 1572872 | tf_op jit(solution)/shard_map/ppermute | solution.py:230
  25.9 16.9 %collective-permute-start.7 = (bf16[128,2048]{1,0:T(8,128)(2,1)S(1)}, bf16[128,2048]{1,0:T(8,128)(2,1)S(1)}, u32[]{:S(2)}, u32[]{:S(2)}) collective-permute-start(bf16[128,2048]{1,0:T(8,128)(2,1)S(1)} %get-tuple-element.36), channel_id=1, source_target_pairs={{8,4},{4,8},{9,5},{5,9},{10,6},{6,10},{11,7},{7,11},{24,20},{20,24... | collective-permute-start | bytes 1572872 | tf_op jit(solution)/shard_map/ppermute | solution.py:231
  26.7 16.2 %collective-permute-start.3 = (f32[2,1,64,128]{3,2,1,0:T(8,128)S(1)}, f32[2,1,64,128]{3,2,1,0:T(8,128)S(1)}, u32[]{:S(2)}, u32[]{:S(2)}) collective-permute-start(f32[2,1,64,128]{3,2,1,0:T(8,128)S(1)} %add.31.sum_ref.refs_0_), channel_id=1, source_target_pairs={{0,8},{4,12},{8,0},{12,4},{1,9},{5,13},{9,1},{13,5},{2,10},{6,14},... | collective-permute-start | bytes 196616 | tf_op jit(solution)/shard_map/ppermute | solution.py:665
  43.5 8.8 %collective-permute-start.8 = (bf16[64,2048]{1,0:T(8,128)(2,1)S(1)}, bf16[64,2048]{1,0:T(8,128)(2,1)S(1)}, u32[]{:S(2)}, u32[]{:S(2)}) collective-permute-start(bf16[64,2048]{1,0:T(8,128)(2,1)S(1)} %get-tuple-element.37.home_ref), channel_id=1, source_target_pairs={{0,4},{4,0},{8,12},{12,8},{1,5},{5,1},{9,13},{13,9},{2,6},{6,2},{1... | collective-permute-start | bytes 786440 | tf_op jit(solution)/shard_map/ppermute | solution.py:240
  43.6 11.9 %collective-permute-start.9 = (bf16[64,2048]{1,0:T(8,128)(2,1)S(1)}, bf16[64,2048]{1,0:T(8,128)(2,1)S(1)}, u32[]{:S(2)}, u32[]{:S(2)}) collective-permute-start(bf16[64,2048]{1,0:T(8,128)(2,1)S(1)} %get-tuple-element.37.home_ref), channel_id=1, source_target_pairs={{4,8},{8,4},{5,9},{9,5},{6,10},{10,6},{7,11},{11,7},{20,24},{24,20... | collective-permute-start | bytes 786440 | tf_op jit(solution)/shard_map/ppermute | solution.py:241
  44.3 12.5 %collective-permute-start.13 = (bf16[64,2048]{1,0:T(8,128)(2,1)S(1)}, bf16[64,2048]{1,0:T(8,128)(2,1)S(1)}, u32[]{:S(2)}, u32[]{:S(2)}) collective-permute-start(bf16[64,2048]{1,0:T(8,128)(2,1)S(1)} %get-tuple-element.38.home_ref), channel_id=1, source_target_pairs={{0,4},{4,0},{8,12},{12,8},{1,5},{5,1},{9,13},{13,9},{2,6},{6,2},{1... | collective-permute-start | bytes 786440 | tf_op jit(solution)/shard_map/ppermute | solution.py:240
  48.5 9.0 %collective-permute-start.15 = (bf16[64,2048]{1,0:T(8,128)(2,1)S(1)}, bf16[64,2048]{1,0:T(8,128)(2,1)S(1)}, u32[]{:S(2)}, u32[]{:S(2)}) collective-permute-start(bf16[64,2048]{1,0:T(8,128)(2,1)S(1)} %get-tuple-element.38.home_ref), channel_id=1, source_target_pairs={{4,8},{8,4},{5,9},{9,5},{6,10},{10,6},{7,11},{11,7},{20,24},{24,20... | collective-permute-start | bytes 786440 | tf_op jit(solution)/shard_map/ppermute | solution.py:241
  53.9 20.1 %collective-permute-start.21 = (bf16[1,64,4096]{2,1,0:T(8,128)(2,1)S(1)}, bf16[1,64,4096]{2,1,0:T(8,128)(2,1)S(1)}, u32[]{:S(2)}, u32[]{:S(2)}) collective-permute-start(bf16[1,64,4096]{2,1,0:T(8,128)(2,1)S(1)} %get-tuple-element.43.refs_0_), channel_id=1, source_target_pairs={{0,2},{1,3},{2,0},{3,1},{4,6},{5,7},{6,4},{7,5},{8,10},{9,11},{10,... | collective-permute-start | bytes 1572872 | tf_op jit(solution)/shard_map/ppermute | solution.py:662
  55.5 11.1 %collective-permute-start.11 = (bf16[64,2048]{1,0:T(8,128)(2,1)S(1)}, bf16[64,2048]{1,0:T(8,128)(2,1)S(1)}, u32[]{:S(2)}, u32[]{:S(2)}) collective-permute-start(bf16[64,2048]{1,0:T(8,128)(2,1)S(1)} %collective-permute-done.9.refs_0_), channel_id=1, source_target_pairs={{4,0},{8,12},{5,1},{9,13},{6,2},{10,14},{7,3},{11,15},{20,16},{24,... | collective-permute-start | bytes 786440 | tf_op jit(solution)/shard_map/ppermute | solution.py:242
  56.8 9.8 %collective-permute-start.14 = (bf16[64,2048]{1,0:T(8,128)(2,1)S(1)}, bf16[64,2048]{1,0:T(8,128)(2,1)S(1)}, u32[]{:S(2)}, u32[]{:S(2)}) collective-permute-start(bf16[64,2048]{1,0:T(8,128)(2,1)S(1)} %collective-permute-done.13.refs_0_.outer_ref), channel_id=1, source_target_pairs={{4,8},{8,4},{5,9},{9,5},{6,10},{10,6},{7,11},{11,7},{20,24},{24,20... | collective-permute-start | bytes 786440 | tf_op jit(solution)/shard_map/ppermute | solution.py:243
  57.5 13.1 %collective-permute-start.16 = (bf16[64,2048]{1,0:T(8,128)(2,1)S(1)}, bf16[64,2048]{1,0:T(8,128)(2,1)S(1)}, u32[]{:S(2)}, u32[]{:S(2)}) collective-permute-start(bf16[64,2048]{1,0:T(8,128)(2,1)S(1)} %collective-permute-done.15.refs_1_.refs_0_), channel_id=1, source_target_pairs={{4,0},{8,12},{5,1},{9,13},{6,2},{10,14},{7,3},{11,15},{20,16},{24,... | collective-permute-start | bytes 786440 | tf_op jit(solution)/shard_map/ppermute | solution.py:242
  58.8 14.6 %collective-permute-start.12 = (bf16[64,2048]{1,0:T(8,128)(2,1)S(1)}, bf16[64,2048]{1,0:T(8,128)(2,1)S(1)}, u32[]{:S(2)}, u32[]{:S(2)}) collective-permute-start(bf16[64,2048]{1,0:T(8,128)(2,1)S(1)} %collective-permute-done.10.refs_1_), channel_id=1, source_target_pairs={{4,0},{8,12},{5,1},{9,13},{6,2},{10,14},{7,3},{11,15},{20,16},{24,... | collective-permute-start | bytes 786440 | tf_op jit(solution)/shard_map/ppermute | solution.py:244
  76.5 10.6 %collective-permute-start.20 = (bf16[64,2048]{1,0:T(8,128)(2,1)S(1)}, bf16[64,2048]{1,0:T(8,128)(2,1)S(1)}, u32[]{:S(2)}, u32[]{:S(2)}) collective-permute-start(bf16[64,2048]{1,0:T(8,128)(2,1)S(1)} %collective-permute-done.14.refs_4_.refs_1_), channel_id=1, source_target_pairs={{4,0},{8,12},{5,1},{9,13},{6,2},{10,14},{7,3},{11,15},{20,16},{24,... | collective-permute-start | bytes 786440 | tf_op jit(solution)/shard_map/ppermute | solution.py:244
  78.1 12.7 %collective-permute-start.32 = (bf16[64,2048]{1,0:T(8,128)(2,1)S(1)}, bf16[64,2048]{1,0:T(8,128)(2,1)S(1)}, u32[]{:S(2)}, u32[]{:S(2)}) collective-permute-start(bf16[64,2048]{1,0:T(8,128)(2,1)S(1)} %add_convert_fusion.2.refs_4_), channel_id=1, source_target_pairs={{0,2},{1,3},{2,0},{3,1},{4,6},{5,7},{6,4},{7,5},{8,10},{9,11},{10,... | collective-permute-start | bytes 786440 | tf_op jit(solution)/shard_map/ppermute | solution.py:662
  81.4 12.3 %collective-permute-start.18 = (bf16[64,2048]{1,0:T(8,128)(2,1)S(1)}, bf16[64,2048]{1,0:T(8,128)(2,1)S(1)}, u32[]{:S(2)}, u32[]{:S(2)}) collective-permute-start(bf16[64,2048]{1,0:T(8,128)(2,1)S(1)} %get-tuple-element.42), channel_id=1, source_target_pairs={{0,1},{1,0},{2,3},{3,2},{4,5},{5,4},{6,7},{7,6},{8,9},{9,8},{10,11... | collective-permute-start | bytes 786440 | tf_op jit(solution)/shard_map/ppermute | solution.py:659
  81.5 13.0 %collective-permute-start.26 = (bf16[1,64,4096]{2,1,0:T(8,128)(2,1)S(1)}, bf16[1,64,4096]{2,1,0:T(8,128)(2,1)S(1)}, u32[]{:S(2)}, u32[]{:S(2)}) collective-permute-start(bf16[1,64,4096]{2,1,0:T(8,128)(2,1)S(1)} %get-tuple-element.43.refs_0_), channel_id=1, source_target_pairs={{0,1},{1,0},{2,3},{3,2},{4,5},{5,4},{6,7},{7,6},{8,9},{9,8},{10,11... | collective-permute-start | bytes 1572872 | tf_op jit(solution)/shard_map/ppermute | solution.py:659
  82.0 13.4 %collective-permute-start.27 = (bf16[1,64,4096]{2,1,0:T(8,128)(2,1)S(1)}, bf16[1,64,4096]{2,1,0:T(8,128)(2,1)S(1)}, u32[]{:S(2)}, u32[]{:S(2)}) collective-permute-start(bf16[1,64,4096]{2,1,0:T(8,128)(2,1)S(1)} %collective-permute-done.21.refs_0_.refs_1_), channel_id=1, source_target_pairs={{0,1},{1,0},{2,3},{3,2},{4,5},{5,4},{6,7},{7,6},{8,9},{9,8},{10,11... | collective-permute-start | bytes 1572872 | tf_op jit(solution)/shard_map/ppermute | solution.py:659
  93.8 17.5 %collective-permute-start.17 = (bf16[64,2048]{1,0:T(8,128)(2,1)S(1)}, bf16[64,2048]{1,0:T(8,128)(2,1)S(1)}, u32[]{:S(2)}, u32[]{:S(2)}) collective-permute-start(bf16[64,2048]{1,0:T(8,128)(2,1)S(1)} %get-tuple-element.40), channel_id=1, source_target_pairs={{0,1},{1,0},{2,3},{3,2},{4,5},{5,4},{6,7},{7,6},{8,9},{9,8},{10,11... | collective-permute-start | bytes 786440 | tf_op jit(solution)/shard_map/ppermute | solution.py:659
  94.5 16.9 %collective-permute-start.19 = (bf16[64,2048]{1,0:T(8,128)(2,1)S(1)}, bf16[64,2048]{1,0:T(8,128)(2,1)S(1)}, u32[]{:S(2)}, u32[]{:S(2)}) collective-permute-start(bf16[64,2048]{1,0:T(8,128)(2,1)S(1)} %add_convert_fusion.3), channel_id=1, source_target_pairs={{0,2},{1,3},{2,0},{3,1},{4,6},{5,7},{6,4},{7,5},{8,10},{9,11},{10,... | collective-permute-start | bytes 786440 | tf_op jit(solution)/shard_map/ppermute | solution.py:662
  99.3 9.9 %collective-permute-start.35 = (bf16[64,2048]{1,0:T(8,128)(2,1)S(1)}, bf16[64,2048]{1,0:T(8,128)(2,1)S(1)}, u32[]{:S(2)}, u32[]{:S(2)}) collective-permute-start(bf16[64,2048]{1,0:T(8,128)(2,1)S(1)} %add_convert_fusion), channel_id=1, source_target_pairs={{0,2},{1,3},{2,0},{3,1},{4,6},{5,7},{6,4},{7,5},{8,10},{9,11},{10,... | collective-permute-start | bytes 786440 | tf_op jit(solution)/shard_map/ppermute | solution.py:662
  100.5 10.8 %collective-permute-start.28 = (bf16[64,2048]{1,0:T(8,128)(2,1)S(1)}, bf16[64,2048]{1,0:T(8,128)(2,1)S(1)}, u32[]{:S(2)}, u32[]{:S(2)}) collective-permute-start(bf16[64,2048]{1,0:T(8,128)(2,1)S(1)} %get-tuple-element.48), channel_id=1, source_target_pairs={{0,1},{1,0},{2,3},{3,2},{4,5},{5,4},{6,7},{7,6},{8,9},{9,8},{10,11... | collective-permute-start | bytes 786440 | tf_op jit(solution)/shard_map/ppermute | solution.py:659
  100.6 13.8 %collective-permute-start.30 = (bf16[64,2048]{1,0:T(8,128)(2,1)S(1)}, bf16[64,2048]{1,0:T(8,128)(2,1)S(1)}, u32[]{:S(2)}, u32[]{:S(2)}) collective-permute-start(bf16[64,2048]{1,0:T(8,128)(2,1)S(1)} %add_convert_fusion.1), channel_id=1, source_target_pairs={{0,2},{1,3},{2,0},{3,1},{4,6},{5,7},{6,4},{7,5},{8,10},{9,11},{10,... | collective-permute-start | bytes 786440 | tf_op jit(solution)/shard_map/ppermute | solution.py:662
  (15 other events, 112.0 us)
